TPU v7x, 32 devices: a whole 2x2x4 slice. The times are simulated.
32 devices in a mesh: groups: 2 (over y), fsdp: 4 (over z), tp: 2 (over x), rep: 2 (over core).
Axes of the slice: x: 2, y: 2, z: 4, core: 2. Of those that a mesh axis runs over, the one named last changes fastest.
Arguments:
- hidden: bfloat16 [1280, 16384], P(('groups', 'tp'), ('fsdp', 'rep')), parts along dimension 0, may hold values from -6 to 6
- w_query: bfloat16 [16384, 16384], P(('fsdp', 'rep'), 'tp'), may hold values from -0.046875 to 0.046875
- w_key: bfloat16 [16384, 1024], P(('fsdp', 'rep'), 'tp'), may hold values from -0.046875 to 0.046875
- w_value: bfloat16 [16384, 1024], P(('fsdp', 'rep'), 'tp'), may hold values from -0.046875 to 0.046875
- canary_rows: int32 [1280], P('groups'), parts along dimension 0, may hold values from 0 to 639, each once
- positions: int32 [1280], P('groups'), parts along dimension 0, may hold values from 0 to 4095
Outputs:
- scores: bfloat16 [2, 64, 1280, 640], P('tp', 'fsdp', 'groups'), parts along dimension 2
- values: bfloat16 [1280, 1024], P('groups', 'tp'), parts along dimension 0
There are 2 independent parts, one for each index of `groups`. A program takes and returns all parts, laid end to end along the dimension named above; an argument that names none is the same for every part. Nothing has to cross between parts.
All inputs are finite; a program needn't handle non-finite values.
Results may differ from a plain program's by a relative error of at most 0.0058.
Values may be sent and summed in bfloat16 or wider, within the bound.
No kernel may reach another device: no remote copies, remote signals or barrier semaphores. Data moves between devices by JAX's collectives and lax.ppermute only.
A program may use at most 256 MiB of HBM per device.

v0:
```python
import math

import jax
import jax.numpy as jnp
from jax import lax
from jax.sharding import PartitionSpec as P

HQ = 128
KV = 8
DH = 128


def rope_tables(positions, width):
    half = width // 2
    expo = jnp.arange(half, dtype=jnp.float32) * (2.0 / width)
    freq = jnp.power(jnp.float32(500000.0), -expo)
    wavelen = 2.0 * math.pi / freq
    smooth = (8192.0 / wavelen - 1.0) / 3.0
    mixed = (1.0 - smooth) * freq / 8.0 + smooth * freq
    freq = jnp.where(wavelen > 8192.0, freq / 8.0, jnp.where(wavelen < 2048.0, freq, mixed))
    angle = positions.astype(jnp.float32)[:, None] * freq[None, :]
    return (jnp.cos(angle)[:, None, :], jnp.sin(angle)[:, None, :])


def rotate(heads, cosine, sine):
    half = heads.shape[-1] // 2
    first = heads[..., :half]
    second = heads[..., half:]
    return jnp.concatenate(
        [first * cosine - second * sine, second * cosine + first * sine], axis=-1
    )


def body(hidden, w_query, w_key, w_value, canary_rows, positions):
    shards = lax.axis_size("fsdp")
    findex = lax.axis_index("fsdp")
    head_cols = w_query.shape[1] // shards
    kv_cols = w_key.shape[1]
    regrouped = lax.all_to_all(w_query, "fsdp", split_axis=1, concat_axis=0, tiled=True)
    rows_all = lax.all_gather(hidden, "tp", axis=0, tiled=True)
    key_part = jnp.dot(rows_all, w_key, preferred_element_type=jnp.float32)
    value_part = jnp.dot(rows_all, w_value, preferred_element_type=jnp.float32)
    query_part = jnp.dot(
        lax.all_gather(rows_all, "fsdp", axis=1, tiled=True),
        regrouped,
        preferred_element_type=jnp.float32,
    )
    rows = query_part.shape[0]
    heads_here = head_cols // DH
    cosine, sine = rope_tables(positions, DH)
    query_sum = lax.psum(query_part, "rep")
    key_sum, value_sum = lax.psum((key_part, value_part), ("fsdp", "rep"))
    key_sel = jnp.take(key_sum, canary_rows, axis=0).reshape(rows, kv_cols // DH, DH)
    values = jnp.take(value_sum, canary_rows, axis=0).astype(jnp.bfloat16)
    key_rot = rotate(key_sel, cosine, sine).astype(jnp.bfloat16)
    query_sel = jnp.take(query_sum, canary_rows, axis=0).reshape(rows, heads_here, DH)
    query_rot = rotate(query_sel, cosine, sine).astype(jnp.bfloat16)
    kv_local = (findex * heads_here + jnp.arange(heads_here, dtype=jnp.int32)) // (HQ // KV)
    key_heads = jnp.take(key_rot, kv_local, axis=1)
    products = jnp.einsum("ihd,jhd->hij", query_rot, key_heads, preferred_element_type=jnp.float32)
    scores = (products * DH ** (-0.5)).astype(jnp.bfloat16).reshape(1, heads_here, rows, rows)
    return (scores, values)


def solution(mesh):
    in_specs = (
        P(("groups", "tp"), ("fsdp", "rep")),
        P(("fsdp", "rep"), "tp"),
        P(("fsdp", "rep"), "tp"),
        P(("fsdp", "rep"), "tp"),
        P("groups"),
        P("groups"),
    )
    out_specs = (P("tp", "fsdp", "groups", None), P("groups", "tp"))
    return jax.shard_map(body, mesh=mesh, in_specs=in_specs, out_specs=out_specs, check_vma=False)
```

profile of v0, /device:TPU:0, one launch (start us, length us, event | category | flops | bytes accessed | tf_op | source)
XLA Modules:
  0.0 1172.2 jit_solution(17874065155370999153)
XLA Ops:
  7.2 0.0 copy-start
  7.2 44.6 %copy.12 = bf16[2048,8192]{0,1:T(8,128)(2,1)} copy(bf16[2048,8192]{1,0:T(8,128)(2,1)} %param.9) | data formatting | bytes 67108864 | tf_op args[1]
  51.8 9.7 all-to-all-start
  61.5 0.0 all-gather.3.cloned.1.call-start
  61.6 0.7 all-gather.3.cloned.1.call-update
  62.3 0.0 all-gather.5.cloned.1.call-start
  62.3 43.5 %all-gather.3.cloned.1.call-done = bf16[640,2048]{1,0:T(8,128)(2,1)} async-done(((bf16[320,2048]{1,0:T(8,128)(2,1)}), bf16[640,2048]{1,0:T(8,128)(2,1)}) %all-gather.3.cloned.1.call-update) | async-done | bytes 2621456 | tf_op jit(solution)/shard_map/all_gather | solution.py:40
  105.8 0.0 all-gather.5.cloned.1.call-update
  105.8 0.0 all-reduce.6.cloned.1.call-start
  105.9 0.0 copy-done
  105.9 4.3 fusion.13
  110.2 0.0 all-reduce.6.cloned.1.call-update
  110.3 0.0 all-reduce.4.cloned.1.call-start
  110.3 868.4 %all-to-all-done = bf16[2048,4,2048]{0,2,1:T(8,128)(2,1)} async-done(((bf16[2048,4,2048]{0,2,1:T(8,128)(2,1)}), bf16[2048,4,2048]{0,2,1:T(8,128)(2,1)}, u32[]{:S(2)}, u32[]{:S(2)}) %all-to-all-start) | async-done | bytes 33554464 | tf_op jit(solution)/shard_map/all_to_all | solution.py:39
  978.7 42.7 %copy.13 = bf16[4,2048,2048]{2,1,0:T(8,128)(2,1)} copy(bf16[4,2048,2048]{1,2,0:T(8,128)(2,1)} %bitcast.1) | data formatting | bytes 67108864 | tf_op jit(solution)/shard_map/all_to_all | solution.py:39
  1021.4 0.0 all-gather.5.cloned.1.call-done
  1021.4 28.9 %fusion.12 = f32[640,2048]{1,0:T(8,128)} fusion(bf16[640,8192]{1,0:T(8,128)(2,1)} %all-gather.5.cloned.1.call-done, bf16[8192,2048]{1,0:T(8,128)(2,1)} %bitcast.18), kind=kOutput, calls=%fused_computation.44 | convolution fusion | flops 21474836480 | bytes 49283072 | tf_op jit(solution)/shard_map/dot_general | solution.py:43
  1050.2 0.0 copy-start.3
  1050.2 0.0 copy-start.2
  1050.3 0.0 all-reduce.4.cloned.1.call-update
  1050.3 0.7 copy-done.3
  1051.0 0.0 copy-done.2
  1051.1 1.2 multiply_cosine_fusion
  1052.3 3.9 fusion.14
  1056.2 57.3 %all-reduce.7 = bf16[640,512]{1,0:T(8,128)(2,1)S(1)} all-reduce(f32[640,512]{1,0:T(8,128)S(1)} %fusion.14), channel_id=1, replica_groups=mesh['groups'=2,'fsdp'=4,'tp'=2,'rep'=2] {'fsdp','rep'}, use_global_device_ids=true, to_apply=%region_2.0 | all-reduce | flops 327680 | bytes 1966080 | tf_op jit(solution)/shard_map/psum | solution.py:52
  1113.5 2.8 gather_fusion.3
  1116.3 1.1 select_convert_fusion
  1117.3 0.0 all-reduce.6.cloned.1.call-done
  1117.3 4.1 gather_fusion.2
  1121.4 0.2 broadcast_select_fusion.1
  1121.6 0.5 reshape.162
  1122.1 0.7 fusion.11
  1122.8 0.3 subtract_convert_fusion.1
  1123.2 0.4 pad_maximum_fusion
  1123.5 2.4 gather_fusion.1
  1125.9 0.0 all-reduce.4.cloned.1.call-done
  1125.9 9.3 gather_fusion
  1135.2 5.9 copy.14
  1141.1 5.9 copy.15
  1147.0 3.1 broadcast_select_fusion
  1150.1 3.5 subtract_convert_fusion
  1153.6 0.0 copy-start.1
  1153.6 12.1 %fusion = bf16[1,16,640,640]{3,2,1,0:T(8,128)(2,1)} fusion(bf16[640,16,64]{2,0,1:T(8,128)(2,1)} %get-tuple-element.4, bf16[640,16,64]{2,0,1:T(8,128)(2,1)} %get-tuple-element.3, bf16[16,640,128]{2,1,0:T(8,128)(2,1)} %gather_fusion.1, pred[16]{0:T(512)(128)(4,1)S(1)} %compare_and_fusion.1), kind=kOutput, calls=%fused_computation.5 | convolution fusion | flops 1697382400 | bytes 18350096 | tf_op jit(solution)/shard_map/ihd,jhd->hij/dot_general | solution.py:60
  1165.7 0.0 copy-done.1
  (8 shorter events, 0.1 us)
Async XLA Ops:
  7.2 98.7 %copy-start = (bf16[2048,512]{1,0:T(8,128)(2,1)S(1)}, bf16[2048,512]{1,0:T(8,128)(2,1)}, u32[]{:S(2)}) copy-start(bf16[2048,512]{1,0:T(8,128)(2,1)} %param.10) | copy-start | bytes 6291460
  51.8 926.9 %all-to-all-start = ((bf16[2048,4,2048]{0,2,1:T(8,128)(2,1)}), bf16[2048,4,2048]{0,2,1:T(8,128)(2,1)}, u32[]{:S(2)}, u32[]{:S(2)}) async-start(bf16[2048,4,2048]{0,2,1:T(8,128)(2,1)} %bitcast.17), calls=%async_computation | async-start | bytes 67108864 | tf_op jit(solution)/shard_map/all_to_all | solution.py:39
  61.5 44.3 %all-gather.3.cloned.1.call-start = ((), (), s32[]{:S(2)}) async-start(), calls=%async_computation.1 | async-start | bytes 3932160 | tf_op jit(solution)/shard_map/all_gather | solution.py:40
  62.3 959.1 %all-gather.5.cloned.1.call-start = ((), (), s32[]{:S(2)}) async-start(), calls=%async_computation.2 | async-start | bytes 13107200 | tf_op jit(solution)/shard_map/all_gather | solution.py:44
  105.8 1011.5 %all-reduce.6.cloned.1.call-start = ((), (), s32[]{:S(2)}) async-start(), calls=%async_computation.4 | async-start | bytes 2621440 | tf_op jit(solution)/shard_map/psum | solution.py:52
  110.3 1015.6 %all-reduce.4.cloned.1.call-start = ((), (), s32[]{:S(2)}) async-start(), calls=%async_computation.3 | async-start | bytes 10485760 | tf_op jit(solution)/shard_map/psum | solution.py:51
  1050.2 0.7 copy-start.3
  1050.2 0.8 copy-start.2
  1153.6 12.1 %copy-start.1 = (bf16[2048,512]{1,0:T(8,128)(2,1)S(1)}, bf16[2048,512]{1,0:T(8,128)(2,1)}, u32[]{:S(2)}) copy-start(bf16[2048,512]{1,0:T(8,128)(2,1)} %param.10) | copy-start | bytes 6291460
Sparse Core Ops, SparseCore 0:
  63.9 41.8 all-gather.2
  107.4 393.1 all-gather.4
  503.0 330.6 all-reduce.5
  1050.4 29.2 all-reduce.3
where the time goes:
time: 1170 us
  waiting for transfers between devices  913 us (78%)
  local copies, waits for them, and re-layouts  119 us (10%)
  blocking collectives  57.3 us (5%)
  matrix products  49.2 us (4%)
  between operations  13.9 us (1%)
    all_to_all x1, waiting for transfers between devices, body(): lax.all_to_all(w_query, 'fsdp', split_axis=1, concat_axis=0, tiled=True)  868 us
    psum x1, blocking collectives, body(): key_sum, value_sum = lax.psum((key_part, value_part), ('fsdp', 'rep'))  57.3 us
    unnamed x9, local copies, waits for them, and re-layouts  45.3 us
    all_gather x1, waiting for transfers between devices, body(): rows_all = lax.all_gather(hidden, 'tp', axis=0, tiled=True)  43.5 us
    all_to_all x1, local copies, waits for them, and re-layouts, body(): lax.all_to_all(w_query, 'fsdp', split_axis=1, concat_axis=0, tiled=True)  42.7 us
    dot_general x1, matrix products, body(): jnp.dot(lax.all_gather(rows_all, 'fsdp', axis=1, tiled=True), regrouped,...  28.9 us
  transfers between devices with their start and end apart: 5, of which 2 were waited for; matrix products, arithmetic and copies ran while one was open for 8% of the time, Pallas kernels for 0%

commit v1 on v0

--- a/solution.py
+++ b/solution.py
@@ -34,21 +34,30 @@
 def body(hidden, w_query, w_key, w_value, canary_rows, positions):
     shards = lax.axis_size("fsdp")
     findex = lax.axis_index("fsdp")
-    head_cols = w_query.shape[1] // shards
+    cols = w_query.shape[1]
+    head_cols = cols // shards
     kv_cols = w_key.shape[1]
-    regrouped = lax.all_to_all(w_query, "fsdp", split_axis=1, concat_axis=0, tiled=True)
     rows_all = lax.all_gather(hidden, "tp", axis=0, tiled=True)
+    rows = rows_all.shape[0]
     key_part = jnp.dot(rows_all, w_key, preferred_element_type=jnp.float32)
     value_part = jnp.dot(rows_all, w_value, preferred_element_type=jnp.float32)
-    query_part = jnp.dot(
-        lax.all_gather(rows_all, "fsdp", axis=1, tiled=True),
-        regrouped,
-        preferred_element_type=jnp.float32,
-    )
-    rows = query_part.shape[0]
+    query_part = jnp.dot(rows_all, w_query, preferred_element_type=jnp.float32)
+    rep = lax.axis_size("rep")
+    rindex = lax.axis_index("rep")
+    own = rows // rep
+    query_bf = query_part.astype(jnp.bfloat16).reshape(rep, own, cols)
+    mine = lax.dynamic_index_in_dim(query_bf, rindex, 0, keepdims=False).astype(jnp.float32)
+    for step in range(1, rep):
+        give = lax.dynamic_index_in_dim(query_bf, (rindex + step) % rep, 0, keepdims=False)
+        got = lax.ppermute(give, "rep", [(i, (i + step) % rep) for i in range(rep)])
+        mine = mine + got.astype(jnp.float32)
+    pieces = mine.astype(jnp.bfloat16).reshape(own, shards, head_cols)
+    pieces = pieces.transpose(1, 0, 2)
+    landed = lax.all_to_all(pieces, "fsdp", split_axis=0, concat_axis=0, tiled=True)
+    query_own = jnp.sum(landed.astype(jnp.float32), axis=0).astype(jnp.bfloat16)
+    query_sum = lax.all_gather(query_own, "rep", axis=0, tiled=True).astype(jnp.float32)
     heads_here = head_cols // DH
     cosine, sine = rope_tables(positions, DH)
-    query_sum = lax.psum(query_part, "rep")
     key_sum, value_sum = lax.psum((key_part, value_part), ("fsdp", "rep"))
     key_sel = jnp.take(key_sum, canary_rows, axis=0).reshape(rows, kv_cols // DH, DH)
     values = jnp.take(value_sum, canary_rows, axis=0).astype(jnp.bfloat16)

time: 1170 us -> 391 us (0.33)
  waiting for transfers between devices: 913 us -> 183 us
  local copies, waits for them, and re-layouts: 119 us -> 54.7 us
  other arithmetic: 9.84 us -> 29 us
    all_to_all x1, waiting for transfers between devices: 868 us -> 130 us  [body(): lax.all_to_all(pieces, 'fsdp', split_axis=0, concat_axis=0, tiled=True)]
    all_to_all x1 -> x0, local copies, waits for them, and re-layouts: 42.7 us -> none  [body(): lax.all_to_all(w_query, 'fsdp', split_axis=1, concat_axis=0, tiled=True)]
    unnamed x9 -> x14, local copies, waits for them, and re-layouts: 45.3 us -> 2.7 us
    convert_element_type x0 -> x2, other arithmetic: none -> 13.3 us  [the longest x1 8.53 us: body(): pieces = mine.astype(jnp.bfloat16).reshape(own, shards, head_cols)]
  transfers between devices with their start and end apart: 5 -> 5, of which waited for: 2 -> 3; matrix products, arithmetic and copies ran while one was open for 8% -> 7% of each run, Pallas kernels for 0% -> 0%
where the time goes in v1:
time: 391 us; the launch traced here: 390 us
  waiting for transfers between devices  183 us (47%)
  blocking collectives  57.2 us (15%)
  local copies, waits for them, and re-layouts  54.7 us (14%)
  matrix products  46.8 us (12%)
  other arithmetic  29 us (7%)
  between operations  14 us (4%)
  starting transfers between devices  5.49 us (1%)
    all_to_all x1, waiting for transfers between devices, body(): lax.all_to_all(pieces, 'fsdp', split_axis=0, concat_axis=0, tiled=True)  130 us
    psum x1, blocking collectives, body(): key_sum, value_sum = lax.psum((key_part, value_part), ('fsdp', 'rep'))  57.2 us
    all_gather x1, waiting for transfers between devices, body(): rows_all = lax.all_gather(hidden, 'tp', axis=0, tiled=True)  43.4 us
    dot_general x1, matrix products, body(): query_part = jnp.dot(rows_all, w_query, preferred_element_type=jnp.float32)  26.5 us
    gather x3, local copies, waits for them, and re-layouts, body(): jnp.take(query_sum, canary_rows, axis=0).reshape(rows, heads_here, DH)  21.1 us
    dot_general x1, matrix products, body(): jnp.einsum('ihd,jhd->hij', query_rot, key_heads, preferred_element_type=j...  12.1 us
    reshape x1, local copies, waits for them, and re-layouts, body(): pieces = mine.astype(jnp.bfloat16).reshape(own, shards, head_cols)  9.48 us
    ppermute x1, waiting for transfers between devices, body(): got = lax.ppermute(give, 'rep', [(i, (i + step) % rep) for i in range(rep)])  9 us
  transfers between devices with their start and end apart: 5, of which 3 were waited for; matrix products, arithmetic and copies ran while one was open for 7% of the time, Pallas kernels for 0%

profile of v1, /device:TPU:0, one launch (start us, length us, event | category | flops | bytes accessed | tf_op | source)
XLA Modules:
  0.0 390.3 jit_solution(4194778562845569470)
XLA Ops:
  7.2 0.0 copy-start
  7.2 0.0 all-gather.3.cloned.1.call-start
  7.2 0.7 all-gather.3.cloned.1.call-update
  7.9 43.4 %all-gather.3.cloned.1.call-done = bf16[640,2048]{1,0:T(8,128)(2,1)} async-done(((bf16[320,2048]{1,0:T(8,128)(2,1)}), bf16[640,2048]{1,0:T(8,128)(2,1)}) %all-gather.3.cloned.1.call-update) | async-done | bytes 2621456 | tf_op jit(solution)/shard_map/all_gather | solution.py:40
  51.3 26.5 %convolution_convert_fusion = bf16[640,8192]{1,0:T(8,128)(2,1)S(1)} fusion(bf16[640,2048]{1,0:T(8,128)(2,1)} %all-gather.3.cloned.1.call-done, bf16[2048,8192]{1,0:T(8,128)(2,1)} %param.9), kind=kOutput, calls=%fused_computation.6 | convolution fusion | flops 21480079360 | bytes 46661632 | tf_op jit(solution)/shard_map/dot_general | solution.py:44
  77.8 0.0 copy-start.2
  77.8 3.3 dynamic-slice_bitcast_fusion
  81.1 2.4 copy-done.2
  83.5 0.0 collective-permute-start
  83.5 9.0 %collective-permute-done = bf16[320,8192]{1,0:T(8,128)(2,1)} collective-permute-done((bf16[320,8192]{1,0:T(8,128)(2,1)}, bf16[320,8192]{1,0:T(8,128)(2,1)}, u32[]{:S(2)}, u32[]{:S(2)}) %collective-permute-start) | collective-permute-done | bytes 5242912 | tf_op jit(solution)/shard_map/ppermute | solution.py:52
  92.5 8.5 %fusion.1 = bf16[320,8192]{1,0:T(8,128)(2,1)} fusion(bf16[320,8192]{1,0:T(8,128)(2,1)} %collective-permute-done, bf16[2,320,8192]{2,1,0:T(8,128)(2,1)} %bitcast.24, s32[]{:T(128)S(6)} %select_n.81), kind=kLoop, calls=%fused_computation.8 | loop fusion | flops 10485760 | bytes 15728644 | tf_op jit(solution)/shard_map/convert_element_type | solution.py:54
  101.0 9.5 %reshape.168 = bf16[320,4,2048]{2,1,0:T(4,128)(2,1)} reshape(bf16[320,8192]{1,0:T(8,128)(2,1)} %fusion.1) | data formatting | bytes 10485760 | tf_op jit(solution)/shard_map/reshape | solution.py:54
  110.5 7.7 %copy.16 = bf16[4,320,2048]{2,1,0:T(8,128)(2,1)} copy(bf16[4,320,2048]{2,0,1:T(4,128)(2,1)} %bitcast.21) | data formatting | bytes 10485760 | tf_op jit(solution)/shard_map/transpose | solution.py:55
  118.2 5.2 %all-to-all-start = ((bf16[4,320,2048]{2,1,0:T(8,128)(2,1)}), bf16[4,320,2048]{2,1,0:T(8,128)(2,1)}, u32[]{:S(2)}, u32[]{:S(2)}) async-start(bf16[4,320,2048]{2,1,0:T(8,128)(2,1)} %copy.16), calls=%async_computation | async-start | bytes 10485760 | tf_op jit(solution)/shard_map/all_to_all | solution.py:56
  123.4 0.0 all-reduce.3.cloned.1.call-start
  123.4 0.0 copy-done.6
  123.5 0.0 copy-done.5
  123.6 2.1 multiply_cosine_fusion
  125.7 0.0 copy-done
  125.7 4.3 %fusion.13 = f32[640,512]{1,0:T(8,128)} fusion(bf16[640,2048]{1,0:T(8,128)(2,1)} %all-gather.3.cloned.1.call-done, bf16[2048,512]{1,0:T(8,128)(2,1)S(1)} %copy-done), kind=kOutput, calls=%fused_computation.48 | convolution fusion | flops 1342177280 | bytes 6029312 | tf_op jit(solution)/shard_map/dot_general | solution.py:42
  130.0 0.0 all-reduce.3.cloned.1.call-update
  130.0 0.2 all-gather.5.cloned.1.call-start
  130.3 3.9 fusion.14
  134.2 130.1 %all-to-all-done = bf16[4,320,2048]{2,1,0:T(8,128)(2,1)} async-done(((bf16[4,320,2048]{2,1,0:T(8,128)(2,1)}), bf16[4,320,2048]{2,1,0:T(8,128)(2,1)}, u32[]{:S(2)}, u32[]{:S(2)}) %all-to-all-start) | async-done | bytes 5242912 | tf_op jit(solution)/shard_map/all_to_all | solution.py:56
  264.2 4.9 %reduce_sum.12 = bf16[320,2048]{1,0:T(8,128)(2,1)} reduce(bf16[4,320,2048]{2,1,0:T(8,128)(2,1)} %all-to-all-done, bf16[]{:T(256)} %constant.89.clone.1), dimensions={0}, to_apply=%region_0.1 | reduce | flops 1966080 | bytes 6553602 | tf_op jit(solution)/shard_map/reduce_sum | solution.py:57
  269.2 0.0 all-gather.5.cloned.1.call-update
  269.2 57.2 %all-reduce.4 = bf16[640,512]{1,0:T(8,128)(2,1)S(1)} all-reduce(f32[640,512]{1,0:T(8,128)S(1)} %fusion.14), channel_id=1, replica_groups=mesh['groups'=2,'fsdp'=4,'tp'=2,'rep'=2] {'fsdp','rep'}, use_global_device_ids=true, to_apply=%region_2.4 | all-reduce | flops 327680 | bytes 1966080 | tf_op jit(solution)/shard_map/psum | solution.py:61
  326.4 2.8 gather_fusion.3
  329.2 1.1 select_convert_fusion
  330.2 4.1 %gather_fusion.2 = f32[640,512]{1,0:T(8,128)S(1)} fusion(f32[640,512]{1,0:T(8,128)} %all-reduce.3.cloned.1.call-done, s32[1024]{0:T(1024)S(1)} %pad_clamp_fusion.1), kind=kCustom, calls=%fused_computation.clone | custom fusion | bytes 2624000 | tf_op jit(solution)/shard_map/jit(_take)/gather | solution.py:62
  334.3 0.2 broadcast_select_fusion.1
  334.5 0.5 reshape.169
  334.9 0.0 copy-start.3
  335.0 0.0 copy-start.4
  335.0 0.7 fusion.12
  335.7 0.2 copy-done.3
  335.9 0.1 copy-done.4
  336.0 0.3 subtract_convert_fusion.1
  336.4 0.4 pad_maximum_fusion
  336.7 2.4 gather_fusion.1
  339.1 4.8 %convert_element_type.36 = f32[640,2048]{1,0:T(8,128)} convert(bf16[640,2048]{1,0:T(8,128)(2,1)} %all-gather.5.cloned.1.call-done) | non-fusion elementwise | flops 1310720 | bytes 7864320 | tf_op jit(solution)/shard_map/convert_element_type | solution.py:58
  343.9 9.3 %gather_fusion = f32[640,2048]{1,0:T(8,128)} fusion(f32[640,2048]{1,0:T(8,128)} %convert_element_type.36, s32[1024]{0:T(1024)S(1)} %pad_clamp_fusion.1), kind=kCustom, calls=%fused_computation.2 | custom fusion | bytes 10488320 | tf_op jit(solution)/shard_map/jit(_take)/gather | solution.py:65
  353.2 5.9 %copy.17 = f32[640,2048]{0,1:T(8,128)} copy(f32[640,2048]{1,0:T(8,128)} %gather_fusion) | data formatting | bytes 10485760 | tf_op jit(solution)/shard_map/jit(_take)/gather | solution.py:65
  359.1 5.9 %copy.18 = f32[640,16,128]{2,0,1:T(8,128)} copy(f32[640,16,128]{0,2,1:T(8,128)} %bitcast.22) | data formatting | bytes 10485760 | tf_op jit(solution)/shard_map/jit(_take)/gather | solution.py:65
  365.0 3.1 broadcast_select_fusion
  368.2 3.5 subtract_convert_fusion
  371.7 12.1 %fusion = bf16[1,16,640,640]{3,2,1,0:T(8,128)(2,1)} fusion(bf16[640,16,64]{2,0,1:T(8,128)(2,1)} %get-tuple-element.4, bf16[640,16,64]{2,0,1:T(8,128)(2,1)} %get-tuple-element.3, bf16[16,640,128]{2,1,0:T(8,128)(2,1)} %gather_fusion.1, pred[16]{0:T(512)(128)(4,1)S(1)} %compare_and_fusion.1), kind=kOutput, calls=%fused_computation.5 | convolution fusion | flops 1697382400 | bytes 18350096 | tf_op jit(solution)/shard_map/ihd,jhd->hij/dot_general | solution.py:69
  383.7 0.0 copy-done.1
  (13 shorter events, 0.1 us)
Async XLA Ops:
  7.2 118.5 %copy-start = (bf16[2048,512]{1,0:T(8,128)(2,1)S(1)}, bf16[2048,512]{1,0:T(8,128)(2,1)}, u32[]{:S(2)}) copy-start(bf16[2048,512]{1,0:T(8,128)(2,1)} %param.10) | copy-start | bytes 6291460
  7.2 44.1 %all-gather.3.cloned.1.call-start = ((), (), s32[]{:S(2)}) async-start(), calls=%async_computation.1 | async-start | bytes 3932160 | tf_op jit(solution)/shard_map/all_gather | solution.py:40
  77.8 5.7 %copy-start.2 = (bf16[640,8192]{1,0:T(8,128)(2,1)}, bf16[640,8192]{1,0:T(8,128)(2,1)S(1)}, u32[]{:S(2)}) copy-start(bf16[640,8192]{1,0:T(8,128)(2,1)S(1)} %convolution_convert_fusion) | copy-start | bytes 31457284
  83.5 9.0 %collective-permute-start = (bf16[320,8192]{1,0:T(8,128)(2,1)}, bf16[320,8192]{1,0:T(8,128)(2,1)}, u32[]{:S(2)}, u32[]{:S(2)}) collective-permute-start(bf16[320,8192]{1,0:T(8,128)(2,1)} %dynamic-slice_bitcast_fusion), channel_id=1, source_target_pairs={{0,1},{1,0},{2,3},{3,2},{4,5},{5,4},{6,7},{7,6},{8,9},{9,8},{10,11... | collective-permute-start | bytes 15728648 | tf_op jit(solution)/shard_map/ppermute | solution.py:52
  118.2 5.2 %copy-start.6 = (s32[640]{0:T(1024)S(1)}, s32[640]{0:T(1024)}, u32[]{:S(2)}) copy-start(s32[640]{0:T(1024)} %param.13) | copy-start | bytes 7684
  118.2 5.3 %copy-start.5 = (s32[640]{0:T(1024)S(1)}, s32[640]{0:T(1024)}, u32[]{:S(2)}) copy-start(s32[640]{0:T(1024)} %param.12) | copy-start | bytes 7684
  118.2 146.0 %all-to-all-start = ((bf16[4,320,2048]{2,1,0:T(8,128)(2,1)}), bf16[4,320,2048]{2,1,0:T(8,128)(2,1)}, u32[]{:S(2)}, u32[]{:S(2)}) async-start(bf16[4,320,2048]{2,1,0:T(8,128)(2,1)} %copy.16), calls=%async_computation | async-start | bytes 10485760 | tf_op jit(solution)/shard_map/all_to_all | solution.py:56
  123.4 206.8 %all-reduce.3.cloned.1.call-start = ((), (), s32[]{:S(2)}) async-start(), calls=%async_computation.3 | async-start | bytes 2621440 | tf_op jit(solution)/shard_map/psum | solution.py:61
  130.0 209.1 %all-gather.5.cloned.1.call-start = ((), (), s32[]{:S(2)}) async-start(), calls=%async_computation.2 | async-start | bytes 3932160 | tf_op jit(solution)/shard_map/all_gather | solution.py:58
  334.9 1.0 copy-start.3
  335.0 1.1 copy-start.4
  371.7 12.1 %copy-start.1 = (bf16[2048,512]{1,0:T(8,128)(2,1)S(1)}, bf16[2048,512]{1,0:T(8,128)(2,1)}, u32[]{:S(2)}) copy-start(bf16[2048,512]{1,0:T(8,128)(2,1)} %param.10) | copy-start | bytes 6291460
Sparse Core Ops, SparseCore 0:
  9.6 41.7 all-gather.2
  130.1 134.1 all-reduce.2
  269.3 9.5 all-gather.4

commit v2 on v0

v2 whole, which is shorter than its diff:
```python
import functools
import math

import jax
import jax.numpy as jnp
from jax import lax
from jax.experimental import pallas as pl
from jax.experimental.pallas import tpu as pltpu
from jax.sharding import PartitionSpec as P

HQ = 128
KV = 8
DH = 128
VMEM_BYTES = 40 * 1024 * 1024


def rope_tables(positions):
    half = DH // 2
    expo = jnp.arange(half, dtype=jnp.float32) * (2.0 / DH)
    freq = jnp.power(jnp.float32(500000.0), -expo)
    wavelen = 2.0 * math.pi / freq
    smooth = (8192.0 / wavelen - 1.0) / 3.0
    mixed = (1.0 - smooth) * freq / 8.0 + smooth * freq
    freq = jnp.where(wavelen > 8192.0, freq / 8.0, jnp.where(wavelen < 2048.0, freq, mixed))
    angle = positions.astype(jnp.float32)[:, None] * freq[None, :]
    cosine, sine = jnp.cos(angle), jnp.sin(angle)
    return jnp.concatenate([cosine, cosine], axis=1), jnp.concatenate([-sine, sine], axis=1)


def split_rows(place_ref, result, keep_ref, give_ref):
    half = result.shape[0] // 2
    first = place_ref[0] == 0
    top, low = result[:half], result[half:]
    keep_ref[0] = jnp.where(first, top, low).astype(keep_ref.dtype)
    give_ref[0] = jnp.where(first, low, top).astype(give_ref.dtype)


def query_kernel(place_ref, x_ref, w_ref, keep_ref, give_ref):
    result = jnp.dot(x_ref[...], w_ref[...], preferred_element_type=jnp.float32)
    split_rows(place_ref, result, keep_ref, give_ref)


def project_query(rindex, findex, slots, x, w, cols):
    rows, depth = x.shape
    tile = min(512, cols)
    tiles = cols // tile
    place = jnp.stack([rindex] + [findex ^ slot for slot in slots]).astype(jnp.int32)
    out = pl.BlockSpec((1, rows // 2, tile), lambda s, j, place: (s, 0, j))
    shape = (len(slots), rows // 2, cols)
    return pl.pallas_call(
        query_kernel,
        grid_spec=pltpu.PrefetchScalarGridSpec(
            num_scalar_prefetch=1,
            grid=(len(slots), tiles),
            in_specs=[
                pl.BlockSpec((rows, depth), lambda s, j, place: (0, 0)),
                pl.BlockSpec((depth, tile), lambda s, j, place: (0, place[1 + s] * tiles + j)),
            ],
            out_specs=[out, out],
        ),
        out_shape=[
            jax.ShapeDtypeStruct(shape, jnp.float32),
            jax.ShapeDtypeStruct(shape, jnp.bfloat16),
        ],
        compiler_params=pltpu.CompilerParams(vmem_limit_bytes=VMEM_BYTES),
        cost_estimate=pl.CostEstimate(
            flops=2 * rows * depth * cols * len(slots),
            bytes_accessed=2 * depth * cols * len(slots),
            transcendentals=0,
        ),
        name="query_products",
    )(place, x, w)


def pair_kernel(place_ref, x_ref, wk_ref, wv_ref, keep_ref, give_ref):
    weights = jnp.concatenate([wk_ref[...], wv_ref[...]], axis=1)
    result = jnp.dot(x_ref[...], weights, preferred_element_type=jnp.float32)
    split_rows(place_ref, result, keep_ref, give_ref)


def project_pair(rindex, findex, slots, x, w_key, w_value):
    rows, depth = x.shape
    place = jnp.stack([rindex] + [findex ^ slot for slot in slots]).astype(jnp.int32)
    weight = pl.BlockSpec((depth, DH), lambda s, place: (0, place[1 + s]))
    out = pl.BlockSpec((1, rows // 2, 2 * DH), lambda s, place: (s, 0, 0))
    shape = jax.ShapeDtypeStruct((len(slots), rows // 2, 2 * DH), jnp.float32)
    return pl.pallas_call(
        pair_kernel,
        grid_spec=pltpu.PrefetchScalarGridSpec(
            num_scalar_prefetch=1,
            grid=(len(slots),),
            in_specs=[pl.BlockSpec((rows, depth), lambda s, place: (0, 0)), weight, weight],
            out_specs=[out, out],
        ),
        out_shape=[shape, shape],
        compiler_params=pltpu.CompilerParams(vmem_limit_bytes=VMEM_BYTES),
        cost_estimate=pl.CostEstimate(
            flops=4 * rows * depth * DH * len(slots),
            bytes_accessed=4 * depth * DH * len(slots),
            transcendentals=0,
        ),
        name="key_value_products",
    )(place, x, w_key, w_value)


def rotate_kernel(cos_ref, sin_ref, *refs):
    *terms, out_ref = refs
    total = terms[0][...].astype(jnp.float32)
    for term in terms[1:]:
        total = total + term[...].astype(jnp.float32)
    cosine, sine = cos_ref[...], sin_ref[...]
    for head in range(total.shape[1] // DH):
        part = total[:, head * DH : (head + 1) * DH]
        turned = pltpu.roll(part, DH // 2, axis=1)
        out_ref[:, head * DH : (head + 1) * DH] = (part * cosine + turned * sine).astype(out_ref.dtype)


def sum_and_rotate(cosine, sine, terms):
    rows, cols = terms[0].shape
    tile = min(512, cols)
    table = pl.BlockSpec((rows, DH), lambda j: (0, 0))
    block = pl.BlockSpec((rows, tile), lambda j: (0, j))
    return pl.pallas_call(
        rotate_kernel,
        grid=(cols // tile,),
        in_specs=[table, table] + [block] * len(terms),
        out_specs=block,
        out_shape=jax.ShapeDtypeStruct((rows, cols), jnp.bfloat16),
        compiler_params=pltpu.CompilerParams(vmem_limit_bytes=VMEM_BYTES),
        cost_estimate=pl.CostEstimate(
            flops=8 * rows * cols, bytes_accessed=12 * rows * cols, transcendentals=0
        ),
        name="sum_and_rotate",
    )(cosine, sine, *terms)


def score_kernel(canary_ref, ids_ref, key_ref, *refs):
    *queries, out_ref, order_ref, key_t_ref = refs

    @pl.when(pl.program_id(0) == 0)
    def _():
        order = jnp.where(canary_ref[...] == ids_ref[...], 1.0, 0.0).astype(jnp.bfloat16)
        order_ref[...] = order
        keys = jnp.dot(order, key_ref[...], preferred_element_type=jnp.float32)
        key_t_ref[...] = keys.T.astype(jnp.bfloat16)

    stacked = jnp.concatenate([query[...] for query in queries], axis=0)
    chosen = jnp.dot(order_ref[...], stacked, preferred_element_type=jnp.float32).astype(jnp.bfloat16)
    for head in range(stacked.shape[1] // DH):
        products = jnp.dot(
            chosen[:, head * DH : (head + 1) * DH], key_t_ref[...], preferred_element_type=jnp.float32
        )
        out_ref[0, head] = (products * DH ** (-0.5)).astype(out_ref.dtype)


def score_heads(canary_rows, ids, key, queries):
    rows = key.shape[0]
    part, cols = queries[0].shape
    heads = cols // DH
    step = 2 if heads % 2 == 0 else 1
    return pl.pallas_call(
        score_kernel,
        grid=(heads // step,),
        in_specs=[
            pl.BlockSpec((rows, 1), lambda j: (0, 0)),
            pl.BlockSpec((1, rows), lambda j: (0, 0)),
            pl.BlockSpec((rows, DH), lambda j: (0, 0)),
        ]
        + [pl.BlockSpec((part, step * DH), lambda j: (0, j))] * len(queries),
        out_specs=pl.BlockSpec((1, step, rows, rows), lambda j: (0, j, 0, 0)),
        out_shape=jax.ShapeDtypeStruct((1, heads, rows, rows), jnp.bfloat16),
        scratch_shapes=[pltpu.VMEM((rows, rows), jnp.bfloat16), pltpu.VMEM((DH, rows), jnp.bfloat16)],
        compiler_params=pltpu.CompilerParams(vmem_limit_bytes=VMEM_BYTES),
        cost_estimate=pl.CostEstimate(
            flops=4 * rows * rows * cols, bytes_accessed=2 * rows * rows * heads, transcendentals=0
        ),
        name="score_heads",
    )(canary_rows.reshape(rows, 1), ids.reshape(1, rows), key, *queries)


def body(hidden, w_query, w_key, w_value, canary_rows, positions):
    shards = lax.axis_size("fsdp")
    findex = lax.axis_index("fsdp")
    tps = lax.axis_size("tp")
    tindex = lax.axis_index("tp")
    rindex = lax.axis_index("rep")
    local, depth = hidden.shape
    half = local // 2
    rows = local * tps
    head_cols = w_query.shape[1] // shards
    heads_here = head_cols // DH
    group = HQ // KV
    assert shards & (shards - 1) == 0 and lax.axis_size("rep") == 2

    def swap(x, bit):
        return lax.ppermute(x, "fsdp", [(i, i ^ bit) for i in range(shards)])

    def other_core(x):
        return lax.ppermute(x, "rep", [(0, 1), (1, 0)])

    def low(x):
        return x.astype(jnp.bfloat16)

    far = [x for x in range(3, shards, 2)]
    even = [x for x in range(0, shards, 2)]

    def finish(own_terms, live):
        terms = list(own_terms)
        bit = 2
        while bit < shards:
            sent = [x for x in sorted(live) if x & bit]
            landed = swap(jnp.stack([low(live[x]) for x in sent]), bit)
            for k, x in enumerate(sent):
                if x == bit:
                    terms.append(landed[k])
                else:
                    live[x ^ bit] = live[x ^ bit] + landed[k].astype(jnp.float32)
                del live[x]
            bit *= 2
        return terms

    blocks = [hidden] + [
        lax.ppermute(hidden, "tp", [(i, (i - b) % tps) for i in range(tps)]) for b in range(1, tps)
    ]

    block_ids = ((tindex + jnp.arange(tps, dtype=jnp.int32)) % tps * local)[:, None]
    own_ids = (block_ids + rindex * half + jnp.arange(half, dtype=jnp.int32)[None]).reshape(-1)
    other_ids = (block_ids + (1 - rindex) * half + jnp.arange(half, dtype=jnp.int32)[None]).reshape(-1)
    ids = jnp.concatenate([own_ids, other_ids])
    own_positions = jnp.sum(
        jnp.where(own_ids[:, None] == canary_rows[None, :], positions[None, :], 0), axis=1
    )
    cosine, sine = rope_tables(own_positions)

    queries = []
    for b, block in enumerate(blocks):
        far_keep, far_give = project_query(rindex, findex, far, block, w_query, head_cols)
        far_got = other_core(far_give)
        near_keep, near_give = project_query(rindex, findex, [1], block, w_query, head_cols)
        far_landed = swap(low(far_keep + far_got.astype(jnp.float32)), 1)
        near_got = other_core(near_give)
        even_keep, even_give = project_query(rindex, findex, even[1:] + [0], block, w_query, head_cols)
        near_landed = swap(low(near_keep + near_got.astype(jnp.float32)), 1)
        even_got = other_core(even_give)
        live = {
            x: even_keep[k] + even_got[k].astype(jnp.float32) + far_landed[k].astype(jnp.float32)
            for k, x in enumerate(even[1:])
        }
        terms = finish([even_keep[-1], even_got[-1], near_landed[0]], live)
        table = slice(b * half, (b + 1) * half)
        queries.append(sum_and_rotate(cosine[table], sine[table], terms))

    if heads_here == group:
        kept, got = [], []
        for block in blocks:
            keep, give = project_pair(rindex, findex, list(range(shards)), block, w_key, w_value)
            kept.append(keep)
            got.append(other_core(give))
        pair = jnp.concatenate([k + g for k, g in zip(kept, got)], axis=1)
        odd_landed = swap(low(pair[1::2]), 1).astype(jnp.float32)
        live = {x: pair[x] + odd_landed[x // 2] for x in even}
        own = live.pop(0)
        for term in finish([], live):
            own = own + term.astype(jnp.float32)
        key_own, value_own = own[:, :DH], low(own[:, DH:])
        value_both = jnp.concatenate([value_own, other_core(value_own)], axis=0)
        value_rows = lax.all_gather(value_both, "fsdp", axis=1, tiled=True)
    else:
        x = jnp.concatenate(blocks, axis=0)
        key_sum, value_sum = lax.psum(
            (
                jnp.dot(x, w_key, preferred_element_type=jnp.float32),
                jnp.dot(x, w_value, preferred_element_type=jnp.float32),
            ),
            ("fsdp", "rep"),
        )

        def of_core(y, core):
            parts = y.reshape(tps, 2, half, -1)
            return lax.dynamic_index_in_dim(parts, core, 1, keepdims=False).reshape(tps * half, -1)

        mine = lax.dynamic_slice_in_dim(key_sum, findex * heads_here // group * DH, DH, 1)
        key_own = of_core(mine, rindex)
        value_rows = low(jnp.concatenate([of_core(value_sum, rindex), of_core(value_sum, 1 - rindex)]))

    key_rot = sum_and_rotate(cosine, sine, [key_own])
    key_both = jnp.concatenate([key_rot, other_core(key_rot)], axis=0)
    order = (canary_rows[:, None] == ids[None, :]).astype(jnp.bfloat16)
    values = low(jnp.dot(order, value_rows, preferred_element_type=jnp.float32))
    scores = score_heads(canary_rows, ids, key_both, queries + [other_core(q) for q in queries])
    return (scores, values)


def solution(mesh):
    in_specs = (
        P(("groups", "tp"), ("fsdp", "rep")),
        P(("fsdp", "rep"), "tp"),
        P(("fsdp", "rep"), "tp"),
        P(("fsdp", "rep"), "tp"),
        P("groups"),
        P("groups"),
    )
    out_specs = (P("tp", "fsdp", "groups", None), P("groups", "tp"))
    return jax.shard_map(body, mesh=mesh, in_specs=in_specs, out_specs=out_specs, check_vma=False)
```

time: 1170 us -> 198 us (0.17)
  waiting for transfers between devices: 913 us -> 65 us
  local copies, waits for them, and re-layouts: 119 us -> 9.87 us
  Pallas kernels: 0 us -> 75 us
  matrix products: 49.2 us -> 1.56 us
  blocking collectives: 57.3 us -> 16.6 us
  between operations: 13.9 us -> 1.05 us
    all_to_all x1 -> x0, waiting for transfers between devices: 868 us -> none  [body(): lax.all_to_all(w_query, 'fsdp', split_axis=1, concat_axis=0, tiled=True)]
    pallas_call x0 -> x12, Pallas kernels: none -> 75 us  [the longest x6 52.7 us: project_query(): pl.pallas_call(query_kernel, grid_spec=pltpu.PrefetchScalarGridSpec(num_s...]
    ppermute x0 -> x21, waiting for transfers between devices: none -> 65 us  [the longest x8 64.9 us: swap(): return lax.ppermute(x, 'fsdp', [(i, i ^ bit) for i in range(shards)])]
    psum x1 -> x0, blocking collectives: 57.3 us -> none  [body(): key_sum, value_sum = lax.psum((key_part, value_part), ('fsdp', 'rep'))]
    dot_general x4 -> x1, matrix products: 49.2 us -> 1.56 us  [body(): values = low(jnp.dot(order, value_rows, preferred_element_type=jnp.float32))]
    all_gather x2 -> x0, waiting for transfers between devices: 43.5 us -> none  [the longest x1 43.5 us: body(): rows_all = lax.all_gather(hidden, 'tp', axis=0, tiled=True)]
    all_to_all x1 -> x0, local copies, waits for them, and re-layouts: 42.7 us -> none  [body(): lax.all_to_all(w_query, 'fsdp', split_axis=1, concat_axis=0, tiled=True)]
    unnamed x9 -> x36, local copies, waits for them, and re-layouts: 45.3 us -> 8.24 us
  transfers between devices with their start and end apart: 5 -> 21, of which waited for: 2 -> 5; matrix products, arithmetic and copies ran while one was open for 8% -> 7% of each run, Pallas kernels for 0% -> 32%
where the time goes in v2:
time: 198 us; the launch traced here: 197 us
  Pallas kernels  75 us (38%)
  waiting for transfers between devices  65 us (33%)
  starting transfers between devices  17.3 us (9%)
  blocking collectives  16.6 us (8%)
  other arithmetic  10.4 us (5%)
  local copies, waits for them, and re-layouts  9.87 us (5%)
    ppermute x8, waiting for transfers between devices, swap(): return lax.ppermute(x, 'fsdp', [(i, i ^ bit) for i in range(shards)])  64.9 us
    pallas_call x6, Pallas kernels, project_query(): pl.pallas_call(query_kernel, grid_spec=pltpu.PrefetchScalarGridSpec(num_s...  52.7 us
    all_gather x1, blocking collectives, body(): value_rows = lax.all_gather(value_both, 'fsdp', axis=1, tiled=True)  16.6 us
    pallas_call x1, Pallas kernels, score_heads(): pl.pallas_call(score_kernel, grid=(heads // step,), in_specs=[pl.BlockSpe...  12.6 us
    ppermute x8, starting transfers between devices, swap(): return lax.ppermute(x, 'fsdp', [(i, i ^ bit) for i in range(shards)])  11.7 us
    unnamed x36, local copies, waits for them, and re-layouts  8.24 us
    pallas_call x2, Pallas kernels, project_pair(): pl.pallas_call(pair_kernel, grid_spec=pltpu.PrefetchScalarGridSpec(num_sc...  7.52 us
    convert_element_type x7, other arithmetic, low(): return x.astype(jnp.bfloat16)  4.88 us
  transfers between devices with their start and end apart: 21, of which 5 were waited for; matrix products, arithmetic and copies ran while one was open for 7% of the time, Pallas kernels for 32%

profile of v2, /device:TPU:0, one launch (start us, length us, event | category | flops | bytes accessed | tf_op | source)
XLA Modules:
  0.0 196.8 jit_solution(6328708636933870162)
XLA Ops:
  0.6 3.0 %collective-permute-start.1 = (bf16[320,2048]{1,0:T(8,128)(2,1)}, bf16[320,2048]{1,0:T(8,128)(2,1)S(1)}, u32[]{:S(2)}, u32[]{:S(2)}) collective-permute-start(bf16[320,2048]{1,0:T(8,128)(2,1)} %x_ref.7), channel_id=1, source_target_pairs={{0,2},{2,0},{1,3},{3,1},{4,6},{6,4},{5,7},{7,5},{8,10},{10,8},{9,1... | collective-permute-start | bytes 3932168 | tf_op jit(solution)/shard_map/ppermute | solution.py:223
  3.7 1.3 copy-done
  5.0 7.3 %query_products.8 = (f32[1,160,2048]{2,1,0:T(8,128)S(1)}, bf16[1,160,2048]{2,1,0:T(8,128)(2,1)}) custom-call(s32[2]{0:T(128)S(1)} %get-tuple-element.48.place_ref, bf16[320,2048]{1,0:T(8,128)(2,1)S(1)} %copy-done, bf16[2048,8192]{1,0:T(8,128)(2,1)} %w_ref.11), custom_call_target="tpu_custom_call" | custom-call | flops 2684354560 | bytes 8388608 | tf_op jit(solution)/shard_map/query_products/pallas_call | solution.py:50
  12.3 1.1 copy-done.8
  13.5 12.7 %query_products.6 = (f32[2,160,2048]{2,1,0:T(8,128)S(1)}, bf16[2,160,2048]{2,1,0:T(8,128)(2,1)}) custom-call(s32[3]{0:T(128)S(1)} %pad_add_fusion.1.place_ref, bf16[320,2048]{1,0:T(8,128)(2,1)S(1)} %copy-done.1, bf16[2048,8192]{1,0:T(8,128)(2,1)} %w_ref.11), custom_call_target="tpu_custom_call" | custom-call | flops 5368709120 | bytes 16777216 | tf_op jit(solution)/shard_map/query_products/pallas_call | solution.py:50
  26.1 1.5 copy-done.6
  27.6 0.5 collective-permute-start.6
  28.1 7.3 %query_products.7 = (f32[1,160,2048]{2,1,0:T(8,128)S(1)}, bf16[1,160,2048]{2,1,0:T(8,128)(2,1)}) custom-call(s32[2]{0:T(128)S(1)} %get-tuple-element.47.place_ref, bf16[320,2048]{1,0:T(8,128)(2,1)S(1)} %copy-done.1, bf16[2048,8192]{1,0:T(8,128)(2,1)} %w_ref.11), custom_call_target="tpu_custom_call" | custom-call | flops 2684354560 | bytes 8388608 | tf_op jit(solution)/shard_map/query_products/pallas_call | solution.py:50
  35.4 1.1 copy-done.10
  36.6 1.6 copy-done.2
  38.2 1.6 copy-done.4
  39.8 4.1 %key_value_products.2 = (f32[4,160,256]{2,1,0:T(8,128)S(1)}, f32[4,160,256]{2,1,0:T(8,128)}) custom-call(s32[5]{0:T(128)S(1)} %stack.23.place_ref, bf16[320,2048]{1,0:T(8,128)(2,1)S(1)} %copy-done.1, bf16[2048,512]{1,0:T(8,128)(2,1)S(1)} %copy-done.2, bf16[2048,512]{1,0:T(8,128)(2,1)S(1)} %copy-done.4), custom_call_target="tpu_custom_call" | custom-call | flops 1342177280 | bytes 4194304 | tf_op jit(solution)/shard_map/key_value_products/pallas_call | solution.py:87
  43.9 0.5 collective-permute-start
  44.6 0.2 select_reduce_fusion
  44.8 0.7 fusion.19
  45.5 0.8 fusion.16
  46.5 0.7 fusion.18
  47.5 1.1 pad_maximum_fusion.3.cos_ref
  48.7 1.4 add_convert_fusion.4
  50.0 1.6 collective-permute-start.10
  51.7 1.3 add_convert_fusion.5
  53.0 0.5 collective-permute-start.8
  53.5 1.2 add.162
  54.7 6.6 %query_products.11 = (f32[1,160,2048]{2,1,0:T(8,128)S(1)}, bf16[1,160,2048]{2,1,0:T(8,128)(2,1)S(1)}) custom-call(s32[2]{0:T(128)S(1)} %get-tuple-element.48.place_ref, bf16[320,2048]{1,0:T(8,128)(2,1)S(1)} %collective-permute-done.1.x_ref, bf16[2048,8192]{1,0:T(8,128)(2,1)} %w_ref.11), custom_call_target="tpu_custom_call" | custom-call | flops 2684354560 | bytes 8388608 | tf_op jit(solution)/shard_map/query_products/pallas_call | solution.py:50
  61.3 12.2 %query_products.9 = (f32[2,160,2048]{2,1,0:T(8,128)S(1)}, bf16[2,160,2048]{2,1,0:T(8,128)(2,1)S(1)}) custom-call(s32[3]{0:T(128)S(1)} %pad_add_fusion.1.place_ref, bf16[320,2048]{1,0:T(8,128)(2,1)S(1)} %collective-permute-done.1.x_ref, bf16[2048,8192]{1,0:T(8,128)(2,1)} %w_ref.11), custom_call_target="tpu_custom_call" | custom-call | flops 5368709120 | bytes 16777216 | tf_op jit(solution)/shard_map/query_products/pallas_call | solution.py:50
  73.8 3.4 %key_value_products.3 = (f32[4,160,256]{2,1,0:T(8,128)S(1)}, f32[4,160,256]{2,1,0:T(8,128)S(1)}) custom-call(s32[5]{0:T(128)S(1)} %stack.23.place_ref, bf16[320,2048]{1,0:T(8,128)(2,1)S(1)} %collective-permute-done.1.x_ref, bf16[2048,512]{1,0:T(8,128)(2,1)S(1)} %copy-done.3, bf16[2048,512]{1,0:T(8,128)(2,1)S(1)} %copy-done.5), custom_call_target="tpu_custom_call" | custom-call | flops 1342177280 | bytes 4194304 | tf_op jit(solution)/shard_map/key_value_products/pallas_call | solution.py:87
  77.2 6.8 %query_products.10 = (f32[1,160,2048]{2,1,0:T(8,128)S(1)}, bf16[1,160,2048]{2,1,0:T(8,128)(2,1)S(1)}) custom-call(s32[2]{0:T(128)S(1)} %get-tuple-element.47.place_ref, bf16[320,2048]{1,0:T(8,128)(2,1)S(1)} %collective-permute-done.1.x_ref, bf16[2048,8192]{1,0:T(8,128)(2,1)} %w_ref.11), custom_call_target="tpu_custom_call" | custom-call | flops 2684354560 | bytes 8388608 | tf_op jit(solution)/shard_map/query_products/pallas_call | solution.py:50
  84.0 0.4 collective-permute-start.13
  84.6 1.5 add_convert_fusion.3
  86.1 1.1 slice_bitcast_fusion.3.refs_1_
  87.3 2.7 %collective-permute-start.11 = (bf16[1,160,2048]{2,1,0:T(8,128)(2,1)S(1)}, bf16[1,160,2048]{2,1,0:T(8,128)(2,1)S(1)}, u32[]{:S(2)}, u32[]{:S(2)}) collective-permute-start(bf16[1,160,2048]{2,1,0:T(8,128)(2,1)S(1)} %get-tuple-element.36), channel_id=1, source_target_pairs={{0,8},{4,12},{8,0},{12,4},{1,9},{5,13},{9,1},{13,5},{2,10},{6,14},... | collective-permute-start | bytes 1966088 | tf_op jit(solution)/shard_map/ppermute | solution.py:196
  90.1 1.6 collective-permute-start.16
  91.9 0.5 collective-permute-start.3
  92.6 1.6 collective-permute-start.14
  94.3 25.1 %collective-permute-done.11 = bf16[1,160,2048]{2,1,0:T(8,128)(2,1)S(1)} collective-permute-done((bf16[1,160,2048]{2,1,0:T(8,128)(2,1)S(1)}, bf16[1,160,2048]{2,1,0:T(8,128)(2,1)S(1)}, u32[]{:S(2)}, u32[]{:S(2)}) %collective-permute-start.11) | collective-permute-done | bytes 655392 | tf_op jit(solution)/shard_map/ppermute | solution.py:196
  119.4 1.0 sum_and_rotate.4.refs_0_
  120.4 7.3 %collective-permute-done.3 = bf16[2,320,256]{2,1,0:T(8,128)(2,1)S(1)} collective-permute-done((bf16[2,320,256]{2,1,0:T(8,128)(2,1)S(1)}, bf16[2,320,256]{2,1,0:T(8,128)(2,1)S(1)}, u32[]{:S(2)}, u32[]{:S(2)}) %collective-permute-start.3) | collective-permute-done | bytes 327712 | tf_op jit(solution)/shard_map/ppermute | solution.py:196
  127.8 0.9 collective-permute-start.4
  128.6 0.4 add_convert_fusion
  129.1 2.2 %collective-permute-start.17 = (bf16[1,160,2048]{2,1,0:T(8,128)(2,1)S(1)}, bf16[1,160,2048]{2,1,0:T(8,128)(2,1)S(1)}, u32[]{:S(2)}, u32[]{:S(2)}) collective-permute-start(bf16[1,160,2048]{2,1,0:T(8,128)(2,1)S(1)} %get-tuple-element.34), channel_id=1, source_target_pairs={{0,8},{4,12},{8,0},{12,4},{1,9},{5,13},{9,1},{13,5},{2,10},{6,14},... | collective-permute-start | bytes 1966088 | tf_op jit(solution)/shard_map/ppermute | solution.py:196
  131.3 12.4 %collective-permute-done.4 = bf16[1,320,256]{2,1,0:T(8,128)(2,1)S(1)} collective-permute-done((bf16[1,320,256]{2,1,0:T(8,128)(2,1)S(1)}, bf16[1,320,256]{2,1,0:T(8,128)(2,1)S(1)}, u32[]{:S(2)}, u32[]{:S(2)}) %collective-permute-start.4) | collective-permute-done | bytes 163872 | tf_op jit(solution)/shard_map/ppermute | solution.py:196
  144.0 0.6 collective-permute-start.5
  144.7 7.9 %collective-permute-done.14 = bf16[1,160,2048]{2,1,0:T(8,128)(2,1)S(1)} collective-permute-done((bf16[1,160,2048]{2,1,0:T(8,128)(2,1)S(1)}, bf16[1,160,2048]{2,1,0:T(8,128)(2,1)S(1)}, u32[]{:S(2)}, u32[]{:S(2)}) %collective-permute-start.14) | collective-permute-done | bytes 655392 | tf_op jit(solution)/shard_map/ppermute | solution.py:196
  152.6 12.2 %collective-permute-done.17 = bf16[1,160,2048]{2,1,0:T(8,128)(2,1)S(1)} collective-permute-done((bf16[1,160,2048]{2,1,0:T(8,128)(2,1)S(1)}, bf16[1,160,2048]{2,1,0:T(8,128)(2,1)S(1)}, u32[]{:S(2)}, u32[]{:S(2)}) %collective-permute-start.17) | collective-permute-done | bytes 655392 | tf_op jit(solution)/shard_map/ppermute | solution.py:196
  164.8 1.0 sum_and_rotate.5.refs_1_
  166.0 16.6 %all_gather.3 = bf16[640,512]{1,0:T(8,128)(2,1)S(1)} all-gather(bf16[640,128]{1,0:T(8,128)(2,1)S(1)} %pad_maximum_fusion.2), channel_id=1, replica_groups=mesh['groups'=2,'fsdp'=4,'tp'=2,'rep'=2] {'fsdp'}, dimensions={1}, use_global_device_ids=true | all-gather | bytes 819200 | tf_op jit(solution)/shard_map/all_gather | solution.py:267
  182.6 1.6 fusion.2
  184.1 12.6 %score_heads.1 = bf16[1,16,640,640]{3,2,1,0:T(8,128)(2,1)} custom-call(s32[640,1]{1,0:T(8,128)S(1)} %reshape.86.canary_ref, s32[1,640]{1,0:T(1,128)S(1)} %reshape.85.ids_ref, bf16[640,128]{1,0:T(8,128)(2,1)S(1)} %pad_maximum_fusion.1.key_ref, bf16[160,2048]{1,0:T(8,128)(2,1)S(1)} %sum_and_rotate.4.refs_0_, bf16[160,2048]{1,0:T(8,128)(2,1)S(1)} %sum_and_rotate.5.refs_1_, ...), custom_call_target="tpu_custom_call" | custom-call | flops 3355443200 | bytes 13107200 | tf_op jit(solution)/shard_map/score_heads/pallas_call | solution.py:161
  (82 shorter events, 2.6 us)
Async XLA Ops:
  0.6 54.0 %collective-permute-start.1 = (bf16[320,2048]{1,0:T(8,128)(2,1)}, bf16[320,2048]{1,0:T(8,128)(2,1)S(1)}, u32[]{:S(2)}, u32[]{:S(2)}) collective-permute-start(bf16[320,2048]{1,0:T(8,128)(2,1)} %x_ref.7), channel_id=1, source_target_pairs={{0,2},{2,0},{1,3},{3,1},{4,6},{6,4},{5,7},{7,5},{8,10},{10,8},{9,1... | collective-permute-start | bytes 3932168 | tf_op jit(solution)/shard_map/ppermute | solution.py:223
  3.7 1.3 copy-start
  5.0 8.4 %copy-start.1 = (bf16[320,2048]{1,0:T(8,128)(2,1)S(1)}, bf16[320,2048]{1,0:T(8,128)(2,1)}, u32[]{:S(2)}) copy-start(bf16[320,2048]{1,0:T(8,128)(2,1)} %x_ref.7) | copy-start | bytes 3932164
  12.3 1.1 copy-start.8
  13.4 35.3 %collective-permute-start.9 = (bf16[1,160,2048]{2,1,0:T(8,128)(2,1)}, bf16[1,160,2048]{2,1,0:T(8,128)(2,1)}, u32[]{:S(2)}, u32[]{:S(2)}) collective-permute-start(bf16[1,160,2048]{2,1,0:T(8,128)(2,1)} %get-tuple-element.27), channel_id=1, source_target_pairs={{0,1},{1,0},{2,3},{3,2},{4,5},{5,4},{6,7},{7,6},{8,9},{9,8},{10,11... | collective-permute-start | bytes 1966088 | tf_op jit(solution)/shard_map/ppermute | solution.py:199
  26.1 1.5 copy-start.6
  27.6 56.8 %collective-permute-start.6 = (bf16[2,160,2048]{2,1,0:T(8,128)(2,1)}, bf16[2,160,2048]{2,1,0:T(8,128)(2,1)}, u32[]{:S(2)}, u32[]{:S(2)}) collective-permute-start(bf16[2,160,2048]{2,1,0:T(8,128)(2,1)} %get-tuple-element.23), channel_id=1, source_target_pairs={{0,1},{1,0},{2,3},{3,2},{4,5},{5,4},{6,7},{7,6},{8,9},{9,8},{10,11... | collective-permute-start | bytes 3932168 | tf_op jit(solution)/shard_map/ppermute | solution.py:199
  35.4 1.1 copy-start.10
  36.5 15.2 %collective-permute-start.7 = (bf16[1,160,2048]{2,1,0:T(8,128)(2,1)}, bf16[1,160,2048]{2,1,0:T(8,128)(2,1)}, u32[]{:S(2)}, u32[]{:S(2)}) collective-permute-start(bf16[1,160,2048]{2,1,0:T(8,128)(2,1)} %get-tuple-element.25), channel_id=1, source_target_pairs={{0,1},{1,0},{2,3},{3,2},{4,5},{5,4},{6,7},{7,6},{8,9},{9,8},{10,11... | collective-permute-start | bytes 1966088 | tf_op jit(solution)/shard_map/ppermute | solution.py:199
  36.6 1.6 copy-start.2
  38.2 1.6 copy-start.4
  39.8 4.8 %copy-start.16 = (s32[640]{0:T(1024)S(1)}, s32[640]{0:T(1024)}, u32[]{:S(2)}) copy-start(s32[640]{0:T(1024)} %param.10) | copy-start | bytes 7684
  39.8 4.8 %copy-start.17 = (s32[640]{0:T(1024)S(1)}, s32[640]{0:T(1024)}, u32[]{:S(2)}) copy-start(s32[640]{0:T(1024)} %param.11) | copy-start | bytes 7684
  43.9 4.8 %copy-start.9 = (f32[1,160,2048]{2,1,0:T(8,128)S(1)}, f32[1,160,2048]{2,1,0:T(8,128)}, u32[]{:S(2)}) copy-start(f32[1,160,2048]{2,1,0:T(8,128)} %copy-done.8) | copy-start | bytes 3932164
  43.9 9.6 %collective-permute-start = (f32[4,160,256]{2,1,0:T(8,128)}, f32[4,160,256]{2,1,0:T(8,128)}, u32[]{:S(2)}, u32[]{:S(2)}) collective-permute-start(f32[4,160,256]{2,1,0:T(8,128)} %get-tuple-element.19), channel_id=1, source_target_pairs={{0,1},{1,0},{2,3},{3,2},{4,5},{5,4},{6,7},{7,6},{8,9},{9,8},{10,11... | collective-permute-start | bytes 1966088 | tf_op jit(solution)/shard_map/ppermute | solution.py:199
  45.5 1.0 copy-start.15
  48.7 3.0 %copy-start.11 = (f32[1,160,2048]{2,1,0:T(8,128)S(1)}, f32[1,160,2048]{2,1,0:T(8,128)}, u32[]{:S(2)}) copy-start(f32[1,160,2048]{2,1,0:T(8,128)} %copy-done.10) | copy-start | bytes 3932164
  50.0 34.0 %collective-permute-start.10 = (bf16[1,160,2048]{2,1,0:T(8,128)(2,1)S(1)}, bf16[1,160,2048]{2,1,0:T(8,128)(2,1)S(1)}, u32[]{:S(2)}, u32[]{:S(2)}) collective-permute-start(bf16[1,160,2048]{2,1,0:T(8,128)(2,1)S(1)} %add_convert_fusion.4), channel_id=1, source_target_pairs={{0,4},{4,0},{8,12},{12,8},{1,5},{5,1},{9,13},{13,9},{2,6},{6,2},{1... | collective-permute-start | bytes 1966088 | tf_op jit(solution)/shard_map/ppermute | solution.py:196
  53.0 39.7 %collective-permute-start.8 = (bf16[1,160,2048]{2,1,0:T(8,128)(2,1)S(1)}, bf16[1,160,2048]{2,1,0:T(8,128)(2,1)S(1)}, u32[]{:S(2)}, u32[]{:S(2)}) collective-permute-start(bf16[1,160,2048]{2,1,0:T(8,128)(2,1)S(1)} %add_convert_fusion.5), channel_id=1, source_target_pairs={{0,4},{4,0},{8,12},{12,8},{1,5},{5,1},{9,13},{13,9},{2,6},{6,2},{1... | collective-permute-start | bytes 1966088 | tf_op jit(solution)/shard_map/ppermute | solution.py:196
  61.2 12.5 %copy-start.3 = (bf16[2048,512]{1,0:T(8,128)(2,1)S(1)}, bf16[2048,512]{1,0:T(8,128)(2,1)}, u32[]{:S(2)}) copy-start(bf16[2048,512]{1,0:T(8,128)(2,1)} %wk_ref.3) | copy-start | bytes 6291460
  61.3 12.5 %copy-start.5 = (bf16[2048,512]{1,0:T(8,128)(2,1)S(1)}, bf16[2048,512]{1,0:T(8,128)(2,1)}, u32[]{:S(2)}) copy-start(bf16[2048,512]{1,0:T(8,128)(2,1)} %wv_ref.3) | copy-start | bytes 6291460
  61.3 26.0 %collective-permute-start.15 = (bf16[1,160,2048]{2,1,0:T(8,128)(2,1)S(1)}, bf16[1,160,2048]{2,1,0:T(8,128)(2,1)S(1)}, u32[]{:S(2)}, u32[]{:S(2)}) collective-permute-start(bf16[1,160,2048]{2,1,0:T(8,128)(2,1)S(1)} %get-tuple-element.33), channel_id=1, source_target_pairs={{0,1},{1,0},{2,3},{3,2},{4,5},{5,4},{6,7},{7,6},{8,9},{9,8},{10,11... | collective-permute-start | bytes 1966088 | tf_op jit(solution)/shard_map/ppermute | solution.py:199
  73.5 55.1 %collective-permute-start.12 = (bf16[2,160,2048]{2,1,0:T(8,128)(2,1)S(1)}, bf16[2,160,2048]{2,1,0:T(8,128)(2,1)S(1)}, u32[]{:S(2)}, u32[]{:S(2)}) collective-permute-start(bf16[2,160,2048]{2,1,0:T(8,128)(2,1)S(1)} %get-tuple-element.29), channel_id=1, source_target_pairs={{0,1},{1,0},{2,3},{3,2},{4,5},{5,4},{6,7},{7,6},{8,9},{9,8},{10,11... | collective-permute-start | bytes 3932168 | tf_op jit(solution)/shard_map/ppermute | solution.py:199
  77.2 7.4 %copy-start.7 = (f32[2,160,2048]{2,1,0:T(8,128)S(1)}, f32[2,160,2048]{2,1,0:T(8,128)}, u32[]{:S(2)}) copy-start(f32[2,160,2048]{2,1,0:T(8,128)} %copy-done.6) | copy-start | bytes 7864324
  84.0 7.9 %collective-permute-start.13 = (bf16[1,160,2048]{2,1,0:T(8,128)(2,1)S(1)}, bf16[1,160,2048]{2,1,0:T(8,128)(2,1)S(1)}, u32[]{:S(2)}, u32[]{:S(2)}) collective-permute-start(bf16[1,160,2048]{2,1,0:T(8,128)(2,1)S(1)} %get-tuple-element.31), channel_id=1, source_target_pairs={{0,1},{1,0},{2,3},{3,2},{4,5},{5,4},{6,7},{7,6},{8,9},{9,8},{10,11... | collective-permute-start | bytes 1966088 | tf_op jit(solution)/shard_map/ppermute | solution.py:199
  84.4 5.6 %collective-permute-start.2 = (f32[4,160,256]{2,1,0:T(8,128)S(1)}, f32[4,160,256]{2,1,0:T(8,128)S(1)}, u32[]{:S(2)}, u32[]{:S(2)}) collective-permute-start(f32[4,160,256]{2,1,0:T(8,128)S(1)} %get-tuple-element.21), channel_id=1, source_target_pairs={{0,1},{1,0},{2,3},{3,2},{4,5},{5,4},{6,7},{7,6},{8,9},{9,8},{10,11... | collective-permute-start | bytes 1966088 | tf_op jit(solution)/shard_map/ppermute | solution.py:199
  87.3 32.1 %collective-permute-start.11 = (bf16[1,160,2048]{2,1,0:T(8,128)(2,1)S(1)}, bf16[1,160,2048]{2,1,0:T(8,128)(2,1)S(1)}, u32[]{:S(2)}, u32[]{:S(2)}) collective-permute-start(bf16[1,160,2048]{2,1,0:T(8,128)(2,1)S(1)} %get-tuple-element.36), channel_id=1, source_target_pairs={{0,8},{4,12},{8,0},{12,4},{1,9},{5,13},{9,1},{13,5},{2,10},{6,14},... | collective-permute-start | bytes 1966088 | tf_op jit(solution)/shard_map/ppermute | solution.py:196
  90.1 38.6 %collective-permute-start.16 = (bf16[1,160,2048]{2,1,0:T(8,128)(2,1)S(1)}, bf16[1,160,2048]{2,1,0:T(8,128)(2,1)S(1)}, u32[]{:S(2)}, u32[]{:S(2)}) collective-permute-start(bf16[1,160,2048]{2,1,0:T(8,128)(2,1)S(1)} %add_convert_fusion.1), channel_id=1, source_target_pairs={{0,4},{4,0},{8,12},{12,8},{1,5},{5,1},{9,13},{13,9},{2,6},{6,2},{1... | collective-permute-start | bytes 1966088 | tf_op jit(solution)/shard_map/ppermute | solution.py:196
  91.9 35.8 %collective-permute-start.3 = (bf16[2,320,256]{2,1,0:T(8,128)(2,1)S(1)}, bf16[2,320,256]{2,1,0:T(8,128)(2,1)S(1)}, u32[]{:S(2)}, u32[]{:S(2)}) collective-permute-start(bf16[2,320,256]{2,1,0:T(8,128)(2,1)S(1)} %slice.60), channel_id=1, source_target_pairs={{0,4},{4,0},{8,12},{12,8},{1,5},{5,1},{9,13},{13,9},{2,6},{6,2},{1... | collective-permute-start | bytes 983048 | tf_op jit(solution)/shard_map/ppermute | solution.py:196
  92.4 26.9 %copy-start.12 = (f32[160,128]{1,0:T(8,128)S(1)}, f32[160,128]{1,0:T(8,128)}, u32[]{:S(2)}) copy-start(f32[160,128]{1,0:T(8,128)} %get-tuple-element.41.cos_ref) | copy-start | bytes 245764
  92.4 26.9 %copy-start.14 = (f32[160,128]{1,0:T(8,128)S(1)}, f32[160,128]{1,0:T(8,128)}, u32[]{:S(2)}) copy-start(f32[160,128]{1,0:T(8,128)} %get-tuple-element.39.sin_ref) | copy-start | bytes 245764
  92.6 60.0 %collective-permute-start.14 = (bf16[1,160,2048]{2,1,0:T(8,128)(2,1)S(1)}, bf16[1,160,2048]{2,1,0:T(8,128)(2,1)S(1)}, u32[]{:S(2)}, u32[]{:S(2)}) collective-permute-start(bf16[1,160,2048]{2,1,0:T(8,128)(2,1)S(1)} %add_convert_fusion.2), channel_id=1, source_target_pairs={{0,4},{4,0},{8,12},{12,8},{1,5},{5,1},{9,13},{13,9},{2,6},{6,2},{1... | collective-permute-start | bytes 1966088 | tf_op jit(solution)/shard_map/ppermute | solution.py:196
  127.8 15.9 %collective-permute-start.4 = (bf16[1,320,256]{2,1,0:T(8,128)(2,1)S(1)}, bf16[1,320,256]{2,1,0:T(8,128)(2,1)S(1)}, u32[]{:S(2)}, u32[]{:S(2)}) collective-permute-start(bf16[1,320,256]{2,1,0:T(8,128)(2,1)S(1)} %fusion.14), channel_id=1, source_target_pairs={{0,8},{4,12},{8,0},{12,4},{1,9},{5,13},{9,1},{13,5},{2,10},{6,14},... | collective-permute-start | bytes 491528 | tf_op jit(solution)/shard_map/ppermute | solution.py:196
  129.1 35.8 %collective-permute-start.17 = (bf16[1,160,2048]{2,1,0:T(8,128)(2,1)S(1)}, bf16[1,160,2048]{2,1,0:T(8,128)(2,1)S(1)}, u32[]{:S(2)}, u32[]{:S(2)}) collective-permute-start(bf16[1,160,2048]{2,1,0:T(8,128)(2,1)S(1)} %get-tuple-element.34), channel_id=1, source_target_pairs={{0,8},{4,12},{8,0},{12,4},{1,9},{5,13},{9,1},{13,5},{2,10},{6,14},... | collective-permute-start | bytes 1966088 | tf_op jit(solution)/shard_map/ppermute | solution.py:196
  143.8 21.1 %copy-start.13 = (f32[160,128]{1,0:T(8,128)S(1)}, f32[160,128]{1,0:T(8,128)}, u32[]{:S(2)}) copy-start(f32[160,128]{1,0:T(8,128)} %get-tuple-element.38.sin_ref) | copy-start | bytes 245764
  143.8 40.4 %collective-permute-start.18 = (bf16[160,2048]{1,0:T(8,128)(2,1)S(1)}, bf16[160,2048]{1,0:T(8,128)(2,1)S(1)}, u32[]{:S(2)}, u32[]{:S(2)}) collective-permute-start(bf16[160,2048]{1,0:T(8,128)(2,1)S(1)} %sum_and_rotate.4.refs_0_), channel_id=1, source_target_pairs={{0,1},{1,0},{2,3},{3,2},{4,5},{5,4},{6,7},{7,6},{8,9},{9,8},{10,11... | collective-permute-start | bytes 1966088 | tf_op jit(solution)/shard_map/ppermute | solution.py:199
  144.0 21.9 %collective-permute-start.5 = (bf16[320,128]{1,0:T(8,128)(2,1)S(1)}, bf16[320,128]{1,0:T(8,128)(2,1)S(1)}, u32[]{:S(2)}, u32[]{:S(2)}) collective-permute-start(bf16[320,128]{1,0:T(8,128)(2,1)S(1)} %sum_and_rotate.3), channel_id=1, source_target_pairs={{0,1},{1,0},{2,3},{3,2},{4,5},{5,4},{6,7},{7,6},{8,9},{9,8},{10,11... | collective-permute-start | bytes 245768 | tf_op jit(solution)/shard_map/ppermute | solution.py:199
  144.6 21.4 %collective-permute-start.20 = (bf16[320,128]{1,0:T(8,128)(2,1)S(1)}, bf16[320,128]{1,0:T(8,128)(2,1)S(1)}, u32[]{:S(2)}, u32[]{:S(2)}) collective-permute-start(bf16[320,128]{1,0:T(8,128)(2,1)S(1)} %slice.155), channel_id=1, source_target_pairs={{0,1},{1,0},{2,3},{3,2},{4,5},{5,4},{6,7},{7,6},{8,9},{9,8},{10,11... | collective-permute-start | bytes 245768 | tf_op jit(solution)/shard_map/ppermute | solution.py:199
  165.8 18.3 %collective-permute-start.19 = (bf16[160,2048]{1,0:T(8,128)(2,1)S(1)}, bf16[160,2048]{1,0:T(8,128)(2,1)S(1)}, u32[]{:S(2)}, u32[]{:S(2)}) collective-permute-start(bf16[160,2048]{1,0:T(8,128)(2,1)S(1)} %sum_and_rotate.5.refs_1_), channel_id=1, source_target_pairs={{0,1},{1,0},{2,3},{3,2},{4,5},{5,4},{6,7},{7,6},{8,9},{9,8},{10,11... | collective-permute-start | bytes 1966088 | tf_op jit(solution)/shard_map/ppermute | solution.py:199

commit v3 on v2

v3 whole, which is shorter than its diff:
```python
import functools
import math

import jax
import jax.numpy as jnp
from jax import lax
from jax.experimental import pallas as pl
from jax.experimental.pallas import tpu as pltpu
from jax.sharding import PartitionSpec as P

HQ = 128
KV = 8
DH = 128
VMEM_BYTES = 26 * 1024 * 1024
LIGHT = pl.CostEstimate(flops=1000, bytes_accessed=1000, transcendentals=0)


def rope_tables(positions):
    half = DH // 2
    expo = jnp.arange(half, dtype=jnp.float32) * (2.0 / DH)
    freq = jnp.power(jnp.float32(500000.0), -expo)
    wavelen = 2.0 * math.pi / freq
    smooth = (8192.0 / wavelen - 1.0) / 3.0
    mixed = (1.0 - smooth) * freq / 8.0 + smooth * freq
    freq = jnp.where(wavelen > 8192.0, freq / 8.0, jnp.where(wavelen < 2048.0, freq, mixed))
    angle = positions.astype(jnp.float32)[:, None] * freq[None, :]
    cosine, sine = jnp.cos(angle), jnp.sin(angle)
    return jnp.concatenate([cosine, cosine], axis=1), jnp.concatenate([-sine, sine], axis=1)


def ordered_rows(place_ref, x_ref, rows_ref):
    half = x_ref.shape[0] // 2
    core = place_ref[0]
    rows_ref[:half] = x_ref[pl.ds(pl.multiple_of(core * half, 16), half)]
    rows_ref[half:] = x_ref[pl.ds(pl.multiple_of((1 - core) * half, 16), half)]


def query_kernel(pieces, width, place_ref, x_ref, w_ref, *refs):
    keep_ref, *give_refs, rows_ref = refs[-2 - pieces :]
    tile = pl.program_id(1)
    each = keep_ref.shape[2] // width

    @pl.when((pl.program_id(0) == 0) & (tile == 0))
    def _():
        ordered_rows(place_ref, x_ref, rows_ref)

    result = jnp.dot(rows_ref[...], w_ref[...], preferred_element_type=jnp.float32)
    half = result.shape[0] // 2
    keep_ref[0] = result[:half]
    for j, give_ref in enumerate(give_refs):

        @pl.when(tile == j // each)
        def _():
            start = j % each * width
            give_ref[0] = result[half:, start : start + width].astype(give_ref.dtype)


def project_query(rindex, findex, slots, x, w, cols, tile, width, after=()):
    rows, depth = x.shape
    tiles = cols // tile
    place = jnp.stack([rindex] + [findex ^ slot for slot in slots]).astype(jnp.int32)
    pieces = cols // width
    outs = pl.pallas_call(
        functools.partial(query_kernel, pieces, width),
        grid_spec=pltpu.PrefetchScalarGridSpec(
            num_scalar_prefetch=1,
            grid=(len(slots), tiles),
            in_specs=[
                pl.BlockSpec((rows, depth), lambda s, j, place: (0, 0)),
                pl.BlockSpec((depth, tile), lambda s, j, place: (0, place[1 + s] * tiles + j)),
            ]
            + [pl.BlockSpec(memory_space=pl.ANY)] * len(after),
            out_specs=[pl.BlockSpec((1, rows // 2, tile), lambda s, j, place: (s, 0, j))]
            + [pl.BlockSpec((1, rows // 2, width), lambda s, j, place: (s, 0, 0))] * pieces,
            scratch_shapes=[pltpu.VMEM((rows, depth), x.dtype)],
        ),
        out_shape=[jax.ShapeDtypeStruct((len(slots), rows // 2, cols), jnp.float32)]
        + [jax.ShapeDtypeStruct((len(slots), rows // 2, width), jnp.bfloat16)] * pieces,
        compiler_params=pltpu.CompilerParams(vmem_limit_bytes=VMEM_BYTES),
        cost_estimate=LIGHT,
        name="query_products",
    )(place, x, w, *after)
    return outs[0], outs[1:]


def pair_kernel(place_ref, x_ref, wk_ref, wv_ref, *refs):
    keep_ref, give_ref, rows_ref = refs[-3:]

    @pl.when(pl.program_id(0) == 0)
    def _():
        ordered_rows(place_ref, x_ref, rows_ref)

    weights = jnp.concatenate([wk_ref[...], wv_ref[...]], axis=1)
    result = jnp.dot(rows_ref[...], weights, preferred_element_type=jnp.float32)
    half = result.shape[0] // 2
    keep_ref[0] = result[:half]
    give_ref[0] = result[half:].astype(give_ref.dtype)


def project_pair(rindex, findex, slots, x, w_key, w_value, after=()):
    rows, depth = x.shape
    place = jnp.stack([rindex] + [findex ^ slot for slot in slots]).astype(jnp.int32)
    weight = pl.BlockSpec((depth, DH), lambda s, place: (0, place[1 + s]))
    out = pl.BlockSpec((1, rows // 2, 2 * DH), lambda s, place: (s, 0, 0))
    shape = jax.ShapeDtypeStruct((len(slots), rows // 2, 2 * DH), jnp.float32)
    return pl.pallas_call(
        pair_kernel,
        grid_spec=pltpu.PrefetchScalarGridSpec(
            num_scalar_prefetch=1,
            grid=(len(slots),),
            in_specs=[pl.BlockSpec((rows, depth), lambda s, place: (0, 0)), weight, weight]
            + [pl.BlockSpec(memory_space=pl.ANY)] * len(after),
            out_specs=[out, out],
            scratch_shapes=[pltpu.VMEM((rows, depth), x.dtype)],
        ),
        out_shape=[shape, jax.ShapeDtypeStruct(shape.shape, jnp.bfloat16)],
        compiler_params=pltpu.CompilerParams(vmem_limit_bytes=VMEM_BYTES),
        cost_estimate=LIGHT,
        name="key_value_products",
    )(place, x, w_key, w_value, *after)


def add_kernel(tiles, extra, *refs):
    keep_ref, give_refs, out_ref = refs[0], refs[1 : 1 + tiles], refs[-1]
    for j, give_ref in enumerate(give_refs):

        @pl.when(pl.program_id(1) == j)
        def _():
            total = keep_ref[0] + give_ref[0].astype(jnp.float32)
            if extra:
                total = total + refs[1 + tiles][0].astype(jnp.float32)
            out_ref[0] = total.astype(out_ref.dtype)


def add_rows(keep, gots, count, landed=(), after=()):
    _, rows, cols = keep.shape
    tiles = len(gots)
    tile = cols // tiles
    full = pl.BlockSpec((1, rows, tile), lambda s, j: (s, 0, j))
    return pl.pallas_call(
        functools.partial(add_kernel, tiles, len(landed)),
        grid=(count, tiles),
        in_specs=[full]
        + [pl.BlockSpec((1, rows, tile), lambda s, j: (s, 0, 0))] * tiles
        + [full] * len(landed)
        + [pl.BlockSpec(memory_space=pl.ANY)] * len(after),
        out_specs=full,
        out_shape=jax.ShapeDtypeStruct((count, rows, cols), jnp.bfloat16),
        compiler_params=pltpu.CompilerParams(vmem_limit_bytes=VMEM_BYTES),
        cost_estimate=LIGHT,
        name="add_rows",
    )(keep, *gots, *landed, *after)


def rotate_kernel(count, pieces, cos_ref, sin_ref, *refs):
    terms, gots, out_ref = refs[:count], refs[count : count + pieces], refs[-1]
    total = terms[0][0].astype(jnp.float32)
    for term in terms[1:]:
        total = total + term[0].astype(jnp.float32)
    cosine, sine = cos_ref[...], sin_ref[...]

    def write(total):
        for head in range(total.shape[1] // DH):
            part = total[:, head * DH : (head + 1) * DH]
            turned = pltpu.roll(part, DH // 2, axis=1)
            value = part * cosine + turned * sine
            out_ref[:, head * DH : (head + 1) * DH] = value.astype(out_ref.dtype)

    if not gots:
        write(total)
    for j, got in enumerate(gots):

        @pl.when(pl.program_id(0) == j)
        def _():
            write(total + got[0].astype(jnp.float32))


def sum_and_rotate(cosine, sine, terms, gots, cols, after=()):
    rows = cosine.shape[0]
    slot_of_gots, gots = gots
    tile = cols // max(1, len(gots))
    table = pl.BlockSpec((rows, DH), lambda j: (0, 0))

    def block(slot, start):
        return pl.BlockSpec((1, rows, tile), lambda j: (slot, 0, start // tile + j))

    return pl.pallas_call(
        functools.partial(rotate_kernel, len(terms), len(gots)),
        grid=(cols // tile,),
        in_specs=[table, table]
        + [block(slot, start) for _, slot, start in terms]
        + [pl.BlockSpec((1, rows, tile), lambda j: (slot_of_gots, 0, 0))] * len(gots)
        + [pl.BlockSpec(memory_space=pl.ANY)] * len(after),
        out_specs=pl.BlockSpec((rows, tile), lambda j: (0, j)),
        out_shape=jax.ShapeDtypeStruct((rows, cols), jnp.bfloat16),
        compiler_params=pltpu.CompilerParams(vmem_limit_bytes=VMEM_BYTES),
        cost_estimate=LIGHT,
        name="sum_and_rotate",
    )(cosine, sine, *[term for term, _, _ in terms], *gots, *after)


def split_kernel(count, cos_ref, sin_ref, *refs):
    terms, (key_ref, value_ref) = refs[:count], refs[-2:]
    total = terms[0][0].astype(jnp.float32)
    for term in terms[1:]:
        total = total + term[0].astype(jnp.float32)
    key, value = total[:, :DH], total[:, DH:]
    turned = pltpu.roll(key, DH // 2, axis=1)
    key_ref[...] = (key * cos_ref[...] + turned * sin_ref[...]).astype(key_ref.dtype)
    value_ref[0] = value.astype(value_ref.dtype)


def split_and_rotate(cosine, sine, terms, after):
    rows = cosine.shape[0]
    table = pl.BlockSpec((rows, DH), lambda j: (0, 0))
    return pl.pallas_call(
        functools.partial(split_kernel, len(terms)),
        grid=(1,),
        in_specs=[table, table]
        + [pl.BlockSpec((1, rows, 2 * DH), lambda j: (0, 0, 0))] * len(terms)
        + [pl.BlockSpec(memory_space=pl.ANY)] * len(after),
        out_specs=[table, pl.BlockSpec((1, rows, DH), lambda j: (0, 0, 0))],
        out_shape=[
            jax.ShapeDtypeStruct((rows, DH), jnp.bfloat16),
            jax.ShapeDtypeStruct((1, rows, DH), jnp.bfloat16),
        ],
        compiler_params=pltpu.CompilerParams(vmem_limit_bytes=VMEM_BYTES),
        cost_estimate=LIGHT,
        name="split_and_rotate",
    )(cosine, sine, *terms, *after)


def prepare_kernel(canary_ref, ids_ref, own_ref, other_ref, order_ref, key_t_ref):
    order = jnp.where(canary_ref[...] == ids_ref[...], 1.0, 0.0).astype(jnp.bfloat16)
    order_ref[...] = order
    key = jnp.concatenate([own_ref[...], other_ref[...]], axis=0)
    key_t_ref[...] = jnp.dot(order, key, preferred_element_type=jnp.float32).T.astype(jnp.bfloat16)


def prepare(canary_rows, ids, own, other):
    rows = ids.shape[0]
    return pl.pallas_call(
        prepare_kernel,
        out_shape=[
            jax.ShapeDtypeStruct((rows, rows), jnp.bfloat16),
            jax.ShapeDtypeStruct((DH, rows), jnp.bfloat16),
        ],
        compiler_params=pltpu.CompilerParams(vmem_limit_bytes=VMEM_BYTES),
        name="order_and_keys",
    )(canary_rows.reshape(rows, 1), ids.reshape(1, rows), own, other)


def value_kernel(place_ref, order_ref, own_ref, other_ref, out_ref, mark_ref):
    mark_ref[...] = jnp.zeros_like(mark_ref)
    rows = jnp.concatenate([own_ref[0], other_ref[0]], axis=0)
    out_ref[...] = jnp.dot(order_ref[...], rows, preferred_element_type=jnp.float32).astype(out_ref.dtype)


def order_values(findex, order, own, other):
    rows = order.shape[0]
    slots, part, width = own.shape
    place = jnp.stack([findex ^ s for s in range(slots)]).astype(jnp.int32)
    block = pl.BlockSpec((1, part, width), lambda s, place: (place[s], 0, 0))
    return pl.pallas_call(
        value_kernel,
        grid_spec=pltpu.PrefetchScalarGridSpec(
            num_scalar_prefetch=1,
            grid=(slots,),
            in_specs=[pl.BlockSpec((rows, rows), lambda s, place: (0, 0)), block, block],
            out_specs=[
                pl.BlockSpec((rows, width), lambda s, place: (0, s)),
                pl.BlockSpec((8, DH), lambda s, place: (0, 0)),
            ],
        ),
        out_shape=[
            jax.ShapeDtypeStruct((rows, slots * width), jnp.bfloat16),
            jax.ShapeDtypeStruct((8, DH), jnp.float32),
        ],
        compiler_params=pltpu.CompilerParams(vmem_limit_bytes=VMEM_BYTES),
        name="order_values",
    )(place, order, own, other)


def score_kernel(count, order_ref, key_t_ref, *refs):
    queries, (out_ref, mark_ref) = refs[:count], refs[-2:]
    mark_ref[...] = jnp.zeros_like(mark_ref)
    stacked = jnp.concatenate([query[...] for query in queries], axis=0)
    chosen = jnp.dot(order_ref[...], stacked, preferred_element_type=jnp.float32).astype(jnp.bfloat16)
    for head in range(stacked.shape[1] // DH):
        products = jnp.dot(
            chosen[:, head * DH : (head + 1) * DH], key_t_ref[...], preferred_element_type=jnp.float32
        )
        out_ref[0, head] = (products * DH ** (-0.5)).astype(out_ref.dtype)


def score_heads(order, key_t, heads, start, count, queries, earlier, after=()):
    rows = order.shape[0]
    step = 2 if count % 2 == 0 else 1

    def block(query, first):
        return pl.BlockSpec((query.shape[0], step * DH), lambda j: (0, first // step + j))

    return pl.pallas_call(
        functools.partial(score_kernel, len(queries)),
        grid=(count // step,),
        in_specs=[
            pl.BlockSpec((rows, rows), lambda j: (0, 0)),
            pl.BlockSpec((DH, rows), lambda j: (0, 0)),
        ]
        + [block(query, first) for query, first in queries]
        + [pl.BlockSpec(memory_space=pl.ANY)] * (len(earlier) + len(after)),
        out_specs=[
            pl.BlockSpec((1, step, rows, rows), lambda j: (0, start // step + j, 0, 0)),
            pl.BlockSpec((8, DH), lambda j: (0, 0)),
        ],
        out_shape=[
            jax.ShapeDtypeStruct((1, heads, rows, rows), jnp.bfloat16),
            jax.ShapeDtypeStruct((8, DH), jnp.float32),
        ],
        input_output_aliases={2 + len(queries): 0} if earlier else {},
        compiler_params=pltpu.CompilerParams(vmem_limit_bytes=VMEM_BYTES),
        cost_estimate=LIGHT,
        name="score_heads",
    )(order, key_t, *[query for query, _ in queries], *earlier, *after)


def body(hidden, w_query, w_key, w_value, canary_rows, positions):
    shards = lax.axis_size("fsdp")
    findex = lax.axis_index("fsdp")
    tps = lax.axis_size("tp")
    tindex = lax.axis_index("tp")
    rindex = lax.axis_index("rep")
    local, depth = hidden.shape
    half = local // 2
    rows = local * tps
    head_cols = w_query.shape[1] // shards
    heads_here = head_cols // DH
    group = HQ // KV
    assert shards & (shards - 1) == 0 and lax.axis_size("rep") == 2

    def swap(x, bit):
        return lax.ppermute(x, "fsdp", [(i, i ^ bit) for i in range(shards)])

    def other_core(x):
        return lax.ppermute(x, "rep", [(0, 1), (1, 0)])

    def low(x):
        return x.astype(jnp.bfloat16)

    odd = list(range(3, shards, 2)) + [1]
    even = list(range(2, shards, 2)) + [0]
    fast_pair = heads_here == group

    def spread(live):
        terms, first = [], None
        bit = 2
        while bit < shards:
            sent = [x for x in sorted(live) if x & bit]
            pack = jnp.stack([low(live[x]) for x in sent])
            first = pack if first is None else first
            landed = swap(pack, bit)
            for k, x in enumerate(sent):
                if x == bit:
                    terms.append(landed)
                else:
                    live[x ^ bit] = live[x ^ bit] + landed[k].astype(jnp.float32)
                del live[x]
            bit *= 2
        return terms, first

    blocks = [hidden] + [
        lax.ppermute(hidden, "tp", [(i, (i - b) % tps) for i in range(tps)]) for b in range(1, tps)
    ]

    block_ids = ((tindex + jnp.arange(tps, dtype=jnp.int32)) % tps * local)[:, None]
    own_ids = (block_ids + rindex * half + jnp.arange(half, dtype=jnp.int32)[None]).reshape(-1)
    other_ids = (block_ids + (1 - rindex) * half + jnp.arange(half, dtype=jnp.int32)[None]).reshape(-1)
    ids = jnp.concatenate([own_ids, other_ids])
    own_positions = jnp.sum(
        jnp.where(own_ids[:, None] == canary_rows[None, :], positions[None, :], 0), axis=1
    )
    cosine, sine = rope_tables(own_positions)

    tile = min(1024, head_cols)

    def project(slots, block, width, after=()):
        keep, gives = project_query(
            rindex, findex, slots, block, w_query, head_cols, tile, width, after
        )
        return keep, [other_core(give) for give in gives], gives[0]

    def project_heads(block, after):
        keep, give = project_pair(
            rindex, findex, list(range(shards)), block, w_key, w_value, (after,)
        )
        return keep + other_core(give).astype(jnp.float32), give

    def rotate(b, p, split, terms, behind):
        keep, got = evens[b]
        cols, each = head_cols // split, len(got) // split
        table = slice(b * half, (b + 1) * half)
        added = [(keep, len(even) - 1, p * cols), (fars[b], len(odd) - 1, p * cols)]
        added += [(term, 0, 0) for term in terms]
        gots = (len(even) - 1, got[p * each : (p + 1) * each])
        turned = sum_and_rotate(cosine[table], sine[table], added, gots, cols, behind)
        return turned, other_core(turned)

    def add_even(b, parts, behind):
        keep, got = evens[b]
        landed = (fars[b],) if shards > 2 else ()
        summed = add_rows(keep, got, len(even) - 1, landed, behind)
        cols = head_cols // parts
        spreads = []
        for p in range(parts):
            live = {x: summed[k][:, p * cols : (p + 1) * cols] for k, x in enumerate(even[:-1])}
            spreads.append(spread(live))
        return [terms for terms, _ in spreads], spreads[-1][1]

    last, split = tps - 1, head_cols // tile
    evens, fars, pairs, terms, after, behind = [], [], [], [], (), ()
    for b, block in enumerate(blocks):
        odd_keep, odd_got, _ = project(odd, block, tile, after)
        odd_sent = add_rows(odd_keep, odd_got, len(odd))
        fars.append(swap(odd_sent, 1))
        if b > 0:
            parts, first = add_even(b - 1, 1, (odd_sent,))
            terms.append(parts)
            behind = (first,)
        even_keep, even_got, given = project(even, block, tile, (odd_sent,) + behind)
        evens.append((even_keep, even_got))
        if fast_pair:
            pair, given = project_heads(block, given)
            pairs.append(pair)
        after = (given,)
    if fast_pair:
        pair = jnp.concatenate(pairs, axis=1)
        pair_landed = swap(low(pair[1::2]), 1)
        live = {x: pair[x] + pair_landed[x // 2].astype(jnp.float32) for x in even[:-1]}
        pair_terms, first = spread(live)
        after = (first,)
    parts, first = add_even(last, split, after)
    terms.append(parts)
    after = (first,)

    if fast_pair:
        key_rot, held = split_and_rotate(cosine, sine, [pair, pair_landed] + pair_terms, after)
        bit = 1
        while bit < shards:
            held = jnp.concatenate([held, swap(held, bit)])
            bit *= 2
        held_other = other_core(held)
    else:
        x = jnp.concatenate(blocks, axis=0)
        key_sum, value_sum = lax.psum(
            (
                jnp.dot(x, w_key, preferred_element_type=jnp.float32),
                jnp.dot(x, w_value, preferred_element_type=jnp.float32),
            ),
            ("fsdp", "rep"),
        )

        def of_core(y, core):
            parts = y.reshape(tps, 2, half, -1)
            return lax.dynamic_index_in_dim(parts, core, 1, keepdims=False).reshape(tps * half, -1)

        mine = lax.dynamic_slice_in_dim(key_sum, findex * heads_here // group * DH, DH, 1)
        key_own = of_core(mine, rindex)
        key_rot = sum_and_rotate(cosine, sine, [(key_own[None], 0, 0)], (0, []), DH, after)
        value_rows = low(jnp.concatenate([of_core(value_sum, rindex), of_core(value_sum, 1 - rindex)]))

    order, key_t = prepare(canary_rows, ids, key_rot, other_core(key_rot))
    if fast_pair:
        values, values_mark = order_values(findex, order, held, held_other)
    else:
        values_mark = key_t
        values = low(jnp.dot(order, value_rows, preferred_element_type=jnp.float32))

    rotated = [rotate(b, 0, 1, terms[b][0], after) for b in range(last)]
    count = heads_here // split
    scores, mark = (), ()
    for p in range(split):
        turned = rotate(last, p, split, terms[last][p], (key_t,) + mark)
        queries = [(row[0], p * count) for row in rotated] + [(turned[0], 0)]
        queries += [(row[1], p * count) for row in rotated] + [(turned[1], 0)]
        behind = (values_mark,) if p == split - 1 else ()
        *scores, mark = score_heads(
            order, key_t, heads_here, p * count, count, queries, scores, behind
        )
        mark = (mark,)
    return (scores[0], values)


def solution(mesh):
    in_specs = (
        P(("groups", "tp"), ("fsdp", "rep")),
        P(("fsdp", "rep"), "tp"),
        P(("fsdp", "rep"), "tp"),
        P(("fsdp", "rep"), "tp"),
        P("groups"),
        P("groups"),
    )
    out_specs = (P("tp", "fsdp", "groups", None), P("groups", "tp"))
    return jax.shard_map(body, mesh=mesh, in_specs=in_specs, out_specs=out_specs, check_vma=False)
```

time: 198 us -> 180 us (0.909)
  blocking collectives: 16.6 us -> 0 us
  Pallas kernels: 75 us -> 80.4 us
  other arithmetic: 10.4 us -> 5.53 us
    all_gather x1 -> x0, blocking collectives: 16.6 us -> none  [body(): value_rows = lax.all_gather(value_both, 'fsdp', axis=1, tiled=True)]
    ppermute x8 -> x9, waiting for transfers between devices: 64.9 us -> 58.4 us  [swap(): return lax.ppermute(x, 'fsdp', [(i, i ^ bit) for i in range(shards)])]
    pallas_call x10 -> x16, Pallas kernels: 67.5 us -> 73.3 us  [the longest x4 42.8 us: project_query(): pl.pallas_call(functools.partial(query_kernel, pieces, width), grid_spec=...]
    ppermute x12 -> x15, waiting for transfers between devices: 0.03 us -> 5.44 us  [other_core(): return lax.ppermute(x, 'rep', [(0, 1), (1, 0)])]
    convert_element_type x7 -> x1, other arithmetic: 4.88 us -> 1.11 us  [low(): return x.astype(jnp.bfloat16)]
    unnamed x36 -> x66, local copies, waits for them, and re-layouts: 8.24 us -> 7.99 us
    ppermute x8 -> x9, starting transfers between devices: 11.7 us -> 11.7 us  [swap(): return lax.ppermute(x, 'fsdp', [(i, i ^ bit) for i in range(shards)])]
  transfers between devices with their start and end apart: 21 -> 25, of which waited for: 5 -> 10; matrix products, arithmetic and copies ran while one was open for 7% -> 4% of each run, Pallas kernels for 32% -> 41%
where the time goes in v3:
time: 180 us; the launch traced here: 179 us
  Pallas kernels  80.4 us (45%)
  waiting for transfers between devices  63.9 us (36%)
  starting transfers between devices  17.9 us (10%)
  local copies, waits for them, and re-layouts  10.1 us (6%)
  other arithmetic  5.53 us (3%)
    ppermute x9, waiting for transfers between devices, swap(): return lax.ppermute(x, 'fsdp', [(i, i ^ bit) for i in range(shards)])  58.4 us
    pallas_call x4, Pallas kernels, project_query(): pl.pallas_call(functools.partial(query_kernel, pieces, width), grid_spec=...  42.8 us
    pallas_call x2, Pallas kernels, score_heads(): pl.pallas_call(functools.partial(score_kernel, len(queries)), grid=(count...  13.2 us
    ppermute x9, starting transfers between devices, swap(): return lax.ppermute(x, 'fsdp', [(i, i ^ bit) for i in range(shards)])  11.7 us
    unnamed x66, local copies, waits for them, and re-layouts  7.99 us
    pallas_call x4, Pallas kernels, add_rows(): pl.pallas_call(functools.partial(add_kernel, tiles, len(landed)), grid=(c...  7.66 us
    pallas_call x2, Pallas kernels, project_pair(): pl.pallas_call(pair_kernel, grid_spec=pltpu.PrefetchScalarGridSpec(num_sc...  7.06 us
    ppermute x15, waiting for transfers between devices, other_core(): return lax.ppermute(x, 'rep', [(0, 1), (1, 0)])  5.44 us
  transfers between devices with their start and end apart: 25, of which 10 were waited for; matrix products, arithmetic and copies ran while one was open for 4% of the time, Pallas kernels for 41%

profile of v3, /device:TPU:0, one launch (start us, length us, event | category | flops | bytes accessed | tf_op | source)
XLA Modules:
  0.0 178.9 jit_solution(8413078173698385662)
XLA Ops:
  0.6 3.0 %collective-permute-start.3 = (bf16[320,2048]{1,0:T(8,128)(2,1)}, bf16[320,2048]{1,0:T(8,128)(2,1)S(1)}, u32[]{:S(2)}, u32[]{:S(2)}) collective-permute-start(bf16[320,2048]{1,0:T(8,128)(2,1)} %x_ref.5), channel_id=1, source_target_pairs={{0,2},{2,0},{1,3},{3,1},{4,6},{6,4},{5,7},{7,5},{8,10},{10,8},{9,1... | collective-permute-start | bytes 3932168 | tf_op jit(solution)/shard_map/ppermute | solution.py:372
  3.7 1.3 copy-done
  5.0 10.0 %query_products.4 = (f32[2,160,2048]{2,1,0:T(8,128)S(1)}, bf16[2,160,1024]{2,1,0:T(8,128)(2,1)S(1)}, bf16[2,160,1024]{2,1,0:T(8,128)(2,1)S(1)}) custom-call(s32[3]{0:T(128)S(1)} %pad_add_fusion.2.place_ref, bf16[320,2048]{1,0:T(8,128)(2,1)S(1)} %copy-done, bf16[2048,8192]{1,0:T(8,128)(2,1)} %w_ref.7), custom_call_target="tpu_custom_call" | custom-call | flops 1000 | bytes 1000 | tf_op jit(solution)/shard_map/query_products/pallas_call | solution.py:63
  15.6 1.6 collective-permute-done.refs_1_
  17.2 0.9 collective-permute-done.1.refs_2_
  18.2 1.9 %add_rows.4.refs_0_ = bf16[2,160,2048]{2,1,0:T(8,128)(2,1)} custom-call(f32[2,160,2048]{2,1,0:T(8,128)S(1)} %get-tuple-element.27.refs_0_, bf16[2,160,1024]{2,1,0:T(8,128)(2,1)S(1)} %collective-permute-done.refs_1_, bf16[2,160,1024]{2,1,0:T(8,128)(2,1)S(1)} %collective-permute-done.1.refs_2_), custom_call_target="tpu_custom_call" | custom-call | flops 1000 | bytes 1000 | tf_op jit(solution)/shard_map/add_rows/pallas_call | solution.py:140
  20.0 1.6 collective-permute-start.8
  21.8 10.3 %query_products.5 = (f32[2,160,2048]{2,1,0:T(8,128)S(1)}, bf16[2,160,1024]{2,1,0:T(8,128)(2,1)S(1)}, bf16[2,160,1024]{2,1,0:T(8,128)(2,1)S(1)}) custom-call(s32[3]{0:T(128)S(1)} %pad_add_fusion.1.place_ref, bf16[320,2048]{1,0:T(8,128)(2,1)S(1)} %copy-done.1, bf16[2048,8192]{1,0:T(8,128)(2,1)} %w_ref.7, bf16[2,160,2048]{2,1,0:T(8,128)(2,1)} %add_rows.4.refs_0_), custom_call_target="tpu_custom_call" | custom-call | flops 1000 | bytes 1000 | tf_op jit(solution)/shard_map/query_products/pallas_call | solution.py:63
  32.1 1.5 copy-done.4
  33.6 0.9 copy-done.23
  34.4 3.5 %key_value_products.2 = (f32[4,160,256]{2,1,0:T(8,128)S(1)}, bf16[4,160,256]{2,1,0:T(8,128)(2,1)S(1)}) custom-call(s32[5]{0:T(128)S(1)} %stack.27.place_ref, bf16[320,2048]{1,0:T(8,128)(2,1)S(1)} %copy-done.1, bf16[2048,512]{1,0:T(8,128)(2,1)S(1)} %copy-done.7, bf16[2048,512]{1,0:T(8,128)(2,1)S(1)} %copy-done.9, ...), custom_call_target="tpu_custom_call" | custom-call | flops 1000 | bytes 1000 | tf_op jit(solution)/shard_map/key_value_products/pallas_call | solution.py:106
  38.0 11.1 %query_products.6 = (f32[2,160,2048]{2,1,0:T(8,128)S(1)}, bf16[2,160,1024]{2,1,0:T(8,128)(2,1)}, bf16[2,160,1024]{2,1,0:T(8,128)(2,1)S(1)}) custom-call(s32[3]{0:T(128)S(1)} %pad_add_fusion.2.place_ref, bf16[320,2048]{1,0:T(8,128)(2,1)S(1)} %collective-permute-done.3.x_ref, bf16[2048,8192]{1,0:T(8,128)(2,1)} %w_ref.7, ...), custom_call_target="tpu_custom_call" | custom-call | flops 1000 | bytes 1000 | tf_op jit(solution)/shard_map/query_products/pallas_call | solution.py:63
  49.1 1.5 copy-done.15
  50.6 0.9 copy-done.24
  51.7 0.5 collective-permute-start.6
  53.0 0.7 fusion.7
  54.0 2.6 %collective-permute-done.5.refs_2_ = bf16[2,160,1024]{2,1,0:T(8,128)(2,1)S(1)} collective-permute-done((bf16[2,160,1024]{2,1,0:T(8,128)(2,1)}, bf16[2,160,1024]{2,1,0:T(8,128)(2,1)S(1)}, u32[]{:S(2)}, u32[]{:S(2)}) %collective-permute-start.5) | collective-permute-done | bytes 655392 | tf_op jit(solution)/shard_map/ppermute | solution.py:345
  56.6 1.7 copy-done.16
  58.4 1.8 %add_rows.5.refs_4_.refs_0_ = bf16[2,160,2048]{2,1,0:T(8,128)(2,1)} custom-call(f32[2,160,2048]{2,1,0:T(8,128)S(1)} %copy-done.16, bf16[2,160,1024]{2,1,0:T(8,128)(2,1)S(1)} %collective-permute-done.4.refs_1_, bf16[2,160,1024]{2,1,0:T(8,128)(2,1)S(1)} %collective-permute-done.5.refs_2_), custom_call_target="tpu_custom_call" | custom-call | flops 1000 | bytes 1000 | tf_op jit(solution)/shard_map/add_rows/pallas_call | solution.py:140
  60.3 2.4 %add_rows.6.refs_1_ = bf16[1,160,2048]{2,1,0:T(8,128)(2,1)} custom-call(f32[2,160,2048]{2,1,0:T(8,128)S(1)} %copy-done.5, bf16[2,160,1024]{2,1,0:T(8,128)(2,1)S(1)} %collective-permute-done.6.refs_1_.refs_3_, bf16[2,160,1024]{2,1,0:T(8,128)(2,1)S(1)} %collective-permute-done.7.refs_2_.refs_4_, bf16[2,160,2048]{2,1,0:T(8,128)(2,1)} %collective-permute-done.8.refs_3_.refs_1_, ...), custom_call_target="tpu_custom_call" | custom-call | flops 1000 | bytes 1000 | tf_op jit(solution)/shard_map/add_rows/pallas_call | solution.py:140
  63.2 11.4 %query_products.7 = (f32[2,160,2048]{2,1,0:T(8,128)S(1)}, bf16[2,160,1024]{2,1,0:T(8,128)(2,1)}, bf16[2,160,1024]{2,1,0:T(8,128)(2,1)}) custom-call(s32[3]{0:T(128)S(1)} %pad_add_fusion.1.place_ref, bf16[320,2048]{1,0:T(8,128)(2,1)S(1)} %copy-done.3, bf16[2048,8192]{1,0:T(8,128)(2,1)} %w_ref.7, bf16[2,160,2048]{2,1,0:T(8,128)(2,1)} %add_rows.5.refs_4_.refs_0_, ...), custom_call_target="tpu_custom_call" | custom-call | flops 1000 | bytes 1000 | tf_op jit(solution)/shard_map/query_products/pallas_call | solution.py:63
  74.6 3.5 %key_value_products.3 = (f32[4,160,256]{2,1,0:T(8,128)S(1)}, bf16[4,160,256]{2,1,0:T(8,128)(2,1)S(1)}) custom-call(s32[5]{0:T(128)S(1)} %stack.27.place_ref, bf16[320,2048]{1,0:T(8,128)(2,1)S(1)} %copy-done.3, bf16[2048,512]{1,0:T(8,128)(2,1)S(1)} %copy-done.8, bf16[2048,512]{1,0:T(8,128)(2,1)S(1)} %copy-done.10, bf16[2,160,1024]{2,1,0:T(8,128)(2,1)} %get-tuple-element.38.refs_0_), custom_call_target="tpu_custom_call" | custom-call | flops 1000 | bytes 1000 | tf_op jit(solution)/shard_map/key_value_products/pallas_call | solution.py:106
  78.2 0.8 pad_maximum_fusion.3.sin_ref
  79.0 0.6 collective-permute-start.12
  79.9 0.9 slice.30
  80.9 1.6 collective-permute-start.10
  82.4 0.7 fusion.4
  83.2 2.6 %collective-permute-start.16 = (bf16[1,160,2048]{2,1,0:T(8,128)(2,1)}, bf16[1,160,2048]{2,1,0:T(8,128)(2,1)}, u32[]{:S(2)}, u32[]{:S(2)}) collective-permute-start(bf16[1,160,2048]{2,1,0:T(8,128)(2,1)} %add_rows.6.refs_1_), channel_id=1, source_target_pairs={{0,8},{4,12},{8,0},{12,4},{1,9},{5,13},{9,1},{13,5},{2,10},{6,14},... | collective-permute-start | bytes 1966088 | tf_op jit(solution)/shard_map/ppermute | solution.py:342
  85.9 0.9 reshape.81.canary_ref
  86.8 1.1 fusion.6
  88.0 26.9 %collective-permute-done.10.refs_1_ = bf16[2,320,256]{2,1,0:T(8,128)(2,1)} collective-permute-done((bf16[2,320,256]{2,1,0:T(8,128)(2,1)}, bf16[2,320,256]{2,1,0:T(8,128)(2,1)}, u32[]{:S(2)}, u32[]{:S(2)}) %collective-permute-start.10) | collective-permute-done | bytes 327712 | tf_op jit(solution)/shard_map/ppermute | solution.py:342
  114.9 1.1 fusion.2.refs_4_
  116.3 1.6 add_rows.7
  118.0 2.8 %collective-permute-start.18 = (bf16[1,160,1024]{2,1,0:T(8,128)(2,1)S(1)}, bf16[1,160,1024]{2,1,0:T(8,128)(2,1)S(1)}, u32[]{:S(2)}, u32[]{:S(2)}) collective-permute-start(bf16[1,160,1024]{2,1,0:T(8,128)(2,1)S(1)} %get-tuple-element.52), channel_id=1, source_target_pairs={{0,8},{4,12},{8,0},{12,4},{1,9},{5,13},{9,1},{13,5},{2,10},{6,14},... | collective-permute-start | bytes 983048 | tf_op jit(solution)/shard_map/ppermute | solution.py:342
  120.8 2.3 %sum_and_rotate.3.refs_0_ = bf16[160,2048]{1,0:T(8,128)(2,1)S(1)} custom-call(f32[160,128]{1,0:T(8,128)S(1)} %get-tuple-element.57.cos_ref, f32[160,128]{1,0:T(8,128)S(1)} %copy-done.22, f32[2,160,2048]{2,1,0:T(8,128)S(1)} %copy-done.6, bf16[2,160,2048]{2,1,0:T(8,128)(2,1)} %collective-permute-done.8.refs_3_.refs_1_, ...), custom_call_target="tpu_custom_call" | custom-call | flops 1000 | bytes 1000 | tf_op jit(solution)/shard_map/sum_and_rotate/pallas_call | solution.py:187
  123.3 9.1 %collective-permute-done.11.refs_2_ = bf16[1,320,256]{2,1,0:T(8,128)(2,1)S(1)} collective-permute-done((bf16[1,320,256]{2,1,0:T(8,128)(2,1)S(1)}, bf16[1,320,256]{2,1,0:T(8,128)(2,1)S(1)}, u32[]{:S(2)}, u32[]{:S(2)}) %collective-permute-start.11) | collective-permute-done | bytes 163872 | tf_op jit(solution)/shard_map/ppermute | solution.py:342
  132.5 1.0 split_and_rotate.1
  133.7 2.3 %collective-permute-start.17 = (bf16[1,160,1024]{2,1,0:T(8,128)(2,1)S(1)}, bf16[1,160,1024]{2,1,0:T(8,128)(2,1)S(1)}, u32[]{:S(2)}, u32[]{:S(2)}) collective-permute-start(bf16[1,160,1024]{2,1,0:T(8,128)(2,1)S(1)} %get-tuple-element.53.refs_3_.refs_5_), channel_id=1, source_target_pairs={{0,8},{4,12},{8,0},{12,4},{1,9},{5,13},{9,1},{13,5},{2,10},{6,14},... | collective-permute-start | bytes 983048 | tf_op jit(solution)/shard_map/ppermute | solution.py:342
  136.0 4.1 %collective-permute-done.22 = bf16[1,320,128]{2,1,0:T(8,128)(2,1)S(1)} collective-permute-done((bf16[1,320,128]{2,1,0:T(8,128)(2,1)S(1)}, bf16[1,320,128]{2,1,0:T(8,128)(2,1)S(1)}, u32[]{:S(2)}, u32[]{:S(2)}) %collective-permute-start.22) | collective-permute-done | bytes 81952 | tf_op jit(solution)/shard_map/ppermute | solution.py:342
  140.2 0.6 order_and_keys.1
  140.8 9.3 %collective-permute-done.18.refs_2_ = bf16[1,160,1024]{2,1,0:T(8,128)(2,1)S(1)} collective-permute-done((bf16[1,160,1024]{2,1,0:T(8,128)(2,1)S(1)}, bf16[1,160,1024]{2,1,0:T(8,128)(2,1)S(1)}, u32[]{:S(2)}, u32[]{:S(2)}) %collective-permute-start.18) | collective-permute-done | bytes 327712 | tf_op jit(solution)/shard_map/ppermute | solution.py:342
  150.1 1.4 sum_and_rotate.4.refs_1_
  151.6 8.9 %collective-permute-done.23 = bf16[2,320,128]{2,1,0:T(8,128)(2,1)S(1)} collective-permute-done((bf16[2,320,128]{2,1,0:T(8,128)(2,1)S(1)}, bf16[2,320,128]{2,1,0:T(8,128)(2,1)S(1)}, u32[]{:S(2)}, u32[]{:S(2)}) %collective-permute-start.23) | collective-permute-done | bytes 163872 | tf_op jit(solution)/shard_map/ppermute | solution.py:342
  160.6 6.6 %score_heads.2 = (bf16[1,16,640,640]{3,2,1,0:T(8,128)(2,1)}, f32[8,128]{1,0:T(8,128)S(1)}) custom-call(bf16[640,640]{1,0:T(8,128)(2,1)S(1)} %get-tuple-element.44.order_ref, bf16[128,640]{1,0:T(8,128)(2,1)S(1)} %get-tuple-element.45.refs_4_.key_t_ref, bf16[160,2048]{1,0:T(8,128)(2,1)S(1)} %sum_and_rotate.3.refs_0_, ...), custom_call_target="tpu_custom_call" | custom-call | flops 1000 | bytes 1000 | tf_op jit(solution)/shard_map/score_heads/pallas_call | solution.py:303
  167.2 1.3 sum_and_rotate.5.refs_1_
  168.6 0.5 collective-permute-start.21
  169.2 3.1 %order_values.1 = (bf16[640,512]{1,0:T(8,128)(2,1)}, f32[8,128]{1,0:T(8,128)S(1)}) custom-call(s32[4]{0:T(128)S(1)} %pad_add_fusion.3.place_ref, bf16[640,640]{1,0:T(8,128)(2,1)S(1)} %get-tuple-element.44.order_ref, bf16[4,320,128]{2,1,0:T(8,128)(2,1)S(1)} %constant_dynamic-update-slice_fusion.own_ref, bf16[4,320,128]{2,1,0:T(8,128)(2,1)S(1)} %collective-permute-done.24.other_ref), custom_call_target="tpu_custom_call" | custom-call | tf_op jit(solution)/shard_map/order_values/pallas_call | solution.py:264
  172.2 6.6 %score_heads.3 = (bf16[1,16,640,640]{3,2,1,0:T(8,128)(2,1)}, f32[8,128]{1,0:T(8,128)}) custom-call(bf16[640,640]{1,0:T(8,128)(2,1)S(1)} %get-tuple-element.44.order_ref, bf16[128,640]{1,0:T(8,128)(2,1)S(1)} %get-tuple-element.45.refs_4_.key_t_ref, bf16[160,2048]{1,0:T(8,128)(2,1)S(1)} %sum_and_rotate.3.refs_0_, ...), custom_call_target="tpu_custom_call", output_to_operand_aliasing={{0}: (6, {})} | custom-call | flops 1000 | bytes 1000 | tf_op jit(solution)/shard_map/score_heads/pallas_call | solution.py:303
  (115 shorter events, 4.5 us)
Async XLA Ops:
  0.6 37.4 %collective-permute-start.3 = (bf16[320,2048]{1,0:T(8,128)(2,1)}, bf16[320,2048]{1,0:T(8,128)(2,1)S(1)}, u32[]{:S(2)}, u32[]{:S(2)}) collective-permute-start(bf16[320,2048]{1,0:T(8,128)(2,1)} %x_ref.5), channel_id=1, source_target_pairs={{0,2},{2,0},{1,3},{3,1},{4,6},{6,4},{5,7},{7,5},{8,10},{10,8},{9,1... | collective-permute-start | bytes 3932168 | tf_op jit(solution)/shard_map/ppermute | solution.py:372
  15.1 2.2 %collective-permute-start = (bf16[2,160,1024]{2,1,0:T(8,128)(2,1)S(1)}, bf16[2,160,1024]{2,1,0:T(8,128)(2,1)S(1)}, u32[]{:S(2)}, u32[]{:S(2)}) collective-permute-start(bf16[2,160,1024]{2,1,0:T(8,128)(2,1)S(1)} %get-tuple-element.28), channel_id=1, source_target_pairs={{0,1},{1,0},{2,3},{3,2},{4,5},{5,4},{6,7},{7,6},{8,9},{9,8},{10,11... | collective-permute-start | bytes 1966088 | tf_op jit(solution)/shard_map/ppermute | solution.py:345
  15.1 3.0 %collective-permute-start.1 = (bf16[2,160,1024]{2,1,0:T(8,128)(2,1)S(1)}, bf16[2,160,1024]{2,1,0:T(8,128)(2,1)S(1)}, u32[]{:S(2)}, u32[]{:S(2)}) collective-permute-start(bf16[2,160,1024]{2,1,0:T(8,128)(2,1)S(1)} %get-tuple-element.29), channel_id=1, source_target_pairs={{0,1},{1,0},{2,3},{3,2},{4,5},{5,4},{6,7},{7,6},{8,9},{9,8},{10,11... | collective-permute-start | bytes 1966088 | tf_op jit(solution)/shard_map/ppermute | solution.py:345
  18.2 3.6 %copy-start.1 = (bf16[320,2048]{1,0:T(8,128)(2,1)S(1)}, bf16[320,2048]{1,0:T(8,128)(2,1)}, u32[]{:S(2)}) copy-start(bf16[320,2048]{1,0:T(8,128)(2,1)} %x_ref.5) | copy-start | bytes 3932164
  20.0 40.2 %collective-permute-start.8 = (bf16[2,160,2048]{2,1,0:T(8,128)(2,1)}, bf16[2,160,2048]{2,1,0:T(8,128)(2,1)}, u32[]{:S(2)}, u32[]{:S(2)}) collective-permute-start(bf16[2,160,2048]{2,1,0:T(8,128)(2,1)} %add_rows.4.refs_0_), channel_id=1, source_target_pairs={{0,4},{4,0},{8,12},{12,8},{1,5},{5,1},{9,13},{13,9},{2,6},{6,2},{1... | collective-permute-start | bytes 3932168 | tf_op jit(solution)/shard_map/ppermute | solution.py:342
  21.8 12.6 %copy-start.7 = (bf16[2048,512]{1,0:T(8,128)(2,1)S(1)}, bf16[2048,512]{1,0:T(8,128)(2,1)}, u32[]{:S(2)}) copy-start(bf16[2048,512]{1,0:T(8,128)(2,1)} %wk_ref.3) | copy-start | bytes 6291460
  21.8 12.6 %copy-start.9 = (bf16[2048,512]{1,0:T(8,128)(2,1)S(1)}, bf16[2048,512]{1,0:T(8,128)(2,1)}, u32[]{:S(2)}) copy-start(bf16[2048,512]{1,0:T(8,128)(2,1)} %wv_ref.3) | copy-start | bytes 6291460
  34.4 3.5 %copy-start.19 = (bf16[2,160,1024]{2,1,0:T(8,128)(2,1)}, bf16[2,160,1024]{2,1,0:T(8,128)(2,1)S(1)}, u32[]{:S(2)}) copy-start(bf16[2,160,1024]{2,1,0:T(8,128)(2,1)S(1)} %get-tuple-element.30.refs_0_) | copy-start | bytes 1966084
  38.0 11.1 %copy-start.21 = (bf16[4,160,256]{2,1,0:T(8,128)(2,1)}, bf16[4,160,256]{2,1,0:T(8,128)(2,1)S(1)}, u32[]{:S(2)}) copy-start(bf16[4,160,256]{2,1,0:T(8,128)(2,1)S(1)} %get-tuple-element.32.refs_0_) | copy-start | bytes 983044
  38.0 11.1 %copy-start.2 = (bf16[320,2048]{1,0:T(8,128)(2,1)}, bf16[320,2048]{1,0:T(8,128)(2,1)S(1)}, u32[]{:S(2)}) copy-start(bf16[320,2048]{1,0:T(8,128)(2,1)S(1)} %collective-permute-done.3.x_ref) | copy-start | bytes 3932164
  38.0 13.6 %copy-start.20 = (bf16[2,160,1024]{2,1,0:T(8,128)(2,1)S(1)}, bf16[2,160,1024]{2,1,0:T(8,128)(2,1)}, u32[]{:S(2)}) copy-start(bf16[2,160,1024]{2,1,0:T(8,128)(2,1)} %copy-done.19) | copy-start | bytes 1966084
  38.0 14.7 %copy-start.30 = (s32[640]{0:T(1024)S(1)}, s32[640]{0:T(1024)}, u32[]{:S(2)}) copy-start(s32[640]{0:T(1024)} %param.10) | copy-start | bytes 7684
  38.0 14.7 %copy-start.31 = (s32[640]{0:T(1024)S(1)}, s32[640]{0:T(1024)}, u32[]{:S(2)}) copy-start(s32[640]{0:T(1024)} %param.11) | copy-start | bytes 7684
  51.5 2.3 %collective-permute-start.4 = (bf16[2,160,1024]{2,1,0:T(8,128)(2,1)}, bf16[2,160,1024]{2,1,0:T(8,128)(2,1)S(1)}, u32[]{:S(2)}, u32[]{:S(2)}) collective-permute-start(bf16[2,160,1024]{2,1,0:T(8,128)(2,1)} %get-tuple-element.34), channel_id=1, source_target_pairs={{0,1},{1,0},{2,3},{3,2},{4,5},{5,4},{6,7},{7,6},{8,9},{9,8},{10,11... | collective-permute-start | bytes 1966088 | tf_op jit(solution)/shard_map/ppermute | solution.py:345
  51.7 8.6 %collective-permute-start.6 = (bf16[2,160,1024]{2,1,0:T(8,128)(2,1)S(1)}, bf16[2,160,1024]{2,1,0:T(8,128)(2,1)S(1)}, u32[]{:S(2)}, u32[]{:S(2)}) collective-permute-start(bf16[2,160,1024]{2,1,0:T(8,128)(2,1)S(1)} %copy-done.20), channel_id=1, source_target_pairs={{0,1},{1,0},{2,3},{3,2},{4,5},{5,4},{6,7},{7,6},{8,9},{9,8},{10,11... | collective-permute-start | bytes 1966088 | tf_op jit(solution)/shard_map/ppermute | solution.py:345
  52.2 8.0 %collective-permute-start.7 = (bf16[2,160,1024]{2,1,0:T(8,128)(2,1)}, bf16[2,160,1024]{2,1,0:T(8,128)(2,1)S(1)}, u32[]{:S(2)}, u32[]{:S(2)}) collective-permute-start(bf16[2,160,1024]{2,1,0:T(8,128)(2,1)} %copy-done.23), channel_id=1, source_target_pairs={{0,1},{1,0},{2,3},{3,2},{4,5},{5,4},{6,7},{7,6},{8,9},{9,8},{10,11... | collective-permute-start | bytes 1966088 | tf_op jit(solution)/shard_map/ppermute | solution.py:345
  52.2 4.4 %collective-permute-start.5 = (bf16[2,160,1024]{2,1,0:T(8,128)(2,1)}, bf16[2,160,1024]{2,1,0:T(8,128)(2,1)S(1)}, u32[]{:S(2)}, u32[]{:S(2)}) collective-permute-start(bf16[2,160,1024]{2,1,0:T(8,128)(2,1)} %copy-done.24), channel_id=1, source_target_pairs={{0,1},{1,0},{2,3},{3,2},{4,5},{5,4},{6,7},{7,6},{8,9},{9,8},{10,11... | collective-permute-start | bytes 1966088 | tf_op jit(solution)/shard_map/ppermute | solution.py:345
  53.6 32.1 %copy-start.29 = (f32[320,64]{1,0:T(8,128)}, f32[320,64]{1,0:T(8,128)S(1)}, u32[]{:S(2)}) copy-start(f32[320,64]{1,0:T(8,128)S(1)} %get-tuple-element.60) | copy-start | bytes 245764
  53.8 25.1 %collective-permute-start.2 = (bf16[4,160,256]{2,1,0:T(8,128)(2,1)}, bf16[4,160,256]{2,1,0:T(8,128)(2,1)S(1)}, u32[]{:S(2)}, u32[]{:S(2)}) collective-permute-start(bf16[4,160,256]{2,1,0:T(8,128)(2,1)} %copy-done.21), channel_id=1, source_target_pairs={{0,1},{1,0},{2,3},{3,2},{4,5},{5,4},{6,7},{7,6},{8,9},{9,8},{10,11... | collective-permute-start | bytes 983048 | tf_op jit(solution)/shard_map/ppermute | solution.py:345
  60.2 2.5 %copy-start.13 = (bf16[2,160,1024]{2,1,0:T(8,128)(2,1)}, bf16[2,160,1024]{2,1,0:T(8,128)(2,1)S(1)}, u32[]{:S(2)}) copy-start(bf16[2,160,1024]{2,1,0:T(8,128)(2,1)S(1)} %collective-permute-done.7.refs_2_.refs_4_) | copy-start | bytes 1966084
  60.2 2.5 %copy-start.11 = (bf16[2,160,1024]{2,1,0:T(8,128)(2,1)}, bf16[2,160,1024]{2,1,0:T(8,128)(2,1)S(1)}, u32[]{:S(2)}) copy-start(bf16[2,160,1024]{2,1,0:T(8,128)(2,1)S(1)} %collective-permute-done.6.refs_1_.refs_3_) | copy-start | bytes 1966084
  60.3 2.8 %copy-start.3 = (bf16[320,2048]{1,0:T(8,128)(2,1)S(1)}, bf16[320,2048]{1,0:T(8,128)(2,1)}, u32[]{:S(2)}) copy-start(bf16[320,2048]{1,0:T(8,128)(2,1)} %copy-done.2) | copy-start | bytes 3932164
  62.7 53.6 %collective-permute-start.14 = (bf16[2,160,2048]{2,1,0:T(8,128)(2,1)}, bf16[2,160,2048]{2,1,0:T(8,128)(2,1)}, u32[]{:S(2)}, u32[]{:S(2)}) collective-permute-start(bf16[2,160,2048]{2,1,0:T(8,128)(2,1)} %add_rows.5.refs_4_.refs_0_), channel_id=1, source_target_pairs={{0,4},{4,0},{8,12},{12,8},{1,5},{5,1},{9,13},{13,9},{2,6},{6,2},{1... | collective-permute-start | bytes 3932168 | tf_op jit(solution)/shard_map/ppermute | solution.py:342
  63.2 11.4 %copy-start.8 = (bf16[2048,512]{1,0:T(8,128)(2,1)S(1)}, bf16[2048,512]{1,0:T(8,128)(2,1)}, u32[]{:S(2)}) copy-start(bf16[2048,512]{1,0:T(8,128)(2,1)} %wk_ref.3) | copy-start | bytes 6291460
  63.2 11.4 %copy-start.10 = (bf16[2048,512]{1,0:T(8,128)(2,1)S(1)}, bf16[2048,512]{1,0:T(8,128)(2,1)}, u32[]{:S(2)}) copy-start(bf16[2048,512]{1,0:T(8,128)(2,1)} %wv_ref.3) | copy-start | bytes 6291460
  78.1 1.7 collective-permute-start.9
  79.0 6.7 %copy-start.25 = (f32[4,160,256]{2,1,0:T(8,128)}, f32[4,160,256]{2,1,0:T(8,128)S(1)}, u32[]{:S(2)}) copy-start(f32[4,160,256]{2,1,0:T(8,128)S(1)} %convert_add_fusion.1) | copy-start | bytes 1966084
  79.0 37.2 %collective-permute-start.12 = (bf16[2,160,1024]{2,1,0:T(8,128)(2,1)}, bf16[2,160,1024]{2,1,0:T(8,128)(2,1)}, u32[]{:S(2)}, u32[]{:S(2)}) collective-permute-start(bf16[2,160,1024]{2,1,0:T(8,128)(2,1)} %get-tuple-element.38.refs_0_), channel_id=1, source_target_pairs={{0,1},{1,0},{2,3},{3,2},{4,5},{5,4},{6,7},{7,6},{8,9},{9,8},{10,11... | collective-permute-start | bytes 1966088 | tf_op jit(solution)/shard_map/ppermute | solution.py:345
  79.6 36.7 %collective-permute-start.13 = (bf16[2,160,1024]{2,1,0:T(8,128)(2,1)}, bf16[2,160,1024]{2,1,0:T(8,128)(2,1)S(1)}, u32[]{:S(2)}, u32[]{:S(2)}) collective-permute-start(bf16[2,160,1024]{2,1,0:T(8,128)(2,1)} %get-tuple-element.42), channel_id=1, source_target_pairs={{0,1},{1,0},{2,3},{3,2},{4,5},{5,4},{6,7},{7,6},{8,9},{9,8},{10,11... | collective-permute-start | bytes 1966088 | tf_op jit(solution)/shard_map/ppermute | solution.py:345
  79.9 3.3 %copy-start.27 = (f32[4,160,256]{2,1,0:T(8,128)}, f32[4,160,256]{2,1,0:T(8,128)S(1)}, u32[]{:S(2)}) copy-start(f32[4,160,256]{2,1,0:T(8,128)S(1)} %convert_add_fusion) | copy-start | bytes 1966084
  80.9 34.0 %collective-permute-start.10 = (bf16[2,320,256]{2,1,0:T(8,128)(2,1)}, bf16[2,320,256]{2,1,0:T(8,128)(2,1)}, u32[]{:S(2)}, u32[]{:S(2)}) collective-permute-start(bf16[2,320,256]{2,1,0:T(8,128)(2,1)} %slice.30), channel_id=1, source_target_pairs={{0,4},{4,0},{8,12},{12,8},{1,5},{5,1},{9,13},{13,9},{2,6},{6,2},{1... | collective-permute-start | bytes 983048 | tf_op jit(solution)/shard_map/ppermute | solution.py:342
  83.2 37.6 %collective-permute-start.16 = (bf16[1,160,2048]{2,1,0:T(8,128)(2,1)}, bf16[1,160,2048]{2,1,0:T(8,128)(2,1)}, u32[]{:S(2)}, u32[]{:S(2)}) collective-permute-start(bf16[1,160,2048]{2,1,0:T(8,128)(2,1)} %add_rows.6.refs_1_), channel_id=1, source_target_pairs={{0,8},{4,12},{8,0},{12,4},{1,9},{5,13},{9,1},{13,5},{2,10},{6,14},... | collective-permute-start | bytes 1966088 | tf_op jit(solution)/shard_map/ppermute | solution.py:342
  116.0 16.5 %collective-permute-start.11 = (bf16[1,320,256]{2,1,0:T(8,128)(2,1)S(1)}, bf16[1,320,256]{2,1,0:T(8,128)(2,1)S(1)}, u32[]{:S(2)}, u32[]{:S(2)}) collective-permute-start(bf16[1,320,256]{2,1,0:T(8,128)(2,1)S(1)} %fusion.2.refs_4_), channel_id=1, source_target_pairs={{0,8},{4,12},{8,0},{12,4},{1,9},{5,13},{9,1},{13,5},{2,10},{6,14},... | collective-permute-start | bytes 491528 | tf_op jit(solution)/shard_map/ppermute | solution.py:342
  116.3 4.5 %copy-start.6 = (f32[2,160,2048]{2,1,0:T(8,128)S(1)}, f32[2,160,2048]{2,1,0:T(8,128)}, u32[]{:S(2)}) copy-start(f32[2,160,2048]{2,1,0:T(8,128)} %copy-done.4) | copy-start | bytes 7864324
  116.3 4.5 %copy-start.22 = (f32[160,128]{1,0:T(8,128)S(1)}, f32[160,128]{1,0:T(8,128)}, u32[]{:S(2)}) copy-start(f32[160,128]{1,0:T(8,128)} %get-tuple-element.55.sin_ref) | copy-start | bytes 245764
  117.9 2.9 %copy-start.12 = (bf16[2,160,1024]{2,1,0:T(8,128)(2,1)S(1)}, bf16[2,160,1024]{2,1,0:T(8,128)(2,1)}, u32[]{:S(2)}) copy-start(bf16[2,160,1024]{2,1,0:T(8,128)(2,1)} %copy-done.11) | copy-start | bytes 1966084
  117.9 2.9 %copy-start.14 = (bf16[2,160,1024]{2,1,0:T(8,128)(2,1)S(1)}, bf16[2,160,1024]{2,1,0:T(8,128)(2,1)}, u32[]{:S(2)}) copy-start(bf16[2,160,1024]{2,1,0:T(8,128)(2,1)} %copy-done.13) | copy-start | bytes 1966084
  118.0 32.1 %collective-permute-start.18 = (bf16[1,160,1024]{2,1,0:T(8,128)(2,1)S(1)}, bf16[1,160,1024]{2,1,0:T(8,128)(2,1)S(1)}, u32[]{:S(2)}, u32[]{:S(2)}) collective-permute-start(bf16[1,160,1024]{2,1,0:T(8,128)(2,1)S(1)} %get-tuple-element.52), channel_id=1, source_target_pairs={{0,8},{4,12},{8,0},{12,4},{1,9},{5,13},{9,1},{13,5},{2,10},{6,14},... | collective-permute-start | bytes 983048 | tf_op jit(solution)/shard_map/ppermute | solution.py:342
  123.1 9.4 %copy-start.18 = (f32[320,128]{1,0:T(8,128)S(1)}, f32[320,128]{1,0:T(8,128)}, u32[]{:S(2)}) copy-start(f32[320,128]{1,0:T(8,128)} %pad_maximum_fusion.3.sin_ref) | copy-start | bytes 491524
  123.1 37.5 %collective-permute-start.19 = (bf16[160,2048]{1,0:T(8,128)(2,1)S(1)}, bf16[160,2048]{1,0:T(8,128)(2,1)S(1)}, u32[]{:S(2)}, u32[]{:S(2)}) collective-permute-start(bf16[160,2048]{1,0:T(8,128)(2,1)S(1)} %sum_and_rotate.3.refs_0_), channel_id=1, source_target_pairs={{0,1},{1,0},{2,3},{3,2},{4,5},{5,4},{6,7},{7,6},{8,9},{9,8},{10,11... | collective-permute-start | bytes 1966088 | tf_op jit(solution)/shard_map/ppermute | solution.py:345
  123.3 16.9 %copy-start.17 = (s32[640,1]{1,0:T(8,128)S(1)}, s32[640,1]{1,0:T(8,128)}, u32[]{:S(2)}) copy-start(s32[640,1]{1,0:T(8,128)} %reshape.81.canary_ref) | copy-start | bytes 7684
  133.5 6.6 %collective-permute-start.22 = (bf16[1,320,128]{2,1,0:T(8,128)(2,1)S(1)}, bf16[1,320,128]{2,1,0:T(8,128)(2,1)S(1)}, u32[]{:S(2)}, u32[]{:S(2)}) collective-permute-start(bf16[1,320,128]{2,1,0:T(8,128)(2,1)S(1)} %get-tuple-element.48), channel_id=1, source_target_pairs={{0,4},{4,0},{8,12},{12,8},{1,5},{5,1},{9,13},{13,9},{2,6},{6,2},{1... | collective-permute-start | bytes 245768 | tf_op jit(solution)/shard_map/ppermute | solution.py:342
  133.7 33.6 %collective-permute-start.17 = (bf16[1,160,1024]{2,1,0:T(8,128)(2,1)S(1)}, bf16[1,160,1024]{2,1,0:T(8,128)(2,1)S(1)}, u32[]{:S(2)}, u32[]{:S(2)}) collective-permute-start(bf16[1,160,1024]{2,1,0:T(8,128)(2,1)S(1)} %get-tuple-element.53.refs_3_.refs_5_), channel_id=1, source_target_pairs={{0,8},{4,12},{8,0},{12,4},{1,9},{5,13},{9,1},{13,5},{2,10},{6,14},... | collective-permute-start | bytes 983048 | tf_op jit(solution)/shard_map/ppermute | solution.py:342
  136.0 4.2 %collective-permute-start.15 = (bf16[320,128]{1,0:T(8,128)(2,1)S(1)}, bf16[320,128]{1,0:T(8,128)(2,1)S(1)}, u32[]{:S(2)}, u32[]{:S(2)}) collective-permute-start(bf16[320,128]{1,0:T(8,128)(2,1)S(1)} %get-tuple-element.43.own_ref), channel_id=1, source_target_pairs={{0,1},{1,0},{2,3},{3,2},{4,5},{5,4},{6,7},{7,6},{8,9},{9,8},{10,11... | collective-permute-start | bytes 245768 | tf_op jit(solution)/shard_map/ppermute | solution.py:345
  140.1 20.4 %collective-permute-start.23 = (bf16[2,320,128]{2,1,0:T(8,128)(2,1)S(1)}, bf16[2,320,128]{2,1,0:T(8,128)(2,1)S(1)}, u32[]{:S(2)}, u32[]{:S(2)}) collective-permute-start(bf16[2,320,128]{2,1,0:T(8,128)(2,1)S(1)} %pad_maximum_fusion.1), channel_id=1, source_target_pairs={{0,8},{4,12},{8,0},{12,4},{1,9},{5,13},{9,1},{13,5},{2,10},{6,14},... | collective-permute-start | bytes 491528 | tf_op jit(solution)/shard_map/ppermute | solution.py:342
  151.5 9.1 %collective-permute-start.20 = (bf16[160,1024]{1,0:T(8,128)(2,1)S(1)}, bf16[160,1024]{1,0:T(8,128)(2,1)S(1)}, u32[]{:S(2)}, u32[]{:S(2)}) collective-permute-start(bf16[160,1024]{1,0:T(8,128)(2,1)S(1)} %sum_and_rotate.4.refs_1_), channel_id=1, source_target_pairs={{0,1},{1,0},{2,3},{3,2},{4,5},{5,4},{6,7},{7,6},{8,9},{9,8},{10,11... | collective-permute-start | bytes 983048 | tf_op jit(solution)/shard_map/ppermute | solution.py:345
  160.5 8.6 %collective-permute-start.24 = (bf16[4,320,128]{2,1,0:T(8,128)(2,1)S(1)}, bf16[4,320,128]{2,1,0:T(8,128)(2,1)S(1)}, u32[]{:S(2)}, u32[]{:S(2)}) collective-permute-start(bf16[4,320,128]{2,1,0:T(8,128)(2,1)S(1)} %constant_dynamic-update-slice_fusion.own_ref), channel_id=1, source_target_pairs={{0,1},{1,0},{2,3},{3,2},{4,5},{5,4},{6,7},{7,6},{8,9},{9,8},{10,11... | collective-permute-start | bytes 983048 | tf_op jit(solution)/shard_map/ppermute | solution.py:345
  168.6 3.7 %collective-permute-start.21 = (bf16[160,1024]{1,0:T(8,128)(2,1)S(1)}, bf16[160,1024]{1,0:T(8,128)(2,1)S(1)}, u32[]{:S(2)}, u32[]{:S(2)}) collective-permute-start(bf16[160,1024]{1,0:T(8,128)(2,1)S(1)} %sum_and_rotate.5.refs_1_), channel_id=1, source_target_pairs={{0,1},{1,0},{2,3},{3,2},{4,5},{5,4},{6,7},{7,6},{8,9},{9,8},{10,11... | collective-permute-start | bytes 983048 | tf_op jit(solution)/shard_map/ppermute | solution.py:345
  (9 other events, 14.6 us)

commit v4 on v3

--- a/solution.py
+++ b/solution.py
@@ -11,8 +11,13 @@
 HQ = 128
 KV = 8
 DH = 128
-VMEM_BYTES = 26 * 1024 * 1024
+VMEM_BYTES = 28 * 1024 * 1024
 LIGHT = pl.CostEstimate(flops=1000, bytes_accessed=1000, transcendentals=0)
+HEAVY = pl.CostEstimate(flops=10**11, bytes_accessed=10**8, transcendentals=0)
+
+
+def in_hbm(arrays):
+    return [pltpu.with_memory_space_constraint(x, pltpu.HBM) for x in arrays]
 
 
 def rope_tables(positions):
@@ -28,21 +33,24 @@
     return jnp.concatenate([cosine, cosine], axis=1), jnp.concatenate([-sine, sine], axis=1)
 
 
-def ordered_rows(place_ref, x_ref, rows_ref):
-    half = x_ref.shape[0] // 2
+def ordered_rows(place_ref, x_refs, rows_ref):
     core = place_ref[0]
-    rows_ref[:half] = x_ref[pl.ds(pl.multiple_of(core * half, 16), half)]
-    rows_ref[half:] = x_ref[pl.ds(pl.multiple_of((1 - core) * half, 16), half)]
-
-
-def query_kernel(pieces, width, place_ref, x_ref, w_ref, *refs):
+    half = x_refs[0].shape[0] // 2
+    for b, x_ref in enumerate(x_refs):
+        kept, given = b * half, (len(x_refs) + b) * half
+        rows_ref[kept : kept + half] = x_ref[pl.ds(pl.multiple_of(core * half, 16), half)]
+        rows_ref[given : given + half] = x_ref[pl.ds(pl.multiple_of((1 - core) * half, 16), half)]
+
+
+def query_kernel(count, pieces, width, place_ref, *refs):
+    x_refs, w_ref = refs[:count], refs[count]
     keep_ref, *give_refs, rows_ref = refs[-2 - pieces :]
     tile = pl.program_id(1)
     each = keep_ref.shape[2] // width
 
     @pl.when((pl.program_id(0) == 0) & (tile == 0))
     def _():
-        ordered_rows(place_ref, x_ref, rows_ref)
+        ordered_rows(place_ref, x_refs, rows_ref)
 
     result = jnp.dot(rows_ref[...], w_ref[...], preferred_element_type=jnp.float32)
     half = result.shape[0] // 2
@@ -55,101 +63,136 @@
             give_ref[0] = result[half:, start : start + width].astype(give_ref.dtype)
 
 
-def project_query(rindex, findex, slots, x, w, cols, tile, width, after=()):
-    rows, depth = x.shape
-    tiles = cols // tile
+def project_query(rindex, findex, slots, blocks, w, cols, tile, width, after, cost):
+    rows, depth = blocks[0].shape
+    count = len(blocks)
+    half = rows // 2 * count
+    tiles, pieces = cols // tile, cols // width
     place = jnp.stack([rindex] + [findex ^ slot for slot in slots]).astype(jnp.int32)
-    pieces = cols // width
+    x_spec = pl.BlockSpec((rows, depth), lambda s, j, place: (0, 0), pipeline_mode=pl.Buffered(1))
     outs = pl.pallas_call(
-        functools.partial(query_kernel, pieces, width),
+        functools.partial(query_kernel, count, pieces, width),
         grid_spec=pltpu.PrefetchScalarGridSpec(
             num_scalar_prefetch=1,
             grid=(len(slots), tiles),
-            in_specs=[
-                pl.BlockSpec((rows, depth), lambda s, j, place: (0, 0)),
-                pl.BlockSpec((depth, tile), lambda s, j, place: (0, place[1 + s] * tiles + j)),
-            ]
+            in_specs=[x_spec] * count
+            + [pl.BlockSpec((depth, tile), lambda s, j, place: (0, place[1 + s] * tiles + j))]
             + [pl.BlockSpec(memory_space=pl.ANY)] * len(after),
-            out_specs=[pl.BlockSpec((1, rows // 2, tile), lambda s, j, place: (s, 0, j))]
-            + [pl.BlockSpec((1, rows // 2, width), lambda s, j, place: (s, 0, 0))] * pieces,
-            scratch_shapes=[pltpu.VMEM((rows, depth), x.dtype)],
+            out_specs=[pl.BlockSpec((1, half, tile), lambda s, j, place: (s, 0, j))]
+            + [pl.BlockSpec((1, half, width), lambda s, j, place: (s, 0, 0))] * pieces,
+            scratch_shapes=[pltpu.VMEM((2 * half, depth), w.dtype)],
         ),
-        out_shape=[jax.ShapeDtypeStruct((len(slots), rows // 2, cols), jnp.float32)]
-        + [jax.ShapeDtypeStruct((len(slots), rows // 2, width), jnp.bfloat16)] * pieces,
-        compiler_params=pltpu.CompilerParams(vmem_limit_bytes=VMEM_BYTES),
-        cost_estimate=LIGHT,
+        out_shape=[pltpu.HBM((len(slots), half, cols), jnp.float32)]
+        + [pltpu.HBM((len(slots), half, width), jnp.bfloat16)] * pieces,
+        compiler_params=pltpu.CompilerParams(vmem_limit_bytes=VMEM_BYTES),
+        cost_estimate=cost,
         name="query_products",
-    )(place, x, w, *after)
+    )(place, *blocks, *in_hbm([w]), *in_hbm(after[:1]), *after[1:])
     return outs[0], outs[1:]
 
 
-def pair_kernel(place_ref, x_ref, wk_ref, wv_ref, *refs):
+def pair_kernel(count, place_ref, *refs):
+    x_refs, (wk_ref, wv_ref) = refs[:count], refs[count : count + 2]
     keep_ref, give_ref, rows_ref = refs[-3:]
 
     @pl.when(pl.program_id(0) == 0)
     def _():
-        ordered_rows(place_ref, x_ref, rows_ref)
+        ordered_rows(place_ref, x_refs, rows_ref)
 
     weights = jnp.concatenate([wk_ref[...], wv_ref[...]], axis=1)
     result = jnp.dot(rows_ref[...], weights, preferred_element_type=jnp.float32)
-    half = result.shape[0] // 2
-    keep_ref[0] = result[:half]
-    give_ref[0] = result[half:].astype(give_ref.dtype)
-
-
-def project_pair(rindex, findex, slots, x, w_key, w_value, after=()):
-    rows, depth = x.shape
+    half, width = x_refs[0].shape[0] // 2, weights.shape[1]
+    for b in range(count):
+        kept, given = b * half, (count + b) * half
+        cols = slice(b * width, (b + 1) * width)
+        keep_ref[0, :, cols] = result[kept : kept + half]
+        give_ref[0, :, cols] = result[given : given + half].astype(give_ref.dtype)
+
+
+def project_pair(rindex, findex, slots, blocks, w_key, w_value, after=()):
+    rows, depth = blocks[0].shape
+    count = len(blocks)
     place = jnp.stack([rindex] + [findex ^ slot for slot in slots]).astype(jnp.int32)
     weight = pl.BlockSpec((depth, DH), lambda s, place: (0, place[1 + s]))
-    out = pl.BlockSpec((1, rows // 2, 2 * DH), lambda s, place: (s, 0, 0))
-    shape = jax.ShapeDtypeStruct((len(slots), rows // 2, 2 * DH), jnp.float32)
-    return pl.pallas_call(
-        pair_kernel,
+    shape = (len(slots), rows // 2, 2 * DH * count)
+    out = pl.BlockSpec((1,) + shape[1:], lambda s, place: (s, 0, 0))
+    return pl.pallas_call(
+        functools.partial(pair_kernel, count),
         grid_spec=pltpu.PrefetchScalarGridSpec(
             num_scalar_prefetch=1,
             grid=(len(slots),),
-            in_specs=[pl.BlockSpec((rows, depth), lambda s, place: (0, 0)), weight, weight]
+            in_specs=[pl.BlockSpec((rows, depth), lambda s, place: (0, 0))] * count
+            + [weight, weight]
             + [pl.BlockSpec(memory_space=pl.ANY)] * len(after),
             out_specs=[out, out],
-            scratch_shapes=[pltpu.VMEM((rows, depth), x.dtype)],
+            scratch_shapes=[pltpu.VMEM((count * rows, depth), blocks[0].dtype)],
         ),
-        out_shape=[shape, jax.ShapeDtypeStruct(shape.shape, jnp.bfloat16)],
+        out_shape=[
+            pltpu.HBM(shape, jnp.float32),
+            pltpu.HBM(shape, jnp.bfloat16),
+        ],
         compiler_params=pltpu.CompilerParams(vmem_limit_bytes=VMEM_BYTES),
         cost_estimate=LIGHT,
         name="key_value_products",
-    )(place, x, w_key, w_value, *after)
-
-
-def add_kernel(tiles, extra, *refs):
+    )(place, *blocks, *in_hbm([w_key, w_value, *after]))
+
+
+def add_kernel(tiles, per, paired, extra, *refs):
     keep_ref, give_refs, out_ref = refs[0], refs[1 : 1 + tiles], refs[-1]
-    for j, give_ref in enumerate(give_refs):
-
-        @pl.when(pl.program_id(1) == j)
+    pair_refs = refs[1 + tiles : 1 + tiles + 2 * paired]
+    landed_refs = refs[1 + tiles + 2 * paired :][:extra]
+    j = pl.program_id(1)
+
+    def write(first_ref, second_ref):
+        total = first_ref[0] + second_ref[0].astype(jnp.float32)
+        for landed_ref in landed_refs:
+            total = total + landed_ref[0].astype(jnp.float32)
+        out_ref[0] = total.astype(out_ref.dtype)
+
+    for t, give_ref in enumerate(give_refs):
+
+        @pl.when(j // per == t)
         def _():
-            total = keep_ref[0] + give_ref[0].astype(jnp.float32)
-            if extra:
-                total = total + refs[1 + tiles][0].astype(jnp.float32)
-            out_ref[0] = total.astype(out_ref.dtype)
-
-
-def add_rows(keep, gots, count, landed=(), after=()):
-    _, rows, cols = keep.shape
-    tiles = len(gots)
-    tile = cols // tiles
-    full = pl.BlockSpec((1, rows, tile), lambda s, j: (s, 0, j))
-    return pl.pallas_call(
-        functools.partial(add_kernel, tiles, len(landed)),
-        grid=(count, tiles),
-        in_specs=[full]
-        + [pl.BlockSpec((1, rows, tile), lambda s, j: (s, 0, 0))] * tiles
-        + [full] * len(landed)
+            write(keep_ref, give_ref)
+
+    if paired:
+
+        @pl.when(j >= tiles * per)
+        def _():
+            write(*pair_refs)
+
+
+def add_rows(count, rows, b, keep, gots, start, pair=(), slot=0, landed=(), after=()):
+    whole = keep.shape[2]
+    width = gots[0].shape[2]
+    step = math.gcd(width, pair[0].shape[2]) if pair else width
+    per, query = width // step, len(gots) * width // step
+    total = query + (pair[0].shape[2] // step if pair else 0)
+    first = start // step
+
+    def got(t):
+        return pl.BlockSpec((1, rows, step), lambda s, j: (s, b, jnp.clip(j - t * per, 0, per - 1)))
+
+    def columns(s, j):
+        return (s, 0, jnp.where(j < query, first + j, whole // step + j - query))
+
+    paired = pl.BlockSpec((1, rows, step), lambda s, j: (slot + s, 0, jnp.maximum(j - query, 0)))
+    return pl.pallas_call(
+        functools.partial(add_kernel, len(gots), per, len(pair) // 2, len(landed)),
+        grid=(count, total),
+        in_specs=[
+            pl.BlockSpec((1, rows, step), lambda s, j: (s, b, first + jnp.minimum(j, query - 1)))
+        ]
+        + [got(t) for t in range(len(gots))]
+        + [paired] * len(pair)
+        + [pl.BlockSpec((1, rows, step), columns)] * len(landed)
         + [pl.BlockSpec(memory_space=pl.ANY)] * len(after),
-        out_specs=full,
-        out_shape=jax.ShapeDtypeStruct((count, rows, cols), jnp.bfloat16),
+        out_specs=pl.BlockSpec((1, rows, step), lambda s, j: (s, 0, j)),
+        out_shape=pltpu.HBM((count, rows, total * step), jnp.bfloat16),
         compiler_params=pltpu.CompilerParams(vmem_limit_bytes=VMEM_BYTES),
         cost_estimate=LIGHT,
         name="add_rows",
-    )(keep, *gots, *landed, *after)
+    )(*in_hbm([keep]), *gots, *in_hbm(pair[:1]), *pair[1:], *landed, *in_hbm(after))
 
 
 def rotate_kernel(count, pieces, cos_ref, sin_ref, *refs):
@@ -177,26 +220,26 @@
 
 def sum_and_rotate(cosine, sine, terms, gots, cols, after=()):
     rows = cosine.shape[0]
-    slot_of_gots, gots = gots
+    slot_of_gots, block_of_gots, gots = gots
     tile = cols // max(1, len(gots))
     table = pl.BlockSpec((rows, DH), lambda j: (0, 0))
 
-    def block(slot, start):
-        return pl.BlockSpec((1, rows, tile), lambda j: (slot, 0, start // tile + j))
+    def block(slot, b, start):
+        return pl.BlockSpec((1, rows, tile), lambda j: (slot, b, start // tile + j))
 
     return pl.pallas_call(
         functools.partial(rotate_kernel, len(terms), len(gots)),
         grid=(cols // tile,),
         in_specs=[table, table]
-        + [block(slot, start) for _, slot, start in terms]
-        + [pl.BlockSpec((1, rows, tile), lambda j: (slot_of_gots, 0, 0))] * len(gots)
+        + [block(slot, b, start) for _, slot, b, start in terms]
+        + [pl.BlockSpec((1, rows, tile), lambda j: (slot_of_gots, block_of_gots, 0))] * len(gots)
         + [pl.BlockSpec(memory_space=pl.ANY)] * len(after),
         out_specs=pl.BlockSpec((rows, tile), lambda j: (0, j)),
         out_shape=jax.ShapeDtypeStruct((rows, cols), jnp.bfloat16),
         compiler_params=pltpu.CompilerParams(vmem_limit_bytes=VMEM_BYTES),
         cost_estimate=LIGHT,
         name="sum_and_rotate",
-    )(cosine, sine, *[term for term, _, _ in terms], *gots, *after)
+    )(cosine, sine, *in_hbm([terms[0][0]]), *[term[0] for term in terms[1:]], *gots, *after)
 
 
 def split_kernel(count, cos_ref, sin_ref, *refs):
@@ -204,21 +247,27 @@
     total = terms[0][0].astype(jnp.float32)
     for term in terms[1:]:
         total = total + term[0].astype(jnp.float32)
-    key, value = total[:, :DH], total[:, DH:]
-    turned = pltpu.roll(key, DH // 2, axis=1)
-    key_ref[...] = (key * cos_ref[...] + turned * sin_ref[...]).astype(key_ref.dtype)
-    value_ref[0] = value.astype(value_ref.dtype)
-
-
-def split_and_rotate(cosine, sine, terms, after):
+    half = total.shape[0]
+    for b in range(total.shape[1] // (2 * DH)):
+        rows = slice(b * half, (b + 1) * half)
+        key = total[:, 2 * b * DH : (2 * b + 1) * DH]
+        turned = pltpu.roll(key, DH // 2, axis=1)
+        key_ref[rows] = (key * cos_ref[rows] + turned * sin_ref[rows]).astype(key_ref.dtype)
+        value_ref[0, rows] = total[:, (2 * b + 1) * DH : (2 * b + 2) * DH].astype(value_ref.dtype)
+
+
+def split_and_rotate(cosine, sine, terms, width):
     rows = cosine.shape[0]
+    half = terms[0][0].shape[1]
     table = pl.BlockSpec((rows, DH), lambda j: (0, 0))
+
+    def block(slot, start):
+        return pl.BlockSpec((1, half, width), lambda j: (slot, 0, start // width))
+
     return pl.pallas_call(
         functools.partial(split_kernel, len(terms)),
         grid=(1,),
-        in_specs=[table, table]
-        + [pl.BlockSpec((1, rows, 2 * DH), lambda j: (0, 0, 0))] * len(terms)
-        + [pl.BlockSpec(memory_space=pl.ANY)] * len(after),
+        in_specs=[table, table] + [block(slot, start) for _, slot, start in terms],
         out_specs=[table, pl.BlockSpec((1, rows, DH), lambda j: (0, 0, 0))],
         out_shape=[
             jax.ShapeDtypeStruct((rows, DH), jnp.bfloat16),
@@ -227,7 +276,7 @@
         compiler_params=pltpu.CompilerParams(vmem_limit_bytes=VMEM_BYTES),
         cost_estimate=LIGHT,
         name="split_and_rotate",
-    )(cosine, sine, *terms, *after)
+    )(cosine, sine, *in_hbm([terms[0][0]]), *[term for term, _, _ in terms[1:]])
 
 
 def prepare_kernel(canary_ref, ids_ref, own_ref, other_ref, order_ref, key_t_ref):
@@ -383,67 +432,64 @@
 
     tile = min(1024, head_cols)
 
-    def project(slots, block, width, after=()):
+    def project(slots, blocks, width, after=(), cost=LIGHT):
         keep, gives = project_query(
-            rindex, findex, slots, block, w_query, head_cols, tile, width, after
+            rindex, findex, slots, blocks, w_query, head_cols, tile, width, after, cost
         )
         return keep, [other_core(give) for give in gives], gives[0]
 
-    def project_heads(block, after):
-        keep, give = project_pair(
-            rindex, findex, list(range(shards)), block, w_key, w_value, (after,)
-        )
-        return keep + other_core(give).astype(jnp.float32), give
-
     def rotate(b, p, split, terms, behind):
-        keep, got = evens[b]
-        cols, each = head_cols // split, len(got) // split
+        cols, each = head_cols // split, len(even_got) // split
         table = slice(b * half, (b + 1) * half)
-        added = [(keep, len(even) - 1, p * cols), (fars[b], len(odd) - 1, p * cols)]
-        added += [(term, 0, 0) for term in terms]
-        gots = (len(even) - 1, got[p * each : (p + 1) * each])
+        added = [(even_keep, len(even) - 1, b, p * cols), (fars[b], len(odd) - 1, 0, p * cols)]
+        added += [(term, 0, 0, 0) for term in terms]
+        gots = (len(even) - 1, b, even_got[p * each : (p + 1) * each])
         turned = sum_and_rotate(cosine[table], sine[table], added, gots, cols, behind)
         return turned, other_core(turned)
 
-    def add_even(b, parts, behind):
-        keep, got = evens[b]
+    last, split = tps - 1, head_cols // tile
+    fars, pair, after = [], (), ()
+    placed = in_hbm(blocks[:1]) + blocks[1:]
+    for b, block in enumerate(placed):
+        if fast_pair and b == last:
+            pair_keep, give = project_pair(rindex, findex, odd + even, placed, w_key, w_value, after)
+            pair = (pair_keep, other_core(give))
+            after = (give,)
+        odd_keep, odd_got, _ = project(odd, [block], tile, after)
+        odd_sent = add_rows(len(odd), half, 0, odd_keep, odd_got, 0, pair)
+        fars.append(swap(odd_sent, 1))
+        after = (odd_sent,)
+
+    even_keep, even_got, given = project(even, placed, min(512, tile), after + tuple(fars[:last]), HEAVY)
+    after = (given,)
+
+    def add_even(b, start, gots, pair, behind):
         landed = (fars[b],) if shards > 2 else ()
-        summed = add_rows(keep, got, len(even) - 1, landed, behind)
-        cols = head_cols // parts
-        spreads = []
+        summed = add_rows(
+            len(even) - 1, half, b, even_keep, gots, start, pair, len(odd), landed, behind
+        )
+        return spread({x: summed[k] for k, x in enumerate(even[:-1])})
+
+    terms = []
+    for b in range(tps):
+        parts = split if b == last else 1
+        each = len(even_got) // parts
+        row = []
         for p in range(parts):
-            live = {x: summed[k][:, p * cols : (p + 1) * cols] for k, x in enumerate(even[:-1])}
-            spreads.append(spread(live))
-        return [terms for terms, _ in spreads], spreads[-1][1]
-
-    last, split = tps - 1, head_cols // tile
-    evens, fars, pairs, terms, after, behind = [], [], [], [], (), ()
-    for b, block in enumerate(blocks):
-        odd_keep, odd_got, _ = project(odd, block, tile, after)
-        odd_sent = add_rows(odd_keep, odd_got, len(odd))
-        fars.append(swap(odd_sent, 1))
-        if b > 0:
-            parts, first = add_even(b - 1, 1, (odd_sent,))
-            terms.append(parts)
-            behind = (first,)
-        even_keep, even_got, given = project(even, block, tile, (odd_sent,) + behind)
-        evens.append((even_keep, even_got))
-        if fast_pair:
-            pair, given = project_heads(block, given)
-            pairs.append(pair)
-        after = (given,)
+            gots = even_got[p * each : (p + 1) * each]
+            cols = p * head_cols // parts
+            paired = pair if b == last and p == 0 else ()
+            added, first = add_even(b, cols, gots, paired, after)
+            row.append(added)
+            after = (first,)
+        terms.append(row)
+    parts = terms[last]
+
     if fast_pair:
-        pair = jnp.concatenate(pairs, axis=1)
-        pair_landed = swap(low(pair[1::2]), 1)
-        live = {x: pair[x] + pair_landed[x // 2].astype(jnp.float32) for x in even[:-1]}
-        pair_terms, first = spread(live)
-        after = (first,)
-    parts, first = add_even(last, split, after)
-    terms.append(parts)
-    after = (first,)
-
-    if fast_pair:
-        key_rot, held = split_and_rotate(cosine, sine, [pair, pair_landed] + pair_terms, after)
+        width = 2 * DH * tps
+        pieces = [(array, shards - 1, 0) for array in pair]
+        pieces += [(fars[last], len(odd) - 1, head_cols)] + [(term, 0, tile) for term in parts[0]]
+        key_rot, held = split_and_rotate(cosine, sine, pieces, width)
         bit = 1
         while bit < shards:
             held = jnp.concatenate([held, swap(held, bit)])
@@ -465,7 +511,7 @@
 
         mine = lax.dynamic_slice_in_dim(key_sum, findex * heads_here // group * DH, DH, 1)
         key_own = of_core(mine, rindex)
-        key_rot = sum_and_rotate(cosine, sine, [(key_own[None], 0, 0)], (0, []), DH, after)
+        key_rot = sum_and_rotate(cosine, sine, [(key_own[None], 0, 0, 0)], (0, 0, []), DH, after)
         value_rows = low(jnp.concatenate([of_core(value_sum, rindex), of_core(value_sum, 1 - rindex)]))
 
     order, key_t = prepare(canary_rows, ids, key_rot, other_core(key_rot))

time: 180 us -> 187 us (1.039)
  Pallas kernels: 80.4 us -> 90.9 us
  local copies, waits for them, and re-layouts: 10.1 us -> 1.21 us
  waiting for transfers between devices: 63.9 us -> 71.8 us
  starting transfers between devices: 17.9 us -> 15.8 us
    pallas_call x10 -> x9, Pallas kernels: 57.5 us -> 66.3 us  [the longest x3 40.2 us: project_query(): pl.pallas_call(functools.partial(query_kernel, count, pieces, width), gri...]
    ppermute x1, waiting for transfers between devices: 0.01 us -> 8.21 us  [body(): lax.ppermute(hidden, 'tp', [(i, (i - b) % tps) for i in range(tps)])]
    unnamed x66 -> x16, local copies, waits for them, and re-layouts: 7.99 us -> 0.05 us
    ppermute x9 -> x7, waiting for transfers between devices: 58.4 us -> 54.4 us  [swap(): return lax.ppermute(x, 'fsdp', [(i, i ^ bit) for i in range(shards)])]
    ppermute x15 -> x14, waiting for transfers between devices: 5.44 us -> 9.18 us  [other_core(): return lax.ppermute(x, 'rep', [(0, 1), (1, 0)])]
    ppermute x9 -> x7, starting transfers between devices: 11.7 us -> 10.2 us  [swap(): return lax.ppermute(x, 'fsdp', [(i, i ^ bit) for i in range(shards)])]
  transfers between devices with their start and end apart: 25 -> 22, of which waited for: 10 -> 13; matrix products, arithmetic and copies ran while one was open for 4% -> 4% of each run, Pallas kernels for 41% -> 45%
where the time goes in v4:
time: 187 us; the launch traced here: 186 us
  Pallas kernels  90.9 us (49%)
  waiting for transfers between devices  71.8 us (38%)
  starting transfers between devices  15.8 us (8%)
  other arithmetic  5.65 us (3%)
    ppermute x7, waiting for transfers between devices, swap(): return lax.ppermute(x, 'fsdp', [(i, i ^ bit) for i in range(shards)])  54.4 us
    pallas_call x3, Pallas kernels, project_query(): pl.pallas_call(functools.partial(query_kernel, count, pieces, width), gri...  40.2 us
    pallas_call x5, Pallas kernels, add_rows(): pl.pallas_call(functools.partial(add_kernel, len(gots), per, len(pair) //...  18.9 us
    pallas_call x2, Pallas kernels, score_heads(): pl.pallas_call(functools.partial(score_kernel, len(queries)), grid=(count...  13.4 us
    ppermute x7, starting transfers between devices, swap(): return lax.ppermute(x, 'fsdp', [(i, i ^ bit) for i in range(shards)])  10.2 us
    ppermute x14, waiting for transfers between devices, other_core(): return lax.ppermute(x, 'rep', [(0, 1), (1, 0)])  9.18 us
    ppermute x1, waiting for transfers between devices, body(): lax.ppermute(hidden, 'tp', [(i, (i - b) % tps) for i in range(tps)])  8.21 us
    pallas_call x1, Pallas kernels, project_pair(): pl.pallas_call(functools.partial(pair_kernel, count), grid_spec=pltpu.Pre...  7.09 us
  transfers between devices with their start and end apart: 22, of which 13 were waited for; matrix products, arithmetic and copies ran while one was open for 4% of the time, Pallas kernels for 45%

profile of v4, /device:TPU:0, one launch (start us, length us, event | category | flops | bytes accessed | tf_op | source)
XLA Modules:
  0.0 186.2 jit_solution(16979792598449077525)
XLA Ops:
  0.6 3.0 %collective-permute-start = (bf16[320,2048]{1,0:T(8,128)(2,1)}, bf16[320,2048]{1,0:T(8,128)(2,1)S(1)}, u32[]{:S(2)}, u32[]{:S(2)}) collective-permute-start(bf16[320,2048]{1,0:T(8,128)(2,1)} %refs_0_.5), channel_id=1, source_target_pairs={{0,2},{2,0},{1,3},{3,1},{4,6},{6,4},{5,7},{7,5},{8,10},{10,8},{9,1... | collective-permute-start | bytes 3932168 | tf_op jit(solution)/shard_map/ppermute | solution.py:421
  3.7 11.9 %query_products.3 = (f32[2,160,2048]{2,1,0:T(8,128)}, bf16[2,160,1024]{2,1,0:T(8,128)(2,1)}, bf16[2,160,1024]{2,1,0:T(8,128)(2,1)}) custom-call(s32[3]{0:T(128)S(1)} %pad_add_fusion.1.place_ref, bf16[320,2048]{1,0:T(8,128)(2,1)} %refs_0_.5, bf16[2048,8192]{1,0:T(8,128)(2,1)} %refs_2_.3), custom_call_target="tpu_custom_call" | custom-call | flops 1000 | bytes 1000 | tf_op jit(solution)/shard_map/query_products/pallas_call | solution.py:73
  15.6 0.5 collective-permute-start.2
  16.1 1.8 collective-permute-done.1.refs_1_
  17.9 0.9 collective-permute-done.2.refs_2_
  18.9 3.9 %add_rows.5.refs_4_ = bf16[2,160,2048]{2,1,0:T(8,128)(2,1)} custom-call(f32[2,160,2048]{2,1,0:T(8,128)} %get-tuple-element.24.refs_0_, bf16[2,160,1024]{2,1,0:T(8,128)(2,1)S(1)} %collective-permute-done.1.refs_1_, bf16[2,160,1024]{2,1,0:T(8,128)(2,1)S(1)} %collective-permute-done.2.refs_2_), custom_call_target="tpu_custom_call" | custom-call | flops 1000 | bytes 1000 | tf_op jit(solution)/shard_map/add_rows/pallas_call | solution.py:180
  22.7 1.6 collective-permute-start.7
  24.4 8.2 %collective-permute-done.refs_1_.refs_0_ = bf16[320,2048]{1,0:T(8,128)(2,1)S(1)} collective-permute-done((bf16[320,2048]{1,0:T(8,128)(2,1)}, bf16[320,2048]{1,0:T(8,128)(2,1)S(1)}, u32[]{:S(2)}, u32[]{:S(2)}) %collective-permute-start) | collective-permute-done | bytes 1310752 | tf_op jit(solution)/shard_map/ppermute | solution.py:421
  32.6 7.1 %key_value_products.1 = (f32[4,160,512]{2,1,0:T(8,128)}, bf16[4,160,512]{2,1,0:T(8,128)(2,1)}) custom-call(s32[5]{0:T(128)S(1)} %stack.46.place_ref, bf16[320,2048]{1,0:T(8,128)(2,1)} %refs_0_.5, bf16[320,2048]{1,0:T(8,128)(2,1)S(1)} %collective-permute-done.refs_1_.refs_0_, bf16[2048,512]{1,0:T(8,128)(2,1)} %refs_2_.2, bf16[2048,512]{1,0:T(8,128)(2,1)} %refs_3_.1, ...), custom_call_target="tpu_custom_call" | custom-call | flops 1000 | bytes 1000 | tf_op jit(solution)/shard_map/key_value_products/pallas_call | solution.py:119
  39.7 11.5 %query_products.4 = (f32[2,160,2048]{2,1,0:T(8,128)}, bf16[2,160,1024]{2,1,0:T(8,128)(2,1)}, bf16[2,160,1024]{2,1,0:T(8,128)(2,1)}) custom-call(s32[3]{0:T(128)S(1)} %pad_add_fusion.1.place_ref, bf16[320,2048]{1,0:T(8,128)(2,1)S(1)} %collective-permute-done.refs_1_.refs_0_, bf16[2048,8192]{1,0:T(8,128)(2,1)} %refs_2_.3, ...), custom_call_target="tpu_custom_call" | custom-call | flops 1000 | bytes 1000 | tf_op jit(solution)/shard_map/query_products/pallas_call | solution.py:73
  51.2 0.5 collective-permute-start.4
  51.8 1.8 collective-permute-done.4.refs_1_
  53.6 0.9 collective-permute-done.5.refs_2_
  54.6 6.7 %add_rows.6.refs_3_ = bf16[2,160,2560]{2,1,0:T(8,128)(2,1)} custom-call(f32[2,160,2048]{2,1,0:T(8,128)} %get-tuple-element.29.refs_0_, bf16[2,160,1024]{2,1,0:T(8,128)(2,1)S(1)} %collective-permute-done.4.refs_1_, bf16[2,160,1024]{2,1,0:T(8,128)(2,1)S(1)} %collective-permute-done.5.refs_2_, f32[4,160,512]{2,1,0:T(8,128)} %get-tuple-element.27.refs_3_.refs_0_, ...), custom_call_target="tpu_custom_call" | custom-call | flops 1000 | bytes 1000 | tf_op jit(solution)/shard_map/add_rows/pallas_call | solution.py:180
  61.3 1.9 %collective-permute-start.6 = (bf16[2,160,2560]{2,1,0:T(8,128)(2,1)}, bf16[2,160,2560]{2,1,0:T(8,128)(2,1)S(1)}, u32[]{:S(2)}, u32[]{:S(2)}) collective-permute-start(bf16[2,160,2560]{2,1,0:T(8,128)(2,1)} %add_rows.6.refs_3_), channel_id=1, source_target_pairs={{0,4},{4,0},{8,12},{12,8},{1,5},{5,1},{9,13},{13,9},{2,6},{6,2},{1... | collective-permute-start | bytes 4915208 | tf_op jit(solution)/shard_map/ppermute | solution.py:391
  63.2 16.9 %query_products.5 = (f32[2,320,2048]{2,1,0:T(8,128)}, bf16[2,320,512]{2,1,0:T(8,128)(2,1)}, bf16[2,320,512]{2,1,0:T(8,128)(2,1)}, bf16[2,320,512]{2,1,0:T(8,128)(2,1)}, bf16[2,320,512]{2,1,0:T(8,128)(2,1)}) custom-call(s32[3]{0:T(128)S(1)} %pad_add_fusion.2.place_ref, bf16[320,2048]{1,0:T(8,128)(2,1)} %refs_0_.5, ...), custom_call_target="tpu_custom_call" | custom-call | flops 99999997952 | bytes 100000000 | tf_op jit(solution)/shard_map/query_products/pallas_call | solution.py:73
  80.1 0.4 collective-permute-start.10
  80.6 0.4 collective-permute-start.8
  81.3 0.2 select_reduce_fusion
  81.5 1.1 collective-permute-done.9.refs_2_.refs_4_
  82.6 1.5 collective-permute-done.10.refs_3_.refs_1_.refs_5_
  84.1 1.1 collective-permute-done.11.refs_4_.refs_2_.refs_6_
  85.2 3.8 %add_rows.7.refs_6_ = bf16[1,160,2048]{2,1,0:T(8,128)(2,1)} custom-call(f32[2,320,2048]{2,1,0:T(8,128)} %get-tuple-element.32.refs_0_, bf16[2,320,512]{2,1,0:T(8,128)(2,1)} %collective-permute-done.8.refs_1_.refs_3_, bf16[2,320,512]{2,1,0:T(8,128)(2,1)} %collective-permute-done.9.refs_2_.refs_4_, ...), custom_call_target="tpu_custom_call" | custom-call | flops 1000 | bytes 1000 | tf_op jit(solution)/shard_map/add_rows/pallas_call | solution.py:180
  89.0 2.6 %collective-permute-start.14 = (bf16[1,160,2048]{2,1,0:T(8,128)(2,1)}, bf16[1,160,2048]{2,1,0:T(8,128)(2,1)}, u32[]{:S(2)}, u32[]{:S(2)}) collective-permute-start(bf16[1,160,2048]{2,1,0:T(8,128)(2,1)} %add_rows.7.refs_6_), channel_id=1, source_target_pairs={{0,8},{4,12},{8,0},{12,4},{1,9},{5,13},{9,1},{13,5},{2,10},{6,14},... | collective-permute-start | bytes 1966088 | tf_op jit(solution)/shard_map/ppermute | solution.py:391
  91.6 1.5 fusion.4
  93.0 15.8 %collective-permute-done.6.refs_5_.refs_2_.refs_3_.refs_1_ = bf16[2,160,2560]{2,1,0:T(8,128)(2,1)S(1)} collective-permute-done((bf16[2,160,2560]{2,1,0:T(8,128)(2,1)}, bf16[2,160,2560]{2,1,0:T(8,128)(2,1)S(1)}, u32[]{:S(2)}, u32[]{:S(2)}) %collective-permute-start.6) | collective-permute-done | bytes 1638432 | tf_op jit(solution)/shard_map/ppermute | solution.py:391
  108.8 2.7 %add_rows.8.refs_4_ = bf16[1,160,1536]{2,1,0:T(8,128)(2,1)} custom-call(f32[2,320,2048]{2,1,0:T(8,128)} %get-tuple-element.32.refs_0_, bf16[2,320,512]{2,1,0:T(8,128)(2,1)} %collective-permute-done.8.refs_1_.refs_3_, bf16[2,320,512]{2,1,0:T(8,128)(2,1)} %collective-permute-done.9.refs_2_.refs_4_, f32[4,160,512]{2,1,0:T(8,128)} %get-tuple-element.27.refs_3_.refs_0_, ...), custom_call_target="tpu_custom_call" | custom-call | flops 1000 | bytes 1000 | tf_op jit(solution)/shard_map/add_rows/pallas_call | solution.py:180
  111.5 0.8 collective-permute-start.12
  112.4 0.9 reshape.81.canary_ref
  113.3 1.1 pad_maximum_fusion.2.sin_ref
  114.5 1.1 fusion.1
  115.6 1.1 fusion.3
  116.7 1.8 add_rows.9.refs_7_
  118.5 13.8 %collective-permute-done.14.refs_2_ = bf16[1,160,2048]{2,1,0:T(8,128)(2,1)} collective-permute-done((bf16[1,160,2048]{2,1,0:T(8,128)(2,1)}, bf16[1,160,2048]{2,1,0:T(8,128)(2,1)}, u32[]{:S(2)}, u32[]{:S(2)}) %collective-permute-start.14) | collective-permute-done | bytes 655392 | tf_op jit(solution)/shard_map/ppermute | solution.py:391
  132.4 3.3 %sum_and_rotate.3.refs_0_ = bf16[160,2048]{1,0:T(8,128)(2,1)S(1)} custom-call(f32[160,128]{1,0:T(8,128)S(1)} %get-tuple-element.49.cos_ref, f32[160,128]{1,0:T(8,128)S(1)} %get-tuple-element.47.sin_ref, f32[2,320,2048]{2,1,0:T(8,128)} %get-tuple-element.32.refs_0_, bf16[2,160,2048]{2,1,0:T(8,128)(2,1)} %collective-permute-done.7.refs_4_.refs_5_.refs_1_, ...), custom_call_target="tpu_custom_call" | custom-call | flops 1000 | bytes 1000 | tf_op jit(solution)/shard_map/sum_and_rotate/pallas_call | solution.py:230
  135.9 6.1 %collective-permute-done.12.refs_3_.refs_2_ = bf16[1,160,1536]{2,1,0:T(8,128)(2,1)S(1)} collective-permute-done((bf16[1,160,1536]{2,1,0:T(8,128)(2,1)}, bf16[1,160,1536]{2,1,0:T(8,128)(2,1)S(1)}, u32[]{:S(2)}, u32[]{:S(2)}) %collective-permute-start.12) | collective-permute-done | bytes 491552 | tf_op jit(solution)/shard_map/ppermute | solution.py:391
  142.1 1.1 split_and_rotate.1
  143.4 3.0 %collective-permute-start.15 = (bf16[1,160,1024]{2,1,0:T(8,128)(2,1)}, bf16[1,160,1024]{2,1,0:T(8,128)(2,1)S(1)}, u32[]{:S(2)}, u32[]{:S(2)}) collective-permute-start(bf16[1,160,1024]{2,1,0:T(8,128)(2,1)} %add_rows.9.refs_7_), channel_id=1, source_target_pairs={{0,8},{4,12},{8,0},{12,4},{1,9},{5,13},{9,1},{13,5},{2,10},{6,14},... | collective-permute-start | bytes 983048 | tf_op jit(solution)/shard_map/ppermute | solution.py:391
  146.4 2.8 %collective-permute-done.19 = bf16[1,320,128]{2,1,0:T(8,128)(2,1)S(1)} collective-permute-done((bf16[1,320,128]{2,1,0:T(8,128)(2,1)S(1)}, bf16[1,320,128]{2,1,0:T(8,128)(2,1)S(1)}, u32[]{:S(2)}, u32[]{:S(2)}) %collective-permute-start.19) | collective-permute-done | bytes 81952 | tf_op jit(solution)/shard_map/ppermute | solution.py:391
  149.2 0.2 collective-permute-start.20
  149.4 0.6 order_and_keys.1
  149.9 1.6 sum_and_rotate.4.refs_1_
  151.7 15.9 %collective-permute-done.20 = bf16[2,320,128]{2,1,0:T(8,128)(2,1)S(1)} collective-permute-done((bf16[2,320,128]{2,1,0:T(8,128)(2,1)S(1)}, bf16[2,320,128]{2,1,0:T(8,128)(2,1)S(1)}, u32[]{:S(2)}, u32[]{:S(2)}) %collective-permute-start.20) | collective-permute-done | bytes 163872 | tf_op jit(solution)/shard_map/ppermute | solution.py:391
  167.7 6.8 %score_heads.2 = (bf16[1,16,640,640]{3,2,1,0:T(8,128)(2,1)}, f32[8,128]{1,0:T(8,128)S(1)}) custom-call(bf16[640,640]{1,0:T(8,128)(2,1)S(1)} %get-tuple-element.38.order_ref, bf16[128,640]{1,0:T(8,128)(2,1)S(1)} %get-tuple-element.39.refs_5_.key_t_ref, bf16[160,2048]{1,0:T(8,128)(2,1)S(1)} %sum_and_rotate.3.refs_0_, ...), custom_call_target="tpu_custom_call" | custom-call | flops 1000 | bytes 1000 | tf_op jit(solution)/shard_map/score_heads/pallas_call | solution.py:352
  174.5 1.5 sum_and_rotate.5.refs_1_
  176.1 0.4 collective-permute-start.18
  176.5 3.1 %order_values.1 = (bf16[640,512]{1,0:T(8,128)(2,1)}, f32[8,128]{1,0:T(8,128)S(1)}) custom-call(s32[4]{0:T(128)S(1)} %pad_add_fusion.3.place_ref, bf16[640,640]{1,0:T(8,128)(2,1)S(1)} %get-tuple-element.38.order_ref, bf16[4,320,128]{2,1,0:T(8,128)(2,1)S(1)} %constant_dynamic-update-slice_fusion.own_ref, bf16[4,320,128]{2,1,0:T(8,128)(2,1)S(1)} %collective-permute-done.21.other_ref), custom_call_target="tpu_custom_call" | custom-call | tf_op jit(solution)/shard_map/order_values/pallas_call | solution.py:313
  179.6 6.6 %score_heads.3 = (bf16[1,16,640,640]{3,2,1,0:T(8,128)(2,1)}, f32[8,128]{1,0:T(8,128)}) custom-call(bf16[640,640]{1,0:T(8,128)(2,1)S(1)} %get-tuple-element.38.order_ref, bf16[128,640]{1,0:T(8,128)(2,1)S(1)} %get-tuple-element.39.refs_5_.key_t_ref, bf16[160,2048]{1,0:T(8,128)(2,1)S(1)} %sum_and_rotate.3.refs_0_, ...), custom_call_target="tpu_custom_call", output_to_operand_aliasing={{0}: (6, {})} | custom-call | flops 1000 | bytes 1000 | tf_op jit(solution)/shard_map/score_heads/pallas_call | solution.py:352
  (51 shorter events, 1.4 us)
Async XLA Ops:
  0.6 32.0 %collective-permute-start = (bf16[320,2048]{1,0:T(8,128)(2,1)}, bf16[320,2048]{1,0:T(8,128)(2,1)S(1)}, u32[]{:S(2)}, u32[]{:S(2)}) collective-permute-start(bf16[320,2048]{1,0:T(8,128)(2,1)} %refs_0_.5), channel_id=1, source_target_pairs={{0,2},{2,0},{1,3},{3,1},{4,6},{6,4},{5,7},{7,5},{8,10},{10,8},{9,1... | collective-permute-start | bytes 3932168 | tf_op jit(solution)/shard_map/ppermute | solution.py:421
  15.6 2.3 %collective-permute-start.1 = (bf16[2,160,1024]{2,1,0:T(8,128)(2,1)}, bf16[2,160,1024]{2,1,0:T(8,128)(2,1)S(1)}, u32[]{:S(2)}, u32[]{:S(2)}) collective-permute-start(bf16[2,160,1024]{2,1,0:T(8,128)(2,1)} %get-tuple-element.25), channel_id=1, source_target_pairs={{0,1},{1,0},{2,3},{3,2},{4,5},{5,4},{6,7},{7,6},{8,9},{9,8},{10,11... | collective-permute-start | bytes 1966088 | tf_op jit(solution)/shard_map/ppermute | solution.py:394
  15.6 3.2 %collective-permute-start.2 = (bf16[2,160,1024]{2,1,0:T(8,128)(2,1)}, bf16[2,160,1024]{2,1,0:T(8,128)(2,1)S(1)}, u32[]{:S(2)}, u32[]{:S(2)}) collective-permute-start(bf16[2,160,1024]{2,1,0:T(8,128)(2,1)} %get-tuple-element.26), channel_id=1, source_target_pairs={{0,1},{1,0},{2,3},{3,2},{4,5},{5,4},{6,7},{7,6},{8,9},{9,8},{10,11... | collective-permute-start | bytes 1966088 | tf_op jit(solution)/shard_map/ppermute | solution.py:394
  22.7 40.4 %collective-permute-start.7 = (bf16[2,160,2048]{2,1,0:T(8,128)(2,1)}, bf16[2,160,2048]{2,1,0:T(8,128)(2,1)}, u32[]{:S(2)}, u32[]{:S(2)}) collective-permute-start(bf16[2,160,2048]{2,1,0:T(8,128)(2,1)} %add_rows.5.refs_4_), channel_id=1, source_target_pairs={{0,4},{4,0},{8,12},{12,8},{1,5},{5,1},{9,13},{13,9},{2,6},{6,2},{1... | collective-permute-start | bytes 3932168 | tf_op jit(solution)/shard_map/ppermute | solution.py:391
  39.7 12.1 %collective-permute-start.3 = (bf16[4,160,512]{2,1,0:T(8,128)(2,1)}, bf16[4,160,512]{2,1,0:T(8,128)(2,1)S(1)}, u32[]{:S(2)}, u32[]{:S(2)}) collective-permute-start(bf16[4,160,512]{2,1,0:T(8,128)(2,1)} %get-tuple-element.28.refs_2_), channel_id=1, source_target_pairs={{0,1},{1,0},{2,3},{3,2},{4,5},{5,4},{6,7},{7,6},{8,9},{9,8},{10,11... | collective-permute-start | bytes 1966088 | tf_op jit(solution)/shard_map/ppermute | solution.py:394
  51.2 2.4 %collective-permute-start.4 = (bf16[2,160,1024]{2,1,0:T(8,128)(2,1)}, bf16[2,160,1024]{2,1,0:T(8,128)(2,1)S(1)}, u32[]{:S(2)}, u32[]{:S(2)}) collective-permute-start(bf16[2,160,1024]{2,1,0:T(8,128)(2,1)} %get-tuple-element.30), channel_id=1, source_target_pairs={{0,1},{1,0},{2,3},{3,2},{4,5},{5,4},{6,7},{7,6},{8,9},{9,8},{10,11... | collective-permute-start | bytes 1966088 | tf_op jit(solution)/shard_map/ppermute | solution.py:394
  51.7 2.9 %collective-permute-start.5 = (bf16[2,160,1024]{2,1,0:T(8,128)(2,1)}, bf16[2,160,1024]{2,1,0:T(8,128)(2,1)S(1)}, u32[]{:S(2)}, u32[]{:S(2)}) collective-permute-start(bf16[2,160,1024]{2,1,0:T(8,128)(2,1)} %get-tuple-element.31), channel_id=1, source_target_pairs={{0,1},{1,0},{2,3},{3,2},{4,5},{5,4},{6,7},{7,6},{8,9},{9,8},{10,11... | collective-permute-start | bytes 1966088 | tf_op jit(solution)/shard_map/ppermute | solution.py:394
  51.8 9.5 %copy-start = (bf16[4,160,512]{2,1,0:T(8,128)(2,1)}, bf16[4,160,512]{2,1,0:T(8,128)(2,1)S(1)}, u32[]{:S(2)}) copy-start(bf16[4,160,512]{2,1,0:T(8,128)(2,1)S(1)} %collective-permute-done.3.refs_4_.refs_1_) | copy-start | bytes 1966084
  61.3 20.0 %copy-start.5 = (s32[640]{0:T(1024)S(1)}, s32[640]{0:T(1024)}, u32[]{:S(2)}) copy-start(s32[640]{0:T(1024)} %param.10) | copy-start | bytes 7684
  61.3 20.0 %copy-start.6 = (s32[640]{0:T(1024)S(1)}, s32[640]{0:T(1024)}, u32[]{:S(2)}) copy-start(s32[640]{0:T(1024)} %param.11) | copy-start | bytes 7684
  61.3 47.5 %collective-permute-start.6 = (bf16[2,160,2560]{2,1,0:T(8,128)(2,1)}, bf16[2,160,2560]{2,1,0:T(8,128)(2,1)S(1)}, u32[]{:S(2)}, u32[]{:S(2)}) collective-permute-start(bf16[2,160,2560]{2,1,0:T(8,128)(2,1)} %add_rows.6.refs_3_), channel_id=1, source_target_pairs={{0,4},{4,0},{8,12},{12,8},{1,5},{5,1},{9,13},{13,9},{2,6},{6,2},{1... | collective-permute-start | bytes 4915208 | tf_op jit(solution)/shard_map/ppermute | solution.py:391
  80.1 2.6 %collective-permute-start.9 = (bf16[2,320,512]{2,1,0:T(8,128)(2,1)}, bf16[2,320,512]{2,1,0:T(8,128)(2,1)}, u32[]{:S(2)}, u32[]{:S(2)}) collective-permute-start(bf16[2,320,512]{2,1,0:T(8,128)(2,1)} %get-tuple-element.34), channel_id=1, source_target_pairs={{0,1},{1,0},{2,3},{3,2},{4,5},{5,4},{6,7},{7,6},{8,9},{9,8},{10,11... | collective-permute-start | bytes 1966088 | tf_op jit(solution)/shard_map/ppermute | solution.py:394
  80.1 4.0 %collective-permute-start.10 = (bf16[2,320,512]{2,1,0:T(8,128)(2,1)}, bf16[2,320,512]{2,1,0:T(8,128)(2,1)S(1)}, u32[]{:S(2)}, u32[]{:S(2)}) collective-permute-start(bf16[2,320,512]{2,1,0:T(8,128)(2,1)} %get-tuple-element.35), channel_id=1, source_target_pairs={{0,1},{1,0},{2,3},{3,2},{4,5},{5,4},{6,7},{7,6},{8,9},{9,8},{10,11... | collective-permute-start | bytes 1966088 | tf_op jit(solution)/shard_map/ppermute | solution.py:394
  80.6 4.6 %collective-permute-start.11 = (bf16[2,320,512]{2,1,0:T(8,128)(2,1)}, bf16[2,320,512]{2,1,0:T(8,128)(2,1)S(1)}, u32[]{:S(2)}, u32[]{:S(2)}) collective-permute-start(bf16[2,320,512]{2,1,0:T(8,128)(2,1)} %get-tuple-element.36), channel_id=1, source_target_pairs={{0,1},{1,0},{2,3},{3,2},{4,5},{5,4},{6,7},{7,6},{8,9},{9,8},{10,11... | collective-permute-start | bytes 1966088 | tf_op jit(solution)/shard_map/ppermute | solution.py:394
  80.6 4.5 %collective-permute-start.8 = (bf16[2,320,512]{2,1,0:T(8,128)(2,1)}, bf16[2,320,512]{2,1,0:T(8,128)(2,1)}, u32[]{:S(2)}, u32[]{:S(2)}) collective-permute-start(bf16[2,320,512]{2,1,0:T(8,128)(2,1)} %get-tuple-element.33.refs_6_), channel_id=1, source_target_pairs={{0,1},{1,0},{2,3},{3,2},{4,5},{5,4},{6,7},{7,6},{8,9},{9,8},{10,11... | collective-permute-start | bytes 1966088 | tf_op jit(solution)/shard_map/ppermute | solution.py:394
  85.2 23.6 %copy-start.1 = (bf16[4,160,512]{2,1,0:T(8,128)(2,1)S(1)}, bf16[4,160,512]{2,1,0:T(8,128)(2,1)}, u32[]{:S(2)}) copy-start(bf16[4,160,512]{2,1,0:T(8,128)(2,1)} %copy-done) | copy-start | bytes 1966084
  89.0 43.4 %collective-permute-start.14 = (bf16[1,160,2048]{2,1,0:T(8,128)(2,1)}, bf16[1,160,2048]{2,1,0:T(8,128)(2,1)}, u32[]{:S(2)}, u32[]{:S(2)}) collective-permute-start(bf16[1,160,2048]{2,1,0:T(8,128)(2,1)} %add_rows.7.refs_6_), channel_id=1, source_target_pairs={{0,8},{4,12},{8,0},{12,4},{1,9},{5,13},{9,1},{13,5},{2,10},{6,14},... | collective-permute-start | bytes 1966088 | tf_op jit(solution)/shard_map/ppermute | solution.py:391
  111.5 30.6 %collective-permute-start.12 = (bf16[1,160,1536]{2,1,0:T(8,128)(2,1)}, bf16[1,160,1536]{2,1,0:T(8,128)(2,1)S(1)}, u32[]{:S(2)}, u32[]{:S(2)}) collective-permute-start(bf16[1,160,1536]{2,1,0:T(8,128)(2,1)} %add_rows.8.refs_4_), channel_id=1, source_target_pairs={{0,8},{4,12},{8,0},{12,4},{1,9},{5,13},{9,1},{13,5},{2,10},{6,14},... | collective-permute-start | bytes 1474568 | tf_op jit(solution)/shard_map/ppermute | solution.py:391
  132.4 3.4 %copy-start.4 = (f32[320,64]{1,0:T(8,128)S(1)}, f32[320,64]{1,0:T(8,128)}, u32[]{:S(2)}) copy-start(f32[320,64]{1,0:T(8,128)} %get-tuple-element.52) | copy-start | bytes 245764
  132.4 9.7 %copy-start.2 = (bf16[4,160,512]{2,1,0:T(8,128)(2,1)S(1)}, bf16[4,160,512]{2,1,0:T(8,128)(2,1)}, u32[]{:S(2)}) copy-start(bf16[4,160,512]{2,1,0:T(8,128)(2,1)} %copy-done) | copy-start | bytes 1966084
  135.7 32.0 %collective-permute-start.16 = (bf16[160,2048]{1,0:T(8,128)(2,1)S(1)}, bf16[160,2048]{1,0:T(8,128)(2,1)S(1)}, u32[]{:S(2)}, u32[]{:S(2)}) collective-permute-start(bf16[160,2048]{1,0:T(8,128)(2,1)S(1)} %sum_and_rotate.3.refs_0_), channel_id=1, source_target_pairs={{0,1},{1,0},{2,3},{3,2},{4,5},{5,4},{6,7},{7,6},{8,9},{9,8},{10,11... | collective-permute-start | bytes 1966088 | tf_op jit(solution)/shard_map/ppermute | solution.py:394
  135.9 13.4 %copy-start.3 = (s32[640,1]{1,0:T(8,128)S(1)}, s32[640,1]{1,0:T(8,128)}, u32[]{:S(2)}) copy-start(s32[640,1]{1,0:T(8,128)} %reshape.81.canary_ref) | copy-start | bytes 7684
  143.2 5.9 %collective-permute-start.19 = (bf16[1,320,128]{2,1,0:T(8,128)(2,1)S(1)}, bf16[1,320,128]{2,1,0:T(8,128)(2,1)S(1)}, u32[]{:S(2)}, u32[]{:S(2)}) collective-permute-start(bf16[1,320,128]{2,1,0:T(8,128)(2,1)S(1)} %get-tuple-element.42), channel_id=1, source_target_pairs={{0,4},{4,0},{8,12},{12,8},{1,5},{5,1},{9,13},{13,9},{2,6},{6,2},{1... | collective-permute-start | bytes 245768 | tf_op jit(solution)/shard_map/ppermute | solution.py:391
  143.4 31.2 %collective-permute-start.15 = (bf16[1,160,1024]{2,1,0:T(8,128)(2,1)}, bf16[1,160,1024]{2,1,0:T(8,128)(2,1)S(1)}, u32[]{:S(2)}, u32[]{:S(2)}) collective-permute-start(bf16[1,160,1024]{2,1,0:T(8,128)(2,1)} %add_rows.9.refs_7_), channel_id=1, source_target_pairs={{0,8},{4,12},{8,0},{12,4},{1,9},{5,13},{9,1},{13,5},{2,10},{6,14},... | collective-permute-start | bytes 983048 | tf_op jit(solution)/shard_map/ppermute | solution.py:391
  146.4 3.0 %collective-permute-start.13 = (bf16[320,128]{1,0:T(8,128)(2,1)S(1)}, bf16[320,128]{1,0:T(8,128)(2,1)S(1)}, u32[]{:S(2)}, u32[]{:S(2)}) collective-permute-start(bf16[320,128]{1,0:T(8,128)(2,1)S(1)} %get-tuple-element.37.own_ref), channel_id=1, source_target_pairs={{0,1},{1,0},{2,3},{3,2},{4,5},{5,4},{6,7},{7,6},{8,9},{9,8},{10,11... | collective-permute-start | bytes 245768 | tf_op jit(solution)/shard_map/ppermute | solution.py:394
  149.2 18.5 %collective-permute-start.20 = (bf16[2,320,128]{2,1,0:T(8,128)(2,1)S(1)}, bf16[2,320,128]{2,1,0:T(8,128)(2,1)S(1)}, u32[]{:S(2)}, u32[]{:S(2)}) collective-permute-start(bf16[2,320,128]{2,1,0:T(8,128)(2,1)S(1)} %pad_maximum_fusion), channel_id=1, source_target_pairs={{0,8},{4,12},{8,0},{12,4},{1,9},{5,13},{9,1},{13,5},{2,10},{6,14},... | collective-permute-start | bytes 491528 | tf_op jit(solution)/shard_map/ppermute | solution.py:391
  151.6 16.2 %collective-permute-start.17 = (bf16[160,1024]{1,0:T(8,128)(2,1)S(1)}, bf16[160,1024]{1,0:T(8,128)(2,1)S(1)}, u32[]{:S(2)}, u32[]{:S(2)}) collective-permute-start(bf16[160,1024]{1,0:T(8,128)(2,1)S(1)} %sum_and_rotate.4.refs_1_), channel_id=1, source_target_pairs={{0,1},{1,0},{2,3},{3,2},{4,5},{5,4},{6,7},{7,6},{8,9},{9,8},{10,11... | collective-permute-start | bytes 983048 | tf_op jit(solution)/shard_map/ppermute | solution.py:394
  167.6 8.8 %collective-permute-start.21 = (bf16[4,320,128]{2,1,0:T(8,128)(2,1)S(1)}, bf16[4,320,128]{2,1,0:T(8,128)(2,1)S(1)}, u32[]{:S(2)}, u32[]{:S(2)}) collective-permute-start(bf16[4,320,128]{2,1,0:T(8,128)(2,1)S(1)} %constant_dynamic-update-slice_fusion.own_ref), channel_id=1, source_target_pairs={{0,1},{1,0},{2,3},{3,2},{4,5},{5,4},{6,7},{7,6},{8,9},{9,8},{10,11... | collective-permute-start | bytes 983048 | tf_op jit(solution)/shard_map/ppermute | solution.py:394
  176.1 3.5 %collective-permute-start.18 = (bf16[160,1024]{1,0:T(8,128)(2,1)S(1)}, bf16[160,1024]{1,0:T(8,128)(2,1)S(1)}, u32[]{:S(2)}, u32[]{:S(2)}) collective-permute-start(bf16[160,1024]{1,0:T(8,128)(2,1)S(1)} %sum_and_rotate.5.refs_1_), channel_id=1, source_target_pairs={{0,1},{1,0},{2,3},{3,2},{4,5},{5,4},{6,7},{7,6},{8,9},{9,8},{10,11... | collective-permute-start | bytes 983048 | tf_op jit(solution)/shard_map/ppermute | solution.py:394

commit v5 on v4

--- a/solution.py
+++ b/solution.py
@@ -42,11 +42,12 @@
         rows_ref[given : given + half] = x_ref[pl.ds(pl.multiple_of((1 - core) * half, 16), half)]
 
 
-def query_kernel(count, pieces, width, place_ref, *refs):
+def query_kernel(count, pieces, place_ref, *refs):
     x_refs, w_ref = refs[:count], refs[count]
     keep_ref, *give_refs, rows_ref = refs[-2 - pieces :]
     tile = pl.program_id(1)
-    each = keep_ref.shape[2] // width
+    size = give_refs[0].shape[2]
+    each = keep_ref.shape[2] // size
 
     @pl.when((pl.program_id(0) == 0) & (tile == 0))
     def _():
@@ -57,10 +58,10 @@
     keep_ref[0] = result[:half]
     for j, give_ref in enumerate(give_refs):
 
-        @pl.when(tile == j // each)
+        @pl.when((tile == j // each) | (pieces == 1))
         def _():
-            start = j % each * width
-            give_ref[0] = result[half:, start : start + width].astype(give_ref.dtype)
+            start = j % each * size
+            give_ref[0] = result[half:, start : start + size].astype(give_ref.dtype)
 
 
 def project_query(rindex, findex, slots, blocks, w, cols, tile, width, after, cost):
@@ -69,17 +70,18 @@
     half = rows // 2 * count
     tiles, pieces = cols // tile, cols // width
     place = jnp.stack([rindex] + [findex ^ slot for slot in slots]).astype(jnp.int32)
+    keep_spec = pl.BlockSpec((1, half, tile), lambda s, j, place: (s, 0, j))
+    give_spec = pl.BlockSpec((1, half, width), lambda s, j, place: (s, 0, 0))
     x_spec = pl.BlockSpec((rows, depth), lambda s, j, place: (0, 0), pipeline_mode=pl.Buffered(1))
     outs = pl.pallas_call(
-        functools.partial(query_kernel, count, pieces, width),
+        functools.partial(query_kernel, count, pieces),
         grid_spec=pltpu.PrefetchScalarGridSpec(
             num_scalar_prefetch=1,
             grid=(len(slots), tiles),
             in_specs=[x_spec] * count
             + [pl.BlockSpec((depth, tile), lambda s, j, place: (0, place[1 + s] * tiles + j))]
             + [pl.BlockSpec(memory_space=pl.ANY)] * len(after),
-            out_specs=[pl.BlockSpec((1, half, tile), lambda s, j, place: (s, 0, j))]
-            + [pl.BlockSpec((1, half, width), lambda s, j, place: (s, 0, 0))] * pieces,
+            out_specs=[keep_spec] + ([keep_spec] if pieces == 1 else [give_spec] * pieces),
             scratch_shapes=[pltpu.VMEM((2 * half, depth), w.dtype)],
         ),
         out_shape=[pltpu.HBM((len(slots), half, cols), jnp.float32)]
@@ -137,62 +139,62 @@
     )(place, *blocks, *in_hbm([w_key, w_value, *after]))
 
 
-def add_kernel(tiles, per, paired, extra, *refs):
-    keep_ref, give_refs, out_ref = refs[0], refs[1 : 1 + tiles], refs[-1]
-    pair_refs = refs[1 + tiles : 1 + tiles + 2 * paired]
-    landed_refs = refs[1 + tiles + 2 * paired :][:extra]
-    j = pl.program_id(1)
-
-    def write(first_ref, second_ref):
-        total = first_ref[0] + second_ref[0].astype(jnp.float32)
-        for landed_ref in landed_refs:
-            total = total + landed_ref[0].astype(jnp.float32)
-        out_ref[0] = total.astype(out_ref.dtype)
-
-    for t, give_ref in enumerate(give_refs):
-
-        @pl.when(j // per == t)
-        def _():
-            write(keep_ref, give_ref)
-
+def add_kernel(gots, paired, extra, *refs):
+    keep_ref, got_refs, out_ref = refs[0], refs[1 : 1 + gots], refs[-1]
+    pair_refs = refs[1 + gots : 1 + gots + 2 * paired]
+    landed_refs = refs[1 + gots + 2 * paired :][: extra * (1 + paired)]
+    width = got_refs[0].shape[2]
+    cols = gots * width
+
+    def total(first, second, landed):
+        value = first + second.astype(jnp.float32)
+        for term in landed:
+            value = value + term.astype(jnp.float32)
+        return value.astype(out_ref.dtype)
+
+    for t, got_ref in enumerate(got_refs):
+        part = slice(t * width, (t + 1) * width)
+        landed = [landed_refs[0][0, :, part]] if extra else []
+        out_ref[0, :, part] = total(keep_ref[0, :, part], got_ref[0], landed)
     if paired:
-
-        @pl.when(j >= tiles * per)
-        def _():
-            write(*pair_refs)
-
-
-def add_rows(count, rows, b, keep, gots, start, pair=(), slot=0, landed=(), after=()):
+        landed = [landed_refs[1][0]] if extra else []
+        out_ref[0, :, cols:] = total(pair_refs[0][0], pair_refs[1][0], landed)
+
+
+def add_rows(first, count, rows, b, keep, gots, start, cols, pair=(), slot=0, landed=(), after=()):
     whole = keep.shape[2]
-    width = gots[0].shape[2]
-    step = math.gcd(width, pair[0].shape[2]) if pair else width
-    per, query = width // step, len(gots) * width // step
-    total = query + (pair[0].shape[2] // step if pair else 0)
-    first = start // step
-
-    def got(t):
-        return pl.BlockSpec((1, rows, step), lambda s, j: (s, b, jnp.clip(j - t * per, 0, per - 1)))
-
-    def columns(s, j):
-        return (s, 0, jnp.where(j < query, first + j, whole // step + j - query))
-
-    paired = pl.BlockSpec((1, rows, step), lambda s, j: (slot + s, 0, jnp.maximum(j - query, 0)))
-    return pl.pallas_call(
-        functools.partial(add_kernel, len(gots), per, len(pair) // 2, len(landed)),
-        grid=(count, total),
-        in_specs=[
-            pl.BlockSpec((1, rows, step), lambda s, j: (s, b, first + jnp.minimum(j, query - 1)))
-        ]
-        + [got(t) for t in range(len(gots))]
-        + [paired] * len(pair)
-        + [pl.BlockSpec((1, rows, step), columns)] * len(landed)
+    width = cols // len(gots)
+    shift = start // cols if gots[0].shape[2] == whole else 0
+    more = pair[0].shape[2] if pair else 0
+    keep_spec = pl.BlockSpec((1, rows, cols), lambda s: (first + s, b, start // cols))
+    got_spec = pl.BlockSpec((1, rows, width), lambda s: (first + s, b, shift))
+    pair_spec = pl.BlockSpec((1, rows, more), lambda s: (slot + s, 0, 0))
+    landed_specs = [pl.BlockSpec((1, rows, cols), lambda s: (s, 0, start // cols))]
+    if pair:
+        landed_specs.append(pl.BlockSpec((1, rows, more), lambda s: (s, 0, whole // more)))
+    landed_specs = landed_specs * len(landed)
+    return pl.pallas_call(
+        functools.partial(add_kernel, len(gots), len(pair) // 2, len(landed)),
+        grid=(count,),
+        in_specs=[keep_spec]
+        + [got_spec] * len(gots)
+        + [pair_spec] * len(pair)
+        + landed_specs
         + [pl.BlockSpec(memory_space=pl.ANY)] * len(after),
-        out_specs=pl.BlockSpec((1, rows, step), lambda s, j: (s, 0, j)),
-        out_shape=pltpu.HBM((count, rows, total * step), jnp.bfloat16),
+        out_specs=pl.BlockSpec((1, rows, cols + more), lambda s: (s, 0, 0)),
+        out_shape=pltpu.HBM((count, rows, cols + more), jnp.bfloat16),
         compiler_params=pltpu.CompilerParams(vmem_limit_bytes=VMEM_BYTES),
         cost_estimate=LIGHT,
         name="add_rows",
-    )(*in_hbm([keep]), *gots, *in_hbm(pair[:1]), *pair[1:], *landed, *in_hbm(after))
+    )(
+        *in_hbm([keep]),
+        *gots,
+        *in_hbm(pair[:1]),
+        *pair[1:],
+        *(list(landed) * (2 if pair else 1)),
+        *in_hbm(after[:1]),
+        *after[1:],
+    )
 
 
 def rotate_kernel(count, pieces, cos_ref, sin_ref, *refs):
@@ -220,7 +222,7 @@
 
 def sum_and_rotate(cosine, sine, terms, gots, cols, after=()):
     rows = cosine.shape[0]
-    slot_of_gots, block_of_gots, gots = gots
+    slot_of_gots, block_of_gots, shift, gots = gots
     tile = cols // max(1, len(gots))
     table = pl.BlockSpec((rows, DH), lambda j: (0, 0))
 
@@ -232,7 +234,7 @@
         grid=(cols // tile,),
         in_specs=[table, table]
         + [block(slot, b, start) for _, slot, b, start in terms]
-        + [pl.BlockSpec((1, rows, tile), lambda j: (slot_of_gots, block_of_gots, 0))] * len(gots)
+        + [pl.BlockSpec((1, rows, tile), lambda j: (slot_of_gots, block_of_gots, shift))] * len(gots)
         + [pl.BlockSpec(memory_space=pl.ANY)] * len(after),
         out_specs=pl.BlockSpec((rows, tile), lambda j: (0, j)),
         out_shape=jax.ShapeDtypeStruct((rows, cols), jnp.bfloat16),
@@ -397,7 +399,7 @@
         return x.astype(jnp.bfloat16)
 
     odd = list(range(3, shards, 2)) + [1]
-    even = list(range(2, shards, 2)) + [0]
+    even = list(range(2, shards, 2))
     fast_pair = heads_here == group
 
     def spread(live):
@@ -439,56 +441,65 @@
         return keep, [other_core(give) for give in gives], gives[0]
 
     def rotate(b, p, split, terms, behind):
-        cols, each = head_cols // split, len(even_got) // split
+        cols = head_cols // split
         table = slice(b * half, (b + 1) * half)
-        added = [(even_keep, len(even) - 1, b, p * cols), (fars[b], len(odd) - 1, 0, p * cols)]
-        added += [(term, 0, 0, 0) for term in terms]
-        gots = (len(even) - 1, b, even_got[p * each : (p + 1) * each])
-        turned = sum_and_rotate(cosine[table], sine[table], added, gots, cols, behind)
+        added = [(own_keep, 0, b, p * cols)] + terms
+        turned = sum_and_rotate(cosine[table], sine[table], added, (0, b, p, own_got), cols, behind)
         return turned, other_core(turned)
 
+    def add_even(b, start, cols, pair, behind):
+        if shards == 2:
+            return [], behind
+        keep, got = evens[b]
+        each = len(got) * cols // head_cols
+        got = got[start // cols * each :][:each]
+        summed = add_rows(
+            0, len(even), half, 0, keep, got, start, cols, pair, len(odd), (fars[b],), behind
+        )
+        terms, first = spread({x: summed[k] for k, x in enumerate(even)})
+        return [(term, 0, 0, 0) for term in terms], (first,)
+
     last, split = tps - 1, head_cols // tile
-    fars, pair, after = [], (), ()
     placed = in_hbm(blocks[:1]) + blocks[1:]
+    evens, fars, terms, pair, after = [], [], [], (), ()
     for b, block in enumerate(placed):
         if fast_pair and b == last:
-            pair_keep, give = project_pair(rindex, findex, odd + even, placed, w_key, w_value, after)
+            slots = odd + even + [0]
+            pair_keep, give = project_pair(rindex, findex, slots, placed, w_key, w_value, after)
             pair = (pair_keep, other_core(give))
             after = (give,)
-        odd_keep, odd_got, _ = project(odd, [block], tile, after)
-        odd_sent = add_rows(len(odd), half, 0, odd_keep, odd_got, 0, pair)
+        odd_keep, odd_got, given = project(odd, [block], tile, after)
+        count = len(odd) - 1 if b == last else len(odd)
+        odd_sent = add_rows(0, count, half, 0, odd_keep, odd_got, 0, head_cols, pair)
         fars.append(swap(odd_sent, 1))
         after = (odd_sent,)
-
-    even_keep, even_got, given = project(even, placed, min(512, tile), after + tuple(fars[:last]), HEAVY)
-    after = (given,)
-
-    def add_even(b, start, gots, pair, behind):
-        landed = (fars[b],) if shards > 2 else ()
-        summed = add_rows(
-            len(even) - 1, half, b, even_keep, gots, start, pair, len(odd), landed, behind
+        if b > 0:
+            added, after = add_even(b - 1, 0, head_cols, (), after)
+            terms.append([(fars[b - 1], len(odd) - 1, 0, 0)] + added)
+            after = (odd_sent,) + after
+        if b == last:
+            own_keep, own_got, given = project([0], placed, head_cols, after, HEAVY)
+            after = (given,)
+        even_keep, even_got, given = project(even, [block], tile, after)
+        evens.append((even_keep, even_got))
+        after = (given,)
+    parts, behind = [], tuple(term[0] for row in terms for term in row[1:])
+    for p in range(split):
+        near_sent = add_rows(
+            len(odd) - 1, 1, half, 0, odd_keep, odd_got[p : p + 1], p * tile, tile,
+            pair if p == 0 else (), len(odd) - 1, (), after,
         )
-        return spread({x: summed[k] for k, x in enumerate(even[:-1])})
-
-    terms = []
-    for b in range(tps):
-        parts = split if b == last else 1
-        each = len(even_got) // parts
-        row = []
-        for p in range(parts):
-            gots = even_got[p * each : (p + 1) * each]
-            cols = p * head_cols // parts
-            paired = pair if b == last and p == 0 else ()
-            added, first = add_even(b, cols, gots, paired, after)
-            row.append(added)
-            after = (first,)
-        terms.append(row)
-    parts = terms[last]
+        parts.append([(swap(near_sent, 1), 0, 0, 0)])
+        after = (near_sent,)
+    after = after + behind
+    for p in range(split):
+        added, after = add_even(last, p * tile, tile, pair if p == 0 else (), after)
+        parts[p] += added
 
     if fast_pair:
         width = 2 * DH * tps
         pieces = [(array, shards - 1, 0) for array in pair]
-        pieces += [(fars[last], len(odd) - 1, head_cols)] + [(term, 0, tile) for term in parts[0]]
+        pieces += [(term, 0, tile) for term, _, _, _ in parts[0]]
         key_rot, held = split_and_rotate(cosine, sine, pieces, width)
         bit = 1
         while bit < shards:
@@ -511,7 +522,7 @@
 
         mine = lax.dynamic_slice_in_dim(key_sum, findex * heads_here // group * DH, DH, 1)
         key_own = of_core(mine, rindex)
-        key_rot = sum_and_rotate(cosine, sine, [(key_own[None], 0, 0, 0)], (0, 0, []), DH, after)
+        key_rot = sum_and_rotate(cosine, sine, [(key_own[None], 0, 0, 0)], (0, 0, 0, []), DH, after)
         value_rows = low(jnp.concatenate([of_core(value_sum, rindex), of_core(value_sum, 1 - rindex)]))
 
     order, key_t = prepare(canary_rows, ids, key_rot, other_core(key_rot))
@@ -521,16 +532,15 @@
         values_mark = key_t
         values = low(jnp.dot(order, value_rows, preferred_element_type=jnp.float32))
 
-    rotated = [rotate(b, 0, 1, terms[b][0], after) for b in range(last)]
+    rotated = [rotate(b, 0, 1, terms[b], (key_rot,)) for b in range(last)]
     count = heads_here // split
     scores, mark = (), ()
     for p in range(split):
-        turned = rotate(last, p, split, terms[last][p], (key_t,) + mark)
+        turned = rotate(last, p, split, parts[p], (key_t,) + mark)
         queries = [(row[0], p * count) for row in rotated] + [(turned[0], 0)]
         queries += [(row[1], p * count) for row in rotated] + [(turned[1], 0)]
-        behind = (values_mark,) if p == split - 1 else ()
         *scores, mark = score_heads(
-            order, key_t, heads_here, p * count, count, queries, scores, behind
+            order, key_t, heads_here, p * count, count, queries, scores
         )
         mark = (mark,)
     return (scores[0], values)

time: 187 us -> 173 us (0.925)
  waiting for transfers between devices: 71.8 us -> 50.2 us
  starting transfers between devices: 15.8 us -> 20.8 us
  Pallas kernels: 90.9 us -> 94.7 us
  other arithmetic: 5.65 us -> 1.91 us
  local copies, waits for them, and re-layouts: 1.21 us -> 3.44 us
    ppermute x7 -> x9, waiting for transfers between devices: 54.4 us -> 42.4 us  [swap(): return lax.ppermute(x, 'fsdp', [(i, i ^ bit) for i in range(shards)])]
    ppermute x1, waiting for transfers between devices: 8.21 us -> 1.91 us  [body(): lax.ppermute(hidden, 'tp', [(i, (i - b) % tps) for i in range(tps)])]
    pallas_call x8 -> x12, Pallas kernels: 59.2 us -> 64.8 us  [the longest x5 48.2 us: project_query(): pl.pallas_call(functools.partial(query_kernel, count, pieces), grid_spec=...]
    ppermute x7 -> x9, starting transfers between devices: 10.2 us -> 14.3 us  [swap(): return lax.ppermute(x, 'fsdp', [(i, i ^ bit) for i in range(shards)])]
    ppermute x14 -> x15, waiting for transfers between devices: 9.18 us -> 5.9 us  [other_core(): return lax.ppermute(x, 'rep', [(0, 1), (1, 0)])]
    unnamed x16 -> x30, local copies, waits for them, and re-layouts: 0.05 us -> 2.28 us
    concatenate x2, other arithmetic: 2.22 us -> 0.22 us  [rope_tables(): jnp.concatenate([-sine, sine], axis=1)]
  transfers between devices with their start and end apart: 22 -> 25, of which waited for: 13 -> 10; matrix products, arithmetic and copies ran while one was open for 4% -> 2% of each run, Pallas kernels for 45% -> 51%
where the time goes in v5:
time: 173 us; the launch traced here: 172 us
  Pallas kernels  94.7 us (55%)
  waiting for transfers between devices  50.2 us (29%)
  starting transfers between devices  20.8 us (12%)
  local copies, waits for them, and re-layouts  3.44 us (2%)
  other arithmetic  1.91 us (1%)
    pallas_call x5, Pallas kernels, project_query(): pl.pallas_call(functools.partial(query_kernel, count, pieces), grid_spec=...  48.2 us
    ppermute x9, waiting for transfers between devices, swap(): return lax.ppermute(x, 'fsdp', [(i, i ^ bit) for i in range(shards)])  42.4 us
    pallas_call x7, Pallas kernels, add_rows(): pl.pallas_call(functools.partial(add_kernel, len(gots), len(pair) // 2, l...  16.5 us
    ppermute x9, starting transfers between devices, swap(): return lax.ppermute(x, 'fsdp', [(i, i ^ bit) for i in range(shards)])  14.3 us
    pallas_call x2, Pallas kernels, score_heads(): pl.pallas_call(functools.partial(score_kernel, len(queries)), grid=(count...  13.2 us
    pallas_call x1, Pallas kernels, project_pair(): pl.pallas_call(functools.partial(pair_kernel, count), grid_spec=pltpu.Pre...  7.09 us
    ppermute x15, waiting for transfers between devices, other_core(): return lax.ppermute(x, 'rep', [(0, 1), (1, 0)])  5.9 us
    pallas_call x3, Pallas kernels, sum_and_rotate(): pl.pallas_call(functools.partial(rotate_kernel, len(terms), len(gots)), g...  4.76 us
  transfers between devices with their start and end apart: 25, of which 10 were waited for; matrix products, arithmetic and copies ran while one was open for 2% of the time, Pallas kernels for 51%

profile of v5, /device:TPU:0, one launch (start us, length us, event | category | flops | bytes accessed | tf_op | source)
XLA Modules:
  0.0 172.0 jit_solution(1935122423108312800)
XLA Ops:
  0.6 3.0 %collective-permute-start = (bf16[320,2048]{1,0:T(8,128)(2,1)}, bf16[320,2048]{1,0:T(8,128)(2,1)S(1)}, u32[]{:S(2)}, u32[]{:S(2)}) collective-permute-start(bf16[320,2048]{1,0:T(8,128)(2,1)} %refs_0_.7), channel_id=1, source_target_pairs={{0,2},{2,0},{1,3},{3,1},{4,6},{6,4},{5,7},{7,5},{8,10},{10,8},{9,1... | collective-permute-start | bytes 3932168 | tf_op jit(solution)/shard_map/ppermute | solution.py:423
  3.7 11.9 %query_products.5 = (f32[2,160,2048]{2,1,0:T(8,128)}, bf16[2,160,1024]{2,1,0:T(8,128)(2,1)}, bf16[2,160,1024]{2,1,0:T(8,128)(2,1)}) custom-call(s32[3]{0:T(128)S(1)} %pad_add_fusion.2.place_ref, bf16[320,2048]{1,0:T(8,128)(2,1)} %refs_0_.7, bf16[2048,8192]{1,0:T(8,128)(2,1)} %refs_1_.7), custom_call_target="tpu_custom_call" | custom-call | flops 1000 | bytes 1000 | tf_op jit(solution)/shard_map/query_products/pallas_call | solution.py:76
  15.6 0.5 collective-permute-start.2
  16.1 1.8 %collective-permute-done.1.refs_1_ = bf16[2,160,1024]{2,1,0:T(8,128)(2,1)S(1)} collective-permute-done((bf16[2,160,1024]{2,1,0:T(8,128)(2,1)}, bf16[2,160,1024]{2,1,0:T(8,128)(2,1)S(1)}, u32[]{:S(2)}, u32[]{:S(2)}) %collective-permute-start.1) | collective-permute-done | bytes 655392 | tf_op jit(solution)/shard_map/ppermute | solution.py:396
  17.9 0.9 collective-permute-done.2.refs_2_
  18.9 2.7 %add_rows.7.refs_2_ = bf16[2,160,2048]{2,1,0:T(8,128)(2,1)} custom-call(f32[2,160,2048]{2,1,0:T(8,128)} %get-tuple-element.26.refs_0_, bf16[2,160,1024]{2,1,0:T(8,128)(2,1)S(1)} %collective-permute-done.1.refs_1_, bf16[2,160,1024]{2,1,0:T(8,128)(2,1)S(1)} %collective-permute-done.2.refs_2_), custom_call_target="tpu_custom_call" | custom-call | flops 1000 | bytes 1000 | tf_op jit(solution)/shard_map/add_rows/pallas_call | solution.py:176
  21.5 1.6 collective-permute-start.8
  23.3 7.5 %query_products.6 = (f32[1,160,2048]{2,1,0:T(8,128)}, bf16[1,160,1024]{2,1,0:T(8,128)(2,1)}, bf16[1,160,1024]{2,1,0:T(8,128)(2,1)}) custom-call(s32[2]{0:T(128)S(1)} %pad_add_fusion.1.place_ref, bf16[320,2048]{1,0:T(8,128)(2,1)} %refs_0_.7, bf16[2048,8192]{1,0:T(8,128)(2,1)} %refs_1_.7, bf16[2,160,2048]{2,1,0:T(8,128)(2,1)} %add_rows.7.refs_2_), custom_call_target="tpu_custom_call" | custom-call | flops 1000 | bytes 1000 | tf_op jit(solution)/shard_map/query_products/pallas_call | solution.py:76
  30.7 1.9 %collective-permute-done.refs_1_.refs_0_ = bf16[320,2048]{1,0:T(8,128)(2,1)S(1)} collective-permute-done((bf16[320,2048]{1,0:T(8,128)(2,1)}, bf16[320,2048]{1,0:T(8,128)(2,1)S(1)}, u32[]{:S(2)}, u32[]{:S(2)}) %collective-permute-start) | collective-permute-done | bytes 1310752 | tf_op jit(solution)/shard_map/ppermute | solution.py:423
  32.6 7.1 %key_value_products.1 = (f32[4,160,512]{2,1,0:T(8,128)}, bf16[4,160,512]{2,1,0:T(8,128)(2,1)}) custom-call(s32[5]{0:T(128)S(1)} %stack.25.place_ref, bf16[320,2048]{1,0:T(8,128)(2,1)} %refs_0_.7, bf16[320,2048]{1,0:T(8,128)(2,1)S(1)} %collective-permute-done.refs_1_.refs_0_, bf16[2048,512]{1,0:T(8,128)(2,1)} %refs_2_.2, bf16[2048,512]{1,0:T(8,128)(2,1)} %refs_3_.1, ...), custom_call_target="tpu_custom_call" | custom-call | flops 1000 | bytes 1000 | tf_op jit(solution)/shard_map/key_value_products/pallas_call | solution.py:121
  39.8 11.5 %query_products.7 = (f32[2,160,2048]{2,1,0:T(8,128)}, bf16[2,160,1024]{2,1,0:T(8,128)(2,1)}, bf16[2,160,1024]{2,1,0:T(8,128)(2,1)}) custom-call(s32[3]{0:T(128)S(1)} %pad_add_fusion.2.place_ref, bf16[320,2048]{1,0:T(8,128)(2,1)S(1)} %collective-permute-done.refs_1_.refs_0_, bf16[2048,8192]{1,0:T(8,128)(2,1)} %refs_1_.7, ...), custom_call_target="tpu_custom_call" | custom-call | flops 1000 | bytes 1000 | tf_op jit(solution)/shard_map/query_products/pallas_call | solution.py:76
  51.3 0.5 collective-permute-start.4
  52.4 1.3 collective-permute-done.4.refs_1_
  53.7 1.9 %collective-permute-done.5.refs_2_.refs_1_ = bf16[2,160,1024]{2,1,0:T(8,128)(2,1)S(1)} collective-permute-done((bf16[2,160,1024]{2,1,0:T(8,128)(2,1)}, bf16[2,160,1024]{2,1,0:T(8,128)(2,1)S(1)}, u32[]{:S(2)}, u32[]{:S(2)}) %collective-permute-start.5) | collective-permute-done | bytes 655392 | tf_op jit(solution)/shard_map/ppermute | solution.py:396
  55.6 2.6 %add_rows.8.refs_4_.refs_3_ = bf16[1,160,2560]{2,1,0:T(8,128)(2,1)} custom-call(f32[2,160,2048]{2,1,0:T(8,128)} %get-tuple-element.32.refs_0_, bf16[2,160,1024]{2,1,0:T(8,128)(2,1)S(1)} %collective-permute-done.4.refs_1_, bf16[2,160,1024]{2,1,0:T(8,128)(2,1)S(1)} %collective-permute-done.5.refs_2_.refs_1_, ...), custom_call_target="tpu_custom_call" | custom-call | flops 1000 | bytes 1000 | tf_op jit(solution)/shard_map/add_rows/pallas_call | solution.py:176
  58.2 1.8 %collective-permute-start.11 = (bf16[1,160,2560]{2,1,0:T(8,128)(2,1)}, bf16[1,160,2560]{2,1,0:T(8,128)(2,1)}, u32[]{:S(2)}, u32[]{:S(2)}) collective-permute-start(bf16[1,160,2560]{2,1,0:T(8,128)(2,1)} %add_rows.8.refs_4_.refs_3_), channel_id=1, source_target_pairs={{0,4},{4,0},{8,12},{12,8},{1,5},{5,1},{9,13},{13,9},{2,6},{6,2},{1... | collective-permute-start | bytes 2457608 | tf_op jit(solution)/shard_map/ppermute | solution.py:393
  60.1 2.8 %add_rows.9.refs_4_ = bf16[1,160,2048]{2,1,0:T(8,128)(2,1)} custom-call(f32[1,160,2048]{2,1,0:T(8,128)} %get-tuple-element.35.refs_0_, bf16[1,160,1024]{2,1,0:T(8,128)(2,1)S(1)} %collective-permute-done.6.refs_1_, bf16[1,160,1024]{2,1,0:T(8,128)(2,1)S(1)} %collective-permute-done.7.refs_2_, bf16[2,160,2048]{2,1,0:T(8,128)(2,1)S(1)} %collective-permute-done.8.refs_3_.refs_1_, ...), custom_call_target="tpu_custom_call" | custom-call | flops 1000 | bytes 1000 | tf_op jit(solution)/shard_map/add_rows/pallas_call | solution.py:176
  62.9 2.6 %collective-permute-start.12 = (bf16[1,160,2048]{2,1,0:T(8,128)(2,1)}, bf16[1,160,2048]{2,1,0:T(8,128)(2,1)}, u32[]{:S(2)}, u32[]{:S(2)}) collective-permute-start(bf16[1,160,2048]{2,1,0:T(8,128)(2,1)} %add_rows.9.refs_4_), channel_id=1, source_target_pairs={{0,8},{4,12},{8,0},{12,4},{1,9},{5,13},{9,1},{13,5},{2,10},{6,14},... | collective-permute-start | bytes 1966088 | tf_op jit(solution)/shard_map/ppermute | solution.py:393
  65.5 1.1 copy-done.9
  66.6 10.3 %query_products.8 = (f32[1,320,2048]{2,1,0:T(8,128)}, bf16[1,320,2048]{2,1,0:T(8,128)(2,1)}) custom-call(s32[2]{0:T(128)S(1)} %pad_add_fusion.3.place_ref, bf16[320,2048]{1,0:T(8,128)(2,1)} %refs_0_.7, bf16[320,2048]{1,0:T(8,128)(2,1)S(1)} %collective-permute-done.refs_1_.refs_0_, bf16[2048,8192]{1,0:T(8,128)(2,1)} %refs_1_.7, ...), custom_call_target="tpu_custom_call" | custom-call | flops 99999997952 | bytes 100000000 | tf_op jit(solution)/shard_map/query_products/pallas_call | solution.py:76
  77.0 7.0 %query_products.9 = (f32[1,160,2048]{2,1,0:T(8,128)}, bf16[1,160,1024]{2,1,0:T(8,128)(2,1)}, bf16[1,160,1024]{2,1,0:T(8,128)(2,1)}) custom-call(s32[2]{0:T(128)S(1)} %pad_add_fusion.1.place_ref, bf16[320,2048]{1,0:T(8,128)(2,1)S(1)} %collective-permute-done.refs_1_.refs_0_, bf16[2048,8192]{1,0:T(8,128)(2,1)} %refs_1_.7, ...), custom_call_target="tpu_custom_call" | custom-call | flops 1000 | bytes 1000 | tf_op jit(solution)/shard_map/query_products/pallas_call | solution.py:76
  84.0 0.5 collective-permute-start.10
  85.0 1.1 copy-done.5
  86.1 2.1 %add_rows.10.refs_2_ = bf16[1,160,1536]{2,1,0:T(8,128)(2,1)} custom-call(f32[2,160,2048]{2,1,0:T(8,128)} %get-tuple-element.32.refs_0_, bf16[2,160,1024]{2,1,0:T(8,128)(2,1)S(1)} %copy-done.5, f32[4,160,512]{2,1,0:T(8,128)} %get-tuple-element.30.refs_3_.refs_2_.refs_0_, bf16[4,160,512]{2,1,0:T(8,128)(2,1)S(1)} %collective-permute-done.3.refs_4_.refs_3_.refs_1_, ...), custom_call_target="tpu_custom_call" | custom-call | flops 1000 | bytes 1000 | tf_op jit(solution)/shard_map/add_rows/pallas_call | solution.py:176
  88.6 1.9 %add_rows.11.refs_6_ = bf16[1,160,1024]{2,1,0:T(8,128)(2,1)} custom-call(f32[2,160,2048]{2,1,0:T(8,128)} %get-tuple-element.32.refs_0_, bf16[2,160,1024]{2,1,0:T(8,128)(2,1)S(1)} %copy-done.3, bf16[1,160,1536]{2,1,0:T(8,128)(2,1)} %add_rows.10.refs_2_), custom_call_target="tpu_custom_call" | custom-call | flops 1000 | bytes 1000 | tf_op jit(solution)/shard_map/add_rows/pallas_call | solution.py:176
  90.5 2.5 %collective-permute-done.12.refs_7_.refs_2_ = bf16[1,160,2048]{2,1,0:T(8,128)(2,1)} collective-permute-done((bf16[1,160,2048]{2,1,0:T(8,128)(2,1)}, bf16[1,160,2048]{2,1,0:T(8,128)(2,1)}, u32[]{:S(2)}, u32[]{:S(2)}) %collective-permute-start.12) | collective-permute-done | bytes 655392 | tf_op jit(solution)/shard_map/ppermute | solution.py:393
  93.0 0.6 collective-permute-done.11.refs_4_.refs_5_.refs_2_
  93.6 2.3 %add_rows.12.refs_3_ = bf16[1,160,1536]{2,1,0:T(8,128)(2,1)} custom-call(f32[1,160,2048]{2,1,0:T(8,128)} %get-tuple-element.39.refs_0_, bf16[1,160,1024]{2,1,0:T(8,128)(2,1)} %collective-permute-done.10.refs_1_, f32[4,160,512]{2,1,0:T(8,128)} %get-tuple-element.30.refs_3_.refs_2_.refs_0_, ...), custom_call_target="tpu_custom_call" | custom-call | flops 1000 | bytes 1000 | tf_op jit(solution)/shard_map/add_rows/pallas_call | solution.py:176
  96.0 2.8 %collective-permute-start.13 = (bf16[1,160,1536]{2,1,0:T(8,128)(2,1)}, bf16[1,160,1536]{2,1,0:T(8,128)(2,1)S(1)}, u32[]{:S(2)}, u32[]{:S(2)}) collective-permute-start(bf16[1,160,1536]{2,1,0:T(8,128)(2,1)} %add_rows.12.refs_3_), channel_id=1, source_target_pairs={{0,8},{4,12},{8,0},{12,4},{1,9},{5,13},{9,1},{13,5},{2,10},{6,14},... | collective-permute-start | bytes 1474568 | tf_op jit(solution)/shard_map/ppermute | solution.py:393
  98.8 0.6 fusion.4
  100.0 10.6 %collective-permute-done.9.refs_2_.refs_1_ = bf16[1,160,1536]{2,1,0:T(8,128)(2,1)S(1)} collective-permute-done((bf16[1,160,1536]{2,1,0:T(8,128)(2,1)}, bf16[1,160,1536]{2,1,0:T(8,128)(2,1)S(1)}, u32[]{:S(2)}, u32[]{:S(2)}) %collective-permute-start.9) | collective-permute-done | bytes 491552 | tf_op jit(solution)/shard_map/ppermute | solution.py:393
  110.6 9.4 %collective-permute-done.13.refs_3_.refs_2_ = bf16[1,160,1536]{2,1,0:T(8,128)(2,1)S(1)} collective-permute-done((bf16[1,160,1536]{2,1,0:T(8,128)(2,1)}, bf16[1,160,1536]{2,1,0:T(8,128)(2,1)S(1)}, u32[]{:S(2)}, u32[]{:S(2)}) %collective-permute-start.13) | collective-permute-done | bytes 491552 | tf_op jit(solution)/shard_map/ppermute | solution.py:393
  120.0 1.3 split_and_rotate.1
  121.3 2.0 %sum_and_rotate.3.refs_0_ = bf16[160,2048]{1,0:T(8,128)(2,1)S(1)} custom-call(f32[160,128]{1,0:T(8,128)S(1)} %get-tuple-element.53.cos_ref, f32[160,128]{1,0:T(8,128)S(1)} %get-tuple-element.51.sin_ref, f32[1,320,2048]{2,1,0:T(8,128)} %get-tuple-element.43.refs_0_, bf16[2,160,2048]{2,1,0:T(8,128)(2,1)S(1)} %copy-done.1, ...), custom_call_target="tpu_custom_call" | custom-call | flops 1000 | bytes 1000 | tf_op jit(solution)/shard_map/sum_and_rotate/pallas_call | solution.py:232
  123.5 0.9 reshape.81.canary_ref
  124.5 0.5 collective-permute-start.14
  125.4 1.7 collective-permute-start.16
  127.1 2.1 %add_rows.13 = bf16[1,160,1024]{2,1,0:T(8,128)(2,1)} custom-call(f32[1,160,2048]{2,1,0:T(8,128)} %get-tuple-element.39.refs_0_, bf16[1,160,1024]{2,1,0:T(8,128)(2,1)} %collective-permute-done.17.refs_1_, bf16[1,160,2560]{2,1,0:T(8,128)(2,1)} %collective-permute-done.11.refs_4_.refs_5_.refs_2_, bf16[1,160,1536]{2,1,0:T(8,128)(2,1)} %add_rows.12.refs_3_), custom_call_target="tpu_custom_call" | custom-call | flops 1000 | bytes 1000 | tf_op jit(solution)/shard_map/add_rows/pallas_call | solution.py:176
  129.2 1.7 collective-permute-start.18
  131.0 0.6 order_and_keys.1
  131.5 1.3 sum_and_rotate.4.refs_1_
  133.0 1.3 collective-permute-start.23
  134.3 19.3 %collective-permute-done.23 = bf16[2,320,128]{2,1,0:T(8,128)(2,1)S(1)} collective-permute-done((bf16[2,320,128]{2,1,0:T(8,128)(2,1)S(1)}, bf16[2,320,128]{2,1,0:T(8,128)(2,1)S(1)}, u32[]{:S(2)}, u32[]{:S(2)}) %collective-permute-start.23) | collective-permute-done | bytes 163872 | tf_op jit(solution)/shard_map/ppermute | solution.py:393
  153.7 6.6 %score_heads.2 = (bf16[1,16,640,640]{3,2,1,0:T(8,128)(2,1)}, f32[8,128]{1,0:T(8,128)S(1)}) custom-call(bf16[640,640]{1,0:T(8,128)(2,1)S(1)} %get-tuple-element.41.order_ref, bf16[128,640]{1,0:T(8,128)(2,1)S(1)} %get-tuple-element.42.refs_4_.key_t_ref, bf16[160,2048]{1,0:T(8,128)(2,1)S(1)} %sum_and_rotate.3.refs_0_, ...), custom_call_target="tpu_custom_call" | custom-call | flops 1000 | bytes 1000 | tf_op jit(solution)/shard_map/score_heads/pallas_call | solution.py:354
  160.3 1.4 sum_and_rotate.5.refs_1_
  161.7 0.5 collective-permute-start.21
  162.3 3.1 %order_values.1 = (bf16[640,512]{1,0:T(8,128)(2,1)}, f32[8,128]{1,0:T(8,128)}) custom-call(s32[4]{0:T(128)S(1)} %pad_add_fusion.4.place_ref, bf16[640,640]{1,0:T(8,128)(2,1)S(1)} %get-tuple-element.41.order_ref, bf16[4,320,128]{2,1,0:T(8,128)(2,1)S(1)} %constant_dynamic-update-slice_fusion.own_ref, bf16[4,320,128]{2,1,0:T(8,128)(2,1)S(1)} %collective-permute-done.24.other_ref), custom_call_target="tpu_custom_call" | custom-call | tf_op jit(solution)/shard_map/order_values/pallas_call | solution.py:315
  165.3 6.6 %score_heads.3 = (bf16[1,16,640,640]{3,2,1,0:T(8,128)(2,1)}, f32[8,128]{1,0:T(8,128)}) custom-call(bf16[640,640]{1,0:T(8,128)(2,1)S(1)} %get-tuple-element.41.order_ref, bf16[128,640]{1,0:T(8,128)(2,1)S(1)} %get-tuple-element.42.refs_4_.key_t_ref, bf16[160,2048]{1,0:T(8,128)(2,1)S(1)} %sum_and_rotate.3.refs_0_, ...), custom_call_target="tpu_custom_call", output_to_operand_aliasing={{0}: (6, {})} | custom-call | flops 1000 | bytes 1000 | tf_op jit(solution)/shard_map/score_heads/pallas_call | solution.py:354
  (76 shorter events, 3.4 us)
Async XLA Ops:
  0.6 32.0 %collective-permute-start = (bf16[320,2048]{1,0:T(8,128)(2,1)}, bf16[320,2048]{1,0:T(8,128)(2,1)S(1)}, u32[]{:S(2)}, u32[]{:S(2)}) collective-permute-start(bf16[320,2048]{1,0:T(8,128)(2,1)} %refs_0_.7), channel_id=1, source_target_pairs={{0,2},{2,0},{1,3},{3,1},{4,6},{6,4},{5,7},{7,5},{8,10},{10,8},{9,1... | collective-permute-start | bytes 3932168 | tf_op jit(solution)/shard_map/ppermute | solution.py:423
  15.6 2.3 %collective-permute-start.1 = (bf16[2,160,1024]{2,1,0:T(8,128)(2,1)}, bf16[2,160,1024]{2,1,0:T(8,128)(2,1)S(1)}, u32[]{:S(2)}, u32[]{:S(2)}) collective-permute-start(bf16[2,160,1024]{2,1,0:T(8,128)(2,1)} %get-tuple-element.27), channel_id=1, source_target_pairs={{0,1},{1,0},{2,3},{3,2},{4,5},{5,4},{6,7},{7,6},{8,9},{9,8},{10,11... | collective-permute-start | bytes 1966088 | tf_op jit(solution)/shard_map/ppermute | solution.py:396
  15.6 3.2 %collective-permute-start.2 = (bf16[2,160,1024]{2,1,0:T(8,128)(2,1)}, bf16[2,160,1024]{2,1,0:T(8,128)(2,1)S(1)}, u32[]{:S(2)}, u32[]{:S(2)}) collective-permute-start(bf16[2,160,1024]{2,1,0:T(8,128)(2,1)} %get-tuple-element.28), channel_id=1, source_target_pairs={{0,1},{1,0},{2,3},{3,2},{4,5},{5,4},{6,7},{7,6},{8,9},{9,8},{10,11... | collective-permute-start | bytes 1966088 | tf_op jit(solution)/shard_map/ppermute | solution.py:396
  21.5 38.5 %collective-permute-start.8 = (bf16[2,160,2048]{2,1,0:T(8,128)(2,1)}, bf16[2,160,2048]{2,1,0:T(8,128)(2,1)S(1)}, u32[]{:S(2)}, u32[]{:S(2)}) collective-permute-start(bf16[2,160,2048]{2,1,0:T(8,128)(2,1)} %add_rows.7.refs_2_), channel_id=1, source_target_pairs={{0,4},{4,0},{8,12},{12,8},{1,5},{5,1},{9,13},{13,9},{2,6},{6,2},{1... | collective-permute-start | bytes 3932168 | tf_op jit(solution)/shard_map/ppermute | solution.py:393
  39.7 12.1 %copy-start.10 = (bf16[1,160,1024]{2,1,0:T(8,128)(2,1)S(1)}, bf16[1,160,1024]{2,1,0:T(8,128)(2,1)}, u32[]{:S(2)}) copy-start(bf16[1,160,1024]{2,1,0:T(8,128)(2,1)} %get-tuple-element.29.refs_4_) | copy-start | bytes 983044
  39.7 12.6 %copy-start.13 = (bf16[1,160,1024]{2,1,0:T(8,128)(2,1)S(1)}, bf16[1,160,1024]{2,1,0:T(8,128)(2,1)}, u32[]{:S(2)}) copy-start(bf16[1,160,1024]{2,1,0:T(8,128)(2,1)} %get-tuple-element.36) | copy-start | bytes 983044
  39.7 12.6 %collective-permute-start.3 = (bf16[4,160,512]{2,1,0:T(8,128)(2,1)}, bf16[4,160,512]{2,1,0:T(8,128)(2,1)S(1)}, u32[]{:S(2)}, u32[]{:S(2)}) collective-permute-start(bf16[4,160,512]{2,1,0:T(8,128)(2,1)} %get-tuple-element.31.refs_2_), channel_id=1, source_target_pairs={{0,1},{1,0},{2,3},{3,2},{4,5},{5,4},{6,7},{7,6},{8,9},{9,8},{10,11... | collective-permute-start | bytes 1966088 | tf_op jit(solution)/shard_map/ppermute | solution.py:396
  51.3 2.4 %collective-permute-start.4 = (bf16[2,160,1024]{2,1,0:T(8,128)(2,1)}, bf16[2,160,1024]{2,1,0:T(8,128)(2,1)S(1)}, u32[]{:S(2)}, u32[]{:S(2)}) collective-permute-start(bf16[2,160,1024]{2,1,0:T(8,128)(2,1)} %get-tuple-element.33), channel_id=1, source_target_pairs={{0,1},{1,0},{2,3},{3,2},{4,5},{5,4},{6,7},{7,6},{8,9},{9,8},{10,11... | collective-permute-start | bytes 1966088 | tf_op jit(solution)/shard_map/ppermute | solution.py:396
  51.8 3.8 %collective-permute-start.5 = (bf16[2,160,1024]{2,1,0:T(8,128)(2,1)}, bf16[2,160,1024]{2,1,0:T(8,128)(2,1)S(1)}, u32[]{:S(2)}, u32[]{:S(2)}) collective-permute-start(bf16[2,160,1024]{2,1,0:T(8,128)(2,1)} %get-tuple-element.34), channel_id=1, source_target_pairs={{0,1},{1,0},{2,3},{3,2},{4,5},{5,4},{6,7},{7,6},{8,9},{9,8},{10,11... | collective-permute-start | bytes 1966088 | tf_op jit(solution)/shard_map/ppermute | solution.py:396
  51.8 8.3 %collective-permute-start.6 = (bf16[1,160,1024]{2,1,0:T(8,128)(2,1)S(1)}, bf16[1,160,1024]{2,1,0:T(8,128)(2,1)S(1)}, u32[]{:S(2)}, u32[]{:S(2)}) collective-permute-start(bf16[1,160,1024]{2,1,0:T(8,128)(2,1)S(1)} %copy-done.10), channel_id=1, source_target_pairs={{0,1},{1,0},{2,3},{3,2},{4,5},{5,4},{6,7},{7,6},{8,9},{9,8},{10,11... | collective-permute-start | bytes 983048 | tf_op jit(solution)/shard_map/ppermute | solution.py:396
  52.3 7.8 %collective-permute-start.7 = (bf16[1,160,1024]{2,1,0:T(8,128)(2,1)S(1)}, bf16[1,160,1024]{2,1,0:T(8,128)(2,1)S(1)}, u32[]{:S(2)}, u32[]{:S(2)}) collective-permute-start(bf16[1,160,1024]{2,1,0:T(8,128)(2,1)S(1)} %copy-done.13), channel_id=1, source_target_pairs={{0,1},{1,0},{2,3},{3,2},{4,5},{5,4},{6,7},{7,6},{8,9},{9,8},{10,11... | collective-permute-start | bytes 983048 | tf_op jit(solution)/shard_map/ppermute | solution.py:396
  53.7 4.5 %copy-start.4 = (bf16[2,160,1024]{2,1,0:T(8,128)(2,1)}, bf16[2,160,1024]{2,1,0:T(8,128)(2,1)S(1)}, u32[]{:S(2)}) copy-start(bf16[2,160,1024]{2,1,0:T(8,128)(2,1)S(1)} %collective-permute-done.4.refs_1_) | copy-start | bytes 1966084
  55.6 2.6 %copy-start.2 = (bf16[2,160,1024]{2,1,0:T(8,128)(2,1)}, bf16[2,160,1024]{2,1,0:T(8,128)(2,1)S(1)}, u32[]{:S(2)}) copy-start(bf16[2,160,1024]{2,1,0:T(8,128)(2,1)S(1)} %collective-permute-done.5.refs_2_.refs_1_) | copy-start | bytes 1966084
  58.2 35.4 %collective-permute-start.11 = (bf16[1,160,2560]{2,1,0:T(8,128)(2,1)}, bf16[1,160,2560]{2,1,0:T(8,128)(2,1)}, u32[]{:S(2)}, u32[]{:S(2)}) collective-permute-start(bf16[1,160,2560]{2,1,0:T(8,128)(2,1)} %add_rows.8.refs_4_.refs_3_), channel_id=1, source_target_pairs={{0,4},{4,0},{8,12},{12,8},{1,5},{5,1},{9,13},{13,9},{2,6},{6,2},{1... | collective-permute-start | bytes 2457608 | tf_op jit(solution)/shard_map/ppermute | solution.py:393
  60.1 2.8 %copy-start = (bf16[2,160,2048]{2,1,0:T(8,128)(2,1)}, bf16[2,160,2048]{2,1,0:T(8,128)(2,1)S(1)}, u32[]{:S(2)}) copy-start(bf16[2,160,2048]{2,1,0:T(8,128)(2,1)S(1)} %collective-permute-done.8.refs_3_.refs_1_) | copy-start | bytes 3932164
  62.9 30.1 %collective-permute-start.12 = (bf16[1,160,2048]{2,1,0:T(8,128)(2,1)}, bf16[1,160,2048]{2,1,0:T(8,128)(2,1)}, u32[]{:S(2)}, u32[]{:S(2)}) collective-permute-start(bf16[1,160,2048]{2,1,0:T(8,128)(2,1)} %add_rows.9.refs_4_), channel_id=1, source_target_pairs={{0,8},{4,12},{8,0},{12,4},{1,9},{5,13},{9,1},{13,5},{2,10},{6,14},... | collective-permute-start | bytes 1966088 | tf_op jit(solution)/shard_map/ppermute | solution.py:393
  65.5 1.1 copy-start.9
  77.0 44.3 %collective-permute-start.15 = (bf16[1,320,2048]{2,1,0:T(8,128)(2,1)}, bf16[1,320,2048]{2,1,0:T(8,128)(2,1)S(1)}, u32[]{:S(2)}, u32[]{:S(2)}) collective-permute-start(bf16[1,320,2048]{2,1,0:T(8,128)(2,1)} %get-tuple-element.37.refs_2_), channel_id=1, source_target_pairs={{0,1},{1,0},{2,3},{3,2},{4,5},{5,4},{6,7},{7,6},{8,9},{9,8},{10,11... | collective-permute-start | bytes 3932168 | tf_op jit(solution)/shard_map/ppermute | solution.py:396
  77.0 7.7 %copy-start.11 = (s32[640]{0:T(1024)S(1)}, s32[640]{0:T(1024)}, u32[]{:S(2)}) copy-start(s32[640]{0:T(1024)} %param.10) | copy-start | bytes 7684
  77.0 7.7 %copy-start.12 = (s32[640]{0:T(1024)S(1)}, s32[640]{0:T(1024)}, u32[]{:S(2)}) copy-start(s32[640]{0:T(1024)} %param.11) | copy-start | bytes 7684
  84.0 6.5 %collective-permute-start.10 = (bf16[1,160,1024]{2,1,0:T(8,128)(2,1)}, bf16[1,160,1024]{2,1,0:T(8,128)(2,1)}, u32[]{:S(2)}, u32[]{:S(2)}) collective-permute-start(bf16[1,160,1024]{2,1,0:T(8,128)(2,1)} %get-tuple-element.38.refs_4_), channel_id=1, source_target_pairs={{0,1},{1,0},{2,3},{3,2},{4,5},{5,4},{6,7},{7,6},{8,9},{9,8},{10,11... | collective-permute-start | bytes 983048 | tf_op jit(solution)/shard_map/ppermute | solution.py:396
  85.0 1.1 copy-start.5
  86.1 2.6 %copy-start.3 = (bf16[2,160,1024]{2,1,0:T(8,128)(2,1)S(1)}, bf16[2,160,1024]{2,1,0:T(8,128)(2,1)}, u32[]{:S(2)}) copy-start(bf16[2,160,1024]{2,1,0:T(8,128)(2,1)} %copy-done.2) | copy-start | bytes 1966084
  88.2 22.4 %collective-permute-start.9 = (bf16[1,160,1536]{2,1,0:T(8,128)(2,1)}, bf16[1,160,1536]{2,1,0:T(8,128)(2,1)S(1)}, u32[]{:S(2)}, u32[]{:S(2)}) collective-permute-start(bf16[1,160,1536]{2,1,0:T(8,128)(2,1)} %add_rows.10.refs_2_), channel_id=1, source_target_pairs={{0,4},{4,0},{8,12},{12,8},{1,5},{5,1},{9,13},{13,9},{2,6},{6,2},{1... | collective-permute-start | bytes 1474568 | tf_op jit(solution)/shard_map/ppermute | solution.py:393
  96.0 24.0 %collective-permute-start.13 = (bf16[1,160,1536]{2,1,0:T(8,128)(2,1)}, bf16[1,160,1536]{2,1,0:T(8,128)(2,1)S(1)}, u32[]{:S(2)}, u32[]{:S(2)}) collective-permute-start(bf16[1,160,1536]{2,1,0:T(8,128)(2,1)} %add_rows.12.refs_3_), channel_id=1, source_target_pairs={{0,8},{4,12},{8,0},{12,4},{1,9},{5,13},{9,1},{13,5},{2,10},{6,14},... | collective-permute-start | bytes 1474568 | tf_op jit(solution)/shard_map/ppermute | solution.py:393
  99.9 21.4 %copy-start.1 = (bf16[2,160,2048]{2,1,0:T(8,128)(2,1)S(1)}, bf16[2,160,2048]{2,1,0:T(8,128)(2,1)}, u32[]{:S(2)}) copy-start(bf16[2,160,2048]{2,1,0:T(8,128)(2,1)} %copy-done) | copy-start | bytes 3932164
  99.9 27.2 %collective-permute-start.17 = (bf16[1,160,1024]{2,1,0:T(8,128)(2,1)}, bf16[1,160,1024]{2,1,0:T(8,128)(2,1)}, u32[]{:S(2)}, u32[]{:S(2)}) collective-permute-start(bf16[1,160,1024]{2,1,0:T(8,128)(2,1)} %get-tuple-element.44), channel_id=1, source_target_pairs={{0,1},{1,0},{2,3},{3,2},{4,5},{5,4},{6,7},{7,6},{8,9},{9,8},{10,11... | collective-permute-start | bytes 983048 | tf_op jit(solution)/shard_map/ppermute | solution.py:396
  120.0 1.3 copy-start.6
  123.4 30.3 %collective-permute-start.19 = (bf16[160,2048]{1,0:T(8,128)(2,1)S(1)}, bf16[160,2048]{1,0:T(8,128)(2,1)S(1)}, u32[]{:S(2)}, u32[]{:S(2)}) collective-permute-start(bf16[160,2048]{1,0:T(8,128)(2,1)S(1)} %sum_and_rotate.3.refs_0_), channel_id=1, source_target_pairs={{0,1},{1,0},{2,3},{3,2},{4,5},{5,4},{6,7},{7,6},{8,9},{9,8},{10,11... | collective-permute-start | bytes 1966088 | tf_op jit(solution)/shard_map/ppermute | solution.py:396
  124.5 6.5 %collective-permute-start.14 = (bf16[320,128]{1,0:T(8,128)(2,1)S(1)}, bf16[320,128]{1,0:T(8,128)(2,1)S(1)}, u32[]{:S(2)}, u32[]{:S(2)}) collective-permute-start(bf16[320,128]{1,0:T(8,128)(2,1)S(1)} %get-tuple-element.40.own_ref.refs_4_), channel_id=1, source_target_pairs={{0,1},{1,0},{2,3},{3,2},{4,5},{5,4},{6,7},{7,6},{8,9},{9,8},{10,11... | collective-permute-start | bytes 245768 | tf_op jit(solution)/shard_map/ppermute | solution.py:396
  125.0 8.0 %collective-permute-start.22 = (bf16[1,320,128]{2,1,0:T(8,128)(2,1)S(1)}, bf16[1,320,128]{2,1,0:T(8,128)(2,1)S(1)}, u32[]{:S(2)}, u32[]{:S(2)}) collective-permute-start(bf16[1,320,128]{2,1,0:T(8,128)(2,1)S(1)} %get-tuple-element.48), channel_id=1, source_target_pairs={{0,4},{4,0},{8,12},{12,8},{1,5},{5,1},{9,13},{13,9},{2,6},{6,2},{1... | collective-permute-start | bytes 245768 | tf_op jit(solution)/shard_map/ppermute | solution.py:393
  125.4 5.5 %copy-start.8 = (s32[640,1]{1,0:T(8,128)S(1)}, s32[640,1]{1,0:T(8,128)}, u32[]{:S(2)}) copy-start(s32[640,1]{1,0:T(8,128)} %reshape.81.canary_ref) | copy-start | bytes 7684
  125.4 6.1 %copy-start.7 = (bf16[1,160,1536]{2,1,0:T(8,128)(2,1)S(1)}, bf16[1,160,1536]{2,1,0:T(8,128)(2,1)}, u32[]{:S(2)}) copy-start(bf16[1,160,1536]{2,1,0:T(8,128)(2,1)} %copy-done.6) | copy-start | bytes 1474564
  125.4 34.8 %collective-permute-start.16 = (bf16[1,160,1024]{2,1,0:T(8,128)(2,1)}, bf16[1,160,1024]{2,1,0:T(8,128)(2,1)S(1)}, u32[]{:S(2)}, u32[]{:S(2)}) collective-permute-start(bf16[1,160,1024]{2,1,0:T(8,128)(2,1)} %add_rows.11.refs_6_), channel_id=1, source_target_pairs={{0,4},{4,0},{8,12},{12,8},{1,5},{5,1},{9,13},{13,9},{2,6},{6,2},{1... | collective-permute-start | bytes 983048 | tf_op jit(solution)/shard_map/ppermute | solution.py:393
  129.2 31.1 %collective-permute-start.18 = (bf16[1,160,1024]{2,1,0:T(8,128)(2,1)}, bf16[1,160,1024]{2,1,0:T(8,128)(2,1)S(1)}, u32[]{:S(2)}, u32[]{:S(2)}) collective-permute-start(bf16[1,160,1024]{2,1,0:T(8,128)(2,1)} %add_rows.13), channel_id=1, source_target_pairs={{0,8},{4,12},{8,0},{12,4},{1,9},{5,13},{9,1},{13,5},{2,10},{6,14},... | collective-permute-start | bytes 983048 | tf_op jit(solution)/shard_map/ppermute | solution.py:393
  132.9 20.8 %collective-permute-start.20 = (bf16[160,1024]{1,0:T(8,128)(2,1)S(1)}, bf16[160,1024]{1,0:T(8,128)(2,1)S(1)}, u32[]{:S(2)}, u32[]{:S(2)}) collective-permute-start(bf16[160,1024]{1,0:T(8,128)(2,1)S(1)} %sum_and_rotate.4.refs_1_), channel_id=1, source_target_pairs={{0,1},{1,0},{2,3},{3,2},{4,5},{5,4},{6,7},{7,6},{8,9},{9,8},{10,11... | collective-permute-start | bytes 983048 | tf_op jit(solution)/shard_map/ppermute | solution.py:396
  133.0 20.6 %collective-permute-start.23 = (bf16[2,320,128]{2,1,0:T(8,128)(2,1)S(1)}, bf16[2,320,128]{2,1,0:T(8,128)(2,1)S(1)}, u32[]{:S(2)}, u32[]{:S(2)}) collective-permute-start(bf16[2,320,128]{2,1,0:T(8,128)(2,1)S(1)} %pad_maximum_fusion), channel_id=1, source_target_pairs={{0,8},{4,12},{8,0},{12,4},{1,9},{5,13},{9,1},{13,5},{2,10},{6,14},... | collective-permute-start | bytes 491528 | tf_op jit(solution)/shard_map/ppermute | solution.py:393
  153.6 8.7 %collective-permute-start.24 = (bf16[4,320,128]{2,1,0:T(8,128)(2,1)S(1)}, bf16[4,320,128]{2,1,0:T(8,128)(2,1)S(1)}, u32[]{:S(2)}, u32[]{:S(2)}) collective-permute-start(bf16[4,320,128]{2,1,0:T(8,128)(2,1)S(1)} %constant_dynamic-update-slice_fusion.own_ref), channel_id=1, source_target_pairs={{0,1},{1,0},{2,3},{3,2},{4,5},{5,4},{6,7},{7,6},{8,9},{9,8},{10,11... | collective-permute-start | bytes 983048 | tf_op jit(solution)/shard_map/ppermute | solution.py:396
  161.7 3.7 %collective-permute-start.21 = (bf16[160,1024]{1,0:T(8,128)(2,1)S(1)}, bf16[160,1024]{1,0:T(8,128)(2,1)S(1)}, u32[]{:S(2)}, u32[]{:S(2)}) collective-permute-start(bf16[160,1024]{1,0:T(8,128)(2,1)S(1)} %sum_and_rotate.5.refs_1_), channel_id=1, source_target_pairs={{0,1},{1,0},{2,3},{3,2},{4,5},{5,4},{6,7},{7,6},{8,9},{9,8},{10,11... | collective-permute-start | bytes 983048 | tf_op jit(solution)/shard_map/ppermute | solution.py:396

commit v6 on v5

--- a/solution.py
+++ b/solution.py
@@ -258,7 +258,7 @@
         value_ref[0, rows] = total[:, (2 * b + 1) * DH : (2 * b + 2) * DH].astype(value_ref.dtype)
 
 
-def split_and_rotate(cosine, sine, terms, width):
+def split_and_rotate(cosine, sine, terms, width, after):
     rows = cosine.shape[0]
     half = terms[0][0].shape[1]
     table = pl.BlockSpec((rows, DH), lambda j: (0, 0))
@@ -269,7 +269,9 @@
     return pl.pallas_call(
         functools.partial(split_kernel, len(terms)),
         grid=(1,),
-        in_specs=[table, table] + [block(slot, start) for _, slot, start in terms],
+        in_specs=[table, table]
+        + [block(slot, start) for _, slot, start in terms]
+        + [pl.BlockSpec(memory_space=pl.ANY)] * len(after),
         out_specs=[table, pl.BlockSpec((1, rows, DH), lambda j: (0, 0, 0))],
         out_shape=[
             jax.ShapeDtypeStruct((rows, DH), jnp.bfloat16),
@@ -278,7 +280,7 @@
         compiler_params=pltpu.CompilerParams(vmem_limit_bytes=VMEM_BYTES),
         cost_estimate=LIGHT,
         name="split_and_rotate",
-    )(cosine, sine, *in_hbm([terms[0][0]]), *[term for term, _, _ in terms[1:]])
+    )(cosine, sine, *in_hbm([terms[0][0]]), *[term for term, _, _ in terms[1:]], *after)
 
 
 def prepare_kernel(canary_ref, ids_ref, own_ref, other_ref, order_ref, key_t_ref):
@@ -301,8 +303,30 @@
     )(canary_rows.reshape(rows, 1), ids.reshape(1, rows), own, other)
 
 
-def value_kernel(place_ref, order_ref, own_ref, other_ref, out_ref, mark_ref):
-    mark_ref[...] = jnp.zeros_like(mark_ref)
+def stack_kernel(count, *refs):
+    out_ref, start = refs[-1], 0
+    for ref in refs[:count]:
+        out_ref[start : start + ref.shape[0]] = ref[...]
+        start += ref.shape[0]
+
+
+def stack_slots(arrays, after):
+    slots = sum(x.shape[0] for x in arrays)
+    shape = (slots,) + arrays[0].shape[1:]
+    return pl.pallas_call(
+        functools.partial(stack_kernel, len(arrays)),
+        grid=(1,),
+        in_specs=[pl.BlockSpec(x.shape, lambda j: (0, 0, 0)) for x in arrays]
+        + [pl.BlockSpec(memory_space=pl.ANY)] * len(after),
+        out_specs=pl.BlockSpec(shape, lambda j: (0, 0, 0)),
+        out_shape=jax.ShapeDtypeStruct(shape, arrays[0].dtype),
+        compiler_params=pltpu.CompilerParams(vmem_limit_bytes=VMEM_BYTES),
+        cost_estimate=LIGHT,
+        name="stack_slots",
+    )(*arrays, *after)
+
+
+def value_kernel(place_ref, order_ref, own_ref, other_ref, out_ref):
     rows = jnp.concatenate([own_ref[0], other_ref[0]], axis=0)
     out_ref[...] = jnp.dot(order_ref[...], rows, preferred_element_type=jnp.float32).astype(out_ref.dtype)
 
@@ -318,15 +342,9 @@
             num_scalar_prefetch=1,
             grid=(slots,),
             in_specs=[pl.BlockSpec((rows, rows), lambda s, place: (0, 0)), block, block],
-            out_specs=[
-                pl.BlockSpec((rows, width), lambda s, place: (0, s)),
-                pl.BlockSpec((8, DH), lambda s, place: (0, 0)),
-            ],
+            out_specs=pl.BlockSpec((rows, width), lambda s, place: (0, s)),
         ),
-        out_shape=[
-            jax.ShapeDtypeStruct((rows, slots * width), jnp.bfloat16),
-            jax.ShapeDtypeStruct((8, DH), jnp.float32),
-        ],
+        out_shape=jax.ShapeDtypeStruct((rows, slots * width), jnp.bfloat16),
         compiler_params=pltpu.CompilerParams(vmem_limit_bytes=VMEM_BYTES),
         name="order_values",
     )(place, order, own, other)
@@ -443,8 +461,9 @@
     def rotate(b, p, split, terms, behind):
         cols = head_cols // split
         table = slice(b * half, (b + 1) * half)
-        added = [(own_keep, 0, b, p * cols)] + terms
-        turned = sum_and_rotate(cosine[table], sine[table], added, (0, b, p, own_got), cols, behind)
+        keep, got = owns[b]
+        added = [(keep, 0, 0, p * cols)] + terms
+        turned = sum_and_rotate(cosine[table], sine[table], added, (0, 0, p, got), cols, behind)
         return turned, other_core(turned)
 
     def add_even(b, start, cols, pair, behind):
@@ -461,7 +480,7 @@
 
     last, split = tps - 1, head_cols // tile
     placed = in_hbm(blocks[:1]) + blocks[1:]
-    evens, fars, terms, pair, after = [], [], [], (), ()
+    evens, owns, fars, terms, pair, after = [], [], [], [], (), ()
     for b, block in enumerate(placed):
         if fast_pair and b == last:
             slots = odd + even + [0]
@@ -478,8 +497,11 @@
             terms.append([(fars[b - 1], len(odd) - 1, 0, 0)] + added)
             after = (odd_sent,) + after
         if b == last:
-            own_keep, own_got, given = project([0], placed, head_cols, after, HEAVY)
-            after = (given,)
+            for c, near in enumerate(placed):
+                cost = LIGHT if c else HEAVY
+                own_keep, own_got, given = project([0], [near], head_cols, after, cost)
+                owns.append((own_keep, own_got))
+                after = (given,)
         even_keep, even_got, given = project(even, [block], tile, after)
         evens.append((even_keep, even_got))
         after = (given,)
@@ -500,12 +522,11 @@
         width = 2 * DH * tps
         pieces = [(array, shards - 1, 0) for array in pair]
         pieces += [(term, 0, tile) for term, _, _, _ in parts[0]]
-        key_rot, held = split_and_rotate(cosine, sine, pieces, width)
-        bit = 1
-        while bit < shards:
-            held = jnp.concatenate([held, swap(held, bit)])
-            bit *= 2
-        held_other = other_core(held)
+        key_rot, held = split_and_rotate(cosine, sine, pieces, width, after)
+        held = [held]
+        while 2 ** len(held) <= shards:
+            known = held[0] if len(held) == 1 else jnp.concatenate(held)
+            held.append(swap(known, 2 ** (len(held) - 1)))
     else:
         x = jnp.concatenate(blocks, axis=0)
         key_sum, value_sum = lax.psum(
@@ -526,23 +547,23 @@
         value_rows = low(jnp.concatenate([of_core(value_sum, rindex), of_core(value_sum, 1 - rindex)]))
 
     order, key_t = prepare(canary_rows, ids, key_rot, other_core(key_rot))
-    if fast_pair:
-        values, values_mark = order_values(findex, order, held, held_other)
-    else:
-        values_mark = key_t
+    if not fast_pair:
         values = low(jnp.dot(order, value_rows, preferred_element_type=jnp.float32))
 
-    rotated = [rotate(b, 0, 1, terms[b], (key_rot,)) for b in range(last)]
+    rotated = [rotate(b, 0, 1, terms[b], after) for b in range(last)]
     count = heads_here // split
     scores, mark = (), ()
     for p in range(split):
-        turned = rotate(last, p, split, parts[p], (key_t,) + mark)
+        turned = rotate(last, p, split, parts[p], mark)
         queries = [(row[0], p * count) for row in rotated] + [(turned[0], 0)]
         queries += [(row[1], p * count) for row in rotated] + [(turned[1], 0)]
         *scores, mark = score_heads(
             order, key_t, heads_here, p * count, count, queries, scores
         )
         mark = (mark,)
+        if fast_pair and p == 0:
+            held = stack_slots(held, mark)
+            values = order_values(findex, order, held, other_core(held))
     return (scores[0], values)
 
 

time: 173 us -> 163 us (0.942)
  waiting for transfers between devices: 50.2 us -> 33.5 us
  local copies, waits for them, and re-layouts: 3.44 us -> 8.55 us
  Pallas kernels: 94.7 us -> 99.8 us
  starting transfers between devices: 20.8 us -> 16.8 us
    ppermute x9, waiting for transfers between devices: 42.4 us -> 25.7 us  [swap(): return lax.ppermute(x, 'fsdp', [(i, i ^ bit) for i in range(shards)])]
    unnamed x30 -> x34, local copies, waits for them, and re-layouts: 2.28 us -> 8.16 us
    ppermute x9, starting transfers between devices: 14.3 us -> 10.2 us  [swap(): return lax.ppermute(x, 'fsdp', [(i, i ^ bit) for i in range(shards)])]
    pallas_call x5 -> x6, Pallas kernels: 48.2 us -> 52.1 us  [project_query(): pl.pallas_call(functools.partial(query_kernel, count, pieces), grid_spec=...]
    ppermute x15 -> x16, waiting for transfers between devices: 5.9 us -> 6 us  [other_core(): return lax.ppermute(x, 'rep', [(0, 1), (1, 0)])]
    ppermute x15 -> x16, starting transfers between devices: 3.48 us -> 3.54 us  [other_core(): return lax.ppermute(x, 'rep', [(0, 1), (1, 0)])]
  transfers between devices with their start and end apart: 25 -> 26, of which waited for: 10 -> 9; matrix products, arithmetic and copies ran while one was open for 2% -> 2% of each run, Pallas kernels for 51% -> 60%
where the time goes in v6:
time: 163 us; the launch traced here: 162 us
  Pallas kernels  99.8 us (61%)
  waiting for transfers between devices  33.5 us (21%)
  starting transfers between devices  16.8 us (10%)
  local copies, waits for them, and re-layouts  8.55 us (5%)
  other arithmetic  2.57 us (2%)
    pallas_call x6, Pallas kernels, project_query(): pl.pallas_call(functools.partial(query_kernel, count, pieces), grid_spec=...  52.1 us
    ppermute x9, waiting for transfers between devices, swap(): return lax.ppermute(x, 'fsdp', [(i, i ^ bit) for i in range(shards)])  25.7 us
    pallas_call x7, Pallas kernels, add_rows(): pl.pallas_call(functools.partial(add_kernel, len(gots), len(pair) // 2, l...  15.7 us
    pallas_call x2, Pallas kernels, score_heads(): pl.pallas_call(functools.partial(score_kernel, len(queries)), grid=(count...  14 us
    ppermute x9, starting transfers between devices, swap(): return lax.ppermute(x, 'fsdp', [(i, i ^ bit) for i in range(shards)])  10.2 us
    unnamed x34, local copies, waits for them, and re-layouts  8.16 us
    pallas_call x1, Pallas kernels, project_pair(): pl.pallas_call(functools.partial(pair_kernel, count), grid_spec=pltpu.Pre...  7.09 us
    ppermute x16, waiting for transfers between devices, other_core(): return lax.ppermute(x, 'rep', [(0, 1), (1, 0)])  6 us
  transfers between devices with their start and end apart: 26, of which 9 were waited for; matrix products, arithmetic and copies ran while one was open for 2% of the time, Pallas kernels for 60%

profile of v6, /device:TPU:0, one launch (start us, length us, event | category | flops | bytes accessed | tf_op | source)
XLA Modules:
  0.0 162.0 jit_solution(14988497098518348345)
XLA Ops:
  0.6 3.0 %collective-permute-start = (bf16[320,2048]{1,0:T(8,128)(2,1)}, bf16[320,2048]{1,0:T(8,128)(2,1)S(1)}, u32[]{:S(2)}, u32[]{:S(2)}) collective-permute-start(bf16[320,2048]{1,0:T(8,128)(2,1)} %refs_0_.7), channel_id=1, source_target_pairs={{0,2},{2,0},{1,3},{3,1},{4,6},{6,4},{5,7},{7,5},{8,10},{10,8},{9,1... | collective-permute-start | bytes 3932168 | tf_op jit(solution)/shard_map/ppermute | solution.py:441
  3.7 11.9 %query_products.6 = (f32[2,160,2048]{2,1,0:T(8,128)}, bf16[2,160,1024]{2,1,0:T(8,128)(2,1)}, bf16[2,160,1024]{2,1,0:T(8,128)(2,1)}) custom-call(s32[3]{0:T(128)S(1)} %pad_add_fusion.2.place_ref, bf16[320,2048]{1,0:T(8,128)(2,1)} %refs_0_.7, bf16[2048,8192]{1,0:T(8,128)(2,1)} %refs_1_.11), custom_call_target="tpu_custom_call" | custom-call | flops 1000 | bytes 1000 | tf_op jit(solution)/shard_map/query_products/pallas_call | solution.py:76
  16.1 1.8 %collective-permute-done.1.refs_1_ = bf16[2,160,1024]{2,1,0:T(8,128)(2,1)S(1)} collective-permute-done((bf16[2,160,1024]{2,1,0:T(8,128)(2,1)}, bf16[2,160,1024]{2,1,0:T(8,128)(2,1)S(1)}, u32[]{:S(2)}, u32[]{:S(2)}) %collective-permute-start.1) | collective-permute-done | bytes 655392 | tf_op jit(solution)/shard_map/ppermute | solution.py:414
  17.9 0.9 collective-permute-done.2.refs_2_
  18.9 2.7 %add_rows.7.refs_2_ = bf16[2,160,2048]{2,1,0:T(8,128)(2,1)} custom-call(f32[2,160,2048]{2,1,0:T(8,128)} %get-tuple-element.27.refs_0_, bf16[2,160,1024]{2,1,0:T(8,128)(2,1)S(1)} %collective-permute-done.1.refs_1_, bf16[2,160,1024]{2,1,0:T(8,128)(2,1)S(1)} %collective-permute-done.2.refs_2_), custom_call_target="tpu_custom_call" | custom-call | flops 1000 | bytes 1000 | tf_op jit(solution)/shard_map/add_rows/pallas_call | solution.py:176
  21.5 1.6 collective-permute-start.8
  23.3 7.5 %query_products.7 = (f32[1,160,2048]{2,1,0:T(8,128)}, bf16[1,160,1024]{2,1,0:T(8,128)(2,1)}, bf16[1,160,1024]{2,1,0:T(8,128)(2,1)}) custom-call(s32[2]{0:T(128)S(1)} %pad_add_fusion.1.place_ref, bf16[320,2048]{1,0:T(8,128)(2,1)} %refs_0_.7, bf16[2048,8192]{1,0:T(8,128)(2,1)} %refs_1_.11, bf16[2,160,2048]{2,1,0:T(8,128)(2,1)} %add_rows.7.refs_2_), custom_call_target="tpu_custom_call" | custom-call | flops 1000 | bytes 1000 | tf_op jit(solution)/shard_map/query_products/pallas_call | solution.py:76
  30.8 1.8 %collective-permute-done.refs_1_.refs_0_ = bf16[320,2048]{1,0:T(8,128)(2,1)S(1)} collective-permute-done((bf16[320,2048]{1,0:T(8,128)(2,1)}, bf16[320,2048]{1,0:T(8,128)(2,1)S(1)}, u32[]{:S(2)}, u32[]{:S(2)}) %collective-permute-start) | collective-permute-done | bytes 1310752 | tf_op jit(solution)/shard_map/ppermute | solution.py:441
  32.6 7.1 %key_value_products.1 = (f32[4,160,512]{2,1,0:T(8,128)}, bf16[4,160,512]{2,1,0:T(8,128)(2,1)}) custom-call(s32[5]{0:T(128)S(1)} %stack.25.place_ref, bf16[320,2048]{1,0:T(8,128)(2,1)} %refs_0_.7, bf16[320,2048]{1,0:T(8,128)(2,1)S(1)} %collective-permute-done.refs_1_.refs_0_, bf16[2048,512]{1,0:T(8,128)(2,1)} %refs_2_.1, bf16[2048,512]{1,0:T(8,128)(2,1)} %refs_3_.1, ...), custom_call_target="tpu_custom_call" | custom-call | flops 1000 | bytes 1000 | tf_op jit(solution)/shard_map/key_value_products/pallas_call | solution.py:121
  39.7 11.5 %query_products.8 = (f32[2,160,2048]{2,1,0:T(8,128)}, bf16[2,160,1024]{2,1,0:T(8,128)(2,1)}, bf16[2,160,1024]{2,1,0:T(8,128)(2,1)}) custom-call(s32[3]{0:T(128)S(1)} %pad_add_fusion.2.place_ref, bf16[320,2048]{1,0:T(8,128)(2,1)S(1)} %collective-permute-done.refs_1_.refs_0_, bf16[2048,8192]{1,0:T(8,128)(2,1)} %refs_1_.11, ...), custom_call_target="tpu_custom_call" | custom-call | flops 1000 | bytes 1000 | tf_op jit(solution)/shard_map/query_products/pallas_call | solution.py:76
  52.3 1.3 collective-permute-done.4.refs_1_
  53.6 1.9 %collective-permute-done.5.refs_2_.refs_1_ = bf16[2,160,1024]{2,1,0:T(8,128)(2,1)S(1)} collective-permute-done((bf16[2,160,1024]{2,1,0:T(8,128)(2,1)}, bf16[2,160,1024]{2,1,0:T(8,128)(2,1)S(1)}, u32[]{:S(2)}, u32[]{:S(2)}) %collective-permute-start.5) | collective-permute-done | bytes 655392 | tf_op jit(solution)/shard_map/ppermute | solution.py:414
  55.5 2.4 %add_rows.8.refs_4_.refs_2_ = bf16[1,160,2560]{2,1,0:T(8,128)(2,1)} custom-call(f32[2,160,2048]{2,1,0:T(8,128)} %get-tuple-element.33.refs_0_, bf16[2,160,1024]{2,1,0:T(8,128)(2,1)S(1)} %collective-permute-done.4.refs_1_, bf16[2,160,1024]{2,1,0:T(8,128)(2,1)S(1)} %collective-permute-done.5.refs_2_.refs_1_, ...), custom_call_target="tpu_custom_call" | custom-call | flops 1000 | bytes 1000 | tf_op jit(solution)/shard_map/add_rows/pallas_call | solution.py:176
  57.9 0.8 copy-done.2
  58.7 1.8 %collective-permute-start.11 = (bf16[1,160,2560]{2,1,0:T(8,128)(2,1)}, bf16[1,160,2560]{2,1,0:T(8,128)(2,1)S(1)}, u32[]{:S(2)}, u32[]{:S(2)}) collective-permute-start(bf16[1,160,2560]{2,1,0:T(8,128)(2,1)} %add_rows.8.refs_4_.refs_2_), channel_id=1, source_target_pairs={{0,4},{4,0},{8,12},{12,8},{1,5},{5,1},{9,13},{13,9},{2,6},{6,2},{1... | collective-permute-start | bytes 2457608 | tf_op jit(solution)/shard_map/ppermute | solution.py:411
  60.6 2.7 %add_rows.9.refs_3_ = bf16[1,160,2048]{2,1,0:T(8,128)(2,1)} custom-call(f32[1,160,2048]{2,1,0:T(8,128)} %get-tuple-element.36.refs_0_, bf16[1,160,1024]{2,1,0:T(8,128)(2,1)} %collective-permute-done.6.refs_1_, bf16[1,160,1024]{2,1,0:T(8,128)(2,1)} %collective-permute-done.7.refs_2_, bf16[2,160,2048]{2,1,0:T(8,128)(2,1)} %collective-permute-done.8.refs_3_.refs_1_, ...), custom_call_target="tpu_custom_call" | custom-call | flops 1000 | bytes 1000 | tf_op jit(solution)/shard_map/add_rows/pallas_call | solution.py:176
  63.3 2.6 %collective-permute-start.12 = (bf16[1,160,2048]{2,1,0:T(8,128)(2,1)}, bf16[1,160,2048]{2,1,0:T(8,128)(2,1)}, u32[]{:S(2)}, u32[]{:S(2)}) collective-permute-start(bf16[1,160,2048]{2,1,0:T(8,128)(2,1)} %add_rows.9.refs_3_), channel_id=1, source_target_pairs={{0,8},{4,12},{8,0},{12,4},{1,9},{5,13},{9,1},{13,5},{2,10},{6,14},... | collective-permute-start | bytes 1966088 | tf_op jit(solution)/shard_map/ppermute | solution.py:411
  65.9 1.1 copy-done.6
  67.0 7.3 %query_products.9 = (f32[1,160,2048]{2,1,0:T(8,128)}, bf16[1,160,2048]{2,1,0:T(8,128)(2,1)}) custom-call(s32[2]{0:T(128)S(1)} %pad_add_fusion.3.place_ref, bf16[320,2048]{1,0:T(8,128)(2,1)} %refs_0_.7, bf16[2048,8192]{1,0:T(8,128)(2,1)} %refs_1_.11, bf16[1,160,2560]{2,1,0:T(8,128)(2,1)} %add_rows.8.refs_4_.refs_2_, bf16[1,160,2048]{2,1,0:T(8,128)(2,1)S(1)} %copy-done.6), custom_call_target="tpu_custom_call" | custom-call | flops 99999997952 | bytes 100000000 | tf_op jit(solution)/shard_map/query_products/pallas_call | solution.py:76
  74.3 6.8 %query_products.10 = (f32[1,160,2048]{2,1,0:T(8,128)}, bf16[1,160,2048]{2,1,0:T(8,128)(2,1)}) custom-call(s32[2]{0:T(128)S(1)} %pad_add_fusion.3.place_ref, bf16[320,2048]{1,0:T(8,128)(2,1)S(1)} %collective-permute-done.refs_1_.refs_0_, bf16[2048,8192]{1,0:T(8,128)(2,1)} %refs_1_.11, bf16[1,160,2048]{2,1,0:T(8,128)(2,1)} %get-tuple-element.38.refs_2_), custom_call_target="tpu_custom_call" | custom-call | flops 1000 | bytes 1000 | tf_op jit(solution)/shard_map/query_products/pallas_call | solution.py:76
  81.1 7.1 %query_products.11 = (f32[1,160,2048]{2,1,0:T(8,128)}, bf16[1,160,1024]{2,1,0:T(8,128)(2,1)}, bf16[1,160,1024]{2,1,0:T(8,128)(2,1)}) custom-call(s32[2]{0:T(128)S(1)} %pad_add_fusion.1.place_ref, bf16[320,2048]{1,0:T(8,128)(2,1)S(1)} %collective-permute-done.refs_1_.refs_0_, bf16[2048,8192]{1,0:T(8,128)(2,1)} %refs_1_.11, ...), custom_call_target="tpu_custom_call" | custom-call | flops 1000 | bytes 1000 | tf_op jit(solution)/shard_map/query_products/pallas_call | solution.py:76
  89.2 1.1 copy-done.3
  90.3 2.0 %add_rows.10.refs_2_ = bf16[1,160,1536]{2,1,0:T(8,128)(2,1)} custom-call(f32[2,160,2048]{2,1,0:T(8,128)} %get-tuple-element.33.refs_0_, bf16[2,160,1024]{2,1,0:T(8,128)(2,1)S(1)} %copy-done.3, f32[4,160,512]{2,1,0:T(8,128)} %get-tuple-element.31.refs_3_.refs_2_.refs_0_, bf16[4,160,512]{2,1,0:T(8,128)(2,1)S(1)} %collective-permute-done.3.refs_4_.refs_3_.refs_1_, ...), custom_call_target="tpu_custom_call" | custom-call | flops 1000 | bytes 1000 | tf_op jit(solution)/shard_map/add_rows/pallas_call | solution.py:176
  92.7 1.9 %add_rows.11.refs_6_ = bf16[1,160,1024]{2,1,0:T(8,128)(2,1)} custom-call(f32[2,160,2048]{2,1,0:T(8,128)} %get-tuple-element.33.refs_0_, bf16[2,160,1024]{2,1,0:T(8,128)(2,1)S(1)} %collective-permute-done.5.refs_2_.refs_1_, bf16[1,160,1536]{2,1,0:T(8,128)(2,1)} %add_rows.10.refs_2_), custom_call_target="tpu_custom_call" | custom-call | flops 1000 | bytes 1000 | tf_op jit(solution)/shard_map/add_rows/pallas_call | solution.py:176
  94.6 0.7 copy-done.7
  95.9 1.0 copy-done.8
  96.9 2.1 %add_rows.12.refs_3_ = bf16[1,160,1536]{2,1,0:T(8,128)(2,1)} custom-call(f32[1,160,2048]{2,1,0:T(8,128)} %get-tuple-element.41.refs_0_, bf16[1,160,1024]{2,1,0:T(8,128)(2,1)S(1)} %copy-done.8, f32[4,160,512]{2,1,0:T(8,128)} %get-tuple-element.31.refs_3_.refs_2_.refs_0_, bf16[4,160,512]{2,1,0:T(8,128)(2,1)S(1)} %collective-permute-done.3.refs_4_.refs_3_.refs_1_, ...), custom_call_target="tpu_custom_call" | custom-call | flops 1000 | bytes 1000 | tf_op jit(solution)/shard_map/add_rows/pallas_call | solution.py:176
  98.9 0.6 collective-permute-start.13
  99.5 0.6 fusion.4
  100.4 1.9 %add_rows.13.refs_4_ = bf16[1,160,1024]{2,1,0:T(8,128)(2,1)} custom-call(f32[1,160,2048]{2,1,0:T(8,128)} %get-tuple-element.41.refs_0_, bf16[1,160,1024]{2,1,0:T(8,128)(2,1)S(1)} %collective-permute-done.14.refs_1_, bf16[1,160,2560]{2,1,0:T(8,128)(2,1)S(1)} %collective-permute-done.11.refs_4_.refs_5_.refs_2_, bf16[1,160,1536]{2,1,0:T(8,128)(2,1)} %add_rows.12.refs_3_), custom_call_target="tpu_custom_call" | custom-call | flops 1000 | bytes 1000 | tf_op jit(solution)/shard_map/add_rows/pallas_call | solution.py:176
  102.4 1.0 copy-done
  103.3 2.3 %sum_and_rotate.3.refs_0_ = bf16[160,2048]{1,0:T(8,128)(2,1)S(1)} custom-call(f32[160,128]{1,0:T(8,128)S(1)} %get-tuple-element.55.cos_ref, f32[160,128]{1,0:T(8,128)S(1)} %get-tuple-element.53.sin_ref, f32[1,160,2048]{2,1,0:T(8,128)} %get-tuple-element.46.refs_0_, bf16[2,160,2048]{2,1,0:T(8,128)(2,1)} %collective-permute-done.8.refs_3_.refs_1_, ...), custom_call_target="tpu_custom_call" | custom-call | flops 1000 | bytes 1000 | tf_op jit(solution)/shard_map/sum_and_rotate/pallas_call | solution.py:232
  106.2 3.1 %collective-permute-done.9.refs_2_.refs_1_ = bf16[1,160,1536]{2,1,0:T(8,128)(2,1)S(1)} collective-permute-done((bf16[1,160,1536]{2,1,0:T(8,128)(2,1)}, bf16[1,160,1536]{2,1,0:T(8,128)(2,1)S(1)}, u32[]{:S(2)}, u32[]{:S(2)}) %collective-permute-start.9) | collective-permute-done | bytes 491552 | tf_op jit(solution)/shard_map/ppermute | solution.py:411
  109.3 14.5 %collective-permute-done.13.refs_3_.refs_2_ = bf16[1,160,1536]{2,1,0:T(8,128)(2,1)S(1)} collective-permute-done((bf16[1,160,1536]{2,1,0:T(8,128)(2,1)}, bf16[1,160,1536]{2,1,0:T(8,128)(2,1)S(1)}, u32[]{:S(2)}, u32[]{:S(2)}) %collective-permute-start.13) | collective-permute-done | bytes 491552 | tf_op jit(solution)/shard_map/ppermute | solution.py:411
  123.8 1.1 split_and_rotate.1
  125.0 2.0 %collective-permute-start.17 = (bf16[1,160,1024]{2,1,0:T(8,128)(2,1)}, bf16[1,160,1024]{2,1,0:T(8,128)(2,1)}, u32[]{:S(2)}, u32[]{:S(2)}) collective-permute-start(bf16[1,160,1024]{2,1,0:T(8,128)(2,1)} %add_rows.11.refs_6_), channel_id=1, source_target_pairs={{0,4},{4,0},{8,12},{12,8},{1,5},{5,1},{9,13},{13,9},{2,6},{6,2},{1... | collective-permute-start | bytes 983048 | tf_op jit(solution)/shard_map/ppermute | solution.py:411
  127.1 1.1 collective-permute-start.18
  128.2 1.3 sum_and_rotate.4.refs_1_
  129.5 7.9 %collective-permute-done.23.refs_1_ = bf16[1,320,128]{2,1,0:T(8,128)(2,1)S(1)} collective-permute-done((bf16[1,320,128]{2,1,0:T(8,128)(2,1)S(1)}, bf16[1,320,128]{2,1,0:T(8,128)(2,1)S(1)}, u32[]{:S(2)}, u32[]{:S(2)}) %collective-permute-start.23) | collective-permute-done | bytes 81952 | tf_op jit(solution)/shard_map/ppermute | solution.py:411
  137.4 0.7 pad_maximum_fusion
  138.1 0.6 copy-done.11
  139.1 0.9 copy-done.10
  140.0 0.9 copy-done.12
  141.5 7.4 %score_heads.2 = (bf16[1,16,640,640]{3,2,1,0:T(8,128)(2,1)}, f32[8,128]{1,0:T(8,128)S(1)}) custom-call(bf16[640,640]{1,0:T(8,128)(2,1)S(1)} %get-tuple-element.44.order_ref, bf16[128,640]{1,0:T(8,128)(2,1)S(1)} %get-tuple-element.45.key_t_ref, bf16[160,2048]{1,0:T(8,128)(2,1)S(1)} %sum_and_rotate.3.refs_0_, bf16[160,1024]{1,0:T(8,128)(2,1)S(1)} %sum_and_rotate.4.refs_1_, ...), custom_call_target="tpu_custom_call" | custom-call | flops 1000 | bytes 1000 | tf_op jit(solution)/shard_map/score_heads/pallas_call | solution.py:372
  148.9 1.5 sum_and_rotate.5.refs_1_
  151.1 0.9 stack_slots.1.own_ref
  152.3 6.6 %score_heads.3 = (bf16[1,16,640,640]{3,2,1,0:T(8,128)(2,1)}, f32[8,128]{1,0:T(8,128)}) custom-call(bf16[640,640]{1,0:T(8,128)(2,1)S(1)} %get-tuple-element.44.order_ref, bf16[128,640]{1,0:T(8,128)(2,1)S(1)} %get-tuple-element.45.key_t_ref, bf16[160,2048]{1,0:T(8,128)(2,1)S(1)} %sum_and_rotate.3.refs_0_, ...), custom_call_target="tpu_custom_call", output_to_operand_aliasing={{0}: (6, {})} | custom-call | flops 1000 | bytes 1000 | tf_op jit(solution)/shard_map/score_heads/pallas_call | solution.py:372
  158.9 3.1 %order_values.1 = bf16[640,512]{1,0:T(8,128)(2,1)} custom-call(s32[4]{0:T(128)S(1)} %pad_add_fusion.4.place_ref, bf16[640,640]{1,0:T(8,128)(2,1)S(1)} %get-tuple-element.44.order_ref, bf16[4,320,128]{2,1,0:T(8,128)(2,1)S(1)} %stack_slots.1.own_ref, bf16[4,320,128]{2,1,0:T(8,128)(2,1)S(1)} %collective-permute-done.25.other_ref), custom_call_target="tpu_custom_call" | custom-call | tf_op jit(solution)/shard_map/order_values/pallas_call | solution.py:339
  (83 shorter events, 6.4 us)
Async XLA Ops:
  0.6 32.0 %collective-permute-start = (bf16[320,2048]{1,0:T(8,128)(2,1)}, bf16[320,2048]{1,0:T(8,128)(2,1)S(1)}, u32[]{:S(2)}, u32[]{:S(2)}) collective-permute-start(bf16[320,2048]{1,0:T(8,128)(2,1)} %refs_0_.7), channel_id=1, source_target_pairs={{0,2},{2,0},{1,3},{3,1},{4,6},{6,4},{5,7},{7,5},{8,10},{10,8},{9,1... | collective-permute-start | bytes 3932168 | tf_op jit(solution)/shard_map/ppermute | solution.py:441
  15.6 2.3 %collective-permute-start.1 = (bf16[2,160,1024]{2,1,0:T(8,128)(2,1)}, bf16[2,160,1024]{2,1,0:T(8,128)(2,1)S(1)}, u32[]{:S(2)}, u32[]{:S(2)}) collective-permute-start(bf16[2,160,1024]{2,1,0:T(8,128)(2,1)} %get-tuple-element.28), channel_id=1, source_target_pairs={{0,1},{1,0},{2,3},{3,2},{4,5},{5,4},{6,7},{7,6},{8,9},{9,8},{10,11... | collective-permute-start | bytes 1966088 | tf_op jit(solution)/shard_map/ppermute | solution.py:414
  15.6 3.2 %collective-permute-start.2 = (bf16[2,160,1024]{2,1,0:T(8,128)(2,1)}, bf16[2,160,1024]{2,1,0:T(8,128)(2,1)S(1)}, u32[]{:S(2)}, u32[]{:S(2)}) collective-permute-start(bf16[2,160,1024]{2,1,0:T(8,128)(2,1)} %get-tuple-element.29), channel_id=1, source_target_pairs={{0,1},{1,0},{2,3},{3,2},{4,5},{5,4},{6,7},{7,6},{8,9},{9,8},{10,11... | collective-permute-start | bytes 1966088 | tf_op jit(solution)/shard_map/ppermute | solution.py:414
  21.5 39.1 %collective-permute-start.8 = (bf16[2,160,2048]{2,1,0:T(8,128)(2,1)}, bf16[2,160,2048]{2,1,0:T(8,128)(2,1)}, u32[]{:S(2)}, u32[]{:S(2)}) collective-permute-start(bf16[2,160,2048]{2,1,0:T(8,128)(2,1)} %add_rows.7.refs_2_), channel_id=1, source_target_pairs={{0,4},{4,0},{8,12},{12,8},{1,5},{5,1},{9,13},{13,9},{2,6},{6,2},{1... | collective-permute-start | bytes 3932168 | tf_op jit(solution)/shard_map/ppermute | solution.py:411
  39.7 12.5 %collective-permute-start.3 = (bf16[4,160,512]{2,1,0:T(8,128)(2,1)}, bf16[4,160,512]{2,1,0:T(8,128)(2,1)S(1)}, u32[]{:S(2)}, u32[]{:S(2)}) collective-permute-start(bf16[4,160,512]{2,1,0:T(8,128)(2,1)} %get-tuple-element.32.refs_2_), channel_id=1, source_target_pairs={{0,1},{1,0},{2,3},{3,2},{4,5},{5,4},{6,7},{7,6},{8,9},{9,8},{10,11... | collective-permute-start | bytes 1966088 | tf_op jit(solution)/shard_map/ppermute | solution.py:414
  51.2 2.4 %collective-permute-start.4 = (bf16[2,160,1024]{2,1,0:T(8,128)(2,1)}, bf16[2,160,1024]{2,1,0:T(8,128)(2,1)S(1)}, u32[]{:S(2)}, u32[]{:S(2)}) collective-permute-start(bf16[2,160,1024]{2,1,0:T(8,128)(2,1)} %get-tuple-element.34), channel_id=1, source_target_pairs={{0,1},{1,0},{2,3},{3,2},{4,5},{5,4},{6,7},{7,6},{8,9},{9,8},{10,11... | collective-permute-start | bytes 1966088 | tf_op jit(solution)/shard_map/ppermute | solution.py:414
  51.7 3.8 %collective-permute-start.5 = (bf16[2,160,1024]{2,1,0:T(8,128)(2,1)}, bf16[2,160,1024]{2,1,0:T(8,128)(2,1)S(1)}, u32[]{:S(2)}, u32[]{:S(2)}) collective-permute-start(bf16[2,160,1024]{2,1,0:T(8,128)(2,1)} %get-tuple-element.35), channel_id=1, source_target_pairs={{0,1},{1,0},{2,3},{3,2},{4,5},{5,4},{6,7},{7,6},{8,9},{9,8},{10,11... | collective-permute-start | bytes 1966088 | tf_op jit(solution)/shard_map/ppermute | solution.py:414
  51.7 8.9 %collective-permute-start.6 = (bf16[1,160,1024]{2,1,0:T(8,128)(2,1)}, bf16[1,160,1024]{2,1,0:T(8,128)(2,1)}, u32[]{:S(2)}, u32[]{:S(2)}) collective-permute-start(bf16[1,160,1024]{2,1,0:T(8,128)(2,1)} %get-tuple-element.30.refs_4_), channel_id=1, source_target_pairs={{0,1},{1,0},{2,3},{3,2},{4,5},{5,4},{6,7},{7,6},{8,9},{9,8},{10,11... | collective-permute-start | bytes 983048 | tf_op jit(solution)/shard_map/ppermute | solution.py:414
  52.2 8.4 %collective-permute-start.7 = (bf16[1,160,1024]{2,1,0:T(8,128)(2,1)}, bf16[1,160,1024]{2,1,0:T(8,128)(2,1)}, u32[]{:S(2)}, u32[]{:S(2)}) collective-permute-start(bf16[1,160,1024]{2,1,0:T(8,128)(2,1)} %get-tuple-element.37), channel_id=1, source_target_pairs={{0,1},{1,0},{2,3},{3,2},{4,5},{5,4},{6,7},{7,6},{8,9},{9,8},{10,11... | collective-permute-start | bytes 983048 | tf_op jit(solution)/shard_map/ppermute | solution.py:414
  57.9 0.8 copy-start.2
  58.7 37.1 %collective-permute-start.11 = (bf16[1,160,2560]{2,1,0:T(8,128)(2,1)}, bf16[1,160,2560]{2,1,0:T(8,128)(2,1)S(1)}, u32[]{:S(2)}, u32[]{:S(2)}) collective-permute-start(bf16[1,160,2560]{2,1,0:T(8,128)(2,1)} %add_rows.8.refs_4_.refs_2_), channel_id=1, source_target_pairs={{0,4},{4,0},{8,12},{12,8},{1,5},{5,1},{9,13},{13,9},{2,6},{6,2},{1... | collective-permute-start | bytes 2457608 | tf_op jit(solution)/shard_map/ppermute | solution.py:411
  63.3 32.0 %collective-permute-start.12 = (bf16[1,160,2048]{2,1,0:T(8,128)(2,1)}, bf16[1,160,2048]{2,1,0:T(8,128)(2,1)}, u32[]{:S(2)}, u32[]{:S(2)}) collective-permute-start(bf16[1,160,2048]{2,1,0:T(8,128)(2,1)} %add_rows.9.refs_3_), channel_id=1, source_target_pairs={{0,8},{4,12},{8,0},{12,4},{1,9},{5,13},{9,1},{13,5},{2,10},{6,14},... | collective-permute-start | bytes 1966088 | tf_op jit(solution)/shard_map/ppermute | solution.py:411
  65.9 1.1 copy-start.6
  81.1 7.7 %copy-start.14 = (s32[640]{0:T(1024)S(1)}, s32[640]{0:T(1024)}, u32[]{:S(2)}) copy-start(s32[640]{0:T(1024)} %param.10) | copy-start | bytes 7684
  81.1 7.7 %copy-start.15 = (s32[640]{0:T(1024)S(1)}, s32[640]{0:T(1024)}, u32[]{:S(2)}) copy-start(s32[640]{0:T(1024)} %param.11) | copy-start | bytes 7684
  88.2 6.4 %collective-permute-start.10 = (bf16[1,160,1024]{2,1,0:T(8,128)(2,1)}, bf16[1,160,1024]{2,1,0:T(8,128)(2,1)S(1)}, u32[]{:S(2)}, u32[]{:S(2)}) collective-permute-start(bf16[1,160,1024]{2,1,0:T(8,128)(2,1)} %get-tuple-element.40.refs_4_), channel_id=1, source_target_pairs={{0,1},{1,0},{2,3},{3,2},{4,5},{5,4},{6,7},{7,6},{8,9},{9,8},{10,11... | collective-permute-start | bytes 983048 | tf_op jit(solution)/shard_map/ppermute | solution.py:414
  88.4 14.0 %collective-permute-start.16 = (bf16[1,160,2048]{2,1,0:T(8,128)(2,1)}, bf16[1,160,2048]{2,1,0:T(8,128)(2,1)S(1)}, u32[]{:S(2)}, u32[]{:S(2)}) collective-permute-start(bf16[1,160,2048]{2,1,0:T(8,128)(2,1)} %get-tuple-element.38.refs_2_), channel_id=1, source_target_pairs={{0,1},{1,0},{2,3},{3,2},{4,5},{5,4},{6,7},{7,6},{8,9},{9,8},{10,11... | collective-permute-start | bytes 1966088 | tf_op jit(solution)/shard_map/ppermute | solution.py:414
  89.2 1.1 copy-start.3
  92.3 3.1 %copy-start.13 = (bf16[1,160,2048]{2,1,0:T(8,128)(2,1)S(1)}, bf16[1,160,2048]{2,1,0:T(8,128)(2,1)}, u32[]{:S(2)}) copy-start(bf16[1,160,2048]{2,1,0:T(8,128)(2,1)} %get-tuple-element.39.refs_2_) | copy-start | bytes 1966084
  92.3 3.1 %copy-start.16 = (bf16[1,160,1024]{2,1,0:T(8,128)(2,1)S(1)}, bf16[1,160,1024]{2,1,0:T(8,128)(2,1)}, u32[]{:S(2)}) copy-start(bf16[1,160,1024]{2,1,0:T(8,128)(2,1)} %get-tuple-element.42) | copy-start | bytes 983044
  92.3 17.0 %collective-permute-start.9 = (bf16[1,160,1536]{2,1,0:T(8,128)(2,1)}, bf16[1,160,1536]{2,1,0:T(8,128)(2,1)S(1)}, u32[]{:S(2)}, u32[]{:S(2)}) collective-permute-start(bf16[1,160,1536]{2,1,0:T(8,128)(2,1)} %add_rows.10.refs_2_), channel_id=1, source_target_pairs={{0,4},{4,0},{8,12},{12,8},{1,5},{5,1},{9,13},{13,9},{2,6},{6,2},{1... | collective-permute-start | bytes 1474568 | tf_op jit(solution)/shard_map/ppermute | solution.py:411
  94.6 0.7 copy-start.7
  95.4 32.8 %collective-permute-start.19 = (bf16[1,160,2048]{2,1,0:T(8,128)(2,1)S(1)}, bf16[1,160,2048]{2,1,0:T(8,128)(2,1)S(1)}, u32[]{:S(2)}, u32[]{:S(2)}) collective-permute-start(bf16[1,160,2048]{2,1,0:T(8,128)(2,1)S(1)} %copy-done.13), channel_id=1, source_target_pairs={{0,1},{1,0},{2,3},{3,2},{4,5},{5,4},{6,7},{7,6},{8,9},{9,8},{10,11... | collective-permute-start | bytes 1966088 | tf_op jit(solution)/shard_map/ppermute | solution.py:414
  95.4 5.1 %collective-permute-start.14 = (bf16[1,160,1024]{2,1,0:T(8,128)(2,1)S(1)}, bf16[1,160,1024]{2,1,0:T(8,128)(2,1)S(1)}, u32[]{:S(2)}, u32[]{:S(2)}) collective-permute-start(bf16[1,160,1024]{2,1,0:T(8,128)(2,1)S(1)} %copy-done.16), channel_id=1, source_target_pairs={{0,1},{1,0},{2,3},{3,2},{4,5},{5,4},{6,7},{7,6},{8,9},{9,8},{10,11... | collective-permute-start | bytes 983048 | tf_op jit(solution)/shard_map/ppermute | solution.py:414
  95.9 1.0 copy-start.8
  98.9 24.9 %collective-permute-start.13 = (bf16[1,160,1536]{2,1,0:T(8,128)(2,1)}, bf16[1,160,1536]{2,1,0:T(8,128)(2,1)S(1)}, u32[]{:S(2)}, u32[]{:S(2)}) collective-permute-start(bf16[1,160,1536]{2,1,0:T(8,128)(2,1)} %add_rows.12.refs_3_), channel_id=1, source_target_pairs={{0,8},{4,12},{8,0},{12,4},{1,9},{5,13},{9,1},{13,5},{2,10},{6,14},... | collective-permute-start | bytes 1474568 | tf_op jit(solution)/shard_map/ppermute | solution.py:411
  100.4 27.8 %copy-start.4 = (f32[160,128]{1,0:T(8,128)}, f32[160,128]{1,0:T(8,128)S(1)}, u32[]{:S(2)}) copy-start(f32[160,128]{1,0:T(8,128)S(1)} %get-tuple-element.52.sin_ref) | copy-start | bytes 245764
  102.4 1.0 copy-start
  103.3 20.5 %copy-start.1 = (bf16[1,160,1024]{2,1,0:T(8,128)(2,1)S(1)}, bf16[1,160,1024]{2,1,0:T(8,128)(2,1)}, u32[]{:S(2)}) copy-start(bf16[1,160,1024]{2,1,0:T(8,128)(2,1)} %add_rows.13.refs_4_) | copy-start | bytes 983044
  105.6 35.9 %collective-permute-start.20 = (bf16[160,2048]{1,0:T(8,128)(2,1)S(1)}, bf16[160,2048]{1,0:T(8,128)(2,1)S(1)}, u32[]{:S(2)}, u32[]{:S(2)}) collective-permute-start(bf16[160,2048]{1,0:T(8,128)(2,1)S(1)} %sum_and_rotate.3.refs_0_), channel_id=1, source_target_pairs={{0,1},{1,0},{2,3},{3,2},{4,5},{5,4},{6,7},{7,6},{8,9},{9,8},{10,11... | collective-permute-start | bytes 1966088 | tf_op jit(solution)/shard_map/ppermute | solution.py:414
  125.0 4.6 %copy-start.9 = (bf16[320,128]{1,0:T(8,128)(2,1)}, bf16[320,128]{1,0:T(8,128)(2,1)S(1)}, u32[]{:S(2)}) copy-start(bf16[320,128]{1,0:T(8,128)(2,1)S(1)} %get-tuple-element.43.own_ref) | copy-start | bytes 245764
  125.0 12.5 %collective-permute-start.23 = (bf16[1,320,128]{2,1,0:T(8,128)(2,1)S(1)}, bf16[1,320,128]{2,1,0:T(8,128)(2,1)S(1)}, u32[]{:S(2)}, u32[]{:S(2)}) collective-permute-start(bf16[1,320,128]{2,1,0:T(8,128)(2,1)S(1)} %get-tuple-element.51.refs_0_), channel_id=1, source_target_pairs={{0,4},{4,0},{8,12},{12,8},{1,5},{5,1},{9,13},{13,9},{2,6},{6,2},{1... | collective-permute-start | bytes 245768 | tf_op jit(solution)/shard_map/ppermute | solution.py:411
  125.0 23.9 %collective-permute-start.17 = (bf16[1,160,1024]{2,1,0:T(8,128)(2,1)}, bf16[1,160,1024]{2,1,0:T(8,128)(2,1)}, u32[]{:S(2)}, u32[]{:S(2)}) collective-permute-start(bf16[1,160,1024]{2,1,0:T(8,128)(2,1)} %add_rows.11.refs_6_), channel_id=1, source_target_pairs={{0,4},{4,0},{8,12},{12,8},{1,5},{5,1},{9,13},{13,9},{2,6},{6,2},{1... | collective-permute-start | bytes 983048 | tf_op jit(solution)/shard_map/ppermute | solution.py:411
  127.1 21.9 %collective-permute-start.18 = (bf16[1,160,1024]{2,1,0:T(8,128)(2,1)S(1)}, bf16[1,160,1024]{2,1,0:T(8,128)(2,1)}, u32[]{:S(2)}, u32[]{:S(2)}) collective-permute-start(bf16[1,160,1024]{2,1,0:T(8,128)(2,1)S(1)} %copy-done.1), channel_id=1, source_target_pairs={{0,8},{4,12},{8,0},{12,4},{1,9},{5,13},{9,1},{13,5},{2,10},{6,14},... | collective-permute-start | bytes 983048 | tf_op jit(solution)/shard_map/ppermute | solution.py:411
  128.2 10.0 %collective-permute-start.15 = (bf16[320,128]{1,0:T(8,128)(2,1)S(1)}, bf16[320,128]{1,0:T(8,128)(2,1)S(1)}, u32[]{:S(2)}, u32[]{:S(2)}) collective-permute-start(bf16[320,128]{1,0:T(8,128)(2,1)S(1)} %get-tuple-element.43.own_ref), channel_id=1, source_target_pairs={{0,1},{1,0},{2,3},{3,2},{4,5},{5,4},{6,7},{7,6},{8,9},{9,8},{10,11... | collective-permute-start | bytes 245768 | tf_op jit(solution)/shard_map/ppermute | solution.py:414
  137.4 4.1 %collective-permute-start.21 = (bf16[160,1024]{1,0:T(8,128)(2,1)S(1)}, bf16[160,1024]{1,0:T(8,128)(2,1)}, u32[]{:S(2)}, u32[]{:S(2)}) collective-permute-start(bf16[160,1024]{1,0:T(8,128)(2,1)S(1)} %sum_and_rotate.4.refs_1_), channel_id=1, source_target_pairs={{0,1},{1,0},{2,3},{3,2},{4,5},{5,4},{6,7},{7,6},{8,9},{9,8},{10,11... | collective-permute-start | bytes 983048 | tf_op jit(solution)/shard_map/ppermute | solution.py:414
  138.1 0.6 copy-start.11
  138.8 12.4 %collective-permute-start.24 = (bf16[2,320,128]{2,1,0:T(8,128)(2,1)}, bf16[2,320,128]{2,1,0:T(8,128)(2,1)}, u32[]{:S(2)}, u32[]{:S(2)}) collective-permute-start(bf16[2,320,128]{2,1,0:T(8,128)(2,1)} %pad_maximum_fusion), channel_id=1, source_target_pairs={{0,8},{4,12},{8,0},{12,4},{1,9},{5,13},{9,1},{13,5},{2,10},{6,14},... | collective-permute-start | bytes 491528 | tf_op jit(solution)/shard_map/ppermute | solution.py:411
  139.1 0.9 copy-start.10
  140.0 0.9 copy-start.12
  141.5 7.4 %copy-start.5 = (f32[160,128]{1,0:T(8,128)S(1)}, f32[160,128]{1,0:T(8,128)}, u32[]{:S(2)}) copy-start(f32[160,128]{1,0:T(8,128)} %copy-done.4) | copy-start | bytes 245764
  150.5 1.8 %collective-permute-start.22 = (bf16[160,1024]{1,0:T(8,128)(2,1)S(1)}, bf16[160,1024]{1,0:T(8,128)(2,1)S(1)}, u32[]{:S(2)}, u32[]{:S(2)}) collective-permute-start(bf16[160,1024]{1,0:T(8,128)(2,1)S(1)} %sum_and_rotate.5.refs_1_), channel_id=1, source_target_pairs={{0,1},{1,0},{2,3},{3,2},{4,5},{5,4},{6,7},{7,6},{8,9},{9,8},{10,11... | collective-permute-start | bytes 983048 | tf_op jit(solution)/shard_map/ppermute | solution.py:414
  152.1 6.9 %collective-permute-start.25 = (bf16[4,320,128]{2,1,0:T(8,128)(2,1)S(1)}, bf16[4,320,128]{2,1,0:T(8,128)(2,1)S(1)}, u32[]{:S(2)}, u32[]{:S(2)}) collective-permute-start(bf16[4,320,128]{2,1,0:T(8,128)(2,1)S(1)} %stack_slots.1.own_ref), channel_id=1, source_target_pairs={{0,1},{1,0},{2,3},{3,2},{4,5},{5,4},{6,7},{7,6},{8,9},{9,8},{10,11... | collective-permute-start | bytes 983048 | tf_op jit(solution)/shard_map/ppermute | solution.py:414

commit v7 on v6

--- a/solution.py
+++ b/solution.py
@@ -42,7 +42,7 @@
         rows_ref[given : given + half] = x_ref[pl.ds(pl.multiple_of((1 - core) * half, 16), half)]
 
 
-def query_kernel(count, pieces, place_ref, *refs):
+def query_kernel(count, pieces, by_slot, place_ref, *refs):
     x_refs, w_ref = refs[:count], refs[count]
     keep_ref, *give_refs, rows_ref = refs[-2 - pieces :]
     tile = pl.program_id(1)
@@ -58,34 +58,45 @@
     keep_ref[0] = result[:half]
     for j, give_ref in enumerate(give_refs):
 
-        @pl.when((tile == j // each) | (pieces == 1))
+        @pl.when(pl.program_id(0) == j if by_slot else (tile == j // each) | (pieces == 1))
         def _():
             start = j % each * size
             give_ref[0] = result[half:, start : start + size].astype(give_ref.dtype)
 
 
-def project_query(rindex, findex, slots, blocks, w, cols, tile, width, after, cost):
+def project_query(rindex, findex, slots, blocks, w, cols, tile, width, after, cost, by_slot):
     rows, depth = blocks[0].shape
     count = len(blocks)
     half = rows // 2 * count
-    tiles, pieces = cols // tile, cols // width
+    tiles, pieces = cols // tile, len(slots) if by_slot else cols // width
     place = jnp.stack([rindex] + [findex ^ slot for slot in slots]).astype(jnp.int32)
     keep_spec = pl.BlockSpec((1, half, tile), lambda s, j, place: (s, 0, j))
     give_spec = pl.BlockSpec((1, half, width), lambda s, j, place: (s, 0, 0))
+
+    def slot_spec(k):
+        def index(s, j, place):
+            return (0, 0, jnp.where(s < k, 0, jnp.where(s > k, tiles - 1, j)))
+
+        return pl.BlockSpec((1, half, tile), index)
+
+    give_specs = [keep_spec] if pieces == 1 else [give_spec] * pieces
+    given = (len(slots), half, width)
+    if by_slot:
+        give_specs, given = [slot_spec(k) for k in range(pieces)], (1, half, cols)
     x_spec = pl.BlockSpec((rows, depth), lambda s, j, place: (0, 0), pipeline_mode=pl.Buffered(1))
     outs = pl.pallas_call(
-        functools.partial(query_kernel, count, pieces),
+        functools.partial(query_kernel, count, pieces, by_slot),
         grid_spec=pltpu.PrefetchScalarGridSpec(
             num_scalar_prefetch=1,
             grid=(len(slots), tiles),
             in_specs=[x_spec] * count
             + [pl.BlockSpec((depth, tile), lambda s, j, place: (0, place[1 + s] * tiles + j))]
             + [pl.BlockSpec(memory_space=pl.ANY)] * len(after),
-            out_specs=[keep_spec] + ([keep_spec] if pieces == 1 else [give_spec] * pieces),
+            out_specs=[keep_spec] + give_specs,
             scratch_shapes=[pltpu.VMEM((2 * half, depth), w.dtype)],
         ),
         out_shape=[pltpu.HBM((len(slots), half, cols), jnp.float32)]
-        + [pltpu.HBM((len(slots), half, width), jnp.bfloat16)] * pieces,
+        + [pltpu.HBM(given, jnp.bfloat16)] * pieces,
         compiler_params=pltpu.CompilerParams(vmem_limit_bytes=VMEM_BYTES),
         cost_estimate=cost,
         name="query_products",
@@ -452,18 +463,19 @@
 
     tile = min(1024, head_cols)
 
-    def project(slots, blocks, width, after=(), cost=LIGHT):
+    def project(slots, blocks, width, after=(), cost=LIGHT, by_slot=False):
         keep, gives = project_query(
-            rindex, findex, slots, blocks, w_query, head_cols, tile, width, after, cost
+            rindex, findex, slots, blocks, w_query, head_cols, tile, width, after, cost, by_slot
         )
         return keep, [other_core(give) for give in gives], gives[0]
 
     def rotate(b, p, split, terms, behind):
         cols = head_cols // split
         table = slice(b * half, (b + 1) * half)
-        keep, got = owns[b]
-        added = [(keep, 0, 0, p * cols)] + terms
-        turned = sum_and_rotate(cosine[table], sine[table], added, (0, 0, p, got), cols, behind)
+        keep, slot, got = owns[b]
+        added = [(keep, slot, 0, p * cols)] + terms
+        gots = (0, 0, p, got) if len(got) == 1 else (0, 0, 0, got[p : p + 1])
+        turned = sum_and_rotate(cosine[table], sine[table], added, gots, cols, behind)
         return turned, other_core(turned)
 
     def add_even(b, start, cols, pair, behind):
@@ -496,14 +508,13 @@
             added, after = add_even(b - 1, 0, head_cols, (), after)
             terms.append([(fars[b - 1], len(odd) - 1, 0, 0)] + added)
             after = (odd_sent,) + after
-        if b == last:
-            for c, near in enumerate(placed):
-                cost = LIGHT if c else HEAVY
-                own_keep, own_got, given = project([0], [near], head_cols, after, cost)
-                owns.append((own_keep, own_got))
-                after = (given,)
-        even_keep, even_got, given = project(even, [block], tile, after)
-        evens.append((even_keep, even_got))
+        if b < last:
+            keep, got, given = project(even + [0], [block], head_cols, after, LIGHT, True)
+            evens.append((keep, got[:1] if len(even) == 1 else [jnp.concatenate(got[:-1])]))
+            owns.append((keep, len(even), got[-1:]))
+        else:
+            keep, got, given = project(even, [block], tile, after, HEAVY)
+            evens.append((keep, got))
         after = (given,)
     parts, behind = [], tuple(term[0] for row in terms for term in row[1:])
     for p in range(split):
@@ -517,16 +528,14 @@
     for p in range(split):
         added, after = add_even(last, p * tile, tile, pair if p == 0 else (), after)
         parts[p] += added
+    keep, got, _ = project([0], placed[last:], tile, after, HEAVY)
+    owns.append((keep, 0, got))
 
     if fast_pair:
         width = 2 * DH * tps
         pieces = [(array, shards - 1, 0) for array in pair]
         pieces += [(term, 0, tile) for term, _, _, _ in parts[0]]
         key_rot, held = split_and_rotate(cosine, sine, pieces, width, after)
-        held = [held]
-        while 2 ** len(held) <= shards:
-            known = held[0] if len(held) == 1 else jnp.concatenate(held)
-            held.append(swap(known, 2 ** (len(held) - 1)))
     else:
         x = jnp.concatenate(blocks, axis=0)
         key_sum, value_sum = lax.psum(
@@ -562,7 +571,10 @@
         )
         mark = (mark,)
         if fast_pair and p == 0:
-            held = stack_slots(held, mark)
+            bit = 1
+            while bit < shards:
+                held = stack_slots([held, swap(held, bit)], mark)
+                bit *= 2
             values = order_values(findex, order, held, other_core(held))
     return (scores[0], values)
 

time: 163 us -> 164 us (level)
  local copies, waits for them, and re-layouts: 8.55 us -> 3.42 us
  waiting for transfers between devices: 33.5 us -> 38.5 us
  starting transfers between devices: 16.8 us -> 20.6 us
  Pallas kernels: 99.8 us -> 96.8 us
    ppermute x9, waiting for transfers between devices: 25.7 us -> 34.2 us  [swap(): return lax.ppermute(x, 'fsdp', [(i, i ^ bit) for i in range(shards)])]
    unnamed x34 -> x24, local copies, waits for them, and re-layouts: 8.16 us -> 3.02 us
    ppermute x9, starting transfers between devices: 10.2 us -> 14 us  [swap(): return lax.ppermute(x, 'fsdp', [(i, i ^ bit) for i in range(shards)])]
    pallas_call x6 -> x5, Pallas kernels: 52.1 us -> 49.3 us  [project_query(): pl.pallas_call(functools.partial(query_kernel, count, pieces, by_slot), g...]
    ppermute x1, waiting for transfers between devices: 1.81 us -> 0.01 us  [body(): lax.ppermute(hidden, 'tp', [(i, (i - b) % tps) for i in range(tps)])]
    ppermute x16, waiting for transfers between devices: 6 us -> 4.22 us  [other_core(): return lax.ppermute(x, 'rep', [(0, 1), (1, 0)])]
  transfers between devices with their start and end apart: 26 -> 26, of which waited for: 9 -> 10; matrix products, arithmetic and copies ran while one was open for 2% -> 2% of each run, Pallas kernels for 60% -> 58%
where the time goes in v7:
time: 164 us; the launch traced here: 163 us
  Pallas kernels  96.8 us (59%)
  waiting for transfers between devices  38.5 us (23%)
  starting transfers between devices  20.6 us (13%)
  local copies, waits for them, and re-layouts  3.42 us (2%)
  other arithmetic  2.51 us (2%)
    pallas_call x5, Pallas kernels, project_query(): pl.pallas_call(functools.partial(query_kernel, count, pieces, by_slot), g...  49.3 us
    ppermute x9, waiting for transfers between devices, swap(): return lax.ppermute(x, 'fsdp', [(i, i ^ bit) for i in range(shards)])  34.2 us
    pallas_call x7, Pallas kernels, add_rows(): pl.pallas_call(functools.partial(add_kernel, len(gots), len(pair) // 2, l...  15.8 us
    pallas_call x2, Pallas kernels, score_heads(): pl.pallas_call(functools.partial(score_kernel, len(queries)), grid=(count...  14.9 us
    ppermute x9, starting transfers between devices, swap(): return lax.ppermute(x, 'fsdp', [(i, i ^ bit) for i in range(shards)])  14 us
    pallas_call x1, Pallas kernels, project_pair(): pl.pallas_call(functools.partial(pair_kernel, count), grid_spec=pltpu.Pre...  7.11 us
    pallas_call x3, Pallas kernels, sum_and_rotate(): pl.pallas_call(functools.partial(rotate_kernel, len(terms), len(gots)), g...  4.95 us
    ppermute x16, waiting for transfers between devices, other_core(): return lax.ppermute(x, 'rep', [(0, 1), (1, 0)])  4.22 us
  transfers between devices with their start and end apart: 26, of which 10 were waited for; matrix products, arithmetic and copies ran while one was open for 2% of the time, Pallas kernels for 58%

profile of v7, /device:TPU:0, one launch (start us, length us, event | category | flops | bytes accessed | tf_op | source)
XLA Modules:
  0.0 162.6 jit_solution(136972953961939193)
XLA Ops:
  0.6 3.0 %collective-permute-start = (bf16[320,2048]{1,0:T(8,128)(2,1)}, bf16[320,2048]{1,0:T(8,128)(2,1)S(1)}, u32[]{:S(2)}, u32[]{:S(2)}) collective-permute-start(bf16[320,2048]{1,0:T(8,128)(2,1)} %refs_0_.5), channel_id=1, source_target_pairs={{0,2},{2,0},{1,3},{3,1},{4,6},{6,4},{5,7},{7,5},{8,10},{10,8},{9,1... | collective-permute-start | bytes 3932168 | tf_op jit(solution)/shard_map/ppermute | solution.py:452
  3.7 11.9 %query_products.5 = (f32[2,160,2048]{2,1,0:T(8,128)}, bf16[2,160,1024]{2,1,0:T(8,128)(2,1)}, bf16[2,160,1024]{2,1,0:T(8,128)(2,1)}) custom-call(s32[3]{0:T(128)S(1)} %pad_add_fusion.2.place_ref, bf16[320,2048]{1,0:T(8,128)(2,1)} %refs_0_.5, bf16[2048,8192]{1,0:T(8,128)(2,1)} %refs_1_.9), custom_call_target="tpu_custom_call" | custom-call | flops 1000 | bytes 1000 | tf_op jit(solution)/shard_map/query_products/pallas_call | solution.py:87
  15.6 0.5 collective-permute-start.2
  16.1 1.8 %collective-permute-done.1.refs_1_ = bf16[2,160,1024]{2,1,0:T(8,128)(2,1)S(1)} collective-permute-done((bf16[2,160,1024]{2,1,0:T(8,128)(2,1)}, bf16[2,160,1024]{2,1,0:T(8,128)(2,1)S(1)}, u32[]{:S(2)}, u32[]{:S(2)}) %collective-permute-start.1) | collective-permute-done | bytes 655392 | tf_op jit(solution)/shard_map/ppermute | solution.py:425
  17.9 0.9 collective-permute-done.2.refs_2_
  18.8 2.7 %add_rows.7.refs_2_ = bf16[2,160,2048]{2,1,0:T(8,128)(2,1)} custom-call(f32[2,160,2048]{2,1,0:T(8,128)} %get-tuple-element.26.refs_0_, bf16[2,160,1024]{2,1,0:T(8,128)(2,1)S(1)} %collective-permute-done.1.refs_1_, bf16[2,160,1024]{2,1,0:T(8,128)(2,1)S(1)} %collective-permute-done.2.refs_2_), custom_call_target="tpu_custom_call" | custom-call | flops 1000 | bytes 1000 | tf_op jit(solution)/shard_map/add_rows/pallas_call | solution.py:187
  21.5 1.6 collective-permute-start.7
  23.2 0.5 broadcast_add_fusion
  23.8 11.8 %query_products.6 = (f32[2,160,2048]{2,1,0:T(8,128)}, bf16[1,160,2048]{2,1,0:T(8,128)(2,1)}, bf16[1,160,2048]{2,1,0:T(8,128)(2,1)}) custom-call(s32[3]{0:T(128)S(1)} %pad_add_fusion.1.place_ref, bf16[320,2048]{1,0:T(8,128)(2,1)} %refs_0_.5, bf16[2048,8192]{1,0:T(8,128)(2,1)} %refs_1_.9, bf16[2,160,2048]{2,1,0:T(8,128)(2,1)} %add_rows.7.refs_2_), custom_call_target="tpu_custom_call" | custom-call | flops 1000 | bytes 1000 | tf_op jit(solution)/shard_map/query_products/pallas_call | solution.py:87
  35.6 7.1 %key_value_products.1 = (f32[4,160,512]{2,1,0:T(8,128)}, bf16[4,160,512]{2,1,0:T(8,128)(2,1)}) custom-call(s32[5]{0:T(128)S(1)} %stack.27.place_ref, bf16[320,2048]{1,0:T(8,128)(2,1)} %refs_0_.5, bf16[320,2048]{1,0:T(8,128)(2,1)S(1)} %collective-permute-done.refs_1_.refs_0_, bf16[2048,512]{1,0:T(8,128)(2,1)} %refs_2_.1, bf16[2048,512]{1,0:T(8,128)(2,1)} %refs_3_.1, ...), custom_call_target="tpu_custom_call" | custom-call | flops 1000 | bytes 1000 | tf_op jit(solution)/shard_map/key_value_products/pallas_call | solution.py:132
  42.8 0.6 collective-permute-start.3
  43.3 11.5 %query_products.7 = (f32[2,160,2048]{2,1,0:T(8,128)}, bf16[2,160,1024]{2,1,0:T(8,128)(2,1)}, bf16[2,160,1024]{2,1,0:T(8,128)(2,1)}) custom-call(s32[3]{0:T(128)S(1)} %pad_add_fusion.2.place_ref, bf16[320,2048]{1,0:T(8,128)(2,1)S(1)} %collective-permute-done.refs_1_.refs_0_, bf16[2048,8192]{1,0:T(8,128)(2,1)} %refs_1_.9, ...), custom_call_target="tpu_custom_call" | custom-call | flops 1000 | bytes 1000 | tf_op jit(solution)/shard_map/query_products/pallas_call | solution.py:87
  55.9 0.7 fusion.4
  56.6 0.5 collective-permute-done.4.refs_1_
  57.1 0.9 collective-permute-done.5.refs_2_.refs_1_
  58.1 2.4 %add_rows.8.refs_3_.refs_2_ = bf16[1,160,2560]{2,1,0:T(8,128)(2,1)} custom-call(f32[2,160,2048]{2,1,0:T(8,128)} %get-tuple-element.32.refs_0_, bf16[2,160,1024]{2,1,0:T(8,128)(2,1)S(1)} %collective-permute-done.4.refs_1_, bf16[2,160,1024]{2,1,0:T(8,128)(2,1)S(1)} %collective-permute-done.5.refs_2_.refs_1_, ...), custom_call_target="tpu_custom_call" | custom-call | flops 1000 | bytes 1000 | tf_op jit(solution)/shard_map/add_rows/pallas_call | solution.py:187
  60.9 2.7 %add_rows.9.refs_3_ = bf16[1,160,2048]{2,1,0:T(8,128)(2,1)} custom-call(f32[2,160,2048]{2,1,0:T(8,128)} %get-tuple-element.35.refs_0_, bf16[1,160,2048]{2,1,0:T(8,128)(2,1)} %collective-permute-done.6.refs_1_, bf16[2,160,2048]{2,1,0:T(8,128)(2,1)} %collective-permute-done.7.refs_2_.refs_1_, bf16[1,160,2560]{2,1,0:T(8,128)(2,1)} %add_rows.8.refs_3_.refs_2_), custom_call_target="tpu_custom_call" | custom-call | flops 1000 | bytes 1000 | tf_op jit(solution)/shard_map/add_rows/pallas_call | solution.py:187
  63.6 2.6 %collective-permute-start.11 = (bf16[1,160,2048]{2,1,0:T(8,128)(2,1)}, bf16[1,160,2048]{2,1,0:T(8,128)(2,1)S(1)}, u32[]{:S(2)}, u32[]{:S(2)}) collective-permute-start(bf16[1,160,2048]{2,1,0:T(8,128)(2,1)} %add_rows.9.refs_3_), channel_id=1, source_target_pairs={{0,8},{4,12},{8,0},{12,4},{1,9},{5,13},{9,1},{13,5},{2,10},{6,14},... | collective-permute-start | bytes 1966088 | tf_op jit(solution)/shard_map/ppermute | solution.py:422
  66.2 1.1 copy-done.2
  67.4 7.0 %query_products.8 = (f32[1,160,2048]{2,1,0:T(8,128)}, bf16[1,160,1024]{2,1,0:T(8,128)(2,1)}, bf16[1,160,1024]{2,1,0:T(8,128)(2,1)}) custom-call(s32[2]{0:T(128)S(1)} %pad_add_fusion.3.place_ref, bf16[320,2048]{1,0:T(8,128)(2,1)S(1)} %collective-permute-done.refs_1_.refs_0_, bf16[2048,8192]{1,0:T(8,128)(2,1)} %refs_1_.9, ...), custom_call_target="tpu_custom_call" | custom-call | flops 99999997952 | bytes 100000000 | tf_op jit(solution)/shard_map/query_products/pallas_call | solution.py:87
  74.4 0.5 collective-permute-start.13
  75.1 2.1 %add_rows.10.refs_2_ = bf16[1,160,1536]{2,1,0:T(8,128)(2,1)} custom-call(f32[2,160,2048]{2,1,0:T(8,128)} %get-tuple-element.32.refs_0_, bf16[2,160,1024]{2,1,0:T(8,128)(2,1)S(1)} %collective-permute-done.4.refs_1_, f32[4,160,512]{2,1,0:T(8,128)} %get-tuple-element.30.refs_3_.refs_2_.refs_0_, ...), custom_call_target="tpu_custom_call" | custom-call | flops 1000 | bytes 1000 | tf_op jit(solution)/shard_map/add_rows/pallas_call | solution.py:187
  77.3 1.9 %add_rows.11.refs_6_ = bf16[1,160,1024]{2,1,0:T(8,128)(2,1)} custom-call(f32[2,160,2048]{2,1,0:T(8,128)} %get-tuple-element.32.refs_0_, bf16[2,160,1024]{2,1,0:T(8,128)(2,1)S(1)} %collective-permute-done.5.refs_2_.refs_1_, bf16[1,160,1536]{2,1,0:T(8,128)(2,1)} %add_rows.10.refs_2_), custom_call_target="tpu_custom_call" | custom-call | flops 1000 | bytes 1000 | tf_op jit(solution)/shard_map/add_rows/pallas_call | solution.py:187
  79.2 1.6 collective-permute-start.8
  80.8 13.1 %collective-permute-done.11.refs_7_.refs_2_ = bf16[1,160,2048]{2,1,0:T(8,128)(2,1)S(1)} collective-permute-done((bf16[1,160,2048]{2,1,0:T(8,128)(2,1)}, bf16[1,160,2048]{2,1,0:T(8,128)(2,1)S(1)}, u32[]{:S(2)}, u32[]{:S(2)}) %collective-permute-start.11) | collective-permute-done | bytes 655392 | tf_op jit(solution)/shard_map/ppermute | solution.py:422
  93.9 1.9 %collective-permute-done.10.refs_4_.refs_5_.refs_2_ = bf16[1,160,2560]{2,1,0:T(8,128)(2,1)S(1)} collective-permute-done((bf16[1,160,2560]{2,1,0:T(8,128)(2,1)}, bf16[1,160,2560]{2,1,0:T(8,128)(2,1)S(1)}, u32[]{:S(2)}, u32[]{:S(2)}) %collective-permute-start.10) | collective-permute-done | bytes 819232 | tf_op jit(solution)/shard_map/ppermute | solution.py:422
  95.8 2.1 %add_rows.12.refs_3_ = bf16[1,160,1536]{2,1,0:T(8,128)(2,1)} custom-call(f32[1,160,2048]{2,1,0:T(8,128)} %get-tuple-element.37.refs_0_, bf16[1,160,1024]{2,1,0:T(8,128)(2,1)S(1)} %collective-permute-done.9.refs_1_, f32[4,160,512]{2,1,0:T(8,128)} %get-tuple-element.30.refs_3_.refs_2_.refs_0_, ...), custom_call_target="tpu_custom_call" | custom-call | flops 1000 | bytes 1000 | tf_op jit(solution)/shard_map/add_rows/pallas_call | solution.py:187
  97.9 1.4 collective-permute-start.12
  99.3 1.9 %add_rows.13.refs_4_.refs_2_ = bf16[1,160,1024]{2,1,0:T(8,128)(2,1)} custom-call(f32[1,160,2048]{2,1,0:T(8,128)} %get-tuple-element.37.refs_0_, bf16[1,160,1024]{2,1,0:T(8,128)(2,1)S(1)} %collective-permute-done.13.refs_1_, bf16[1,160,2560]{2,1,0:T(8,128)(2,1)S(1)} %collective-permute-done.10.refs_4_.refs_5_.refs_2_, bf16[1,160,1536]{2,1,0:T(8,128)(2,1)} %add_rows.12.refs_3_), custom_call_target="tpu_custom_call" | custom-call | flops 1000 | bytes 1000 | tf_op jit(solution)/shard_map/add_rows/pallas_call | solution.py:187
  101.2 1.0 copy-done
  102.2 2.0 %sum_and_rotate.3.refs_0_ = bf16[160,2048]{1,0:T(8,128)(2,1)S(1)} custom-call(f32[160,128]{1,0:T(8,128)S(1)} %get-tuple-element.53.cos_ref, f32[160,128]{1,0:T(8,128)S(1)} %get-tuple-element.51.sin_ref, f32[2,160,2048]{2,1,0:T(8,128)} %get-tuple-element.35.refs_0_, bf16[2,160,2048]{2,1,0:T(8,128)(2,1)} %collective-permute-done.7.refs_2_.refs_1_, ...), custom_call_target="tpu_custom_call" | custom-call | flops 1000 | bytes 1000 | tf_op jit(solution)/shard_map/sum_and_rotate/pallas_call | solution.py:243
  104.3 7.0 %query_products.9 = (f32[1,160,2048]{2,1,0:T(8,128)}, bf16[1,160,1024]{2,1,0:T(8,128)(2,1)}, bf16[1,160,1024]{2,1,0:T(8,128)(2,1)}) custom-call(s32[2]{0:T(128)S(1)} %pad_add_fusion.4.place_ref, bf16[320,2048]{1,0:T(8,128)(2,1)S(1)} %collective-permute-done.refs_1_.refs_0_, bf16[2048,8192]{1,0:T(8,128)(2,1)} %refs_1_.9, ...), custom_call_target="tpu_custom_call" | custom-call | flops 99999997952 | bytes 100000000 | tf_op jit(solution)/shard_map/query_products/pallas_call | solution.py:87
  112.1 1.0 collective-permute-done.8.refs_2_.refs_1_
  113.0 8.2 %collective-permute-done.12.refs_3_.refs_2_ = bf16[1,160,1536]{2,1,0:T(8,128)(2,1)S(1)} collective-permute-done((bf16[1,160,1536]{2,1,0:T(8,128)(2,1)}, bf16[1,160,1536]{2,1,0:T(8,128)(2,1)S(1)}, u32[]{:S(2)}, u32[]{:S(2)}) %collective-permute-start.12) | collective-permute-done | bytes 491552 | tf_op jit(solution)/shard_map/ppermute | solution.py:422
  121.2 1.1 split_and_rotate.1
  122.5 0.8 collective-permute-start.16
  123.2 3.3 %collective-permute-start.17 = (bf16[1,160,1024]{2,1,0:T(8,128)(2,1)S(1)}, bf16[1,160,1024]{2,1,0:T(8,128)(2,1)}, u32[]{:S(2)}, u32[]{:S(2)}) collective-permute-start(bf16[1,160,1024]{2,1,0:T(8,128)(2,1)S(1)} %copy-done.1), channel_id=1, source_target_pairs={{0,8},{4,12},{8,0},{12,4},{1,9},{5,13},{9,1},{13,5},{2,10},{6,14},... | collective-permute-start | bytes 983048 | tf_op jit(solution)/shard_map/ppermute | solution.py:422
  126.5 1.4 sum_and_rotate.4.refs_1_
  127.9 0.6 collective-permute-start.21
  128.9 0.9 copy-done.4
  129.8 0.6 order_and_keys.1
  130.4 7.4 %score_heads.2 = (bf16[1,16,640,640]{3,2,1,0:T(8,128)(2,1)}, f32[8,128]{1,0:T(8,128)S(1)}) custom-call(bf16[640,640]{1,0:T(8,128)(2,1)S(1)} %get-tuple-element.40.order_ref, bf16[128,640]{1,0:T(8,128)(2,1)S(1)} %get-tuple-element.41.key_t_ref, bf16[160,2048]{1,0:T(8,128)(2,1)S(1)} %sum_and_rotate.3.refs_0_, bf16[160,1024]{1,0:T(8,128)(2,1)S(1)} %sum_and_rotate.4.refs_1_, ...), custom_call_target="tpu_custom_call" | custom-call | flops 1000 | bytes 1000 | tf_op jit(solution)/shard_map/score_heads/pallas_call | solution.py:383
  137.8 3.8 %collective-permute-done.23.refs_1_ = bf16[1,320,128]{2,1,0:T(8,128)(2,1)S(1)} collective-permute-done((bf16[1,320,128]{2,1,0:T(8,128)(2,1)S(1)}, bf16[1,320,128]{2,1,0:T(8,128)(2,1)S(1)}, u32[]{:S(2)}, u32[]{:S(2)}) %collective-permute-start.23) | collective-permute-done | bytes 81952 | tf_op jit(solution)/shard_map/ppermute | solution.py:422
  141.6 2.3 %collective-permute-start.24 = (bf16[2,320,128]{2,1,0:T(8,128)(2,1)S(1)}, bf16[2,320,128]{2,1,0:T(8,128)(2,1)S(1)}, u32[]{:S(2)}, u32[]{:S(2)}) collective-permute-start(bf16[2,320,128]{2,1,0:T(8,128)(2,1)S(1)} %stack_slots.2.refs_0_), channel_id=1, source_target_pairs={{0,8},{4,12},{8,0},{12,4},{1,9},{5,13},{9,1},{13,5},{2,10},{6,14},... | collective-permute-start | bytes 491528 | tf_op jit(solution)/shard_map/ppermute | solution.py:422
  143.9 1.6 sum_and_rotate.5.refs_1_
  145.6 6.3 %collective-permute-done.24.refs_1_ = bf16[2,320,128]{2,1,0:T(8,128)(2,1)S(1)} collective-permute-done((bf16[2,320,128]{2,1,0:T(8,128)(2,1)S(1)}, bf16[2,320,128]{2,1,0:T(8,128)(2,1)S(1)}, u32[]{:S(2)}, u32[]{:S(2)}) %collective-permute-start.24) | collective-permute-done | bytes 163872 | tf_op jit(solution)/shard_map/ppermute | solution.py:422
  152.1 7.4 %score_heads.3 = (bf16[1,16,640,640]{3,2,1,0:T(8,128)(2,1)}, f32[8,128]{1,0:T(8,128)}) custom-call(bf16[640,640]{1,0:T(8,128)(2,1)S(1)} %get-tuple-element.40.order_ref, bf16[128,640]{1,0:T(8,128)(2,1)S(1)} %get-tuple-element.41.key_t_ref, bf16[160,2048]{1,0:T(8,128)(2,1)S(1)} %sum_and_rotate.3.refs_0_, ...), custom_call_target="tpu_custom_call", output_to_operand_aliasing={{0}: (6, {})} | custom-call | flops 1000 | bytes 1000 | tf_op jit(solution)/shard_map/score_heads/pallas_call | solution.py:383
  159.5 3.1 %order_values.1 = bf16[640,512]{1,0:T(8,128)(2,1)} custom-call(s32[4]{0:T(128)S(1)} %pad_add_fusion.5.place_ref, bf16[640,640]{1,0:T(8,128)(2,1)S(1)} %get-tuple-element.40.order_ref, bf16[4,320,128]{2,1,0:T(8,128)(2,1)S(1)} %stack_slots.3.own_ref, bf16[4,320,128]{2,1,0:T(8,128)(2,1)S(1)} %collective-permute-done.25.other_ref), custom_call_target="tpu_custom_call" | custom-call | tf_op jit(solution)/shard_map/order_values/pallas_call | solution.py:350
  (73 shorter events, 3.8 us)
Async XLA Ops:
  0.6 35.0 %collective-permute-start = (bf16[320,2048]{1,0:T(8,128)(2,1)}, bf16[320,2048]{1,0:T(8,128)(2,1)S(1)}, u32[]{:S(2)}, u32[]{:S(2)}) collective-permute-start(bf16[320,2048]{1,0:T(8,128)(2,1)} %refs_0_.5), channel_id=1, source_target_pairs={{0,2},{2,0},{1,3},{3,1},{4,6},{6,4},{5,7},{7,5},{8,10},{10,8},{9,1... | collective-permute-start | bytes 3932168 | tf_op jit(solution)/shard_map/ppermute | solution.py:452
  15.6 2.3 %collective-permute-start.1 = (bf16[2,160,1024]{2,1,0:T(8,128)(2,1)}, bf16[2,160,1024]{2,1,0:T(8,128)(2,1)S(1)}, u32[]{:S(2)}, u32[]{:S(2)}) collective-permute-start(bf16[2,160,1024]{2,1,0:T(8,128)(2,1)} %get-tuple-element.27), channel_id=1, source_target_pairs={{0,1},{1,0},{2,3},{3,2},{4,5},{5,4},{6,7},{7,6},{8,9},{9,8},{10,11... | collective-permute-start | bytes 1966088 | tf_op jit(solution)/shard_map/ppermute | solution.py:425
  15.6 3.2 %collective-permute-start.2 = (bf16[2,160,1024]{2,1,0:T(8,128)(2,1)}, bf16[2,160,1024]{2,1,0:T(8,128)(2,1)S(1)}, u32[]{:S(2)}, u32[]{:S(2)}) collective-permute-start(bf16[2,160,1024]{2,1,0:T(8,128)(2,1)} %get-tuple-element.28), channel_id=1, source_target_pairs={{0,1},{1,0},{2,3},{3,2},{4,5},{5,4},{6,7},{7,6},{8,9},{9,8},{10,11... | collective-permute-start | bytes 1966088 | tf_op jit(solution)/shard_map/ppermute | solution.py:425
  21.5 39.4 %collective-permute-start.7 = (bf16[2,160,2048]{2,1,0:T(8,128)(2,1)}, bf16[2,160,2048]{2,1,0:T(8,128)(2,1)}, u32[]{:S(2)}, u32[]{:S(2)}) collective-permute-start(bf16[2,160,2048]{2,1,0:T(8,128)(2,1)} %add_rows.7.refs_2_), channel_id=1, source_target_pairs={{0,4},{4,0},{8,12},{12,8},{1,5},{5,1},{9,13},{13,9},{2,6},{6,2},{1... | collective-permute-start | bytes 3932168 | tf_op jit(solution)/shard_map/ppermute | solution.py:422
  35.6 25.3 %collective-permute-start.6 = (bf16[1,160,2048]{2,1,0:T(8,128)(2,1)}, bf16[1,160,2048]{2,1,0:T(8,128)(2,1)}, u32[]{:S(2)}, u32[]{:S(2)}) collective-permute-start(bf16[1,160,2048]{2,1,0:T(8,128)(2,1)} %get-tuple-element.29.refs_4_), channel_id=1, source_target_pairs={{0,1},{1,0},{2,3},{3,2},{4,5},{5,4},{6,7},{7,6},{8,9},{9,8},{10,11... | collective-permute-start | bytes 1966088 | tf_op jit(solution)/shard_map/ppermute | solution.py:425
  42.7 12.7 %copy-start.8 = (s32[640]{0:T(1024)S(1)}, s32[640]{0:T(1024)}, u32[]{:S(2)}) copy-start(s32[640]{0:T(1024)} %param.10) | copy-start | bytes 7684
  42.8 12.7 %copy-start.10 = (s32[640]{0:T(1024)S(1)}, s32[640]{0:T(1024)}, u32[]{:S(2)}) copy-start(s32[640]{0:T(1024)} %param.11) | copy-start | bytes 7684
  42.8 13.8 %collective-permute-start.3 = (bf16[4,160,512]{2,1,0:T(8,128)(2,1)}, bf16[4,160,512]{2,1,0:T(8,128)(2,1)S(1)}, u32[]{:S(2)}, u32[]{:S(2)}) collective-permute-start(bf16[4,160,512]{2,1,0:T(8,128)(2,1)} %get-tuple-element.31.refs_2_), channel_id=1, source_target_pairs={{0,1},{1,0},{2,3},{3,2},{4,5},{5,4},{6,7},{7,6},{8,9},{9,8},{10,11... | collective-permute-start | bytes 1966088 | tf_op jit(solution)/shard_map/ppermute | solution.py:425
  54.8 2.3 %collective-permute-start.4 = (bf16[2,160,1024]{2,1,0:T(8,128)(2,1)}, bf16[2,160,1024]{2,1,0:T(8,128)(2,1)S(1)}, u32[]{:S(2)}, u32[]{:S(2)}) collective-permute-start(bf16[2,160,1024]{2,1,0:T(8,128)(2,1)} %get-tuple-element.33), channel_id=1, source_target_pairs={{0,1},{1,0},{2,3},{3,2},{4,5},{5,4},{6,7},{7,6},{8,9},{9,8},{10,11... | collective-permute-start | bytes 1966088 | tf_op jit(solution)/shard_map/ppermute | solution.py:425
  54.8 3.2 %collective-permute-start.5 = (bf16[2,160,1024]{2,1,0:T(8,128)(2,1)}, bf16[2,160,1024]{2,1,0:T(8,128)(2,1)S(1)}, u32[]{:S(2)}, u32[]{:S(2)}) collective-permute-start(bf16[2,160,1024]{2,1,0:T(8,128)(2,1)} %get-tuple-element.34), channel_id=1, source_target_pairs={{0,1},{1,0},{2,3},{3,2},{4,5},{5,4},{6,7},{7,6},{8,9},{9,8},{10,11... | collective-permute-start | bytes 1966088 | tf_op jit(solution)/shard_map/ppermute | solution.py:425
  55.5 5.0 %copy-start.6 = (s32[320]{0:T(512)}, s32[320]{0:T(512)S(1)}, u32[]{:S(2)}) copy-start(s32[320]{0:T(512)S(1)} %add.106) | copy-start | bytes 3844
  56.5 44.7 %collective-permute-start.15 = (bf16[1,160,2048]{2,1,0:T(8,128)(2,1)}, bf16[1,160,2048]{2,1,0:T(8,128)(2,1)S(1)}, u32[]{:S(2)}, u32[]{:S(2)}) collective-permute-start(bf16[1,160,2048]{2,1,0:T(8,128)(2,1)} %get-tuple-element.42), channel_id=1, source_target_pairs={{0,1},{1,0},{2,3},{3,2},{4,5},{5,4},{6,7},{7,6},{8,9},{9,8},{10,11... | collective-permute-start | bytes 1966088 | tf_op jit(solution)/shard_map/ppermute | solution.py:425
  60.5 35.3 %collective-permute-start.10 = (bf16[1,160,2560]{2,1,0:T(8,128)(2,1)}, bf16[1,160,2560]{2,1,0:T(8,128)(2,1)S(1)}, u32[]{:S(2)}, u32[]{:S(2)}) collective-permute-start(bf16[1,160,2560]{2,1,0:T(8,128)(2,1)} %add_rows.8.refs_3_.refs_2_), channel_id=1, source_target_pairs={{0,4},{4,0},{8,12},{12,8},{1,5},{5,1},{9,13},{13,9},{2,6},{6,2},{1... | collective-permute-start | bytes 2457608 | tf_op jit(solution)/shard_map/ppermute | solution.py:422
  63.6 30.3 %collective-permute-start.11 = (bf16[1,160,2048]{2,1,0:T(8,128)(2,1)}, bf16[1,160,2048]{2,1,0:T(8,128)(2,1)S(1)}, u32[]{:S(2)}, u32[]{:S(2)}) collective-permute-start(bf16[1,160,2048]{2,1,0:T(8,128)(2,1)} %add_rows.9.refs_3_), channel_id=1, source_target_pairs={{0,8},{4,12},{8,0},{12,4},{1,9},{5,13},{9,1},{13,5},{2,10},{6,14},... | collective-permute-start | bytes 1966088 | tf_op jit(solution)/shard_map/ppermute | solution.py:422
  66.2 1.1 copy-start.2
  74.4 4.9 %collective-permute-start.9 = (bf16[1,160,1024]{2,1,0:T(8,128)(2,1)}, bf16[1,160,1024]{2,1,0:T(8,128)(2,1)S(1)}, u32[]{:S(2)}, u32[]{:S(2)}) collective-permute-start(bf16[1,160,1024]{2,1,0:T(8,128)(2,1)} %get-tuple-element.36.refs_4_), channel_id=1, source_target_pairs={{0,1},{1,0},{2,3},{3,2},{4,5},{5,4},{6,7},{7,6},{8,9},{9,8},{10,11... | collective-permute-start | bytes 983048 | tf_op jit(solution)/shard_map/ppermute | solution.py:425
  74.4 24.9 %collective-permute-start.13 = (bf16[1,160,1024]{2,1,0:T(8,128)(2,1)}, bf16[1,160,1024]{2,1,0:T(8,128)(2,1)S(1)}, u32[]{:S(2)}, u32[]{:S(2)}) collective-permute-start(bf16[1,160,1024]{2,1,0:T(8,128)(2,1)} %get-tuple-element.38), channel_id=1, source_target_pairs={{0,1},{1,0},{2,3},{3,2},{4,5},{5,4},{6,7},{7,6},{8,9},{9,8},{10,11... | collective-permute-start | bytes 983048 | tf_op jit(solution)/shard_map/ppermute | solution.py:425
  77.2 2.0 %copy-start.5 = (bf16[1,160,1536]{2,1,0:T(8,128)(2,1)S(1)}, bf16[1,160,1536]{2,1,0:T(8,128)(2,1)}, u32[]{:S(2)}) copy-start(bf16[1,160,1536]{2,1,0:T(8,128)(2,1)} %add_rows.10.refs_2_) | copy-start | bytes 1474564
  79.2 33.8 %collective-permute-start.8 = (bf16[1,160,1536]{2,1,0:T(8,128)(2,1)S(1)}, bf16[1,160,1536]{2,1,0:T(8,128)(2,1)S(1)}, u32[]{:S(2)}, u32[]{:S(2)}) collective-permute-start(bf16[1,160,1536]{2,1,0:T(8,128)(2,1)S(1)} %copy-done.5), channel_id=1, source_target_pairs={{0,4},{4,0},{8,12},{12,8},{1,5},{5,1},{9,13},{13,9},{2,6},{6,2},{1... | collective-permute-start | bytes 1474568 | tf_op jit(solution)/shard_map/ppermute | solution.py:422
  97.9 23.3 %collective-permute-start.12 = (bf16[1,160,1536]{2,1,0:T(8,128)(2,1)}, bf16[1,160,1536]{2,1,0:T(8,128)(2,1)S(1)}, u32[]{:S(2)}, u32[]{:S(2)}) collective-permute-start(bf16[1,160,1536]{2,1,0:T(8,128)(2,1)} %add_rows.12.refs_3_), channel_id=1, source_target_pairs={{0,8},{4,12},{8,0},{12,4},{1,9},{5,13},{9,1},{13,5},{2,10},{6,14},... | collective-permute-start | bytes 1474568 | tf_op jit(solution)/shard_map/ppermute | solution.py:422
  101.2 1.0 copy-start
  104.2 17.0 %copy-start.1 = (bf16[1,160,1024]{2,1,0:T(8,128)(2,1)S(1)}, bf16[1,160,1024]{2,1,0:T(8,128)(2,1)}, u32[]{:S(2)}) copy-start(bf16[1,160,1024]{2,1,0:T(8,128)(2,1)} %add_rows.13.refs_4_.refs_2_) | copy-start | bytes 983044
  104.3 24.5 %collective-permute-start.20 = (bf16[160,2048]{1,0:T(8,128)(2,1)S(1)}, bf16[160,2048]{1,0:T(8,128)(2,1)}, u32[]{:S(2)}, u32[]{:S(2)}) collective-permute-start(bf16[160,2048]{1,0:T(8,128)(2,1)S(1)} %sum_and_rotate.3.refs_0_), channel_id=1, source_target_pairs={{0,1},{1,0},{2,3},{3,2},{4,5},{5,4},{6,7},{7,6},{8,9},{9,8},{10,11... | collective-permute-start | bytes 1966088 | tf_op jit(solution)/shard_map/ppermute | solution.py:425
  111.4 15.1 %collective-permute-start.19 = (bf16[1,160,1024]{2,1,0:T(8,128)(2,1)}, bf16[1,160,1024]{2,1,0:T(8,128)(2,1)S(1)}, u32[]{:S(2)}, u32[]{:S(2)}) collective-permute-start(bf16[1,160,1024]{2,1,0:T(8,128)(2,1)} %get-tuple-element.45), channel_id=1, source_target_pairs={{0,1},{1,0},{2,3},{3,2},{4,5},{5,4},{6,7},{7,6},{8,9},{9,8},{10,11... | collective-permute-start | bytes 983048 | tf_op jit(solution)/shard_map/ppermute | solution.py:425
  122.3 6.1 %copy-start.3 = (bf16[320,128]{1,0:T(8,128)(2,1)}, bf16[320,128]{1,0:T(8,128)(2,1)S(1)}, u32[]{:S(2)}) copy-start(bf16[320,128]{1,0:T(8,128)(2,1)S(1)} %get-tuple-element.39.own_ref) | copy-start | bytes 245764
  122.4 6.1 %copy-start.11 = (s32[2]{0:T(128)S(1)}, s32[2]{0:T(128)}, u32[]{:S(2)}) copy-start(s32[2]{0:T(128)} %get-tuple-element.57) | copy-start | bytes 28
  122.4 6.1 %copy-start.9 = (s32[640]{0:T(1024)S(1)}, s32[640]{0:T(1024)}, u32[]{:S(2)}) copy-start(s32[640]{0:T(1024)} %param.10) | copy-start | bytes 7684
  122.4 6.5 %copy-start.7 = (s32[320]{0:T(512)S(1)}, s32[320]{0:T(512)}, u32[]{:S(2)}) copy-start(s32[320]{0:T(512)} %copy-done.6) | copy-start | bytes 3844
  122.4 5.5 %collective-permute-start.14 = (bf16[320,128]{1,0:T(8,128)(2,1)S(1)}, bf16[320,128]{1,0:T(8,128)(2,1)S(1)}, u32[]{:S(2)}, u32[]{:S(2)}) collective-permute-start(bf16[320,128]{1,0:T(8,128)(2,1)S(1)} %get-tuple-element.39.own_ref), channel_id=1, source_target_pairs={{0,1},{1,0},{2,3},{3,2},{4,5},{5,4},{6,7},{7,6},{8,9},{9,8},{10,11... | collective-permute-start | bytes 245768 | tf_op jit(solution)/shard_map/ppermute | solution.py:425
  122.5 21.4 %collective-permute-start.16 = (bf16[1,160,1024]{2,1,0:T(8,128)(2,1)}, bf16[1,160,1024]{2,1,0:T(8,128)(2,1)S(1)}, u32[]{:S(2)}, u32[]{:S(2)}) collective-permute-start(bf16[1,160,1024]{2,1,0:T(8,128)(2,1)} %add_rows.11.refs_6_), channel_id=1, source_target_pairs={{0,4},{4,0},{8,12},{12,8},{1,5},{5,1},{9,13},{13,9},{2,6},{6,2},{1... | collective-permute-start | bytes 983048 | tf_op jit(solution)/shard_map/ppermute | solution.py:422
  123.2 20.7 %collective-permute-start.17 = (bf16[1,160,1024]{2,1,0:T(8,128)(2,1)S(1)}, bf16[1,160,1024]{2,1,0:T(8,128)(2,1)}, u32[]{:S(2)}, u32[]{:S(2)}) collective-permute-start(bf16[1,160,1024]{2,1,0:T(8,128)(2,1)S(1)} %copy-done.1), channel_id=1, source_target_pairs={{0,8},{4,12},{8,0},{12,4},{1,9},{5,13},{9,1},{13,5},{2,10},{6,14},... | collective-permute-start | bytes 983048 | tf_op jit(solution)/shard_map/ppermute | solution.py:422
  126.5 17.4 %collective-permute-start.18 = (bf16[1,160,1024]{2,1,0:T(8,128)(2,1)}, bf16[1,160,1024]{2,1,0:T(8,128)(2,1)}, u32[]{:S(2)}, u32[]{:S(2)}) collective-permute-start(bf16[1,160,1024]{2,1,0:T(8,128)(2,1)} %get-tuple-element.44), channel_id=1, source_target_pairs={{0,1},{1,0},{2,3},{3,2},{4,5},{5,4},{6,7},{7,6},{8,9},{9,8},{10,11... | collective-permute-start | bytes 983048 | tf_op jit(solution)/shard_map/ppermute | solution.py:425
  127.9 2.5 %collective-permute-start.21 = (bf16[160,1024]{1,0:T(8,128)(2,1)S(1)}, bf16[160,1024]{1,0:T(8,128)(2,1)}, u32[]{:S(2)}, u32[]{:S(2)}) collective-permute-start(bf16[160,1024]{1,0:T(8,128)(2,1)S(1)} %sum_and_rotate.4.refs_1_), channel_id=1, source_target_pairs={{0,1},{1,0},{2,3},{3,2},{4,5},{5,4},{6,7},{7,6},{8,9},{9,8},{10,11... | collective-permute-start | bytes 983048 | tf_op jit(solution)/shard_map/ppermute | solution.py:425
  128.8 12.8 %collective-permute-start.23 = (bf16[1,320,128]{2,1,0:T(8,128)(2,1)S(1)}, bf16[1,320,128]{2,1,0:T(8,128)(2,1)S(1)}, u32[]{:S(2)}, u32[]{:S(2)}) collective-permute-start(bf16[1,320,128]{2,1,0:T(8,128)(2,1)S(1)} %get-tuple-element.49.refs_0_), channel_id=1, source_target_pairs={{0,4},{4,0},{8,12},{12,8},{1,5},{5,1},{9,13},{13,9},{2,6},{6,2},{1... | collective-permute-start | bytes 245768 | tf_op jit(solution)/shard_map/ppermute | solution.py:422
  128.9 0.9 copy-start.4
  141.6 10.3 %collective-permute-start.24 = (bf16[2,320,128]{2,1,0:T(8,128)(2,1)S(1)}, bf16[2,320,128]{2,1,0:T(8,128)(2,1)S(1)}, u32[]{:S(2)}, u32[]{:S(2)}) collective-permute-start(bf16[2,320,128]{2,1,0:T(8,128)(2,1)S(1)} %stack_slots.2.refs_0_), channel_id=1, source_target_pairs={{0,8},{4,12},{8,0},{12,4},{1,9},{5,13},{9,1},{13,5},{2,10},{6,14},... | collective-permute-start | bytes 491528 | tf_op jit(solution)/shard_map/ppermute | solution.py:422
  145.5 6.6 %collective-permute-start.22 = (bf16[160,1024]{1,0:T(8,128)(2,1)S(1)}, bf16[160,1024]{1,0:T(8,128)(2,1)S(1)}, u32[]{:S(2)}, u32[]{:S(2)}) collective-permute-start(bf16[160,1024]{1,0:T(8,128)(2,1)S(1)} %sum_and_rotate.5.refs_1_), channel_id=1, source_target_pairs={{0,1},{1,0},{2,3},{3,2},{4,5},{5,4},{6,7},{7,6},{8,9},{9,8},{10,11... | collective-permute-start | bytes 983048 | tf_op jit(solution)/shard_map/ppermute | solution.py:425
  151.9 7.6 %collective-permute-start.25 = (bf16[4,320,128]{2,1,0:T(8,128)(2,1)S(1)}, bf16[4,320,128]{2,1,0:T(8,128)(2,1)S(1)}, u32[]{:S(2)}, u32[]{:S(2)}) collective-permute-start(bf16[4,320,128]{2,1,0:T(8,128)(2,1)S(1)} %stack_slots.3.own_ref), channel_id=1, source_target_pairs={{0,1},{1,0},{2,3},{3,2},{4,5},{5,4},{6,7},{7,6},{8,9},{9,8},{10,11... | collective-permute-start | bytes 983048 | tf_op jit(solution)/shard_map/ppermute | solution.py:425

commit v8 on v7

--- a/solution.py
+++ b/solution.py
@@ -150,62 +150,34 @@
     )(place, *blocks, *in_hbm([w_key, w_value, *after]))
 
 
-def add_kernel(gots, paired, extra, *refs):
+def add_kernel(gots, extra, *refs):
     keep_ref, got_refs, out_ref = refs[0], refs[1 : 1 + gots], refs[-1]
-    pair_refs = refs[1 + gots : 1 + gots + 2 * paired]
-    landed_refs = refs[1 + gots + 2 * paired :][: extra * (1 + paired)]
+    landed_refs = refs[1 + gots :][:extra]
     width = got_refs[0].shape[2]
-    cols = gots * width
-
-    def total(first, second, landed):
-        value = first + second.astype(jnp.float32)
-        for term in landed:
-            value = value + term.astype(jnp.float32)
-        return value.astype(out_ref.dtype)
-
     for t, got_ref in enumerate(got_refs):
         part = slice(t * width, (t + 1) * width)
-        landed = [landed_refs[0][0, :, part]] if extra else []
-        out_ref[0, :, part] = total(keep_ref[0, :, part], got_ref[0], landed)
-    if paired:
-        landed = [landed_refs[1][0]] if extra else []
-        out_ref[0, :, cols:] = total(pair_refs[0][0], pair_refs[1][0], landed)
-
-
-def add_rows(first, count, rows, b, keep, gots, start, cols, pair=(), slot=0, landed=(), after=()):
-    whole = keep.shape[2]
-    width = cols // len(gots)
-    shift = start // cols if gots[0].shape[2] == whole else 0
-    more = pair[0].shape[2] if pair else 0
-    keep_spec = pl.BlockSpec((1, rows, cols), lambda s: (first + s, b, start // cols))
-    got_spec = pl.BlockSpec((1, rows, width), lambda s: (first + s, b, shift))
-    pair_spec = pl.BlockSpec((1, rows, more), lambda s: (slot + s, 0, 0))
-    landed_specs = [pl.BlockSpec((1, rows, cols), lambda s: (s, 0, start // cols))]
-    if pair:
-        landed_specs.append(pl.BlockSpec((1, rows, more), lambda s: (s, 0, whole // more)))
-    landed_specs = landed_specs * len(landed)
-    return pl.pallas_call(
-        functools.partial(add_kernel, len(gots), len(pair) // 2, len(landed)),
+        value = keep_ref[0, :, part] + got_ref[0].astype(jnp.float32)
+        for landed_ref in landed_refs:
+            value = value + landed_ref[0, :, part].astype(jnp.float32)
+        out_ref[0, :, part] = value.astype(out_ref.dtype)
+
+
+def add_rows(first, count, keep, gots, start, cols, landed=(), after=()):
+    rows, width = keep.shape[1], cols // len(gots)
+    columns = start // cols
+    return pl.pallas_call(
+        functools.partial(add_kernel, len(gots), len(landed)),
         grid=(count,),
-        in_specs=[keep_spec]
-        + [got_spec] * len(gots)
-        + [pair_spec] * len(pair)
-        + landed_specs
+        in_specs=[pl.BlockSpec((1, rows, cols), lambda s: (first + s, 0, columns))]
+        + [pl.BlockSpec((1, rows, width), lambda s: (first + s, 0, 0))] * len(gots)
+        + [pl.BlockSpec((1, rows, cols), lambda s: (s, 0, columns))] * len(landed)
         + [pl.BlockSpec(memory_space=pl.ANY)] * len(after),
-        out_specs=pl.BlockSpec((1, rows, cols + more), lambda s: (s, 0, 0)),
-        out_shape=pltpu.HBM((count, rows, cols + more), jnp.bfloat16),
+        out_specs=pl.BlockSpec((1, rows, cols), lambda s: (s, 0, 0)),
+        out_shape=pltpu.HBM((count, rows, cols), jnp.bfloat16),
         compiler_params=pltpu.CompilerParams(vmem_limit_bytes=VMEM_BYTES),
         cost_estimate=LIGHT,
         name="add_rows",
-    )(
-        *in_hbm([keep]),
-        *gots,
-        *in_hbm(pair[:1]),
-        *pair[1:],
-        *(list(landed) * (2 if pair else 1)),
-        *in_hbm(after[:1]),
-        *after[1:],
-    )
+    )(*in_hbm([keep]), *gots, *landed, *in_hbm(after[:1]), *after[1:])
 
 
 def rotate_kernel(count, pieces, cos_ref, sin_ref, *refs):
@@ -478,36 +450,44 @@
         turned = sum_and_rotate(cosine[table], sine[table], added, gots, cols, behind)
         return turned, other_core(turned)
 
-    def add_even(b, start, cols, pair, behind):
+    def add_even(b, start, cols, behind):
         if shards == 2:
             return [], behind
         keep, got = evens[b]
         each = len(got) * cols // head_cols
         got = got[start // cols * each :][:each]
-        summed = add_rows(
-            0, len(even), half, 0, keep, got, start, cols, pair, len(odd), (fars[b],), behind
-        )
+        summed = add_rows(0, len(even), keep, got, start, cols, (fars[b],), behind)
         terms, first = spread({x: summed[k] for k, x in enumerate(even)})
         return [(term, 0, 0, 0) for term in terms], (first,)
 
     last, split = tps - 1, head_cols // tile
     placed = in_hbm(blocks[:1]) + blocks[1:]
-    evens, owns, fars, terms, pair, after = [], [], [], [], (), ()
+    evens, owns, fars, terms, after = [], [], [], [], ()
     for b, block in enumerate(placed):
         if fast_pair and b == last:
+            width = 2 * DH * tps
             slots = odd + even + [0]
-            pair_keep, give = project_pair(rindex, findex, slots, placed, w_key, w_value, after)
-            pair = (pair_keep, other_core(give))
+            pair, give = project_pair(rindex, findex, slots, placed, w_key, w_value, after)
+            pair_got = [other_core(give)]
             after = (give,)
         odd_keep, odd_got, given = project(odd, [block], tile, after)
+        after = ()
+        if fast_pair and b == last:
+            pair_sent = add_rows(0, len(odd), pair, pair_got, 0, width, (), (given,))
+            pair_landed = swap(pair_sent, 1)
+            after = (pair_sent,)
         count = len(odd) - 1 if b == last else len(odd)
-        odd_sent = add_rows(0, count, half, 0, odd_keep, odd_got, 0, head_cols, pair)
+        odd_sent = add_rows(0, count, odd_keep, odd_got, 0, head_cols, (), after)
         fars.append(swap(odd_sent, 1))
         after = (odd_sent,)
+        if fast_pair and b == last:
+            summed = add_rows(len(odd), len(even), pair, pair_got, 0, width, (pair_landed,), after)
+            pair_terms, first = spread({x: summed[k] for k, x in enumerate(even)})
+            after = (odd_sent, first)
         if b > 0:
-            added, after = add_even(b - 1, 0, head_cols, (), after)
+            added, behind = add_even(b - 1, 0, head_cols, after)
             terms.append([(fars[b - 1], len(odd) - 1, 0, 0)] + added)
-            after = (odd_sent,) + after
+            after = after + behind
         if b < last:
             keep, got, given = project(even + [0], [block], head_cols, after, LIGHT, True)
             evens.append((keep, got[:1] if len(even) == 1 else [jnp.concatenate(got[:-1])]))
@@ -516,26 +496,30 @@
             keep, got, given = project(even, [block], tile, after, HEAVY)
             evens.append((keep, got))
         after = (given,)
-    parts, behind = [], tuple(term[0] for row in terms for term in row[1:])
+    parts, landed = [], tuple(term[0] for row in terms for term in row[1:])
     for p in range(split):
         near_sent = add_rows(
-            len(odd) - 1, 1, half, 0, odd_keep, odd_got[p : p + 1], p * tile, tile,
-            pair if p == 0 else (), len(odd) - 1, (), after,
+            len(odd) - 1, 1, odd_keep, odd_got[p : p + 1], p * tile, tile, (), after
         )
         parts.append([(swap(near_sent, 1), 0, 0, 0)])
         after = (near_sent,)
-    after = after + behind
+    after = after + landed
     for p in range(split):
-        added, after = add_even(last, p * tile, tile, pair if p == 0 else (), after)
+        added, after = add_even(last, p * tile, tile, after)
         parts[p] += added
-    keep, got, _ = project([0], placed[last:], tile, after, HEAVY)
+    if fast_pair:
+        pieces = [(array, shards - 1, 0) for array in [pair] + pair_got]
+        pieces += [(pair_landed, len(odd) - 1, 0)] + [(term, 0, 0) for term in pair_terms]
+        key_rot, held = split_and_rotate(cosine, sine, pieces, width, after)
+    done = after + ((key_rot,) if fast_pair else ())
+    keep, got, _ = project([0], placed[last:], tile, done, HEAVY)
     owns.append((keep, 0, got))
 
     if fast_pair:
-        width = 2 * DH * tps
-        pieces = [(array, shards - 1, 0) for array in pair]
-        pieces += [(term, 0, tile) for term, _, _, _ in parts[0]]
-        key_rot, held = split_and_rotate(cosine, sine, pieces, width, after)
+        bit, behind = 1, after
+        while bit < shards:
+            held = stack_slots([held, swap(held, bit)], behind)
+            bit *= 2
     else:
         x = jnp.concatenate(blocks, axis=0)
         key_sum, value_sum = lax.psum(
@@ -571,10 +555,6 @@
         )
         mark = (mark,)
         if fast_pair and p == 0:
-            bit = 1
-            while bit < shards:
-                held = stack_slots([held, swap(held, bit)], mark)
-                bit *= 2
             values = order_values(findex, order, held, other_core(held))
     return (scores[0], values)
 

time: 164 us -> 170 us (1.037)
  local copies, waits for them, and re-layouts: 3.42 us -> 6.54 us
  starting transfers between devices: 20.6 us -> 22.8 us
  Pallas kernels: 96.8 us -> 98.6 us
    unnamed x24 -> x34, local copies, waits for them, and re-layouts: 3.02 us -> 6.14 us
    pallas_call x7 -> x9, Pallas kernels: 15.8 us -> 18.5 us  [add_rows(): pl.pallas_call(functools.partial(add_kernel, len(gots), len(landed)), gri...]
    ppermute x9 -> x11, starting transfers between devices: 14 us -> 16.3 us  [swap(): return lax.ppermute(x, 'fsdp', [(i, i ^ bit) for i in range(shards)])]
    ppermute x9 -> x11, waiting for transfers between devices: 34.2 us -> 34.9 us  [swap(): return lax.ppermute(x, 'fsdp', [(i, i ^ bit) for i in range(shards)])]
  transfers between devices with their start and end apart: 26 -> 28, of which waited for: 10 -> 9; matrix products, arithmetic and copies ran while one was open for 2% -> 2% of each run, Pallas kernels for 58% -> 54%
where the time goes in v8:
time: 170 us; the launch traced here: 169 us
  Pallas kernels  98.6 us (58%)
  waiting for transfers between devices  37.7 us (22%)
  starting transfers between devices  22.8 us (13%)
  local copies, waits for them, and re-layouts  6.54 us (4%)
  other arithmetic  2.55 us (1%)
    pallas_call x5, Pallas kernels, project_query(): pl.pallas_call(functools.partial(query_kernel, count, pieces, by_slot), g...  49.4 us
    ppermute x11, waiting for transfers between devices, swap(): return lax.ppermute(x, 'fsdp', [(i, i ^ bit) for i in range(shards)])  34.9 us
    pallas_call x9, Pallas kernels, add_rows(): pl.pallas_call(functools.partial(add_kernel, len(gots), len(landed)), gri...  18.5 us
    ppermute x11, starting transfers between devices, swap(): return lax.ppermute(x, 'fsdp', [(i, i ^ bit) for i in range(shards)])  16.3 us
    pallas_call x2, Pallas kernels, score_heads(): pl.pallas_call(functools.partial(score_kernel, len(queries)), grid=(count...  14 us
    pallas_call x1, Pallas kernels, project_pair(): pl.pallas_call(functools.partial(pair_kernel, count), grid_spec=pltpu.Pre...  7.13 us
    unnamed x34, local copies, waits for them, and re-layouts  6.14 us
    pallas_call x3, Pallas kernels, sum_and_rotate(): pl.pallas_call(functools.partial(rotate_kernel, len(terms), len(gots)), g...  4.94 us
  transfers between devices with their start and end apart: 28, of which 9 were waited for; matrix products, arithmetic and copies ran while one was open for 2% of the time, Pallas kernels for 54%

profile of v8, /device:TPU:0, one launch (start us, length us, event | category | flops | bytes accessed | tf_op | source)
XLA Modules:
  0.0 169.1 jit_solution(2132004645007710789)
XLA Ops:
  0.6 3.0 %collective-permute-start = (bf16[320,2048]{1,0:T(8,128)(2,1)}, bf16[320,2048]{1,0:T(8,128)(2,1)S(1)}, u32[]{:S(2)}, u32[]{:S(2)}) collective-permute-start(bf16[320,2048]{1,0:T(8,128)(2,1)} %refs_0_.5), channel_id=1, source_target_pairs={{0,2},{2,0},{1,3},{3,1},{4,6},{6,4},{5,7},{7,5},{8,10},{10,8},{9,1... | collective-permute-start | bytes 3932168 | tf_op jit(solution)/shard_map/ppermute | solution.py:424
  3.7 11.9 %query_products.5 = (f32[2,160,2048]{2,1,0:T(8,128)}, bf16[2,160,1024]{2,1,0:T(8,128)(2,1)}, bf16[2,160,1024]{2,1,0:T(8,128)(2,1)}) custom-call(s32[3]{0:T(128)S(1)} %pad_add_fusion.2.place_ref, bf16[320,2048]{1,0:T(8,128)(2,1)} %refs_0_.5, bf16[2048,8192]{1,0:T(8,128)(2,1)} %refs_1_.9), custom_call_target="tpu_custom_call" | custom-call | flops 1000 | bytes 1000 | tf_op jit(solution)/shard_map/query_products/pallas_call | solution.py:87
  16.1 1.8 %collective-permute-done.1.refs_1_ = bf16[2,160,1024]{2,1,0:T(8,128)(2,1)S(1)} collective-permute-done((bf16[2,160,1024]{2,1,0:T(8,128)(2,1)}, bf16[2,160,1024]{2,1,0:T(8,128)(2,1)S(1)}, u32[]{:S(2)}, u32[]{:S(2)}) %collective-permute-start.1) | collective-permute-done | bytes 655392 | tf_op jit(solution)/shard_map/ppermute | solution.py:397
  17.9 0.9 collective-permute-done.2.refs_2_
  18.9 2.7 %add_rows.9.refs_2_ = bf16[2,160,2048]{2,1,0:T(8,128)(2,1)} custom-call(f32[2,160,2048]{2,1,0:T(8,128)} %get-tuple-element.26.refs_0_, bf16[2,160,1024]{2,1,0:T(8,128)(2,1)S(1)} %collective-permute-done.1.refs_1_, bf16[2,160,1024]{2,1,0:T(8,128)(2,1)S(1)} %collective-permute-done.2.refs_2_), custom_call_target="tpu_custom_call" | custom-call | flops 1000 | bytes 1000 | tf_op jit(solution)/shard_map/add_rows/pallas_call | solution.py:168
  21.6 1.6 collective-permute-start.9
  23.3 11.8 %query_products.6 = (f32[2,160,2048]{2,1,0:T(8,128)}, bf16[1,160,2048]{2,1,0:T(8,128)(2,1)}, bf16[1,160,2048]{2,1,0:T(8,128)(2,1)}) custom-call(s32[3]{0:T(128)S(1)} %pad_add_fusion.1.place_ref, bf16[320,2048]{1,0:T(8,128)(2,1)} %refs_0_.5, bf16[2048,8192]{1,0:T(8,128)(2,1)} %refs_1_.9, bf16[2,160,2048]{2,1,0:T(8,128)(2,1)} %add_rows.9.refs_2_), custom_call_target="tpu_custom_call" | custom-call | flops 1000 | bytes 1000 | tf_op jit(solution)/shard_map/query_products/pallas_call | solution.py:87
  35.1 7.1 %key_value_products.1 = (f32[4,160,512]{2,1,0:T(8,128)}, bf16[4,160,512]{2,1,0:T(8,128)(2,1)}) custom-call(s32[5]{0:T(128)S(1)} %stack.27.place_ref, bf16[320,2048]{1,0:T(8,128)(2,1)} %refs_0_.5, bf16[320,2048]{1,0:T(8,128)(2,1)S(1)} %collective-permute-done.refs_1_.refs_0_, bf16[2048,512]{1,0:T(8,128)(2,1)} %refs_2_.1, bf16[2048,512]{1,0:T(8,128)(2,1)} %refs_3_.1, ...), custom_call_target="tpu_custom_call" | custom-call | flops 1000 | bytes 1000 | tf_op jit(solution)/shard_map/key_value_products/pallas_call | solution.py:132
  42.2 0.6 broadcast_add_fusion
  43.5 11.6 %query_products.7 = (f32[2,160,2048]{2,1,0:T(8,128)}, bf16[2,160,1024]{2,1,0:T(8,128)(2,1)}, bf16[2,160,1024]{2,1,0:T(8,128)(2,1)}) custom-call(s32[3]{0:T(128)S(1)} %pad_add_fusion.2.place_ref, bf16[320,2048]{1,0:T(8,128)(2,1)S(1)} %collective-permute-done.refs_1_.refs_0_, bf16[2048,8192]{1,0:T(8,128)(2,1)} %refs_1_.9, ...), custom_call_target="tpu_custom_call" | custom-call | flops 1000 | bytes 1000 | tf_op jit(solution)/shard_map/query_products/pallas_call | solution.py:87
  56.0 1.8 %add_rows.10.refs_3_ = bf16[2,160,512]{2,1,0:T(8,128)(2,1)} custom-call(f32[4,160,512]{2,1,0:T(8,128)} %get-tuple-element.30.refs_0_, bf16[4,160,512]{2,1,0:T(8,128)(2,1)S(1)} %collective-permute-done.3.refs_1_, bf16[2,160,1024]{2,1,0:T(8,128)(2,1)} %get-tuple-element.32.refs_2_), custom_call_target="tpu_custom_call" | custom-call | flops 1000 | bytes 1000 | tf_op jit(solution)/shard_map/add_rows/pallas_call | solution.py:168
  58.2 0.6 fusion.4
  59.0 2.3 %add_rows.11.refs_3_.refs_2_ = bf16[1,160,2048]{2,1,0:T(8,128)(2,1)} custom-call(f32[2,160,2048]{2,1,0:T(8,128)} %get-tuple-element.33.refs_0_, bf16[2,160,1024]{2,1,0:T(8,128)(2,1)S(1)} %collective-permute-done.5.refs_1_, bf16[2,160,1024]{2,1,0:T(8,128)(2,1)S(1)} %collective-permute-done.6.refs_2_.refs_1_, bf16[2,160,512]{2,1,0:T(8,128)(2,1)} %add_rows.10.refs_3_), custom_call_target="tpu_custom_call" | custom-call | flops 1000 | bytes 1000 | tf_op jit(solution)/shard_map/add_rows/pallas_call | solution.py:168
  61.3 1.6 collective-permute-start.11
  62.9 5.7 %collective-permute-done.4.refs_2_ = bf16[2,160,512]{2,1,0:T(8,128)(2,1)S(1)} collective-permute-done((bf16[2,160,512]{2,1,0:T(8,128)(2,1)}, bf16[2,160,512]{2,1,0:T(8,128)(2,1)S(1)}, u32[]{:S(2)}, u32[]{:S(2)}) %collective-permute-start.4) | collective-permute-done | bytes 327712 | tf_op jit(solution)/shard_map/ppermute | solution.py:394
  68.5 1.7 %add_rows.12.refs_4_.refs_3_ = bf16[1,160,512]{2,1,0:T(8,128)(2,1)} custom-call(f32[4,160,512]{2,1,0:T(8,128)} %get-tuple-element.30.refs_0_, bf16[4,160,512]{2,1,0:T(8,128)(2,1)S(1)} %collective-permute-done.3.refs_1_, bf16[2,160,512]{2,1,0:T(8,128)(2,1)S(1)} %collective-permute-done.4.refs_2_, bf16[1,160,2048]{2,1,0:T(8,128)(2,1)} %add_rows.11.refs_3_.refs_2_), custom_call_target="tpu_custom_call" | custom-call | flops 1000 | bytes 1000 | tf_op jit(solution)/shard_map/add_rows/pallas_call | solution.py:168
  70.2 2.3 %add_rows.13.refs_4_ = bf16[1,160,2048]{2,1,0:T(8,128)(2,1)} custom-call(f32[2,160,2048]{2,1,0:T(8,128)} %get-tuple-element.35.refs_0_, bf16[1,160,2048]{2,1,0:T(8,128)(2,1)S(1)} %collective-permute-done.8.refs_1_, bf16[2,160,2048]{2,1,0:T(8,128)(2,1)S(1)} %collective-permute-done.9.refs_2_.refs_1_, bf16[1,160,2048]{2,1,0:T(8,128)(2,1)} %add_rows.11.refs_3_.refs_2_, ...), custom_call_target="tpu_custom_call" | custom-call | flops 1000 | bytes 1000 | tf_op jit(solution)/shard_map/add_rows/pallas_call | solution.py:168
  72.6 2.6 %collective-permute-start.13 = (bf16[1,160,2048]{2,1,0:T(8,128)(2,1)}, bf16[1,160,2048]{2,1,0:T(8,128)(2,1)S(1)}, u32[]{:S(2)}, u32[]{:S(2)}) collective-permute-start(bf16[1,160,2048]{2,1,0:T(8,128)(2,1)} %add_rows.13.refs_4_), channel_id=1, source_target_pairs={{0,8},{4,12},{8,0},{12,4},{1,9},{5,13},{9,1},{13,5},{2,10},{6,14},... | collective-permute-start | bytes 1966088 | tf_op jit(solution)/shard_map/ppermute | solution.py:394
  75.2 1.1 copy-done.2
  76.3 7.1 %query_products.8 = (f32[1,160,2048]{2,1,0:T(8,128)}, bf16[1,160,1024]{2,1,0:T(8,128)(2,1)}, bf16[1,160,1024]{2,1,0:T(8,128)(2,1)}) custom-call(s32[2]{0:T(128)S(1)} %pad_add_fusion.3.place_ref, bf16[320,2048]{1,0:T(8,128)(2,1)S(1)} %collective-permute-done.refs_1_.refs_0_, bf16[2048,8192]{1,0:T(8,128)(2,1)} %refs_1_.9, ...), custom_call_target="tpu_custom_call" | custom-call | flops 99999997952 | bytes 100000000 | tf_op jit(solution)/shard_map/query_products/pallas_call | solution.py:87
  84.5 1.9 %add_rows.14.refs_2_ = bf16[1,160,1024]{2,1,0:T(8,128)(2,1)} custom-call(f32[2,160,2048]{2,1,0:T(8,128)} %get-tuple-element.33.refs_0_, bf16[2,160,1024]{2,1,0:T(8,128)(2,1)S(1)} %collective-permute-done.5.refs_1_, bf16[1,160,1024]{2,1,0:T(8,128)(2,1)} %get-tuple-element.38.refs_2_), custom_call_target="tpu_custom_call" | custom-call | flops 1000 | bytes 1000 | tf_op jit(solution)/shard_map/add_rows/pallas_call | solution.py:168
  86.5 1.9 %add_rows.15.refs_3_ = bf16[1,160,1024]{2,1,0:T(8,128)(2,1)} custom-call(f32[2,160,2048]{2,1,0:T(8,128)} %get-tuple-element.33.refs_0_, bf16[2,160,1024]{2,1,0:T(8,128)(2,1)S(1)} %collective-permute-done.6.refs_2_.refs_1_, bf16[1,160,1024]{2,1,0:T(8,128)(2,1)} %add_rows.14.refs_2_), custom_call_target="tpu_custom_call" | custom-call | flops 1000 | bytes 1000 | tf_op jit(solution)/shard_map/add_rows/pallas_call | solution.py:168
  88.4 2.4 %collective-permute-done.11.refs_2_ = bf16[1,160,2048]{2,1,0:T(8,128)(2,1)S(1)} collective-permute-done((bf16[1,160,2048]{2,1,0:T(8,128)(2,1)}, bf16[1,160,2048]{2,1,0:T(8,128)(2,1)S(1)}, u32[]{:S(2)}, u32[]{:S(2)}) %collective-permute-start.11) | collective-permute-done | bytes 655392 | tf_op jit(solution)/shard_map/ppermute | solution.py:394
  90.9 17.0 %collective-permute-done.13.refs_4_.refs_2_ = bf16[1,160,2048]{2,1,0:T(8,128)(2,1)S(1)} collective-permute-done((bf16[1,160,2048]{2,1,0:T(8,128)(2,1)}, bf16[1,160,2048]{2,1,0:T(8,128)(2,1)S(1)}, u32[]{:S(2)}, u32[]{:S(2)}) %collective-permute-start.13) | collective-permute-done | bytes 655392 | tf_op jit(solution)/shard_map/ppermute | solution.py:394
  107.9 1.9 %add_rows.16.refs_3_ = bf16[1,160,1024]{2,1,0:T(8,128)(2,1)} custom-call(f32[1,160,2048]{2,1,0:T(8,128)} %get-tuple-element.36.refs_0_, bf16[1,160,1024]{2,1,0:T(8,128)(2,1)S(1)} %collective-permute-done.12.refs_1_, bf16[1,160,2048]{2,1,0:T(8,128)(2,1)S(1)} %collective-permute-done.11.refs_2_, bf16[1,160,1024]{2,1,0:T(8,128)(2,1)} %add_rows.15.refs_3_, ...), custom_call_target="tpu_custom_call" | custom-call | flops 1000 | bytes 1000 | tf_op jit(solution)/shard_map/add_rows/pallas_call | solution.py:168
  109.8 1.9 %add_rows.17.refs_4_.refs_2_ = bf16[1,160,1024]{2,1,0:T(8,128)(2,1)} custom-call(f32[1,160,2048]{2,1,0:T(8,128)} %get-tuple-element.36.refs_0_, bf16[1,160,1024]{2,1,0:T(8,128)(2,1)S(1)} %collective-permute-done.10.refs_1_, bf16[1,160,2048]{2,1,0:T(8,128)(2,1)S(1)} %collective-permute-done.11.refs_2_, bf16[1,160,1024]{2,1,0:T(8,128)(2,1)} %add_rows.16.refs_3_), custom_call_target="tpu_custom_call" | custom-call | flops 1000 | bytes 1000 | tf_op jit(solution)/shard_map/add_rows/pallas_call | solution.py:168
  111.8 2.0 %collective-permute-done.7.refs_3_ = bf16[1,160,512]{2,1,0:T(8,128)(2,1)S(1)} collective-permute-done((bf16[1,160,512]{2,1,0:T(8,128)(2,1)}, bf16[1,160,512]{2,1,0:T(8,128)(2,1)S(1)}, u32[]{:S(2)}, u32[]{:S(2)}) %collective-permute-start.7) | collective-permute-done | bytes 163872 | tf_op jit(solution)/shard_map/ppermute | solution.py:394
  113.7 1.0 copy-done
  114.7 1.1 split_and_rotate.1
  115.8 7.1 %query_products.9 = (f32[1,160,2048]{2,1,0:T(8,128)}, bf16[1,160,1024]{2,1,0:T(8,128)(2,1)}, bf16[1,160,1024]{2,1,0:T(8,128)(2,1)}) custom-call(s32[2]{0:T(128)S(1)} %pad_add_fusion.4.place_ref, bf16[320,2048]{1,0:T(8,128)(2,1)S(1)} %collective-permute-done.refs_1_.refs_0_, bf16[2048,8192]{1,0:T(8,128)(2,1)} %refs_1_.9, ...), custom_call_target="tpu_custom_call" | custom-call | flops 99999997952 | bytes 100000000 | tf_op jit(solution)/shard_map/query_products/pallas_call | solution.py:87
  123.0 1.9 %sum_and_rotate.3.refs_0_ = bf16[160,2048]{1,0:T(8,128)(2,1)S(1)} custom-call(f32[160,128]{1,0:T(8,128)S(1)} %get-tuple-element.53.cos_ref, f32[160,128]{1,0:T(8,128)S(1)} %get-tuple-element.51.sin_ref, f32[2,160,2048]{2,1,0:T(8,128)} %get-tuple-element.35.refs_0_, bf16[2,160,2048]{2,1,0:T(8,128)(2,1)S(1)} %collective-permute-done.9.refs_2_.refs_1_, ...), custom_call_target="tpu_custom_call" | custom-call | flops 1000 | bytes 1000 | tf_op jit(solution)/shard_map/sum_and_rotate/pallas_call | solution.py:215
  125.5 4.4 %collective-permute-start.25 = (bf16[1,320,128]{2,1,0:T(8,128)(2,1)S(1)}, bf16[1,320,128]{2,1,0:T(8,128)(2,1)S(1)}, u32[]{:S(2)}, u32[]{:S(2)}) collective-permute-start(bf16[1,320,128]{2,1,0:T(8,128)(2,1)S(1)} %get-tuple-element.49.refs_0_), channel_id=1, source_target_pairs={{0,4},{4,0},{8,12},{12,8},{1,5},{5,1},{9,13},{13,9},{2,6},{6,2},{1... | collective-permute-start | bytes 245768 | tf_op jit(solution)/shard_map/ppermute | solution.py:394
  129.9 2.7 %collective-permute-done.25.refs_1_ = bf16[1,320,128]{2,1,0:T(8,128)(2,1)S(1)} collective-permute-done((bf16[1,320,128]{2,1,0:T(8,128)(2,1)S(1)}, bf16[1,320,128]{2,1,0:T(8,128)(2,1)S(1)}, u32[]{:S(2)}, u32[]{:S(2)}) %collective-permute-start.25) | collective-permute-done | bytes 81952 | tf_op jit(solution)/shard_map/ppermute | solution.py:394
  132.6 3.3 %collective-permute-start.26 = (bf16[2,320,128]{2,1,0:T(8,128)(2,1)S(1)}, bf16[2,320,128]{2,1,0:T(8,128)(2,1)S(1)}, u32[]{:S(2)}, u32[]{:S(2)}) collective-permute-start(bf16[2,320,128]{2,1,0:T(8,128)(2,1)S(1)} %stack_slots.2.refs_0_), channel_id=1, source_target_pairs={{0,8},{4,12},{8,0},{12,4},{1,9},{5,13},{9,1},{13,5},{2,10},{6,14},... | collective-permute-start | bytes 491528 | tf_op jit(solution)/shard_map/ppermute | solution.py:394
  136.1 1.8 %collective-permute-start.16 = (bf16[1,160,1024]{2,1,0:T(8,128)(2,1)}, bf16[1,160,1024]{2,1,0:T(8,128)(2,1)}, u32[]{:S(2)}, u32[]{:S(2)}) collective-permute-start(bf16[1,160,1024]{2,1,0:T(8,128)(2,1)} %add_rows.15.refs_3_), channel_id=1, source_target_pairs={{0,4},{4,0},{8,12},{12,8},{1,5},{5,1},{9,13},{13,9},{2,6},{6,2},{1... | collective-permute-start | bytes 983048 | tf_op jit(solution)/shard_map/ppermute | solution.py:394
  138.1 1.4 sum_and_rotate.4.refs_1_
  139.5 0.6 copy-done.7
  140.2 4.0 %collective-permute-done.26.refs_1_ = bf16[2,320,128]{2,1,0:T(8,128)(2,1)S(1)} collective-permute-done((bf16[2,320,128]{2,1,0:T(8,128)(2,1)S(1)}, bf16[2,320,128]{2,1,0:T(8,128)(2,1)S(1)}, u32[]{:S(2)}, u32[]{:S(2)}) %collective-permute-start.26) | collective-permute-done | bytes 163872 | tf_op jit(solution)/shard_map/ppermute | solution.py:394
  144.2 0.7 copy-done.5
  145.1 0.9 copy-done.8
  146.5 0.9 copy-done.4
  147.5 0.9 copy-done.6
  148.4 0.6 collective-permute-start.27
  149.0 7.4 %score_heads.2 = (bf16[1,16,640,640]{3,2,1,0:T(8,128)(2,1)}, f32[8,128]{1,0:T(8,128)S(1)}) custom-call(bf16[640,640]{1,0:T(8,128)(2,1)S(1)} %get-tuple-element.40.order_ref, bf16[128,640]{1,0:T(8,128)(2,1)S(1)} %get-tuple-element.41.key_t_ref, bf16[160,2048]{1,0:T(8,128)(2,1)S(1)} %sum_and_rotate.3.refs_0_, bf16[160,1024]{1,0:T(8,128)(2,1)S(1)} %sum_and_rotate.4.refs_1_, ...), custom_call_target="tpu_custom_call" | custom-call | flops 1000 | bytes 1000 | tf_op jit(solution)/shard_map/score_heads/pallas_call | solution.py:355
  156.4 1.2 collective-permute-done.17.refs_2_
  157.6 1.7 sum_and_rotate.5.refs_1_
  159.4 3.1 %order_values.1 = bf16[640,512]{1,0:T(8,128)(2,1)} custom-call(s32[4]{0:T(128)S(1)} %pad_add_fusion.5.place_ref, bf16[640,640]{1,0:T(8,128)(2,1)S(1)} %get-tuple-element.40.order_ref, bf16[4,320,128]{2,1,0:T(8,128)(2,1)S(1)} %stack_slots.3.own_ref, bf16[4,320,128]{2,1,0:T(8,128)(2,1)S(1)} %collective-permute-done.27.other_ref), custom_call_target="tpu_custom_call" | custom-call | tf_op jit(solution)/shard_map/order_values/pallas_call | solution.py:322
  162.5 6.6 %score_heads.3 = (bf16[1,16,640,640]{3,2,1,0:T(8,128)(2,1)}, f32[8,128]{1,0:T(8,128)}) custom-call(bf16[640,640]{1,0:T(8,128)(2,1)S(1)} %get-tuple-element.40.order_ref, bf16[128,640]{1,0:T(8,128)(2,1)S(1)} %get-tuple-element.41.key_t_ref, bf16[160,2048]{1,0:T(8,128)(2,1)S(1)} %sum_and_rotate.3.refs_0_, ...), custom_call_target="tpu_custom_call", output_to_operand_aliasing={{0}: (6, {})} | custom-call | flops 1000 | bytes 1000 | tf_op jit(solution)/shard_map/score_heads/pallas_call | solution.py:355
  (89 shorter events, 6.3 us)
Async XLA Ops:
  0.6 34.4 %collective-permute-start = (bf16[320,2048]{1,0:T(8,128)(2,1)}, bf16[320,2048]{1,0:T(8,128)(2,1)S(1)}, u32[]{:S(2)}, u32[]{:S(2)}) collective-permute-start(bf16[320,2048]{1,0:T(8,128)(2,1)} %refs_0_.5), channel_id=1, source_target_pairs={{0,2},{2,0},{1,3},{3,1},{4,6},{6,4},{5,7},{7,5},{8,10},{10,8},{9,1... | collective-permute-start | bytes 3932168 | tf_op jit(solution)/shard_map/ppermute | solution.py:424
  15.6 2.3 %collective-permute-start.1 = (bf16[2,160,1024]{2,1,0:T(8,128)(2,1)}, bf16[2,160,1024]{2,1,0:T(8,128)(2,1)S(1)}, u32[]{:S(2)}, u32[]{:S(2)}) collective-permute-start(bf16[2,160,1024]{2,1,0:T(8,128)(2,1)} %get-tuple-element.27), channel_id=1, source_target_pairs={{0,1},{1,0},{2,3},{3,2},{4,5},{5,4},{6,7},{7,6},{8,9},{9,8},{10,11... | collective-permute-start | bytes 1966088 | tf_op jit(solution)/shard_map/ppermute | solution.py:397
  15.6 3.2 %collective-permute-start.2 = (bf16[2,160,1024]{2,1,0:T(8,128)(2,1)}, bf16[2,160,1024]{2,1,0:T(8,128)(2,1)S(1)}, u32[]{:S(2)}, u32[]{:S(2)}) collective-permute-start(bf16[2,160,1024]{2,1,0:T(8,128)(2,1)} %get-tuple-element.28), channel_id=1, source_target_pairs={{0,1},{1,0},{2,3},{3,2},{4,5},{5,4},{6,7},{7,6},{8,9},{9,8},{10,11... | collective-permute-start | bytes 1966088 | tf_op jit(solution)/shard_map/ppermute | solution.py:397
  21.6 48.7 %collective-permute-start.9 = (bf16[2,160,2048]{2,1,0:T(8,128)(2,1)}, bf16[2,160,2048]{2,1,0:T(8,128)(2,1)S(1)}, u32[]{:S(2)}, u32[]{:S(2)}) collective-permute-start(bf16[2,160,2048]{2,1,0:T(8,128)(2,1)} %add_rows.9.refs_2_), channel_id=1, source_target_pairs={{0,4},{4,0},{8,12},{12,8},{1,5},{5,1},{9,13},{13,9},{2,6},{6,2},{1... | collective-permute-start | bytes 3932168 | tf_op jit(solution)/shard_map/ppermute | solution.py:394
  42.2 13.8 %collective-permute-start.3 = (bf16[4,160,512]{2,1,0:T(8,128)(2,1)}, bf16[4,160,512]{2,1,0:T(8,128)(2,1)S(1)}, u32[]{:S(2)}, u32[]{:S(2)}) collective-permute-start(bf16[4,160,512]{2,1,0:T(8,128)(2,1)} %get-tuple-element.31.refs_2_), channel_id=1, source_target_pairs={{0,1},{1,0},{2,3},{3,2},{4,5},{5,4},{6,7},{7,6},{8,9},{9,8},{10,11... | collective-permute-start | bytes 1966088 | tf_op jit(solution)/shard_map/ppermute | solution.py:397
  43.0 12.6 %copy-start.10 = (s32[320]{0:T(512)}, s32[320]{0:T(512)S(1)}, u32[]{:S(2)}) copy-start(s32[320]{0:T(512)S(1)} %add.106) | copy-start | bytes 3844
  43.0 12.6 %copy-start.12 = (s32[640]{0:T(1024)S(1)}, s32[640]{0:T(1024)}, u32[]{:S(2)}) copy-start(s32[640]{0:T(1024)} %param.10) | copy-start | bytes 7684
  43.0 12.6 %copy-start.14 = (s32[640]{0:T(1024)S(1)}, s32[640]{0:T(1024)}, u32[]{:S(2)}) copy-start(s32[640]{0:T(1024)} %param.11) | copy-start | bytes 7684
  43.0 27.3 %collective-permute-start.8 = (bf16[1,160,2048]{2,1,0:T(8,128)(2,1)}, bf16[1,160,2048]{2,1,0:T(8,128)(2,1)S(1)}, u32[]{:S(2)}, u32[]{:S(2)}) collective-permute-start(bf16[1,160,2048]{2,1,0:T(8,128)(2,1)} %get-tuple-element.29.refs_4_), channel_id=1, source_target_pairs={{0,1},{1,0},{2,3},{3,2},{4,5},{5,4},{6,7},{7,6},{8,9},{9,8},{10,11... | collective-permute-start | bytes 1966088 | tf_op jit(solution)/shard_map/ppermute | solution.py:397
  55.1 3.9 %collective-permute-start.5 = (bf16[2,160,1024]{2,1,0:T(8,128)(2,1)}, bf16[2,160,1024]{2,1,0:T(8,128)(2,1)S(1)}, u32[]{:S(2)}, u32[]{:S(2)}) collective-permute-start(bf16[2,160,1024]{2,1,0:T(8,128)(2,1)} %get-tuple-element.32.refs_2_), channel_id=1, source_target_pairs={{0,1},{1,0},{2,3},{3,2},{4,5},{5,4},{6,7},{7,6},{8,9},{9,8},{10,11... | collective-permute-start | bytes 1966088 | tf_op jit(solution)/shard_map/ppermute | solution.py:397
  55.1 3.9 %collective-permute-start.6 = (bf16[2,160,1024]{2,1,0:T(8,128)(2,1)}, bf16[2,160,1024]{2,1,0:T(8,128)(2,1)S(1)}, u32[]{:S(2)}, u32[]{:S(2)}) collective-permute-start(bf16[2,160,1024]{2,1,0:T(8,128)(2,1)} %get-tuple-element.34), channel_id=1, source_target_pairs={{0,1},{1,0},{2,3},{3,2},{4,5},{5,4},{6,7},{7,6},{8,9},{9,8},{10,11... | collective-permute-start | bytes 1966088 | tf_op jit(solution)/shard_map/ppermute | solution.py:397
  57.8 10.8 %collective-permute-start.4 = (bf16[2,160,512]{2,1,0:T(8,128)(2,1)}, bf16[2,160,512]{2,1,0:T(8,128)(2,1)S(1)}, u32[]{:S(2)}, u32[]{:S(2)}) collective-permute-start(bf16[2,160,512]{2,1,0:T(8,128)(2,1)} %add_rows.10.refs_3_), channel_id=1, source_target_pairs={{0,4},{4,0},{8,12},{12,8},{1,5},{5,1},{9,13},{13,9},{2,6},{6,2},{1... | collective-permute-start | bytes 983048 | tf_op jit(solution)/shard_map/ppermute | solution.py:394
  61.3 29.6 %collective-permute-start.11 = (bf16[1,160,2048]{2,1,0:T(8,128)(2,1)}, bf16[1,160,2048]{2,1,0:T(8,128)(2,1)S(1)}, u32[]{:S(2)}, u32[]{:S(2)}) collective-permute-start(bf16[1,160,2048]{2,1,0:T(8,128)(2,1)} %add_rows.11.refs_3_.refs_2_), channel_id=1, source_target_pairs={{0,4},{4,0},{8,12},{12,8},{1,5},{5,1},{9,13},{13,9},{2,6},{6,2},{1... | collective-permute-start | bytes 1966088 | tf_op jit(solution)/shard_map/ppermute | solution.py:394
  72.6 35.3 %collective-permute-start.13 = (bf16[1,160,2048]{2,1,0:T(8,128)(2,1)}, bf16[1,160,2048]{2,1,0:T(8,128)(2,1)S(1)}, u32[]{:S(2)}, u32[]{:S(2)}) collective-permute-start(bf16[1,160,2048]{2,1,0:T(8,128)(2,1)} %add_rows.13.refs_4_), channel_id=1, source_target_pairs={{0,8},{4,12},{8,0},{12,4},{1,9},{5,13},{9,1},{13,5},{2,10},{6,14},... | collective-permute-start | bytes 1966088 | tf_op jit(solution)/shard_map/ppermute | solution.py:394
  75.2 1.1 copy-start.2
  83.4 26.5 %collective-permute-start.10 = (bf16[1,160,1024]{2,1,0:T(8,128)(2,1)}, bf16[1,160,1024]{2,1,0:T(8,128)(2,1)S(1)}, u32[]{:S(2)}, u32[]{:S(2)}) collective-permute-start(bf16[1,160,1024]{2,1,0:T(8,128)(2,1)} %get-tuple-element.37), channel_id=1, source_target_pairs={{0,1},{1,0},{2,3},{3,2},{4,5},{5,4},{6,7},{7,6},{8,9},{9,8},{10,11... | collective-permute-start | bytes 983048 | tf_op jit(solution)/shard_map/ppermute | solution.py:397
  83.4 7.5 %collective-permute-start.12 = (bf16[1,160,1024]{2,1,0:T(8,128)(2,1)}, bf16[1,160,1024]{2,1,0:T(8,128)(2,1)S(1)}, u32[]{:S(2)}, u32[]{:S(2)}) collective-permute-start(bf16[1,160,1024]{2,1,0:T(8,128)(2,1)} %get-tuple-element.38.refs_2_), channel_id=1, source_target_pairs={{0,1},{1,0},{2,3},{3,2},{4,5},{5,4},{6,7},{7,6},{8,9},{9,8},{10,11... | collective-permute-start | bytes 983048 | tf_op jit(solution)/shard_map/ppermute | solution.py:397
  84.0 29.7 %collective-permute-start.7 = (bf16[1,160,512]{2,1,0:T(8,128)(2,1)}, bf16[1,160,512]{2,1,0:T(8,128)(2,1)S(1)}, u32[]{:S(2)}, u32[]{:S(2)}) collective-permute-start(bf16[1,160,512]{2,1,0:T(8,128)(2,1)} %add_rows.12.refs_4_.refs_3_), channel_id=1, source_target_pairs={{0,8},{4,12},{8,0},{12,4},{1,9},{5,13},{9,1},{13,5},{2,10},{6,14},... | collective-permute-start | bytes 491528 | tf_op jit(solution)/shard_map/ppermute | solution.py:394
  86.4 4.4 %copy-start.16 = (bf16[1,160,2048]{2,1,0:T(8,128)(2,1)S(1)}, bf16[1,160,2048]{2,1,0:T(8,128)(2,1)}, u32[]{:S(2)}) copy-start(bf16[1,160,2048]{2,1,0:T(8,128)(2,1)} %get-tuple-element.42) | copy-start | bytes 1966084
  86.4 4.4 %copy-start.9 = (bf16[1,160,1024]{2,1,0:T(8,128)(2,1)S(1)}, bf16[1,160,1024]{2,1,0:T(8,128)(2,1)}, u32[]{:S(2)}) copy-start(bf16[1,160,1024]{2,1,0:T(8,128)(2,1)} %add_rows.14.refs_2_) | copy-start | bytes 983044
  90.8 32.2 %collective-permute-start.15 = (bf16[1,160,2048]{2,1,0:T(8,128)(2,1)S(1)}, bf16[1,160,2048]{2,1,0:T(8,128)(2,1)S(1)}, u32[]{:S(2)}, u32[]{:S(2)}) collective-permute-start(bf16[1,160,2048]{2,1,0:T(8,128)(2,1)S(1)} %copy-done.16), channel_id=1, source_target_pairs={{0,1},{1,0},{2,3},{3,2},{4,5},{5,4},{6,7},{7,6},{8,9},{9,8},{10,11... | collective-permute-start | bytes 1966088 | tf_op jit(solution)/shard_map/ppermute | solution.py:397
  90.9 45.1 %collective-permute-start.19 = (bf16[1,160,1024]{2,1,0:T(8,128)(2,1)S(1)}, bf16[1,160,1024]{2,1,0:T(8,128)(2,1)S(1)}, u32[]{:S(2)}, u32[]{:S(2)}) collective-permute-start(bf16[1,160,1024]{2,1,0:T(8,128)(2,1)S(1)} %copy-done.9), channel_id=1, source_target_pairs={{0,4},{4,0},{8,12},{12,8},{1,5},{5,1},{9,13},{13,9},{2,6},{6,2},{1... | collective-permute-start | bytes 983048 | tf_op jit(solution)/shard_map/ppermute | solution.py:394
  109.8 26.3 %collective-permute-start.20 = (bf16[1,160,1024]{2,1,0:T(8,128)(2,1)}, bf16[1,160,1024]{2,1,0:T(8,128)(2,1)S(1)}, u32[]{:S(2)}, u32[]{:S(2)}) collective-permute-start(bf16[1,160,1024]{2,1,0:T(8,128)(2,1)} %add_rows.16.refs_3_), channel_id=1, source_target_pairs={{0,8},{4,12},{8,0},{12,4},{1,9},{5,13},{9,1},{13,5},{2,10},{6,14},... | collective-permute-start | bytes 983048 | tf_op jit(solution)/shard_map/ppermute | solution.py:394
  113.7 1.0 copy-start
  115.8 7.2 %copy-start.1 = (bf16[1,160,1024]{2,1,0:T(8,128)(2,1)S(1)}, bf16[1,160,1024]{2,1,0:T(8,128)(2,1)}, u32[]{:S(2)}) copy-start(bf16[1,160,1024]{2,1,0:T(8,128)(2,1)} %add_rows.17.refs_4_.refs_2_) | copy-start | bytes 983044
  122.9 15.1 %collective-permute-start.21 = (bf16[1,160,1024]{2,1,0:T(8,128)(2,1)}, bf16[1,160,1024]{2,1,0:T(8,128)(2,1)S(1)}, u32[]{:S(2)}, u32[]{:S(2)}) collective-permute-start(bf16[1,160,1024]{2,1,0:T(8,128)(2,1)} %get-tuple-element.45), channel_id=1, source_target_pairs={{0,1},{1,0},{2,3},{3,2},{4,5},{5,4},{6,7},{7,6},{8,9},{9,8},{10,11... | collective-permute-start | bytes 983048 | tf_op jit(solution)/shard_map/ppermute | solution.py:397
  123.0 12.9 %copy-start.13 = (s32[640]{0:T(1024)S(1)}, s32[640]{0:T(1024)}, u32[]{:S(2)}) copy-start(s32[640]{0:T(1024)} %param.10) | copy-start | bytes 7684
  124.9 19.9 %copy-start.15 = (s32[2]{0:T(128)S(1)}, s32[2]{0:T(128)}, u32[]{:S(2)}) copy-start(s32[2]{0:T(128)} %get-tuple-element.57) | copy-start | bytes 28
  125.0 20.1 %copy-start.11 = (s32[320]{0:T(512)S(1)}, s32[320]{0:T(512)}, u32[]{:S(2)}) copy-start(s32[320]{0:T(512)} %copy-done.10) | copy-start | bytes 3844
  125.0 23.4 %collective-permute-start.22 = (bf16[160,2048]{1,0:T(8,128)(2,1)S(1)}, bf16[160,2048]{1,0:T(8,128)(2,1)S(1)}, u32[]{:S(2)}, u32[]{:S(2)}) collective-permute-start(bf16[160,2048]{1,0:T(8,128)(2,1)S(1)} %sum_and_rotate.3.refs_0_), channel_id=1, source_target_pairs={{0,1},{1,0},{2,3},{3,2},{4,5},{5,4},{6,7},{7,6},{8,9},{9,8},{10,11... | collective-permute-start | bytes 1966088 | tf_op jit(solution)/shard_map/ppermute | solution.py:397
  125.5 7.1 %collective-permute-start.25 = (bf16[1,320,128]{2,1,0:T(8,128)(2,1)S(1)}, bf16[1,320,128]{2,1,0:T(8,128)(2,1)S(1)}, u32[]{:S(2)}, u32[]{:S(2)}) collective-permute-start(bf16[1,320,128]{2,1,0:T(8,128)(2,1)S(1)} %get-tuple-element.49.refs_0_), channel_id=1, source_target_pairs={{0,4},{4,0},{8,12},{12,8},{1,5},{5,1},{9,13},{13,9},{2,6},{6,2},{1... | collective-permute-start | bytes 245768 | tf_op jit(solution)/shard_map/ppermute | solution.py:394
  132.6 12.5 %copy-start.3 = (bf16[2,320,128]{2,1,0:T(8,128)(2,1)}, bf16[2,320,128]{2,1,0:T(8,128)(2,1)S(1)}, u32[]{:S(2)}) copy-start(bf16[2,320,128]{2,1,0:T(8,128)(2,1)S(1)} %stack_slots.2.refs_0_) | copy-start | bytes 491524
  132.6 11.5 %collective-permute-start.26 = (bf16[2,320,128]{2,1,0:T(8,128)(2,1)S(1)}, bf16[2,320,128]{2,1,0:T(8,128)(2,1)S(1)}, u32[]{:S(2)}, u32[]{:S(2)}) collective-permute-start(bf16[2,320,128]{2,1,0:T(8,128)(2,1)S(1)} %stack_slots.2.refs_0_), channel_id=1, source_target_pairs={{0,8},{4,12},{8,0},{12,4},{1,9},{5,13},{9,1},{13,5},{2,10},{6,14},... | collective-permute-start | bytes 491528 | tf_op jit(solution)/shard_map/ppermute | solution.py:394
  136.0 3.5 %collective-permute-start.14 = (bf16[320,128]{1,0:T(8,128)(2,1)S(1)}, bf16[320,128]{1,0:T(8,128)(2,1)S(1)}, u32[]{:S(2)}, u32[]{:S(2)}) collective-permute-start(bf16[320,128]{1,0:T(8,128)(2,1)S(1)} %get-tuple-element.39.own_ref.refs_3_), channel_id=1, source_target_pairs={{0,1},{1,0},{2,3},{3,2},{4,5},{5,4},{6,7},{7,6},{8,9},{9,8},{10,11... | collective-permute-start | bytes 245768 | tf_op jit(solution)/shard_map/ppermute | solution.py:397
  136.1 20.2 %collective-permute-start.16 = (bf16[1,160,1024]{2,1,0:T(8,128)(2,1)}, bf16[1,160,1024]{2,1,0:T(8,128)(2,1)}, u32[]{:S(2)}, u32[]{:S(2)}) collective-permute-start(bf16[1,160,1024]{2,1,0:T(8,128)(2,1)} %add_rows.15.refs_3_), channel_id=1, source_target_pairs={{0,4},{4,0},{8,12},{12,8},{1,5},{5,1},{9,13},{13,9},{2,6},{6,2},{1... | collective-permute-start | bytes 983048 | tf_op jit(solution)/shard_map/ppermute | solution.py:394
  138.0 19.6 %collective-permute-start.17 = (bf16[1,160,1024]{2,1,0:T(8,128)(2,1)S(1)}, bf16[1,160,1024]{2,1,0:T(8,128)(2,1)}, u32[]{:S(2)}, u32[]{:S(2)}) collective-permute-start(bf16[1,160,1024]{2,1,0:T(8,128)(2,1)S(1)} %copy-done.1), channel_id=1, source_target_pairs={{0,8},{4,12},{8,0},{12,4},{1,9},{5,13},{9,1},{13,5},{2,10},{6,14},... | collective-permute-start | bytes 983048 | tf_op jit(solution)/shard_map/ppermute | solution.py:394
  139.5 0.6 copy-start.7
  140.1 17.5 %collective-permute-start.18 = (bf16[1,160,1024]{2,1,0:T(8,128)(2,1)}, bf16[1,160,1024]{2,1,0:T(8,128)(2,1)}, u32[]{:S(2)}, u32[]{:S(2)}) collective-permute-start(bf16[1,160,1024]{2,1,0:T(8,128)(2,1)} %get-tuple-element.44), channel_id=1, source_target_pairs={{0,1},{1,0},{2,3},{3,2},{4,5},{5,4},{6,7},{7,6},{8,9},{9,8},{10,11... | collective-permute-start | bytes 983048 | tf_op jit(solution)/shard_map/ppermute | solution.py:397
  144.2 0.7 copy-start.5
  144.8 4.1 %collective-permute-start.23 = (bf16[160,1024]{1,0:T(8,128)(2,1)S(1)}, bf16[160,1024]{1,0:T(8,128)(2,1)}, u32[]{:S(2)}, u32[]{:S(2)}) collective-permute-start(bf16[160,1024]{1,0:T(8,128)(2,1)S(1)} %sum_and_rotate.4.refs_1_), channel_id=1, source_target_pairs={{0,1},{1,0},{2,3},{3,2},{4,5},{5,4},{6,7},{7,6},{8,9},{9,8},{10,11... | collective-permute-start | bytes 983048 | tf_op jit(solution)/shard_map/ppermute | solution.py:397
  145.1 0.9 copy-start.8
  146.5 0.9 copy-start.4
  147.5 0.9 copy-start.6
  148.4 11.0 %collective-permute-start.27 = (bf16[4,320,128]{2,1,0:T(8,128)(2,1)S(1)}, bf16[4,320,128]{2,1,0:T(8,128)(2,1)S(1)}, u32[]{:S(2)}, u32[]{:S(2)}) collective-permute-start(bf16[4,320,128]{2,1,0:T(8,128)(2,1)S(1)} %stack_slots.3.own_ref), channel_id=1, source_target_pairs={{0,1},{1,0},{2,3},{3,2},{4,5},{5,4},{6,7},{7,6},{8,9},{9,8},{10,11... | collective-permute-start | bytes 983048 | tf_op jit(solution)/shard_map/ppermute | solution.py:397
  159.3 3.2 %collective-permute-start.24 = (bf16[160,1024]{1,0:T(8,128)(2,1)S(1)}, bf16[160,1024]{1,0:T(8,128)(2,1)S(1)}, u32[]{:S(2)}, u32[]{:S(2)}) collective-permute-start(bf16[160,1024]{1,0:T(8,128)(2,1)S(1)} %sum_and_rotate.5.refs_1_), channel_id=1, source_target_pairs={{0,1},{1,0},{2,3},{3,2},{4,5},{5,4},{6,7},{7,6},{8,9},{9,8},{10,11... | collective-permute-start | bytes 983048 | tf_op jit(solution)/shard_map/ppermute | solution.py:397

commit v9 on v7

--- a/solution.py
+++ b/solution.py
@@ -500,14 +500,14 @@
             pair = (pair_keep, other_core(give))
             after = (give,)
         odd_keep, odd_got, given = project(odd, [block], tile, after)
+        after = ()
+        if b > 0:
+            added, after = add_even(b - 1, 0, head_cols, (), (given,))
+            terms.append([(fars[b - 1], len(odd) - 1, 0, 0)] + added)
         count = len(odd) - 1 if b == last else len(odd)
-        odd_sent = add_rows(0, count, half, 0, odd_keep, odd_got, 0, head_cols, pair)
+        odd_sent = add_rows(0, count, half, 0, odd_keep, odd_got, 0, head_cols, pair, 0, (), after)
         fars.append(swap(odd_sent, 1))
-        after = (odd_sent,)
-        if b > 0:
-            added, after = add_even(b - 1, 0, head_cols, (), after)
-            terms.append([(fars[b - 1], len(odd) - 1, 0, 0)] + added)
-            after = (odd_sent,) + after
+        after = (odd_sent,) + after
         if b < last:
             keep, got, given = project(even + [0], [block], head_cols, after, LIGHT, True)
             evens.append((keep, got[:1] if len(even) == 1 else [jnp.concatenate(got[:-1])]))
@@ -563,7 +563,8 @@
     count = heads_here // split
     scores, mark = (), ()
     for p in range(split):
-        turned = rotate(last, p, split, parts[p], mark)
+        behind = mark or tuple(row[1] for row in rotated)
+        turned = rotate(last, p, split, parts[p], behind)
         queries = [(row[0], p * count) for row in rotated] + [(turned[0], 0)]
         queries += [(row[1], p * count) for row in rotated] + [(turned[1], 0)]
         *scores, mark = score_heads(
@@ -571,10 +572,8 @@
         )
         mark = (mark,)
         if fast_pair and p == 0:
-            bit = 1
-            while bit < shards:
-                held = stack_slots([held, swap(held, bit)], mark)
-                bit *= 2
+            held = stack_slots([held], mark)
+            held = stack_slots([held] + [swap(held, x) for x in range(1, shards)], ())
             values = order_values(findex, order, held, other_core(held))
     return (scores[0], values)
 

time: 164 us -> 170 us (1.037)
  waiting for transfers between devices: 38.5 us -> 45.9 us
    ppermute x9 -> x10, waiting for transfers between devices: 34.2 us -> 42.3 us  [swap(): return lax.ppermute(x, 'fsdp', [(i, i ^ bit) for i in range(shards)])]
    ppermute x9 -> x10, starting transfers between devices: 14 us -> 13.5 us  [swap(): return lax.ppermute(x, 'fsdp', [(i, i ^ bit) for i in range(shards)])]
  transfers between devices with their start and end apart: 26 -> 27, of which waited for: 10 -> 7; matrix products, arithmetic and copies ran while one was open for 2% -> 2% of each run, Pallas kernels for 58% -> 56%
where the time goes in v9:
time: 170 us; the launch traced here: 169 us
  Pallas kernels  96.7 us (57%)
  waiting for transfers between devices  45.9 us (27%)
  starting transfers between devices  20.1 us (12%)
  other arithmetic  2.55 us (1%)
  local copies, waits for them, and re-layouts  2.51 us (1%)
    pallas_call x5, Pallas kernels, project_query(): pl.pallas_call(functools.partial(query_kernel, count, pieces, by_slot), g...  49.3 us
    ppermute x10, waiting for transfers between devices, swap(): return lax.ppermute(x, 'fsdp', [(i, i ^ bit) for i in range(shards)])  42.3 us
    pallas_call x7, Pallas kernels, add_rows(): pl.pallas_call(functools.partial(add_kernel, len(gots), len(pair) // 2, l...  16.6 us
    pallas_call x2, Pallas kernels, score_heads(): pl.pallas_call(functools.partial(score_kernel, len(queries)), grid=(count...  14 us
    ppermute x10, starting transfers between devices, swap(): return lax.ppermute(x, 'fsdp', [(i, i ^ bit) for i in range(shards)])  13.5 us
    pallas_call x1, Pallas kernels, project_pair(): pl.pallas_call(functools.partial(pair_kernel, count), grid_spec=pltpu.Pre...  7.12 us
    pallas_call x3, Pallas kernels, sum_and_rotate(): pl.pallas_call(functools.partial(rotate_kernel, len(terms), len(gots)), g...  4.98 us
    ppermute x16, waiting for transfers between devices, other_core(): return lax.ppermute(x, 'rep', [(0, 1), (1, 0)])  3.61 us
  transfers between devices with their start and end apart: 27, of which 7 were waited for; matrix products, arithmetic and copies ran while one was open for 2% of the time, Pallas kernels for 56%

profile of v9, /device:TPU:0, one launch (start us, length us, event | category | flops | bytes accessed | tf_op | source)
XLA Modules:
  0.0 168.7 jit_solution(4758173042606000289)
XLA Ops:
  0.6 3.0 %collective-permute-start = (bf16[320,2048]{1,0:T(8,128)(2,1)}, bf16[320,2048]{1,0:T(8,128)(2,1)S(1)}, u32[]{:S(2)}, u32[]{:S(2)}) collective-permute-start(bf16[320,2048]{1,0:T(8,128)(2,1)} %refs_0_.5), channel_id=1, source_target_pairs={{0,2},{2,0},{1,3},{3,1},{4,6},{6,4},{5,7},{7,5},{8,10},{10,8},{9,1... | collective-permute-start | bytes 3932168 | tf_op jit(solution)/shard_map/ppermute | solution.py:452
  3.7 11.9 %query_products.5 = (f32[2,160,2048]{2,1,0:T(8,128)}, bf16[2,160,1024]{2,1,0:T(8,128)(2,1)}, bf16[2,160,1024]{2,1,0:T(8,128)(2,1)}) custom-call(s32[3]{0:T(128)S(1)} %pad_add_fusion.2.place_ref, bf16[320,2048]{1,0:T(8,128)(2,1)} %refs_0_.5, bf16[2048,8192]{1,0:T(8,128)(2,1)} %refs_1_.9), custom_call_target="tpu_custom_call" | custom-call | flops 1000 | bytes 1000 | tf_op jit(solution)/shard_map/query_products/pallas_call | solution.py:87
  15.6 0.5 collective-permute-start.2
  16.1 1.8 %collective-permute-done.1.refs_1_ = bf16[2,160,1024]{2,1,0:T(8,128)(2,1)S(1)} collective-permute-done((bf16[2,160,1024]{2,1,0:T(8,128)(2,1)}, bf16[2,160,1024]{2,1,0:T(8,128)(2,1)S(1)}, u32[]{:S(2)}, u32[]{:S(2)}) %collective-permute-start.1) | collective-permute-done | bytes 655392 | tf_op jit(solution)/shard_map/ppermute | solution.py:425
  17.9 0.9 collective-permute-done.2.refs_2_
  18.9 2.7 %add_rows.7.refs_2_ = bf16[2,160,2048]{2,1,0:T(8,128)(2,1)} custom-call(f32[2,160,2048]{2,1,0:T(8,128)} %get-tuple-element.26.refs_0_, bf16[2,160,1024]{2,1,0:T(8,128)(2,1)S(1)} %collective-permute-done.1.refs_1_, bf16[2,160,1024]{2,1,0:T(8,128)(2,1)S(1)} %collective-permute-done.2.refs_2_), custom_call_target="tpu_custom_call" | custom-call | flops 1000 | bytes 1000 | tf_op jit(solution)/shard_map/add_rows/pallas_call | solution.py:187
  21.6 1.6 collective-permute-start.7
  23.2 0.6 broadcast_add_fusion
  23.9 11.8 %query_products.6 = (f32[2,160,2048]{2,1,0:T(8,128)}, bf16[1,160,2048]{2,1,0:T(8,128)(2,1)}, bf16[1,160,2048]{2,1,0:T(8,128)(2,1)}) custom-call(s32[3]{0:T(128)S(1)} %pad_add_fusion.1.place_ref, bf16[320,2048]{1,0:T(8,128)(2,1)} %refs_0_.5, bf16[2048,8192]{1,0:T(8,128)(2,1)} %refs_1_.9, bf16[2,160,2048]{2,1,0:T(8,128)(2,1)} %add_rows.7.refs_2_), custom_call_target="tpu_custom_call" | custom-call | flops 1000 | bytes 1000 | tf_op jit(solution)/shard_map/query_products/pallas_call | solution.py:87
  35.7 7.1 %key_value_products.1 = (f32[4,160,512]{2,1,0:T(8,128)}, bf16[4,160,512]{2,1,0:T(8,128)(2,1)}) custom-call(s32[5]{0:T(128)S(1)} %stack.27.place_ref, bf16[320,2048]{1,0:T(8,128)(2,1)} %refs_0_.5, bf16[320,2048]{1,0:T(8,128)(2,1)S(1)} %collective-permute-done.refs_1_.refs_0_, bf16[2048,512]{1,0:T(8,128)(2,1)} %refs_2_.1, bf16[2048,512]{1,0:T(8,128)(2,1)} %refs_3_.1, ...), custom_call_target="tpu_custom_call" | custom-call | flops 1000 | bytes 1000 | tf_op jit(solution)/shard_map/key_value_products/pallas_call | solution.py:132
  42.8 0.6 collective-permute-start.3
  43.4 11.5 %query_products.7 = (f32[2,160,2048]{2,1,0:T(8,128)}, bf16[2,160,1024]{2,1,0:T(8,128)(2,1)}, bf16[2,160,1024]{2,1,0:T(8,128)(2,1)}) custom-call(s32[3]{0:T(128)S(1)} %pad_add_fusion.2.place_ref, bf16[320,2048]{1,0:T(8,128)(2,1)S(1)} %collective-permute-done.refs_1_.refs_0_, bf16[2048,8192]{1,0:T(8,128)(2,1)} %refs_1_.9, ...), custom_call_target="tpu_custom_call" | custom-call | flops 1000 | bytes 1000 | tf_op jit(solution)/shard_map/query_products/pallas_call | solution.py:87
  54.9 0.5 collective-permute-start.5
  55.6 0.2 select_reduce_fusion
  55.9 0.7 fusion.4
  56.7 3.0 %add_rows.8.refs_5_.refs_3_ = bf16[1,160,2048]{2,1,0:T(8,128)(2,1)} custom-call(f32[2,160,2048]{2,1,0:T(8,128)} %get-tuple-element.35.refs_0_, bf16[1,160,2048]{2,1,0:T(8,128)(2,1)} %collective-permute-done.6.refs_1_, bf16[2,160,2048]{2,1,0:T(8,128)(2,1)S(1)} %collective-permute-done.7.refs_2_.refs_1_, bf16[2,160,1024]{2,1,0:T(8,128)(2,1)} %get-tuple-element.33.refs_3_), custom_call_target="tpu_custom_call" | custom-call | flops 1000 | bytes 1000 | tf_op jit(solution)/shard_map/add_rows/pallas_call | solution.py:187
  59.7 2.6 %collective-permute-start.11 = (bf16[1,160,2048]{2,1,0:T(8,128)(2,1)}, bf16[1,160,2048]{2,1,0:T(8,128)(2,1)S(1)}, u32[]{:S(2)}, u32[]{:S(2)}) collective-permute-start(bf16[1,160,2048]{2,1,0:T(8,128)(2,1)} %add_rows.8.refs_5_.refs_3_), channel_id=1, source_target_pairs={{0,8},{4,12},{8,0},{12,4},{1,9},{5,13},{9,1},{13,5},{2,10},{6,14},... | collective-permute-start | bytes 1966088 | tf_op jit(solution)/shard_map/ppermute | solution.py:422
  62.3 2.7 %add_rows.9.refs_2_ = bf16[1,160,2560]{2,1,0:T(8,128)(2,1)} custom-call(f32[2,160,2048]{2,1,0:T(8,128)} %get-tuple-element.32.refs_0_, bf16[2,160,1024]{2,1,0:T(8,128)(2,1)} %collective-permute-done.4.refs_1_, bf16[2,160,1024]{2,1,0:T(8,128)(2,1)} %collective-permute-done.5.refs_2_.refs_1_, f32[4,160,512]{2,1,0:T(8,128)} %get-tuple-element.30.refs_3_.refs_2_.refs_0_, ...), custom_call_target="tpu_custom_call" | custom-call | flops 1000 | bytes 1000 | tf_op jit(solution)/shard_map/add_rows/pallas_call | solution.py:187
  65.0 0.5 collective-permute-start.10
  65.4 7.1 %query_products.8 = (f32[1,160,2048]{2,1,0:T(8,128)}, bf16[1,160,1024]{2,1,0:T(8,128)(2,1)}, bf16[1,160,1024]{2,1,0:T(8,128)(2,1)}) custom-call(s32[2]{0:T(128)S(1)} %pad_add_fusion.3.place_ref, bf16[320,2048]{1,0:T(8,128)(2,1)S(1)} %collective-permute-done.refs_1_.refs_0_, bf16[2048,8192]{1,0:T(8,128)(2,1)} %refs_1_.9, ...), custom_call_target="tpu_custom_call" | custom-call | flops 99999997952 | bytes 100000000 | tf_op jit(solution)/shard_map/query_products/pallas_call | solution.py:87
  72.5 0.5 collective-permute-start.13
  73.2 2.2 %add_rows.10.refs_2_ = bf16[1,160,1536]{2,1,0:T(8,128)(2,1)} custom-call(f32[2,160,2048]{2,1,0:T(8,128)} %get-tuple-element.32.refs_0_, bf16[2,160,1024]{2,1,0:T(8,128)(2,1)} %collective-permute-done.4.refs_1_, f32[4,160,512]{2,1,0:T(8,128)} %get-tuple-element.30.refs_3_.refs_2_.refs_0_, ...), custom_call_target="tpu_custom_call" | custom-call | flops 1000 | bytes 1000 | tf_op jit(solution)/shard_map/add_rows/pallas_call | solution.py:187
  75.5 2.0 %add_rows.11.refs_6_ = bf16[1,160,1024]{2,1,0:T(8,128)(2,1)} custom-call(f32[2,160,2048]{2,1,0:T(8,128)} %get-tuple-element.32.refs_0_, bf16[2,160,1024]{2,1,0:T(8,128)(2,1)} %collective-permute-done.5.refs_2_.refs_1_, bf16[1,160,1536]{2,1,0:T(8,128)(2,1)} %add_rows.10.refs_2_), custom_call_target="tpu_custom_call" | custom-call | flops 1000 | bytes 1000 | tf_op jit(solution)/shard_map/add_rows/pallas_call | solution.py:187
  77.4 1.6 collective-permute-start.8
  79.0 12.9 %collective-permute-done.11.refs_7_.refs_2_ = bf16[1,160,2048]{2,1,0:T(8,128)(2,1)S(1)} collective-permute-done((bf16[1,160,2048]{2,1,0:T(8,128)(2,1)}, bf16[1,160,2048]{2,1,0:T(8,128)(2,1)S(1)}, u32[]{:S(2)}, u32[]{:S(2)}) %collective-permute-start.11) | collective-permute-done | bytes 655392 | tf_op jit(solution)/shard_map/ppermute | solution.py:422
  91.9 8.3 %collective-permute-done.10.refs_4_.refs_5_.refs_2_ = bf16[1,160,2560]{2,1,0:T(8,128)(2,1)S(1)} collective-permute-done((bf16[1,160,2560]{2,1,0:T(8,128)(2,1)}, bf16[1,160,2560]{2,1,0:T(8,128)(2,1)S(1)}, u32[]{:S(2)}, u32[]{:S(2)}) %collective-permute-start.10) | collective-permute-done | bytes 819232 | tf_op jit(solution)/shard_map/ppermute | solution.py:422
  100.2 2.1 %add_rows.12.refs_3_ = bf16[1,160,1536]{2,1,0:T(8,128)(2,1)} custom-call(f32[1,160,2048]{2,1,0:T(8,128)} %get-tuple-element.37.refs_0_, bf16[1,160,1024]{2,1,0:T(8,128)(2,1)S(1)} %collective-permute-done.9.refs_1_, f32[4,160,512]{2,1,0:T(8,128)} %get-tuple-element.30.refs_3_.refs_2_.refs_0_, ...), custom_call_target="tpu_custom_call" | custom-call | flops 1000 | bytes 1000 | tf_op jit(solution)/shard_map/add_rows/pallas_call | solution.py:187
  102.3 2.0 %add_rows.13.refs_4_.refs_2_ = bf16[1,160,1024]{2,1,0:T(8,128)(2,1)} custom-call(f32[1,160,2048]{2,1,0:T(8,128)} %get-tuple-element.37.refs_0_, bf16[1,160,1024]{2,1,0:T(8,128)(2,1)S(1)} %collective-permute-done.13.refs_1_, bf16[1,160,2560]{2,1,0:T(8,128)(2,1)S(1)} %collective-permute-done.10.refs_4_.refs_5_.refs_2_, bf16[1,160,1536]{2,1,0:T(8,128)(2,1)} %add_rows.12.refs_3_), custom_call_target="tpu_custom_call" | custom-call | flops 1000 | bytes 1000 | tf_op jit(solution)/shard_map/add_rows/pallas_call | solution.py:187
  104.3 1.9 %sum_and_rotate.3.refs_0_ = bf16[160,2048]{1,0:T(8,128)(2,1)S(1)} custom-call(f32[160,128]{1,0:T(8,128)S(1)} %get-tuple-element.53.cos_ref, f32[160,128]{1,0:T(8,128)S(1)} %get-tuple-element.51.sin_ref, f32[2,160,2048]{2,1,0:T(8,128)} %get-tuple-element.35.refs_0_, bf16[2,160,2048]{2,1,0:T(8,128)(2,1)S(1)} %copy-done.1, ...), custom_call_target="tpu_custom_call" | custom-call | flops 1000 | bytes 1000 | tf_op jit(solution)/shard_map/sum_and_rotate/pallas_call | solution.py:243
  106.3 7.0 %query_products.9 = (f32[1,160,2048]{2,1,0:T(8,128)}, bf16[1,160,1024]{2,1,0:T(8,128)(2,1)}, bf16[1,160,1024]{2,1,0:T(8,128)(2,1)}) custom-call(s32[2]{0:T(128)S(1)} %pad_add_fusion.4.place_ref, bf16[320,2048]{1,0:T(8,128)(2,1)S(1)} %collective-permute-done.refs_1_.refs_0_, bf16[2048,8192]{1,0:T(8,128)(2,1)} %refs_1_.9, ...), custom_call_target="tpu_custom_call" | custom-call | flops 99999997952 | bytes 100000000 | tf_op jit(solution)/shard_map/query_products/pallas_call | solution.py:87
  113.3 0.5 collective-permute-start.19
  113.9 2.9 %collective-permute-start.17 = (bf16[1,160,1024]{2,1,0:T(8,128)(2,1)}, bf16[1,160,1024]{2,1,0:T(8,128)(2,1)}, u32[]{:S(2)}, u32[]{:S(2)}) collective-permute-start(bf16[1,160,1024]{2,1,0:T(8,128)(2,1)} %add_rows.13.refs_4_.refs_2_), channel_id=1, source_target_pairs={{0,8},{4,12},{8,0},{12,4},{1,9},{5,13},{9,1},{13,5},{2,10},{6,14},... | collective-permute-start | bytes 983048 | tf_op jit(solution)/shard_map/ppermute | solution.py:422
  116.8 17.4 %collective-permute-done.12.refs_3_.refs_2_ = bf16[1,160,1536]{2,1,0:T(8,128)(2,1)S(1)} collective-permute-done((bf16[1,160,1536]{2,1,0:T(8,128)(2,1)}, bf16[1,160,1536]{2,1,0:T(8,128)(2,1)S(1)}, u32[]{:S(2)}, u32[]{:S(2)}) %collective-permute-start.12) | collective-permute-done | bytes 491552 | tf_op jit(solution)/shard_map/ppermute | solution.py:422
  134.2 1.5 sum_and_rotate.4.refs_1_
  136.0 0.1 reshape.81.canary_ref
  136.3 1.0 copy-done.4
  137.4 1.0 copy-done.6
  138.4 1.1 split_and_rotate.1
  139.5 0.6 collective-permute-start.14
  140.2 0.8 collective-permute-done.14.other_ref
  141.0 0.6 order_and_keys.1
  141.6 7.4 %score_heads.2 = (bf16[1,16,640,640]{3,2,1,0:T(8,128)(2,1)}, f32[8,128]{1,0:T(8,128)S(1)}) custom-call(bf16[640,640]{1,0:T(8,128)(2,1)S(1)} %get-tuple-element.40.order_ref, bf16[128,640]{1,0:T(8,128)(2,1)S(1)} %get-tuple-element.41.key_t_ref, bf16[160,2048]{1,0:T(8,128)(2,1)S(1)} %sum_and_rotate.3.refs_0_, bf16[160,1024]{1,0:T(8,128)(2,1)S(1)} %sum_and_rotate.4.refs_1_, ...), custom_call_target="tpu_custom_call" | custom-call | flops 1000 | bytes 1000 | tf_op jit(solution)/shard_map/score_heads/pallas_call | solution.py:383
  149.0 0.7 collective-permute-start.24
  149.8 3.7 %collective-permute-start.25 = (bf16[1,320,128]{2,1,0:T(8,128)(2,1)S(1)}, bf16[1,320,128]{2,1,0:T(8,128)(2,1)S(1)}, u32[]{:S(2)}, u32[]{:S(2)}) collective-permute-start(bf16[1,320,128]{2,1,0:T(8,128)(2,1)S(1)} %stack_slots.2.refs_0_), channel_id=1, source_target_pairs={{0,12},{4,8},{8,4},{12,0},{1,13},{5,9},{9,5},{13,1},{2,14},{6,10},... | collective-permute-start | bytes 245768 | tf_op jit(solution)/shard_map/ppermute | solution.py:422
  153.4 1.6 sum_and_rotate.5.refs_1_
  155.1 3.7 %collective-permute-done.24.refs_2_ = bf16[1,320,128]{2,1,0:T(8,128)(2,1)S(1)} collective-permute-done((bf16[1,320,128]{2,1,0:T(8,128)(2,1)S(1)}, bf16[1,320,128]{2,1,0:T(8,128)(2,1)S(1)}, u32[]{:S(2)}, u32[]{:S(2)}) %collective-permute-start.24) | collective-permute-done | bytes 81952 | tf_op jit(solution)/shard_map/ppermute | solution.py:422
  159.0 6.6 %score_heads.3 = (bf16[1,16,640,640]{3,2,1,0:T(8,128)(2,1)}, f32[8,128]{1,0:T(8,128)}) custom-call(bf16[640,640]{1,0:T(8,128)(2,1)S(1)} %get-tuple-element.40.order_ref, bf16[128,640]{1,0:T(8,128)(2,1)S(1)} %get-tuple-element.41.key_t_ref, bf16[160,2048]{1,0:T(8,128)(2,1)S(1)} %sum_and_rotate.3.refs_0_, ...), custom_call_target="tpu_custom_call", output_to_operand_aliasing={{0}: (6, {})} | custom-call | flops 1000 | bytes 1000 | tf_op jit(solution)/shard_map/score_heads/pallas_call | solution.py:383
  165.6 3.1 %order_values.1 = bf16[640,512]{1,0:T(8,128)(2,1)} custom-call(s32[4]{0:T(128)S(1)} %pad_add_fusion.5.place_ref, bf16[640,640]{1,0:T(8,128)(2,1)S(1)} %get-tuple-element.40.order_ref, bf16[4,320,128]{2,1,0:T(8,128)(2,1)S(1)} %stack_slots.3.own_ref, bf16[4,320,128]{2,1,0:T(8,128)(2,1)S(1)} %collective-permute-done.26.other_ref), custom_call_target="tpu_custom_call" | custom-call | tf_op jit(solution)/shard_map/order_values/pallas_call | solution.py:350
  (79 shorter events, 1.9 us)
Async XLA Ops:
  0.6 35.0 %collective-permute-start = (bf16[320,2048]{1,0:T(8,128)(2,1)}, bf16[320,2048]{1,0:T(8,128)(2,1)S(1)}, u32[]{:S(2)}, u32[]{:S(2)}) collective-permute-start(bf16[320,2048]{1,0:T(8,128)(2,1)} %refs_0_.5), channel_id=1, source_target_pairs={{0,2},{2,0},{1,3},{3,1},{4,6},{6,4},{5,7},{7,5},{8,10},{10,8},{9,1... | collective-permute-start | bytes 3932168 | tf_op jit(solution)/shard_map/ppermute | solution.py:452
  15.6 2.3 %collective-permute-start.1 = (bf16[2,160,1024]{2,1,0:T(8,128)(2,1)}, bf16[2,160,1024]{2,1,0:T(8,128)(2,1)S(1)}, u32[]{:S(2)}, u32[]{:S(2)}) collective-permute-start(bf16[2,160,1024]{2,1,0:T(8,128)(2,1)} %get-tuple-element.27), channel_id=1, source_target_pairs={{0,1},{1,0},{2,3},{3,2},{4,5},{5,4},{6,7},{7,6},{8,9},{9,8},{10,11... | collective-permute-start | bytes 1966088 | tf_op jit(solution)/shard_map/ppermute | solution.py:425
  15.6 3.2 %collective-permute-start.2 = (bf16[2,160,1024]{2,1,0:T(8,128)(2,1)}, bf16[2,160,1024]{2,1,0:T(8,128)(2,1)S(1)}, u32[]{:S(2)}, u32[]{:S(2)}) collective-permute-start(bf16[2,160,1024]{2,1,0:T(8,128)(2,1)} %get-tuple-element.28), channel_id=1, source_target_pairs={{0,1},{1,0},{2,3},{3,2},{4,5},{5,4},{6,7},{7,6},{8,9},{9,8},{10,11... | collective-permute-start | bytes 1966088 | tf_op jit(solution)/shard_map/ppermute | solution.py:425
  21.6 35.1 %collective-permute-start.7 = (bf16[2,160,2048]{2,1,0:T(8,128)(2,1)}, bf16[2,160,2048]{2,1,0:T(8,128)(2,1)S(1)}, u32[]{:S(2)}, u32[]{:S(2)}) collective-permute-start(bf16[2,160,2048]{2,1,0:T(8,128)(2,1)} %add_rows.7.refs_2_), channel_id=1, source_target_pairs={{0,4},{4,0},{8,12},{12,8},{1,5},{5,1},{9,13},{13,9},{2,6},{6,2},{1... | collective-permute-start | bytes 3932168 | tf_op jit(solution)/shard_map/ppermute | solution.py:422
  35.7 20.9 %collective-permute-start.6 = (bf16[1,160,2048]{2,1,0:T(8,128)(2,1)}, bf16[1,160,2048]{2,1,0:T(8,128)(2,1)}, u32[]{:S(2)}, u32[]{:S(2)}) collective-permute-start(bf16[1,160,2048]{2,1,0:T(8,128)(2,1)} %get-tuple-element.29.refs_4_), channel_id=1, source_target_pairs={{0,1},{1,0},{2,3},{3,2},{4,5},{5,4},{6,7},{7,6},{8,9},{9,8},{10,11... | collective-permute-start | bytes 1966088 | tf_op jit(solution)/shard_map/ppermute | solution.py:425
  42.8 12.8 %copy-start.10 = (s32[640]{0:T(1024)S(1)}, s32[640]{0:T(1024)}, u32[]{:S(2)}) copy-start(s32[640]{0:T(1024)} %param.10) | copy-start | bytes 7684
  42.8 12.8 %copy-start.12 = (s32[640]{0:T(1024)S(1)}, s32[640]{0:T(1024)}, u32[]{:S(2)}) copy-start(s32[640]{0:T(1024)} %param.11) | copy-start | bytes 7684
  42.8 19.5 %collective-permute-start.3 = (bf16[4,160,512]{2,1,0:T(8,128)(2,1)}, bf16[4,160,512]{2,1,0:T(8,128)(2,1)S(1)}, u32[]{:S(2)}, u32[]{:S(2)}) collective-permute-start(bf16[4,160,512]{2,1,0:T(8,128)(2,1)} %get-tuple-element.31.refs_2_), channel_id=1, source_target_pairs={{0,1},{1,0},{2,3},{3,2},{4,5},{5,4},{6,7},{7,6},{8,9},{9,8},{10,11... | collective-permute-start | bytes 1966088 | tf_op jit(solution)/shard_map/ppermute | solution.py:425
  54.9 7.4 %collective-permute-start.4 = (bf16[2,160,1024]{2,1,0:T(8,128)(2,1)}, bf16[2,160,1024]{2,1,0:T(8,128)(2,1)}, u32[]{:S(2)}, u32[]{:S(2)}) collective-permute-start(bf16[2,160,1024]{2,1,0:T(8,128)(2,1)} %get-tuple-element.33.refs_3_), channel_id=1, source_target_pairs={{0,1},{1,0},{2,3},{3,2},{4,5},{5,4},{6,7},{7,6},{8,9},{9,8},{10,11... | collective-permute-start | bytes 1966088 | tf_op jit(solution)/shard_map/ppermute | solution.py:425
  54.9 7.4 %collective-permute-start.5 = (bf16[2,160,1024]{2,1,0:T(8,128)(2,1)}, bf16[2,160,1024]{2,1,0:T(8,128)(2,1)}, u32[]{:S(2)}, u32[]{:S(2)}) collective-permute-start(bf16[2,160,1024]{2,1,0:T(8,128)(2,1)} %get-tuple-element.34), channel_id=1, source_target_pairs={{0,1},{1,0},{2,3},{3,2},{4,5},{5,4},{6,7},{7,6},{8,9},{9,8},{10,11... | collective-permute-start | bytes 1966088 | tf_op jit(solution)/shard_map/ppermute | solution.py:425
  55.6 4.1 %copy-start.8 = (s32[320]{0:T(512)}, s32[320]{0:T(512)S(1)}, u32[]{:S(2)}) copy-start(s32[320]{0:T(512)S(1)} %add.106) | copy-start | bytes 3844
  56.6 47.7 %collective-permute-start.15 = (bf16[1,160,2048]{2,1,0:T(8,128)(2,1)}, bf16[1,160,2048]{2,1,0:T(8,128)(2,1)S(1)}, u32[]{:S(2)}, u32[]{:S(2)}) collective-permute-start(bf16[1,160,2048]{2,1,0:T(8,128)(2,1)} %get-tuple-element.42), channel_id=1, source_target_pairs={{0,1},{1,0},{2,3},{3,2},{4,5},{5,4},{6,7},{7,6},{8,9},{9,8},{10,11... | collective-permute-start | bytes 1966088 | tf_op jit(solution)/shard_map/ppermute | solution.py:425
  56.7 3.0 %copy-start = (bf16[2,160,2048]{2,1,0:T(8,128)(2,1)}, bf16[2,160,2048]{2,1,0:T(8,128)(2,1)S(1)}, u32[]{:S(2)}) copy-start(bf16[2,160,2048]{2,1,0:T(8,128)(2,1)S(1)} %collective-permute-done.7.refs_2_.refs_1_) | copy-start | bytes 3932164
  59.7 32.3 %collective-permute-start.11 = (bf16[1,160,2048]{2,1,0:T(8,128)(2,1)}, bf16[1,160,2048]{2,1,0:T(8,128)(2,1)S(1)}, u32[]{:S(2)}, u32[]{:S(2)}) collective-permute-start(bf16[1,160,2048]{2,1,0:T(8,128)(2,1)} %add_rows.8.refs_5_.refs_3_), channel_id=1, source_target_pairs={{0,8},{4,12},{8,0},{12,4},{1,9},{5,13},{9,1},{13,5},{2,10},{6,14},... | collective-permute-start | bytes 1966088 | tf_op jit(solution)/shard_map/ppermute | solution.py:422
  62.3 3.1 %copy-start.2 = (bf16[1,160,2048]{2,1,0:T(8,128)(2,1)S(1)}, bf16[1,160,2048]{2,1,0:T(8,128)(2,1)}, u32[]{:S(2)}) copy-start(bf16[1,160,2048]{2,1,0:T(8,128)(2,1)} %add_rows.8.refs_5_.refs_3_) | copy-start | bytes 1966084
  65.0 35.2 %collective-permute-start.10 = (bf16[1,160,2560]{2,1,0:T(8,128)(2,1)}, bf16[1,160,2560]{2,1,0:T(8,128)(2,1)S(1)}, u32[]{:S(2)}, u32[]{:S(2)}) collective-permute-start(bf16[1,160,2560]{2,1,0:T(8,128)(2,1)} %add_rows.9.refs_2_), channel_id=1, source_target_pairs={{0,4},{4,0},{8,12},{12,8},{1,5},{5,1},{9,13},{13,9},{2,6},{6,2},{1... | collective-permute-start | bytes 2457608 | tf_op jit(solution)/shard_map/ppermute | solution.py:422
  72.5 5.0 %collective-permute-start.9 = (bf16[1,160,1024]{2,1,0:T(8,128)(2,1)}, bf16[1,160,1024]{2,1,0:T(8,128)(2,1)S(1)}, u32[]{:S(2)}, u32[]{:S(2)}) collective-permute-start(bf16[1,160,1024]{2,1,0:T(8,128)(2,1)} %get-tuple-element.36.refs_4_), channel_id=1, source_target_pairs={{0,1},{1,0},{2,3},{3,2},{4,5},{5,4},{6,7},{7,6},{8,9},{9,8},{10,11... | collective-permute-start | bytes 983048 | tf_op jit(solution)/shard_map/ppermute | solution.py:425
  72.5 29.8 %collective-permute-start.13 = (bf16[1,160,1024]{2,1,0:T(8,128)(2,1)}, bf16[1,160,1024]{2,1,0:T(8,128)(2,1)S(1)}, u32[]{:S(2)}, u32[]{:S(2)}) collective-permute-start(bf16[1,160,1024]{2,1,0:T(8,128)(2,1)} %get-tuple-element.38), channel_id=1, source_target_pairs={{0,1},{1,0},{2,3},{3,2},{4,5},{5,4},{6,7},{7,6},{8,9},{9,8},{10,11... | collective-permute-start | bytes 983048 | tf_op jit(solution)/shard_map/ppermute | solution.py:425
  75.4 2.1 %copy-start.7 = (bf16[1,160,1536]{2,1,0:T(8,128)(2,1)S(1)}, bf16[1,160,1536]{2,1,0:T(8,128)(2,1)}, u32[]{:S(2)}) copy-start(bf16[1,160,1536]{2,1,0:T(8,128)(2,1)} %add_rows.10.refs_2_) | copy-start | bytes 1474564
  77.4 36.5 %collective-permute-start.8 = (bf16[1,160,1536]{2,1,0:T(8,128)(2,1)S(1)}, bf16[1,160,1536]{2,1,0:T(8,128)(2,1)S(1)}, u32[]{:S(2)}, u32[]{:S(2)}) collective-permute-start(bf16[1,160,1536]{2,1,0:T(8,128)(2,1)S(1)} %copy-done.7), channel_id=1, source_target_pairs={{0,4},{4,0},{8,12},{12,8},{1,5},{5,1},{9,13},{13,9},{2,6},{6,2},{1... | collective-permute-start | bytes 1474568 | tf_op jit(solution)/shard_map/ppermute | solution.py:422
  102.3 2.0 %copy-start.1 = (bf16[2,160,2048]{2,1,0:T(8,128)(2,1)S(1)}, bf16[2,160,2048]{2,1,0:T(8,128)(2,1)}, u32[]{:S(2)}) copy-start(bf16[2,160,2048]{2,1,0:T(8,128)(2,1)} %copy-done) | copy-start | bytes 3932164
  102.3 31.9 %collective-permute-start.12 = (bf16[1,160,1536]{2,1,0:T(8,128)(2,1)}, bf16[1,160,1536]{2,1,0:T(8,128)(2,1)S(1)}, u32[]{:S(2)}, u32[]{:S(2)}) collective-permute-start(bf16[1,160,1536]{2,1,0:T(8,128)(2,1)} %add_rows.12.refs_3_), channel_id=1, source_target_pairs={{0,8},{4,12},{8,0},{12,4},{1,9},{5,13},{9,1},{13,5},{2,10},{6,14},... | collective-permute-start | bytes 1474568 | tf_op jit(solution)/shard_map/ppermute | solution.py:422
  106.2 7.6 %copy-start.13 = (s32[2]{0:T(128)S(1)}, s32[2]{0:T(128)}, u32[]{:S(2)}) copy-start(s32[2]{0:T(128)} %get-tuple-element.57) | copy-start | bytes 28
  106.2 28.0 %collective-permute-start.20 = (bf16[160,2048]{1,0:T(8,128)(2,1)S(1)}, bf16[160,2048]{1,0:T(8,128)(2,1)S(1)}, u32[]{:S(2)}, u32[]{:S(2)}) collective-permute-start(bf16[160,2048]{1,0:T(8,128)(2,1)S(1)} %sum_and_rotate.3.refs_0_), channel_id=1, source_target_pairs={{0,1},{1,0},{2,3},{3,2},{4,5},{5,4},{6,7},{7,6},{8,9},{9,8},{10,11... | collective-permute-start | bytes 1966088 | tf_op jit(solution)/shard_map/ppermute | solution.py:425
  113.3 22.6 %copy-start.11 = (s32[640]{0:T(1024)S(1)}, s32[640]{0:T(1024)}, u32[]{:S(2)}) copy-start(s32[640]{0:T(1024)} %param.10) | copy-start | bytes 7684
  113.3 3.5 %collective-permute-start.19 = (bf16[1,160,1024]{2,1,0:T(8,128)(2,1)}, bf16[1,160,1024]{2,1,0:T(8,128)(2,1)S(1)}, u32[]{:S(2)}, u32[]{:S(2)}) collective-permute-start(bf16[1,160,1024]{2,1,0:T(8,128)(2,1)} %get-tuple-element.45), channel_id=1, source_target_pairs={{0,1},{1,0},{2,3},{3,2},{4,5},{5,4},{6,7},{7,6},{8,9},{9,8},{10,11... | collective-permute-start | bytes 983048 | tf_op jit(solution)/shard_map/ppermute | solution.py:425
  113.9 35.9 %collective-permute-start.16 = (bf16[1,160,1024]{2,1,0:T(8,128)(2,1)}, bf16[1,160,1024]{2,1,0:T(8,128)(2,1)S(1)}, u32[]{:S(2)}, u32[]{:S(2)}) collective-permute-start(bf16[1,160,1024]{2,1,0:T(8,128)(2,1)} %add_rows.11.refs_6_), channel_id=1, source_target_pairs={{0,4},{4,0},{8,12},{12,8},{1,5},{5,1},{9,13},{13,9},{2,6},{6,2},{1... | collective-permute-start | bytes 983048 | tf_op jit(solution)/shard_map/ppermute | solution.py:422
  113.9 22.2 %copy-start.3 = (bf16[1,160,1536]{2,1,0:T(8,128)(2,1)}, bf16[1,160,1536]{2,1,0:T(8,128)(2,1)S(1)}, u32[]{:S(2)}) copy-start(bf16[1,160,1536]{2,1,0:T(8,128)(2,1)S(1)} %collective-permute-done.8.refs_2_.refs_1_) | copy-start | bytes 1474564
  113.9 39.5 %collective-permute-start.17 = (bf16[1,160,1024]{2,1,0:T(8,128)(2,1)}, bf16[1,160,1024]{2,1,0:T(8,128)(2,1)}, u32[]{:S(2)}, u32[]{:S(2)}) collective-permute-start(bf16[1,160,1024]{2,1,0:T(8,128)(2,1)} %add_rows.13.refs_4_.refs_2_), channel_id=1, source_target_pairs={{0,8},{4,12},{8,0},{12,4},{1,9},{5,13},{9,1},{13,5},{2,10},{6,14},... | collective-permute-start | bytes 983048 | tf_op jit(solution)/shard_map/ppermute | solution.py:422
  116.8 36.6 %collective-permute-start.18 = (bf16[1,160,1024]{2,1,0:T(8,128)(2,1)}, bf16[1,160,1024]{2,1,0:T(8,128)(2,1)}, u32[]{:S(2)}, u32[]{:S(2)}) collective-permute-start(bf16[1,160,1024]{2,1,0:T(8,128)(2,1)} %get-tuple-element.44), channel_id=1, source_target_pairs={{0,1},{1,0},{2,3},{3,2},{4,5},{5,4},{6,7},{7,6},{8,9},{9,8},{10,11... | collective-permute-start | bytes 983048 | tf_op jit(solution)/shard_map/ppermute | solution.py:425
  134.2 1.9 %copy-start.5 = (bf16[1,160,1536]{2,1,0:T(8,128)(2,1)}, bf16[1,160,1536]{2,1,0:T(8,128)(2,1)S(1)}, u32[]{:S(2)}) copy-start(bf16[1,160,1536]{2,1,0:T(8,128)(2,1)S(1)} %collective-permute-done.12.refs_3_.refs_2_) | copy-start | bytes 1474564
  135.8 5.8 %collective-permute-start.21 = (bf16[160,1024]{1,0:T(8,128)(2,1)S(1)}, bf16[160,1024]{1,0:T(8,128)(2,1)}, u32[]{:S(2)}, u32[]{:S(2)}) collective-permute-start(bf16[160,1024]{1,0:T(8,128)(2,1)S(1)} %sum_and_rotate.4.refs_1_), channel_id=1, source_target_pairs={{0,1},{1,0},{2,3},{3,2},{4,5},{5,4},{6,7},{7,6},{8,9},{9,8},{10,11... | collective-permute-start | bytes 983048 | tf_op jit(solution)/shard_map/ppermute | solution.py:425
  136.1 3.9 %copy-start.9 = (s32[320]{0:T(512)S(1)}, s32[320]{0:T(512)}, u32[]{:S(2)}) copy-start(s32[320]{0:T(512)} %copy-done.8) | copy-start | bytes 3844
  136.3 1.0 copy-start.4
  137.4 1.0 copy-start.6
  139.5 1.5 collective-permute-start.14
  149.0 6.1 %collective-permute-start.23 = (bf16[1,320,128]{2,1,0:T(8,128)(2,1)S(1)}, bf16[1,320,128]{2,1,0:T(8,128)(2,1)S(1)}, u32[]{:S(2)}, u32[]{:S(2)}) collective-permute-start(bf16[1,320,128]{2,1,0:T(8,128)(2,1)S(1)} %stack_slots.2.refs_0_), channel_id=1, source_target_pairs={{0,4},{4,0},{8,12},{12,8},{1,5},{5,1},{9,13},{13,9},{2,6},{6,2},{1... | collective-permute-start | bytes 245768 | tf_op jit(solution)/shard_map/ppermute | solution.py:422
  149.0 9.8 %collective-permute-start.24 = (bf16[1,320,128]{2,1,0:T(8,128)(2,1)S(1)}, bf16[1,320,128]{2,1,0:T(8,128)(2,1)S(1)}, u32[]{:S(2)}, u32[]{:S(2)}) collective-permute-start(bf16[1,320,128]{2,1,0:T(8,128)(2,1)S(1)} %stack_slots.2.refs_0_), channel_id=1, source_target_pairs={{0,8},{4,12},{8,0},{12,4},{1,9},{5,13},{9,1},{13,5},{2,10},{6,14},... | collective-permute-start | bytes 245768 | tf_op jit(solution)/shard_map/ppermute | solution.py:422
  149.8 9.1 %collective-permute-start.25 = (bf16[1,320,128]{2,1,0:T(8,128)(2,1)S(1)}, bf16[1,320,128]{2,1,0:T(8,128)(2,1)S(1)}, u32[]{:S(2)}, u32[]{:S(2)}) collective-permute-start(bf16[1,320,128]{2,1,0:T(8,128)(2,1)S(1)} %stack_slots.2.refs_0_), channel_id=1, source_target_pairs={{0,12},{4,8},{8,4},{12,0},{1,13},{5,9},{9,5},{13,1},{2,14},{6,10},... | collective-permute-start | bytes 245768 | tf_op jit(solution)/shard_map/ppermute | solution.py:422
  155.0 4.0 %collective-permute-start.22 = (bf16[160,1024]{1,0:T(8,128)(2,1)S(1)}, bf16[160,1024]{1,0:T(8,128)(2,1)S(1)}, u32[]{:S(2)}, u32[]{:S(2)}) collective-permute-start(bf16[160,1024]{1,0:T(8,128)(2,1)S(1)} %sum_and_rotate.5.refs_1_), channel_id=1, source_target_pairs={{0,1},{1,0},{2,3},{3,2},{4,5},{5,4},{6,7},{7,6},{8,9},{9,8},{10,11... | collective-permute-start | bytes 983048 | tf_op jit(solution)/shard_map/ppermute | solution.py:425
  158.9 6.8 %collective-permute-start.26 = (bf16[4,320,128]{2,1,0:T(8,128)(2,1)S(1)}, bf16[4,320,128]{2,1,0:T(8,128)(2,1)S(1)}, u32[]{:S(2)}, u32[]{:S(2)}) collective-permute-start(bf16[4,320,128]{2,1,0:T(8,128)(2,1)S(1)} %stack_slots.3.own_ref), channel_id=1, source_target_pairs={{0,1},{1,0},{2,3},{3,2},{4,5},{5,4},{6,7},{7,6},{8,9},{9,8},{10,11... | collective-permute-start | bytes 983048 | tf_op jit(solution)/shard_map/ppermute | solution.py:425

commit v10 on v7

--- a/solution.py
+++ b/solution.py
@@ -563,18 +563,16 @@
     count = heads_here // split
     scores, mark = (), ()
     for p in range(split):
-        turned = rotate(last, p, split, parts[p], mark)
+        turned = rotate(last, p, split, parts[p], mark or tuple(owns[last][2][1:]))
         queries = [(row[0], p * count) for row in rotated] + [(turned[0], 0)]
         queries += [(row[1], p * count) for row in rotated] + [(turned[1], 0)]
+        behind = in_hbm([values]) if p == split - 1 and p > 0 else ()
         *scores, mark = score_heads(
-            order, key_t, heads_here, p * count, count, queries, scores
+            order, key_t, heads_here, p * count, count, queries, scores, behind
         )
         mark = (mark,)
         if fast_pair and p == 0:
-            bit = 1
-            while bit < shards:
-                held = stack_slots([held, swap(held, bit)], mark)
-                bit *= 2
+            held = stack_slots([held] + [swap(held, x) for x in range(1, shards)], mark)
             values = order_values(findex, order, held, other_core(held))
     return (scores[0], values)
 

time: 164 us -> 163 us (level)
  waiting for transfers between devices: 38.5 us -> 34.9 us
  local copies, waits for them, and re-layouts: 3.42 us -> 6.37 us
  Pallas kernels: 96.8 us -> 95.1 us
    ppermute x9 -> x10, waiting for transfers between devices: 34.2 us -> 28.9 us  [swap(): return lax.ppermute(x, 'fsdp', [(i, i ^ bit) for i in range(shards)])]
    unnamed x24 -> x34, local copies, waits for them, and re-layouts: 3.02 us -> 5.98 us
    ppermute x16, waiting for transfers between devices: 4.22 us -> 5.97 us  [other_core(): return lax.ppermute(x, 'rep', [(0, 1), (1, 0)])]
    pallas_call x2, Pallas kernels: 14.9 us -> 13.2 us  [score_heads(): pl.pallas_call(functools.partial(score_kernel, len(queries)), grid=(count...]
    ppermute x9 -> x10, starting transfers between devices: 14 us -> 15.6 us  [swap(): return lax.ppermute(x, 'fsdp', [(i, i ^ bit) for i in range(shards)])]
  transfers between devices with their start and end apart: 26 -> 27, of which waited for: 10 -> 10; matrix products, arithmetic and copies ran while one was open for 2% -> 2% of each run, Pallas kernels for 58% -> 55%
where the time goes in v10:
time: 163 us; the launch traced here: 162 us
  Pallas kernels  95.1 us (58%)
  waiting for transfers between devices  34.9 us (21%)
  starting transfers between devices  22.1 us (14%)
  local copies, waits for them, and re-layouts  6.37 us (4%)
  other arithmetic  2.47 us (2%)
    pallas_call x5, Pallas kernels, project_query(): pl.pallas_call(functools.partial(query_kernel, count, pieces, by_slot), g...  49.2 us
    ppermute x10, waiting for transfers between devices, swap(): return lax.ppermute(x, 'fsdp', [(i, i ^ bit) for i in range(shards)])  28.9 us
    pallas_call x7, Pallas kernels, add_rows(): pl.pallas_call(functools.partial(add_kernel, len(gots), len(pair) // 2, l...  16.1 us
    ppermute x10, starting transfers between devices, swap(): return lax.ppermute(x, 'fsdp', [(i, i ^ bit) for i in range(shards)])  15.6 us
    pallas_call x2, Pallas kernels, score_heads(): pl.pallas_call(functools.partial(score_kernel, len(queries)), grid=(count...  13.2 us
    pallas_call x1, Pallas kernels, project_pair(): pl.pallas_call(functools.partial(pair_kernel, count), grid_spec=pltpu.Pre...  7.11 us
    unnamed x34, local copies, waits for them, and re-layouts  5.98 us
    ppermute x16, waiting for transfers between devices, other_core(): return lax.ppermute(x, 'rep', [(0, 1), (1, 0)])  5.97 us
  transfers between devices with their start and end apart: 27, of which 10 were waited for; matrix products, arithmetic and copies ran while one was open for 2% of the time, Pallas kernels for 55%

profile of v10, /device:TPU:0, one launch (start us, length us, event | category | flops | bytes accessed | tf_op | source)
XLA Modules:
  0.0 161.8 jit_solution(16341474163948255935)
XLA Ops:
  0.6 3.0 %collective-permute-start = (bf16[320,2048]{1,0:T(8,128)(2,1)}, bf16[320,2048]{1,0:T(8,128)(2,1)S(1)}, u32[]{:S(2)}, u32[]{:S(2)}) collective-permute-start(bf16[320,2048]{1,0:T(8,128)(2,1)} %refs_0_.5), channel_id=1, source_target_pairs={{0,2},{2,0},{1,3},{3,1},{4,6},{6,4},{5,7},{7,5},{8,10},{10,8},{9,1... | collective-permute-start | bytes 3932168 | tf_op jit(solution)/shard_map/ppermute | solution.py:452
  3.7 11.9 %query_products.5 = (f32[2,160,2048]{2,1,0:T(8,128)}, bf16[2,160,1024]{2,1,0:T(8,128)(2,1)}, bf16[2,160,1024]{2,1,0:T(8,128)(2,1)}) custom-call(s32[3]{0:T(128)S(1)} %pad_add_fusion.2.place_ref, bf16[320,2048]{1,0:T(8,128)(2,1)} %refs_0_.5, bf16[2048,8192]{1,0:T(8,128)(2,1)} %refs_1_.9), custom_call_target="tpu_custom_call" | custom-call | flops 1000 | bytes 1000 | tf_op jit(solution)/shard_map/query_products/pallas_call | solution.py:87
  16.1 1.8 %collective-permute-done.1.refs_1_ = bf16[2,160,1024]{2,1,0:T(8,128)(2,1)S(1)} collective-permute-done((bf16[2,160,1024]{2,1,0:T(8,128)(2,1)}, bf16[2,160,1024]{2,1,0:T(8,128)(2,1)S(1)}, u32[]{:S(2)}, u32[]{:S(2)}) %collective-permute-start.1) | collective-permute-done | bytes 655392 | tf_op jit(solution)/shard_map/ppermute | solution.py:425
  17.9 0.9 collective-permute-done.2.refs_2_
  18.9 2.7 %add_rows.7.refs_2_ = bf16[2,160,2048]{2,1,0:T(8,128)(2,1)} custom-call(f32[2,160,2048]{2,1,0:T(8,128)} %get-tuple-element.26.refs_0_, bf16[2,160,1024]{2,1,0:T(8,128)(2,1)S(1)} %collective-permute-done.1.refs_1_, bf16[2,160,1024]{2,1,0:T(8,128)(2,1)S(1)} %collective-permute-done.2.refs_2_), custom_call_target="tpu_custom_call" | custom-call | flops 1000 | bytes 1000 | tf_op jit(solution)/shard_map/add_rows/pallas_call | solution.py:187
  21.5 1.6 collective-permute-start.7
  23.8 11.7 %query_products.6 = (f32[2,160,2048]{2,1,0:T(8,128)}, bf16[1,160,2048]{2,1,0:T(8,128)(2,1)}, bf16[1,160,2048]{2,1,0:T(8,128)(2,1)}) custom-call(s32[3]{0:T(128)S(1)} %pad_add_fusion.1.place_ref, bf16[320,2048]{1,0:T(8,128)(2,1)} %refs_0_.5, bf16[2048,8192]{1,0:T(8,128)(2,1)} %refs_1_.9, bf16[2,160,2048]{2,1,0:T(8,128)(2,1)} %add_rows.7.refs_2_), custom_call_target="tpu_custom_call" | custom-call | flops 1000 | bytes 1000 | tf_op jit(solution)/shard_map/query_products/pallas_call | solution.py:87
  35.6 7.1 %key_value_products.1 = (f32[4,160,512]{2,1,0:T(8,128)}, bf16[4,160,512]{2,1,0:T(8,128)(2,1)}) custom-call(s32[5]{0:T(128)S(1)} %stack.27.place_ref, bf16[320,2048]{1,0:T(8,128)(2,1)} %refs_0_.5, bf16[320,2048]{1,0:T(8,128)(2,1)S(1)} %collective-permute-done.refs_1_.refs_0_, bf16[2048,512]{1,0:T(8,128)(2,1)} %refs_2_.1, bf16[2048,512]{1,0:T(8,128)(2,1)} %refs_3_.1, ...), custom_call_target="tpu_custom_call" | custom-call | flops 1000 | bytes 1000 | tf_op jit(solution)/shard_map/key_value_products/pallas_call | solution.py:132
  42.7 0.6 collective-permute-start.3
  43.2 11.5 %query_products.7 = (f32[2,160,2048]{2,1,0:T(8,128)}, bf16[2,160,1024]{2,1,0:T(8,128)(2,1)}, bf16[2,160,1024]{2,1,0:T(8,128)(2,1)}) custom-call(s32[3]{0:T(128)S(1)} %pad_add_fusion.2.place_ref, bf16[320,2048]{1,0:T(8,128)(2,1)S(1)} %collective-permute-done.refs_1_.refs_0_, bf16[2048,8192]{1,0:T(8,128)(2,1)} %refs_1_.9, ...), custom_call_target="tpu_custom_call" | custom-call | flops 1000 | bytes 1000 | tf_op jit(solution)/shard_map/query_products/pallas_call | solution.py:87
  55.9 1.3 collective-permute-done.4.refs_1_
  57.2 0.9 collective-permute-done.5.refs_2_.refs_1_
  58.1 2.6 %add_rows.8.refs_3_.refs_2_ = bf16[1,160,2560]{2,1,0:T(8,128)(2,1)} custom-call(f32[2,160,2048]{2,1,0:T(8,128)} %get-tuple-element.32.refs_0_, bf16[2,160,1024]{2,1,0:T(8,128)(2,1)} %collective-permute-done.4.refs_1_, bf16[2,160,1024]{2,1,0:T(8,128)(2,1)} %collective-permute-done.5.refs_2_.refs_1_, f32[4,160,512]{2,1,0:T(8,128)} %get-tuple-element.30.refs_3_.refs_2_.refs_0_, ...), custom_call_target="tpu_custom_call" | custom-call | flops 1000 | bytes 1000 | tf_op jit(solution)/shard_map/add_rows/pallas_call | solution.py:187
  61.2 2.5 %add_rows.9.refs_3_ = bf16[1,160,2048]{2,1,0:T(8,128)(2,1)} custom-call(f32[2,160,2048]{2,1,0:T(8,128)} %get-tuple-element.35.refs_0_, bf16[1,160,2048]{2,1,0:T(8,128)(2,1)} %collective-permute-done.6.refs_1_, bf16[2,160,2048]{2,1,0:T(8,128)(2,1)S(1)} %collective-permute-done.7.refs_2_.refs_1_, bf16[1,160,2560]{2,1,0:T(8,128)(2,1)} %add_rows.8.refs_3_.refs_2_), custom_call_target="tpu_custom_call" | custom-call | flops 1000 | bytes 1000 | tf_op jit(solution)/shard_map/add_rows/pallas_call | solution.py:187
  63.7 2.6 %collective-permute-start.11 = (bf16[1,160,2048]{2,1,0:T(8,128)(2,1)}, bf16[1,160,2048]{2,1,0:T(8,128)(2,1)S(1)}, u32[]{:S(2)}, u32[]{:S(2)}) collective-permute-start(bf16[1,160,2048]{2,1,0:T(8,128)(2,1)} %add_rows.9.refs_3_), channel_id=1, source_target_pairs={{0,8},{4,12},{8,0},{12,4},{1,9},{5,13},{9,1},{13,5},{2,10},{6,14},... | collective-permute-start | bytes 1966088 | tf_op jit(solution)/shard_map/ppermute | solution.py:422
  66.3 1.1 copy-done.2
  67.4 7.1 %query_products.8 = (f32[1,160,2048]{2,1,0:T(8,128)}, bf16[1,160,1024]{2,1,0:T(8,128)(2,1)}, bf16[1,160,1024]{2,1,0:T(8,128)(2,1)}) custom-call(s32[2]{0:T(128)S(1)} %pad_add_fusion.3.place_ref, bf16[320,2048]{1,0:T(8,128)(2,1)S(1)} %collective-permute-done.refs_1_.refs_0_, bf16[2048,8192]{1,0:T(8,128)(2,1)} %refs_1_.9, ...), custom_call_target="tpu_custom_call" | custom-call | flops 99999997952 | bytes 100000000 | tf_op jit(solution)/shard_map/query_products/pallas_call | solution.py:87
  75.0 0.6 fusion.4
  75.8 2.2 %add_rows.10.refs_2_ = bf16[1,160,1536]{2,1,0:T(8,128)(2,1)} custom-call(f32[2,160,2048]{2,1,0:T(8,128)} %get-tuple-element.32.refs_0_, bf16[2,160,1024]{2,1,0:T(8,128)(2,1)} %collective-permute-done.4.refs_1_, f32[4,160,512]{2,1,0:T(8,128)} %get-tuple-element.30.refs_3_.refs_2_.refs_0_, ...), custom_call_target="tpu_custom_call" | custom-call | flops 1000 | bytes 1000 | tf_op jit(solution)/shard_map/add_rows/pallas_call | solution.py:187
  78.1 2.0 %add_rows.11.refs_6_ = bf16[1,160,1024]{2,1,0:T(8,128)(2,1)} custom-call(f32[2,160,2048]{2,1,0:T(8,128)} %get-tuple-element.32.refs_0_, bf16[2,160,1024]{2,1,0:T(8,128)(2,1)} %collective-permute-done.5.refs_2_.refs_1_, bf16[1,160,1536]{2,1,0:T(8,128)(2,1)} %add_rows.10.refs_2_), custom_call_target="tpu_custom_call" | custom-call | flops 1000 | bytes 1000 | tf_op jit(solution)/shard_map/add_rows/pallas_call | solution.py:187
  80.1 1.6 collective-permute-start.8
  81.7 12.5 %collective-permute-done.11.refs_7_.refs_2_ = bf16[1,160,2048]{2,1,0:T(8,128)(2,1)S(1)} collective-permute-done((bf16[1,160,2048]{2,1,0:T(8,128)(2,1)}, bf16[1,160,2048]{2,1,0:T(8,128)(2,1)S(1)}, u32[]{:S(2)}, u32[]{:S(2)}) %collective-permute-start.11) | collective-permute-done | bytes 655392 | tf_op jit(solution)/shard_map/ppermute | solution.py:422
  94.2 1.9 %collective-permute-done.10.refs_4_.refs_5_.refs_2_ = bf16[1,160,2560]{2,1,0:T(8,128)(2,1)S(1)} collective-permute-done((bf16[1,160,2560]{2,1,0:T(8,128)(2,1)}, bf16[1,160,2560]{2,1,0:T(8,128)(2,1)S(1)}, u32[]{:S(2)}, u32[]{:S(2)}) %collective-permute-start.10) | collective-permute-done | bytes 819232 | tf_op jit(solution)/shard_map/ppermute | solution.py:422
  96.1 2.1 %add_rows.12.refs_3_ = bf16[1,160,1536]{2,1,0:T(8,128)(2,1)} custom-call(f32[1,160,2048]{2,1,0:T(8,128)} %get-tuple-element.37.refs_0_, bf16[1,160,1024]{2,1,0:T(8,128)(2,1)S(1)} %collective-permute-done.9.refs_1_, f32[4,160,512]{2,1,0:T(8,128)} %get-tuple-element.30.refs_3_.refs_2_.refs_0_, ...), custom_call_target="tpu_custom_call" | custom-call | flops 1000 | bytes 1000 | tf_op jit(solution)/shard_map/add_rows/pallas_call | solution.py:187
  98.2 1.4 collective-permute-start.12
  99.6 1.9 %add_rows.13.refs_4_.refs_2_ = bf16[1,160,1024]{2,1,0:T(8,128)(2,1)} custom-call(f32[1,160,2048]{2,1,0:T(8,128)} %get-tuple-element.37.refs_0_, bf16[1,160,1024]{2,1,0:T(8,128)(2,1)S(1)} %collective-permute-done.13.refs_1_, bf16[1,160,2560]{2,1,0:T(8,128)(2,1)S(1)} %collective-permute-done.10.refs_4_.refs_5_.refs_2_, bf16[1,160,1536]{2,1,0:T(8,128)(2,1)} %add_rows.12.refs_3_), custom_call_target="tpu_custom_call" | custom-call | flops 1000 | bytes 1000 | tf_op jit(solution)/shard_map/add_rows/pallas_call | solution.py:187
  101.5 7.0 %query_products.9 = (f32[1,160,2048]{2,1,0:T(8,128)}, bf16[1,160,1024]{2,1,0:T(8,128)(2,1)}, bf16[1,160,1024]{2,1,0:T(8,128)(2,1)}) custom-call(s32[2]{0:T(128)S(1)} %pad_add_fusion.4.place_ref, bf16[320,2048]{1,0:T(8,128)(2,1)S(1)} %collective-permute-done.refs_1_.refs_0_, bf16[2048,8192]{1,0:T(8,128)(2,1)} %refs_1_.9, ...), custom_call_target="tpu_custom_call" | custom-call | flops 99999997952 | bytes 100000000 | tf_op jit(solution)/shard_map/query_products/pallas_call | solution.py:87
  109.1 1.9 %sum_and_rotate.3.refs_0_ = bf16[160,2048]{1,0:T(8,128)(2,1)S(1)} custom-call(f32[160,128]{1,0:T(8,128)S(1)} %get-tuple-element.53.cos_ref, f32[160,128]{1,0:T(8,128)S(1)} %get-tuple-element.51.sin_ref, f32[2,160,2048]{2,1,0:T(8,128)} %get-tuple-element.35.refs_0_, bf16[2,160,2048]{2,1,0:T(8,128)(2,1)S(1)} %collective-permute-done.7.refs_2_.refs_1_, ...), custom_call_target="tpu_custom_call" | custom-call | flops 1000 | bytes 1000 | tf_op jit(solution)/shard_map/sum_and_rotate/pallas_call | solution.py:243
  111.2 2.1 %collective-permute-done.8.refs_2_.refs_1_ = bf16[1,160,1536]{2,1,0:T(8,128)(2,1)S(1)} collective-permute-done((bf16[1,160,1536]{2,1,0:T(8,128)(2,1)S(1)}, bf16[1,160,1536]{2,1,0:T(8,128)(2,1)S(1)}, u32[]{:S(2)}, u32[]{:S(2)}) %collective-permute-start.8) | collective-permute-done | bytes 491552 | tf_op jit(solution)/shard_map/ppermute | solution.py:422
  113.3 8.2 %collective-permute-done.12.refs_3_.refs_2_ = bf16[1,160,1536]{2,1,0:T(8,128)(2,1)S(1)} collective-permute-done((bf16[1,160,1536]{2,1,0:T(8,128)(2,1)}, bf16[1,160,1536]{2,1,0:T(8,128)(2,1)S(1)}, u32[]{:S(2)}, u32[]{:S(2)}) %collective-permute-start.12) | collective-permute-done | bytes 491552 | tf_op jit(solution)/shard_map/ppermute | solution.py:422
  121.5 1.3 sum_and_rotate.4.refs_1_
  122.9 0.7 copy-done
  124.0 3.3 %collective-permute-start.17 = (bf16[1,160,1024]{2,1,0:T(8,128)(2,1)}, bf16[1,160,1024]{2,1,0:T(8,128)(2,1)}, u32[]{:S(2)}, u32[]{:S(2)}) collective-permute-start(bf16[1,160,1024]{2,1,0:T(8,128)(2,1)} %add_rows.13.refs_4_.refs_2_), channel_id=1, source_target_pairs={{0,8},{4,12},{8,0},{12,4},{1,9},{5,13},{9,1},{13,5},{2,10},{6,14},... | collective-permute-start | bytes 983048 | tf_op jit(solution)/shard_map/ppermute | solution.py:422
  127.3 1.1 split_and_rotate.1
  128.8 0.9 collective-permute-done.14.other_ref
  129.8 0.6 copy-done.7
  130.4 0.8 collective-permute-start.25
  131.3 0.7 collective-permute-start.24
  132.0 0.7 copy-done.3
  132.7 2.8 %collective-permute-start.23 = (bf16[1,320,128]{2,1,0:T(8,128)(2,1)S(1)}, bf16[1,320,128]{2,1,0:T(8,128)(2,1)S(1)}, u32[]{:S(2)}, u32[]{:S(2)}) collective-permute-start(bf16[1,320,128]{2,1,0:T(8,128)(2,1)S(1)} %get-tuple-element.48.refs_0_), channel_id=1, source_target_pairs={{0,4},{4,0},{8,12},{12,8},{1,5},{5,1},{9,13},{13,9},{2,6},{6,2},{1... | collective-permute-start | bytes 245768 | tf_op jit(solution)/shard_map/ppermute | solution.py:422
  135.6 0.9 copy-done.6
  136.5 0.9 copy-done.8
  138.0 1.0 copy-done.4
  138.9 6.6 %score_heads.2 = (bf16[1,16,640,640]{3,2,1,0:T(8,128)(2,1)}, f32[8,128]{1,0:T(8,128)S(1)}) custom-call(bf16[640,640]{1,0:T(8,128)(2,1)S(1)} %get-tuple-element.40.order_ref, bf16[128,640]{1,0:T(8,128)(2,1)S(1)} %get-tuple-element.41.key_t_ref, bf16[160,2048]{1,0:T(8,128)(2,1)S(1)} %sum_and_rotate.3.refs_0_, bf16[160,1024]{1,0:T(8,128)(2,1)S(1)} %sum_and_rotate.4.refs_1_, ...), custom_call_target="tpu_custom_call" | custom-call | flops 1000 | bytes 1000 | tf_op jit(solution)/shard_map/score_heads/pallas_call | solution.py:383
  145.5 4.2 %collective-permute-done.24.refs_2_ = bf16[1,320,128]{2,1,0:T(8,128)(2,1)S(1)} collective-permute-done((bf16[1,320,128]{2,1,0:T(8,128)(2,1)S(1)}, bf16[1,320,128]{2,1,0:T(8,128)(2,1)S(1)}, u32[]{:S(2)}, u32[]{:S(2)}) %collective-permute-start.24) | collective-permute-done | bytes 81952 | tf_op jit(solution)/shard_map/ppermute | solution.py:422
  149.9 1.6 sum_and_rotate.5.refs_1_
  152.1 3.1 %order_values.1.refs_5_ = bf16[640,512]{1,0:T(8,128)(2,1)} custom-call(s32[4]{0:T(128)S(1)} %pad_add_fusion.5.place_ref, bf16[640,640]{1,0:T(8,128)(2,1)S(1)} %get-tuple-element.40.order_ref, bf16[4,320,128]{2,1,0:T(8,128)(2,1)S(1)} %stack_slots.1.own_ref, bf16[4,320,128]{2,1,0:T(8,128)(2,1)S(1)} %collective-permute-done.26.other_ref), custom_call_target="tpu_custom_call" | custom-call | tf_op jit(solution)/shard_map/order_values/pallas_call | solution.py:350
  155.2 6.6 %score_heads.3 = (bf16[1,16,640,640]{3,2,1,0:T(8,128)(2,1)}, f32[8,128]{1,0:T(8,128)}) custom-call(bf16[640,640]{1,0:T(8,128)(2,1)S(1)} %get-tuple-element.40.order_ref, bf16[128,640]{1,0:T(8,128)(2,1)S(1)} %get-tuple-element.41.key_t_ref, bf16[160,2048]{1,0:T(8,128)(2,1)S(1)} %sum_and_rotate.3.refs_0_, ...), custom_call_target="tpu_custom_call", output_to_operand_aliasing={{0}: (6, {})} | custom-call | flops 1000 | bytes 1000 | tf_op jit(solution)/shard_map/score_heads/pallas_call | solution.py:383
  (84 shorter events, 6.6 us)
Async XLA Ops:
  0.6 34.9 %collective-permute-start = (bf16[320,2048]{1,0:T(8,128)(2,1)}, bf16[320,2048]{1,0:T(8,128)(2,1)S(1)}, u32[]{:S(2)}, u32[]{:S(2)}) collective-permute-start(bf16[320,2048]{1,0:T(8,128)(2,1)} %refs_0_.5), channel_id=1, source_target_pairs={{0,2},{2,0},{1,3},{3,1},{4,6},{6,4},{5,7},{7,5},{8,10},{10,8},{9,1... | collective-permute-start | bytes 3932168 | tf_op jit(solution)/shard_map/ppermute | solution.py:452
  15.6 2.3 %collective-permute-start.1 = (bf16[2,160,1024]{2,1,0:T(8,128)(2,1)}, bf16[2,160,1024]{2,1,0:T(8,128)(2,1)S(1)}, u32[]{:S(2)}, u32[]{:S(2)}) collective-permute-start(bf16[2,160,1024]{2,1,0:T(8,128)(2,1)} %get-tuple-element.27), channel_id=1, source_target_pairs={{0,1},{1,0},{2,3},{3,2},{4,5},{5,4},{6,7},{7,6},{8,9},{9,8},{10,11... | collective-permute-start | bytes 1966088 | tf_op jit(solution)/shard_map/ppermute | solution.py:425
  15.6 3.2 %collective-permute-start.2 = (bf16[2,160,1024]{2,1,0:T(8,128)(2,1)}, bf16[2,160,1024]{2,1,0:T(8,128)(2,1)S(1)}, u32[]{:S(2)}, u32[]{:S(2)}) collective-permute-start(bf16[2,160,1024]{2,1,0:T(8,128)(2,1)} %get-tuple-element.28), channel_id=1, source_target_pairs={{0,1},{1,0},{2,3},{3,2},{4,5},{5,4},{6,7},{7,6},{8,9},{9,8},{10,11... | collective-permute-start | bytes 1966088 | tf_op jit(solution)/shard_map/ppermute | solution.py:425
  21.5 39.6 %collective-permute-start.7 = (bf16[2,160,2048]{2,1,0:T(8,128)(2,1)}, bf16[2,160,2048]{2,1,0:T(8,128)(2,1)S(1)}, u32[]{:S(2)}, u32[]{:S(2)}) collective-permute-start(bf16[2,160,2048]{2,1,0:T(8,128)(2,1)} %add_rows.7.refs_2_), channel_id=1, source_target_pairs={{0,4},{4,0},{8,12},{12,8},{1,5},{5,1},{9,13},{13,9},{2,6},{6,2},{1... | collective-permute-start | bytes 3932168 | tf_op jit(solution)/shard_map/ppermute | solution.py:422
  35.5 25.6 %collective-permute-start.6 = (bf16[1,160,2048]{2,1,0:T(8,128)(2,1)}, bf16[1,160,2048]{2,1,0:T(8,128)(2,1)}, u32[]{:S(2)}, u32[]{:S(2)}) collective-permute-start(bf16[1,160,2048]{2,1,0:T(8,128)(2,1)} %get-tuple-element.29.refs_4_), channel_id=1, source_target_pairs={{0,1},{1,0},{2,3},{3,2},{4,5},{5,4},{6,7},{7,6},{8,9},{9,8},{10,11... | collective-permute-start | bytes 1966088 | tf_op jit(solution)/shard_map/ppermute | solution.py:425
  42.7 12.7 %copy-start.12 = (s32[640]{0:T(1024)S(1)}, s32[640]{0:T(1024)}, u32[]{:S(2)}) copy-start(s32[640]{0:T(1024)} %param.10) | copy-start | bytes 7684
  42.7 12.7 %copy-start.14 = (s32[640]{0:T(1024)S(1)}, s32[640]{0:T(1024)}, u32[]{:S(2)}) copy-start(s32[640]{0:T(1024)} %param.11) | copy-start | bytes 7684
  42.7 13.2 %collective-permute-start.3 = (bf16[4,160,512]{2,1,0:T(8,128)(2,1)}, bf16[4,160,512]{2,1,0:T(8,128)(2,1)S(1)}, u32[]{:S(2)}, u32[]{:S(2)}) collective-permute-start(bf16[4,160,512]{2,1,0:T(8,128)(2,1)} %get-tuple-element.31.refs_2_), channel_id=1, source_target_pairs={{0,1},{1,0},{2,3},{3,2},{4,5},{5,4},{6,7},{7,6},{8,9},{9,8},{10,11... | collective-permute-start | bytes 1966088 | tf_op jit(solution)/shard_map/ppermute | solution.py:425
  54.7 2.4 %collective-permute-start.4 = (bf16[2,160,1024]{2,1,0:T(8,128)(2,1)}, bf16[2,160,1024]{2,1,0:T(8,128)(2,1)}, u32[]{:S(2)}, u32[]{:S(2)}) collective-permute-start(bf16[2,160,1024]{2,1,0:T(8,128)(2,1)} %get-tuple-element.33), channel_id=1, source_target_pairs={{0,1},{1,0},{2,3},{3,2},{4,5},{5,4},{6,7},{7,6},{8,9},{9,8},{10,11... | collective-permute-start | bytes 1966088 | tf_op jit(solution)/shard_map/ppermute | solution.py:425
  54.8 3.4 %collective-permute-start.5 = (bf16[2,160,1024]{2,1,0:T(8,128)(2,1)}, bf16[2,160,1024]{2,1,0:T(8,128)(2,1)}, u32[]{:S(2)}, u32[]{:S(2)}) collective-permute-start(bf16[2,160,1024]{2,1,0:T(8,128)(2,1)} %get-tuple-element.34), channel_id=1, source_target_pairs={{0,1},{1,0},{2,3},{3,2},{4,5},{5,4},{6,7},{7,6},{8,9},{9,8},{10,11... | collective-permute-start | bytes 1966088 | tf_op jit(solution)/shard_map/ppermute | solution.py:425
  55.4 5.3 %copy-start.10 = (s32[320]{0:T(512)}, s32[320]{0:T(512)S(1)}, u32[]{:S(2)}) copy-start(s32[320]{0:T(512)S(1)} %add.106) | copy-start | bytes 3844
  60.7 35.3 %collective-permute-start.10 = (bf16[1,160,2560]{2,1,0:T(8,128)(2,1)}, bf16[1,160,2560]{2,1,0:T(8,128)(2,1)S(1)}, u32[]{:S(2)}, u32[]{:S(2)}) collective-permute-start(bf16[1,160,2560]{2,1,0:T(8,128)(2,1)} %add_rows.8.refs_3_.refs_2_), channel_id=1, source_target_pairs={{0,4},{4,0},{8,12},{12,8},{1,5},{5,1},{9,13},{13,9},{2,6},{6,2},{1... | collective-permute-start | bytes 2457608 | tf_op jit(solution)/shard_map/ppermute | solution.py:422
  63.7 30.5 %collective-permute-start.11 = (bf16[1,160,2048]{2,1,0:T(8,128)(2,1)}, bf16[1,160,2048]{2,1,0:T(8,128)(2,1)S(1)}, u32[]{:S(2)}, u32[]{:S(2)}) collective-permute-start(bf16[1,160,2048]{2,1,0:T(8,128)(2,1)} %add_rows.9.refs_3_), channel_id=1, source_target_pairs={{0,8},{4,12},{8,0},{12,4},{1,9},{5,13},{9,1},{13,5},{2,10},{6,14},... | collective-permute-start | bytes 1966088 | tf_op jit(solution)/shard_map/ppermute | solution.py:422
  66.3 1.1 copy-start.2
  74.5 25.1 %collective-permute-start.13 = (bf16[1,160,1024]{2,1,0:T(8,128)(2,1)}, bf16[1,160,1024]{2,1,0:T(8,128)(2,1)S(1)}, u32[]{:S(2)}, u32[]{:S(2)}) collective-permute-start(bf16[1,160,1024]{2,1,0:T(8,128)(2,1)} %get-tuple-element.38), channel_id=1, source_target_pairs={{0,1},{1,0},{2,3},{3,2},{4,5},{5,4},{6,7},{7,6},{8,9},{9,8},{10,11... | collective-permute-start | bytes 983048 | tf_op jit(solution)/shard_map/ppermute | solution.py:425
  74.5 5.6 %collective-permute-start.9 = (bf16[1,160,1024]{2,1,0:T(8,128)(2,1)}, bf16[1,160,1024]{2,1,0:T(8,128)(2,1)S(1)}, u32[]{:S(2)}, u32[]{:S(2)}) collective-permute-start(bf16[1,160,1024]{2,1,0:T(8,128)(2,1)} %get-tuple-element.36.refs_4_), channel_id=1, source_target_pairs={{0,1},{1,0},{2,3},{3,2},{4,5},{5,4},{6,7},{7,6},{8,9},{9,8},{10,11... | collective-permute-start | bytes 983048 | tf_op jit(solution)/shard_map/ppermute | solution.py:425
  75.8 2.3 %copy-start.16 = (bf16[1,160,2048]{2,1,0:T(8,128)(2,1)S(1)}, bf16[1,160,2048]{2,1,0:T(8,128)(2,1)}, u32[]{:S(2)}) copy-start(bf16[1,160,2048]{2,1,0:T(8,128)(2,1)} %get-tuple-element.42) | copy-start | bytes 1966084
  78.0 2.1 %copy-start.9 = (bf16[1,160,1536]{2,1,0:T(8,128)(2,1)S(1)}, bf16[1,160,1536]{2,1,0:T(8,128)(2,1)}, u32[]{:S(2)}) copy-start(bf16[1,160,1536]{2,1,0:T(8,128)(2,1)} %add_rows.10.refs_2_) | copy-start | bytes 1474564
  78.0 31.1 %collective-permute-start.15 = (bf16[1,160,2048]{2,1,0:T(8,128)(2,1)S(1)}, bf16[1,160,2048]{2,1,0:T(8,128)(2,1)S(1)}, u32[]{:S(2)}, u32[]{:S(2)}) collective-permute-start(bf16[1,160,2048]{2,1,0:T(8,128)(2,1)S(1)} %copy-done.16), channel_id=1, source_target_pairs={{0,1},{1,0},{2,3},{3,2},{4,5},{5,4},{6,7},{7,6},{8,9},{9,8},{10,11... | collective-permute-start | bytes 1966088 | tf_op jit(solution)/shard_map/ppermute | solution.py:425
  80.1 33.2 %collective-permute-start.8 = (bf16[1,160,1536]{2,1,0:T(8,128)(2,1)S(1)}, bf16[1,160,1536]{2,1,0:T(8,128)(2,1)S(1)}, u32[]{:S(2)}, u32[]{:S(2)}) collective-permute-start(bf16[1,160,1536]{2,1,0:T(8,128)(2,1)S(1)} %copy-done.9), channel_id=1, source_target_pairs={{0,4},{4,0},{8,12},{12,8},{1,5},{5,1},{9,13},{13,9},{2,6},{6,2},{1... | collective-permute-start | bytes 1474568 | tf_op jit(solution)/shard_map/ppermute | solution.py:422
  98.2 23.3 %collective-permute-start.12 = (bf16[1,160,1536]{2,1,0:T(8,128)(2,1)}, bf16[1,160,1536]{2,1,0:T(8,128)(2,1)S(1)}, u32[]{:S(2)}, u32[]{:S(2)}) collective-permute-start(bf16[1,160,1536]{2,1,0:T(8,128)(2,1)} %add_rows.12.refs_3_), channel_id=1, source_target_pairs={{0,8},{4,12},{8,0},{12,4},{1,9},{5,13},{9,1},{13,5},{2,10},{6,14},... | collective-permute-start | bytes 1474568 | tf_op jit(solution)/shard_map/ppermute | solution.py:422
  108.5 4.8 %collective-permute-start.18 = (bf16[1,160,1024]{2,1,0:T(8,128)(2,1)}, bf16[1,160,1024]{2,1,0:T(8,128)(2,1)S(1)}, u32[]{:S(2)}, u32[]{:S(2)}) collective-permute-start(bf16[1,160,1024]{2,1,0:T(8,128)(2,1)} %get-tuple-element.44), channel_id=1, source_target_pairs={{0,1},{1,0},{2,3},{3,2},{4,5},{5,4},{6,7},{7,6},{8,9},{9,8},{10,11... | collective-permute-start | bytes 983048 | tf_op jit(solution)/shard_map/ppermute | solution.py:425
  108.5 4.8 %collective-permute-start.19 = (bf16[1,160,1024]{2,1,0:T(8,128)(2,1)}, bf16[1,160,1024]{2,1,0:T(8,128)(2,1)S(1)}, u32[]{:S(2)}, u32[]{:S(2)}) collective-permute-start(bf16[1,160,1024]{2,1,0:T(8,128)(2,1)} %get-tuple-element.45), channel_id=1, source_target_pairs={{0,1},{1,0},{2,3},{3,2},{4,5},{5,4},{6,7},{7,6},{8,9},{9,8},{10,11... | collective-permute-start | bytes 983048 | tf_op jit(solution)/shard_map/ppermute | solution.py:425
  111.0 20.3 %collective-permute-start.20 = (bf16[160,2048]{1,0:T(8,128)(2,1)S(1)}, bf16[160,2048]{1,0:T(8,128)(2,1)S(1)}, u32[]{:S(2)}, u32[]{:S(2)}) collective-permute-start(bf16[160,2048]{1,0:T(8,128)(2,1)S(1)} %sum_and_rotate.3.refs_0_), channel_id=1, source_target_pairs={{0,1},{1,0},{2,3},{3,2},{4,5},{5,4},{6,7},{7,6},{8,9},{9,8},{10,11... | collective-permute-start | bytes 1966088 | tf_op jit(solution)/shard_map/ppermute | solution.py:425
  122.8 0.7 copy-start
  123.6 4.9 %copy-start.15 = (s32[2]{0:T(128)S(1)}, s32[2]{0:T(128)}, u32[]{:S(2)}) copy-start(s32[2]{0:T(128)} %get-tuple-element.57) | copy-start | bytes 28
  123.6 5.0 %copy-start.13 = (s32[640]{0:T(1024)S(1)}, s32[640]{0:T(1024)}, u32[]{:S(2)}) copy-start(s32[640]{0:T(1024)} %param.10) | copy-start | bytes 7684
  123.6 12.0 %copy-start.11 = (s32[320]{0:T(512)S(1)}, s32[320]{0:T(512)}, u32[]{:S(2)}) copy-start(s32[320]{0:T(512)} %copy-done.10) | copy-start | bytes 3844
  123.6 8.4 %collective-permute-start.21 = (bf16[160,1024]{1,0:T(8,128)(2,1)S(1)}, bf16[160,1024]{1,0:T(8,128)(2,1)S(1)}, u32[]{:S(2)}, u32[]{:S(2)}) collective-permute-start(bf16[160,1024]{1,0:T(8,128)(2,1)S(1)} %sum_and_rotate.4.refs_1_), channel_id=1, source_target_pairs={{0,1},{1,0},{2,3},{3,2},{4,5},{5,4},{6,7},{7,6},{8,9},{9,8},{10,11... | collective-permute-start | bytes 983048 | tf_op jit(solution)/shard_map/ppermute | solution.py:425
  123.7 26.2 %collective-permute-start.16 = (bf16[1,160,1024]{2,1,0:T(8,128)(2,1)}, bf16[1,160,1024]{2,1,0:T(8,128)(2,1)}, u32[]{:S(2)}, u32[]{:S(2)}) collective-permute-start(bf16[1,160,1024]{2,1,0:T(8,128)(2,1)} %add_rows.11.refs_6_), channel_id=1, source_target_pairs={{0,4},{4,0},{8,12},{12,8},{1,5},{5,1},{9,13},{13,9},{2,6},{6,2},{1... | collective-permute-start | bytes 983048 | tf_op jit(solution)/shard_map/ppermute | solution.py:422
  124.0 25.8 %collective-permute-start.17 = (bf16[1,160,1024]{2,1,0:T(8,128)(2,1)}, bf16[1,160,1024]{2,1,0:T(8,128)(2,1)}, u32[]{:S(2)}, u32[]{:S(2)}) collective-permute-start(bf16[1,160,1024]{2,1,0:T(8,128)(2,1)} %add_rows.13.refs_4_.refs_2_), channel_id=1, source_target_pairs={{0,8},{4,12},{8,0},{12,4},{1,9},{5,13},{9,1},{13,5},{2,10},{6,14},... | collective-permute-start | bytes 983048 | tf_op jit(solution)/shard_map/ppermute | solution.py:422
  128.4 7.2 %copy-start.5 = (bf16[320,128]{1,0:T(8,128)(2,1)}, bf16[320,128]{1,0:T(8,128)(2,1)S(1)}, u32[]{:S(2)}) copy-start(bf16[320,128]{1,0:T(8,128)(2,1)S(1)} %get-tuple-element.39.own_ref) | copy-start | bytes 245764
  128.4 1.3 collective-permute-start.14
  128.7 21.1 %copy-start.1 = (bf16[1,160,1024]{2,1,0:T(8,128)(2,1)S(1)}, bf16[1,160,1024]{2,1,0:T(8,128)(2,1)}, u32[]{:S(2)}) copy-start(bf16[1,160,1024]{2,1,0:T(8,128)(2,1)} %copy-done) | copy-start | bytes 983044
  129.8 0.6 copy-start.7
  130.4 15.1 %collective-permute-start.25 = (bf16[1,320,128]{2,1,0:T(8,128)(2,1)S(1)}, bf16[1,320,128]{2,1,0:T(8,128)(2,1)S(1)}, u32[]{:S(2)}, u32[]{:S(2)}) collective-permute-start(bf16[1,320,128]{2,1,0:T(8,128)(2,1)S(1)} %get-tuple-element.48.refs_0_), channel_id=1, source_target_pairs={{0,12},{4,8},{8,4},{12,0},{1,13},{5,9},{9,5},{13,1},{2,14},{6,10},... | collective-permute-start | bytes 245768 | tf_op jit(solution)/shard_map/ppermute | solution.py:422
  131.3 18.5 %collective-permute-start.24 = (bf16[1,320,128]{2,1,0:T(8,128)(2,1)S(1)}, bf16[1,320,128]{2,1,0:T(8,128)(2,1)S(1)}, u32[]{:S(2)}, u32[]{:S(2)}) collective-permute-start(bf16[1,320,128]{2,1,0:T(8,128)(2,1)S(1)} %get-tuple-element.48.refs_0_), channel_id=1, source_target_pairs={{0,8},{4,12},{8,0},{12,4},{1,9},{5,13},{9,1},{13,5},{2,10},{6,14},... | collective-permute-start | bytes 245768 | tf_op jit(solution)/shard_map/ppermute | solution.py:422
  132.0 0.7 copy-start.3
  132.7 17.1 %collective-permute-start.23 = (bf16[1,320,128]{2,1,0:T(8,128)(2,1)S(1)}, bf16[1,320,128]{2,1,0:T(8,128)(2,1)S(1)}, u32[]{:S(2)}, u32[]{:S(2)}) collective-permute-start(bf16[1,320,128]{2,1,0:T(8,128)(2,1)S(1)} %get-tuple-element.48.refs_0_), channel_id=1, source_target_pairs={{0,4},{4,0},{8,12},{12,8},{1,5},{5,1},{9,13},{13,9},{2,6},{6,2},{1... | collective-permute-start | bytes 245768 | tf_op jit(solution)/shard_map/ppermute | solution.py:422
  135.6 0.9 copy-start.6
  136.5 0.9 copy-start.8
  138.0 1.0 copy-start.4
  149.8 2.3 %collective-permute-start.26 = (bf16[4,320,128]{2,1,0:T(8,128)(2,1)S(1)}, bf16[4,320,128]{2,1,0:T(8,128)(2,1)S(1)}, u32[]{:S(2)}, u32[]{:S(2)}) collective-permute-start(bf16[4,320,128]{2,1,0:T(8,128)(2,1)S(1)} %stack_slots.1.own_ref), channel_id=1, source_target_pairs={{0,1},{1,0},{2,3},{3,2},{4,5},{5,4},{6,7},{7,6},{8,9},{9,8},{10,11... | collective-permute-start | bytes 983048 | tf_op jit(solution)/shard_map/ppermute | solution.py:425
  151.5 3.7 %collective-permute-start.22 = (bf16[160,1024]{1,0:T(8,128)(2,1)S(1)}, bf16[160,1024]{1,0:T(8,128)(2,1)S(1)}, u32[]{:S(2)}, u32[]{:S(2)}) collective-permute-start(bf16[160,1024]{1,0:T(8,128)(2,1)S(1)} %sum_and_rotate.5.refs_1_), channel_id=1, source_target_pairs={{0,1},{1,0},{2,3},{3,2},{4,5},{5,4},{6,7},{7,6},{8,9},{9,8},{10,11... | collective-permute-start | bytes 983048 | tf_op jit(solution)/shard_map/ppermute | solution.py:425

commit v11 on v10

--- a/solution.py
+++ b/solution.py
@@ -114,12 +114,14 @@
 
     weights = jnp.concatenate([wk_ref[...], wv_ref[...]], axis=1)
     result = jnp.dot(rows_ref[...], weights, preferred_element_type=jnp.float32)
-    half, width = x_refs[0].shape[0] // 2, weights.shape[1]
+    half = x_refs[0].shape[0] // 2
     for b in range(count):
         kept, given = b * half, (count + b) * half
-        cols = slice(b * width, (b + 1) * width)
-        keep_ref[0, :, cols] = result[kept : kept + half]
-        give_ref[0, :, cols] = result[given : given + half].astype(give_ref.dtype)
+        for part in range(2):
+            cols = slice((part * count + b) * DH, (part * count + b + 1) * DH)
+            there = slice(part * DH, (part + 1) * DH)
+            keep_ref[0, :, cols] = result[kept : kept + half, there]
+            give_ref[0, :, cols] = result[given : given + half, there].astype(give_ref.dtype)
 
 
 def project_pair(rindex, findex, slots, blocks, w_key, w_value, after=()):
@@ -176,10 +178,10 @@
     whole = keep.shape[2]
     width = cols // len(gots)
     shift = start // cols if gots[0].shape[2] == whole else 0
-    more = pair[0].shape[2] if pair else 0
+    more = pair[0].shape[2] // 2 if pair else 0
     keep_spec = pl.BlockSpec((1, rows, cols), lambda s: (first + s, b, start // cols))
     got_spec = pl.BlockSpec((1, rows, width), lambda s: (first + s, b, shift))
-    pair_spec = pl.BlockSpec((1, rows, more), lambda s: (slot + s, 0, 0))
+    pair_spec = pl.BlockSpec((1, rows, more), lambda s: (slot + 2 * s, 0, 0))
     landed_specs = [pl.BlockSpec((1, rows, cols), lambda s: (s, 0, start // cols))]
     if pair:
         landed_specs.append(pl.BlockSpec((1, rows, more), lambda s: (s, 0, whole // more)))
@@ -255,21 +257,20 @@
     )(cosine, sine, *in_hbm([terms[0][0]]), *[term[0] for term in terms[1:]], *gots, *after)
 
 
-def split_kernel(count, cos_ref, sin_ref, *refs):
-    terms, (key_ref, value_ref) = refs[:count], refs[-2:]
+def keys_kernel(count, cos_ref, sin_ref, *refs):
+    terms, key_ref = refs[:count], refs[-1]
     total = terms[0][0].astype(jnp.float32)
     for term in terms[1:]:
         total = total + term[0].astype(jnp.float32)
     half = total.shape[0]
-    for b in range(total.shape[1] // (2 * DH)):
+    for b in range(total.shape[1] // DH):
         rows = slice(b * half, (b + 1) * half)
-        key = total[:, 2 * b * DH : (2 * b + 1) * DH]
+        key = total[:, b * DH : (b + 1) * DH]
         turned = pltpu.roll(key, DH // 2, axis=1)
         key_ref[rows] = (key * cos_ref[rows] + turned * sin_ref[rows]).astype(key_ref.dtype)
-        value_ref[0, rows] = total[:, (2 * b + 1) * DH : (2 * b + 2) * DH].astype(value_ref.dtype)
-
-
-def split_and_rotate(cosine, sine, terms, width, after):
+
+
+def rotate_keys(cosine, sine, terms, width):
     rows = cosine.shape[0]
     half = terms[0][0].shape[1]
     table = pl.BlockSpec((rows, DH), lambda j: (0, 0))
@@ -278,63 +279,79 @@
         return pl.BlockSpec((1, half, width), lambda j: (slot, 0, start // width))
 
     return pl.pallas_call(
-        functools.partial(split_kernel, len(terms)),
+        functools.partial(keys_kernel, len(terms)),
         grid=(1,),
-        in_specs=[table, table]
-        + [block(slot, start) for _, slot, start in terms]
+        in_specs=[table, table] + [block(slot, start) for _, slot, start in terms],
+        out_specs=table,
+        out_shape=jax.ShapeDtypeStruct((rows, DH), jnp.bfloat16),
+        compiler_params=pltpu.CompilerParams(vmem_limit_bytes=VMEM_BYTES),
+        cost_estimate=LIGHT,
+        name="rotate_keys",
+    )(cosine, sine, *in_hbm([terms[0][0]]), *[term for term, _, _ in terms[1:]])
+
+
+def sum_values_kernel(count, blocks, *refs):
+    out_ref = refs[-1]
+    total = refs[0][0].astype(jnp.float32)
+    for ref in refs[1:count]:
+        total = total + ref[0].astype(jnp.float32)
+    if blocks == 1:
+        out_ref[0] = total.astype(out_ref.dtype)
+    for b in range(blocks if blocks > 1 else 0):
+        half = total.shape[0]
+        out_ref[0, b * half : (b + 1) * half] = total[:, b * DH : (b + 1) * DH].astype(out_ref.dtype)
+
+
+def sum_values(pair, landed, final, after=()):
+    slots, half, width = pair[0].shape
+    width //= 2
+    blocks = width // DH if final else 1
+    shape = (slots, half * blocks, width // blocks)
+
+    def block(bit):
+        return pl.BlockSpec((1, half, width), lambda s: (s ^ bit, 0, 0))
+
+    return pl.pallas_call(
+        functools.partial(sum_values_kernel, 2 + len(landed), blocks),
+        grid=(slots,),
+        in_specs=[pl.BlockSpec((1, half, width), lambda s: (s, 0, 1))] * 2
+        + [block(bit) for _, bit in landed]
         + [pl.BlockSpec(memory_space=pl.ANY)] * len(after),
-        out_specs=[table, pl.BlockSpec((1, rows, DH), lambda j: (0, 0, 0))],
-        out_shape=[
-            jax.ShapeDtypeStruct((rows, DH), jnp.bfloat16),
-            jax.ShapeDtypeStruct((1, rows, DH), jnp.bfloat16),
-        ],
+        out_specs=pl.BlockSpec((1,) + shape[1:], lambda s: (s, 0, 0)),
+        out_shape=pltpu.HBM(shape, jnp.bfloat16),
         compiler_params=pltpu.CompilerParams(vmem_limit_bytes=VMEM_BYTES),
         cost_estimate=LIGHT,
-        name="split_and_rotate",
-    )(cosine, sine, *in_hbm([terms[0][0]]), *[term for term, _, _ in terms[1:]], *after)
-
-
-def prepare_kernel(canary_ref, ids_ref, own_ref, other_ref, order_ref, key_t_ref):
-    order = jnp.where(canary_ref[...] == ids_ref[...], 1.0, 0.0).astype(jnp.bfloat16)
-    order_ref[...] = order
+        name="sum_values",
+    )(*in_hbm(pair[:1]), *pair[1:], *[array for array, _ in landed], *in_hbm(after))
+
+
+def order_kernel(canary_ref, ids_ref, order_ref):
+    order_ref[...] = jnp.where(canary_ref[...] == ids_ref[...], 1.0, 0.0).astype(order_ref.dtype)
+
+
+def order_matrix(canary_rows, ids):
+    rows = ids.shape[0]
+    return pl.pallas_call(
+        order_kernel,
+        out_shape=jax.ShapeDtypeStruct((rows, rows), jnp.bfloat16),
+        compiler_params=pltpu.CompilerParams(vmem_limit_bytes=VMEM_BYTES),
+        name="order_matrix",
+    )(canary_rows.reshape(rows, 1), ids.reshape(1, rows))
+
+
+def ordered_keys_kernel(order_ref, own_ref, other_ref, key_t_ref):
     key = jnp.concatenate([own_ref[...], other_ref[...]], axis=0)
-    key_t_ref[...] = jnp.dot(order, key, preferred_element_type=jnp.float32).T.astype(jnp.bfloat16)
-
-
-def prepare(canary_rows, ids, own, other):
-    rows = ids.shape[0]
-    return pl.pallas_call(
-        prepare_kernel,
-        out_shape=[
-            jax.ShapeDtypeStruct((rows, rows), jnp.bfloat16),
-            jax.ShapeDtypeStruct((DH, rows), jnp.bfloat16),
-        ],
-        compiler_params=pltpu.CompilerParams(vmem_limit_bytes=VMEM_BYTES),
-        name="order_and_keys",
-    )(canary_rows.reshape(rows, 1), ids.reshape(1, rows), own, other)
-
-
-def stack_kernel(count, *refs):
-    out_ref, start = refs[-1], 0
-    for ref in refs[:count]:
-        out_ref[start : start + ref.shape[0]] = ref[...]
-        start += ref.shape[0]
-
-
-def stack_slots(arrays, after):
-    slots = sum(x.shape[0] for x in arrays)
-    shape = (slots,) + arrays[0].shape[1:]
-    return pl.pallas_call(
-        functools.partial(stack_kernel, len(arrays)),
-        grid=(1,),
-        in_specs=[pl.BlockSpec(x.shape, lambda j: (0, 0, 0)) for x in arrays]
-        + [pl.BlockSpec(memory_space=pl.ANY)] * len(after),
-        out_specs=pl.BlockSpec(shape, lambda j: (0, 0, 0)),
-        out_shape=jax.ShapeDtypeStruct(shape, arrays[0].dtype),
-        compiler_params=pltpu.CompilerParams(vmem_limit_bytes=VMEM_BYTES),
-        cost_estimate=LIGHT,
-        name="stack_slots",
-    )(*arrays, *after)
+    keys = jnp.dot(order_ref[...], key, preferred_element_type=jnp.float32)
+    key_t_ref[...] = keys.T.astype(key_t_ref.dtype)
+
+
+def ordered_keys(order, own, other):
+    return pl.pallas_call(
+        ordered_keys_kernel,
+        out_shape=jax.ShapeDtypeStruct((DH, order.shape[0]), jnp.bfloat16),
+        compiler_params=pltpu.CompilerParams(vmem_limit_bytes=VMEM_BYTES),
+        name="ordered_keys",
+    )(order, own, other)
 
 
 def value_kernel(place_ref, order_ref, own_ref, other_ref, out_ref):
@@ -485,7 +502,7 @@
         each = len(got) * cols // head_cols
         got = got[start // cols * each :][:each]
         summed = add_rows(
-            0, len(even), half, 0, keep, got, start, cols, pair, len(odd), (fars[b],), behind
+            0, len(even), half, 0, keep, got, start, cols, pair, 2, (fars[b],), behind
         )
         terms, first = spread({x: summed[k] for k, x in enumerate(even)})
         return [(term, 0, 0, 0) for term in terms], (first,)
@@ -495,15 +512,17 @@
     evens, owns, fars, terms, pair, after = [], [], [], [], (), ()
     for b, block in enumerate(placed):
         if fast_pair and b == last:
-            slots = odd + even + [0]
+            slots = list(range(shards))
             pair_keep, give = project_pair(rindex, findex, slots, placed, w_key, w_value, after)
             pair = (pair_keep, other_core(give))
             after = (give,)
         odd_keep, odd_got, given = project(odd, [block], tile, after)
         count = len(odd) - 1 if b == last else len(odd)
-        odd_sent = add_rows(0, count, half, 0, odd_keep, odd_got, 0, head_cols, pair)
+        odd_sent = add_rows(0, count, half, 0, odd_keep, odd_got, 0, head_cols, pair, 3)
         fars.append(swap(odd_sent, 1))
         after = (odd_sent,)
+        if fast_pair and b == last:
+            value_sums = [(swap(sum_values(pair, [], False, after), 1), 1)]
         if b > 0:
             added, after = add_even(b - 1, 0, head_cols, (), after)
             terms.append([(fars[b - 1], len(odd) - 1, 0, 0)] + added)
@@ -516,11 +535,16 @@
             keep, got, given = project(even, [block], tile, after, HEAVY)
             evens.append((keep, got))
         after = (given,)
+    if fast_pair:
+        bit = 2
+        while bit < shards:
+            value_sums.append((swap(sum_values(pair, value_sums, False, after), bit), bit))
+            bit *= 2
     parts, behind = [], tuple(term[0] for row in terms for term in row[1:])
     for p in range(split):
         near_sent = add_rows(
             len(odd) - 1, 1, half, 0, odd_keep, odd_got[p : p + 1], p * tile, tile,
-            pair if p == 0 else (), len(odd) - 1, (), after,
+            pair if p == 0 else (), 1, (), after,
         )
         parts.append([(swap(near_sent, 1), 0, 0, 0)])
         after = (near_sent,)
@@ -528,14 +552,16 @@
     for p in range(split):
         added, after = add_even(last, p * tile, tile, pair if p == 0 else (), after)
         parts[p] += added
+    if fast_pair:
+        held = sum_values(pair, value_sums, True, after)
+        after = after + (held,)
     keep, got, _ = project([0], placed[last:], tile, after, HEAVY)
     owns.append((keep, 0, got))
 
     if fast_pair:
-        width = 2 * DH * tps
-        pieces = [(array, shards - 1, 0) for array in pair]
+        pieces = [(array, 0, 0) for array in pair]
         pieces += [(term, 0, tile) for term, _, _, _ in parts[0]]
-        key_rot, held = split_and_rotate(cosine, sine, pieces, width, after)
+        key_rot = rotate_keys(cosine, sine, pieces, DH * tps)
     else:
         x = jnp.concatenate(blocks, axis=0)
         key_sum, value_sum = lax.psum(
@@ -555,25 +581,24 @@
         key_rot = sum_and_rotate(cosine, sine, [(key_own[None], 0, 0, 0)], (0, 0, 0, []), DH, after)
         value_rows = low(jnp.concatenate([of_core(value_sum, rindex), of_core(value_sum, 1 - rindex)]))
 
-    order, key_t = prepare(canary_rows, ids, key_rot, other_core(key_rot))
-    if not fast_pair:
+    order = order_matrix(canary_rows, ids)
+    key_t = ordered_keys(order, key_rot, other_core(key_rot))
+    if fast_pair:
+        values = order_values(findex, order, held, other_core(held))
+    else:
         values = low(jnp.dot(order, value_rows, preferred_element_type=jnp.float32))
 
     rotated = [rotate(b, 0, 1, terms[b], after) for b in range(last)]
     count = heads_here // split
     scores, mark = (), ()
     for p in range(split):
-        turned = rotate(last, p, split, parts[p], mark or tuple(owns[last][2][1:]))
+        turned = rotate(last, p, split, parts[p], mark or tuple(owns[last][2][1:]) + tuple(in_hbm([values])))
         queries = [(row[0], p * count) for row in rotated] + [(turned[0], 0)]
         queries += [(row[1], p * count) for row in rotated] + [(turned[1], 0)]
-        behind = in_hbm([values]) if p == split - 1 and p > 0 else ()
         *scores, mark = score_heads(
-            order, key_t, heads_here, p * count, count, queries, scores, behind
+            order, key_t, heads_here, p * count, count, queries, scores
         )
         mark = (mark,)
-        if fast_pair and p == 0:
-            held = stack_slots([held] + [swap(held, x) for x in range(1, shards)], mark)
-            values = order_values(findex, order, held, other_core(held))
     return (scores[0], values)
 
 

time: 163 us -> 175 us (1.074)
  Pallas kernels: 95.1 us -> 106 us
  starting transfers between devices: 22.1 us -> 17.9 us
  waiting for transfers between devices: 34.9 us -> 38.9 us
    pallas_call x3 -> x6, Pallas kernels: 1.69 us -> 11.3 us  [the longest x3 9.52 us: sum_values(): pl.pallas_call(functools.partial(sum_values_kernel, 2 + len(landed), bloc...]
    ppermute x10 -> x9, starting transfers between devices: 15.6 us -> 11.6 us  [swap(): return lax.ppermute(x, 'fsdp', [(i, i ^ bit) for i in range(shards)])]
    ppermute x10 -> x9, waiting for transfers between devices: 28.9 us -> 31.6 us  [swap(): return lax.ppermute(x, 'fsdp', [(i, i ^ bit) for i in range(shards)])]
    unnamed x34 -> x48, local copies, waits for them, and re-layouts: 5.98 us -> 6.56 us
  transfers between devices with their start and end apart: 27 -> 26, of which waited for: 10 -> 10; matrix products, arithmetic and copies ran while one was open for 2% -> 2% of each run, Pallas kernels for 55% -> 56%
where the time goes in v11:
time: 175 us; the launch traced here: 174 us
  Pallas kernels  106 us (61%)
  waiting for transfers between devices  38.9 us (22%)
  starting transfers between devices  17.9 us (10%)
  local copies, waits for them, and re-layouts  6.95 us (4%)
  other arithmetic  2.56 us (1%)
    pallas_call x5, Pallas kernels, project_query(): pl.pallas_call(functools.partial(query_kernel, count, pieces, by_slot), g...  49.3 us
    ppermute x9, waiting for transfers between devices, swap(): return lax.ppermute(x, 'fsdp', [(i, i ^ bit) for i in range(shards)])  31.6 us
    pallas_call x7, Pallas kernels, add_rows(): pl.pallas_call(functools.partial(add_kernel, len(gots), len(pair) // 2, l...  15.8 us
    pallas_call x2, Pallas kernels, score_heads(): pl.pallas_call(functools.partial(score_kernel, len(queries)), grid=(count...  14.8 us
    ppermute x9, starting transfers between devices, swap(): return lax.ppermute(x, 'fsdp', [(i, i ^ bit) for i in range(shards)])  11.6 us
    pallas_call x3, Pallas kernels, sum_values(): pl.pallas_call(functools.partial(sum_values_kernel, 2 + len(landed), bloc...  9.52 us
    ppermute x16, waiting for transfers between devices, other_core(): return lax.ppermute(x, 'rep', [(0, 1), (1, 0)])  7.28 us
    pallas_call x1, Pallas kernels, project_pair(): pl.pallas_call(functools.partial(pair_kernel, count), grid_spec=pltpu.Pre...  7.1 us
  transfers between devices with their start and end apart: 26, of which 10 were waited for; matrix products, arithmetic and copies ran while one was open for 2% of the time, Pallas kernels for 56%

profile of v11, /device:TPU:0, one launch (start us, length us, event | category | flops | bytes accessed | tf_op | source)
XLA Modules:
  0.0 173.5 jit_solution(2083947932045488850)
XLA Ops:
  0.6 3.0 %collective-permute-start = (bf16[320,2048]{1,0:T(8,128)(2,1)}, bf16[320,2048]{1,0:T(8,128)(2,1)S(1)}, u32[]{:S(2)}, u32[]{:S(2)}) collective-permute-start(bf16[320,2048]{1,0:T(8,128)(2,1)} %refs_0_.5), channel_id=1, source_target_pairs={{0,2},{2,0},{1,3},{3,1},{4,6},{6,4},{5,7},{7,5},{8,10},{10,8},{9,1... | collective-permute-start | bytes 3932168 | tf_op jit(solution)/shard_map/ppermute | solution.py:469
  3.7 11.9 %query_products.5 = (f32[2,160,2048]{2,1,0:T(8,128)}, bf16[2,160,1024]{2,1,0:T(8,128)(2,1)}, bf16[2,160,1024]{2,1,0:T(8,128)(2,1)}) custom-call(s32[3]{0:T(128)S(1)} %pad_add_fusion.2.place_ref, bf16[320,2048]{1,0:T(8,128)(2,1)} %refs_0_.5, bf16[2048,8192]{1,0:T(8,128)(2,1)} %refs_1_.9), custom_call_target="tpu_custom_call" | custom-call | flops 1000 | bytes 1000 | tf_op jit(solution)/shard_map/query_products/pallas_call | solution.py:87
  16.1 1.8 %collective-permute-done.1.refs_1_ = bf16[2,160,1024]{2,1,0:T(8,128)(2,1)S(1)} collective-permute-done((bf16[2,160,1024]{2,1,0:T(8,128)(2,1)}, bf16[2,160,1024]{2,1,0:T(8,128)(2,1)S(1)}, u32[]{:S(2)}, u32[]{:S(2)}) %collective-permute-start.1) | collective-permute-done | bytes 655392 | tf_op jit(solution)/shard_map/ppermute | solution.py:442
  17.9 0.9 collective-permute-done.2.refs_2_
  18.9 2.7 %add_rows.7.refs_2_ = bf16[2,160,2048]{2,1,0:T(8,128)(2,1)} custom-call(f32[2,160,2048]{2,1,0:T(8,128)} %get-tuple-element.22.refs_0_, bf16[2,160,1024]{2,1,0:T(8,128)(2,1)S(1)} %collective-permute-done.1.refs_1_, bf16[2,160,1024]{2,1,0:T(8,128)(2,1)S(1)} %collective-permute-done.2.refs_2_), custom_call_target="tpu_custom_call" | custom-call | flops 1000 | bytes 1000 | tf_op jit(solution)/shard_map/add_rows/pallas_call | solution.py:189
  21.5 1.6 collective-permute-start.7
  23.9 11.7 %query_products.6 = (f32[2,160,2048]{2,1,0:T(8,128)}, bf16[1,160,2048]{2,1,0:T(8,128)(2,1)}, bf16[1,160,2048]{2,1,0:T(8,128)(2,1)}) custom-call(s32[3]{0:T(128)S(1)} %pad_add_fusion.1.place_ref, bf16[320,2048]{1,0:T(8,128)(2,1)} %refs_0_.5, bf16[2048,8192]{1,0:T(8,128)(2,1)} %refs_1_.9, bf16[2,160,2048]{2,1,0:T(8,128)(2,1)} %add_rows.7.refs_2_), custom_call_target="tpu_custom_call" | custom-call | flops 1000 | bytes 1000 | tf_op jit(solution)/shard_map/query_products/pallas_call | solution.py:87
  35.6 7.1 %key_value_products.1 = (f32[4,160,512]{2,1,0:T(8,128)}, bf16[4,160,512]{2,1,0:T(8,128)(2,1)}) custom-call(s32[5]{0:T(128)S(1)} %stack.27.place_ref, bf16[320,2048]{1,0:T(8,128)(2,1)} %refs_0_.5, bf16[320,2048]{1,0:T(8,128)(2,1)S(1)} %collective-permute-done.refs_1_.refs_0_, bf16[2048,512]{1,0:T(8,128)(2,1)} %refs_2_.1, bf16[2048,512]{1,0:T(8,128)(2,1)} %refs_3_.1, ...), custom_call_target="tpu_custom_call" | custom-call | flops 1000 | bytes 1000 | tf_op jit(solution)/shard_map/key_value_products/pallas_call | solution.py:134
  43.3 11.5 %query_products.7 = (f32[2,160,2048]{2,1,0:T(8,128)}, bf16[2,160,1024]{2,1,0:T(8,128)(2,1)}, bf16[2,160,1024]{2,1,0:T(8,128)(2,1)}) custom-call(s32[3]{0:T(128)S(1)} %pad_add_fusion.2.place_ref, bf16[320,2048]{1,0:T(8,128)(2,1)S(1)} %collective-permute-done.refs_1_.refs_0_, bf16[2048,8192]{1,0:T(8,128)(2,1)} %refs_1_.9, ...), custom_call_target="tpu_custom_call" | custom-call | flops 1000 | bytes 1000 | tf_op jit(solution)/shard_map/query_products/pallas_call | solution.py:87
  55.8 0.7 fusion.4
  56.5 0.7 collective-permute-done.4.refs_1_
  57.2 0.9 collective-permute-done.5.refs_2_.refs_1_
  58.2 2.5 %add_rows.8.refs_3_.refs_2_ = bf16[1,160,2304]{2,1,0:T(8,128)(2,1)} custom-call(f32[2,160,2048]{2,1,0:T(8,128)} %get-tuple-element.28.refs_0_, bf16[2,160,1024]{2,1,0:T(8,128)(2,1)} %collective-permute-done.4.refs_1_, bf16[2,160,1024]{2,1,0:T(8,128)(2,1)} %collective-permute-done.5.refs_2_.refs_1_, f32[4,160,512]{2,1,0:T(8,128)} %get-tuple-element.26.refs_3_.refs_2_.refs_0_, ...), custom_call_target="tpu_custom_call" | custom-call | flops 1000 | bytes 1000 | tf_op jit(solution)/shard_map/add_rows/pallas_call | solution.py:189
  61.1 3.1 %sum_values.3 = bf16[4,160,256]{2,1,0:T(8,128)(2,1)} custom-call(f32[4,160,512]{2,1,0:T(8,128)} %get-tuple-element.26.refs_3_.refs_2_.refs_0_, bf16[4,160,512]{2,1,0:T(8,128)(2,1)S(1)} %collective-permute-done.3.refs_4_.refs_3_.refs_1_, bf16[1,160,2304]{2,1,0:T(8,128)(2,1)} %add_rows.8.refs_3_.refs_2_), custom_call_target="tpu_custom_call" | custom-call | flops 1000 | bytes 1000 | tf_op jit(solution)/shard_map/sum_values/pallas_call | solution.py:314
  64.3 1.6 collective-permute-start.16
  65.9 2.5 %add_rows.9.refs_3_ = bf16[1,160,2048]{2,1,0:T(8,128)(2,1)} custom-call(f32[2,160,2048]{2,1,0:T(8,128)} %get-tuple-element.31.refs_0_, bf16[1,160,2048]{2,1,0:T(8,128)(2,1)} %collective-permute-done.6.refs_1_, bf16[2,160,2048]{2,1,0:T(8,128)(2,1)S(1)} %collective-permute-done.7.refs_2_.refs_1_, bf16[1,160,2304]{2,1,0:T(8,128)(2,1)} %add_rows.8.refs_3_.refs_2_), custom_call_target="tpu_custom_call" | custom-call | flops 1000 | bytes 1000 | tf_op jit(solution)/shard_map/add_rows/pallas_call | solution.py:189
  68.4 2.6 %collective-permute-start.11 = (bf16[1,160,2048]{2,1,0:T(8,128)(2,1)}, bf16[1,160,2048]{2,1,0:T(8,128)(2,1)S(1)}, u32[]{:S(2)}, u32[]{:S(2)}) collective-permute-start(bf16[1,160,2048]{2,1,0:T(8,128)(2,1)} %add_rows.9.refs_3_), channel_id=1, source_target_pairs={{0,8},{4,12},{8,0},{12,4},{1,9},{5,13},{9,1},{13,5},{2,10},{6,14},... | collective-permute-start | bytes 1966088 | tf_op jit(solution)/shard_map/ppermute | solution.py:439
  71.0 1.1 copy-done.7
  72.1 7.1 %query_products.8 = (f32[1,160,2048]{2,1,0:T(8,128)}, bf16[1,160,1024]{2,1,0:T(8,128)(2,1)}, bf16[1,160,1024]{2,1,0:T(8,128)(2,1)}) custom-call(s32[2]{0:T(128)S(1)} %pad_add_fusion.3.place_ref, bf16[320,2048]{1,0:T(8,128)(2,1)S(1)} %collective-permute-done.refs_1_.refs_0_, bf16[2048,8192]{1,0:T(8,128)(2,1)} %refs_1_.9, ...), custom_call_target="tpu_custom_call" | custom-call | flops 99999997952 | bytes 100000000 | tf_op jit(solution)/shard_map/query_products/pallas_call | solution.py:87
  79.7 20.8 %collective-permute-done.16.refs_2_ = bf16[4,160,256]{2,1,0:T(8,128)(2,1)S(1)} collective-permute-done((bf16[4,160,256]{2,1,0:T(8,128)(2,1)}, bf16[4,160,256]{2,1,0:T(8,128)(2,1)S(1)}, u32[]{:S(2)}, u32[]{:S(2)}) %collective-permute-start.16) | collective-permute-done | bytes 327712 | tf_op jit(solution)/shard_map/ppermute | solution.py:439
  100.5 3.2 %sum_values.4 = bf16[4,160,256]{2,1,0:T(8,128)(2,1)} custom-call(f32[4,160,512]{2,1,0:T(8,128)} %get-tuple-element.26.refs_3_.refs_2_.refs_0_, bf16[4,160,512]{2,1,0:T(8,128)(2,1)S(1)} %collective-permute-done.3.refs_4_.refs_3_.refs_1_, bf16[4,160,256]{2,1,0:T(8,128)(2,1)S(1)} %collective-permute-done.16.refs_2_, ...), custom_call_target="tpu_custom_call" | custom-call | flops 1000 | bytes 1000 | tf_op jit(solution)/shard_map/sum_values/pallas_call | solution.py:314
  103.7 0.7 collective-permute-start.17
  104.6 2.1 %add_rows.10.refs_2_ = bf16[1,160,1280]{2,1,0:T(8,128)(2,1)} custom-call(f32[2,160,2048]{2,1,0:T(8,128)} %get-tuple-element.28.refs_0_, bf16[2,160,1024]{2,1,0:T(8,128)(2,1)} %collective-permute-done.4.refs_1_, f32[4,160,512]{2,1,0:T(8,128)} %get-tuple-element.26.refs_3_.refs_2_.refs_0_, ...), custom_call_target="tpu_custom_call" | custom-call | flops 1000 | bytes 1000 | tf_op jit(solution)/shard_map/add_rows/pallas_call | solution.py:189
  106.7 2.1 %add_rows.11.refs_6_ = bf16[1,160,1024]{2,1,0:T(8,128)(2,1)} custom-call(f32[2,160,2048]{2,1,0:T(8,128)} %get-tuple-element.28.refs_0_, bf16[2,160,1024]{2,1,0:T(8,128)(2,1)} %collective-permute-done.5.refs_2_.refs_1_, bf16[1,160,1280]{2,1,0:T(8,128)(2,1)} %add_rows.10.refs_2_), custom_call_target="tpu_custom_call" | custom-call | flops 1000 | bytes 1000 | tf_op jit(solution)/shard_map/add_rows/pallas_call | solution.py:189
  108.8 2.4 %collective-permute-start.8 = (bf16[1,160,1280]{2,1,0:T(8,128)(2,1)}, bf16[1,160,1280]{2,1,0:T(8,128)(2,1)}, u32[]{:S(2)}, u32[]{:S(2)}) collective-permute-start(bf16[1,160,1280]{2,1,0:T(8,128)(2,1)} %add_rows.10.refs_2_), channel_id=1, source_target_pairs={{0,4},{4,0},{8,12},{12,8},{1,5},{5,1},{9,13},{13,9},{2,6},{6,2},{1... | collective-permute-start | bytes 1228808 | tf_op jit(solution)/shard_map/ppermute | solution.py:439
  111.3 2.0 %add_rows.12.refs_3_ = bf16[1,160,1280]{2,1,0:T(8,128)(2,1)} custom-call(f32[1,160,2048]{2,1,0:T(8,128)} %get-tuple-element.33.refs_0_, bf16[1,160,1024]{2,1,0:T(8,128)(2,1)S(1)} %collective-permute-done.9.refs_1_, f32[4,160,512]{2,1,0:T(8,128)} %get-tuple-element.26.refs_3_.refs_2_.refs_0_, ...), custom_call_target="tpu_custom_call" | custom-call | flops 1000 | bytes 1000 | tf_op jit(solution)/shard_map/add_rows/pallas_call | solution.py:189
  113.3 1.9 %add_rows.13.refs_4_.refs_2_ = bf16[1,160,1024]{2,1,0:T(8,128)(2,1)} custom-call(f32[1,160,2048]{2,1,0:T(8,128)} %get-tuple-element.33.refs_0_, bf16[1,160,1024]{2,1,0:T(8,128)(2,1)S(1)} %collective-permute-done.15.refs_1_, bf16[1,160,2304]{2,1,0:T(8,128)(2,1)S(1)} %collective-permute-done.10.refs_4_.refs_5_.refs_2_, bf16[1,160,1280]{2,1,0:T(8,128)(2,1)} %add_rows.12.refs_3_), custom_call_target="tpu_custom_call" | custom-call | flops 1000 | bytes 1000 | tf_op jit(solution)/shard_map/add_rows/pallas_call | solution.py:189
  115.2 5.5 %collective-permute-done.17.refs_3_ = bf16[4,160,256]{2,1,0:T(8,128)(2,1)S(1)} collective-permute-done((bf16[4,160,256]{2,1,0:T(8,128)(2,1)}, bf16[4,160,256]{2,1,0:T(8,128)(2,1)S(1)}, u32[]{:S(2)}, u32[]{:S(2)}) %collective-permute-start.17) | collective-permute-done | bytes 327712 | tf_op jit(solution)/shard_map/ppermute | solution.py:439
  120.7 3.2 %sum_values.5.refs_5_.refs_3_.own_ref = bf16[4,320,128]{2,1,0:T(8,128)(2,1)} custom-call(f32[4,160,512]{2,1,0:T(8,128)} %get-tuple-element.26.refs_3_.refs_2_.refs_0_, bf16[4,160,512]{2,1,0:T(8,128)(2,1)S(1)} %collective-permute-done.3.refs_4_.refs_3_.refs_1_, bf16[4,160,256]{2,1,0:T(8,128)(2,1)S(1)} %collective-permute-done.16.refs_2_, ...), custom_call_target="tpu_custom_call" | custom-call | flops 1000 | bytes 1000 | tf_op jit(solution)/shard_map/sum_values/pallas_call | solution.py:314
  124.0 1.0 copy-done.2
  125.0 7.1 %query_products.9 = (f32[1,160,2048]{2,1,0:T(8,128)}, bf16[1,160,1024]{2,1,0:T(8,128)(2,1)}, bf16[1,160,1024]{2,1,0:T(8,128)(2,1)}) custom-call(s32[2]{0:T(128)S(1)} %pad_add_fusion.4.place_ref, bf16[320,2048]{1,0:T(8,128)(2,1)S(1)} %collective-permute-done.refs_1_.refs_0_, bf16[2048,8192]{1,0:T(8,128)(2,1)} %refs_1_.9, ...), custom_call_target="tpu_custom_call" | custom-call | flops 99999997952 | bytes 100000000 | tf_op jit(solution)/shard_map/query_products/pallas_call | solution.py:87
  132.6 1.9 %sum_and_rotate.3.refs_0_ = bf16[160,2048]{1,0:T(8,128)(2,1)S(1)} custom-call(f32[160,128]{1,0:T(8,128)S(1)} %get-tuple-element.45.cos_ref, f32[160,128]{1,0:T(8,128)S(1)} %get-tuple-element.43.sin_ref, f32[2,160,2048]{2,1,0:T(8,128)} %get-tuple-element.31.refs_0_, bf16[2,160,2048]{2,1,0:T(8,128)(2,1)S(1)} %collective-permute-done.7.refs_2_.refs_1_, ...), custom_call_target="tpu_custom_call" | custom-call | flops 1000 | bytes 1000 | tf_op jit(solution)/shard_map/sum_and_rotate/pallas_call | solution.py:245
  134.5 0.7 copy-done.8
  136.3 1.0 copy-done.4
  137.3 1.0 copy-done.9
  138.3 3.1 %order_values.1.refs_5_ = bf16[640,512]{1,0:T(8,128)(2,1)} custom-call(s32[4]{0:T(128)S(1)} %pad_add_fusion.5.place_ref, bf16[640,640]{1,0:T(8,128)(2,1)S(1)} %order_matrix.1.order_ref, bf16[4,320,128]{2,1,0:T(8,128)(2,1)S(1)} %copy-done.4, bf16[4,320,128]{2,1,0:T(8,128)(2,1)S(1)} %copy-done.9), custom_call_target="tpu_custom_call" | custom-call | tf_op jit(solution)/shard_map/order_values/pallas_call | solution.py:367
  141.4 0.7 copy-done.5
  142.1 1.0 copy-done.6
  143.1 1.7 sum_and_rotate.4.refs_1_
  145.0 2.3 %collective-permute-start.19 = (bf16[1,160,1024]{2,1,0:T(8,128)(2,1)S(1)}, bf16[1,160,1024]{2,1,0:T(8,128)(2,1)S(1)}, u32[]{:S(2)}, u32[]{:S(2)}) collective-permute-start(bf16[1,160,1024]{2,1,0:T(8,128)(2,1)S(1)} %copy-done.1), channel_id=1, source_target_pairs={{0,8},{4,12},{8,0},{12,4},{1,9},{5,13},{9,1},{13,5},{2,10},{6,14},... | collective-permute-start | bytes 983048 | tf_op jit(solution)/shard_map/ppermute | solution.py:439
  147.5 1.1 rotate_keys.1.own_ref
  148.7 1.3 collective-permute-done.13.other_ref
  150.4 7.4 %score_heads.2 = (bf16[1,16,640,640]{3,2,1,0:T(8,128)(2,1)}, f32[8,128]{1,0:T(8,128)S(1)}) custom-call(bf16[640,640]{1,0:T(8,128)(2,1)S(1)} %order_matrix.1.order_ref, bf16[128,640]{1,0:T(8,128)(2,1)S(1)} %ordered_keys.1.key_t_ref, bf16[160,2048]{1,0:T(8,128)(2,1)S(1)} %sum_and_rotate.3.refs_0_, bf16[160,1024]{1,0:T(8,128)(2,1)S(1)} %sum_and_rotate.4.refs_1_, ...), custom_call_target="tpu_custom_call" | custom-call | flops 1000 | bytes 1000 | tf_op jit(solution)/shard_map/score_heads/pallas_call | solution.py:400
  157.8 3.2 %collective-permute-done.18.refs_1_ = bf16[1,160,1024]{2,1,0:T(8,128)(2,1)S(1)} collective-permute-done((bf16[1,160,1024]{2,1,0:T(8,128)(2,1)S(1)}, bf16[1,160,1024]{2,1,0:T(8,128)(2,1)S(1)}, u32[]{:S(2)}, u32[]{:S(2)}) %collective-permute-start.18) | collective-permute-done | bytes 327712 | tf_op jit(solution)/shard_map/ppermute | solution.py:439
  161.1 2.0 %collective-permute-done.19.refs_2_ = bf16[1,160,1024]{2,1,0:T(8,128)(2,1)S(1)} collective-permute-done((bf16[1,160,1024]{2,1,0:T(8,128)(2,1)S(1)}, bf16[1,160,1024]{2,1,0:T(8,128)(2,1)S(1)}, u32[]{:S(2)}, u32[]{:S(2)}) %collective-permute-start.19) | collective-permute-done | bytes 327712 | tf_op jit(solution)/shard_map/ppermute | solution.py:439
  163.0 1.4 sum_and_rotate.5.refs_1_
  164.5 1.6 collective-permute-done.25.refs_3_
  166.1 7.4 %score_heads.3 = (bf16[1,16,640,640]{3,2,1,0:T(8,128)(2,1)}, f32[8,128]{1,0:T(8,128)}) custom-call(bf16[640,640]{1,0:T(8,128)(2,1)S(1)} %order_matrix.1.order_ref, bf16[128,640]{1,0:T(8,128)(2,1)S(1)} %ordered_keys.1.key_t_ref, bf16[160,2048]{1,0:T(8,128)(2,1)S(1)} %sum_and_rotate.3.refs_0_, ...), custom_call_target="tpu_custom_call", output_to_operand_aliasing={{0}: (6, {})} | custom-call | flops 1000 | bytes 1000 | tf_op jit(solution)/shard_map/score_heads/pallas_call | solution.py:400
  (99 shorter events, 6.9 us)
Async XLA Ops:
  0.6 35.0 %collective-permute-start = (bf16[320,2048]{1,0:T(8,128)(2,1)}, bf16[320,2048]{1,0:T(8,128)(2,1)S(1)}, u32[]{:S(2)}, u32[]{:S(2)}) collective-permute-start(bf16[320,2048]{1,0:T(8,128)(2,1)} %refs_0_.5), channel_id=1, source_target_pairs={{0,2},{2,0},{1,3},{3,1},{4,6},{6,4},{5,7},{7,5},{8,10},{10,8},{9,1... | collective-permute-start | bytes 3932168 | tf_op jit(solution)/shard_map/ppermute | solution.py:469
  15.6 2.3 %collective-permute-start.1 = (bf16[2,160,1024]{2,1,0:T(8,128)(2,1)}, bf16[2,160,1024]{2,1,0:T(8,128)(2,1)S(1)}, u32[]{:S(2)}, u32[]{:S(2)}) collective-permute-start(bf16[2,160,1024]{2,1,0:T(8,128)(2,1)} %get-tuple-element.23), channel_id=1, source_target_pairs={{0,1},{1,0},{2,3},{3,2},{4,5},{5,4},{6,7},{7,6},{8,9},{9,8},{10,11... | collective-permute-start | bytes 1966088 | tf_op jit(solution)/shard_map/ppermute | solution.py:442
  15.6 3.2 %collective-permute-start.2 = (bf16[2,160,1024]{2,1,0:T(8,128)(2,1)}, bf16[2,160,1024]{2,1,0:T(8,128)(2,1)S(1)}, u32[]{:S(2)}, u32[]{:S(2)}) collective-permute-start(bf16[2,160,1024]{2,1,0:T(8,128)(2,1)} %get-tuple-element.24), channel_id=1, source_target_pairs={{0,1},{1,0},{2,3},{3,2},{4,5},{5,4},{6,7},{7,6},{8,9},{9,8},{10,11... | collective-permute-start | bytes 1966088 | tf_op jit(solution)/shard_map/ppermute | solution.py:442
  21.5 44.3 %collective-permute-start.7 = (bf16[2,160,2048]{2,1,0:T(8,128)(2,1)}, bf16[2,160,2048]{2,1,0:T(8,128)(2,1)S(1)}, u32[]{:S(2)}, u32[]{:S(2)}) collective-permute-start(bf16[2,160,2048]{2,1,0:T(8,128)(2,1)} %add_rows.7.refs_2_), channel_id=1, source_target_pairs={{0,4},{4,0},{8,12},{12,8},{1,5},{5,1},{9,13},{13,9},{2,6},{6,2},{1... | collective-permute-start | bytes 3932168 | tf_op jit(solution)/shard_map/ppermute | solution.py:439
  35.6 30.2 %collective-permute-start.6 = (bf16[1,160,2048]{2,1,0:T(8,128)(2,1)}, bf16[1,160,2048]{2,1,0:T(8,128)(2,1)}, u32[]{:S(2)}, u32[]{:S(2)}) collective-permute-start(bf16[1,160,2048]{2,1,0:T(8,128)(2,1)} %get-tuple-element.25.refs_4_), channel_id=1, source_target_pairs={{0,1},{1,0},{2,3},{3,2},{4,5},{5,4},{6,7},{7,6},{8,9},{9,8},{10,11... | collective-permute-start | bytes 1966088 | tf_op jit(solution)/shard_map/ppermute | solution.py:442
  42.7 12.7 %copy-start.19 = (s32[640]{0:T(1024)S(1)}, s32[640]{0:T(1024)}, u32[]{:S(2)}) copy-start(s32[640]{0:T(1024)} %param.10) | copy-start | bytes 7684
  42.7 12.7 %copy-start.21 = (s32[640]{0:T(1024)S(1)}, s32[640]{0:T(1024)}, u32[]{:S(2)}) copy-start(s32[640]{0:T(1024)} %param.11) | copy-start | bytes 7684
  42.7 13.8 %collective-permute-start.3 = (bf16[4,160,512]{2,1,0:T(8,128)(2,1)}, bf16[4,160,512]{2,1,0:T(8,128)(2,1)S(1)}, u32[]{:S(2)}, u32[]{:S(2)}) collective-permute-start(bf16[4,160,512]{2,1,0:T(8,128)(2,1)} %get-tuple-element.27.refs_2_), channel_id=1, source_target_pairs={{0,1},{1,0},{2,3},{3,2},{4,5},{5,4},{6,7},{7,6},{8,9},{9,8},{10,11... | collective-permute-start | bytes 1966088 | tf_op jit(solution)/shard_map/ppermute | solution.py:442
  54.8 2.4 %collective-permute-start.4 = (bf16[2,160,1024]{2,1,0:T(8,128)(2,1)}, bf16[2,160,1024]{2,1,0:T(8,128)(2,1)}, u32[]{:S(2)}, u32[]{:S(2)}) collective-permute-start(bf16[2,160,1024]{2,1,0:T(8,128)(2,1)} %get-tuple-element.29), channel_id=1, source_target_pairs={{0,1},{1,0},{2,3},{3,2},{4,5},{5,4},{6,7},{7,6},{8,9},{9,8},{10,11... | collective-permute-start | bytes 1966088 | tf_op jit(solution)/shard_map/ppermute | solution.py:442
  54.8 3.4 %collective-permute-start.5 = (bf16[2,160,1024]{2,1,0:T(8,128)(2,1)}, bf16[2,160,1024]{2,1,0:T(8,128)(2,1)}, u32[]{:S(2)}, u32[]{:S(2)}) collective-permute-start(bf16[2,160,1024]{2,1,0:T(8,128)(2,1)} %get-tuple-element.30), channel_id=1, source_target_pairs={{0,1},{1,0},{2,3},{3,2},{4,5},{5,4},{6,7},{7,6},{8,9},{9,8},{10,11... | collective-permute-start | bytes 1966088 | tf_op jit(solution)/shard_map/ppermute | solution.py:442
  55.5 5.2 %copy-start.17 = (s32[320]{0:T(512)}, s32[320]{0:T(512)S(1)}, u32[]{:S(2)}) copy-start(s32[320]{0:T(512)S(1)} %add.106) | copy-start | bytes 3844
  56.5 47.8 %copy-start.10 = (f32[320,64]{1,0:T(8,128)}, f32[320,64]{1,0:T(8,128)S(1)}, u32[]{:S(2)}) copy-start(f32[320,64]{1,0:T(8,128)S(1)} %get-tuple-element.48) | copy-start | bytes 245764
  56.5 47.9 %copy-start.12 = (f32[320,64]{1,0:T(8,128)}, f32[320,64]{1,0:T(8,128)S(1)}, u32[]{:S(2)}) copy-start(f32[320,64]{1,0:T(8,128)S(1)} %get-tuple-element.46) | copy-start | bytes 245764
  56.5 47.9 %copy-start.14 = (f32[320,64]{1,0:T(8,128)}, f32[320,64]{1,0:T(8,128)S(1)}, u32[]{:S(2)}) copy-start(f32[320,64]{1,0:T(8,128)S(1)} %get-tuple-element.47) | copy-start | bytes 245764
  60.7 50.6 %collective-permute-start.10 = (bf16[1,160,2304]{2,1,0:T(8,128)(2,1)}, bf16[1,160,2304]{2,1,0:T(8,128)(2,1)S(1)}, u32[]{:S(2)}, u32[]{:S(2)}) collective-permute-start(bf16[1,160,2304]{2,1,0:T(8,128)(2,1)} %add_rows.8.refs_3_.refs_2_), channel_id=1, source_target_pairs={{0,4},{4,0},{8,12},{12,8},{1,5},{5,1},{9,13},{13,9},{2,6},{6,2},{1... | collective-permute-start | bytes 2211848 | tf_op jit(solution)/shard_map/ppermute | solution.py:439
  64.3 36.2 %collective-permute-start.16 = (bf16[4,160,256]{2,1,0:T(8,128)(2,1)}, bf16[4,160,256]{2,1,0:T(8,128)(2,1)S(1)}, u32[]{:S(2)}, u32[]{:S(2)}) collective-permute-start(bf16[4,160,256]{2,1,0:T(8,128)(2,1)} %sum_values.3), channel_id=1, source_target_pairs={{0,4},{4,0},{8,12},{12,8},{1,5},{5,1},{9,13},{13,9},{2,6},{6,2},{1... | collective-permute-start | bytes 983048 | tf_op jit(solution)/shard_map/ppermute | solution.py:439
  68.4 40.5 %collective-permute-start.11 = (bf16[1,160,2048]{2,1,0:T(8,128)(2,1)}, bf16[1,160,2048]{2,1,0:T(8,128)(2,1)S(1)}, u32[]{:S(2)}, u32[]{:S(2)}) collective-permute-start(bf16[1,160,2048]{2,1,0:T(8,128)(2,1)} %add_rows.9.refs_3_), channel_id=1, source_target_pairs={{0,8},{4,12},{8,0},{12,4},{1,9},{5,13},{9,1},{13,5},{2,10},{6,14},... | collective-permute-start | bytes 1966088 | tf_op jit(solution)/shard_map/ppermute | solution.py:439
  71.0 1.1 copy-start.7
  79.1 34.1 %collective-permute-start.15 = (bf16[1,160,1024]{2,1,0:T(8,128)(2,1)}, bf16[1,160,1024]{2,1,0:T(8,128)(2,1)S(1)}, u32[]{:S(2)}, u32[]{:S(2)}) collective-permute-start(bf16[1,160,1024]{2,1,0:T(8,128)(2,1)} %get-tuple-element.35), channel_id=1, source_target_pairs={{0,1},{1,0},{2,3},{3,2},{4,5},{5,4},{6,7},{7,6},{8,9},{9,8},{10,11... | collective-permute-start | bytes 983048 | tf_op jit(solution)/shard_map/ppermute | solution.py:442
  79.1 29.7 %collective-permute-start.9 = (bf16[1,160,1024]{2,1,0:T(8,128)(2,1)}, bf16[1,160,1024]{2,1,0:T(8,128)(2,1)S(1)}, u32[]{:S(2)}, u32[]{:S(2)}) collective-permute-start(bf16[1,160,1024]{2,1,0:T(8,128)(2,1)} %get-tuple-element.32.refs_4_.refs_3_), channel_id=1, source_target_pairs={{0,1},{1,0},{2,3},{3,2},{4,5},{5,4},{6,7},{7,6},{8,9},{9,8},{10,11... | collective-permute-start | bytes 983048 | tf_op jit(solution)/shard_map/ppermute | solution.py:442
  103.7 17.1 %collective-permute-start.17 = (bf16[4,160,256]{2,1,0:T(8,128)(2,1)}, bf16[4,160,256]{2,1,0:T(8,128)(2,1)S(1)}, u32[]{:S(2)}, u32[]{:S(2)}) collective-permute-start(bf16[4,160,256]{2,1,0:T(8,128)(2,1)} %sum_values.4), channel_id=1, source_target_pairs={{0,8},{4,12},{8,0},{12,4},{1,9},{5,13},{9,1},{13,5},{2,10},{6,14},... | collective-permute-start | bytes 983048 | tf_op jit(solution)/shard_map/ppermute | solution.py:439
  106.7 2.1 %copy-start.23 = (bf16[1,160,2048]{2,1,0:T(8,128)(2,1)S(1)}, bf16[1,160,2048]{2,1,0:T(8,128)(2,1)}, u32[]{:S(2)}) copy-start(bf16[1,160,2048]{2,1,0:T(8,128)(2,1)} %get-tuple-element.34) | copy-start | bytes 1966084
  108.8 23.7 %collective-permute-start.14 = (bf16[1,160,2048]{2,1,0:T(8,128)(2,1)S(1)}, bf16[1,160,2048]{2,1,0:T(8,128)(2,1)S(1)}, u32[]{:S(2)}, u32[]{:S(2)}) collective-permute-start(bf16[1,160,2048]{2,1,0:T(8,128)(2,1)S(1)} %copy-done.23), channel_id=1, source_target_pairs={{0,1},{1,0},{2,3},{3,2},{4,5},{5,4},{6,7},{7,6},{8,9},{9,8},{10,11... | collective-permute-start | bytes 1966088 | tf_op jit(solution)/shard_map/ppermute | solution.py:442
  108.8 32.5 %collective-permute-start.8 = (bf16[1,160,1280]{2,1,0:T(8,128)(2,1)}, bf16[1,160,1280]{2,1,0:T(8,128)(2,1)}, u32[]{:S(2)}, u32[]{:S(2)}) collective-permute-start(bf16[1,160,1280]{2,1,0:T(8,128)(2,1)} %add_rows.10.refs_2_), channel_id=1, source_target_pairs={{0,4},{4,0},{8,12},{12,8},{1,5},{5,1},{9,13},{13,9},{2,6},{6,2},{1... | collective-permute-start | bytes 1228808 | tf_op jit(solution)/shard_map/ppermute | solution.py:439
  113.3 28.8 %collective-permute-start.12 = (bf16[1,160,1280]{2,1,0:T(8,128)(2,1)}, bf16[1,160,1280]{2,1,0:T(8,128)(2,1)}, u32[]{:S(2)}, u32[]{:S(2)}) collective-permute-start(bf16[1,160,1280]{2,1,0:T(8,128)(2,1)} %add_rows.12.refs_3_), channel_id=1, source_target_pairs={{0,8},{4,12},{8,0},{12,4},{1,9},{5,13},{9,1},{13,5},{2,10},{6,14},... | collective-permute-start | bytes 1228808 | tf_op jit(solution)/shard_map/ppermute | solution.py:439
  123.9 8.6 %copy-start = (bf16[1,160,1024]{2,1,0:T(8,128)(2,1)S(1)}, bf16[1,160,1024]{2,1,0:T(8,128)(2,1)}, u32[]{:S(2)}) copy-start(bf16[1,160,1024]{2,1,0:T(8,128)(2,1)} %add_rows.13.refs_4_.refs_2_) | copy-start | bytes 983044
  123.9 10.5 %collective-permute-start.22 = (bf16[4,320,128]{2,1,0:T(8,128)(2,1)}, bf16[4,320,128]{2,1,0:T(8,128)(2,1)S(1)}, u32[]{:S(2)}, u32[]{:S(2)}) collective-permute-start(bf16[4,320,128]{2,1,0:T(8,128)(2,1)} %sum_values.5.refs_5_.refs_3_.own_ref), channel_id=1, source_target_pairs={{0,1},{1,0},{2,3},{3,2},{4,5},{5,4},{6,7},{7,6},{8,9},{9,8},{10,11... | collective-permute-start | bytes 983048 | tf_op jit(solution)/shard_map/ppermute | solution.py:442
  123.9 1.0 copy-start.2
  125.0 7.6 %copy-start.3 = (bf16[4,320,128]{2,1,0:T(8,128)(2,1)S(1)}, bf16[4,320,128]{2,1,0:T(8,128)(2,1)}, u32[]{:S(2)}) copy-start(bf16[4,320,128]{2,1,0:T(8,128)(2,1)} %sum_values.5.refs_5_.refs_3_.own_ref) | copy-start | bytes 983044
  132.0 9.3 %collective-permute-start.20 = (bf16[1,160,1024]{2,1,0:T(8,128)(2,1)}, bf16[1,160,1024]{2,1,0:T(8,128)(2,1)S(1)}, u32[]{:S(2)}, u32[]{:S(2)}) collective-permute-start(bf16[1,160,1024]{2,1,0:T(8,128)(2,1)} %get-tuple-element.37), channel_id=1, source_target_pairs={{0,1},{1,0},{2,3},{3,2},{4,5},{5,4},{6,7},{7,6},{8,9},{9,8},{10,11... | collective-permute-start | bytes 983048 | tf_op jit(solution)/shard_map/ppermute | solution.py:442
  132.5 9.6 %collective-permute-start.21 = (bf16[1,160,1024]{2,1,0:T(8,128)(2,1)}, bf16[1,160,1024]{2,1,0:T(8,128)(2,1)}, u32[]{:S(2)}, u32[]{:S(2)}) collective-permute-start(bf16[1,160,1024]{2,1,0:T(8,128)(2,1)} %get-tuple-element.38), channel_id=1, source_target_pairs={{0,1},{1,0},{2,3},{3,2},{4,5},{5,4},{6,7},{7,6},{8,9},{9,8},{10,11... | collective-permute-start | bytes 983048 | tf_op jit(solution)/shard_map/ppermute | solution.py:442
  132.6 3.1 %copy-start.22 = (s32[2]{0:T(128)S(1)}, s32[2]{0:T(128)}, u32[]{:S(2)}) copy-start(s32[2]{0:T(128)} %get-tuple-element.49) | copy-start | bytes 28
  132.6 3.2 %copy-start.20 = (s32[640]{0:T(1024)S(1)}, s32[640]{0:T(1024)}, u32[]{:S(2)}) copy-start(s32[640]{0:T(1024)} %param.10) | copy-start | bytes 7684
  132.6 3.4 %copy-start.18 = (s32[320]{0:T(512)S(1)}, s32[320]{0:T(512)}, u32[]{:S(2)}) copy-start(s32[320]{0:T(512)} %copy-done.17) | copy-start | bytes 3844
  135.2 15.2 %collective-permute-start.23 = (bf16[160,2048]{1,0:T(8,128)(2,1)S(1)}, bf16[160,2048]{1,0:T(8,128)(2,1)}, u32[]{:S(2)}, u32[]{:S(2)}) collective-permute-start(bf16[160,2048]{1,0:T(8,128)(2,1)S(1)} %sum_and_rotate.3.refs_0_), channel_id=1, source_target_pairs={{0,1},{1,0},{2,3},{3,2},{4,5},{5,4},{6,7},{7,6},{8,9},{9,8},{10,11... | collective-permute-start | bytes 1966088 | tf_op jit(solution)/shard_map/ppermute | solution.py:442
  136.3 1.0 copy-start.4
  137.3 1.0 copy-start.9
  138.3 6.6 %copy-start.16 = (bf16[1,160,1024]{2,1,0:T(8,128)(2,1)S(1)}, bf16[1,160,1024]{2,1,0:T(8,128)(2,1)}, u32[]{:S(2)}) copy-start(bf16[1,160,1024]{2,1,0:T(8,128)(2,1)} %add_rows.11.refs_6_) | copy-start | bytes 983044
  138.3 8.9 %copy-start.13 = (f32[320,64]{1,0:T(8,128)S(1)}, f32[320,64]{1,0:T(8,128)}, u32[]{:S(2)}) copy-start(f32[320,64]{1,0:T(8,128)} %copy-done.12) | copy-start | bytes 245764
  138.3 8.9 %copy-start.15 = (f32[320,64]{1,0:T(8,128)S(1)}, f32[320,64]{1,0:T(8,128)}, u32[]{:S(2)}) copy-start(f32[320,64]{1,0:T(8,128)} %copy-done.14) | copy-start | bytes 245764
  141.4 3.6 %copy-start.1 = (bf16[1,160,1024]{2,1,0:T(8,128)(2,1)S(1)}, bf16[1,160,1024]{2,1,0:T(8,128)(2,1)}, u32[]{:S(2)}) copy-start(bf16[1,160,1024]{2,1,0:T(8,128)(2,1)} %add_rows.13.refs_4_.refs_2_) | copy-start | bytes 983044
  142.1 1.0 copy-start.6
  143.1 4.3 %copy-start.11 = (f32[320,64]{1,0:T(8,128)S(1)}, f32[320,64]{1,0:T(8,128)}, u32[]{:S(2)}) copy-start(f32[320,64]{1,0:T(8,128)} %copy-done.10) | copy-start | bytes 245764
  144.8 5.7 %collective-permute-start.24 = (bf16[160,1024]{1,0:T(8,128)(2,1)S(1)}, bf16[160,1024]{1,0:T(8,128)(2,1)S(1)}, u32[]{:S(2)}, u32[]{:S(2)}) collective-permute-start(bf16[160,1024]{1,0:T(8,128)(2,1)S(1)} %sum_and_rotate.4.refs_1_), channel_id=1, source_target_pairs={{0,1},{1,0},{2,3},{3,2},{4,5},{5,4},{6,7},{7,6},{8,9},{9,8},{10,11... | collective-permute-start | bytes 983048 | tf_op jit(solution)/shard_map/ppermute | solution.py:442
  144.9 16.1 %collective-permute-start.18 = (bf16[1,160,1024]{2,1,0:T(8,128)(2,1)S(1)}, bf16[1,160,1024]{2,1,0:T(8,128)(2,1)S(1)}, u32[]{:S(2)}, u32[]{:S(2)}) collective-permute-start(bf16[1,160,1024]{2,1,0:T(8,128)(2,1)S(1)} %copy-done.16), channel_id=1, source_target_pairs={{0,4},{4,0},{8,12},{12,8},{1,5},{5,1},{9,13},{13,9},{2,6},{6,2},{1... | collective-permute-start | bytes 983048 | tf_op jit(solution)/shard_map/ppermute | solution.py:439
  145.0 18.1 %collective-permute-start.19 = (bf16[1,160,1024]{2,1,0:T(8,128)(2,1)S(1)}, bf16[1,160,1024]{2,1,0:T(8,128)(2,1)S(1)}, u32[]{:S(2)}, u32[]{:S(2)}) collective-permute-start(bf16[1,160,1024]{2,1,0:T(8,128)(2,1)S(1)} %copy-done.1), channel_id=1, source_target_pairs={{0,8},{4,12},{8,0},{12,4},{1,9},{5,13},{9,1},{13,5},{2,10},{6,14},... | collective-permute-start | bytes 983048 | tf_op jit(solution)/shard_map/ppermute | solution.py:439
  148.6 1.3 collective-permute-start.13
  164.4 1.7 collective-permute-start.25
  (2 other events, 1.5 us)

commit v12 on v10

--- a/solution.py
+++ b/solution.py
@@ -375,7 +375,7 @@
 
 def score_heads(order, key_t, heads, start, count, queries, earlier, after=()):
     rows = order.shape[0]
-    step = 2 if count % 2 == 0 else 1
+    step = math.gcd(count, 4)
 
     def block(query, first):
         return pl.BlockSpec((query.shape[0], step * DH), lambda j: (0, first // step + j))
@@ -499,9 +499,9 @@
             pair_keep, give = project_pair(rindex, findex, slots, placed, w_key, w_value, after)
             pair = (pair_keep, other_core(give))
             after = (give,)
-        odd_keep, odd_got, given = project(odd, [block], tile, after)
-        count = len(odd) - 1 if b == last else len(odd)
-        odd_sent = add_rows(0, count, half, 0, odd_keep, odd_got, 0, head_cols, pair)
+        sent = odd[:-1] if b == last else odd
+        odd_keep, odd_got, given = project(sent, [block], tile, after)
+        odd_sent = add_rows(0, len(sent), half, 0, odd_keep, odd_got, 0, head_cols, pair)
         fars.append(swap(odd_sent, 1))
         after = (odd_sent,)
         if b > 0:
@@ -516,10 +516,12 @@
             keep, got, given = project(even, [block], tile, after, HEAVY)
             evens.append((keep, got))
         after = (given,)
+    near_keep, near_got, given = project([1], placed[last:], tile, after)
+    after = (given,)
     parts, behind = [], tuple(term[0] for row in terms for term in row[1:])
     for p in range(split):
         near_sent = add_rows(
-            len(odd) - 1, 1, half, 0, odd_keep, odd_got[p : p + 1], p * tile, tile,
+            0, 1, half, 0, near_keep, near_got[p : p + 1], p * tile, tile,
             pair if p == 0 else (), len(odd) - 1, (), after,
         )
         parts.append([(swap(near_sent, 1), 0, 0, 0)])

time: 163 us -> 155 us (0.951)
  waiting for transfers between devices: 34.9 us -> 29.5 us
  local copies, waits for them, and re-layouts: 6.37 us -> 4.13 us
    ppermute x10, waiting for transfers between devices: 28.9 us -> 23.3 us  [swap(): return lax.ppermute(x, 'fsdp', [(i, i ^ bit) for i in range(shards)])]
    pallas_call x2, Pallas kernels: 13.2 us -> 9.81 us  [score_heads(): pl.pallas_call(functools.partial(score_kernel, len(queries)), grid=(count...]
    pallas_call x5 -> x6, Pallas kernels: 49.2 us -> 51.9 us  [project_query(): pl.pallas_call(functools.partial(query_kernel, count, pieces, by_slot), g...]
    unnamed x34 -> x28, local copies, waits for them, and re-layouts: 5.98 us -> 3.74 us
    ppermute x16 -> x18, starting transfers between devices: 3.49 us -> 4.15 us  [other_core(): return lax.ppermute(x, 'rep', [(0, 1), (1, 0)])]
    ppermute x16 -> x18, waiting for transfers between devices: 5.97 us -> 6.23 us  [other_core(): return lax.ppermute(x, 'rep', [(0, 1), (1, 0)])]
  transfers between devices with their start and end apart: 27 -> 29, of which waited for: 10 -> 12; matrix products, arithmetic and copies ran while one was open for 2% -> 2% of each run, Pallas kernels for 55% -> 58%
where the time goes in v12:
time: 155 us; the launch traced here: 154 us
  Pallas kernels  94.2 us (61%)
  waiting for transfers between devices  29.5 us (19%)
  starting transfers between devices  22.8 us (15%)
  local copies, waits for them, and re-layouts  4.13 us (3%)
  other arithmetic  2.6 us (2%)
    pallas_call x6, Pallas kernels, project_query(): pl.pallas_call(functools.partial(query_kernel, count, pieces, by_slot), g...  51.9 us
    ppermute x10, waiting for transfers between devices, swap(): return lax.ppermute(x, 'fsdp', [(i, i ^ bit) for i in range(shards)])  23.3 us
    pallas_call x7, Pallas kernels, add_rows(): pl.pallas_call(functools.partial(add_kernel, len(gots), len(pair) // 2, l...  15.8 us
    ppermute x10, starting transfers between devices, swap(): return lax.ppermute(x, 'fsdp', [(i, i ^ bit) for i in range(shards)])  15.6 us
    pallas_call x2, Pallas kernels, score_heads(): pl.pallas_call(functools.partial(score_kernel, len(queries)), grid=(count...  9.81 us
    pallas_call x1, Pallas kernels, project_pair(): pl.pallas_call(functools.partial(pair_kernel, count), grid_spec=pltpu.Pre...  7.12 us
    ppermute x18, waiting for transfers between devices, other_core(): return lax.ppermute(x, 'rep', [(0, 1), (1, 0)])  6.23 us
    pallas_call x3, Pallas kernels, sum_and_rotate(): pl.pallas_call(functools.partial(rotate_kernel, len(terms), len(gots)), g...  4.81 us
  transfers between devices with their start and end apart: 29, of which 12 were waited for; matrix products, arithmetic and copies ran while one was open for 2% of the time, Pallas kernels for 58%

profile of v12, /device:TPU:0, one launch (start us, length us, event | category | flops | bytes accessed | tf_op | source)
XLA Modules:
  0.0 154.1 jit_solution(14207242673534789177)
XLA Ops:
  0.6 3.0 %collective-permute-start = (bf16[320,2048]{1,0:T(8,128)(2,1)}, bf16[320,2048]{1,0:T(8,128)(2,1)S(1)}, u32[]{:S(2)}, u32[]{:S(2)}) collective-permute-start(bf16[320,2048]{1,0:T(8,128)(2,1)} %refs_0_.5), channel_id=1, source_target_pairs={{0,2},{2,0},{1,3},{3,1},{4,6},{6,4},{5,7},{7,5},{8,10},{10,8},{9,1... | collective-permute-start | bytes 3932168 | tf_op jit(solution)/shard_map/ppermute | solution.py:452
  3.7 11.9 %query_products.6 = (f32[2,160,2048]{2,1,0:T(8,128)}, bf16[2,160,1024]{2,1,0:T(8,128)(2,1)}, bf16[2,160,1024]{2,1,0:T(8,128)(2,1)}) custom-call(s32[3]{0:T(128)S(1)} %pad_add_fusion.2.place_ref, bf16[320,2048]{1,0:T(8,128)(2,1)} %refs_0_.5, bf16[2048,8192]{1,0:T(8,128)(2,1)} %refs_1_.11), custom_call_target="tpu_custom_call" | custom-call | flops 1000 | bytes 1000 | tf_op jit(solution)/shard_map/query_products/pallas_call | solution.py:87
  16.1 1.8 %collective-permute-done.1.refs_1_ = bf16[2,160,1024]{2,1,0:T(8,128)(2,1)S(1)} collective-permute-done((bf16[2,160,1024]{2,1,0:T(8,128)(2,1)}, bf16[2,160,1024]{2,1,0:T(8,128)(2,1)S(1)}, u32[]{:S(2)}, u32[]{:S(2)}) %collective-permute-start.1) | collective-permute-done | bytes 655392 | tf_op jit(solution)/shard_map/ppermute | solution.py:425
  17.9 0.9 collective-permute-done.2.refs_2_
  18.9 2.7 %add_rows.7.refs_2_ = bf16[2,160,2048]{2,1,0:T(8,128)(2,1)} custom-call(f32[2,160,2048]{2,1,0:T(8,128)} %get-tuple-element.29.refs_0_, bf16[2,160,1024]{2,1,0:T(8,128)(2,1)S(1)} %collective-permute-done.1.refs_1_, bf16[2,160,1024]{2,1,0:T(8,128)(2,1)S(1)} %collective-permute-done.2.refs_2_), custom_call_target="tpu_custom_call" | custom-call | flops 1000 | bytes 1000 | tf_op jit(solution)/shard_map/add_rows/pallas_call | solution.py:187
  21.5 1.6 %collective-permute-start.7 = (bf16[2,160,2048]{2,1,0:T(8,128)(2,1)}, bf16[2,160,2048]{2,1,0:T(8,128)(2,1)S(1)}, u32[]{:S(2)}, u32[]{:S(2)}) collective-permute-start(bf16[2,160,2048]{2,1,0:T(8,128)(2,1)} %add_rows.7.refs_2_), channel_id=1, source_target_pairs={{0,4},{4,0},{8,12},{12,8},{1,5},{5,1},{9,13},{13,9},{2,6},{6,2},{1... | collective-permute-start | bytes 3932168 | tf_op jit(solution)/shard_map/ppermute | solution.py:422
  23.3 11.7 %query_products.7 = (f32[2,160,2048]{2,1,0:T(8,128)}, bf16[1,160,2048]{2,1,0:T(8,128)(2,1)}, bf16[1,160,2048]{2,1,0:T(8,128)(2,1)}) custom-call(s32[3]{0:T(128)S(1)} %pad_add_fusion.1.place_ref, bf16[320,2048]{1,0:T(8,128)(2,1)} %refs_0_.5, bf16[2048,8192]{1,0:T(8,128)(2,1)} %refs_1_.11, bf16[2,160,2048]{2,1,0:T(8,128)(2,1)} %add_rows.7.refs_2_), custom_call_target="tpu_custom_call" | custom-call | flops 1000 | bytes 1000 | tf_op jit(solution)/shard_map/query_products/pallas_call | solution.py:87
  35.0 7.1 %key_value_products.1 = (f32[4,160,512]{2,1,0:T(8,128)}, bf16[4,160,512]{2,1,0:T(8,128)(2,1)}) custom-call(s32[5]{0:T(128)S(1)} %stack.62.place_ref, bf16[320,2048]{1,0:T(8,128)(2,1)} %refs_0_.5, bf16[320,2048]{1,0:T(8,128)(2,1)S(1)} %collective-permute-done.refs_1_.refs_0_, bf16[2048,512]{1,0:T(8,128)(2,1)} %refs_2_.1, bf16[2048,512]{1,0:T(8,128)(2,1)} %refs_3_.1, ...), custom_call_target="tpu_custom_call" | custom-call | flops 1000 | bytes 1000 | tf_op jit(solution)/shard_map/key_value_products/pallas_call | solution.py:132
  42.7 0.6 broadcast_add_fusion
  43.3 7.0 %query_products.8 = (f32[1,160,2048]{2,1,0:T(8,128)}, bf16[1,160,1024]{2,1,0:T(8,128)(2,1)}, bf16[1,160,1024]{2,1,0:T(8,128)(2,1)}) custom-call(s32[2]{0:T(128)S(1)} %get-tuple-element.66.place_ref, bf16[320,2048]{1,0:T(8,128)(2,1)S(1)} %collective-permute-done.refs_1_.refs_0_, bf16[2048,8192]{1,0:T(8,128)(2,1)} %refs_1_.11, ...), custom_call_target="tpu_custom_call" | custom-call | flops 1000 | bytes 1000 | tf_op jit(solution)/shard_map/query_products/pallas_call | solution.py:87
  51.1 1.2 collective-permute-done.4.refs_1_
  52.8 2.6 %add_rows.8.refs_3_.refs_2_ = bf16[1,160,2560]{2,1,0:T(8,128)(2,1)} custom-call(f32[1,160,2048]{2,1,0:T(8,128)} %get-tuple-element.35.refs_0_, bf16[1,160,1024]{2,1,0:T(8,128)(2,1)} %collective-permute-done.4.refs_1_, bf16[1,160,1024]{2,1,0:T(8,128)(2,1)} %collective-permute-done.5.refs_2_, f32[4,160,512]{2,1,0:T(8,128)} %get-tuple-element.33.refs_3_.refs_2_.refs_0_, ...), custom_call_target="tpu_custom_call" | custom-call | flops 1000 | bytes 1000 | tf_op jit(solution)/shard_map/add_rows/pallas_call | solution.py:187
  55.8 2.5 %add_rows.9.refs_3_ = bf16[1,160,2048]{2,1,0:T(8,128)(2,1)} custom-call(f32[2,160,2048]{2,1,0:T(8,128)} %get-tuple-element.38.refs_0_, bf16[1,160,2048]{2,1,0:T(8,128)(2,1)} %collective-permute-done.6.refs_1_, bf16[2,160,2048]{2,1,0:T(8,128)(2,1)S(1)} %collective-permute-done.7.refs_2_.refs_1_, bf16[1,160,2560]{2,1,0:T(8,128)(2,1)} %add_rows.8.refs_3_.refs_2_), custom_call_target="tpu_custom_call" | custom-call | flops 1000 | bytes 1000 | tf_op jit(solution)/shard_map/add_rows/pallas_call | solution.py:187
  58.4 2.6 %collective-permute-start.13 = (bf16[1,160,2048]{2,1,0:T(8,128)(2,1)}, bf16[1,160,2048]{2,1,0:T(8,128)(2,1)S(1)}, u32[]{:S(2)}, u32[]{:S(2)}) collective-permute-start(bf16[1,160,2048]{2,1,0:T(8,128)(2,1)} %add_rows.9.refs_3_), channel_id=1, source_target_pairs={{0,8},{4,12},{8,0},{12,4},{1,9},{5,13},{9,1},{13,5},{2,10},{6,14},... | collective-permute-start | bytes 1966088 | tf_op jit(solution)/shard_map/ppermute | solution.py:422
  60.9 1.1 copy-done.2
  62.1 7.0 %query_products.9 = (f32[1,160,2048]{2,1,0:T(8,128)}, bf16[1,160,1024]{2,1,0:T(8,128)(2,1)}, bf16[1,160,1024]{2,1,0:T(8,128)(2,1)}) custom-call(s32[2]{0:T(128)S(1)} %pad_add_fusion.4.place_ref, bf16[320,2048]{1,0:T(8,128)(2,1)S(1)} %collective-permute-done.refs_1_.refs_0_, bf16[2048,8192]{1,0:T(8,128)(2,1)} %refs_1_.11, ...), custom_call_target="tpu_custom_call" | custom-call | flops 99999997952 | bytes 100000000 | tf_op jit(solution)/shard_map/query_products/pallas_call | solution.py:87
  69.1 7.1 %query_products.10 = (f32[1,160,2048]{2,1,0:T(8,128)}, bf16[1,160,1024]{2,1,0:T(8,128)(2,1)}, bf16[1,160,1024]{2,1,0:T(8,128)(2,1)}) custom-call(s32[2]{0:T(128)S(1)} %get-tuple-element.65.place_ref, bf16[320,2048]{1,0:T(8,128)(2,1)S(1)} %collective-permute-done.refs_1_.refs_0_, bf16[2048,8192]{1,0:T(8,128)(2,1)} %refs_1_.11, ...), custom_call_target="tpu_custom_call" | custom-call | flops 1000 | bytes 1000 | tf_op jit(solution)/shard_map/query_products/pallas_call | solution.py:87
  76.6 0.6 collective-permute-start.10
  77.2 0.8 collective-permute-done.8.refs_1_
  78.2 0.6 fusion.4
  79.0 2.1 %add_rows.10.refs_2_ = bf16[1,160,1536]{2,1,0:T(8,128)(2,1)} custom-call(f32[1,160,2048]{2,1,0:T(8,128)} %get-tuple-element.40.refs_0_, bf16[1,160,1024]{2,1,0:T(8,128)(2,1)S(1)} %collective-permute-done.8.refs_1_, f32[4,160,512]{2,1,0:T(8,128)} %get-tuple-element.33.refs_3_.refs_2_.refs_0_, ...), custom_call_target="tpu_custom_call" | custom-call | flops 1000 | bytes 1000 | tf_op jit(solution)/shard_map/add_rows/pallas_call | solution.py:187
  81.5 1.9 %add_rows.11.refs_6_ = bf16[1,160,1024]{2,1,0:T(8,128)(2,1)} custom-call(f32[1,160,2048]{2,1,0:T(8,128)} %get-tuple-element.40.refs_0_, bf16[1,160,1024]{2,1,0:T(8,128)(2,1)S(1)} %collective-permute-done.12.refs_1_, bf16[1,160,1536]{2,1,0:T(8,128)(2,1)} %add_rows.10.refs_2_), custom_call_target="tpu_custom_call" | custom-call | flops 1000 | bytes 1000 | tf_op jit(solution)/shard_map/add_rows/pallas_call | solution.py:187
  83.4 1.6 %collective-permute-start.9 = (bf16[1,160,1536]{2,1,0:T(8,128)(2,1)S(1)}, bf16[1,160,1536]{2,1,0:T(8,128)(2,1)S(1)}, u32[]{:S(2)}, u32[]{:S(2)}) collective-permute-start(bf16[1,160,1536]{2,1,0:T(8,128)(2,1)S(1)} %copy-done.7), channel_id=1, source_target_pairs={{0,4},{4,0},{8,12},{12,8},{1,5},{5,1},{9,13},{13,9},{2,6},{6,2},{1... | collective-permute-start | bytes 1474568 | tf_op jit(solution)/shard_map/ppermute | solution.py:422
  85.0 3.8 %collective-permute-done.13.refs_7_.refs_2_ = bf16[1,160,2048]{2,1,0:T(8,128)(2,1)S(1)} collective-permute-done((bf16[1,160,2048]{2,1,0:T(8,128)(2,1)}, bf16[1,160,2048]{2,1,0:T(8,128)(2,1)S(1)}, u32[]{:S(2)}, u32[]{:S(2)}) %collective-permute-start.13) | collective-permute-done | bytes 655392 | tf_op jit(solution)/shard_map/ppermute | solution.py:422
  88.8 1.9 %collective-permute-done.11.refs_4_.refs_5_.refs_2_ = bf16[1,160,2560]{2,1,0:T(8,128)(2,1)S(1)} collective-permute-done((bf16[1,160,2560]{2,1,0:T(8,128)(2,1)}, bf16[1,160,2560]{2,1,0:T(8,128)(2,1)S(1)}, u32[]{:S(2)}, u32[]{:S(2)}) %collective-permute-start.11) | collective-permute-done | bytes 819232 | tf_op jit(solution)/shard_map/ppermute | solution.py:422
  90.7 2.1 %add_rows.12.refs_3_ = bf16[1,160,1536]{2,1,0:T(8,128)(2,1)} custom-call(f32[1,160,2048]{2,1,0:T(8,128)} %get-tuple-element.42.refs_0_, bf16[1,160,1024]{2,1,0:T(8,128)(2,1)S(1)} %collective-permute-done.10.refs_1_, f32[4,160,512]{2,1,0:T(8,128)} %get-tuple-element.33.refs_3_.refs_2_.refs_0_, ...), custom_call_target="tpu_custom_call" | custom-call | flops 1000 | bytes 1000 | tf_op jit(solution)/shard_map/add_rows/pallas_call | solution.py:187
  92.8 1.4 collective-permute-start.14
  94.2 1.9 %add_rows.13.refs_4_.refs_2_ = bf16[1,160,1024]{2,1,0:T(8,128)(2,1)} custom-call(f32[1,160,2048]{2,1,0:T(8,128)} %get-tuple-element.42.refs_0_, bf16[1,160,1024]{2,1,0:T(8,128)(2,1)S(1)} %collective-permute-done.15.refs_1_, bf16[1,160,2560]{2,1,0:T(8,128)(2,1)S(1)} %collective-permute-done.11.refs_4_.refs_5_.refs_2_, bf16[1,160,1536]{2,1,0:T(8,128)(2,1)} %add_rows.12.refs_3_), custom_call_target="tpu_custom_call" | custom-call | flops 1000 | bytes 1000 | tf_op jit(solution)/shard_map/add_rows/pallas_call | solution.py:187
  96.2 7.1 %query_products.11 = (f32[1,160,2048]{2,1,0:T(8,128)}, bf16[1,160,1024]{2,1,0:T(8,128)(2,1)}, bf16[1,160,1024]{2,1,0:T(8,128)(2,1)}) custom-call(s32[2]{0:T(128)S(1)} %pad_add_fusion.6.place_ref, bf16[320,2048]{1,0:T(8,128)(2,1)S(1)} %collective-permute-done.refs_1_.refs_0_, bf16[2048,8192]{1,0:T(8,128)(2,1)} %refs_1_.11, ...), custom_call_target="tpu_custom_call" | custom-call | flops 99999997952 | bytes 100000000 | tf_op jit(solution)/shard_map/query_products/pallas_call | solution.py:87
  103.9 1.9 %sum_and_rotate.3.refs_0_ = bf16[160,2048]{1,0:T(8,128)(2,1)S(1)} custom-call(f32[160,128]{1,0:T(8,128)S(1)} %get-tuple-element.59.cos_ref, f32[160,128]{1,0:T(8,128)S(1)} %get-tuple-element.57.sin_ref, f32[2,160,2048]{2,1,0:T(8,128)} %get-tuple-element.38.refs_0_, bf16[2,160,2048]{2,1,0:T(8,128)(2,1)S(1)} %collective-permute-done.7.refs_2_.refs_1_, ...), custom_call_target="tpu_custom_call" | custom-call | flops 1000 | bytes 1000 | tf_op jit(solution)/shard_map/sum_and_rotate/pallas_call | solution.py:243
  106.0 2.0 %collective-permute-done.9.refs_2_.refs_1_ = bf16[1,160,1536]{2,1,0:T(8,128)(2,1)S(1)} collective-permute-done((bf16[1,160,1536]{2,1,0:T(8,128)(2,1)S(1)}, bf16[1,160,1536]{2,1,0:T(8,128)(2,1)S(1)}, u32[]{:S(2)}, u32[]{:S(2)}) %collective-permute-start.9) | collective-permute-done | bytes 491552 | tf_op jit(solution)/shard_map/ppermute | solution.py:422
  108.0 8.2 %collective-permute-done.14.refs_3_.refs_2_ = bf16[1,160,1536]{2,1,0:T(8,128)(2,1)S(1)} collective-permute-done((bf16[1,160,1536]{2,1,0:T(8,128)(2,1)}, bf16[1,160,1536]{2,1,0:T(8,128)(2,1)S(1)}, u32[]{:S(2)}, u32[]{:S(2)}) %collective-permute-start.14) | collective-permute-done | bytes 491552 | tf_op jit(solution)/shard_map/ppermute | solution.py:422
  116.1 1.3 sum_and_rotate.4.refs_1_
  118.1 3.3 %collective-permute-start.19 = (bf16[1,160,1024]{2,1,0:T(8,128)(2,1)}, bf16[1,160,1024]{2,1,0:T(8,128)(2,1)}, u32[]{:S(2)}, u32[]{:S(2)}) collective-permute-start(bf16[1,160,1024]{2,1,0:T(8,128)(2,1)} %add_rows.13.refs_4_.refs_2_), channel_id=1, source_target_pairs={{0,8},{4,12},{8,0},{12,4},{1,9},{5,13},{9,1},{13,5},{2,10},{6,14},... | collective-permute-start | bytes 983048 | tf_op jit(solution)/shard_map/ppermute | solution.py:422
  121.3 1.1 split_and_rotate.1
  122.9 1.0 collective-permute-done.16.other_ref
  123.8 0.8 collective-permute-start.27
  124.6 0.7 collective-permute-start.26
  125.4 0.7 copy-done.3
  126.1 2.8 %collective-permute-start.25 = (bf16[1,320,128]{2,1,0:T(8,128)(2,1)S(1)}, bf16[1,320,128]{2,1,0:T(8,128)(2,1)S(1)}, u32[]{:S(2)}, u32[]{:S(2)}) collective-permute-start(bf16[1,320,128]{2,1,0:T(8,128)(2,1)S(1)} %get-tuple-element.54.refs_0_), channel_id=1, source_target_pairs={{0,4},{4,0},{8,12},{12,8},{1,5},{5,1},{9,13},{13,9},{2,6},{6,2},{1... | collective-permute-start | bytes 245768 | tf_op jit(solution)/shard_map/ppermute | solution.py:422
  129.0 0.9 copy-done.6
  130.5 1.0 copy-done.4
  131.4 4.9 %score_heads.2 = (bf16[1,16,640,640]{3,2,1,0:T(8,128)(2,1)}, f32[8,128]{1,0:T(8,128)S(1)}) custom-call(bf16[640,640]{1,0:T(8,128)(2,1)S(1)} %get-tuple-element.46.order_ref, bf16[128,640]{1,0:T(8,128)(2,1)S(1)} %get-tuple-element.47.key_t_ref, bf16[160,2048]{1,0:T(8,128)(2,1)S(1)} %sum_and_rotate.3.refs_0_, bf16[160,1024]{1,0:T(8,128)(2,1)S(1)} %sum_and_rotate.4.refs_1_, ...), custom_call_target="tpu_custom_call" | custom-call | flops 1000 | bytes 1000 | tf_op jit(solution)/shard_map/score_heads/pallas_call | solution.py:383
  136.3 2.1 %collective-permute-done.27.refs_3_ = bf16[1,320,128]{2,1,0:T(8,128)(2,1)S(1)} collective-permute-done((bf16[1,320,128]{2,1,0:T(8,128)(2,1)S(1)}, bf16[1,320,128]{2,1,0:T(8,128)(2,1)S(1)}, u32[]{:S(2)}, u32[]{:S(2)}) %collective-permute-start.27) | collective-permute-done | bytes 81952 | tf_op jit(solution)/shard_map/ppermute | solution.py:422
  138.5 5.3 %collective-permute-done.26.refs_2_ = bf16[1,320,128]{2,1,0:T(8,128)(2,1)S(1)} collective-permute-done((bf16[1,320,128]{2,1,0:T(8,128)(2,1)S(1)}, bf16[1,320,128]{2,1,0:T(8,128)(2,1)S(1)}, u32[]{:S(2)}, u32[]{:S(2)}) %collective-permute-start.26) | collective-permute-done | bytes 81952 | tf_op jit(solution)/shard_map/ppermute | solution.py:422
  143.9 1.6 %sum_and_rotate.5.refs_1_ = bf16[160,1024]{1,0:T(8,128)(2,1)S(1)} custom-call(f32[160,128]{1,0:T(8,128)S(1)} %get-tuple-element.58.cos_ref, f32[160,128]{1,0:T(8,128)S(1)} %get-tuple-element.56.sin_ref, f32[1,160,2048]{2,1,0:T(8,128)} %get-tuple-element.49.refs_0_, bf16[1,160,1024]{2,1,0:T(8,128)(2,1)} %collective-permute-done.18.refs_1_, ...), custom_call_target="tpu_custom_call" | custom-call | flops 1000 | bytes 1000 | tf_op jit(solution)/shard_map/sum_and_rotate/pallas_call | solution.py:243
  146.1 3.1 %order_values.1.refs_5_ = bf16[640,512]{1,0:T(8,128)(2,1)} custom-call(s32[4]{0:T(128)S(1)} %pad_add_fusion.7.place_ref, bf16[640,640]{1,0:T(8,128)(2,1)S(1)} %get-tuple-element.46.order_ref, bf16[4,320,128]{2,1,0:T(8,128)(2,1)S(1)} %stack_slots.1.own_ref, bf16[4,320,128]{2,1,0:T(8,128)(2,1)S(1)} %collective-permute-done.28.other_ref), custom_call_target="tpu_custom_call" | custom-call | tf_op jit(solution)/shard_map/order_values/pallas_call | solution.py:350
  149.2 4.9 %score_heads.3 = (bf16[1,16,640,640]{3,2,1,0:T(8,128)(2,1)}, f32[8,128]{1,0:T(8,128)}) custom-call(bf16[640,640]{1,0:T(8,128)(2,1)S(1)} %get-tuple-element.46.order_ref, bf16[128,640]{1,0:T(8,128)(2,1)S(1)} %get-tuple-element.47.key_t_ref, bf16[160,2048]{1,0:T(8,128)(2,1)S(1)} %sum_and_rotate.3.refs_0_, ...), custom_call_target="tpu_custom_call", output_to_operand_aliasing={{0}: (6, {})} | custom-call | flops 1000 | bytes 1000 | tf_op jit(solution)/shard_map/score_heads/pallas_call | solution.py:383
  (84 shorter events, 7.3 us)
Async XLA Ops:
  0.6 34.4 %collective-permute-start = (bf16[320,2048]{1,0:T(8,128)(2,1)}, bf16[320,2048]{1,0:T(8,128)(2,1)S(1)}, u32[]{:S(2)}, u32[]{:S(2)}) collective-permute-start(bf16[320,2048]{1,0:T(8,128)(2,1)} %refs_0_.5), channel_id=1, source_target_pairs={{0,2},{2,0},{1,3},{3,1},{4,6},{6,4},{5,7},{7,5},{8,10},{10,8},{9,1... | collective-permute-start | bytes 3932168 | tf_op jit(solution)/shard_map/ppermute | solution.py:452
  15.6 2.3 %collective-permute-start.1 = (bf16[2,160,1024]{2,1,0:T(8,128)(2,1)}, bf16[2,160,1024]{2,1,0:T(8,128)(2,1)S(1)}, u32[]{:S(2)}, u32[]{:S(2)}) collective-permute-start(bf16[2,160,1024]{2,1,0:T(8,128)(2,1)} %get-tuple-element.30), channel_id=1, source_target_pairs={{0,1},{1,0},{2,3},{3,2},{4,5},{5,4},{6,7},{7,6},{8,9},{9,8},{10,11... | collective-permute-start | bytes 1966088 | tf_op jit(solution)/shard_map/ppermute | solution.py:425
  15.6 3.2 %collective-permute-start.2 = (bf16[2,160,1024]{2,1,0:T(8,128)(2,1)}, bf16[2,160,1024]{2,1,0:T(8,128)(2,1)S(1)}, u32[]{:S(2)}, u32[]{:S(2)}) collective-permute-start(bf16[2,160,1024]{2,1,0:T(8,128)(2,1)} %get-tuple-element.31), channel_id=1, source_target_pairs={{0,1},{1,0},{2,3},{3,2},{4,5},{5,4},{6,7},{7,6},{8,9},{9,8},{10,11... | collective-permute-start | bytes 1966088 | tf_op jit(solution)/shard_map/ppermute | solution.py:425
  21.5 34.3 %collective-permute-start.7 = (bf16[2,160,2048]{2,1,0:T(8,128)(2,1)}, bf16[2,160,2048]{2,1,0:T(8,128)(2,1)S(1)}, u32[]{:S(2)}, u32[]{:S(2)}) collective-permute-start(bf16[2,160,2048]{2,1,0:T(8,128)(2,1)} %add_rows.7.refs_2_), channel_id=1, source_target_pairs={{0,4},{4,0},{8,12},{12,8},{1,5},{5,1},{9,13},{13,9},{2,6},{6,2},{1... | collective-permute-start | bytes 3932168 | tf_op jit(solution)/shard_map/ppermute | solution.py:422
  42.1 10.6 %collective-permute-start.3 = (bf16[4,160,512]{2,1,0:T(8,128)(2,1)}, bf16[4,160,512]{2,1,0:T(8,128)(2,1)S(1)}, u32[]{:S(2)}, u32[]{:S(2)}) collective-permute-start(bf16[4,160,512]{2,1,0:T(8,128)(2,1)} %get-tuple-element.34.refs_2_), channel_id=1, source_target_pairs={{0,1},{1,0},{2,3},{3,2},{4,5},{5,4},{6,7},{7,6},{8,9},{9,8},{10,11... | collective-permute-start | bytes 1966088 | tf_op jit(solution)/shard_map/ppermute | solution.py:425
  42.1 13.7 %collective-permute-start.6 = (bf16[1,160,2048]{2,1,0:T(8,128)(2,1)}, bf16[1,160,2048]{2,1,0:T(8,128)(2,1)}, u32[]{:S(2)}, u32[]{:S(2)}) collective-permute-start(bf16[1,160,2048]{2,1,0:T(8,128)(2,1)} %get-tuple-element.32.refs_4_), channel_id=1, source_target_pairs={{0,1},{1,0},{2,3},{3,2},{4,5},{5,4},{6,7},{7,6},{8,9},{9,8},{10,11... | collective-permute-start | bytes 1966088 | tf_op jit(solution)/shard_map/ppermute | solution.py:425
  50.3 2.0 %collective-permute-start.4 = (bf16[1,160,1024]{2,1,0:T(8,128)(2,1)}, bf16[1,160,1024]{2,1,0:T(8,128)(2,1)}, u32[]{:S(2)}, u32[]{:S(2)}) collective-permute-start(bf16[1,160,1024]{2,1,0:T(8,128)(2,1)} %get-tuple-element.36), channel_id=1, source_target_pairs={{0,1},{1,0},{2,3},{3,2},{4,5},{5,4},{6,7},{7,6},{8,9},{9,8},{10,11... | collective-permute-start | bytes 983048 | tf_op jit(solution)/shard_map/ppermute | solution.py:425
  50.4 2.4 %collective-permute-start.5 = (bf16[1,160,1024]{2,1,0:T(8,128)(2,1)}, bf16[1,160,1024]{2,1,0:T(8,128)(2,1)}, u32[]{:S(2)}, u32[]{:S(2)}) collective-permute-start(bf16[1,160,1024]{2,1,0:T(8,128)(2,1)} %get-tuple-element.37), channel_id=1, source_target_pairs={{0,1},{1,0},{2,3},{3,2},{4,5},{5,4},{6,7},{7,6},{8,9},{9,8},{10,11... | collective-permute-start | bytes 983048 | tf_op jit(solution)/shard_map/ppermute | solution.py:425
  55.4 35.3 %collective-permute-start.11 = (bf16[1,160,2560]{2,1,0:T(8,128)(2,1)}, bf16[1,160,2560]{2,1,0:T(8,128)(2,1)S(1)}, u32[]{:S(2)}, u32[]{:S(2)}) collective-permute-start(bf16[1,160,2560]{2,1,0:T(8,128)(2,1)} %add_rows.8.refs_3_.refs_2_), channel_id=1, source_target_pairs={{0,4},{4,0},{8,12},{12,8},{1,5},{5,1},{9,13},{13,9},{2,6},{6,2},{1... | collective-permute-start | bytes 2457608 | tf_op jit(solution)/shard_map/ppermute | solution.py:422
  58.4 30.5 %collective-permute-start.13 = (bf16[1,160,2048]{2,1,0:T(8,128)(2,1)}, bf16[1,160,2048]{2,1,0:T(8,128)(2,1)S(1)}, u32[]{:S(2)}, u32[]{:S(2)}) collective-permute-start(bf16[1,160,2048]{2,1,0:T(8,128)(2,1)} %add_rows.9.refs_3_), channel_id=1, source_target_pairs={{0,8},{4,12},{8,0},{12,4},{1,9},{5,13},{9,1},{13,5},{2,10},{6,14},... | collective-permute-start | bytes 1966088 | tf_op jit(solution)/shard_map/ppermute | solution.py:422
  60.9 1.1 copy-start.2
  69.1 7.1 %copy-start.9 = (s32[640]{0:T(1024)S(1)}, s32[640]{0:T(1024)}, u32[]{:S(2)}) copy-start(s32[640]{0:T(1024)} %param.10) | copy-start | bytes 7684
  69.1 7.1 %copy-start.10 = (s32[640]{0:T(1024)S(1)}, s32[640]{0:T(1024)}, u32[]{:S(2)}) copy-start(s32[640]{0:T(1024)} %param.11) | copy-start | bytes 7684
  69.1 7.5 %copy-start.8 = (bf16[1,160,1024]{2,1,0:T(8,128)(2,1)S(1)}, bf16[1,160,1024]{2,1,0:T(8,128)(2,1)}, u32[]{:S(2)}) copy-start(bf16[1,160,1024]{2,1,0:T(8,128)(2,1)} %get-tuple-element.39.refs_2_) | copy-start | bytes 983044
  69.1 8.0 %copy-start.13 = (bf16[1,160,1024]{2,1,0:T(8,128)(2,1)S(1)}, bf16[1,160,1024]{2,1,0:T(8,128)(2,1)}, u32[]{:S(2)}) copy-start(bf16[1,160,1024]{2,1,0:T(8,128)(2,1)} %get-tuple-element.44) | copy-start | bytes 983044
  76.2 1.8 %collective-permute-start.8 = (bf16[1,160,1024]{2,1,0:T(8,128)(2,1)}, bf16[1,160,1024]{2,1,0:T(8,128)(2,1)S(1)}, u32[]{:S(2)}, u32[]{:S(2)}) collective-permute-start(bf16[1,160,1024]{2,1,0:T(8,128)(2,1)} %get-tuple-element.41.refs_4_), channel_id=1, source_target_pairs={{0,1},{1,0},{2,3},{3,2},{4,5},{5,4},{6,7},{7,6},{8,9},{9,8},{10,11... | collective-permute-start | bytes 983048 | tf_op jit(solution)/shard_map/ppermute | solution.py:425
  76.6 6.8 %collective-permute-start.10 = (bf16[1,160,1024]{2,1,0:T(8,128)(2,1)S(1)}, bf16[1,160,1024]{2,1,0:T(8,128)(2,1)S(1)}, u32[]{:S(2)}, u32[]{:S(2)}) collective-permute-start(bf16[1,160,1024]{2,1,0:T(8,128)(2,1)S(1)} %copy-done.8), channel_id=1, source_target_pairs={{0,1},{1,0},{2,3},{3,2},{4,5},{5,4},{6,7},{7,6},{8,9},{9,8},{10,11... | collective-permute-start | bytes 983048 | tf_op jit(solution)/shard_map/ppermute | solution.py:425
  77.2 17.1 %collective-permute-start.15 = (bf16[1,160,1024]{2,1,0:T(8,128)(2,1)S(1)}, bf16[1,160,1024]{2,1,0:T(8,128)(2,1)S(1)}, u32[]{:S(2)}, u32[]{:S(2)}) collective-permute-start(bf16[1,160,1024]{2,1,0:T(8,128)(2,1)S(1)} %copy-done.13), channel_id=1, source_target_pairs={{0,1},{1,0},{2,3},{3,2},{4,5},{5,4},{6,7},{7,6},{8,9},{9,8},{10,11... | collective-permute-start | bytes 983048 | tf_op jit(solution)/shard_map/ppermute | solution.py:425
  78.1 3.0 %collective-permute-start.12 = (bf16[1,160,1024]{2,1,0:T(8,128)(2,1)}, bf16[1,160,1024]{2,1,0:T(8,128)(2,1)S(1)}, u32[]{:S(2)}, u32[]{:S(2)}) collective-permute-start(bf16[1,160,1024]{2,1,0:T(8,128)(2,1)} %get-tuple-element.43), channel_id=1, source_target_pairs={{0,1},{1,0},{2,3},{3,2},{4,5},{5,4},{6,7},{7,6},{8,9},{9,8},{10,11... | collective-permute-start | bytes 983048 | tf_op jit(solution)/shard_map/ppermute | solution.py:425
  79.0 2.1 %copy-start.12 = (bf16[1,160,2048]{2,1,0:T(8,128)(2,1)S(1)}, bf16[1,160,2048]{2,1,0:T(8,128)(2,1)}, u32[]{:S(2)}) copy-start(bf16[1,160,2048]{2,1,0:T(8,128)(2,1)} %get-tuple-element.48) | copy-start | bytes 1966084
  81.1 2.3 %copy-start.7 = (bf16[1,160,1536]{2,1,0:T(8,128)(2,1)S(1)}, bf16[1,160,1536]{2,1,0:T(8,128)(2,1)}, u32[]{:S(2)}) copy-start(bf16[1,160,1536]{2,1,0:T(8,128)(2,1)} %add_rows.10.refs_2_) | copy-start | bytes 1474564
  81.1 22.8 %collective-permute-start.17 = (bf16[1,160,2048]{2,1,0:T(8,128)(2,1)S(1)}, bf16[1,160,2048]{2,1,0:T(8,128)(2,1)S(1)}, u32[]{:S(2)}, u32[]{:S(2)}) collective-permute-start(bf16[1,160,2048]{2,1,0:T(8,128)(2,1)S(1)} %copy-done.12), channel_id=1, source_target_pairs={{0,1},{1,0},{2,3},{3,2},{4,5},{5,4},{6,7},{7,6},{8,9},{9,8},{10,11... | collective-permute-start | bytes 1966088 | tf_op jit(solution)/shard_map/ppermute | solution.py:425
  83.4 24.5 %collective-permute-start.9 = (bf16[1,160,1536]{2,1,0:T(8,128)(2,1)S(1)}, bf16[1,160,1536]{2,1,0:T(8,128)(2,1)S(1)}, u32[]{:S(2)}, u32[]{:S(2)}) collective-permute-start(bf16[1,160,1536]{2,1,0:T(8,128)(2,1)S(1)} %copy-done.7), channel_id=1, source_target_pairs={{0,4},{4,0},{8,12},{12,8},{1,5},{5,1},{9,13},{13,9},{2,6},{6,2},{1... | collective-permute-start | bytes 1474568 | tf_op jit(solution)/shard_map/ppermute | solution.py:422
  92.8 23.3 %collective-permute-start.14 = (bf16[1,160,1536]{2,1,0:T(8,128)(2,1)}, bf16[1,160,1536]{2,1,0:T(8,128)(2,1)S(1)}, u32[]{:S(2)}, u32[]{:S(2)}) collective-permute-start(bf16[1,160,1536]{2,1,0:T(8,128)(2,1)} %add_rows.12.refs_3_), channel_id=1, source_target_pairs={{0,8},{4,12},{8,0},{12,4},{1,9},{5,13},{9,1},{13,5},{2,10},{6,14},... | collective-permute-start | bytes 1474568 | tf_op jit(solution)/shard_map/ppermute | solution.py:422
  103.2 4.7 %collective-permute-start.20 = (bf16[1,160,1024]{2,1,0:T(8,128)(2,1)}, bf16[1,160,1024]{2,1,0:T(8,128)(2,1)S(1)}, u32[]{:S(2)}, u32[]{:S(2)}) collective-permute-start(bf16[1,160,1024]{2,1,0:T(8,128)(2,1)} %get-tuple-element.50), channel_id=1, source_target_pairs={{0,1},{1,0},{2,3},{3,2},{4,5},{5,4},{6,7},{7,6},{8,9},{9,8},{10,11... | collective-permute-start | bytes 983048 | tf_op jit(solution)/shard_map/ppermute | solution.py:425
  103.2 4.7 %collective-permute-start.21 = (bf16[1,160,1024]{2,1,0:T(8,128)(2,1)}, bf16[1,160,1024]{2,1,0:T(8,128)(2,1)S(1)}, u32[]{:S(2)}, u32[]{:S(2)}) collective-permute-start(bf16[1,160,1024]{2,1,0:T(8,128)(2,1)} %get-tuple-element.51), channel_id=1, source_target_pairs={{0,1},{1,0},{2,3},{3,2},{4,5},{5,4},{6,7},{7,6},{8,9},{9,8},{10,11... | collective-permute-start | bytes 983048 | tf_op jit(solution)/shard_map/ppermute | solution.py:425
  105.8 18.9 %collective-permute-start.22 = (bf16[160,2048]{1,0:T(8,128)(2,1)S(1)}, bf16[160,2048]{1,0:T(8,128)(2,1)S(1)}, u32[]{:S(2)}, u32[]{:S(2)}) collective-permute-start(bf16[160,2048]{1,0:T(8,128)(2,1)S(1)} %sum_and_rotate.3.refs_0_), channel_id=1, source_target_pairs={{0,1},{1,0},{2,3},{3,2},{4,5},{5,4},{6,7},{7,6},{8,9},{9,8},{10,11... | collective-permute-start | bytes 1966088 | tf_op jit(solution)/shard_map/ppermute | solution.py:425
  108.0 9.5 %copy-start = (bf16[1,160,1024]{2,1,0:T(8,128)(2,1)}, bf16[1,160,1024]{2,1,0:T(8,128)(2,1)S(1)}, u32[]{:S(2)}) copy-start(bf16[1,160,1024]{2,1,0:T(8,128)(2,1)S(1)} %collective-permute-done.20.refs_4_.refs_3_) | copy-start | bytes 983044
  117.5 7.8 %collective-permute-start.23 = (bf16[160,1024]{1,0:T(8,128)(2,1)S(1)}, bf16[160,1024]{1,0:T(8,128)(2,1)S(1)}, u32[]{:S(2)}, u32[]{:S(2)}) collective-permute-start(bf16[160,1024]{1,0:T(8,128)(2,1)S(1)} %sum_and_rotate.4.refs_1_), channel_id=1, source_target_pairs={{0,1},{1,0},{2,3},{3,2},{4,5},{5,4},{6,7},{7,6},{8,9},{9,8},{10,11... | collective-permute-start | bytes 983048 | tf_op jit(solution)/shard_map/ppermute | solution.py:425
  117.7 4.8 %copy-start.11 = (s32[2]{0:T(128)S(1)}, s32[2]{0:T(128)}, u32[]{:S(2)}) copy-start(s32[2]{0:T(128)} %get-tuple-element.63) | copy-start | bytes 28
  117.7 26.2 %collective-permute-start.18 = (bf16[1,160,1024]{2,1,0:T(8,128)(2,1)}, bf16[1,160,1024]{2,1,0:T(8,128)(2,1)}, u32[]{:S(2)}, u32[]{:S(2)}) collective-permute-start(bf16[1,160,1024]{2,1,0:T(8,128)(2,1)} %add_rows.11.refs_6_), channel_id=1, source_target_pairs={{0,4},{4,0},{8,12},{12,8},{1,5},{5,1},{9,13},{13,9},{2,6},{6,2},{1... | collective-permute-start | bytes 983048 | tf_op jit(solution)/shard_map/ppermute | solution.py:422
  118.1 25.8 %collective-permute-start.19 = (bf16[1,160,1024]{2,1,0:T(8,128)(2,1)}, bf16[1,160,1024]{2,1,0:T(8,128)(2,1)}, u32[]{:S(2)}, u32[]{:S(2)}) collective-permute-start(bf16[1,160,1024]{2,1,0:T(8,128)(2,1)} %add_rows.13.refs_4_.refs_2_), channel_id=1, source_target_pairs={{0,8},{4,12},{8,0},{12,4},{1,9},{5,13},{9,1},{13,5},{2,10},{6,14},... | collective-permute-start | bytes 983048 | tf_op jit(solution)/shard_map/ppermute | solution.py:422
  122.5 6.6 %copy-start.5 = (bf16[320,128]{1,0:T(8,128)(2,1)}, bf16[320,128]{1,0:T(8,128)(2,1)S(1)}, u32[]{:S(2)}) copy-start(bf16[320,128]{1,0:T(8,128)(2,1)S(1)} %get-tuple-element.45.own_ref) | copy-start | bytes 245764
  122.5 1.3 collective-permute-start.16
  123.8 14.6 %collective-permute-start.27 = (bf16[1,320,128]{2,1,0:T(8,128)(2,1)S(1)}, bf16[1,320,128]{2,1,0:T(8,128)(2,1)S(1)}, u32[]{:S(2)}, u32[]{:S(2)}) collective-permute-start(bf16[1,320,128]{2,1,0:T(8,128)(2,1)S(1)} %get-tuple-element.54.refs_0_), channel_id=1, source_target_pairs={{0,12},{4,8},{8,4},{12,0},{1,13},{5,9},{9,5},{13,1},{2,14},{6,10},... | collective-permute-start | bytes 245768 | tf_op jit(solution)/shard_map/ppermute | solution.py:422
  124.6 19.1 %collective-permute-start.26 = (bf16[1,320,128]{2,1,0:T(8,128)(2,1)S(1)}, bf16[1,320,128]{2,1,0:T(8,128)(2,1)S(1)}, u32[]{:S(2)}, u32[]{:S(2)}) collective-permute-start(bf16[1,320,128]{2,1,0:T(8,128)(2,1)S(1)} %get-tuple-element.54.refs_0_), channel_id=1, source_target_pairs={{0,8},{4,12},{8,0},{12,4},{1,9},{5,13},{9,1},{13,5},{2,10},{6,14},... | collective-permute-start | bytes 245768 | tf_op jit(solution)/shard_map/ppermute | solution.py:422
  125.4 0.7 copy-start.3
  126.1 17.7 %collective-permute-start.25 = (bf16[1,320,128]{2,1,0:T(8,128)(2,1)S(1)}, bf16[1,320,128]{2,1,0:T(8,128)(2,1)S(1)}, u32[]{:S(2)}, u32[]{:S(2)}) collective-permute-start(bf16[1,320,128]{2,1,0:T(8,128)(2,1)S(1)} %get-tuple-element.54.refs_0_), channel_id=1, source_target_pairs={{0,4},{4,0},{8,12},{12,8},{1,5},{5,1},{9,13},{13,9},{2,6},{6,2},{1... | collective-permute-start | bytes 245768 | tf_op jit(solution)/shard_map/ppermute | solution.py:422
  129.0 0.9 copy-start.6
  130.5 1.0 copy-start.4
  131.4 12.5 %copy-start.1 = (bf16[1,160,1024]{2,1,0:T(8,128)(2,1)S(1)}, bf16[1,160,1024]{2,1,0:T(8,128)(2,1)}, u32[]{:S(2)}) copy-start(bf16[1,160,1024]{2,1,0:T(8,128)(2,1)} %copy-done) | copy-start | bytes 983044
  143.8 2.3 %collective-permute-start.28 = (bf16[4,320,128]{2,1,0:T(8,128)(2,1)S(1)}, bf16[4,320,128]{2,1,0:T(8,128)(2,1)S(1)}, u32[]{:S(2)}, u32[]{:S(2)}) collective-permute-start(bf16[4,320,128]{2,1,0:T(8,128)(2,1)S(1)} %stack_slots.1.own_ref), channel_id=1, source_target_pairs={{0,1},{1,0},{2,3},{3,2},{4,5},{5,4},{6,7},{7,6},{8,9},{9,8},{10,11... | collective-permute-start | bytes 983048 | tf_op jit(solution)/shard_map/ppermute | solution.py:425
  145.5 3.7 %collective-permute-start.24 = (bf16[160,1024]{1,0:T(8,128)(2,1)S(1)}, bf16[160,1024]{1,0:T(8,128)(2,1)S(1)}, u32[]{:S(2)}, u32[]{:S(2)}) collective-permute-start(bf16[160,1024]{1,0:T(8,128)(2,1)S(1)} %sum_and_rotate.5.refs_1_), channel_id=1, source_target_pairs={{0,1},{1,0},{2,3},{3,2},{4,5},{5,4},{6,7},{7,6},{8,9},{9,8},{10,11... | collective-permute-start | bytes 983048 | tf_op jit(solution)/shard_map/ppermute | solution.py:425

commit v13 on v12

--- a/solution.py
+++ b/solution.py
@@ -150,12 +150,21 @@
     )(place, *blocks, *in_hbm([w_key, w_value, *after]))
 
 
+def segments(arrays, start, stop):
+    parts, first = [], 0
+    for x in arrays:
+        low, high = max(start, first) - first, min(stop - first, x.shape[2])
+        if low < high:
+            parts.append((x, high - low, low // (high - low)))
+        first += x.shape[2]
+    return parts
+
+
 def add_kernel(gots, paired, extra, *refs):
     keep_ref, got_refs, out_ref = refs[0], refs[1 : 1 + gots], refs[-1]
     pair_refs = refs[1 + gots : 1 + gots + 2 * paired]
     landed_refs = refs[1 + gots + 2 * paired :][: extra * (1 + paired)]
-    width = got_refs[0].shape[2]
-    cols = gots * width
+    cols = sum(got_ref.shape[2] for got_ref in got_refs)
 
     def total(first, second, landed):
         value = first + second.astype(jnp.float32)
@@ -163,8 +172,10 @@
             value = value + term.astype(jnp.float32)
         return value.astype(out_ref.dtype)
 
-    for t, got_ref in enumerate(got_refs):
-        part = slice(t * width, (t + 1) * width)
+    start = 0
+    for got_ref in got_refs:
+        part = slice(start, start + got_ref.shape[2])
+        start = part.stop
         landed = [landed_refs[0][0, :, part]] if extra else []
         out_ref[0, :, part] = total(keep_ref[0, :, part], got_ref[0], landed)
     if paired:
@@ -174,11 +185,13 @@
 
 def add_rows(first, count, rows, b, keep, gots, start, cols, pair=(), slot=0, landed=(), after=()):
     whole = keep.shape[2]
-    width = cols // len(gots)
-    shift = start // cols if gots[0].shape[2] == whole else 0
     more = pair[0].shape[2] if pair else 0
     keep_spec = pl.BlockSpec((1, rows, cols), lambda s: (first + s, b, start // cols))
-    got_spec = pl.BlockSpec((1, rows, width), lambda s: (first + s, b, shift))
+    gots = segments(gots, start, start + cols)
+
+    def got_spec(width, column):
+        return pl.BlockSpec((1, rows, width), lambda s: (first + s, b, column))
+
     pair_spec = pl.BlockSpec((1, rows, more), lambda s: (slot + s, 0, 0))
     landed_specs = [pl.BlockSpec((1, rows, cols), lambda s: (s, 0, start // cols))]
     if pair:
@@ -188,7 +201,7 @@
         functools.partial(add_kernel, len(gots), len(pair) // 2, len(landed)),
         grid=(count,),
         in_specs=[keep_spec]
-        + [got_spec] * len(gots)
+        + [got_spec(width, column) for _, width, column in gots]
         + [pair_spec] * len(pair)
         + landed_specs
         + [pl.BlockSpec(memory_space=pl.ANY)] * len(after),
@@ -199,7 +212,7 @@
         name="add_rows",
     )(
         *in_hbm([keep]),
-        *gots,
+        *[got for got, _, _ in gots],
         *in_hbm(pair[:1]),
         *pair[1:],
         *(list(landed) * (2 if pair else 1)),
@@ -210,49 +223,50 @@
 
 def rotate_kernel(count, pieces, cos_ref, sin_ref, *refs):
     terms, gots, out_ref = refs[:count], refs[count : count + pieces], refs[-1]
-    total = terms[0][0].astype(jnp.float32)
-    for term in terms[1:]:
-        total = total + term[0].astype(jnp.float32)
     cosine, sine = cos_ref[...], sin_ref[...]
-
-    def write(total):
+    start = 0
+    for got in gots or terms[:1]:
+        cols = slice(start, start + got.shape[2])
+        start = cols.stop
+        total = terms[0][0, :, cols].astype(jnp.float32)
+        for term in terms[1:]:
+            total = total + term[0, :, cols].astype(jnp.float32)
+        if gots:
+            total = total + got[0].astype(jnp.float32)
         for head in range(total.shape[1] // DH):
             part = total[:, head * DH : (head + 1) * DH]
             turned = pltpu.roll(part, DH // 2, axis=1)
-            value = part * cosine + turned * sine
-            out_ref[:, head * DH : (head + 1) * DH] = value.astype(out_ref.dtype)
-
-    if not gots:
-        write(total)
-    for j, got in enumerate(gots):
-
-        @pl.when(pl.program_id(0) == j)
-        def _():
-            write(total + got[0].astype(jnp.float32))
+            value = (part * cosine + turned * sine).astype(out_ref.dtype)
+            out_ref[:, cols.start + head * DH : cols.start + (head + 1) * DH] = value
 
 
 def sum_and_rotate(cosine, sine, terms, gots, cols, after=()):
     rows = cosine.shape[0]
-    slot_of_gots, block_of_gots, shift, gots = gots
-    tile = cols // max(1, len(gots))
     table = pl.BlockSpec((rows, DH), lambda j: (0, 0))
 
-    def block(slot, b, start):
-        return pl.BlockSpec((1, rows, tile), lambda j: (slot, b, start // tile + j))
+    def block(width, slot, column):
+        return pl.BlockSpec((1, rows, width), lambda j: (slot, 0, column))
 
     return pl.pallas_call(
         functools.partial(rotate_kernel, len(terms), len(gots)),
-        grid=(cols // tile,),
+        grid=(1,),
         in_specs=[table, table]
-        + [block(slot, b, start) for _, slot, b, start in terms]
-        + [pl.BlockSpec((1, rows, tile), lambda j: (slot_of_gots, block_of_gots, shift))] * len(gots)
+        + [block(cols, slot, start // cols) for _, slot, start in terms]
+        + [block(width, 0, column) for _, width, column in gots]
         + [pl.BlockSpec(memory_space=pl.ANY)] * len(after),
-        out_specs=pl.BlockSpec((rows, tile), lambda j: (0, j)),
+        out_specs=pl.BlockSpec((rows, cols), lambda j: (0, 0)),
         out_shape=jax.ShapeDtypeStruct((rows, cols), jnp.bfloat16),
         compiler_params=pltpu.CompilerParams(vmem_limit_bytes=VMEM_BYTES),
         cost_estimate=LIGHT,
         name="sum_and_rotate",
-    )(cosine, sine, *in_hbm([terms[0][0]]), *[term[0] for term in terms[1:]], *gots, *after)
+    )(
+        cosine,
+        sine,
+        *in_hbm([terms[0][0]]),
+        *[term[0] for term in terms[1:]],
+        *[got for got, _, _ in gots],
+        *after,
+    )
 
 
 def split_kernel(count, cos_ref, sin_ref, *refs):
@@ -469,28 +483,27 @@
         )
         return keep, [other_core(give) for give in gives], gives[0]
 
-    def rotate(b, p, split, terms, behind):
-        cols = head_cols // split
+    def rotate(b, start, stop, terms, behind):
         table = slice(b * half, (b + 1) * half)
         keep, slot, got = owns[b]
-        added = [(keep, slot, 0, p * cols)] + terms
-        gots = (0, 0, p, got) if len(got) == 1 else (0, 0, 0, got[p : p + 1])
-        turned = sum_and_rotate(cosine[table], sine[table], added, gots, cols, behind)
+        added = [(keep, slot, start)] + terms
+        gots = segments(got, start, stop)
+        turned = sum_and_rotate(cosine[table], sine[table], added, gots, stop - start, behind)
         return turned, other_core(turned)
 
     def add_even(b, start, cols, pair, behind):
         if shards == 2:
             return [], behind
         keep, got = evens[b]
-        each = len(got) * cols // head_cols
-        got = got[start // cols * each :][:each]
         summed = add_rows(
             0, len(even), half, 0, keep, got, start, cols, pair, len(odd), (fars[b],), behind
         )
         terms, first = spread({x: summed[k] for k, x in enumerate(even)})
-        return [(term, 0, 0, 0) for term in terms], (first,)
-
-    last, split = tps - 1, head_cols // tile
+        return [(term, 0, 0) for term in terms], (first,)
+
+    last = tps - 1
+    bounds = [0, head_cols] if tile == head_cols else [0, head_cols * 3 // 4, head_cols]
+    ranges = list(zip(bounds, bounds[1:]))
     placed = in_hbm(blocks[:1]) + blocks[1:]
     evens, owns, fars, terms, pair, after = [], [], [], [], (), ()
     for b, block in enumerate(placed):
@@ -506,7 +519,7 @@
         after = (odd_sent,)
         if b > 0:
             added, after = add_even(b - 1, 0, head_cols, (), after)
-            terms.append([(fars[b - 1], len(odd) - 1, 0, 0)] + added)
+            terms.append([(fars[b - 1], len(odd) - 1, 0)] + added)
             after = (odd_sent,) + after
         if b < last:
             keep, got, given = project(even + [0], [block], head_cols, after, LIGHT, True)
@@ -519,24 +532,24 @@
     near_keep, near_got, given = project([1], placed[last:], tile, after)
     after = (given,)
     parts, behind = [], tuple(term[0] for row in terms for term in row[1:])
-    for p in range(split):
+    for start, stop in ranges:
+        paired = () if start else pair
         near_sent = add_rows(
-            0, 1, half, 0, near_keep, near_got[p : p + 1], p * tile, tile,
-            pair if p == 0 else (), len(odd) - 1, (), after,
+            0, 1, half, 0, near_keep, near_got, start, stop - start, paired, len(odd) - 1, (), after
         )
-        parts.append([(swap(near_sent, 1), 0, 0, 0)])
+        parts.append([(swap(near_sent, 1), 0, 0)])
         after = (near_sent,)
     after = after + behind
-    for p in range(split):
-        added, after = add_even(last, p * tile, tile, pair if p == 0 else (), after)
-        parts[p] += added
+    for part, (start, stop) in zip(parts, ranges):
+        added, after = add_even(last, start, stop - start, () if start else pair, after)
+        part += added
     keep, got, _ = project([0], placed[last:], tile, after, HEAVY)
     owns.append((keep, 0, got))
 
     if fast_pair:
         width = 2 * DH * tps
         pieces = [(array, shards - 1, 0) for array in pair]
-        pieces += [(term, 0, tile) for term, _, _, _ in parts[0]]
+        pieces += [(term, 0, bounds[1]) for term, _, _ in parts[0]]
         key_rot, held = split_and_rotate(cosine, sine, pieces, width, after)
     else:
         x = jnp.concatenate(blocks, axis=0)
@@ -554,23 +567,23 @@
 
         mine = lax.dynamic_slice_in_dim(key_sum, findex * heads_here // group * DH, DH, 1)
         key_own = of_core(mine, rindex)
-        key_rot = sum_and_rotate(cosine, sine, [(key_own[None], 0, 0, 0)], (0, 0, 0, []), DH, after)
+        key_rot = sum_and_rotate(cosine, sine, [(key_own[None], 0, 0)], [], DH, after)
         value_rows = low(jnp.concatenate([of_core(value_sum, rindex), of_core(value_sum, 1 - rindex)]))
 
     order, key_t = prepare(canary_rows, ids, key_rot, other_core(key_rot))
     if not fast_pair:
         values = low(jnp.dot(order, value_rows, preferred_element_type=jnp.float32))
 
-    rotated = [rotate(b, 0, 1, terms[b], after) for b in range(last)]
-    count = heads_here // split
+    rotated = [rotate(b, 0, head_cols, terms[b], after) for b in range(last)]
     scores, mark = (), ()
-    for p in range(split):
-        turned = rotate(last, p, split, parts[p], mark or tuple(owns[last][2][1:]))
-        queries = [(row[0], p * count) for row in rotated] + [(turned[0], 0)]
-        queries += [(row[1], p * count) for row in rotated] + [(turned[1], 0)]
-        behind = in_hbm([values]) if p == split - 1 and p > 0 else ()
+    for p, (start, stop) in enumerate(ranges):
+        turned = rotate(last, start, stop, parts[p], mark or tuple(owns[last][2][1:]))
+        first = start // DH
+        queries = [(row[0], first) for row in rotated] + [(turned[0], 0)]
+        queries += [(row[1], first) for row in rotated] + [(turned[1], 0)]
+        behind = in_hbm([values]) if p > 0 else ()
         *scores, mark = score_heads(
-            order, key_t, heads_here, p * count, count, queries, scores, behind
+            order, key_t, heads_here, first, (stop - start) // DH, queries, scores, behind
         )
         mark = (mark,)
         if fast_pair and p == 0:

time: 155 us -> 151 us (0.974)
  local copies, waits for them, and re-layouts: 4.13 us -> 1.54 us
    unnamed x28 -> x16, local copies, waits for them, and re-layouts: 3.74 us -> 1.15 us
  transfers between devices with their start and end apart: 29 -> 29, of which waited for: 12 -> 11; matrix products, arithmetic and copies ran while one was open for 2% -> 2% of each run, Pallas kernels for 58% -> 61%
where the time goes in v13:
time: 151 us
  Pallas kernels  95 us (63%)
  waiting for transfers between devices  28.8 us (19%)
  starting transfers between devices  22.5 us (15%)
  other arithmetic  2.04 us (1%)
  local copies, waits for them, and re-layouts  1.54 us (1%)
    pallas_call x6, Pallas kernels, project_query(): pl.pallas_call(functools.partial(query_kernel, count, pieces, by_slot), g...  52 us
    ppermute x10, waiting for transfers between devices, swap(): return lax.ppermute(x, 'fsdp', [(i, i ^ bit) for i in range(shards)])  21.8 us
    pallas_call x7, Pallas kernels, add_rows(): pl.pallas_call(functools.partial(add_kernel, len(gots), len(pair) // 2, l...  15.7 us
    ppermute x10, starting transfers between devices, swap(): return lax.ppermute(x, 'fsdp', [(i, i ^ bit) for i in range(shards)])  15.6 us
    pallas_call x2, Pallas kernels, score_heads(): pl.pallas_call(functools.partial(score_kernel, len(queries)), grid=(count...  10.7 us
    pallas_call x1, Pallas kernels, project_pair(): pl.pallas_call(functools.partial(pair_kernel, count), grid_spec=pltpu.Pre...  7.09 us
    ppermute x18, waiting for transfers between devices, other_core(): return lax.ppermute(x, 'rep', [(0, 1), (1, 0)])  7.05 us
    pallas_call x3, Pallas kernels, sum_and_rotate(): pl.pallas_call(functools.partial(rotate_kernel, len(terms), len(gots)), g...  4.77 us
  transfers between devices with their start and end apart: 29, of which 11 were waited for; matrix products, arithmetic and copies ran while one was open for 2% of the time, Pallas kernels for 61%

profile of v13, /device:TPU:0, one launch (start us, length us, event | category | flops | bytes accessed | tf_op | source)
XLA Modules:
  0.0 150.7 jit_solution(7330442188937289626)
XLA Ops:
  0.6 3.0 %collective-permute-start = (bf16[320,2048]{1,0:T(8,128)(2,1)}, bf16[320,2048]{1,0:T(8,128)(2,1)S(1)}, u32[]{:S(2)}, u32[]{:S(2)}) collective-permute-start(bf16[320,2048]{1,0:T(8,128)(2,1)} %refs_0_.5), channel_id=1, source_target_pairs={{0,2},{2,0},{1,3},{3,1},{4,6},{6,4},{5,7},{7,5},{8,10},{10,8},{9,1... | collective-permute-start | bytes 3932168 | tf_op jit(solution)/shard_map/ppermute | solution.py:466
  3.7 11.9 %query_products.6 = (f32[2,160,2048]{2,1,0:T(8,128)}, bf16[2,160,1024]{2,1,0:T(8,128)(2,1)}, bf16[2,160,1024]{2,1,0:T(8,128)(2,1)}) custom-call(s32[3]{0:T(128)S(1)} %pad_add_fusion.2.place_ref, bf16[320,2048]{1,0:T(8,128)(2,1)} %refs_0_.5, bf16[2048,8192]{1,0:T(8,128)(2,1)} %refs_1_.11), custom_call_target="tpu_custom_call" | custom-call | flops 1000 | bytes 1000 | tf_op jit(solution)/shard_map/query_products/pallas_call | solution.py:87
  15.6 0.5 collective-permute-start.2
  16.1 1.8 %collective-permute-done.1.refs_1_ = bf16[2,160,1024]{2,1,0:T(8,128)(2,1)S(1)} collective-permute-done((bf16[2,160,1024]{2,1,0:T(8,128)(2,1)}, bf16[2,160,1024]{2,1,0:T(8,128)(2,1)S(1)}, u32[]{:S(2)}, u32[]{:S(2)}) %collective-permute-start.1) | collective-permute-done | bytes 655392 | tf_op jit(solution)/shard_map/ppermute | solution.py:439
  17.9 0.9 collective-permute-done.2.refs_2_
  18.9 2.7 %add_rows.7.refs_2_ = bf16[2,160,2048]{2,1,0:T(8,128)(2,1)} custom-call(f32[2,160,2048]{2,1,0:T(8,128)} %get-tuple-element.29.refs_0_, bf16[2,160,1024]{2,1,0:T(8,128)(2,1)S(1)} %collective-permute-done.1.refs_1_, bf16[2,160,1024]{2,1,0:T(8,128)(2,1)S(1)} %collective-permute-done.2.refs_2_), custom_call_target="tpu_custom_call" | custom-call | flops 1000 | bytes 1000 | tf_op jit(solution)/shard_map/add_rows/pallas_call | solution.py:200
  21.5 1.6 %collective-permute-start.7 = (bf16[2,160,2048]{2,1,0:T(8,128)(2,1)}, bf16[2,160,2048]{2,1,0:T(8,128)(2,1)}, u32[]{:S(2)}, u32[]{:S(2)}) collective-permute-start(bf16[2,160,2048]{2,1,0:T(8,128)(2,1)} %add_rows.7.refs_2_), channel_id=1, source_target_pairs={{0,4},{4,0},{8,12},{12,8},{1,5},{5,1},{9,13},{13,9},{2,6},{6,2},{1... | collective-permute-start | bytes 3932168 | tf_op jit(solution)/shard_map/ppermute | solution.py:436
  23.2 11.8 %query_products.7 = (f32[2,160,2048]{2,1,0:T(8,128)}, bf16[1,160,2048]{2,1,0:T(8,128)(2,1)}, bf16[1,160,2048]{2,1,0:T(8,128)(2,1)}) custom-call(s32[3]{0:T(128)S(1)} %pad_add_fusion.1.place_ref, bf16[320,2048]{1,0:T(8,128)(2,1)} %refs_0_.5, bf16[2048,8192]{1,0:T(8,128)(2,1)} %refs_1_.11, bf16[2,160,2048]{2,1,0:T(8,128)(2,1)} %add_rows.7.refs_2_), custom_call_target="tpu_custom_call" | custom-call | flops 1000 | bytes 1000 | tf_op jit(solution)/shard_map/query_products/pallas_call | solution.py:87
  35.0 7.1 %key_value_products.1 = (f32[4,160,512]{2,1,0:T(8,128)}, bf16[4,160,512]{2,1,0:T(8,128)(2,1)}) custom-call(s32[5]{0:T(128)S(1)} %stack.62.place_ref, bf16[320,2048]{1,0:T(8,128)(2,1)} %refs_0_.5, bf16[320,2048]{1,0:T(8,128)(2,1)S(1)} %collective-permute-done.refs_1_.refs_0_, bf16[2048,512]{1,0:T(8,128)(2,1)} %refs_2_.1, bf16[2048,512]{1,0:T(8,128)(2,1)} %refs_3_.1, ...), custom_call_target="tpu_custom_call" | custom-call | flops 1000 | bytes 1000 | tf_op jit(solution)/shard_map/key_value_products/pallas_call | solution.py:132
  42.1 0.5 collective-permute-start.6
  42.7 7.0 %query_products.8 = (f32[1,160,2048]{2,1,0:T(8,128)}, bf16[1,160,1024]{2,1,0:T(8,128)(2,1)}, bf16[1,160,1024]{2,1,0:T(8,128)(2,1)}) custom-call(s32[2]{0:T(128)S(1)} %get-tuple-element.66.place_ref, bf16[320,2048]{1,0:T(8,128)(2,1)S(1)} %collective-permute-done.refs_1_.refs_0_, bf16[2048,8192]{1,0:T(8,128)(2,1)} %refs_1_.11, ...), custom_call_target="tpu_custom_call" | custom-call | flops 1000 | bytes 1000 | tf_op jit(solution)/shard_map/query_products/pallas_call | solution.py:87
  50.3 1.3 collective-permute-done.4.refs_1_
  52.0 2.4 %add_rows.8.refs_3_.refs_2_ = bf16[1,160,2560]{2,1,0:T(8,128)(2,1)} custom-call(f32[1,160,2048]{2,1,0:T(8,128)} %get-tuple-element.35.refs_0_, bf16[1,160,1024]{2,1,0:T(8,128)(2,1)S(1)} %collective-permute-done.4.refs_1_, bf16[1,160,1024]{2,1,0:T(8,128)(2,1)S(1)} %collective-permute-done.5.refs_2_, f32[4,160,512]{2,1,0:T(8,128)} %get-tuple-element.33.refs_3_.refs_0_, ...), custom_call_target="tpu_custom_call" | custom-call | flops 1000 | bytes 1000 | tf_op jit(solution)/shard_map/add_rows/pallas_call | solution.py:200
  54.9 2.5 %add_rows.9.refs_3_ = bf16[1,160,2048]{2,1,0:T(8,128)(2,1)} custom-call(f32[2,160,2048]{2,1,0:T(8,128)} %get-tuple-element.38.refs_0_, bf16[1,160,2048]{2,1,0:T(8,128)(2,1)S(1)} %collective-permute-done.6.refs_1_, bf16[2,160,2048]{2,1,0:T(8,128)(2,1)} %collective-permute-done.7.refs_2_.refs_1_, bf16[1,160,2560]{2,1,0:T(8,128)(2,1)} %add_rows.8.refs_3_.refs_2_), custom_call_target="tpu_custom_call" | custom-call | flops 1000 | bytes 1000 | tf_op jit(solution)/shard_map/add_rows/pallas_call | solution.py:200
  57.4 2.6 %collective-permute-start.14 = (bf16[1,160,2048]{2,1,0:T(8,128)(2,1)}, bf16[1,160,2048]{2,1,0:T(8,128)(2,1)S(1)}, u32[]{:S(2)}, u32[]{:S(2)}) collective-permute-start(bf16[1,160,2048]{2,1,0:T(8,128)(2,1)} %add_rows.9.refs_3_), channel_id=1, source_target_pairs={{0,8},{4,12},{8,0},{12,4},{1,9},{5,13},{9,1},{13,5},{2,10},{6,14},... | collective-permute-start | bytes 1966088 | tf_op jit(solution)/shard_map/ppermute | solution.py:436
  60.0 1.1 copy-done.3
  61.1 7.1 %query_products.9 = (f32[1,160,2048]{2,1,0:T(8,128)}, bf16[1,160,1024]{2,1,0:T(8,128)(2,1)}, bf16[1,160,1024]{2,1,0:T(8,128)(2,1)}) custom-call(s32[2]{0:T(128)S(1)} %pad_add_fusion.4.place_ref, bf16[320,2048]{1,0:T(8,128)(2,1)S(1)} %collective-permute-done.refs_1_.refs_0_, bf16[2048,8192]{1,0:T(8,128)(2,1)} %refs_1_.11, ...), custom_call_target="tpu_custom_call" | custom-call | flops 99999997952 | bytes 100000000 | tf_op jit(solution)/shard_map/query_products/pallas_call | solution.py:87
  68.3 7.1 %query_products.10 = (f32[1,160,2048]{2,1,0:T(8,128)}, bf16[1,160,1024]{2,1,0:T(8,128)(2,1)}, bf16[1,160,1024]{2,1,0:T(8,128)(2,1)}) custom-call(s32[2]{0:T(128)S(1)} %get-tuple-element.65.place_ref, bf16[320,2048]{1,0:T(8,128)(2,1)S(1)} %collective-permute-done.refs_1_.refs_0_, bf16[2048,8192]{1,0:T(8,128)(2,1)} %refs_1_.11, ...), custom_call_target="tpu_custom_call" | custom-call | flops 1000 | bytes 1000 | tf_op jit(solution)/shard_map/query_products/pallas_call | solution.py:87
  75.5 0.5 collective-permute-start.11
  76.1 1.2 collective-permute-done.9.refs_2_.refs_1_
  77.8 1.3 collective-permute-done.8.refs_1_
  79.2 2.4 %add_rows.10.refs_2_ = bf16[1,160,2048]{2,1,0:T(8,128)(2,1)} custom-call(f32[1,160,2048]{2,1,0:T(8,128)} %get-tuple-element.40.refs_0_, bf16[1,160,1024]{2,1,0:T(8,128)(2,1)S(1)} %collective-permute-done.8.refs_1_, bf16[1,160,1024]{2,1,0:T(8,128)(2,1)} %collective-permute-done.9.refs_2_.refs_1_, f32[4,160,512]{2,1,0:T(8,128)} %get-tuple-element.33.refs_3_.refs_0_, ...), custom_call_target="tpu_custom_call" | custom-call | flops 1000 | bytes 1000 | tf_op jit(solution)/shard_map/add_rows/pallas_call | solution.py:200
  81.7 1.8 %add_rows.11.refs_7_ = bf16[1,160,512]{2,1,0:T(8,128)(2,1)} custom-call(f32[1,160,2048]{2,1,0:T(8,128)} %get-tuple-element.40.refs_0_, bf16[1,160,1024]{2,1,0:T(8,128)(2,1)} %collective-permute-done.9.refs_2_.refs_1_, bf16[1,160,2048]{2,1,0:T(8,128)(2,1)} %add_rows.10.refs_2_), custom_call_target="tpu_custom_call" | custom-call | flops 1000 | bytes 1000 | tf_op jit(solution)/shard_map/add_rows/pallas_call | solution.py:200
  83.5 1.6 %collective-permute-start.10 = (bf16[1,160,2048]{2,1,0:T(8,128)(2,1)S(1)}, bf16[1,160,2048]{2,1,0:T(8,128)(2,1)S(1)}, u32[]{:S(2)}, u32[]{:S(2)}) collective-permute-start(bf16[1,160,2048]{2,1,0:T(8,128)(2,1)S(1)} %copy-done.4), channel_id=1, source_target_pairs={{0,4},{4,0},{8,12},{12,8},{1,5},{5,1},{9,13},{13,9},{2,6},{6,2},{1... | collective-permute-start | bytes 1966088 | tf_op jit(solution)/shard_map/ppermute | solution.py:436
  85.1 2.9 %collective-permute-done.14.refs_8_.refs_2_ = bf16[1,160,2048]{2,1,0:T(8,128)(2,1)S(1)} collective-permute-done((bf16[1,160,2048]{2,1,0:T(8,128)(2,1)}, bf16[1,160,2048]{2,1,0:T(8,128)(2,1)S(1)}, u32[]{:S(2)}, u32[]{:S(2)}) %collective-permute-start.14) | collective-permute-done | bytes 655392 | tf_op jit(solution)/shard_map/ppermute | solution.py:436
  87.9 1.9 %collective-permute-done.13.refs_5_.refs_6_.refs_2_ = bf16[1,160,2560]{2,1,0:T(8,128)(2,1)S(1)} collective-permute-done((bf16[1,160,2560]{2,1,0:T(8,128)(2,1)}, bf16[1,160,2560]{2,1,0:T(8,128)(2,1)S(1)}, u32[]{:S(2)}, u32[]{:S(2)}) %collective-permute-start.13) | collective-permute-done | bytes 819232 | tf_op jit(solution)/shard_map/ppermute | solution.py:436
  89.8 2.3 %add_rows.12.refs_3_ = bf16[1,160,2048]{2,1,0:T(8,128)(2,1)} custom-call(f32[1,160,2048]{2,1,0:T(8,128)} %get-tuple-element.43.refs_0_, bf16[1,160,1024]{2,1,0:T(8,128)(2,1)S(1)} %collective-permute-done.11.refs_1_, bf16[1,160,1024]{2,1,0:T(8,128)(2,1)S(1)} %collective-permute-done.12.refs_2_.refs_1_, f32[4,160,512]{2,1,0:T(8,128)} %get-tuple-element.33.refs_3_.refs_0_, ...), custom_call_target="tpu_custom_call" | custom-call | flops 1000 | bytes 1000 | tf_op jit(solution)/shard_map/add_rows/pallas_call | solution.py:200
  92.1 1.4 collective-permute-start.15
  93.5 1.7 %add_rows.13.refs_4_.refs_2_ = bf16[1,160,512]{2,1,0:T(8,128)(2,1)} custom-call(f32[1,160,2048]{2,1,0:T(8,128)} %get-tuple-element.43.refs_0_, bf16[1,160,1024]{2,1,0:T(8,128)(2,1)S(1)} %collective-permute-done.12.refs_2_.refs_1_, bf16[1,160,2560]{2,1,0:T(8,128)(2,1)S(1)} %collective-permute-done.13.refs_5_.refs_6_.refs_2_, ...), custom_call_target="tpu_custom_call" | custom-call | flops 1000 | bytes 1000 | tf_op jit(solution)/shard_map/add_rows/pallas_call | solution.py:200
  95.2 7.1 %query_products.11 = (f32[1,160,2048]{2,1,0:T(8,128)}, bf16[1,160,1024]{2,1,0:T(8,128)(2,1)}, bf16[1,160,1024]{2,1,0:T(8,128)(2,1)}) custom-call(s32[2]{0:T(128)S(1)} %pad_add_fusion.6.place_ref, bf16[320,2048]{1,0:T(8,128)(2,1)S(1)} %collective-permute-done.refs_1_.refs_0_, bf16[2048,8192]{1,0:T(8,128)(2,1)} %refs_1_.11, ...), custom_call_target="tpu_custom_call" | custom-call | flops 99999997952 | bytes 100000000 | tf_op jit(solution)/shard_map/query_products/pallas_call | solution.py:87
  102.3 0.5 collective-permute-start.21
  102.8 0.6 fusion.4
  103.7 2.1 %sum_and_rotate.3.refs_0_ = bf16[160,2048]{1,0:T(8,128)(2,1)S(1)} custom-call(f32[160,128]{1,0:T(8,128)S(1)} %get-tuple-element.59.cos_ref, f32[160,128]{1,0:T(8,128)S(1)} %get-tuple-element.57.sin_ref, f32[2,160,2048]{2,1,0:T(8,128)} %get-tuple-element.38.refs_0_, bf16[2,160,2048]{2,1,0:T(8,128)(2,1)} %collective-permute-done.7.refs_2_.refs_1_, ...), custom_call_target="tpu_custom_call" | custom-call | flops 1000 | bytes 1000 | tf_op jit(solution)/shard_map/sum_and_rotate/pallas_call | solution.py:250
  105.9 7.9 %collective-permute-done.10.refs_2_.refs_1_ = bf16[1,160,2048]{2,1,0:T(8,128)(2,1)S(1)} collective-permute-done((bf16[1,160,2048]{2,1,0:T(8,128)(2,1)S(1)}, bf16[1,160,2048]{2,1,0:T(8,128)(2,1)S(1)}, u32[]{:S(2)}, u32[]{:S(2)}) %collective-permute-start.10) | collective-permute-done | bytes 655392 | tf_op jit(solution)/shard_map/ppermute | solution.py:436
  113.9 8.6 %collective-permute-done.15.refs_3_.refs_2_ = bf16[1,160,2048]{2,1,0:T(8,128)(2,1)S(1)} collective-permute-done((bf16[1,160,2048]{2,1,0:T(8,128)(2,1)}, bf16[1,160,2048]{2,1,0:T(8,128)(2,1)S(1)}, u32[]{:S(2)}, u32[]{:S(2)}) %collective-permute-start.15) | collective-permute-done | bytes 655392 | tf_op jit(solution)/shard_map/ppermute | solution.py:436
  122.4 1.6 %sum_and_rotate.4.refs_1_ = bf16[160,1536]{1,0:T(8,128)(2,1)S(1)} custom-call(f32[160,128]{1,0:T(8,128)S(1)} %get-tuple-element.58.cos_ref, f32[160,128]{1,0:T(8,128)S(1)} %get-tuple-element.56.sin_ref, f32[1,160,2048]{2,1,0:T(8,128)} %get-tuple-element.49.refs_0_, bf16[1,160,2048]{2,1,0:T(8,128)(2,1)S(1)} %collective-permute-done.10.refs_2_.refs_1_, ...), custom_call_target="tpu_custom_call" | custom-call | flops 1000 | bytes 1000 | tf_op jit(solution)/shard_map/sum_and_rotate/pallas_call | solution.py:250
  124.3 1.1 split_and_rotate.1
  125.5 0.6 collective-permute-start.16
  126.3 3.0 %collective-permute-start.27 = (bf16[1,320,128]{2,1,0:T(8,128)(2,1)S(1)}, bf16[1,320,128]{2,1,0:T(8,128)(2,1)S(1)}, u32[]{:S(2)}, u32[]{:S(2)}) collective-permute-start(bf16[1,320,128]{2,1,0:T(8,128)(2,1)S(1)} %get-tuple-element.54.refs_0_), channel_id=1, source_target_pairs={{0,12},{4,8},{8,4},{12,0},{1,13},{5,9},{9,5},{13,1},{2,14},{6,10},... | collective-permute-start | bytes 245768 | tf_op jit(solution)/shard_map/ppermute | solution.py:436
  129.3 1.4 collective-permute-start.25
  130.8 0.6 order_and_keys.1
  131.4 0.7 collective-permute-start.18
  132.1 2.9 %collective-permute-start.19 = (bf16[1,160,512]{2,1,0:T(8,128)(2,1)S(1)}, bf16[1,160,512]{2,1,0:T(8,128)(2,1)S(1)}, u32[]{:S(2)}, u32[]{:S(2)}) collective-permute-start(bf16[1,160,512]{2,1,0:T(8,128)(2,1)S(1)} %copy-done), channel_id=1, source_target_pairs={{0,8},{4,12},{8,0},{12,4},{1,9},{5,13},{9,1},{13,5},{2,10},{6,14},... | collective-permute-start | bytes 491528 | tf_op jit(solution)/shard_map/ppermute | solution.py:436
  135.0 7.4 %score_heads.2 = (bf16[1,16,640,640]{3,2,1,0:T(8,128)(2,1)}, f32[8,128]{1,0:T(8,128)S(1)}) custom-call(bf16[640,640]{1,0:T(8,128)(2,1)S(1)} %get-tuple-element.46.order_ref, bf16[128,640]{1,0:T(8,128)(2,1)S(1)} %get-tuple-element.47.key_t_ref, bf16[160,2048]{1,0:T(8,128)(2,1)S(1)} %sum_and_rotate.3.refs_0_, bf16[160,1536]{1,0:T(8,128)(2,1)S(1)} %sum_and_rotate.4.refs_1_, ...), custom_call_target="tpu_custom_call" | custom-call | flops 1000 | bytes 1000 | tf_op jit(solution)/shard_map/score_heads/pallas_call | solution.py:397
  142.5 0.5 collective-permute-done.18.refs_1_
  143.1 1.1 sum_and_rotate.5.refs_1_
  144.4 3.1 %order_values.1.refs_5_ = bf16[640,512]{1,0:T(8,128)(2,1)} custom-call(s32[4]{0:T(128)S(1)} %pad_add_fusion.7.place_ref, bf16[640,640]{1,0:T(8,128)(2,1)S(1)} %get-tuple-element.46.order_ref, bf16[4,320,128]{2,1,0:T(8,128)(2,1)S(1)} %stack_slots.1.own_ref, bf16[4,320,128]{2,1,0:T(8,128)(2,1)S(1)} %collective-permute-done.28.other_ref), custom_call_target="tpu_custom_call" | custom-call | tf_op jit(solution)/shard_map/order_values/pallas_call | solution.py:364
  147.4 3.2 %score_heads.3 = (bf16[1,16,640,640]{3,2,1,0:T(8,128)(2,1)}, f32[8,128]{1,0:T(8,128)}) custom-call(bf16[640,640]{1,0:T(8,128)(2,1)S(1)} %get-tuple-element.46.order_ref, bf16[128,640]{1,0:T(8,128)(2,1)S(1)} %get-tuple-element.47.key_t_ref, bf16[160,2048]{1,0:T(8,128)(2,1)S(1)} %sum_and_rotate.3.refs_0_, ...), custom_call_target="tpu_custom_call", output_to_operand_aliasing={{0}: (6, {})} | custom-call | flops 1000 | bytes 1000 | tf_op jit(solution)/shard_map/score_heads/pallas_call | solution.py:397
  (72 shorter events, 4.1 us)
Async XLA Ops:
  0.6 34.4 %collective-permute-start = (bf16[320,2048]{1,0:T(8,128)(2,1)}, bf16[320,2048]{1,0:T(8,128)(2,1)S(1)}, u32[]{:S(2)}, u32[]{:S(2)}) collective-permute-start(bf16[320,2048]{1,0:T(8,128)(2,1)} %refs_0_.5), channel_id=1, source_target_pairs={{0,2},{2,0},{1,3},{3,1},{4,6},{6,4},{5,7},{7,5},{8,10},{10,8},{9,1... | collective-permute-start | bytes 3932168 | tf_op jit(solution)/shard_map/ppermute | solution.py:466
  15.6 2.3 %collective-permute-start.1 = (bf16[2,160,1024]{2,1,0:T(8,128)(2,1)}, bf16[2,160,1024]{2,1,0:T(8,128)(2,1)S(1)}, u32[]{:S(2)}, u32[]{:S(2)}) collective-permute-start(bf16[2,160,1024]{2,1,0:T(8,128)(2,1)} %get-tuple-element.30), channel_id=1, source_target_pairs={{0,1},{1,0},{2,3},{3,2},{4,5},{5,4},{6,7},{7,6},{8,9},{9,8},{10,11... | collective-permute-start | bytes 1966088 | tf_op jit(solution)/shard_map/ppermute | solution.py:439
  15.6 3.2 %collective-permute-start.2 = (bf16[2,160,1024]{2,1,0:T(8,128)(2,1)}, bf16[2,160,1024]{2,1,0:T(8,128)(2,1)S(1)}, u32[]{:S(2)}, u32[]{:S(2)}) collective-permute-start(bf16[2,160,1024]{2,1,0:T(8,128)(2,1)} %get-tuple-element.31), channel_id=1, source_target_pairs={{0,1},{1,0},{2,3},{3,2},{4,5},{5,4},{6,7},{7,6},{8,9},{9,8},{10,11... | collective-permute-start | bytes 1966088 | tf_op jit(solution)/shard_map/ppermute | solution.py:439
  21.5 33.4 %collective-permute-start.7 = (bf16[2,160,2048]{2,1,0:T(8,128)(2,1)}, bf16[2,160,2048]{2,1,0:T(8,128)(2,1)}, u32[]{:S(2)}, u32[]{:S(2)}) collective-permute-start(bf16[2,160,2048]{2,1,0:T(8,128)(2,1)} %add_rows.7.refs_2_), channel_id=1, source_target_pairs={{0,4},{4,0},{8,12},{12,8},{1,5},{5,1},{9,13},{13,9},{2,6},{6,2},{1... | collective-permute-start | bytes 3932168 | tf_op jit(solution)/shard_map/ppermute | solution.py:436
  42.1 9.9 %collective-permute-start.3 = (bf16[4,160,512]{2,1,0:T(8,128)(2,1)}, bf16[4,160,512]{2,1,0:T(8,128)(2,1)S(1)}, u32[]{:S(2)}, u32[]{:S(2)}) collective-permute-start(bf16[4,160,512]{2,1,0:T(8,128)(2,1)} %get-tuple-element.34.refs_2_), channel_id=1, source_target_pairs={{0,1},{1,0},{2,3},{3,2},{4,5},{5,4},{6,7},{7,6},{8,9},{9,8},{10,11... | collective-permute-start | bytes 1966088 | tf_op jit(solution)/shard_map/ppermute | solution.py:439
  42.1 12.8 %collective-permute-start.6 = (bf16[1,160,2048]{2,1,0:T(8,128)(2,1)}, bf16[1,160,2048]{2,1,0:T(8,128)(2,1)S(1)}, u32[]{:S(2)}, u32[]{:S(2)}) collective-permute-start(bf16[1,160,2048]{2,1,0:T(8,128)(2,1)} %get-tuple-element.32.refs_4_), channel_id=1, source_target_pairs={{0,1},{1,0},{2,3},{3,2},{4,5},{5,4},{6,7},{7,6},{8,9},{9,8},{10,11... | collective-permute-start | bytes 1966088 | tf_op jit(solution)/shard_map/ppermute | solution.py:439
  49.7 1.8 %collective-permute-start.4 = (bf16[1,160,1024]{2,1,0:T(8,128)(2,1)}, bf16[1,160,1024]{2,1,0:T(8,128)(2,1)S(1)}, u32[]{:S(2)}, u32[]{:S(2)}) collective-permute-start(bf16[1,160,1024]{2,1,0:T(8,128)(2,1)} %get-tuple-element.36), channel_id=1, source_target_pairs={{0,1},{1,0},{2,3},{3,2},{4,5},{5,4},{6,7},{7,6},{8,9},{9,8},{10,11... | collective-permute-start | bytes 983048 | tf_op jit(solution)/shard_map/ppermute | solution.py:439
  49.8 2.3 %collective-permute-start.5 = (bf16[1,160,1024]{2,1,0:T(8,128)(2,1)}, bf16[1,160,1024]{2,1,0:T(8,128)(2,1)S(1)}, u32[]{:S(2)}, u32[]{:S(2)}) collective-permute-start(bf16[1,160,1024]{2,1,0:T(8,128)(2,1)} %get-tuple-element.37), channel_id=1, source_target_pairs={{0,1},{1,0},{2,3},{3,2},{4,5},{5,4},{6,7},{7,6},{8,9},{9,8},{10,11... | collective-permute-start | bytes 983048 | tf_op jit(solution)/shard_map/ppermute | solution.py:439
  54.5 35.3 %collective-permute-start.13 = (bf16[1,160,2560]{2,1,0:T(8,128)(2,1)}, bf16[1,160,2560]{2,1,0:T(8,128)(2,1)S(1)}, u32[]{:S(2)}, u32[]{:S(2)}) collective-permute-start(bf16[1,160,2560]{2,1,0:T(8,128)(2,1)} %add_rows.8.refs_3_.refs_2_), channel_id=1, source_target_pairs={{0,4},{4,0},{8,12},{12,8},{1,5},{5,1},{9,13},{13,9},{2,6},{6,2},{1... | collective-permute-start | bytes 2457608 | tf_op jit(solution)/shard_map/ppermute | solution.py:436
  57.4 30.5 %collective-permute-start.14 = (bf16[1,160,2048]{2,1,0:T(8,128)(2,1)}, bf16[1,160,2048]{2,1,0:T(8,128)(2,1)S(1)}, u32[]{:S(2)}, u32[]{:S(2)}) collective-permute-start(bf16[1,160,2048]{2,1,0:T(8,128)(2,1)} %add_rows.9.refs_3_), channel_id=1, source_target_pairs={{0,8},{4,12},{8,0},{12,4},{1,9},{5,13},{9,1},{13,5},{2,10},{6,14},... | collective-permute-start | bytes 1966088 | tf_op jit(solution)/shard_map/ppermute | solution.py:436
  60.0 1.1 copy-start.3
  68.3 9.2 %copy-start.5 = (s32[640]{0:T(1024)S(1)}, s32[640]{0:T(1024)}, u32[]{:S(2)}) copy-start(s32[640]{0:T(1024)} %param.10) | copy-start | bytes 7684
  68.3 9.2 %copy-start.6 = (s32[640]{0:T(1024)S(1)}, s32[640]{0:T(1024)}, u32[]{:S(2)}) copy-start(s32[640]{0:T(1024)} %param.11) | copy-start | bytes 7684
  75.4 2.0 %collective-permute-start.9 = (bf16[1,160,1024]{2,1,0:T(8,128)(2,1)}, bf16[1,160,1024]{2,1,0:T(8,128)(2,1)}, u32[]{:S(2)}, u32[]{:S(2)}) collective-permute-start(bf16[1,160,1024]{2,1,0:T(8,128)(2,1)} %get-tuple-element.42), channel_id=1, source_target_pairs={{0,1},{1,0},{2,3},{3,2},{4,5},{5,4},{6,7},{7,6},{8,9},{9,8},{10,11... | collective-permute-start | bytes 983048 | tf_op jit(solution)/shard_map/ppermute | solution.py:439
  75.5 9.5 %collective-permute-start.11 = (bf16[1,160,1024]{2,1,0:T(8,128)(2,1)}, bf16[1,160,1024]{2,1,0:T(8,128)(2,1)S(1)}, u32[]{:S(2)}, u32[]{:S(2)}) collective-permute-start(bf16[1,160,1024]{2,1,0:T(8,128)(2,1)} %get-tuple-element.39.refs_2_), channel_id=1, source_target_pairs={{0,1},{1,0},{2,3},{3,2},{4,5},{5,4},{6,7},{7,6},{8,9},{9,8},{10,11... | collective-permute-start | bytes 983048 | tf_op jit(solution)/shard_map/ppermute | solution.py:439
  76.1 7.4 %collective-permute-start.12 = (bf16[1,160,1024]{2,1,0:T(8,128)(2,1)}, bf16[1,160,1024]{2,1,0:T(8,128)(2,1)S(1)}, u32[]{:S(2)}, u32[]{:S(2)}) collective-permute-start(bf16[1,160,1024]{2,1,0:T(8,128)(2,1)} %get-tuple-element.44), channel_id=1, source_target_pairs={{0,1},{1,0},{2,3},{3,2},{4,5},{5,4},{6,7},{7,6},{8,9},{9,8},{10,11... | collective-permute-start | bytes 983048 | tf_op jit(solution)/shard_map/ppermute | solution.py:439
  77.3 1.8 %collective-permute-start.8 = (bf16[1,160,1024]{2,1,0:T(8,128)(2,1)}, bf16[1,160,1024]{2,1,0:T(8,128)(2,1)S(1)}, u32[]{:S(2)}, u32[]{:S(2)}) collective-permute-start(bf16[1,160,1024]{2,1,0:T(8,128)(2,1)} %get-tuple-element.41.refs_5_), channel_id=1, source_target_pairs={{0,1},{1,0},{2,3},{3,2},{4,5},{5,4},{6,7},{7,6},{8,9},{9,8},{10,11... | collective-permute-start | bytes 983048 | tf_op jit(solution)/shard_map/ppermute | solution.py:439
  79.2 2.4 %copy-start.7 = (bf16[1,160,2048]{2,1,0:T(8,128)(2,1)S(1)}, bf16[1,160,2048]{2,1,0:T(8,128)(2,1)}, u32[]{:S(2)}) copy-start(bf16[1,160,2048]{2,1,0:T(8,128)(2,1)} %get-tuple-element.48) | copy-start | bytes 1966084
  81.6 1.9 %copy-start.4 = (bf16[1,160,2048]{2,1,0:T(8,128)(2,1)S(1)}, bf16[1,160,2048]{2,1,0:T(8,128)(2,1)}, u32[]{:S(2)}) copy-start(bf16[1,160,2048]{2,1,0:T(8,128)(2,1)} %add_rows.10.refs_2_) | copy-start | bytes 1966084
  81.6 22.2 %collective-permute-start.17 = (bf16[1,160,2048]{2,1,0:T(8,128)(2,1)S(1)}, bf16[1,160,2048]{2,1,0:T(8,128)(2,1)S(1)}, u32[]{:S(2)}, u32[]{:S(2)}) collective-permute-start(bf16[1,160,2048]{2,1,0:T(8,128)(2,1)S(1)} %copy-done.7), channel_id=1, source_target_pairs={{0,1},{1,0},{2,3},{3,2},{4,5},{5,4},{6,7},{7,6},{8,9},{9,8},{10,11... | collective-permute-start | bytes 1966088 | tf_op jit(solution)/shard_map/ppermute | solution.py:439
  83.5 30.4 %collective-permute-start.10 = (bf16[1,160,2048]{2,1,0:T(8,128)(2,1)S(1)}, bf16[1,160,2048]{2,1,0:T(8,128)(2,1)S(1)}, u32[]{:S(2)}, u32[]{:S(2)}) collective-permute-start(bf16[1,160,2048]{2,1,0:T(8,128)(2,1)S(1)} %copy-done.4), channel_id=1, source_target_pairs={{0,4},{4,0},{8,12},{12,8},{1,5},{5,1},{9,13},{13,9},{2,6},{6,2},{1... | collective-permute-start | bytes 1966088 | tf_op jit(solution)/shard_map/ppermute | solution.py:436
  92.1 30.3 %collective-permute-start.15 = (bf16[1,160,2048]{2,1,0:T(8,128)(2,1)}, bf16[1,160,2048]{2,1,0:T(8,128)(2,1)S(1)}, u32[]{:S(2)}, u32[]{:S(2)}) collective-permute-start(bf16[1,160,2048]{2,1,0:T(8,128)(2,1)} %add_rows.12.refs_3_), channel_id=1, source_target_pairs={{0,8},{4,12},{8,0},{12,4},{1,9},{5,13},{9,1},{13,5},{2,10},{6,14},... | collective-permute-start | bytes 1966088 | tf_op jit(solution)/shard_map/ppermute | solution.py:436
  102.3 1.5 copy-start
  102.3 11.6 %collective-permute-start.20 = (bf16[1,160,1024]{2,1,0:T(8,128)(2,1)}, bf16[1,160,1024]{2,1,0:T(8,128)(2,1)S(1)}, u32[]{:S(2)}, u32[]{:S(2)}) collective-permute-start(bf16[1,160,1024]{2,1,0:T(8,128)(2,1)} %get-tuple-element.50), channel_id=1, source_target_pairs={{0,1},{1,0},{2,3},{3,2},{4,5},{5,4},{6,7},{7,6},{8,9},{9,8},{10,11... | collective-permute-start | bytes 983048 | tf_op jit(solution)/shard_map/ppermute | solution.py:439
  102.3 11.5 %collective-permute-start.21 = (bf16[1,160,1024]{2,1,0:T(8,128)(2,1)}, bf16[1,160,1024]{2,1,0:T(8,128)(2,1)S(1)}, u32[]{:S(2)}, u32[]{:S(2)}) collective-permute-start(bf16[1,160,1024]{2,1,0:T(8,128)(2,1)} %get-tuple-element.51), channel_id=1, source_target_pairs={{0,1},{1,0},{2,3},{3,2},{4,5},{5,4},{6,7},{7,6},{8,9},{9,8},{10,11... | collective-permute-start | bytes 983048 | tf_op jit(solution)/shard_map/ppermute | solution.py:439
  103.7 18.7 %copy-start.1 = (f32[160,128]{1,0:T(8,128)}, f32[160,128]{1,0:T(8,128)S(1)}, u32[]{:S(2)}) copy-start(f32[160,128]{1,0:T(8,128)S(1)} %get-tuple-element.56.sin_ref) | copy-start | bytes 245764
  105.8 25.6 %collective-permute-start.22 = (bf16[160,2048]{1,0:T(8,128)(2,1)S(1)}, bf16[160,2048]{1,0:T(8,128)(2,1)S(1)}, u32[]{:S(2)}, u32[]{:S(2)}) collective-permute-start(bf16[160,2048]{1,0:T(8,128)(2,1)S(1)} %sum_and_rotate.3.refs_0_), channel_id=1, source_target_pairs={{0,1},{1,0},{2,3},{3,2},{4,5},{5,4},{6,7},{7,6},{8,9},{9,8},{10,11... | collective-permute-start | bytes 1966088 | tf_op jit(solution)/shard_map/ppermute | solution.py:439
  124.0 8.0 %collective-permute-start.23 = (bf16[160,1536]{1,0:T(8,128)(2,1)S(1)}, bf16[160,1536]{1,0:T(8,128)(2,1)}, u32[]{:S(2)}, u32[]{:S(2)}) collective-permute-start(bf16[160,1536]{1,0:T(8,128)(2,1)S(1)} %sum_and_rotate.4.refs_1_), channel_id=1, source_target_pairs={{0,1},{1,0},{2,3},{3,2},{4,5},{5,4},{6,7},{7,6},{8,9},{9,8},{10,11... | collective-permute-start | bytes 1474568 | tf_op jit(solution)/shard_map/ppermute | solution.py:439
  125.5 3.9 %collective-permute-start.16 = (bf16[320,128]{1,0:T(8,128)(2,1)S(1)}, bf16[320,128]{1,0:T(8,128)(2,1)S(1)}, u32[]{:S(2)}, u32[]{:S(2)}) collective-permute-start(bf16[320,128]{1,0:T(8,128)(2,1)S(1)} %get-tuple-element.45.own_ref), channel_id=1, source_target_pairs={{0,1},{1,0},{2,3},{3,2},{4,5},{5,4},{6,7},{7,6},{8,9},{9,8},{10,11... | collective-permute-start | bytes 245768 | tf_op jit(solution)/shard_map/ppermute | solution.py:439
  126.3 16.1 %collective-permute-start.27 = (bf16[1,320,128]{2,1,0:T(8,128)(2,1)S(1)}, bf16[1,320,128]{2,1,0:T(8,128)(2,1)S(1)}, u32[]{:S(2)}, u32[]{:S(2)}) collective-permute-start(bf16[1,320,128]{2,1,0:T(8,128)(2,1)S(1)} %get-tuple-element.54.refs_0_), channel_id=1, source_target_pairs={{0,12},{4,8},{8,4},{12,0},{1,13},{5,9},{9,5},{13,1},{2,14},{6,10},... | collective-permute-start | bytes 245768 | tf_op jit(solution)/shard_map/ppermute | solution.py:436
  129.3 13.1 %collective-permute-start.26 = (bf16[1,320,128]{2,1,0:T(8,128)(2,1)S(1)}, bf16[1,320,128]{2,1,0:T(8,128)(2,1)S(1)}, u32[]{:S(2)}, u32[]{:S(2)}) collective-permute-start(bf16[1,320,128]{2,1,0:T(8,128)(2,1)S(1)} %get-tuple-element.54.refs_0_), channel_id=1, source_target_pairs={{0,8},{4,12},{8,0},{12,4},{1,9},{5,13},{9,1},{13,5},{2,10},{6,14},... | collective-permute-start | bytes 245768 | tf_op jit(solution)/shard_map/ppermute | solution.py:436
  129.3 13.1 %collective-permute-start.25 = (bf16[1,320,128]{2,1,0:T(8,128)(2,1)S(1)}, bf16[1,320,128]{2,1,0:T(8,128)(2,1)S(1)}, u32[]{:S(2)}, u32[]{:S(2)}) collective-permute-start(bf16[1,320,128]{2,1,0:T(8,128)(2,1)S(1)} %get-tuple-element.54.refs_0_), channel_id=1, source_target_pairs={{0,4},{4,0},{8,12},{12,8},{1,5},{5,1},{9,13},{13,9},{2,6},{6,2},{1... | collective-permute-start | bytes 245768 | tf_op jit(solution)/shard_map/ppermute | solution.py:436
  131.4 11.7 %collective-permute-start.18 = (bf16[1,160,512]{2,1,0:T(8,128)(2,1)}, bf16[1,160,512]{2,1,0:T(8,128)(2,1)S(1)}, u32[]{:S(2)}, u32[]{:S(2)}) collective-permute-start(bf16[1,160,512]{2,1,0:T(8,128)(2,1)} %add_rows.11.refs_7_), channel_id=1, source_target_pairs={{0,4},{4,0},{8,12},{12,8},{1,5},{5,1},{9,13},{13,9},{2,6},{6,2},{1... | collective-permute-start | bytes 491528 | tf_op jit(solution)/shard_map/ppermute | solution.py:436
  132.1 11.0 %collective-permute-start.19 = (bf16[1,160,512]{2,1,0:T(8,128)(2,1)S(1)}, bf16[1,160,512]{2,1,0:T(8,128)(2,1)S(1)}, u32[]{:S(2)}, u32[]{:S(2)}) collective-permute-start(bf16[1,160,512]{2,1,0:T(8,128)(2,1)S(1)} %copy-done), channel_id=1, source_target_pairs={{0,8},{4,12},{8,0},{12,4},{1,9},{5,13},{9,1},{13,5},{2,10},{6,14},... | collective-permute-start | bytes 491528 | tf_op jit(solution)/shard_map/ppermute | solution.py:436
  135.0 8.1 %copy-start.2 = (f32[160,128]{1,0:T(8,128)S(1)}, f32[160,128]{1,0:T(8,128)}, u32[]{:S(2)}) copy-start(f32[160,128]{1,0:T(8,128)} %copy-done.1) | copy-start | bytes 245764
  142.5 1.9 %collective-permute-start.28 = (bf16[4,320,128]{2,1,0:T(8,128)(2,1)S(1)}, bf16[4,320,128]{2,1,0:T(8,128)(2,1)S(1)}, u32[]{:S(2)}, u32[]{:S(2)}) collective-permute-start(bf16[4,320,128]{2,1,0:T(8,128)(2,1)S(1)} %stack_slots.1.own_ref), channel_id=1, source_target_pairs={{0,1},{1,0},{2,3},{3,2},{4,5},{5,4},{6,7},{7,6},{8,9},{9,8},{10,11... | collective-permute-start | bytes 983048 | tf_op jit(solution)/shard_map/ppermute | solution.py:439
  144.2 3.2 %collective-permute-start.24 = (bf16[160,512]{1,0:T(8,128)(2,1)S(1)}, bf16[160,512]{1,0:T(8,128)(2,1)S(1)}, u32[]{:S(2)}, u32[]{:S(2)}) collective-permute-start(bf16[160,512]{1,0:T(8,128)(2,1)S(1)} %sum_and_rotate.5.refs_1_), channel_id=1, source_target_pairs={{0,1},{1,0},{2,3},{3,2},{4,5},{5,4},{6,7},{7,6},{8,9},{9,8},{10,11... | collective-permute-start | bytes 491528 | tf_op jit(solution)/shard_map/ppermute | solution.py:439

commit v14 on v13

--- a/solution.py
+++ b/solution.py
@@ -183,7 +183,7 @@
         out_ref[0, :, cols:] = total(pair_refs[0][0], pair_refs[1][0], landed)
 
 
-def add_rows(first, count, rows, b, keep, gots, start, cols, pair=(), slot=0, landed=(), after=()):
+def add_rows(first, count, rows, b, keep, gots, start, cols, pair=(), slot=0, landed=(), after=(), shift=0):
     whole = keep.shape[2]
     more = pair[0].shape[2] if pair else 0
     keep_spec = pl.BlockSpec((1, rows, cols), lambda s: (first + s, b, start // cols))
@@ -193,7 +193,7 @@
         return pl.BlockSpec((1, rows, width), lambda s: (first + s, b, column))
 
     pair_spec = pl.BlockSpec((1, rows, more), lambda s: (slot + s, 0, 0))
-    landed_specs = [pl.BlockSpec((1, rows, cols), lambda s: (s, 0, start // cols))]
+    landed_specs = [pl.BlockSpec((1, rows, cols), lambda s: (s, 0, (start + shift) // cols))]
     if pair:
         landed_specs.append(pl.BlockSpec((1, rows, more), lambda s: (s, 0, whole // more)))
     landed_specs = landed_specs * len(landed)
@@ -501,7 +501,7 @@
         terms, first = spread({x: summed[k] for k, x in enumerate(even)})
         return [(term, 0, 0) for term in terms], (first,)
 
-    last = tps - 1
+    last, width = tps - 1, 2 * DH * tps
     bounds = [0, head_cols] if tile == head_cols else [0, head_cols * 3 // 4, head_cols]
     ranges = list(zip(bounds, bounds[1:]))
     placed = in_hbm(blocks[:1]) + blocks[1:]
@@ -532,25 +532,35 @@
     near_keep, near_got, given = project([1], placed[last:], tile, after)
     after = (given,)
     parts, behind = [], tuple(term[0] for row in terms for term in row[1:])
+    if fast_pair:
+        near_pair = add_rows(len(odd) - 1, 1, half, 0, pair[0], pair[1:], 0, width, after=after)
+        after = (near_pair,)
+        near_pair = swap(near_pair, 1)
     for start, stop in ranges:
-        paired = () if start else pair
         near_sent = add_rows(
-            0, 1, half, 0, near_keep, near_got, start, stop - start, paired, len(odd) - 1, (), after
+            0, 1, half, 0, near_keep, near_got, start, stop - start, (), 0, (), after
         )
         parts.append([(swap(near_sent, 1), 0, 0)])
         after = (near_sent,)
     after = after + behind
+    if fast_pair:
+        summed = add_rows(
+            len(odd), len(even), half, 0, pair[0], pair[1:], 0, width,
+            landed=(fars[last],), after=after, shift=head_cols,
+        )
+        pair_terms, first = spread({x: summed[k] for k, x in enumerate(even)})
+        after = (first,)
     for part, (start, stop) in zip(parts, ranges):
-        added, after = add_even(last, start, stop - start, () if start else pair, after)
+        added, after = add_even(last, start, stop - start, (), after)
         part += added
-    keep, got, _ = project([0], placed[last:], tile, after, HEAVY)
+    keep, got, given = project([0], placed[last:], tile, after, HEAVY)
     owns.append((keep, 0, got))
 
     if fast_pair:
-        width = 2 * DH * tps
-        pieces = [(array, shards - 1, 0) for array in pair]
-        pieces += [(term, 0, bounds[1]) for term, _, _ in parts[0]]
-        key_rot, held = split_and_rotate(cosine, sine, pieces, width, after)
+        pieces = [(array, shards - 1, 0) for array in pair] + [(near_pair, 0, 0)]
+        pieces += [(term, 0, 0) for term in pair_terms]
+        key_rot, held = split_and_rotate(cosine, sine, pieces, width, (given,))
+        held = stack_slots([held] + [swap(held, x) for x in range(1, shards)], ())
     else:
         x = jnp.concatenate(blocks, axis=0)
         key_sum, value_sum = lax.psum(
@@ -577,7 +587,7 @@
     rotated = [rotate(b, 0, head_cols, terms[b], after) for b in range(last)]
     scores, mark = (), ()
     for p, (start, stop) in enumerate(ranges):
-        turned = rotate(last, start, stop, parts[p], mark or tuple(owns[last][2][1:]))
+        turned = rotate(last, start, stop, parts[p], mark or tuple(owns[last][2][1:]) + ((held,) if fast_pair else ()))
         first = start // DH
         queries = [(row[0], first) for row in rotated] + [(turned[0], 0)]
         queries += [(row[1], first) for row in rotated] + [(turned[1], 0)]
@@ -587,7 +597,6 @@
         )
         mark = (mark,)
         if fast_pair and p == 0:
-            held = stack_slots([held] + [swap(held, x) for x in range(1, shards)], mark)
             values = order_values(findex, order, held, other_core(held))
     return (scores[0], values)
 

time: 151 us -> 164 us (1.086)
  starting transfers between devices: 22.5 us -> 31.1 us
  Pallas kernels: 95 us -> 98.6 us
  waiting for transfers between devices: 28.8 us -> 25.5 us
  local copies, waits for them, and re-layouts: 1.54 us -> 4.4 us
    ppermute x10 -> x12, starting transfers between devices: 15.6 us -> 23.8 us  [swap(): return lax.ppermute(x, 'fsdp', [(i, i ^ bit) for i in range(shards)])]
    pallas_call x7 -> x9, Pallas kernels: 15.7 us -> 18.8 us  [add_rows(): pl.pallas_call(functools.partial(add_kernel, len(gots), len(pair) // 2, l...]
    unnamed x16 -> x36, local copies, waits for them, and re-layouts: 1.15 us -> 4.01 us
    ppermute x18, waiting for transfers between devices: 7.05 us -> 4.68 us  [other_core(): return lax.ppermute(x, 'rep', [(0, 1), (1, 0)])]
    ppermute x10 -> x12, waiting for transfers between devices: 21.8 us -> 20.8 us  [swap(): return lax.ppermute(x, 'fsdp', [(i, i ^ bit) for i in range(shards)])]
  transfers between devices with their start and end apart: 29 -> 31, of which waited for: 11 -> 10; matrix products, arithmetic and copies ran while one was open for 2% -> 2% of each run, Pallas kernels for 61% -> 58%
where the time goes in v14:
time: 164 us; the launch traced here: 163 us
  Pallas kernels  98.6 us (60%)
  starting transfers between devices  31.1 us (19%)
  waiting for transfers between devices  25.5 us (16%)
  local copies, waits for them, and re-layouts  4.4 us (3%)
  other arithmetic  2.62 us (2%)
    pallas_call x6, Pallas kernels, project_query(): pl.pallas_call(functools.partial(query_kernel, count, pieces, by_slot), g...  51.9 us
    ppermute x12, starting transfers between devices, swap(): return lax.ppermute(x, 'fsdp', [(i, i ^ bit) for i in range(shards)])  23.8 us
    ppermute x12, waiting for transfers between devices, swap(): return lax.ppermute(x, 'fsdp', [(i, i ^ bit) for i in range(shards)])  20.8 us
    pallas_call x9, Pallas kernels, add_rows(): pl.pallas_call(functools.partial(add_kernel, len(gots), len(pair) // 2, l...  18.8 us
    pallas_call x2, Pallas kernels, score_heads(): pl.pallas_call(functools.partial(score_kernel, len(queries)), grid=(count...  9.84 us
    pallas_call x1, Pallas kernels, project_pair(): pl.pallas_call(functools.partial(pair_kernel, count), grid_spec=pltpu.Pre...  7.1 us
    pallas_call x3, Pallas kernels, sum_and_rotate(): pl.pallas_call(functools.partial(rotate_kernel, len(terms), len(gots)), g...  4.74 us
    ppermute x18, waiting for transfers between devices, other_core(): return lax.ppermute(x, 'rep', [(0, 1), (1, 0)])  4.68 us
  transfers between devices with their start and end apart: 31, of which 10 were waited for; matrix products, arithmetic and copies ran while one was open for 2% of the time, Pallas kernels for 58%

profile of v14, /device:TPU:0, one launch (start us, length us, event | category | flops | bytes accessed | tf_op | source)
XLA Modules:
  0.0 163.1 jit_solution(4493290249416408463)
XLA Ops:
  0.6 3.0 %collective-permute-start = (bf16[320,2048]{1,0:T(8,128)(2,1)}, bf16[320,2048]{1,0:T(8,128)(2,1)S(1)}, u32[]{:S(2)}, u32[]{:S(2)}) collective-permute-start(bf16[320,2048]{1,0:T(8,128)(2,1)} %refs_0_.5), channel_id=1, source_target_pairs={{0,2},{2,0},{1,3},{3,1},{4,6},{6,4},{5,7},{7,5},{8,10},{10,8},{9,1... | collective-permute-start | bytes 3932168 | tf_op jit(solution)/shard_map/ppermute | solution.py:466
  3.7 11.9 %query_products.6 = (f32[2,160,2048]{2,1,0:T(8,128)}, bf16[2,160,1024]{2,1,0:T(8,128)(2,1)}, bf16[2,160,1024]{2,1,0:T(8,128)(2,1)}) custom-call(s32[3]{0:T(128)S(1)} %pad_add_fusion.2.place_ref, bf16[320,2048]{1,0:T(8,128)(2,1)} %refs_0_.5, bf16[2048,8192]{1,0:T(8,128)(2,1)} %refs_1_.11), custom_call_target="tpu_custom_call" | custom-call | flops 1000 | bytes 1000 | tf_op jit(solution)/shard_map/query_products/pallas_call | solution.py:87
  16.1 1.8 %collective-permute-done.1.refs_1_ = bf16[2,160,1024]{2,1,0:T(8,128)(2,1)S(1)} collective-permute-done((bf16[2,160,1024]{2,1,0:T(8,128)(2,1)}, bf16[2,160,1024]{2,1,0:T(8,128)(2,1)S(1)}, u32[]{:S(2)}, u32[]{:S(2)}) %collective-permute-start.1) | collective-permute-done | bytes 655392 | tf_op jit(solution)/shard_map/ppermute | solution.py:439
  17.9 0.9 collective-permute-done.2.refs_2_
  18.8 2.7 %add_rows.9.refs_2_ = bf16[2,160,2048]{2,1,0:T(8,128)(2,1)} custom-call(f32[2,160,2048]{2,1,0:T(8,128)} %get-tuple-element.29.refs_0_, bf16[2,160,1024]{2,1,0:T(8,128)(2,1)S(1)} %collective-permute-done.1.refs_1_, bf16[2,160,1024]{2,1,0:T(8,128)(2,1)S(1)} %collective-permute-done.2.refs_2_), custom_call_target="tpu_custom_call" | custom-call | flops 1000 | bytes 1000 | tf_op jit(solution)/shard_map/add_rows/pallas_call | solution.py:200
  21.5 1.6 collective-permute-start.7
  23.2 11.8 %query_products.7 = (f32[2,160,2048]{2,1,0:T(8,128)}, bf16[1,160,2048]{2,1,0:T(8,128)(2,1)}, bf16[1,160,2048]{2,1,0:T(8,128)(2,1)}) custom-call(s32[3]{0:T(128)S(1)} %pad_add_fusion.1.place_ref, bf16[320,2048]{1,0:T(8,128)(2,1)} %refs_0_.5, bf16[2048,8192]{1,0:T(8,128)(2,1)} %refs_1_.11, bf16[2,160,2048]{2,1,0:T(8,128)(2,1)} %add_rows.9.refs_2_), custom_call_target="tpu_custom_call" | custom-call | flops 1000 | bytes 1000 | tf_op jit(solution)/shard_map/query_products/pallas_call | solution.py:87
  35.0 7.1 %key_value_products.1 = (f32[4,160,512]{2,1,0:T(8,128)}, bf16[4,160,512]{2,1,0:T(8,128)(2,1)}) custom-call(s32[5]{0:T(128)S(1)} %stack.62.place_ref, bf16[320,2048]{1,0:T(8,128)(2,1)} %refs_0_.5, bf16[320,2048]{1,0:T(8,128)(2,1)S(1)} %collective-permute-done.refs_1_.refs_0_, bf16[2048,512]{1,0:T(8,128)(2,1)} %refs_2_.1, bf16[2048,512]{1,0:T(8,128)(2,1)} %refs_3_.1, ...), custom_call_target="tpu_custom_call" | custom-call | flops 1000 | bytes 1000 | tf_op jit(solution)/shard_map/key_value_products/pallas_call | solution.py:132
  42.7 0.6 broadcast_add_fusion
  43.3 7.1 %query_products.8 = (f32[1,160,2048]{2,1,0:T(8,128)}, bf16[1,160,1024]{2,1,0:T(8,128)(2,1)}, bf16[1,160,1024]{2,1,0:T(8,128)(2,1)}) custom-call(s32[2]{0:T(128)S(1)} %get-tuple-element.66.place_ref, bf16[320,2048]{1,0:T(8,128)(2,1)S(1)} %collective-permute-done.refs_1_.refs_0_, bf16[2048,8192]{1,0:T(8,128)(2,1)} %refs_1_.11, ...), custom_call_target="tpu_custom_call" | custom-call | flops 1000 | bytes 1000 | tf_op jit(solution)/shard_map/query_products/pallas_call | solution.py:87
  51.4 1.0 collective-permute-done.4.refs_1_
  52.8 2.6 %add_rows.10.refs_3_.refs_2_ = bf16[1,160,2560]{2,1,0:T(8,128)(2,1)} custom-call(f32[1,160,2048]{2,1,0:T(8,128)} %get-tuple-element.35.refs_0_, bf16[1,160,1024]{2,1,0:T(8,128)(2,1)} %collective-permute-done.4.refs_1_, bf16[1,160,1024]{2,1,0:T(8,128)(2,1)} %collective-permute-done.5.refs_2_, f32[4,160,512]{2,1,0:T(8,128)} %get-tuple-element.33.refs_3_.refs_0_, ...), custom_call_target="tpu_custom_call" | custom-call | flops 1000 | bytes 1000 | tf_op jit(solution)/shard_map/add_rows/pallas_call | solution.py:200
  55.9 2.5 %add_rows.11.refs_3_ = bf16[1,160,2048]{2,1,0:T(8,128)(2,1)} custom-call(f32[2,160,2048]{2,1,0:T(8,128)} %get-tuple-element.38.refs_0_, bf16[1,160,2048]{2,1,0:T(8,128)(2,1)} %collective-permute-done.6.refs_1_, bf16[2,160,2048]{2,1,0:T(8,128)(2,1)S(1)} %collective-permute-done.7.refs_2_.refs_1_, bf16[1,160,2560]{2,1,0:T(8,128)(2,1)} %add_rows.10.refs_3_.refs_2_), custom_call_target="tpu_custom_call" | custom-call | flops 1000 | bytes 1000 | tf_op jit(solution)/shard_map/add_rows/pallas_call | solution.py:200
  58.4 2.6 %collective-permute-start.12 = (bf16[1,160,2048]{2,1,0:T(8,128)(2,1)}, bf16[1,160,2048]{2,1,0:T(8,128)(2,1)S(1)}, u32[]{:S(2)}, u32[]{:S(2)}) collective-permute-start(bf16[1,160,2048]{2,1,0:T(8,128)(2,1)} %add_rows.11.refs_3_), channel_id=1, source_target_pairs={{0,8},{4,12},{8,0},{12,4},{1,9},{5,13},{9,1},{13,5},{2,10},{6,14},... | collective-permute-start | bytes 1966088 | tf_op jit(solution)/shard_map/ppermute | solution.py:436
  61.0 1.1 copy-done
  62.1 7.0 %query_products.9 = (f32[1,160,2048]{2,1,0:T(8,128)}, bf16[1,160,1024]{2,1,0:T(8,128)(2,1)}, bf16[1,160,1024]{2,1,0:T(8,128)(2,1)}) custom-call(s32[2]{0:T(128)S(1)} %pad_add_fusion.4.place_ref, bf16[320,2048]{1,0:T(8,128)(2,1)S(1)} %collective-permute-done.refs_1_.refs_0_, bf16[2048,8192]{1,0:T(8,128)(2,1)} %refs_1_.11, ...), custom_call_target="tpu_custom_call" | custom-call | flops 99999997952 | bytes 100000000 | tf_op jit(solution)/shard_map/query_products/pallas_call | solution.py:87
  69.2 7.1 %query_products.10 = (f32[1,160,2048]{2,1,0:T(8,128)}, bf16[1,160,1024]{2,1,0:T(8,128)(2,1)}, bf16[1,160,1024]{2,1,0:T(8,128)(2,1)}) custom-call(s32[2]{0:T(128)S(1)} %get-tuple-element.65.place_ref, bf16[320,2048]{1,0:T(8,128)(2,1)S(1)} %collective-permute-done.refs_1_.refs_0_, bf16[2048,8192]{1,0:T(8,128)(2,1)} %refs_1_.11, ...), custom_call_target="tpu_custom_call" | custom-call | flops 1000 | bytes 1000 | tf_op jit(solution)/shard_map/query_products/pallas_call | solution.py:87
  76.3 0.7 fusion.4
  76.9 0.6 collective-permute-start.15
  78.5 1.7 %add_rows.12.refs_3_ = bf16[1,160,512]{2,1,0:T(8,128)(2,1)} custom-call(f32[4,160,512]{2,1,0:T(8,128)} %get-tuple-element.33.refs_3_.refs_0_, bf16[4,160,512]{2,1,0:T(8,128)(2,1)S(1)} %collective-permute-done.3.refs_4_.refs_1_, bf16[1,160,1024]{2,1,0:T(8,128)(2,1)} %get-tuple-element.40.refs_2_), custom_call_target="tpu_custom_call" | custom-call | flops 1000 | bytes 1000 | tf_op jit(solution)/shard_map/add_rows/pallas_call | solution.py:200
  80.2 2.2 %add_rows.13.refs_2_ = bf16[1,160,1536]{2,1,0:T(8,128)(2,1)} custom-call(f32[1,160,2048]{2,1,0:T(8,128)} %get-tuple-element.41.refs_0_, bf16[1,160,1024]{2,1,0:T(8,128)(2,1)S(1)} %collective-permute-done.11.refs_1_, bf16[1,160,1024]{2,1,0:T(8,128)(2,1)S(1)} %collective-permute-done.10.refs_2_.refs_1_, bf16[1,160,512]{2,1,0:T(8,128)(2,1)} %add_rows.12.refs_3_), custom_call_target="tpu_custom_call" | custom-call | flops 1000 | bytes 1000 | tf_op jit(solution)/shard_map/add_rows/pallas_call | solution.py:200
  82.7 1.7 %add_rows.14.refs_3_ = bf16[1,160,512]{2,1,0:T(8,128)(2,1)} custom-call(f32[1,160,2048]{2,1,0:T(8,128)} %get-tuple-element.41.refs_0_, bf16[1,160,1024]{2,1,0:T(8,128)(2,1)S(1)} %collective-permute-done.10.refs_2_.refs_1_, bf16[1,160,1536]{2,1,0:T(8,128)(2,1)} %add_rows.13.refs_2_), custom_call_target="tpu_custom_call" | custom-call | flops 1000 | bytes 1000 | tf_op jit(solution)/shard_map/add_rows/pallas_call | solution.py:200
  84.4 3.7 %collective-permute-done.12.refs_4_.refs_2_ = bf16[1,160,2048]{2,1,0:T(8,128)(2,1)S(1)} collective-permute-done((bf16[1,160,2048]{2,1,0:T(8,128)(2,1)}, bf16[1,160,2048]{2,1,0:T(8,128)(2,1)S(1)}, u32[]{:S(2)}, u32[]{:S(2)}) %collective-permute-start.12) | collective-permute-done | bytes 655392 | tf_op jit(solution)/shard_map/ppermute | solution.py:436
  88.1 4.5 %collective-permute-start.8 = (bf16[1,160,512]{2,1,0:T(8,128)(2,1)S(1)}, bf16[1,160,512]{2,1,0:T(8,128)(2,1)S(1)}, u32[]{:S(2)}, u32[]{:S(2)}) collective-permute-start(bf16[1,160,512]{2,1,0:T(8,128)(2,1)S(1)} %copy-done.7), channel_id=1, source_target_pairs={{0,4},{4,0},{8,12},{12,8},{1,5},{5,1},{9,13},{13,9},{2,6},{6,2},{1... | collective-permute-start | bytes 491528 | tf_op jit(solution)/shard_map/ppermute | solution.py:436
  92.7 1.7 %add_rows.15.refs_4_ = bf16[1,160,512]{2,1,0:T(8,128)(2,1)} custom-call(f32[4,160,512]{2,1,0:T(8,128)} %get-tuple-element.33.refs_3_.refs_0_, bf16[4,160,512]{2,1,0:T(8,128)(2,1)S(1)} %collective-permute-done.3.refs_4_.refs_1_, bf16[1,160,2560]{2,1,0:T(8,128)(2,1)S(1)} %collective-permute-done.9.refs_2_.refs_3_, bf16[1,160,512]{2,1,0:T(8,128)(2,1)} %add_rows.14.refs_3_, ...), custom_call_target="tpu_custom_call" | custom-call | flops 1000 | bytes 1000 | tf_op jit(solution)/shard_map/add_rows/pallas_call | solution.py:200
  94.4 1.7 %collective-permute-start.13 = (bf16[1,160,512]{2,1,0:T(8,128)(2,1)}, bf16[1,160,512]{2,1,0:T(8,128)(2,1)S(1)}, u32[]{:S(2)}, u32[]{:S(2)}) collective-permute-start(bf16[1,160,512]{2,1,0:T(8,128)(2,1)} %add_rows.15.refs_4_), channel_id=1, source_target_pairs={{0,8},{4,12},{8,0},{12,4},{1,9},{5,13},{9,1},{13,5},{2,10},{6,14},... | collective-permute-start | bytes 491528 | tf_op jit(solution)/shard_map/ppermute | solution.py:436
  96.1 2.1 %add_rows.16.refs_3_ = bf16[1,160,1536]{2,1,0:T(8,128)(2,1)} custom-call(f32[1,160,2048]{2,1,0:T(8,128)} %get-tuple-element.43.refs_0_, bf16[1,160,1024]{2,1,0:T(8,128)(2,1)S(1)} %collective-permute-done.15.refs_1_, bf16[1,160,1024]{2,1,0:T(8,128)(2,1)S(1)} %collective-permute-done.14.refs_2_.refs_1_, ...), custom_call_target="tpu_custom_call" | custom-call | flops 1000 | bytes 1000 | tf_op jit(solution)/shard_map/add_rows/pallas_call | solution.py:200
  98.2 1.2 collective-permute-start.22
  99.4 1.7 %add_rows.17.refs_2_.refs_4_ = bf16[1,160,512]{2,1,0:T(8,128)(2,1)} custom-call(f32[1,160,2048]{2,1,0:T(8,128)} %get-tuple-element.43.refs_0_, bf16[1,160,1024]{2,1,0:T(8,128)(2,1)S(1)} %collective-permute-done.14.refs_2_.refs_1_, bf16[1,160,2560]{2,1,0:T(8,128)(2,1)S(1)} %collective-permute-done.9.refs_2_.refs_3_, bf16[1,160,1536]{2,1,0:T(8,128)(2,1)} %add_rows.16.refs_3_), custom_call_target="tpu_custom_call" | custom-call | flops 1000 | bytes 1000 | tf_op jit(solution)/shard_map/add_rows/pallas_call | solution.py:200
  101.1 7.0 %query_products.11 = (f32[1,160,2048]{2,1,0:T(8,128)}, bf16[1,160,1024]{2,1,0:T(8,128)(2,1)}, bf16[1,160,1024]{2,1,0:T(8,128)(2,1)}) custom-call(s32[2]{0:T(128)S(1)} %pad_add_fusion.6.place_ref, bf16[320,2048]{1,0:T(8,128)(2,1)S(1)} %collective-permute-done.refs_1_.refs_0_, bf16[2048,8192]{1,0:T(8,128)(2,1)} %refs_1_.11, ...), custom_call_target="tpu_custom_call" | custom-call | flops 99999997952 | bytes 100000000 | tf_op jit(solution)/shard_map/query_products/pallas_call | solution.py:87
  108.1 3.3 %collective-permute-done.13.refs_3_ = bf16[1,160,512]{2,1,0:T(8,128)(2,1)S(1)} collective-permute-done((bf16[1,160,512]{2,1,0:T(8,128)(2,1)}, bf16[1,160,512]{2,1,0:T(8,128)(2,1)S(1)}, u32[]{:S(2)}, u32[]{:S(2)}) %collective-permute-start.13) | collective-permute-done | bytes 163872 | tf_op jit(solution)/shard_map/ppermute | solution.py:436
  111.4 1.0 copy-done.1
  112.4 1.2 split_and_rotate.1
  113.6 1.2 collective-permute-start.26
  115.3 8.2 %collective-permute-done.26.refs_3_ = bf16[1,320,128]{2,1,0:T(8,128)(2,1)S(1)} collective-permute-done((bf16[1,320,128]{2,1,0:T(8,128)(2,1)S(1)}, bf16[1,320,128]{2,1,0:T(8,128)(2,1)S(1)}, u32[]{:S(2)}, u32[]{:S(2)}) %collective-permute-start.26) | collective-permute-done | bytes 81952 | tf_op jit(solution)/shard_map/ppermute | solution.py:436
  123.5 8.4 %collective-permute-start.25 = (bf16[1,320,128]{2,1,0:T(8,128)(2,1)S(1)}, bf16[1,320,128]{2,1,0:T(8,128)(2,1)S(1)}, u32[]{:S(2)}, u32[]{:S(2)}) collective-permute-start(bf16[1,320,128]{2,1,0:T(8,128)(2,1)S(1)} %get-tuple-element.52.refs_0_), channel_id=1, source_target_pairs={{0,8},{4,12},{8,0},{12,4},{1,9},{5,13},{9,1},{13,5},{2,10},{6,14},... | collective-permute-start | bytes 245768 | tf_op jit(solution)/shard_map/ppermute | solution.py:436
  132.1 3.3 %collective-permute-done.25.refs_2_ = bf16[1,320,128]{2,1,0:T(8,128)(2,1)S(1)} collective-permute-done((bf16[1,320,128]{2,1,0:T(8,128)(2,1)S(1)}, bf16[1,320,128]{2,1,0:T(8,128)(2,1)S(1)}, u32[]{:S(2)}, u32[]{:S(2)}) %collective-permute-start.25) | collective-permute-done | bytes 81952 | tf_op jit(solution)/shard_map/ppermute | solution.py:436
  135.6 1.9 %sum_and_rotate.3.refs_0_ = bf16[160,2048]{1,0:T(8,128)(2,1)S(1)} custom-call(f32[160,128]{1,0:T(8,128)S(1)} %get-tuple-element.59.cos_ref, f32[160,128]{1,0:T(8,128)S(1)} %get-tuple-element.57.sin_ref, f32[2,160,2048]{2,1,0:T(8,128)} %get-tuple-element.38.refs_0_, bf16[2,160,2048]{2,1,0:T(8,128)(2,1)S(1)} %collective-permute-done.7.refs_2_.refs_1_, ...), custom_call_target="tpu_custom_call" | custom-call | flops 1000 | bytes 1000 | tf_op jit(solution)/shard_map/sum_and_rotate/pallas_call | solution.py:250
  137.5 2.3 %collective-permute-done.24.refs_1_ = bf16[1,320,128]{2,1,0:T(8,128)(2,1)S(1)} collective-permute-done((bf16[1,320,128]{2,1,0:T(8,128)(2,1)S(1)}, bf16[1,320,128]{2,1,0:T(8,128)(2,1)S(1)}, u32[]{:S(2)}, u32[]{:S(2)}) %collective-permute-start.24) | collective-permute-done | bytes 81952 | tf_op jit(solution)/shard_map/ppermute | solution.py:436
  139.9 1.6 sum_and_rotate.4.refs_1_
  141.5 0.6 collective-permute-start.28
  142.3 1.8 %collective-permute-start.19 = (bf16[1,160,512]{2,1,0:T(8,128)(2,1)}, bf16[1,160,512]{2,1,0:T(8,128)(2,1)}, u32[]{:S(2)}, u32[]{:S(2)}) collective-permute-start(bf16[1,160,512]{2,1,0:T(8,128)(2,1)} %add_rows.17.refs_2_.refs_4_), channel_id=1, source_target_pairs={{0,8},{4,12},{8,0},{12,4},{1,9},{5,13},{9,1},{13,5},{2,10},{6,14},... | collective-permute-start | bytes 491528 | tf_op jit(solution)/shard_map/ppermute | solution.py:436
  144.8 0.9 copy-done.3
  145.7 0.9 copy-done.5
  147.1 6.6 %score_heads.2 = (bf16[1,16,640,640]{3,2,1,0:T(8,128)(2,1)}, f32[8,128]{1,0:T(8,128)S(1)}) custom-call(bf16[640,640]{1,0:T(8,128)(2,1)S(1)} %get-tuple-element.47.order_ref, bf16[128,640]{1,0:T(8,128)(2,1)S(1)} %get-tuple-element.48.key_t_ref, bf16[160,2048]{1,0:T(8,128)(2,1)S(1)} %sum_and_rotate.3.refs_0_, bf16[160,1536]{1,0:T(8,128)(2,1)S(1)} %sum_and_rotate.4.refs_1_, ...), custom_call_target="tpu_custom_call" | custom-call | flops 1000 | bytes 1000 | tf_op jit(solution)/shard_map/score_heads/pallas_call | solution.py:397
  153.7 1.3 sum_and_rotate.5.refs_1_
  155.4 4.4 %order_values.1.refs_5_ = bf16[640,512]{1,0:T(8,128)(2,1)} custom-call(s32[4]{0:T(128)S(1)} %pad_add_fusion.7.place_ref, bf16[640,640]{1,0:T(8,128)(2,1)S(1)} %get-tuple-element.47.order_ref, bf16[4,320,128]{2,1,0:T(8,128)(2,1)S(1)} %stack_slots.1.refs_6_.own_ref, bf16[4,320,128]{2,1,0:T(8,128)(2,1)} %collective-permute-done.30.other_ref), custom_call_target="tpu_custom_call" | custom-call | tf_op jit(solution)/shard_map/order_values/pallas_call | solution.py:364
  159.9 3.2 %score_heads.3 = (bf16[1,16,640,640]{3,2,1,0:T(8,128)(2,1)}, f32[8,128]{1,0:T(8,128)}) custom-call(bf16[640,640]{1,0:T(8,128)(2,1)S(1)} %get-tuple-element.47.order_ref, bf16[128,640]{1,0:T(8,128)(2,1)S(1)} %get-tuple-element.48.key_t_ref, bf16[160,2048]{1,0:T(8,128)(2,1)S(1)} %sum_and_rotate.3.refs_0_, ...), custom_call_target="tpu_custom_call", output_to_operand_aliasing={{0}: (6, {})} | custom-call | flops 1000 | bytes 1000 | tf_op jit(solution)/shard_map/score_heads/pallas_call | solution.py:397
  (98 shorter events, 7.5 us)
Async XLA Ops:
  0.6 34.4 %collective-permute-start = (bf16[320,2048]{1,0:T(8,128)(2,1)}, bf16[320,2048]{1,0:T(8,128)(2,1)S(1)}, u32[]{:S(2)}, u32[]{:S(2)}) collective-permute-start(bf16[320,2048]{1,0:T(8,128)(2,1)} %refs_0_.5), channel_id=1, source_target_pairs={{0,2},{2,0},{1,3},{3,1},{4,6},{6,4},{5,7},{7,5},{8,10},{10,8},{9,1... | collective-permute-start | bytes 3932168 | tf_op jit(solution)/shard_map/ppermute | solution.py:466
  15.6 2.3 %collective-permute-start.1 = (bf16[2,160,1024]{2,1,0:T(8,128)(2,1)}, bf16[2,160,1024]{2,1,0:T(8,128)(2,1)S(1)}, u32[]{:S(2)}, u32[]{:S(2)}) collective-permute-start(bf16[2,160,1024]{2,1,0:T(8,128)(2,1)} %get-tuple-element.30), channel_id=1, source_target_pairs={{0,1},{1,0},{2,3},{3,2},{4,5},{5,4},{6,7},{7,6},{8,9},{9,8},{10,11... | collective-permute-start | bytes 1966088 | tf_op jit(solution)/shard_map/ppermute | solution.py:439
  15.6 3.2 %collective-permute-start.2 = (bf16[2,160,1024]{2,1,0:T(8,128)(2,1)}, bf16[2,160,1024]{2,1,0:T(8,128)(2,1)S(1)}, u32[]{:S(2)}, u32[]{:S(2)}) collective-permute-start(bf16[2,160,1024]{2,1,0:T(8,128)(2,1)} %get-tuple-element.31), channel_id=1, source_target_pairs={{0,1},{1,0},{2,3},{3,2},{4,5},{5,4},{6,7},{7,6},{8,9},{9,8},{10,11... | collective-permute-start | bytes 1966088 | tf_op jit(solution)/shard_map/ppermute | solution.py:439
  21.5 34.4 %collective-permute-start.7 = (bf16[2,160,2048]{2,1,0:T(8,128)(2,1)}, bf16[2,160,2048]{2,1,0:T(8,128)(2,1)S(1)}, u32[]{:S(2)}, u32[]{:S(2)}) collective-permute-start(bf16[2,160,2048]{2,1,0:T(8,128)(2,1)} %add_rows.9.refs_2_), channel_id=1, source_target_pairs={{0,4},{4,0},{8,12},{12,8},{1,5},{5,1},{9,13},{13,9},{2,6},{6,2},{1... | collective-permute-start | bytes 3932168 | tf_op jit(solution)/shard_map/ppermute | solution.py:436
  35.0 20.9 %collective-permute-start.6 = (bf16[1,160,2048]{2,1,0:T(8,128)(2,1)}, bf16[1,160,2048]{2,1,0:T(8,128)(2,1)}, u32[]{:S(2)}, u32[]{:S(2)}) collective-permute-start(bf16[1,160,2048]{2,1,0:T(8,128)(2,1)} %get-tuple-element.32.refs_4_), channel_id=1, source_target_pairs={{0,1},{1,0},{2,3},{3,2},{4,5},{5,4},{6,7},{7,6},{8,9},{9,8},{10,11... | collective-permute-start | bytes 1966088 | tf_op jit(solution)/shard_map/ppermute | solution.py:439
  42.1 10.7 %collective-permute-start.3 = (bf16[4,160,512]{2,1,0:T(8,128)(2,1)}, bf16[4,160,512]{2,1,0:T(8,128)(2,1)S(1)}, u32[]{:S(2)}, u32[]{:S(2)}) collective-permute-start(bf16[4,160,512]{2,1,0:T(8,128)(2,1)} %get-tuple-element.34.refs_2_), channel_id=1, source_target_pairs={{0,1},{1,0},{2,3},{3,2},{4,5},{5,4},{6,7},{7,6},{8,9},{9,8},{10,11... | collective-permute-start | bytes 1966088 | tf_op jit(solution)/shard_map/ppermute | solution.py:439
  43.3 7.8 %copy-start.11 = (s32[640]{0:T(1024)S(1)}, s32[640]{0:T(1024)}, u32[]{:S(2)}) copy-start(s32[640]{0:T(1024)} %param.10) | copy-start | bytes 7684
  43.3 7.8 %copy-start.13 = (s32[640]{0:T(1024)S(1)}, s32[640]{0:T(1024)}, u32[]{:S(2)}) copy-start(s32[640]{0:T(1024)} %param.11) | copy-start | bytes 7684
  50.4 2.0 %collective-permute-start.4 = (bf16[1,160,1024]{2,1,0:T(8,128)(2,1)}, bf16[1,160,1024]{2,1,0:T(8,128)(2,1)}, u32[]{:S(2)}, u32[]{:S(2)}) collective-permute-start(bf16[1,160,1024]{2,1,0:T(8,128)(2,1)} %get-tuple-element.36), channel_id=1, source_target_pairs={{0,1},{1,0},{2,3},{3,2},{4,5},{5,4},{6,7},{7,6},{8,9},{9,8},{10,11... | collective-permute-start | bytes 983048 | tf_op jit(solution)/shard_map/ppermute | solution.py:439
  50.4 2.4 %collective-permute-start.5 = (bf16[1,160,1024]{2,1,0:T(8,128)(2,1)}, bf16[1,160,1024]{2,1,0:T(8,128)(2,1)}, u32[]{:S(2)}, u32[]{:S(2)}) collective-permute-start(bf16[1,160,1024]{2,1,0:T(8,128)(2,1)} %get-tuple-element.37), channel_id=1, source_target_pairs={{0,1},{1,0},{2,3},{3,2},{4,5},{5,4},{6,7},{7,6},{8,9},{9,8},{10,11... | collective-permute-start | bytes 983048 | tf_op jit(solution)/shard_map/ppermute | solution.py:439
  51.1 4.4 %copy-start.9 = (s32[320]{0:T(512)}, s32[320]{0:T(512)S(1)}, u32[]{:S(2)}) copy-start(s32[320]{0:T(512)S(1)} %add.106) | copy-start | bytes 3844
  55.4 37.1 %collective-permute-start.9 = (bf16[1,160,2560]{2,1,0:T(8,128)(2,1)}, bf16[1,160,2560]{2,1,0:T(8,128)(2,1)S(1)}, u32[]{:S(2)}, u32[]{:S(2)}) collective-permute-start(bf16[1,160,2560]{2,1,0:T(8,128)(2,1)} %add_rows.10.refs_3_.refs_2_), channel_id=1, source_target_pairs={{0,4},{4,0},{8,12},{12,8},{1,5},{5,1},{9,13},{13,9},{2,6},{6,2},{1... | collective-permute-start | bytes 2457608 | tf_op jit(solution)/shard_map/ppermute | solution.py:436
  58.4 29.7 %collective-permute-start.12 = (bf16[1,160,2048]{2,1,0:T(8,128)(2,1)}, bf16[1,160,2048]{2,1,0:T(8,128)(2,1)S(1)}, u32[]{:S(2)}, u32[]{:S(2)}) collective-permute-start(bf16[1,160,2048]{2,1,0:T(8,128)(2,1)} %add_rows.11.refs_3_), channel_id=1, source_target_pairs={{0,8},{4,12},{8,0},{12,4},{1,9},{5,13},{9,1},{13,5},{2,10},{6,14},... | collective-permute-start | bytes 1966088 | tf_op jit(solution)/shard_map/ppermute | solution.py:436
  61.0 1.1 copy-start
  69.2 7.8 %copy-start.8 = (bf16[1,160,1024]{2,1,0:T(8,128)(2,1)S(1)}, bf16[1,160,1024]{2,1,0:T(8,128)(2,1)}, u32[]{:S(2)}) copy-start(bf16[1,160,1024]{2,1,0:T(8,128)(2,1)} %get-tuple-element.39.refs_2_) | copy-start | bytes 983044
  69.2 8.4 %copy-start.17 = (bf16[1,160,1024]{2,1,0:T(8,128)(2,1)S(1)}, bf16[1,160,1024]{2,1,0:T(8,128)(2,1)}, u32[]{:S(2)}) copy-start(bf16[1,160,1024]{2,1,0:T(8,128)(2,1)} %get-tuple-element.44) | copy-start | bytes 983044
  76.2 1.8 %collective-permute-start.10 = (bf16[1,160,1024]{2,1,0:T(8,128)(2,1)}, bf16[1,160,1024]{2,1,0:T(8,128)(2,1)S(1)}, u32[]{:S(2)}, u32[]{:S(2)}) collective-permute-start(bf16[1,160,1024]{2,1,0:T(8,128)(2,1)} %get-tuple-element.42), channel_id=1, source_target_pairs={{0,1},{1,0},{2,3},{3,2},{4,5},{5,4},{6,7},{7,6},{8,9},{9,8},{10,11... | collective-permute-start | bytes 983048 | tf_op jit(solution)/shard_map/ppermute | solution.py:439
  76.9 19.1 %collective-permute-start.15 = (bf16[1,160,1024]{2,1,0:T(8,128)(2,1)S(1)}, bf16[1,160,1024]{2,1,0:T(8,128)(2,1)S(1)}, u32[]{:S(2)}, u32[]{:S(2)}) collective-permute-start(bf16[1,160,1024]{2,1,0:T(8,128)(2,1)S(1)} %copy-done.8), channel_id=1, source_target_pairs={{0,1},{1,0},{2,3},{3,2},{4,5},{5,4},{6,7},{7,6},{8,9},{9,8},{10,11... | collective-permute-start | bytes 983048 | tf_op jit(solution)/shard_map/ppermute | solution.py:439
  77.5 16.8 %collective-permute-start.14 = (bf16[1,160,1024]{2,1,0:T(8,128)(2,1)S(1)}, bf16[1,160,1024]{2,1,0:T(8,128)(2,1)S(1)}, u32[]{:S(2)}, u32[]{:S(2)}) collective-permute-start(bf16[1,160,1024]{2,1,0:T(8,128)(2,1)S(1)} %copy-done.17), channel_id=1, source_target_pairs={{0,1},{1,0},{2,3},{3,2},{4,5},{5,4},{6,7},{7,6},{8,9},{9,8},{10,11... | collective-permute-start | bytes 983048 | tf_op jit(solution)/shard_map/ppermute | solution.py:439
  78.1 2.1 %collective-permute-start.11 = (bf16[1,160,1024]{2,1,0:T(8,128)(2,1)}, bf16[1,160,1024]{2,1,0:T(8,128)(2,1)S(1)}, u32[]{:S(2)}, u32[]{:S(2)}) collective-permute-start(bf16[1,160,1024]{2,1,0:T(8,128)(2,1)} %get-tuple-element.40.refs_2_), channel_id=1, source_target_pairs={{0,1},{1,0},{2,3},{3,2},{4,5},{5,4},{6,7},{7,6},{8,9},{9,8},{10,11... | collective-permute-start | bytes 983048 | tf_op jit(solution)/shard_map/ppermute | solution.py:439
  80.2 2.2 %copy-start.15 = (bf16[1,160,2048]{2,1,0:T(8,128)(2,1)S(1)}, bf16[1,160,2048]{2,1,0:T(8,128)(2,1)}, u32[]{:S(2)}) copy-start(bf16[1,160,2048]{2,1,0:T(8,128)(2,1)} %get-tuple-element.49) | copy-start | bytes 1966084
  82.4 5.7 %copy-start.7 = (bf16[1,160,512]{2,1,0:T(8,128)(2,1)S(1)}, bf16[1,160,512]{2,1,0:T(8,128)(2,1)}, u32[]{:S(2)}) copy-start(bf16[1,160,512]{2,1,0:T(8,128)(2,1)} %add_rows.12.refs_3_) | copy-start | bytes 491524
  82.4 10.2 %copy-start.6 = (bf16[1,160,1536]{2,1,0:T(8,128)(2,1)S(1)}, bf16[1,160,1536]{2,1,0:T(8,128)(2,1)}, u32[]{:S(2)}) copy-start(bf16[1,160,1536]{2,1,0:T(8,128)(2,1)} %add_rows.13.refs_2_) | copy-start | bytes 1474564
  82.4 32.4 %collective-permute-start.17 = (bf16[1,160,2048]{2,1,0:T(8,128)(2,1)S(1)}, bf16[1,160,2048]{2,1,0:T(8,128)(2,1)S(1)}, u32[]{:S(2)}, u32[]{:S(2)}) collective-permute-start(bf16[1,160,2048]{2,1,0:T(8,128)(2,1)S(1)} %copy-done.15), channel_id=1, source_target_pairs={{0,1},{1,0},{2,3},{3,2},{4,5},{5,4},{6,7},{7,6},{8,9},{9,8},{10,11... | collective-permute-start | bytes 1966088 | tf_op jit(solution)/shard_map/ppermute | solution.py:439
  88.1 20.0 %collective-permute-start.8 = (bf16[1,160,512]{2,1,0:T(8,128)(2,1)S(1)}, bf16[1,160,512]{2,1,0:T(8,128)(2,1)S(1)}, u32[]{:S(2)}, u32[]{:S(2)}) collective-permute-start(bf16[1,160,512]{2,1,0:T(8,128)(2,1)S(1)} %copy-done.7), channel_id=1, source_target_pairs={{0,4},{4,0},{8,12},{12,8},{1,5},{5,1},{9,13},{13,9},{2,6},{6,2},{1... | collective-permute-start | bytes 491528 | tf_op jit(solution)/shard_map/ppermute | solution.py:436
  92.6 47.3 %collective-permute-start.21 = (bf16[1,160,1536]{2,1,0:T(8,128)(2,1)S(1)}, bf16[1,160,1536]{2,1,0:T(8,128)(2,1)S(1)}, u32[]{:S(2)}, u32[]{:S(2)}) collective-permute-start(bf16[1,160,1536]{2,1,0:T(8,128)(2,1)S(1)} %copy-done.6), channel_id=1, source_target_pairs={{0,4},{4,0},{8,12},{12,8},{1,5},{5,1},{9,13},{13,9},{2,6},{6,2},{1... | collective-permute-start | bytes 1474568 | tf_op jit(solution)/shard_map/ppermute | solution.py:436
  94.4 17.1 %collective-permute-start.13 = (bf16[1,160,512]{2,1,0:T(8,128)(2,1)}, bf16[1,160,512]{2,1,0:T(8,128)(2,1)S(1)}, u32[]{:S(2)}, u32[]{:S(2)}) collective-permute-start(bf16[1,160,512]{2,1,0:T(8,128)(2,1)} %add_rows.15.refs_4_), channel_id=1, source_target_pairs={{0,8},{4,12},{8,0},{12,4},{1,9},{5,13},{9,1},{13,5},{2,10},{6,14},... | collective-permute-start | bytes 491528 | tf_op jit(solution)/shard_map/ppermute | solution.py:436
  98.2 41.7 %collective-permute-start.22 = (bf16[1,160,1536]{2,1,0:T(8,128)(2,1)}, bf16[1,160,1536]{2,1,0:T(8,128)(2,1)S(1)}, u32[]{:S(2)}, u32[]{:S(2)}) collective-permute-start(bf16[1,160,1536]{2,1,0:T(8,128)(2,1)} %add_rows.16.refs_3_), channel_id=1, source_target_pairs={{0,8},{4,12},{8,0},{12,4},{1,9},{5,13},{9,1},{13,5},{2,10},{6,14},... | collective-permute-start | bytes 1474568 | tf_op jit(solution)/shard_map/ppermute | solution.py:436
  111.4 1.0 copy-start.1
  112.4 2.4 %copy-start.16 = (bf16[1,160,1024]{2,1,0:T(8,128)(2,1)S(1)}, bf16[1,160,1024]{2,1,0:T(8,128)(2,1)}, u32[]{:S(2)}) copy-start(bf16[1,160,1024]{2,1,0:T(8,128)(2,1)} %get-tuple-element.51) | copy-start | bytes 983044
  113.6 28.5 %copy-start.2 = (bf16[320,128]{1,0:T(8,128)(2,1)}, bf16[320,128]{1,0:T(8,128)(2,1)S(1)}, u32[]{:S(2)}) copy-start(bf16[320,128]{1,0:T(8,128)(2,1)S(1)} %get-tuple-element.46.own_ref) | copy-start | bytes 245764
  113.6 10.0 %collective-permute-start.26 = (bf16[1,320,128]{2,1,0:T(8,128)(2,1)S(1)}, bf16[1,320,128]{2,1,0:T(8,128)(2,1)S(1)}, u32[]{:S(2)}, u32[]{:S(2)}) collective-permute-start(bf16[1,320,128]{2,1,0:T(8,128)(2,1)S(1)} %get-tuple-element.52.refs_0_), channel_id=1, source_target_pairs={{0,12},{4,8},{8,4},{12,0},{1,13},{5,9},{9,5},{13,1},{2,14},{6,10},... | collective-permute-start | bytes 245768 | tf_op jit(solution)/shard_map/ppermute | solution.py:436
  114.8 25.1 %collective-permute-start.23 = (bf16[1,160,1024]{2,1,0:T(8,128)(2,1)S(1)}, bf16[1,160,1024]{2,1,0:T(8,128)(2,1)S(1)}, u32[]{:S(2)}, u32[]{:S(2)}) collective-permute-start(bf16[1,160,1024]{2,1,0:T(8,128)(2,1)S(1)} %copy-done.1), channel_id=1, source_target_pairs={{0,1},{1,0},{2,3},{3,2},{4,5},{5,4},{6,7},{7,6},{8,9},{9,8},{10,11... | collective-permute-start | bytes 983048 | tf_op jit(solution)/shard_map/ppermute | solution.py:439
  114.8 25.1 %collective-permute-start.20 = (bf16[1,160,1024]{2,1,0:T(8,128)(2,1)S(1)}, bf16[1,160,1024]{2,1,0:T(8,128)(2,1)S(1)}, u32[]{:S(2)}, u32[]{:S(2)}) collective-permute-start(bf16[1,160,1024]{2,1,0:T(8,128)(2,1)S(1)} %copy-done.16), channel_id=1, source_target_pairs={{0,1},{1,0},{2,3},{3,2},{4,5},{5,4},{6,7},{7,6},{8,9},{9,8},{10,11... | collective-permute-start | bytes 983048 | tf_op jit(solution)/shard_map/ppermute | solution.py:439
  123.5 11.8 %collective-permute-start.25 = (bf16[1,320,128]{2,1,0:T(8,128)(2,1)S(1)}, bf16[1,320,128]{2,1,0:T(8,128)(2,1)S(1)}, u32[]{:S(2)}, u32[]{:S(2)}) collective-permute-start(bf16[1,320,128]{2,1,0:T(8,128)(2,1)S(1)} %get-tuple-element.52.refs_0_), channel_id=1, source_target_pairs={{0,8},{4,12},{8,0},{12,4},{1,9},{5,13},{9,1},{13,5},{2,10},{6,14},... | collective-permute-start | bytes 245768 | tf_op jit(solution)/shard_map/ppermute | solution.py:436
  135.4 4.4 %collective-permute-start.24 = (bf16[1,320,128]{2,1,0:T(8,128)(2,1)S(1)}, bf16[1,320,128]{2,1,0:T(8,128)(2,1)S(1)}, u32[]{:S(2)}, u32[]{:S(2)}) collective-permute-start(bf16[1,320,128]{2,1,0:T(8,128)(2,1)S(1)} %get-tuple-element.52.refs_0_), channel_id=1, source_target_pairs={{0,4},{4,0},{8,12},{12,8},{1,5},{5,1},{9,13},{13,9},{2,6},{6,2},{1... | collective-permute-start | bytes 245768 | tf_op jit(solution)/shard_map/ppermute | solution.py:436
  139.8 7.3 %collective-permute-start.27 = (bf16[160,2048]{1,0:T(8,128)(2,1)S(1)}, bf16[160,2048]{1,0:T(8,128)(2,1)S(1)}, u32[]{:S(2)}, u32[]{:S(2)}) collective-permute-start(bf16[160,2048]{1,0:T(8,128)(2,1)S(1)} %sum_and_rotate.3.refs_0_), channel_id=1, source_target_pairs={{0,1},{1,0},{2,3},{3,2},{4,5},{5,4},{6,7},{7,6},{8,9},{9,8},{10,11... | collective-permute-start | bytes 1966088 | tf_op jit(solution)/shard_map/ppermute | solution.py:439
  139.9 4.4 %copy-start.14 = (s32[2]{0:T(128)S(1)}, s32[2]{0:T(128)}, u32[]{:S(2)}) copy-start(s32[2]{0:T(128)} %get-tuple-element.63) | copy-start | bytes 28
  139.9 4.5 %copy-start.12 = (s32[640]{0:T(1024)S(1)}, s32[640]{0:T(1024)}, u32[]{:S(2)}) copy-start(s32[640]{0:T(1024)} %param.10) | copy-start | bytes 7684
  139.9 4.7 %copy-start.10 = (s32[320]{0:T(512)S(1)}, s32[320]{0:T(512)}, u32[]{:S(2)}) copy-start(s32[320]{0:T(512)} %copy-done.9) | copy-start | bytes 3844
  141.5 5.6 %collective-permute-start.28 = (bf16[160,1536]{1,0:T(8,128)(2,1)S(1)}, bf16[160,1536]{1,0:T(8,128)(2,1)S(1)}, u32[]{:S(2)}, u32[]{:S(2)}) collective-permute-start(bf16[160,1536]{1,0:T(8,128)(2,1)S(1)} %sum_and_rotate.4.refs_1_), channel_id=1, source_target_pairs={{0,1},{1,0},{2,3},{3,2},{4,5},{5,4},{6,7},{7,6},{8,9},{9,8},{10,11... | collective-permute-start | bytes 1474568 | tf_op jit(solution)/shard_map/ppermute | solution.py:439
  142.1 2.0 %collective-permute-start.16 = (bf16[320,128]{1,0:T(8,128)(2,1)S(1)}, bf16[320,128]{1,0:T(8,128)(2,1)S(1)}, u32[]{:S(2)}, u32[]{:S(2)}) collective-permute-start(bf16[320,128]{1,0:T(8,128)(2,1)S(1)} %get-tuple-element.46.own_ref), channel_id=1, source_target_pairs={{0,1},{1,0},{2,3},{3,2},{4,5},{5,4},{6,7},{7,6},{8,9},{9,8},{10,11... | collective-permute-start | bytes 245768 | tf_op jit(solution)/shard_map/ppermute | solution.py:439
  142.2 11.5 %collective-permute-start.18 = (bf16[1,160,512]{2,1,0:T(8,128)(2,1)}, bf16[1,160,512]{2,1,0:T(8,128)(2,1)}, u32[]{:S(2)}, u32[]{:S(2)}) collective-permute-start(bf16[1,160,512]{2,1,0:T(8,128)(2,1)} %add_rows.14.refs_3_), channel_id=1, source_target_pairs={{0,4},{4,0},{8,12},{12,8},{1,5},{5,1},{9,13},{13,9},{2,6},{6,2},{1... | collective-permute-start | bytes 491528 | tf_op jit(solution)/shard_map/ppermute | solution.py:436
  142.3 11.4 %collective-permute-start.19 = (bf16[1,160,512]{2,1,0:T(8,128)(2,1)}, bf16[1,160,512]{2,1,0:T(8,128)(2,1)}, u32[]{:S(2)}, u32[]{:S(2)}) collective-permute-start(bf16[1,160,512]{2,1,0:T(8,128)(2,1)} %add_rows.17.refs_2_.refs_4_), channel_id=1, source_target_pairs={{0,8},{4,12},{8,0},{12,4},{1,9},{5,13},{9,1},{13,5},{2,10},{6,14},... | collective-permute-start | bytes 491528 | tf_op jit(solution)/shard_map/ppermute | solution.py:436
  144.1 11.3 %collective-permute-start.30 = (bf16[4,320,128]{2,1,0:T(8,128)(2,1)S(1)}, bf16[4,320,128]{2,1,0:T(8,128)(2,1)}, u32[]{:S(2)}, u32[]{:S(2)}) collective-permute-start(bf16[4,320,128]{2,1,0:T(8,128)(2,1)S(1)} %stack_slots.1.refs_6_.own_ref), channel_id=1, source_target_pairs={{0,1},{1,0},{2,3},{3,2},{4,5},{5,4},{6,7},{7,6},{8,9},{9,8},{10,11... | collective-permute-start | bytes 983048 | tf_op jit(solution)/shard_map/ppermute | solution.py:439
  144.8 0.9 copy-start.3
  145.7 0.9 copy-start.5
  155.0 4.9 %collective-permute-start.29 = (bf16[160,512]{1,0:T(8,128)(2,1)S(1)}, bf16[160,512]{1,0:T(8,128)(2,1)S(1)}, u32[]{:S(2)}, u32[]{:S(2)}) collective-permute-start(bf16[160,512]{1,0:T(8,128)(2,1)S(1)} %sum_and_rotate.5.refs_1_), channel_id=1, source_target_pairs={{0,1},{1,0},{2,3},{3,2},{4,5},{5,4},{6,7},{7,6},{8,9},{9,8},{10,11... | collective-permute-start | bytes 491528 | tf_op jit(solution)/shard_map/ppermute | solution.py:439
  (1 other events, 0.6 us)

commit v15 on v13

--- a/solution.py
+++ b/solution.py
@@ -64,7 +64,7 @@
             give_ref[0] = result[half:, start : start + size].astype(give_ref.dtype)
 
 
-def project_query(rindex, findex, slots, blocks, w, cols, tile, width, after, cost, by_slot):
+def project_query(rindex, findex, slots, blocks, w, cols, tile, width, after, cost, by_slot, near):
     rows, depth = blocks[0].shape
     count = len(blocks)
     half = rows // 2 * count
@@ -95,7 +95,7 @@
             out_specs=[keep_spec] + give_specs,
             scratch_shapes=[pltpu.VMEM((2 * half, depth), w.dtype)],
         ),
-        out_shape=[pltpu.HBM((len(slots), half, cols), jnp.float32)]
+        out_shape=[(jax.ShapeDtypeStruct if near else pltpu.HBM)((len(slots), half, cols), jnp.float32)]
         + [pltpu.HBM(given, jnp.bfloat16)] * pieces,
         compiler_params=pltpu.CompilerParams(vmem_limit_bytes=VMEM_BYTES),
         cost_estimate=cost,
@@ -183,7 +183,7 @@
         out_ref[0, :, cols:] = total(pair_refs[0][0], pair_refs[1][0], landed)
 
 
-def add_rows(first, count, rows, b, keep, gots, start, cols, pair=(), slot=0, landed=(), after=()):
+def add_rows(first, count, rows, b, keep, gots, start, cols, pair=(), slot=0, landed=(), after=(), near=False):
     whole = keep.shape[2]
     more = pair[0].shape[2] if pair else 0
     keep_spec = pl.BlockSpec((1, rows, cols), lambda s: (first + s, b, start // cols))
@@ -211,7 +211,7 @@
         cost_estimate=LIGHT,
         name="add_rows",
     )(
-        *in_hbm([keep]),
+        *([keep] if near else in_hbm([keep])),
         *[got for got, _, _ in gots],
         *in_hbm(pair[:1]),
         *pair[1:],
@@ -351,28 +351,36 @@
     )(*arrays, *after)
 
 
-def value_kernel(place_ref, order_ref, own_ref, other_ref, out_ref):
-    rows = jnp.concatenate([own_ref[0], other_ref[0]], axis=0)
+def value_kernel(place_ref, order_ref, *refs):
+    *slots, out_ref = refs
+    own, other = slots[: len(slots) // 2], slots[len(slots) // 2 :]
+    sides = [jnp.concatenate([x[0] for x in side], axis=1) for side in (own, other)]
+    rows = jnp.concatenate(sides, axis=0)
     out_ref[...] = jnp.dot(order_ref[...], rows, preferred_element_type=jnp.float32).astype(out_ref.dtype)
 
 
 def order_values(findex, order, own, other):
     rows = order.shape[0]
     slots, part, width = own.shape
+    step = math.gcd(slots, 2)
     place = jnp.stack([findex ^ s for s in range(slots)]).astype(jnp.int32)
-    block = pl.BlockSpec((1, part, width), lambda s, place: (place[s], 0, 0))
+
+    def block(k):
+        return pl.BlockSpec((1, part, width), lambda s, place: (place[s * step + k], 0, 0))
+
     return pl.pallas_call(
         value_kernel,
         grid_spec=pltpu.PrefetchScalarGridSpec(
             num_scalar_prefetch=1,
-            grid=(slots,),
-            in_specs=[pl.BlockSpec((rows, rows), lambda s, place: (0, 0)), block, block],
-            out_specs=pl.BlockSpec((rows, width), lambda s, place: (0, s)),
+            grid=(slots // step,),
+            in_specs=[pl.BlockSpec((rows, rows), lambda s, place: (0, 0))]
+            + [block(k) for k in range(step)] * 2,
+            out_specs=pl.BlockSpec((rows, step * width), lambda s, place: (0, s)),
         ),
         out_shape=jax.ShapeDtypeStruct((rows, slots * width), jnp.bfloat16),
         compiler_params=pltpu.CompilerParams(vmem_limit_bytes=VMEM_BYTES),
         name="order_values",
-    )(place, order, own, other)
+    )(place, order, *[own] * step, *[other] * step)
 
 
 def score_kernel(count, order_ref, key_t_ref, *refs):
@@ -477,9 +485,9 @@
 
     tile = min(1024, head_cols)
 
-    def project(slots, blocks, width, after=(), cost=LIGHT, by_slot=False):
+    def project(slots, blocks, width, after=(), cost=LIGHT, by_slot=False, near=False):
         keep, gives = project_query(
-            rindex, findex, slots, blocks, w_query, head_cols, tile, width, after, cost, by_slot
+            rindex, findex, slots, blocks, w_query, head_cols, tile, width, after, cost, by_slot, near
         )
         return keep, [other_core(give) for give in gives], gives[0]
 
@@ -513,8 +521,8 @@
             pair = (pair_keep, other_core(give))
             after = (give,)
         sent = odd[:-1] if b == last else odd
-        odd_keep, odd_got, given = project(sent, [block], tile, after)
-        odd_sent = add_rows(0, len(sent), half, 0, odd_keep, odd_got, 0, head_cols, pair)
+        odd_keep, odd_got, given = project(sent, [block], tile, after, near=True)
+        odd_sent = add_rows(0, len(sent), half, 0, odd_keep, odd_got, 0, head_cols, pair, near=True)
         fars.append(swap(odd_sent, 1))
         after = (odd_sent,)
         if b > 0:

time: 151 us -> 148 us (0.980)
  Pallas kernels: 95 us -> 92.1 us
  transfers between devices with their start and end apart: 29 -> 29, of which waited for: 11 -> 11; matrix products, arithmetic and copies ran while one was open for 2% -> 2% of each run, Pallas kernels for 61% -> 60%
where the time goes in v15:
time: 148 us
  Pallas kernels  92.1 us (62%)
  waiting for transfers between devices  28.2 us (19%)
  starting transfers between devices  22.9 us (15%)
  other arithmetic  2.04 us (1%)
  local copies, waits for them, and re-layouts  1.54 us (1%)
    pallas_call x6, Pallas kernels, project_query(): pl.pallas_call(functools.partial(query_kernel, count, pieces, by_slot), g...  51.5 us
    ppermute x10, waiting for transfers between devices, swap(): return lax.ppermute(x, 'fsdp', [(i, i ^ bit) for i in range(shards)])  21.1 us
    ppermute x10, starting transfers between devices, swap(): return lax.ppermute(x, 'fsdp', [(i, i ^ bit) for i in range(shards)])  16.1 us
    pallas_call x7, Pallas kernels, add_rows(): pl.pallas_call(functools.partial(add_kernel, len(gots), len(pair) // 2, l...  14.2 us
    pallas_call x2, Pallas kernels, score_heads(): pl.pallas_call(functools.partial(score_kernel, len(queries)), grid=(count...  10.7 us
    ppermute x18, waiting for transfers between devices, other_core(): return lax.ppermute(x, 'rep', [(0, 1), (1, 0)])  7.19 us
    pallas_call x1, Pallas kernels, project_pair(): pl.pallas_call(functools.partial(pair_kernel, count), grid_spec=pltpu.Pre...  7.11 us
    pallas_call x3, Pallas kernels, sum_and_rotate(): pl.pallas_call(functools.partial(rotate_kernel, len(terms), len(gots)), g...  4.77 us
  transfers between devices with their start and end apart: 29, of which 11 were waited for; matrix products, arithmetic and copies ran while one was open for 2% of the time, Pallas kernels for 60%

profile of v15, /device:TPU:0, one launch (start us, length us, event | category | flops | bytes accessed | tf_op | source)
XLA Modules:
  0.0 147.7 jit_solution(7248287212718724868)
XLA Ops:
  0.6 3.0 %collective-permute-start = (bf16[320,2048]{1,0:T(8,128)(2,1)}, bf16[320,2048]{1,0:T(8,128)(2,1)S(1)}, u32[]{:S(2)}, u32[]{:S(2)}) collective-permute-start(bf16[320,2048]{1,0:T(8,128)(2,1)} %refs_0_.5), channel_id=1, source_target_pairs={{0,2},{2,0},{1,3},{3,1},{4,6},{6,4},{5,7},{7,5},{8,10},{10,8},{9,1... | collective-permute-start | bytes 3932168 | tf_op jit(solution)/shard_map/ppermute | solution.py:474
  3.7 11.5 %query_products.6 = (f32[2,160,2048]{2,1,0:T(8,128)S(1)}, bf16[2,160,1024]{2,1,0:T(8,128)(2,1)}, bf16[2,160,1024]{2,1,0:T(8,128)(2,1)}) custom-call(s32[3]{0:T(128)S(1)} %pad_add_fusion.2.place_ref, bf16[320,2048]{1,0:T(8,128)(2,1)} %refs_0_.5, bf16[2048,8192]{1,0:T(8,128)(2,1)} %refs_1_.11), custom_call_target="tpu_custom_call" | custom-call | flops 1000 | bytes 1000 | tf_op jit(solution)/shard_map/query_products/pallas_call | solution.py:87
  15.2 0.5 collective-permute-start.2
  15.7 1.8 %collective-permute-done.1.refs_1_ = bf16[2,160,1024]{2,1,0:T(8,128)(2,1)S(1)} collective-permute-done((bf16[2,160,1024]{2,1,0:T(8,128)(2,1)}, bf16[2,160,1024]{2,1,0:T(8,128)(2,1)S(1)}, u32[]{:S(2)}, u32[]{:S(2)}) %collective-permute-start.1) | collective-permute-done | bytes 655392 | tf_op jit(solution)/shard_map/ppermute | solution.py:447
  17.5 0.9 collective-permute-done.2.refs_2_
  18.5 1.2 add_rows.7.refs_2_
  19.6 1.6 %collective-permute-start.7 = (bf16[2,160,2048]{2,1,0:T(8,128)(2,1)}, bf16[2,160,2048]{2,1,0:T(8,128)(2,1)}, u32[]{:S(2)}, u32[]{:S(2)}) collective-permute-start(bf16[2,160,2048]{2,1,0:T(8,128)(2,1)} %add_rows.7.refs_2_), channel_id=1, source_target_pairs={{0,4},{4,0},{8,12},{12,8},{1,5},{5,1},{9,13},{13,9},{2,6},{6,2},{1... | collective-permute-start | bytes 3932168 | tf_op jit(solution)/shard_map/ppermute | solution.py:444
  21.4 11.8 %query_products.7 = (f32[2,160,2048]{2,1,0:T(8,128)}, bf16[1,160,2048]{2,1,0:T(8,128)(2,1)}, bf16[1,160,2048]{2,1,0:T(8,128)(2,1)}) custom-call(s32[3]{0:T(128)S(1)} %pad_add_fusion.1.place_ref, bf16[320,2048]{1,0:T(8,128)(2,1)} %refs_0_.5, bf16[2048,8192]{1,0:T(8,128)(2,1)} %refs_1_.11, bf16[2,160,2048]{2,1,0:T(8,128)(2,1)} %add_rows.7.refs_2_), custom_call_target="tpu_custom_call" | custom-call | flops 1000 | bytes 1000 | tf_op jit(solution)/shard_map/query_products/pallas_call | solution.py:87
  33.1 7.1 %key_value_products.1 = (f32[4,160,512]{2,1,0:T(8,128)}, bf16[4,160,512]{2,1,0:T(8,128)(2,1)}) custom-call(s32[5]{0:T(128)S(1)} %stack.62.place_ref, bf16[320,2048]{1,0:T(8,128)(2,1)} %refs_0_.5, bf16[320,2048]{1,0:T(8,128)(2,1)S(1)} %collective-permute-done.refs_1_.refs_0_, bf16[2048,512]{1,0:T(8,128)(2,1)} %refs_2_.1, bf16[2048,512]{1,0:T(8,128)(2,1)} %refs_3_.1, ...), custom_call_target="tpu_custom_call" | custom-call | flops 1000 | bytes 1000 | tf_op jit(solution)/shard_map/key_value_products/pallas_call | solution.py:132
  40.3 0.5 collective-permute-start.6
  40.8 6.9 %query_products.8 = (f32[1,160,2048]{2,1,0:T(8,128)S(1)}, bf16[1,160,1024]{2,1,0:T(8,128)(2,1)}, bf16[1,160,1024]{2,1,0:T(8,128)(2,1)}) custom-call(s32[2]{0:T(128)S(1)} %get-tuple-element.66.place_ref, bf16[320,2048]{1,0:T(8,128)(2,1)S(1)} %collective-permute-done.refs_1_.refs_0_, bf16[2048,8192]{1,0:T(8,128)(2,1)} %refs_1_.11, ...), custom_call_target="tpu_custom_call" | custom-call | flops 1000 | bytes 1000 | tf_op jit(solution)/shard_map/query_products/pallas_call | solution.py:87
  48.3 1.4 collective-permute-done.4.refs_1_
  50.2 2.2 %add_rows.8.refs_3_.refs_2_ = bf16[1,160,2560]{2,1,0:T(8,128)(2,1)} custom-call(f32[1,160,2048]{2,1,0:T(8,128)S(1)} %get-tuple-element.35.refs_0_, bf16[1,160,1024]{2,1,0:T(8,128)(2,1)} %collective-permute-done.4.refs_1_, bf16[1,160,1024]{2,1,0:T(8,128)(2,1)} %collective-permute-done.5.refs_2_, f32[4,160,512]{2,1,0:T(8,128)} %get-tuple-element.33.refs_3_.refs_0_, ...), custom_call_target="tpu_custom_call" | custom-call | flops 1000 | bytes 1000 | tf_op jit(solution)/shard_map/add_rows/pallas_call | solution.py:200
  52.4 1.3 collective-permute-start.13
  53.7 2.7 %add_rows.9.refs_3_ = bf16[1,160,2048]{2,1,0:T(8,128)(2,1)} custom-call(f32[2,160,2048]{2,1,0:T(8,128)} %get-tuple-element.38.refs_0_, bf16[1,160,2048]{2,1,0:T(8,128)(2,1)} %collective-permute-done.6.refs_1_, bf16[2,160,2048]{2,1,0:T(8,128)(2,1)} %collective-permute-done.7.refs_2_.refs_1_, bf16[1,160,2560]{2,1,0:T(8,128)(2,1)} %add_rows.8.refs_3_.refs_2_), custom_call_target="tpu_custom_call" | custom-call | flops 1000 | bytes 1000 | tf_op jit(solution)/shard_map/add_rows/pallas_call | solution.py:200
  56.4 2.6 %collective-permute-start.14 = (bf16[1,160,2048]{2,1,0:T(8,128)(2,1)}, bf16[1,160,2048]{2,1,0:T(8,128)(2,1)S(1)}, u32[]{:S(2)}, u32[]{:S(2)}) collective-permute-start(bf16[1,160,2048]{2,1,0:T(8,128)(2,1)} %add_rows.9.refs_3_), channel_id=1, source_target_pairs={{0,8},{4,12},{8,0},{12,4},{1,9},{5,13},{9,1},{13,5},{2,10},{6,14},... | collective-permute-start | bytes 1966088 | tf_op jit(solution)/shard_map/ppermute | solution.py:444
  59.0 1.1 copy-done.3
  60.1 7.1 %query_products.9 = (f32[1,160,2048]{2,1,0:T(8,128)}, bf16[1,160,1024]{2,1,0:T(8,128)(2,1)}, bf16[1,160,1024]{2,1,0:T(8,128)(2,1)}) custom-call(s32[2]{0:T(128)S(1)} %pad_add_fusion.4.place_ref, bf16[320,2048]{1,0:T(8,128)(2,1)S(1)} %collective-permute-done.refs_1_.refs_0_, bf16[2048,8192]{1,0:T(8,128)(2,1)} %refs_1_.11, ...), custom_call_target="tpu_custom_call" | custom-call | flops 99999997952 | bytes 100000000 | tf_op jit(solution)/shard_map/query_products/pallas_call | solution.py:87
  67.3 7.1 %query_products.10 = (f32[1,160,2048]{2,1,0:T(8,128)}, bf16[1,160,1024]{2,1,0:T(8,128)(2,1)}, bf16[1,160,1024]{2,1,0:T(8,128)(2,1)}) custom-call(s32[2]{0:T(128)S(1)} %get-tuple-element.65.place_ref, bf16[320,2048]{1,0:T(8,128)(2,1)S(1)} %collective-permute-done.refs_1_.refs_0_, bf16[2048,8192]{1,0:T(8,128)(2,1)} %refs_1_.11, ...), custom_call_target="tpu_custom_call" | custom-call | flops 1000 | bytes 1000 | tf_op jit(solution)/shard_map/query_products/pallas_call | solution.py:87
  74.5 0.5 collective-permute-start.11
  75.1 1.2 collective-permute-done.9.refs_2_.refs_1_
  76.8 1.3 collective-permute-done.8.refs_1_
  78.2 2.4 %add_rows.10.refs_2_ = bf16[1,160,2048]{2,1,0:T(8,128)(2,1)} custom-call(f32[1,160,2048]{2,1,0:T(8,128)} %get-tuple-element.40.refs_0_, bf16[1,160,1024]{2,1,0:T(8,128)(2,1)S(1)} %collective-permute-done.8.refs_1_, bf16[1,160,1024]{2,1,0:T(8,128)(2,1)} %collective-permute-done.9.refs_2_.refs_1_, f32[4,160,512]{2,1,0:T(8,128)} %get-tuple-element.33.refs_3_.refs_0_, ...), custom_call_target="tpu_custom_call" | custom-call | flops 1000 | bytes 1000 | tf_op jit(solution)/shard_map/add_rows/pallas_call | solution.py:200
  80.7 1.8 %add_rows.11.refs_7_ = bf16[1,160,512]{2,1,0:T(8,128)(2,1)} custom-call(f32[1,160,2048]{2,1,0:T(8,128)} %get-tuple-element.40.refs_0_, bf16[1,160,1024]{2,1,0:T(8,128)(2,1)} %collective-permute-done.9.refs_2_.refs_1_, bf16[1,160,2048]{2,1,0:T(8,128)(2,1)} %add_rows.10.refs_2_), custom_call_target="tpu_custom_call" | custom-call | flops 1000 | bytes 1000 | tf_op jit(solution)/shard_map/add_rows/pallas_call | solution.py:200
  82.5 0.7 collective-permute-start.10
  83.2 3.5 %collective-permute-done.14.refs_8_.refs_2_ = bf16[1,160,2048]{2,1,0:T(8,128)(2,1)S(1)} collective-permute-done((bf16[1,160,2048]{2,1,0:T(8,128)(2,1)}, bf16[1,160,2048]{2,1,0:T(8,128)(2,1)S(1)}, u32[]{:S(2)}, u32[]{:S(2)}) %collective-permute-start.14) | collective-permute-done | bytes 655392 | tf_op jit(solution)/shard_map/ppermute | solution.py:444
  86.7 1.0 collective-permute-done.13.refs_5_.refs_6_.refs_2_
  87.7 2.3 %add_rows.12.refs_3_ = bf16[1,160,2048]{2,1,0:T(8,128)(2,1)} custom-call(f32[1,160,2048]{2,1,0:T(8,128)} %get-tuple-element.43.refs_0_, bf16[1,160,1024]{2,1,0:T(8,128)(2,1)S(1)} %collective-permute-done.11.refs_1_, bf16[1,160,1024]{2,1,0:T(8,128)(2,1)S(1)} %collective-permute-done.12.refs_2_.refs_1_, f32[4,160,512]{2,1,0:T(8,128)} %get-tuple-element.33.refs_3_.refs_0_, ...), custom_call_target="tpu_custom_call" | custom-call | flops 1000 | bytes 1000 | tf_op jit(solution)/shard_map/add_rows/pallas_call | solution.py:200
  90.0 2.3 %collective-permute-start.15 = (bf16[1,160,2048]{2,1,0:T(8,128)(2,1)}, bf16[1,160,2048]{2,1,0:T(8,128)(2,1)S(1)}, u32[]{:S(2)}, u32[]{:S(2)}) collective-permute-start(bf16[1,160,2048]{2,1,0:T(8,128)(2,1)} %add_rows.12.refs_3_), channel_id=1, source_target_pairs={{0,8},{4,12},{8,0},{12,4},{1,9},{5,13},{9,1},{13,5},{2,10},{6,14},... | collective-permute-start | bytes 1966088 | tf_op jit(solution)/shard_map/ppermute | solution.py:444
  92.3 1.7 %add_rows.13.refs_4_.refs_2_ = bf16[1,160,512]{2,1,0:T(8,128)(2,1)} custom-call(f32[1,160,2048]{2,1,0:T(8,128)} %get-tuple-element.43.refs_0_, bf16[1,160,1024]{2,1,0:T(8,128)(2,1)S(1)} %collective-permute-done.12.refs_2_.refs_1_, bf16[1,160,2560]{2,1,0:T(8,128)(2,1)S(1)} %collective-permute-done.13.refs_5_.refs_6_.refs_2_, ...), custom_call_target="tpu_custom_call" | custom-call | flops 1000 | bytes 1000 | tf_op jit(solution)/shard_map/add_rows/pallas_call | solution.py:200
  94.0 7.1 %query_products.11 = (f32[1,160,2048]{2,1,0:T(8,128)}, bf16[1,160,1024]{2,1,0:T(8,128)(2,1)}, bf16[1,160,1024]{2,1,0:T(8,128)(2,1)}) custom-call(s32[2]{0:T(128)S(1)} %pad_add_fusion.6.place_ref, bf16[320,2048]{1,0:T(8,128)(2,1)S(1)} %collective-permute-done.refs_1_.refs_0_, bf16[2048,8192]{1,0:T(8,128)(2,1)} %refs_1_.11, ...), custom_call_target="tpu_custom_call" | custom-call | flops 99999997952 | bytes 100000000 | tf_op jit(solution)/shard_map/query_products/pallas_call | solution.py:87
  101.1 0.5 collective-permute-start.21
  101.6 0.6 fusion.4
  102.5 2.1 %sum_and_rotate.3.refs_0_ = bf16[160,2048]{1,0:T(8,128)(2,1)S(1)} custom-call(f32[160,128]{1,0:T(8,128)S(1)} %get-tuple-element.59.cos_ref, f32[160,128]{1,0:T(8,128)S(1)} %get-tuple-element.57.sin_ref, f32[2,160,2048]{2,1,0:T(8,128)} %get-tuple-element.38.refs_0_, bf16[2,160,2048]{2,1,0:T(8,128)(2,1)} %collective-permute-done.7.refs_2_.refs_1_, ...), custom_call_target="tpu_custom_call" | custom-call | flops 1000 | bytes 1000 | tf_op jit(solution)/shard_map/sum_and_rotate/pallas_call | solution.py:250
  104.7 7.1 %collective-permute-done.10.refs_2_.refs_1_ = bf16[1,160,2048]{2,1,0:T(8,128)(2,1)S(1)} collective-permute-done((bf16[1,160,2048]{2,1,0:T(8,128)(2,1)S(1)}, bf16[1,160,2048]{2,1,0:T(8,128)(2,1)S(1)}, u32[]{:S(2)}, u32[]{:S(2)}) %collective-permute-start.10) | collective-permute-done | bytes 655392 | tf_op jit(solution)/shard_map/ppermute | solution.py:444
  111.8 8.6 %collective-permute-done.15.refs_3_.refs_2_ = bf16[1,160,2048]{2,1,0:T(8,128)(2,1)S(1)} collective-permute-done((bf16[1,160,2048]{2,1,0:T(8,128)(2,1)}, bf16[1,160,2048]{2,1,0:T(8,128)(2,1)S(1)}, u32[]{:S(2)}, u32[]{:S(2)}) %collective-permute-start.15) | collective-permute-done | bytes 655392 | tf_op jit(solution)/shard_map/ppermute | solution.py:444
  120.4 1.6 %sum_and_rotate.4.refs_1_ = bf16[160,1536]{1,0:T(8,128)(2,1)S(1)} custom-call(f32[160,128]{1,0:T(8,128)S(1)} %get-tuple-element.58.cos_ref, f32[160,128]{1,0:T(8,128)S(1)} %get-tuple-element.56.sin_ref, f32[1,160,2048]{2,1,0:T(8,128)} %get-tuple-element.49.refs_0_, bf16[1,160,2048]{2,1,0:T(8,128)(2,1)S(1)} %collective-permute-done.10.refs_2_.refs_1_, ...), custom_call_target="tpu_custom_call" | custom-call | flops 1000 | bytes 1000 | tf_op jit(solution)/shard_map/sum_and_rotate/pallas_call | solution.py:250
  122.3 1.1 split_and_rotate.1
  123.4 0.6 collective-permute-start.16
  124.2 2.6 %collective-permute-start.27 = (bf16[1,320,128]{2,1,0:T(8,128)(2,1)S(1)}, bf16[1,320,128]{2,1,0:T(8,128)(2,1)S(1)}, u32[]{:S(2)}, u32[]{:S(2)}) collective-permute-start(bf16[1,320,128]{2,1,0:T(8,128)(2,1)S(1)} %get-tuple-element.54.refs_0_), channel_id=1, source_target_pairs={{0,12},{4,8},{8,4},{12,0},{1,13},{5,9},{9,5},{13,1},{2,14},{6,10},... | collective-permute-start | bytes 245768 | tf_op jit(solution)/shard_map/ppermute | solution.py:444
  126.9 1.8 %collective-permute-start.25 = (bf16[1,320,128]{2,1,0:T(8,128)(2,1)S(1)}, bf16[1,320,128]{2,1,0:T(8,128)(2,1)S(1)}, u32[]{:S(2)}, u32[]{:S(2)}) collective-permute-start(bf16[1,320,128]{2,1,0:T(8,128)(2,1)S(1)} %get-tuple-element.54.refs_0_), channel_id=1, source_target_pairs={{0,4},{4,0},{8,12},{12,8},{1,5},{5,1},{9,13},{13,9},{2,6},{6,2},{1... | collective-permute-start | bytes 245768 | tf_op jit(solution)/shard_map/ppermute | solution.py:444
  128.7 0.5 order_and_keys.1
  129.6 2.9 %collective-permute-start.19 = (bf16[1,160,512]{2,1,0:T(8,128)(2,1)S(1)}, bf16[1,160,512]{2,1,0:T(8,128)(2,1)S(1)}, u32[]{:S(2)}, u32[]{:S(2)}) collective-permute-start(bf16[1,160,512]{2,1,0:T(8,128)(2,1)S(1)} %copy-done), channel_id=1, source_target_pairs={{0,8},{4,12},{8,0},{12,4},{1,9},{5,13},{9,1},{13,5},{2,10},{6,14},... | collective-permute-start | bytes 491528 | tf_op jit(solution)/shard_map/ppermute | solution.py:444
  132.6 7.4 %score_heads.2 = (bf16[1,16,640,640]{3,2,1,0:T(8,128)(2,1)}, f32[8,128]{1,0:T(8,128)S(1)}) custom-call(bf16[640,640]{1,0:T(8,128)(2,1)S(1)} %get-tuple-element.46.order_ref, bf16[128,640]{1,0:T(8,128)(2,1)S(1)} %get-tuple-element.47.key_t_ref, bf16[160,2048]{1,0:T(8,128)(2,1)S(1)} %sum_and_rotate.3.refs_0_, bf16[160,1536]{1,0:T(8,128)(2,1)S(1)} %sum_and_rotate.4.refs_1_, ...), custom_call_target="tpu_custom_call" | custom-call | flops 1000 | bytes 1000 | tf_op jit(solution)/shard_map/score_heads/pallas_call | solution.py:405
  140.1 0.8 collective-permute-done.18.refs_1_
  141.0 1.1 sum_and_rotate.5.refs_1_
  142.3 2.2 %order_values.1.refs_5_ = bf16[640,512]{1,0:T(8,128)(2,1)} custom-call(s32[4]{0:T(128)S(1)} %pad_add_fusion.7.place_ref, bf16[640,640]{1,0:T(8,128)(2,1)S(1)} %get-tuple-element.46.order_ref, bf16[4,320,128]{2,1,0:T(8,128)(2,1)S(1)} %stack_slots.1.refs_0_.refs_1_, bf16[4,320,128]{2,1,0:T(8,128)(2,1)S(1)} %stack_slots.1.refs_0_.refs_1_, ...), custom_call_target="tpu_custom_call" | custom-call | tf_op jit(solution)/shard_map/order_values/pallas_call | solution.py:371
  144.4 3.2 %score_heads.3 = (bf16[1,16,640,640]{3,2,1,0:T(8,128)(2,1)}, f32[8,128]{1,0:T(8,128)}) custom-call(bf16[640,640]{1,0:T(8,128)(2,1)S(1)} %get-tuple-element.46.order_ref, bf16[128,640]{1,0:T(8,128)(2,1)S(1)} %get-tuple-element.47.key_t_ref, bf16[160,2048]{1,0:T(8,128)(2,1)S(1)} %sum_and_rotate.3.refs_0_, ...), custom_call_target="tpu_custom_call", output_to_operand_aliasing={{0}: (6, {})} | custom-call | flops 1000 | bytes 1000 | tf_op jit(solution)/shard_map/score_heads/pallas_call | solution.py:405
  (72 shorter events, 3.9 us)
Async XLA Ops:
  0.6 32.5 %collective-permute-start = (bf16[320,2048]{1,0:T(8,128)(2,1)}, bf16[320,2048]{1,0:T(8,128)(2,1)S(1)}, u32[]{:S(2)}, u32[]{:S(2)}) collective-permute-start(bf16[320,2048]{1,0:T(8,128)(2,1)} %refs_0_.5), channel_id=1, source_target_pairs={{0,2},{2,0},{1,3},{3,1},{4,6},{6,4},{5,7},{7,5},{8,10},{10,8},{9,1... | collective-permute-start | bytes 3932168 | tf_op jit(solution)/shard_map/ppermute | solution.py:474
  15.2 2.3 %collective-permute-start.1 = (bf16[2,160,1024]{2,1,0:T(8,128)(2,1)}, bf16[2,160,1024]{2,1,0:T(8,128)(2,1)S(1)}, u32[]{:S(2)}, u32[]{:S(2)}) collective-permute-start(bf16[2,160,1024]{2,1,0:T(8,128)(2,1)} %get-tuple-element.30), channel_id=1, source_target_pairs={{0,1},{1,0},{2,3},{3,2},{4,5},{5,4},{6,7},{7,6},{8,9},{9,8},{10,11... | collective-permute-start | bytes 1966088 | tf_op jit(solution)/shard_map/ppermute | solution.py:447
  15.2 3.2 %collective-permute-start.2 = (bf16[2,160,1024]{2,1,0:T(8,128)(2,1)}, bf16[2,160,1024]{2,1,0:T(8,128)(2,1)S(1)}, u32[]{:S(2)}, u32[]{:S(2)}) collective-permute-start(bf16[2,160,1024]{2,1,0:T(8,128)(2,1)} %get-tuple-element.31), channel_id=1, source_target_pairs={{0,1},{1,0},{2,3},{3,2},{4,5},{5,4},{6,7},{7,6},{8,9},{9,8},{10,11... | collective-permute-start | bytes 1966088 | tf_op jit(solution)/shard_map/ppermute | solution.py:447
  19.6 34.1 %collective-permute-start.7 = (bf16[2,160,2048]{2,1,0:T(8,128)(2,1)}, bf16[2,160,2048]{2,1,0:T(8,128)(2,1)}, u32[]{:S(2)}, u32[]{:S(2)}) collective-permute-start(bf16[2,160,2048]{2,1,0:T(8,128)(2,1)} %add_rows.7.refs_2_), channel_id=1, source_target_pairs={{0,4},{4,0},{8,12},{12,8},{1,5},{5,1},{9,13},{13,9},{2,6},{6,2},{1... | collective-permute-start | bytes 3932168 | tf_op jit(solution)/shard_map/ppermute | solution.py:444
  40.2 9.9 %collective-permute-start.3 = (bf16[4,160,512]{2,1,0:T(8,128)(2,1)}, bf16[4,160,512]{2,1,0:T(8,128)(2,1)S(1)}, u32[]{:S(2)}, u32[]{:S(2)}) collective-permute-start(bf16[4,160,512]{2,1,0:T(8,128)(2,1)} %get-tuple-element.34.refs_2_), channel_id=1, source_target_pairs={{0,1},{1,0},{2,3},{3,2},{4,5},{5,4},{6,7},{7,6},{8,9},{9,8},{10,11... | collective-permute-start | bytes 1966088 | tf_op jit(solution)/shard_map/ppermute | solution.py:447
  40.3 13.4 %collective-permute-start.6 = (bf16[1,160,2048]{2,1,0:T(8,128)(2,1)}, bf16[1,160,2048]{2,1,0:T(8,128)(2,1)}, u32[]{:S(2)}, u32[]{:S(2)}) collective-permute-start(bf16[1,160,2048]{2,1,0:T(8,128)(2,1)} %get-tuple-element.32.refs_4_), channel_id=1, source_target_pairs={{0,1},{1,0},{2,3},{3,2},{4,5},{5,4},{6,7},{7,6},{8,9},{9,8},{10,11... | collective-permute-start | bytes 1966088 | tf_op jit(solution)/shard_map/ppermute | solution.py:447
  47.7 2.0 %collective-permute-start.4 = (bf16[1,160,1024]{2,1,0:T(8,128)(2,1)}, bf16[1,160,1024]{2,1,0:T(8,128)(2,1)}, u32[]{:S(2)}, u32[]{:S(2)}) collective-permute-start(bf16[1,160,1024]{2,1,0:T(8,128)(2,1)} %get-tuple-element.36), channel_id=1, source_target_pairs={{0,1},{1,0},{2,3},{3,2},{4,5},{5,4},{6,7},{7,6},{8,9},{9,8},{10,11... | collective-permute-start | bytes 983048 | tf_op jit(solution)/shard_map/ppermute | solution.py:447
  47.8 2.4 %collective-permute-start.5 = (bf16[1,160,1024]{2,1,0:T(8,128)(2,1)}, bf16[1,160,1024]{2,1,0:T(8,128)(2,1)}, u32[]{:S(2)}, u32[]{:S(2)}) collective-permute-start(bf16[1,160,1024]{2,1,0:T(8,128)(2,1)} %get-tuple-element.37), channel_id=1, source_target_pairs={{0,1},{1,0},{2,3},{3,2},{4,5},{5,4},{6,7},{7,6},{8,9},{9,8},{10,11... | collective-permute-start | bytes 983048 | tf_op jit(solution)/shard_map/ppermute | solution.py:447
  52.4 35.3 %collective-permute-start.13 = (bf16[1,160,2560]{2,1,0:T(8,128)(2,1)}, bf16[1,160,2560]{2,1,0:T(8,128)(2,1)S(1)}, u32[]{:S(2)}, u32[]{:S(2)}) collective-permute-start(bf16[1,160,2560]{2,1,0:T(8,128)(2,1)} %add_rows.8.refs_3_.refs_2_), channel_id=1, source_target_pairs={{0,4},{4,0},{8,12},{12,8},{1,5},{5,1},{9,13},{13,9},{2,6},{6,2},{1... | collective-permute-start | bytes 2457608 | tf_op jit(solution)/shard_map/ppermute | solution.py:444
  56.4 30.3 %collective-permute-start.14 = (bf16[1,160,2048]{2,1,0:T(8,128)(2,1)}, bf16[1,160,2048]{2,1,0:T(8,128)(2,1)S(1)}, u32[]{:S(2)}, u32[]{:S(2)}) collective-permute-start(bf16[1,160,2048]{2,1,0:T(8,128)(2,1)} %add_rows.9.refs_3_), channel_id=1, source_target_pairs={{0,8},{4,12},{8,0},{12,4},{1,9},{5,13},{9,1},{13,5},{2,10},{6,14},... | collective-permute-start | bytes 1966088 | tf_op jit(solution)/shard_map/ppermute | solution.py:444
  59.0 1.1 copy-start.3
  67.3 9.2 %copy-start.5 = (s32[640]{0:T(1024)S(1)}, s32[640]{0:T(1024)}, u32[]{:S(2)}) copy-start(s32[640]{0:T(1024)} %param.10) | copy-start | bytes 7684
  67.3 9.2 %copy-start.6 = (s32[640]{0:T(1024)S(1)}, s32[640]{0:T(1024)}, u32[]{:S(2)}) copy-start(s32[640]{0:T(1024)} %param.11) | copy-start | bytes 7684
  74.3 2.0 %collective-permute-start.9 = (bf16[1,160,1024]{2,1,0:T(8,128)(2,1)}, bf16[1,160,1024]{2,1,0:T(8,128)(2,1)}, u32[]{:S(2)}, u32[]{:S(2)}) collective-permute-start(bf16[1,160,1024]{2,1,0:T(8,128)(2,1)} %get-tuple-element.42), channel_id=1, source_target_pairs={{0,1},{1,0},{2,3},{3,2},{4,5},{5,4},{6,7},{7,6},{8,9},{9,8},{10,11... | collective-permute-start | bytes 983048 | tf_op jit(solution)/shard_map/ppermute | solution.py:447
  74.5 8.6 %collective-permute-start.11 = (bf16[1,160,1024]{2,1,0:T(8,128)(2,1)}, bf16[1,160,1024]{2,1,0:T(8,128)(2,1)S(1)}, u32[]{:S(2)}, u32[]{:S(2)}) collective-permute-start(bf16[1,160,1024]{2,1,0:T(8,128)(2,1)} %get-tuple-element.39.refs_2_), channel_id=1, source_target_pairs={{0,1},{1,0},{2,3},{3,2},{4,5},{5,4},{6,7},{7,6},{8,9},{9,8},{10,11... | collective-permute-start | bytes 983048 | tf_op jit(solution)/shard_map/ppermute | solution.py:447
  75.0 7.4 %collective-permute-start.12 = (bf16[1,160,1024]{2,1,0:T(8,128)(2,1)}, bf16[1,160,1024]{2,1,0:T(8,128)(2,1)S(1)}, u32[]{:S(2)}, u32[]{:S(2)}) collective-permute-start(bf16[1,160,1024]{2,1,0:T(8,128)(2,1)} %get-tuple-element.44), channel_id=1, source_target_pairs={{0,1},{1,0},{2,3},{3,2},{4,5},{5,4},{6,7},{7,6},{8,9},{9,8},{10,11... | collective-permute-start | bytes 983048 | tf_op jit(solution)/shard_map/ppermute | solution.py:447
  76.3 1.8 %collective-permute-start.8 = (bf16[1,160,1024]{2,1,0:T(8,128)(2,1)}, bf16[1,160,1024]{2,1,0:T(8,128)(2,1)S(1)}, u32[]{:S(2)}, u32[]{:S(2)}) collective-permute-start(bf16[1,160,1024]{2,1,0:T(8,128)(2,1)} %get-tuple-element.41.refs_5_), channel_id=1, source_target_pairs={{0,1},{1,0},{2,3},{3,2},{4,5},{5,4},{6,7},{7,6},{8,9},{9,8},{10,11... | collective-permute-start | bytes 983048 | tf_op jit(solution)/shard_map/ppermute | solution.py:447
  78.2 2.4 %copy-start.7 = (bf16[1,160,2048]{2,1,0:T(8,128)(2,1)S(1)}, bf16[1,160,2048]{2,1,0:T(8,128)(2,1)}, u32[]{:S(2)}) copy-start(bf16[1,160,2048]{2,1,0:T(8,128)(2,1)} %get-tuple-element.48) | copy-start | bytes 1966084
  80.5 1.9 %copy-start.4 = (bf16[1,160,2048]{2,1,0:T(8,128)(2,1)S(1)}, bf16[1,160,2048]{2,1,0:T(8,128)(2,1)}, u32[]{:S(2)}) copy-start(bf16[1,160,2048]{2,1,0:T(8,128)(2,1)} %add_rows.10.refs_2_) | copy-start | bytes 1966084
  80.5 22.0 %collective-permute-start.17 = (bf16[1,160,2048]{2,1,0:T(8,128)(2,1)S(1)}, bf16[1,160,2048]{2,1,0:T(8,128)(2,1)S(1)}, u32[]{:S(2)}, u32[]{:S(2)}) collective-permute-start(bf16[1,160,2048]{2,1,0:T(8,128)(2,1)S(1)} %copy-done.7), channel_id=1, source_target_pairs={{0,1},{1,0},{2,3},{3,2},{4,5},{5,4},{6,7},{7,6},{8,9},{9,8},{10,11... | collective-permute-start | bytes 1966088 | tf_op jit(solution)/shard_map/ppermute | solution.py:447
  82.5 29.3 %collective-permute-start.10 = (bf16[1,160,2048]{2,1,0:T(8,128)(2,1)S(1)}, bf16[1,160,2048]{2,1,0:T(8,128)(2,1)S(1)}, u32[]{:S(2)}, u32[]{:S(2)}) collective-permute-start(bf16[1,160,2048]{2,1,0:T(8,128)(2,1)S(1)} %copy-done.4), channel_id=1, source_target_pairs={{0,4},{4,0},{8,12},{12,8},{1,5},{5,1},{9,13},{13,9},{2,6},{6,2},{1... | collective-permute-start | bytes 1966088 | tf_op jit(solution)/shard_map/ppermute | solution.py:444
  90.0 30.3 %collective-permute-start.15 = (bf16[1,160,2048]{2,1,0:T(8,128)(2,1)}, bf16[1,160,2048]{2,1,0:T(8,128)(2,1)S(1)}, u32[]{:S(2)}, u32[]{:S(2)}) collective-permute-start(bf16[1,160,2048]{2,1,0:T(8,128)(2,1)} %add_rows.12.refs_3_), channel_id=1, source_target_pairs={{0,8},{4,12},{8,0},{12,4},{1,9},{5,13},{9,1},{13,5},{2,10},{6,14},... | collective-permute-start | bytes 1966088 | tf_op jit(solution)/shard_map/ppermute | solution.py:444
  101.1 1.5 copy-start
  101.1 10.7 %collective-permute-start.20 = (bf16[1,160,1024]{2,1,0:T(8,128)(2,1)}, bf16[1,160,1024]{2,1,0:T(8,128)(2,1)S(1)}, u32[]{:S(2)}, u32[]{:S(2)}) collective-permute-start(bf16[1,160,1024]{2,1,0:T(8,128)(2,1)} %get-tuple-element.50), channel_id=1, source_target_pairs={{0,1},{1,0},{2,3},{3,2},{4,5},{5,4},{6,7},{7,6},{8,9},{9,8},{10,11... | collective-permute-start | bytes 983048 | tf_op jit(solution)/shard_map/ppermute | solution.py:447
  101.1 10.7 %collective-permute-start.21 = (bf16[1,160,1024]{2,1,0:T(8,128)(2,1)}, bf16[1,160,1024]{2,1,0:T(8,128)(2,1)S(1)}, u32[]{:S(2)}, u32[]{:S(2)}) collective-permute-start(bf16[1,160,1024]{2,1,0:T(8,128)(2,1)} %get-tuple-element.51), channel_id=1, source_target_pairs={{0,1},{1,0},{2,3},{3,2},{4,5},{5,4},{6,7},{7,6},{8,9},{9,8},{10,11... | collective-permute-start | bytes 983048 | tf_op jit(solution)/shard_map/ppermute | solution.py:447
  102.5 17.9 %copy-start.1 = (f32[160,128]{1,0:T(8,128)}, f32[160,128]{1,0:T(8,128)S(1)}, u32[]{:S(2)}) copy-start(f32[160,128]{1,0:T(8,128)S(1)} %get-tuple-element.56.sin_ref) | copy-start | bytes 245764
  104.6 24.7 %collective-permute-start.22 = (bf16[160,2048]{1,0:T(8,128)(2,1)S(1)}, bf16[160,2048]{1,0:T(8,128)(2,1)S(1)}, u32[]{:S(2)}, u32[]{:S(2)}) collective-permute-start(bf16[160,2048]{1,0:T(8,128)(2,1)S(1)} %sum_and_rotate.3.refs_0_), channel_id=1, source_target_pairs={{0,1},{1,0},{2,3},{3,2},{4,5},{5,4},{6,7},{7,6},{8,9},{9,8},{10,11... | collective-permute-start | bytes 1966088 | tf_op jit(solution)/shard_map/ppermute | solution.py:447
  122.0 7.7 %collective-permute-start.23 = (bf16[160,1536]{1,0:T(8,128)(2,1)S(1)}, bf16[160,1536]{1,0:T(8,128)(2,1)}, u32[]{:S(2)}, u32[]{:S(2)}) collective-permute-start(bf16[160,1536]{1,0:T(8,128)(2,1)S(1)} %sum_and_rotate.4.refs_1_), channel_id=1, source_target_pairs={{0,1},{1,0},{2,3},{3,2},{4,5},{5,4},{6,7},{7,6},{8,9},{9,8},{10,11... | collective-permute-start | bytes 1474568 | tf_op jit(solution)/shard_map/ppermute | solution.py:447
  123.4 3.5 %collective-permute-start.16 = (bf16[320,128]{1,0:T(8,128)(2,1)S(1)}, bf16[320,128]{1,0:T(8,128)(2,1)S(1)}, u32[]{:S(2)}, u32[]{:S(2)}) collective-permute-start(bf16[320,128]{1,0:T(8,128)(2,1)S(1)} %get-tuple-element.45.own_ref), channel_id=1, source_target_pairs={{0,1},{1,0},{2,3},{3,2},{4,5},{5,4},{6,7},{7,6},{8,9},{9,8},{10,11... | collective-permute-start | bytes 245768 | tf_op jit(solution)/shard_map/ppermute | solution.py:447
  124.2 15.7 %collective-permute-start.27 = (bf16[1,320,128]{2,1,0:T(8,128)(2,1)S(1)}, bf16[1,320,128]{2,1,0:T(8,128)(2,1)S(1)}, u32[]{:S(2)}, u32[]{:S(2)}) collective-permute-start(bf16[1,320,128]{2,1,0:T(8,128)(2,1)S(1)} %get-tuple-element.54.refs_0_), channel_id=1, source_target_pairs={{0,12},{4,8},{8,4},{12,0},{1,13},{5,9},{9,5},{13,1},{2,14},{6,10},... | collective-permute-start | bytes 245768 | tf_op jit(solution)/shard_map/ppermute | solution.py:444
  126.9 13.1 %collective-permute-start.26 = (bf16[1,320,128]{2,1,0:T(8,128)(2,1)S(1)}, bf16[1,320,128]{2,1,0:T(8,128)(2,1)S(1)}, u32[]{:S(2)}, u32[]{:S(2)}) collective-permute-start(bf16[1,320,128]{2,1,0:T(8,128)(2,1)S(1)} %get-tuple-element.54.refs_0_), channel_id=1, source_target_pairs={{0,8},{4,12},{8,0},{12,4},{1,9},{5,13},{9,1},{13,5},{2,10},{6,14},... | collective-permute-start | bytes 245768 | tf_op jit(solution)/shard_map/ppermute | solution.py:444
  126.9 13.1 %collective-permute-start.25 = (bf16[1,320,128]{2,1,0:T(8,128)(2,1)S(1)}, bf16[1,320,128]{2,1,0:T(8,128)(2,1)S(1)}, u32[]{:S(2)}, u32[]{:S(2)}) collective-permute-start(bf16[1,320,128]{2,1,0:T(8,128)(2,1)S(1)} %get-tuple-element.54.refs_0_), channel_id=1, source_target_pairs={{0,4},{4,0},{8,12},{12,8},{1,5},{5,1},{9,13},{13,9},{2,6},{6,2},{1... | collective-permute-start | bytes 245768 | tf_op jit(solution)/shard_map/ppermute | solution.py:444
  129.3 11.7 %collective-permute-start.18 = (bf16[1,160,512]{2,1,0:T(8,128)(2,1)}, bf16[1,160,512]{2,1,0:T(8,128)(2,1)S(1)}, u32[]{:S(2)}, u32[]{:S(2)}) collective-permute-start(bf16[1,160,512]{2,1,0:T(8,128)(2,1)} %add_rows.11.refs_7_), channel_id=1, source_target_pairs={{0,4},{4,0},{8,12},{12,8},{1,5},{5,1},{9,13},{13,9},{2,6},{6,2},{1... | collective-permute-start | bytes 491528 | tf_op jit(solution)/shard_map/ppermute | solution.py:444
  129.6 11.3 %collective-permute-start.19 = (bf16[1,160,512]{2,1,0:T(8,128)(2,1)S(1)}, bf16[1,160,512]{2,1,0:T(8,128)(2,1)S(1)}, u32[]{:S(2)}, u32[]{:S(2)}) collective-permute-start(bf16[1,160,512]{2,1,0:T(8,128)(2,1)S(1)} %copy-done), channel_id=1, source_target_pairs={{0,8},{4,12},{8,0},{12,4},{1,9},{5,13},{9,1},{13,5},{2,10},{6,14},... | collective-permute-start | bytes 491528 | tf_op jit(solution)/shard_map/ppermute | solution.py:444
  132.6 8.4 %copy-start.2 = (f32[160,128]{1,0:T(8,128)S(1)}, f32[160,128]{1,0:T(8,128)}, u32[]{:S(2)}) copy-start(f32[160,128]{1,0:T(8,128)} %copy-done.1) | copy-start | bytes 245764
  140.0 2.2 %collective-permute-start.28 = (bf16[4,320,128]{2,1,0:T(8,128)(2,1)S(1)}, bf16[4,320,128]{2,1,0:T(8,128)(2,1)S(1)}, u32[]{:S(2)}, u32[]{:S(2)}) collective-permute-start(bf16[4,320,128]{2,1,0:T(8,128)(2,1)S(1)} %stack_slots.1.refs_0_.refs_1_), channel_id=1, source_target_pairs={{0,1},{1,0},{2,3},{3,2},{4,5},{5,4},{6,7},{7,6},{8,9},{9,8},{10,11... | collective-permute-start | bytes 983048 | tf_op jit(solution)/shard_map/ppermute | solution.py:447
  142.1 2.3 %collective-permute-start.24 = (bf16[160,512]{1,0:T(8,128)(2,1)S(1)}, bf16[160,512]{1,0:T(8,128)(2,1)S(1)}, u32[]{:S(2)}, u32[]{:S(2)}) collective-permute-start(bf16[160,512]{1,0:T(8,128)(2,1)S(1)} %sum_and_rotate.5.refs_1_), channel_id=1, source_target_pairs={{0,1},{1,0},{2,3},{3,2},{4,5},{5,4},{6,7},{7,6},{8,9},{9,8},{10,11... | collective-permute-start | bytes 491528 | tf_op jit(solution)/shard_map/ppermute | solution.py:447

commit v16 on v15

--- a/solution.py
+++ b/solution.py
@@ -100,7 +100,7 @@
         compiler_params=pltpu.CompilerParams(vmem_limit_bytes=VMEM_BYTES),
         cost_estimate=cost,
         name="query_products",
-    )(place, *blocks, *in_hbm([w]), *in_hbm(after[:1]), *after[1:])
+    )(place, *blocks, *in_hbm([w, *after]))
     return outs[0], outs[1:]
 
 
@@ -240,7 +240,7 @@
             out_ref[:, cols.start + head * DH : cols.start + (head + 1) * DH] = value
 
 
-def sum_and_rotate(cosine, sine, terms, gots, cols, after=()):
+def sum_and_rotate(cosine, sine, terms, gots, cols, after=(), near=False):
     rows = cosine.shape[0]
     table = pl.BlockSpec((rows, DH), lambda j: (0, 0))
 
@@ -262,7 +262,7 @@
     )(
         cosine,
         sine,
-        *in_hbm([terms[0][0]]),
+        *([terms[0][0]] if near else in_hbm([terms[0][0]])),
         *[term[0] for term in terms[1:]],
         *[got for got, _, _ in gots],
         *after,
@@ -496,7 +496,9 @@
         keep, slot, got = owns[b]
         added = [(keep, slot, start)] + terms
         gots = segments(got, start, stop)
-        turned = sum_and_rotate(cosine[table], sine[table], added, gots, stop - start, behind)
+        turned = sum_and_rotate(
+            cosine[table], sine[table], added, gots, stop - start, behind, b == last
+        )
         return turned, other_core(turned)
 
     def add_even(b, start, cols, pair, behind):
@@ -504,7 +506,7 @@
             return [], behind
         keep, got = evens[b]
         summed = add_rows(
-            0, len(even), half, 0, keep, got, start, cols, pair, len(odd), (fars[b],), behind
+            0, len(even), half, 0, keep, got, start, cols, pair, len(odd), (fars[b],), behind, b == last
         )
         terms, first = spread({x: summed[k] for k, x in enumerate(even)})
         return [(term, 0, 0) for term in terms], (first,)
@@ -534,7 +536,7 @@
             evens.append((keep, got[:1] if len(even) == 1 else [jnp.concatenate(got[:-1])]))
             owns.append((keep, len(even), got[-1:]))
         else:
-            keep, got, given = project(even, [block], tile, after, HEAVY)
+            keep, got, given = project(even, [block], tile, after, HEAVY, near=True)
             evens.append((keep, got))
         after = (given,)
     near_keep, near_got, given = project([1], placed[last:], tile, after)
@@ -551,7 +553,7 @@
     for part, (start, stop) in zip(parts, ranges):
         added, after = add_even(last, start, stop - start, () if start else pair, after)
         part += added
-    keep, got, _ = project([0], placed[last:], tile, after, HEAVY)
+    keep, got, _ = project([0], placed[last:], tile, after, HEAVY, near=True)
     owns.append((keep, 0, got))
 
     if fast_pair:

time: 148 us -> 150 us (1.014)
  waiting for transfers between devices: 28.2 us -> 30.4 us
  transfers between devices with their start and end apart: 29 -> 29, of which waited for: 11 -> 11; matrix products, arithmetic and copies ran while one was open for 2% -> 2% of each run, Pallas kernels for 60% -> 59%
where the time goes in v16:
time: 150 us; the launch traced here: 149 us
  Pallas kernels  91.8 us (61%)
  waiting for transfers between devices  30.4 us (20%)
  starting transfers between devices  23.6 us (16%)
  other arithmetic  2.04 us (1%)
    pallas_call x6, Pallas kernels, project_query(): pl.pallas_call(functools.partial(query_kernel, count, pieces, by_slot), g...  51.1 us
    ppermute x10, waiting for transfers between devices, swap(): return lax.ppermute(x, 'fsdp', [(i, i ^ bit) for i in range(shards)])  22.4 us
    ppermute x10, starting transfers between devices, swap(): return lax.ppermute(x, 'fsdp', [(i, i ^ bit) for i in range(shards)])  16.3 us
    pallas_call x7, Pallas kernels, add_rows(): pl.pallas_call(functools.partial(add_kernel, len(gots), len(pair) // 2, l...  13.1 us
    pallas_call x2, Pallas kernels, score_heads(): pl.pallas_call(functools.partial(score_kernel, len(queries)), grid=(count...  11.7 us
    ppermute x18, waiting for transfers between devices, other_core(): return lax.ppermute(x, 'rep', [(0, 1), (1, 0)])  7.99 us
    pallas_call x1, Pallas kernels, project_pair(): pl.pallas_call(functools.partial(pair_kernel, count), grid_spec=pltpu.Pre...  7.11 us
    ppermute x18, starting transfers between devices, other_core(): return lax.ppermute(x, 'rep', [(0, 1), (1, 0)])  4.23 us
  transfers between devices with their start and end apart: 29, of which 11 were waited for; matrix products, arithmetic and copies ran while one was open for 2% of the time, Pallas kernels for 59%

profile of v16, /device:TPU:0, one launch (start us, length us, event | category | flops | bytes accessed | tf_op | source)
XLA Modules:
  0.0 149.0 jit_solution(887786953698181581)
XLA Ops:
  0.6 3.0 %collective-permute-start = (bf16[320,2048]{1,0:T(8,128)(2,1)}, bf16[320,2048]{1,0:T(8,128)(2,1)S(1)}, u32[]{:S(2)}, u32[]{:S(2)}) collective-permute-start(bf16[320,2048]{1,0:T(8,128)(2,1)} %refs_0_.5), channel_id=1, source_target_pairs={{0,2},{2,0},{1,3},{3,1},{4,6},{6,4},{5,7},{7,5},{8,10},{10,8},{9,1... | collective-permute-start | bytes 3932168 | tf_op jit(solution)/shard_map/ppermute | solution.py:474
  3.7 11.5 %query_products.6 = (f32[2,160,2048]{2,1,0:T(8,128)S(1)}, bf16[2,160,1024]{2,1,0:T(8,128)(2,1)}, bf16[2,160,1024]{2,1,0:T(8,128)(2,1)}) custom-call(s32[3]{0:T(128)S(1)} %pad_add_fusion.2.place_ref, bf16[320,2048]{1,0:T(8,128)(2,1)} %refs_0_.5, bf16[2048,8192]{1,0:T(8,128)(2,1)} %refs_1_.11), custom_call_target="tpu_custom_call" | custom-call | flops 1000 | bytes 1000 | tf_op jit(solution)/shard_map/query_products/pallas_call | solution.py:87
  15.2 0.5 collective-permute-start.2
  15.7 1.8 %collective-permute-done.1.refs_1_ = bf16[2,160,1024]{2,1,0:T(8,128)(2,1)S(1)} collective-permute-done((bf16[2,160,1024]{2,1,0:T(8,128)(2,1)}, bf16[2,160,1024]{2,1,0:T(8,128)(2,1)S(1)}, u32[]{:S(2)}, u32[]{:S(2)}) %collective-permute-start.1) | collective-permute-done | bytes 655392 | tf_op jit(solution)/shard_map/ppermute | solution.py:447
  17.5 0.9 collective-permute-done.2.refs_2_
  18.5 1.2 add_rows.7.refs_2_
  19.6 1.6 %collective-permute-start.7 = (bf16[2,160,2048]{2,1,0:T(8,128)(2,1)}, bf16[2,160,2048]{2,1,0:T(8,128)(2,1)}, u32[]{:S(2)}, u32[]{:S(2)}) collective-permute-start(bf16[2,160,2048]{2,1,0:T(8,128)(2,1)} %add_rows.7.refs_2_), channel_id=1, source_target_pairs={{0,4},{4,0},{8,12},{12,8},{1,5},{5,1},{9,13},{13,9},{2,6},{6,2},{1... | collective-permute-start | bytes 3932168 | tf_op jit(solution)/shard_map/ppermute | solution.py:444
  21.4 11.7 %query_products.7 = (f32[2,160,2048]{2,1,0:T(8,128)}, bf16[1,160,2048]{2,1,0:T(8,128)(2,1)}, bf16[1,160,2048]{2,1,0:T(8,128)(2,1)}) custom-call(s32[3]{0:T(128)S(1)} %pad_add_fusion.1.place_ref, bf16[320,2048]{1,0:T(8,128)(2,1)} %refs_0_.5, bf16[2048,8192]{1,0:T(8,128)(2,1)} %refs_1_.11, bf16[2,160,2048]{2,1,0:T(8,128)(2,1)} %add_rows.7.refs_2_), custom_call_target="tpu_custom_call" | custom-call | flops 1000 | bytes 1000 | tf_op jit(solution)/shard_map/query_products/pallas_call | solution.py:87
  33.1 7.1 %key_value_products.1 = (f32[4,160,512]{2,1,0:T(8,128)}, bf16[4,160,512]{2,1,0:T(8,128)(2,1)}) custom-call(s32[5]{0:T(128)S(1)} %stack.62.place_ref, bf16[320,2048]{1,0:T(8,128)(2,1)} %refs_0_.5, bf16[320,2048]{1,0:T(8,128)(2,1)S(1)} %collective-permute-done.refs_1_.refs_0_, bf16[2048,512]{1,0:T(8,128)(2,1)} %refs_2_.1, bf16[2048,512]{1,0:T(8,128)(2,1)} %refs_3_.1, ...), custom_call_target="tpu_custom_call" | custom-call | flops 1000 | bytes 1000 | tf_op jit(solution)/shard_map/key_value_products/pallas_call | solution.py:132
  40.2 0.5 collective-permute-start.6
  40.8 6.9 %query_products.8 = (f32[1,160,2048]{2,1,0:T(8,128)S(1)}, bf16[1,160,1024]{2,1,0:T(8,128)(2,1)}, bf16[1,160,1024]{2,1,0:T(8,128)(2,1)}) custom-call(s32[2]{0:T(128)S(1)} %get-tuple-element.66.place_ref, bf16[320,2048]{1,0:T(8,128)(2,1)S(1)} %collective-permute-done.refs_1_.refs_0_, bf16[2048,8192]{1,0:T(8,128)(2,1)} %refs_1_.11, ...), custom_call_target="tpu_custom_call" | custom-call | flops 1000 | bytes 1000 | tf_op jit(solution)/shard_map/query_products/pallas_call | solution.py:87
  48.3 1.4 collective-permute-done.4.refs_1_
  49.7 0.5 collective-permute-done.5.refs_2_
  50.1 2.2 %add_rows.8.refs_3_.refs_2_ = bf16[1,160,2560]{2,1,0:T(8,128)(2,1)} custom-call(f32[1,160,2048]{2,1,0:T(8,128)S(1)} %get-tuple-element.35.refs_0_, bf16[1,160,1024]{2,1,0:T(8,128)(2,1)} %collective-permute-done.4.refs_1_, bf16[1,160,1024]{2,1,0:T(8,128)(2,1)} %collective-permute-done.5.refs_2_, f32[4,160,512]{2,1,0:T(8,128)} %get-tuple-element.33.refs_3_.refs_0_, ...), custom_call_target="tpu_custom_call" | custom-call | flops 1000 | bytes 1000 | tf_op jit(solution)/shard_map/add_rows/pallas_call | solution.py:200
  52.4 1.3 collective-permute-start.13
  53.7 2.7 %add_rows.9.refs_3_ = bf16[1,160,2048]{2,1,0:T(8,128)(2,1)} custom-call(f32[2,160,2048]{2,1,0:T(8,128)} %get-tuple-element.38.refs_0_, bf16[1,160,2048]{2,1,0:T(8,128)(2,1)} %collective-permute-done.6.refs_1_, bf16[2,160,2048]{2,1,0:T(8,128)(2,1)} %collective-permute-done.7.refs_2_.refs_1_, bf16[1,160,2560]{2,1,0:T(8,128)(2,1)} %add_rows.8.refs_3_.refs_2_), custom_call_target="tpu_custom_call" | custom-call | flops 1000 | bytes 1000 | tf_op jit(solution)/shard_map/add_rows/pallas_call | solution.py:200
  56.4 2.6 %collective-permute-start.14 = (bf16[1,160,2048]{2,1,0:T(8,128)(2,1)}, bf16[1,160,2048]{2,1,0:T(8,128)(2,1)S(1)}, u32[]{:S(2)}, u32[]{:S(2)}) collective-permute-start(bf16[1,160,2048]{2,1,0:T(8,128)(2,1)} %add_rows.9.refs_3_), channel_id=1, source_target_pairs={{0,8},{4,12},{8,0},{12,4},{1,9},{5,13},{9,1},{13,5},{2,10},{6,14},... | collective-permute-start | bytes 1966088 | tf_op jit(solution)/shard_map/ppermute | solution.py:444
  59.0 6.9 %query_products.9 = (f32[1,160,2048]{2,1,0:T(8,128)S(1)}, bf16[1,160,1024]{2,1,0:T(8,128)(2,1)}, bf16[1,160,1024]{2,1,0:T(8,128)(2,1)}) custom-call(s32[2]{0:T(128)S(1)} %pad_add_fusion.4.place_ref, bf16[320,2048]{1,0:T(8,128)(2,1)S(1)} %collective-permute-done.refs_1_.refs_0_, bf16[2048,8192]{1,0:T(8,128)(2,1)} %refs_1_.11, ...), custom_call_target="tpu_custom_call" | custom-call | flops 99999997952 | bytes 100000000 | tf_op jit(solution)/shard_map/query_products/pallas_call | solution.py:87
  65.9 7.1 %query_products.10 = (f32[1,160,2048]{2,1,0:T(8,128)}, bf16[1,160,1024]{2,1,0:T(8,128)(2,1)}, bf16[1,160,1024]{2,1,0:T(8,128)(2,1)}) custom-call(s32[2]{0:T(128)S(1)} %get-tuple-element.65.place_ref, bf16[320,2048]{1,0:T(8,128)(2,1)S(1)} %collective-permute-done.refs_1_.refs_0_, bf16[2048,8192]{1,0:T(8,128)(2,1)} %refs_1_.11, ...), custom_call_target="tpu_custom_call" | custom-call | flops 1000 | bytes 1000 | tf_op jit(solution)/shard_map/query_products/pallas_call | solution.py:87
  73.3 0.5 collective-permute-start.11
  73.8 1.2 collective-permute-done.9.refs_2_.refs_1_
  75.5 1.3 collective-permute-done.8.refs_1_
  76.9 2.4 %add_rows.10.refs_2_ = bf16[1,160,2048]{2,1,0:T(8,128)(2,1)} custom-call(f32[1,160,2048]{2,1,0:T(8,128)} %get-tuple-element.40.refs_0_, bf16[1,160,1024]{2,1,0:T(8,128)(2,1)S(1)} %collective-permute-done.8.refs_1_, bf16[1,160,1024]{2,1,0:T(8,128)(2,1)} %collective-permute-done.9.refs_2_.refs_1_, f32[4,160,512]{2,1,0:T(8,128)} %get-tuple-element.33.refs_3_.refs_0_, ...), custom_call_target="tpu_custom_call" | custom-call | flops 1000 | bytes 1000 | tf_op jit(solution)/shard_map/add_rows/pallas_call | solution.py:200
  79.5 1.8 %add_rows.11.refs_7_ = bf16[1,160,512]{2,1,0:T(8,128)(2,1)} custom-call(f32[1,160,2048]{2,1,0:T(8,128)} %get-tuple-element.40.refs_0_, bf16[1,160,1024]{2,1,0:T(8,128)(2,1)} %collective-permute-done.9.refs_2_.refs_1_, bf16[1,160,2048]{2,1,0:T(8,128)(2,1)} %add_rows.10.refs_2_), custom_call_target="tpu_custom_call" | custom-call | flops 1000 | bytes 1000 | tf_op jit(solution)/shard_map/add_rows/pallas_call | solution.py:200
  81.3 0.7 collective-permute-start.10
  82.0 4.7 %collective-permute-done.14.refs_8_.refs_2_ = bf16[1,160,2048]{2,1,0:T(8,128)(2,1)S(1)} collective-permute-done((bf16[1,160,2048]{2,1,0:T(8,128)(2,1)}, bf16[1,160,2048]{2,1,0:T(8,128)(2,1)S(1)}, u32[]{:S(2)}, u32[]{:S(2)}) %collective-permute-start.14) | collective-permute-done | bytes 655392 | tf_op jit(solution)/shard_map/ppermute | solution.py:444
  86.7 1.0 collective-permute-done.13.refs_5_.refs_6_.refs_2_
  87.7 2.1 %add_rows.12.refs_3_ = bf16[1,160,2048]{2,1,0:T(8,128)(2,1)} custom-call(f32[1,160,2048]{2,1,0:T(8,128)S(1)} %copy-done.1, bf16[1,160,1024]{2,1,0:T(8,128)(2,1)S(1)} %collective-permute-done.11.refs_1_, bf16[1,160,1024]{2,1,0:T(8,128)(2,1)S(1)} %collective-permute-done.12.refs_2_.refs_1_, f32[4,160,512]{2,1,0:T(8,128)} %get-tuple-element.33.refs_3_.refs_0_, ...), custom_call_target="tpu_custom_call" | custom-call | flops 1000 | bytes 1000 | tf_op jit(solution)/shard_map/add_rows/pallas_call | solution.py:200
  89.8 2.4 %collective-permute-start.15 = (bf16[1,160,2048]{2,1,0:T(8,128)(2,1)}, bf16[1,160,2048]{2,1,0:T(8,128)(2,1)S(1)}, u32[]{:S(2)}, u32[]{:S(2)}) collective-permute-start(bf16[1,160,2048]{2,1,0:T(8,128)(2,1)} %add_rows.12.refs_3_), channel_id=1, source_target_pairs={{0,8},{4,12},{8,0},{12,4},{1,9},{5,13},{9,1},{13,5},{2,10},{6,14},... | collective-permute-start | bytes 1966088 | tf_op jit(solution)/shard_map/ppermute | solution.py:444
  92.2 0.7 add_rows.13.refs_4_.refs_2_
  92.9 6.9 %query_products.11 = (f32[1,160,2048]{2,1,0:T(8,128)S(1)}, bf16[1,160,1024]{2,1,0:T(8,128)(2,1)}, bf16[1,160,1024]{2,1,0:T(8,128)(2,1)}) custom-call(s32[2]{0:T(128)S(1)} %pad_add_fusion.6.place_ref, bf16[320,2048]{1,0:T(8,128)(2,1)S(1)} %collective-permute-done.refs_1_.refs_0_, bf16[2048,8192]{1,0:T(8,128)(2,1)} %refs_1_.11, ...), custom_call_target="tpu_custom_call" | custom-call | flops 99999997952 | bytes 100000000 | tf_op jit(solution)/shard_map/query_products/pallas_call | solution.py:87
  99.8 0.5 collective-permute-start.21
  100.3 0.6 fusion.4
  101.3 2.0 %sum_and_rotate.3.refs_0_ = bf16[160,2048]{1,0:T(8,128)(2,1)S(1)} custom-call(f32[160,128]{1,0:T(8,128)S(1)} %get-tuple-element.59.cos_ref, f32[160,128]{1,0:T(8,128)S(1)} %get-tuple-element.57.sin_ref, f32[2,160,2048]{2,1,0:T(8,128)} %get-tuple-element.38.refs_0_, bf16[2,160,2048]{2,1,0:T(8,128)(2,1)} %collective-permute-done.7.refs_2_.refs_1_, ...), custom_call_target="tpu_custom_call" | custom-call | flops 1000 | bytes 1000 | tf_op jit(solution)/shard_map/sum_and_rotate/pallas_call | solution.py:250
  103.4 8.5 %collective-permute-done.10.refs_2_.refs_1_ = bf16[1,160,2048]{2,1,0:T(8,128)(2,1)S(1)} collective-permute-done((bf16[1,160,2048]{2,1,0:T(8,128)(2,1)S(1)}, bf16[1,160,2048]{2,1,0:T(8,128)(2,1)S(1)}, u32[]{:S(2)}, u32[]{:S(2)}) %collective-permute-start.10) | collective-permute-done | bytes 655392 | tf_op jit(solution)/shard_map/ppermute | solution.py:444
  112.0 8.1 %collective-permute-done.15.refs_3_.refs_2_ = bf16[1,160,2048]{2,1,0:T(8,128)(2,1)S(1)} collective-permute-done((bf16[1,160,2048]{2,1,0:T(8,128)(2,1)}, bf16[1,160,2048]{2,1,0:T(8,128)(2,1)S(1)}, u32[]{:S(2)}, u32[]{:S(2)}) %collective-permute-start.15) | collective-permute-done | bytes 655392 | tf_op jit(solution)/shard_map/ppermute | solution.py:444
  120.1 1.2 sum_and_rotate.4.refs_1_
  121.6 1.8 %split_and_rotate.1 = (bf16[320,128]{1,0:T(8,128)(2,1)}, bf16[1,320,128]{2,1,0:T(8,128)(2,1)S(1)}) custom-call(f32[320,128]{1,0:T(8,128)S(1)} %pad_maximum_fusion.cos_ref, f32[320,128]{1,0:T(8,128)S(1)} %pad_maximum_fusion.1.sin_ref, f32[4,160,512]{2,1,0:T(8,128)} %get-tuple-element.33.refs_3_.refs_0_, ...), custom_call_target="tpu_custom_call" | custom-call | flops 1000 | bytes 1000 | tf_op jit(solution)/shard_map/split_and_rotate/pallas_call | solution.py:294
  123.3 0.5 collective-permute-start.16
  124.1 2.7 %collective-permute-start.27 = (bf16[1,320,128]{2,1,0:T(8,128)(2,1)S(1)}, bf16[1,320,128]{2,1,0:T(8,128)(2,1)S(1)}, u32[]{:S(2)}, u32[]{:S(2)}) collective-permute-start(bf16[1,320,128]{2,1,0:T(8,128)(2,1)S(1)} %get-tuple-element.54.refs_0_), channel_id=1, source_target_pairs={{0,12},{4,8},{8,4},{12,0},{1,13},{5,9},{9,5},{13,1},{2,14},{6,10},... | collective-permute-start | bytes 245768 | tf_op jit(solution)/shard_map/ppermute | solution.py:444
  126.8 1.7 %collective-permute-start.25 = (bf16[1,320,128]{2,1,0:T(8,128)(2,1)S(1)}, bf16[1,320,128]{2,1,0:T(8,128)(2,1)S(1)}, u32[]{:S(2)}, u32[]{:S(2)}) collective-permute-start(bf16[1,320,128]{2,1,0:T(8,128)(2,1)S(1)} %get-tuple-element.54.refs_0_), channel_id=1, source_target_pairs={{0,4},{4,0},{8,12},{12,8},{1,5},{5,1},{9,13},{13,9},{2,6},{6,2},{1... | collective-permute-start | bytes 245768 | tf_op jit(solution)/shard_map/ppermute | solution.py:444
  128.6 1.4 order_and_keys.1
  130.4 2.9 %collective-permute-start.19 = (bf16[1,160,512]{2,1,0:T(8,128)(2,1)S(1)}, bf16[1,160,512]{2,1,0:T(8,128)(2,1)S(1)}, u32[]{:S(2)}, u32[]{:S(2)}) collective-permute-start(bf16[1,160,512]{2,1,0:T(8,128)(2,1)S(1)} %copy-done.4), channel_id=1, source_target_pairs={{0,8},{4,12},{8,0},{12,4},{1,9},{5,13},{9,1},{13,5},{2,10},{6,14},... | collective-permute-start | bytes 491528 | tf_op jit(solution)/shard_map/ppermute | solution.py:444
  133.4 7.6 %score_heads.2 = (bf16[1,16,640,640]{3,2,1,0:T(8,128)(2,1)}, f32[8,128]{1,0:T(8,128)S(1)}) custom-call(bf16[640,640]{1,0:T(8,128)(2,1)S(1)} %get-tuple-element.46.order_ref, bf16[128,640]{1,0:T(8,128)(2,1)S(1)} %get-tuple-element.47.key_t_ref, bf16[160,2048]{1,0:T(8,128)(2,1)S(1)} %sum_and_rotate.3.refs_0_, bf16[160,1536]{1,0:T(8,128)(2,1)} %sum_and_rotate.4.refs_1_, ...), custom_call_target="tpu_custom_call" | custom-call | flops 1000 | bytes 1000 | tf_op jit(solution)/shard_map/score_heads/pallas_call | solution.py:405
  141.2 0.5 collective-permute-start.24
  141.9 0.8 collective-permute-done.28.refs_2_.refs_3_
  142.7 2.2 %order_values.1.refs_5_ = bf16[640,512]{1,0:T(8,128)(2,1)} custom-call(s32[4]{0:T(128)S(1)} %pad_add_fusion.7.place_ref, bf16[640,640]{1,0:T(8,128)(2,1)S(1)} %get-tuple-element.46.order_ref, bf16[4,320,128]{2,1,0:T(8,128)(2,1)S(1)} %stack_slots.1.refs_0_.refs_1_, bf16[4,320,128]{2,1,0:T(8,128)(2,1)S(1)} %stack_slots.1.refs_0_.refs_1_, ...), custom_call_target="tpu_custom_call" | custom-call | tf_op jit(solution)/shard_map/order_values/pallas_call | solution.py:371
  144.8 4.2 %score_heads.3 = (bf16[1,16,640,640]{3,2,1,0:T(8,128)(2,1)}, f32[8,128]{1,0:T(8,128)}) custom-call(bf16[640,640]{1,0:T(8,128)(2,1)S(1)} %get-tuple-element.46.order_ref, bf16[128,640]{1,0:T(8,128)(2,1)S(1)} %get-tuple-element.47.key_t_ref, bf16[160,2048]{1,0:T(8,128)(2,1)S(1)} %sum_and_rotate.3.refs_0_, ...), custom_call_target="tpu_custom_call", output_to_operand_aliasing={{0}: (6, {})} | custom-call | flops 1000 | bytes 1000 | tf_op jit(solution)/shard_map/score_heads/pallas_call | solution.py:405
  (74 shorter events, 3.6 us)
Async XLA Ops:
  0.6 32.5 %collective-permute-start = (bf16[320,2048]{1,0:T(8,128)(2,1)}, bf16[320,2048]{1,0:T(8,128)(2,1)S(1)}, u32[]{:S(2)}, u32[]{:S(2)}) collective-permute-start(bf16[320,2048]{1,0:T(8,128)(2,1)} %refs_0_.5), channel_id=1, source_target_pairs={{0,2},{2,0},{1,3},{3,1},{4,6},{6,4},{5,7},{7,5},{8,10},{10,8},{9,1... | collective-permute-start | bytes 3932168 | tf_op jit(solution)/shard_map/ppermute | solution.py:474
  15.2 2.3 %collective-permute-start.1 = (bf16[2,160,1024]{2,1,0:T(8,128)(2,1)}, bf16[2,160,1024]{2,1,0:T(8,128)(2,1)S(1)}, u32[]{:S(2)}, u32[]{:S(2)}) collective-permute-start(bf16[2,160,1024]{2,1,0:T(8,128)(2,1)} %get-tuple-element.30), channel_id=1, source_target_pairs={{0,1},{1,0},{2,3},{3,2},{4,5},{5,4},{6,7},{7,6},{8,9},{9,8},{10,11... | collective-permute-start | bytes 1966088 | tf_op jit(solution)/shard_map/ppermute | solution.py:447
  15.2 3.2 %collective-permute-start.2 = (bf16[2,160,1024]{2,1,0:T(8,128)(2,1)}, bf16[2,160,1024]{2,1,0:T(8,128)(2,1)S(1)}, u32[]{:S(2)}, u32[]{:S(2)}) collective-permute-start(bf16[2,160,1024]{2,1,0:T(8,128)(2,1)} %get-tuple-element.31), channel_id=1, source_target_pairs={{0,1},{1,0},{2,3},{3,2},{4,5},{5,4},{6,7},{7,6},{8,9},{9,8},{10,11... | collective-permute-start | bytes 1966088 | tf_op jit(solution)/shard_map/ppermute | solution.py:447
  19.6 34.1 %collective-permute-start.7 = (bf16[2,160,2048]{2,1,0:T(8,128)(2,1)}, bf16[2,160,2048]{2,1,0:T(8,128)(2,1)}, u32[]{:S(2)}, u32[]{:S(2)}) collective-permute-start(bf16[2,160,2048]{2,1,0:T(8,128)(2,1)} %add_rows.7.refs_2_), channel_id=1, source_target_pairs={{0,4},{4,0},{8,12},{12,8},{1,5},{5,1},{9,13},{13,9},{2,6},{6,2},{1... | collective-permute-start | bytes 3932168 | tf_op jit(solution)/shard_map/ppermute | solution.py:444
  40.2 9.9 %collective-permute-start.3 = (bf16[4,160,512]{2,1,0:T(8,128)(2,1)}, bf16[4,160,512]{2,1,0:T(8,128)(2,1)S(1)}, u32[]{:S(2)}, u32[]{:S(2)}) collective-permute-start(bf16[4,160,512]{2,1,0:T(8,128)(2,1)} %get-tuple-element.34.refs_2_), channel_id=1, source_target_pairs={{0,1},{1,0},{2,3},{3,2},{4,5},{5,4},{6,7},{7,6},{8,9},{9,8},{10,11... | collective-permute-start | bytes 1966088 | tf_op jit(solution)/shard_map/ppermute | solution.py:447
  40.2 13.5 %collective-permute-start.6 = (bf16[1,160,2048]{2,1,0:T(8,128)(2,1)}, bf16[1,160,2048]{2,1,0:T(8,128)(2,1)}, u32[]{:S(2)}, u32[]{:S(2)}) collective-permute-start(bf16[1,160,2048]{2,1,0:T(8,128)(2,1)} %get-tuple-element.32.refs_4_), channel_id=1, source_target_pairs={{0,1},{1,0},{2,3},{3,2},{4,5},{5,4},{6,7},{7,6},{8,9},{9,8},{10,11... | collective-permute-start | bytes 1966088 | tf_op jit(solution)/shard_map/ppermute | solution.py:447
  47.7 2.0 %collective-permute-start.4 = (bf16[1,160,1024]{2,1,0:T(8,128)(2,1)}, bf16[1,160,1024]{2,1,0:T(8,128)(2,1)}, u32[]{:S(2)}, u32[]{:S(2)}) collective-permute-start(bf16[1,160,1024]{2,1,0:T(8,128)(2,1)} %get-tuple-element.36), channel_id=1, source_target_pairs={{0,1},{1,0},{2,3},{3,2},{4,5},{5,4},{6,7},{7,6},{8,9},{9,8},{10,11... | collective-permute-start | bytes 983048 | tf_op jit(solution)/shard_map/ppermute | solution.py:447
  47.7 2.4 %collective-permute-start.5 = (bf16[1,160,1024]{2,1,0:T(8,128)(2,1)}, bf16[1,160,1024]{2,1,0:T(8,128)(2,1)}, u32[]{:S(2)}, u32[]{:S(2)}) collective-permute-start(bf16[1,160,1024]{2,1,0:T(8,128)(2,1)} %get-tuple-element.37), channel_id=1, source_target_pairs={{0,1},{1,0},{2,3},{3,2},{4,5},{5,4},{6,7},{7,6},{8,9},{9,8},{10,11... | collective-permute-start | bytes 983048 | tf_op jit(solution)/shard_map/ppermute | solution.py:447
  52.4 35.3 %collective-permute-start.13 = (bf16[1,160,2560]{2,1,0:T(8,128)(2,1)}, bf16[1,160,2560]{2,1,0:T(8,128)(2,1)S(1)}, u32[]{:S(2)}, u32[]{:S(2)}) collective-permute-start(bf16[1,160,2560]{2,1,0:T(8,128)(2,1)} %add_rows.8.refs_3_.refs_2_), channel_id=1, source_target_pairs={{0,4},{4,0},{8,12},{12,8},{1,5},{5,1},{9,13},{13,9},{2,6},{6,2},{1... | collective-permute-start | bytes 2457608 | tf_op jit(solution)/shard_map/ppermute | solution.py:444
  56.4 30.3 %collective-permute-start.14 = (bf16[1,160,2048]{2,1,0:T(8,128)(2,1)}, bf16[1,160,2048]{2,1,0:T(8,128)(2,1)S(1)}, u32[]{:S(2)}, u32[]{:S(2)}) collective-permute-start(bf16[1,160,2048]{2,1,0:T(8,128)(2,1)} %add_rows.9.refs_3_), channel_id=1, source_target_pairs={{0,8},{4,12},{8,0},{12,4},{1,9},{5,13},{9,1},{13,5},{2,10},{6,14},... | collective-permute-start | bytes 1966088 | tf_op jit(solution)/shard_map/ppermute | solution.py:444
  65.9 7.1 %copy-start = (f32[1,160,2048]{2,1,0:T(8,128)}, f32[1,160,2048]{2,1,0:T(8,128)S(1)}, u32[]{:S(2)}) copy-start(f32[1,160,2048]{2,1,0:T(8,128)S(1)} %get-tuple-element.43.refs_0_) | copy-start | bytes 3932164
  65.9 9.2 %copy-start.6 = (s32[640]{0:T(1024)S(1)}, s32[640]{0:T(1024)}, u32[]{:S(2)}) copy-start(s32[640]{0:T(1024)} %param.10) | copy-start | bytes 7684
  65.9 9.2 %copy-start.7 = (s32[640]{0:T(1024)S(1)}, s32[640]{0:T(1024)}, u32[]{:S(2)}) copy-start(s32[640]{0:T(1024)} %param.11) | copy-start | bytes 7684
  73.1 2.0 %collective-permute-start.9 = (bf16[1,160,1024]{2,1,0:T(8,128)(2,1)}, bf16[1,160,1024]{2,1,0:T(8,128)(2,1)}, u32[]{:S(2)}, u32[]{:S(2)}) collective-permute-start(bf16[1,160,1024]{2,1,0:T(8,128)(2,1)} %get-tuple-element.42), channel_id=1, source_target_pairs={{0,1},{1,0},{2,3},{3,2},{4,5},{5,4},{6,7},{7,6},{8,9},{9,8},{10,11... | collective-permute-start | bytes 983048 | tf_op jit(solution)/shard_map/ppermute | solution.py:447
  73.3 8.7 %collective-permute-start.11 = (bf16[1,160,1024]{2,1,0:T(8,128)(2,1)}, bf16[1,160,1024]{2,1,0:T(8,128)(2,1)S(1)}, u32[]{:S(2)}, u32[]{:S(2)}) collective-permute-start(bf16[1,160,1024]{2,1,0:T(8,128)(2,1)} %get-tuple-element.39.refs_2_), channel_id=1, source_target_pairs={{0,1},{1,0},{2,3},{3,2},{4,5},{5,4},{6,7},{7,6},{8,9},{9,8},{10,11... | collective-permute-start | bytes 983048 | tf_op jit(solution)/shard_map/ppermute | solution.py:447
  73.8 7.5 %collective-permute-start.12 = (bf16[1,160,1024]{2,1,0:T(8,128)(2,1)}, bf16[1,160,1024]{2,1,0:T(8,128)(2,1)S(1)}, u32[]{:S(2)}, u32[]{:S(2)}) collective-permute-start(bf16[1,160,1024]{2,1,0:T(8,128)(2,1)} %get-tuple-element.44), channel_id=1, source_target_pairs={{0,1},{1,0},{2,3},{3,2},{4,5},{5,4},{6,7},{7,6},{8,9},{9,8},{10,11... | collective-permute-start | bytes 983048 | tf_op jit(solution)/shard_map/ppermute | solution.py:447
  75.1 1.8 %collective-permute-start.8 = (bf16[1,160,1024]{2,1,0:T(8,128)(2,1)}, bf16[1,160,1024]{2,1,0:T(8,128)(2,1)S(1)}, u32[]{:S(2)}, u32[]{:S(2)}) collective-permute-start(bf16[1,160,1024]{2,1,0:T(8,128)(2,1)} %get-tuple-element.41.refs_5_), channel_id=1, source_target_pairs={{0,1},{1,0},{2,3},{3,2},{4,5},{5,4},{6,7},{7,6},{8,9},{9,8},{10,11... | collective-permute-start | bytes 983048 | tf_op jit(solution)/shard_map/ppermute | solution.py:447
  76.9 2.4 %copy-start.8 = (bf16[1,160,2048]{2,1,0:T(8,128)(2,1)S(1)}, bf16[1,160,2048]{2,1,0:T(8,128)(2,1)}, u32[]{:S(2)}) copy-start(bf16[1,160,2048]{2,1,0:T(8,128)(2,1)} %get-tuple-element.48) | copy-start | bytes 1966084
  79.3 2.0 %copy-start.5 = (bf16[1,160,2048]{2,1,0:T(8,128)(2,1)S(1)}, bf16[1,160,2048]{2,1,0:T(8,128)(2,1)}, u32[]{:S(2)}) copy-start(bf16[1,160,2048]{2,1,0:T(8,128)(2,1)} %add_rows.10.refs_2_) | copy-start | bytes 1966084
  79.3 8.4 %copy-start.1 = (f32[1,160,2048]{2,1,0:T(8,128)S(1)}, f32[1,160,2048]{2,1,0:T(8,128)}, u32[]{:S(2)}) copy-start(f32[1,160,2048]{2,1,0:T(8,128)} %copy-done) | copy-start | bytes 3932164
  79.3 22.0 %collective-permute-start.17 = (bf16[1,160,2048]{2,1,0:T(8,128)(2,1)S(1)}, bf16[1,160,2048]{2,1,0:T(8,128)(2,1)S(1)}, u32[]{:S(2)}, u32[]{:S(2)}) collective-permute-start(bf16[1,160,2048]{2,1,0:T(8,128)(2,1)S(1)} %copy-done.8), channel_id=1, source_target_pairs={{0,1},{1,0},{2,3},{3,2},{4,5},{5,4},{6,7},{7,6},{8,9},{9,8},{10,11... | collective-permute-start | bytes 1966088 | tf_op jit(solution)/shard_map/ppermute | solution.py:447
  81.3 30.7 %collective-permute-start.10 = (bf16[1,160,2048]{2,1,0:T(8,128)(2,1)S(1)}, bf16[1,160,2048]{2,1,0:T(8,128)(2,1)S(1)}, u32[]{:S(2)}, u32[]{:S(2)}) collective-permute-start(bf16[1,160,2048]{2,1,0:T(8,128)(2,1)S(1)} %copy-done.5), channel_id=1, source_target_pairs={{0,4},{4,0},{8,12},{12,8},{1,5},{5,1},{9,13},{13,9},{2,6},{6,2},{1... | collective-permute-start | bytes 1966088 | tf_op jit(solution)/shard_map/ppermute | solution.py:444
  86.7 3.1 %copy-start.2 = (bf16[1,160,2048]{2,1,0:T(8,128)(2,1)}, bf16[1,160,2048]{2,1,0:T(8,128)(2,1)S(1)}, u32[]{:S(2)}) copy-start(bf16[1,160,2048]{2,1,0:T(8,128)(2,1)S(1)} %collective-permute-done.14.refs_8_.refs_2_) | copy-start | bytes 1966084
  89.8 30.3 %collective-permute-start.15 = (bf16[1,160,2048]{2,1,0:T(8,128)(2,1)}, bf16[1,160,2048]{2,1,0:T(8,128)(2,1)S(1)}, u32[]{:S(2)}, u32[]{:S(2)}) collective-permute-start(bf16[1,160,2048]{2,1,0:T(8,128)(2,1)} %add_rows.12.refs_3_), channel_id=1, source_target_pairs={{0,8},{4,12},{8,0},{12,4},{1,9},{5,13},{9,1},{13,5},{2,10},{6,14},... | collective-permute-start | bytes 1966088 | tf_op jit(solution)/shard_map/ppermute | solution.py:444
  99.8 1.4 copy-start.3
  99.8 1.4 copy-start.4
  99.8 12.2 %collective-permute-start.20 = (bf16[1,160,1024]{2,1,0:T(8,128)(2,1)}, bf16[1,160,1024]{2,1,0:T(8,128)(2,1)S(1)}, u32[]{:S(2)}, u32[]{:S(2)}) collective-permute-start(bf16[1,160,1024]{2,1,0:T(8,128)(2,1)} %get-tuple-element.50), channel_id=1, source_target_pairs={{0,1},{1,0},{2,3},{3,2},{4,5},{5,4},{6,7},{7,6},{8,9},{9,8},{10,11... | collective-permute-start | bytes 983048 | tf_op jit(solution)/shard_map/ppermute | solution.py:447
  99.8 12.1 %collective-permute-start.21 = (bf16[1,160,1024]{2,1,0:T(8,128)(2,1)}, bf16[1,160,1024]{2,1,0:T(8,128)(2,1)S(1)}, u32[]{:S(2)}, u32[]{:S(2)}) collective-permute-start(bf16[1,160,1024]{2,1,0:T(8,128)(2,1)} %get-tuple-element.51), channel_id=1, source_target_pairs={{0,1},{1,0},{2,3},{3,2},{4,5},{5,4},{6,7},{7,6},{8,9},{9,8},{10,11... | collective-permute-start | bytes 983048 | tf_op jit(solution)/shard_map/ppermute | solution.py:447
  103.3 26.8 %collective-permute-start.22 = (bf16[160,2048]{1,0:T(8,128)(2,1)S(1)}, bf16[160,2048]{1,0:T(8,128)(2,1)}, u32[]{:S(2)}, u32[]{:S(2)}) collective-permute-start(bf16[160,2048]{1,0:T(8,128)(2,1)S(1)} %sum_and_rotate.3.refs_0_), channel_id=1, source_target_pairs={{0,1},{1,0},{2,3},{3,2},{4,5},{5,4},{6,7},{7,6},{8,9},{9,8},{10,11... | collective-permute-start | bytes 1966088 | tf_op jit(solution)/shard_map/ppermute | solution.py:447
  121.3 9.1 %collective-permute-start.23 = (bf16[160,1536]{1,0:T(8,128)(2,1)}, bf16[160,1536]{1,0:T(8,128)(2,1)}, u32[]{:S(2)}, u32[]{:S(2)}) collective-permute-start(bf16[160,1536]{1,0:T(8,128)(2,1)} %sum_and_rotate.4.refs_1_), channel_id=1, source_target_pairs={{0,1},{1,0},{2,3},{3,2},{4,5},{5,4},{6,7},{7,6},{8,9},{9,8},{10,11... | collective-permute-start | bytes 1474568 | tf_op jit(solution)/shard_map/ppermute | solution.py:447
  123.3 3.5 %collective-permute-start.16 = (bf16[320,128]{1,0:T(8,128)(2,1)}, bf16[320,128]{1,0:T(8,128)(2,1)S(1)}, u32[]{:S(2)}, u32[]{:S(2)}) collective-permute-start(bf16[320,128]{1,0:T(8,128)(2,1)} %get-tuple-element.45.own_ref), channel_id=1, source_target_pairs={{0,1},{1,0},{2,3},{3,2},{4,5},{5,4},{6,7},{7,6},{8,9},{9,8},{10,11... | collective-permute-start | bytes 245768 | tf_op jit(solution)/shard_map/ppermute | solution.py:447
  124.1 16.8 %collective-permute-start.27 = (bf16[1,320,128]{2,1,0:T(8,128)(2,1)S(1)}, bf16[1,320,128]{2,1,0:T(8,128)(2,1)S(1)}, u32[]{:S(2)}, u32[]{:S(2)}) collective-permute-start(bf16[1,320,128]{2,1,0:T(8,128)(2,1)S(1)} %get-tuple-element.54.refs_0_), channel_id=1, source_target_pairs={{0,12},{4,8},{8,4},{12,0},{1,13},{5,9},{9,5},{13,1},{2,14},{6,10},... | collective-permute-start | bytes 245768 | tf_op jit(solution)/shard_map/ppermute | solution.py:444
  126.8 14.1 %collective-permute-start.26 = (bf16[1,320,128]{2,1,0:T(8,128)(2,1)S(1)}, bf16[1,320,128]{2,1,0:T(8,128)(2,1)S(1)}, u32[]{:S(2)}, u32[]{:S(2)}) collective-permute-start(bf16[1,320,128]{2,1,0:T(8,128)(2,1)S(1)} %get-tuple-element.54.refs_0_), channel_id=1, source_target_pairs={{0,8},{4,12},{8,0},{12,4},{1,9},{5,13},{9,1},{13,5},{2,10},{6,14},... | collective-permute-start | bytes 245768 | tf_op jit(solution)/shard_map/ppermute | solution.py:444
  126.8 14.1 %collective-permute-start.25 = (bf16[1,320,128]{2,1,0:T(8,128)(2,1)S(1)}, bf16[1,320,128]{2,1,0:T(8,128)(2,1)S(1)}, u32[]{:S(2)}, u32[]{:S(2)}) collective-permute-start(bf16[1,320,128]{2,1,0:T(8,128)(2,1)S(1)} %get-tuple-element.54.refs_0_), channel_id=1, source_target_pairs={{0,4},{4,0},{8,12},{12,8},{1,5},{5,1},{9,13},{13,9},{2,6},{6,2},{1... | collective-permute-start | bytes 245768 | tf_op jit(solution)/shard_map/ppermute | solution.py:444
  130.1 11.0 %collective-permute-start.18 = (bf16[1,160,512]{2,1,0:T(8,128)(2,1)}, bf16[1,160,512]{2,1,0:T(8,128)(2,1)S(1)}, u32[]{:S(2)}, u32[]{:S(2)}) collective-permute-start(bf16[1,160,512]{2,1,0:T(8,128)(2,1)} %add_rows.11.refs_7_), channel_id=1, source_target_pairs={{0,4},{4,0},{8,12},{12,8},{1,5},{5,1},{9,13},{13,9},{2,6},{6,2},{1... | collective-permute-start | bytes 491528 | tf_op jit(solution)/shard_map/ppermute | solution.py:444
  130.4 10.6 %collective-permute-start.19 = (bf16[1,160,512]{2,1,0:T(8,128)(2,1)S(1)}, bf16[1,160,512]{2,1,0:T(8,128)(2,1)S(1)}, u32[]{:S(2)}, u32[]{:S(2)}) collective-permute-start(bf16[1,160,512]{2,1,0:T(8,128)(2,1)S(1)} %copy-done.4), channel_id=1, source_target_pairs={{0,8},{4,12},{8,0},{12,4},{1,9},{5,13},{9,1},{13,5},{2,10},{6,14},... | collective-permute-start | bytes 491528 | tf_op jit(solution)/shard_map/ppermute | solution.py:444
  141.0 1.7 %collective-permute-start.28 = (bf16[4,320,128]{2,1,0:T(8,128)(2,1)S(1)}, bf16[4,320,128]{2,1,0:T(8,128)(2,1)S(1)}, u32[]{:S(2)}, u32[]{:S(2)}) collective-permute-start(bf16[4,320,128]{2,1,0:T(8,128)(2,1)S(1)} %stack_slots.1.refs_0_.refs_1_), channel_id=1, source_target_pairs={{0,1},{1,0},{2,3},{3,2},{4,5},{5,4},{6,7},{7,6},{8,9},{9,8},{10,11... | collective-permute-start | bytes 983048 | tf_op jit(solution)/shard_map/ppermute | solution.py:447
  141.2 3.6 %collective-permute-start.24 = (bf16[160,512]{1,0:T(8,128)(2,1)S(1)}, bf16[160,512]{1,0:T(8,128)(2,1)S(1)}, u32[]{:S(2)}, u32[]{:S(2)}) collective-permute-start(bf16[160,512]{1,0:T(8,128)(2,1)S(1)} %sum_and_rotate.5.refs_1_), channel_id=1, source_target_pairs={{0,1},{1,0},{2,3},{3,2},{4,5},{5,4},{6,7},{7,6},{8,9},{9,8},{10,11... | collective-permute-start | bytes 491528 | tf_op jit(solution)/shard_map/ppermute | solution.py:447

commit v17 on v15

--- a/solution.py
+++ b/solution.py
@@ -100,7 +100,7 @@
         compiler_params=pltpu.CompilerParams(vmem_limit_bytes=VMEM_BYTES),
         cost_estimate=cost,
         name="query_products",
-    )(place, *blocks, *in_hbm([w]), *in_hbm(after[:1]), *after[1:])
+    )(place, *blocks, *in_hbm([w, *after]))
     return outs[0], outs[1:]
 
 
@@ -141,7 +141,7 @@
             scratch_shapes=[pltpu.VMEM((count * rows, depth), blocks[0].dtype)],
         ),
         out_shape=[
-            pltpu.HBM(shape, jnp.float32),
+            jax.ShapeDtypeStruct(shape, jnp.float32),
             pltpu.HBM(shape, jnp.bfloat16),
         ],
         compiler_params=pltpu.CompilerParams(vmem_limit_bytes=VMEM_BYTES),
@@ -213,8 +213,7 @@
     )(
         *([keep] if near else in_hbm([keep])),
         *[got for got, _, _ in gots],
-        *in_hbm(pair[:1]),
-        *pair[1:],
+        *pair,
         *(list(landed) * (2 if pair else 1)),
         *in_hbm(after[:1]),
         *after[1:],
@@ -305,7 +304,7 @@
         compiler_params=pltpu.CompilerParams(vmem_limit_bytes=VMEM_BYTES),
         cost_estimate=LIGHT,
         name="split_and_rotate",
-    )(cosine, sine, *in_hbm([terms[0][0]]), *[term for term, _, _ in terms[1:]], *after)
+    )(cosine, sine, *[term for term, _, _ in terms], *after)
 
 
 def prepare_kernel(canary_ref, ids_ref, own_ref, other_ref, order_ref, key_t_ref):

time: 148 us -> 151 us (1.020)
  transfers between devices with their start and end apart: 29 -> 29, of which waited for: 11 -> 11; matrix products, arithmetic and copies ran while one was open for 2% -> 2% of each run, Pallas kernels for 60% -> 59%
where the time goes in v17:
time: 151 us
  Pallas kernels  92.8 us (61%)
  waiting for transfers between devices  29.3 us (19%)
  starting transfers between devices  22.9 us (15%)
  local copies, waits for them, and re-layouts  2.8 us (2%)
  other arithmetic  2.04 us (1%)
    pallas_call x6, Pallas kernels, project_query(): pl.pallas_call(functools.partial(query_kernel, count, pieces, by_slot), g...  51.3 us
    ppermute x10, waiting for transfers between devices, swap(): return lax.ppermute(x, 'fsdp', [(i, i ^ bit) for i in range(shards)])  22.2 us
    ppermute x10, starting transfers between devices, swap(): return lax.ppermute(x, 'fsdp', [(i, i ^ bit) for i in range(shards)])  16.1 us
    pallas_call x7, Pallas kernels, add_rows(): pl.pallas_call(functools.partial(add_kernel, len(gots), len(pair) // 2, l...  14.2 us
    pallas_call x2, Pallas kernels, score_heads(): pl.pallas_call(functools.partial(score_kernel, len(queries)), grid=(count...  11.7 us
    ppermute x18, waiting for transfers between devices, other_core(): return lax.ppermute(x, 'rep', [(0, 1), (1, 0)])  7.19 us
    pallas_call x1, Pallas kernels, project_pair(): pl.pallas_call(functools.partial(pair_kernel, count), grid_spec=pltpu.Pre...  7.03 us
    pallas_call x3, Pallas kernels, sum_and_rotate(): pl.pallas_call(functools.partial(rotate_kernel, len(terms), len(gots)), g...  5.73 us
  transfers between devices with their start and end apart: 29, of which 11 were waited for; matrix products, arithmetic and copies ran while one was open for 2% of the time, Pallas kernels for 59%

profile of v17, /device:TPU:0, one launch (start us, length us, event | category | flops | bytes accessed | tf_op | source)
XLA Modules:
  0.0 150.8 jit_solution(1783926847735199931)
XLA Ops:
  0.6 3.0 %collective-permute-start = (bf16[320,2048]{1,0:T(8,128)(2,1)}, bf16[320,2048]{1,0:T(8,128)(2,1)S(1)}, u32[]{:S(2)}, u32[]{:S(2)}) collective-permute-start(bf16[320,2048]{1,0:T(8,128)(2,1)} %refs_0_.5), channel_id=1, source_target_pairs={{0,2},{2,0},{1,3},{3,1},{4,6},{6,4},{5,7},{7,5},{8,10},{10,8},{9,1... | collective-permute-start | bytes 3932168 | tf_op jit(solution)/shard_map/ppermute | solution.py:473
  3.7 11.5 %query_products.6 = (f32[2,160,2048]{2,1,0:T(8,128)S(1)}, bf16[2,160,1024]{2,1,0:T(8,128)(2,1)}, bf16[2,160,1024]{2,1,0:T(8,128)(2,1)}) custom-call(s32[3]{0:T(128)S(1)} %pad_add_fusion.2.place_ref, bf16[320,2048]{1,0:T(8,128)(2,1)} %refs_0_.5, bf16[2048,8192]{1,0:T(8,128)(2,1)} %refs_1_.11), custom_call_target="tpu_custom_call" | custom-call | flops 1000 | bytes 1000 | tf_op jit(solution)/shard_map/query_products/pallas_call | solution.py:87
  15.2 0.5 collective-permute-start.2
  15.7 1.8 %collective-permute-done.1.refs_1_ = bf16[2,160,1024]{2,1,0:T(8,128)(2,1)S(1)} collective-permute-done((bf16[2,160,1024]{2,1,0:T(8,128)(2,1)}, bf16[2,160,1024]{2,1,0:T(8,128)(2,1)S(1)}, u32[]{:S(2)}, u32[]{:S(2)}) %collective-permute-start.1) | collective-permute-done | bytes 655392 | tf_op jit(solution)/shard_map/ppermute | solution.py:446
  17.5 0.9 collective-permute-done.2.refs_2_
  18.5 1.2 add_rows.7.refs_2_
  19.6 1.6 %collective-permute-start.7 = (bf16[2,160,2048]{2,1,0:T(8,128)(2,1)}, bf16[2,160,2048]{2,1,0:T(8,128)(2,1)}, u32[]{:S(2)}, u32[]{:S(2)}) collective-permute-start(bf16[2,160,2048]{2,1,0:T(8,128)(2,1)} %add_rows.7.refs_2_), channel_id=1, source_target_pairs={{0,4},{4,0},{8,12},{12,8},{1,5},{5,1},{9,13},{13,9},{2,6},{6,2},{1... | collective-permute-start | bytes 3932168 | tf_op jit(solution)/shard_map/ppermute | solution.py:443
  21.4 11.8 %query_products.7 = (f32[2,160,2048]{2,1,0:T(8,128)}, bf16[1,160,2048]{2,1,0:T(8,128)(2,1)}, bf16[1,160,2048]{2,1,0:T(8,128)(2,1)}) custom-call(s32[3]{0:T(128)S(1)} %pad_add_fusion.1.place_ref, bf16[320,2048]{1,0:T(8,128)(2,1)} %refs_0_.5, bf16[2048,8192]{1,0:T(8,128)(2,1)} %refs_1_.11, bf16[2,160,2048]{2,1,0:T(8,128)(2,1)} %add_rows.7.refs_2_), custom_call_target="tpu_custom_call" | custom-call | flops 1000 | bytes 1000 | tf_op jit(solution)/shard_map/query_products/pallas_call | solution.py:87
  33.1 7.0 %key_value_products.1 = (f32[4,160,512]{2,1,0:T(8,128)S(1)}, bf16[4,160,512]{2,1,0:T(8,128)(2,1)}) custom-call(s32[5]{0:T(128)S(1)} %stack.62.place_ref, bf16[320,2048]{1,0:T(8,128)(2,1)} %refs_0_.5, bf16[320,2048]{1,0:T(8,128)(2,1)S(1)} %collective-permute-done.refs_1_.refs_0_, bf16[2048,512]{1,0:T(8,128)(2,1)} %refs_2_.1, bf16[2048,512]{1,0:T(8,128)(2,1)} %refs_3_.1, ...), custom_call_target="tpu_custom_call" | custom-call | flops 1000 | bytes 1000 | tf_op jit(solution)/shard_map/key_value_products/pallas_call | solution.py:132
  40.2 0.5 collective-permute-start.6
  40.7 6.9 %query_products.8 = (f32[1,160,2048]{2,1,0:T(8,128)S(1)}, bf16[1,160,1024]{2,1,0:T(8,128)(2,1)}, bf16[1,160,1024]{2,1,0:T(8,128)(2,1)}) custom-call(s32[2]{0:T(128)S(1)} %get-tuple-element.66.place_ref, bf16[320,2048]{1,0:T(8,128)(2,1)S(1)} %collective-permute-done.refs_1_.refs_0_, bf16[2048,8192]{1,0:T(8,128)(2,1)} %refs_1_.11, ...), custom_call_target="tpu_custom_call" | custom-call | flops 1000 | bytes 1000 | tf_op jit(solution)/shard_map/query_products/pallas_call | solution.py:87
  47.6 1.1 copy-done.1
  48.7 0.5 collective-permute-start.5
  49.3 1.4 collective-permute-done.4.refs_1_
  51.1 1.3 copy-done.2
  52.5 2.2 %add_rows.8.refs_3_.refs_2_ = bf16[1,160,2560]{2,1,0:T(8,128)(2,1)} custom-call(f32[1,160,2048]{2,1,0:T(8,128)S(1)} %copy-done.2, bf16[1,160,1024]{2,1,0:T(8,128)(2,1)} %collective-permute-done.4.refs_1_, bf16[1,160,1024]{2,1,0:T(8,128)(2,1)} %collective-permute-done.5.refs_2_, f32[4,160,512]{2,1,0:T(8,128)S(1)} %get-tuple-element.33.refs_3_.refs_0_, ...), custom_call_target="tpu_custom_call" | custom-call | flops 1000 | bytes 1000 | tf_op jit(solution)/shard_map/add_rows/pallas_call | solution.py:200
  54.6 1.3 collective-permute-start.13
  55.9 2.7 %add_rows.9.refs_3_ = bf16[1,160,2048]{2,1,0:T(8,128)(2,1)} custom-call(f32[2,160,2048]{2,1,0:T(8,128)} %get-tuple-element.38.refs_0_, bf16[1,160,2048]{2,1,0:T(8,128)(2,1)} %collective-permute-done.6.refs_1_, bf16[2,160,2048]{2,1,0:T(8,128)(2,1)} %collective-permute-done.7.refs_2_.refs_1_, bf16[1,160,2560]{2,1,0:T(8,128)(2,1)} %add_rows.8.refs_3_.refs_2_), custom_call_target="tpu_custom_call" | custom-call | flops 1000 | bytes 1000 | tf_op jit(solution)/shard_map/add_rows/pallas_call | solution.py:200
  58.7 2.6 %collective-permute-start.14 = (bf16[1,160,2048]{2,1,0:T(8,128)(2,1)}, bf16[1,160,2048]{2,1,0:T(8,128)(2,1)}, u32[]{:S(2)}, u32[]{:S(2)}) collective-permute-start(bf16[1,160,2048]{2,1,0:T(8,128)(2,1)} %add_rows.9.refs_3_), channel_id=1, source_target_pairs={{0,8},{4,12},{8,0},{12,4},{1,9},{5,13},{9,1},{13,5},{2,10},{6,14},... | collective-permute-start | bytes 1966088 | tf_op jit(solution)/shard_map/ppermute | solution.py:443
  61.2 7.1 %query_products.9 = (f32[1,160,2048]{2,1,0:T(8,128)}, bf16[1,160,1024]{2,1,0:T(8,128)(2,1)}, bf16[1,160,1024]{2,1,0:T(8,128)(2,1)}) custom-call(s32[2]{0:T(128)S(1)} %pad_add_fusion.4.place_ref, bf16[320,2048]{1,0:T(8,128)(2,1)S(1)} %collective-permute-done.refs_1_.refs_0_, bf16[2048,8192]{1,0:T(8,128)(2,1)} %refs_1_.11, ...), custom_call_target="tpu_custom_call" | custom-call | flops 99999997952 | bytes 100000000 | tf_op jit(solution)/shard_map/query_products/pallas_call | solution.py:87
  68.3 7.1 %query_products.10 = (f32[1,160,2048]{2,1,0:T(8,128)}, bf16[1,160,1024]{2,1,0:T(8,128)(2,1)}, bf16[1,160,1024]{2,1,0:T(8,128)(2,1)}) custom-call(s32[2]{0:T(128)S(1)} %get-tuple-element.65.place_ref, bf16[320,2048]{1,0:T(8,128)(2,1)S(1)} %collective-permute-done.refs_1_.refs_0_, bf16[2048,8192]{1,0:T(8,128)(2,1)} %refs_1_.11, ...), custom_call_target="tpu_custom_call" | custom-call | flops 1000 | bytes 1000 | tf_op jit(solution)/shard_map/query_products/pallas_call | solution.py:87
  75.6 0.5 collective-permute-start.11
  76.2 1.2 collective-permute-done.9.refs_2_.refs_1_
  77.9 1.3 collective-permute-done.8.refs_1_
  79.2 2.2 %add_rows.10.refs_2_ = bf16[1,160,2048]{2,1,0:T(8,128)(2,1)} custom-call(f32[1,160,2048]{2,1,0:T(8,128)} %get-tuple-element.40.refs_0_, bf16[1,160,1024]{2,1,0:T(8,128)(2,1)S(1)} %collective-permute-done.8.refs_1_, bf16[1,160,1024]{2,1,0:T(8,128)(2,1)} %collective-permute-done.9.refs_2_.refs_1_, f32[4,160,512]{2,1,0:T(8,128)S(1)} %get-tuple-element.33.refs_3_.refs_0_, ...), custom_call_target="tpu_custom_call" | custom-call | flops 1000 | bytes 1000 | tf_op jit(solution)/shard_map/add_rows/pallas_call | solution.py:200
  81.6 1.8 %add_rows.11.refs_7_ = bf16[1,160,512]{2,1,0:T(8,128)(2,1)} custom-call(f32[1,160,2048]{2,1,0:T(8,128)} %get-tuple-element.40.refs_0_, bf16[1,160,1024]{2,1,0:T(8,128)(2,1)} %collective-permute-done.9.refs_2_.refs_1_, bf16[1,160,2048]{2,1,0:T(8,128)(2,1)} %add_rows.10.refs_2_), custom_call_target="tpu_custom_call" | custom-call | flops 1000 | bytes 1000 | tf_op jit(solution)/shard_map/add_rows/pallas_call | solution.py:200
  83.4 0.7 collective-permute-start.10
  84.1 4.9 %collective-permute-done.14.refs_8_.refs_2_ = bf16[1,160,2048]{2,1,0:T(8,128)(2,1)} collective-permute-done((bf16[1,160,2048]{2,1,0:T(8,128)(2,1)}, bf16[1,160,2048]{2,1,0:T(8,128)(2,1)}, u32[]{:S(2)}, u32[]{:S(2)}) %collective-permute-start.14) | collective-permute-done | bytes 655392 | tf_op jit(solution)/shard_map/ppermute | solution.py:443
  88.9 1.1 collective-permute-done.13.refs_5_.refs_6_.refs_2_
  90.1 2.4 %add_rows.12.refs_3_ = bf16[1,160,2048]{2,1,0:T(8,128)(2,1)} custom-call(f32[1,160,2048]{2,1,0:T(8,128)} %get-tuple-element.43.refs_0_, bf16[1,160,1024]{2,1,0:T(8,128)(2,1)S(1)} %collective-permute-done.11.refs_1_, bf16[1,160,1024]{2,1,0:T(8,128)(2,1)S(1)} %collective-permute-done.12.refs_2_.refs_1_, f32[4,160,512]{2,1,0:T(8,128)S(1)} %get-tuple-element.33.refs_3_.refs_0_, ...), custom_call_target="tpu_custom_call" | custom-call | flops 1000 | bytes 1000 | tf_op jit(solution)/shard_map/add_rows/pallas_call | solution.py:200
  92.5 2.3 %collective-permute-start.15 = (bf16[1,160,2048]{2,1,0:T(8,128)(2,1)}, bf16[1,160,2048]{2,1,0:T(8,128)(2,1)S(1)}, u32[]{:S(2)}, u32[]{:S(2)}) collective-permute-start(bf16[1,160,2048]{2,1,0:T(8,128)(2,1)} %add_rows.12.refs_3_), channel_id=1, source_target_pairs={{0,8},{4,12},{8,0},{12,4},{1,9},{5,13},{9,1},{13,5},{2,10},{6,14},... | collective-permute-start | bytes 1966088 | tf_op jit(solution)/shard_map/ppermute | solution.py:443
  94.7 1.7 %add_rows.13.refs_4_.refs_2_ = bf16[1,160,512]{2,1,0:T(8,128)(2,1)} custom-call(f32[1,160,2048]{2,1,0:T(8,128)} %get-tuple-element.43.refs_0_, bf16[1,160,1024]{2,1,0:T(8,128)(2,1)S(1)} %collective-permute-done.12.refs_2_.refs_1_, bf16[1,160,2560]{2,1,0:T(8,128)(2,1)} %collective-permute-done.13.refs_5_.refs_6_.refs_2_, bf16[1,160,2048]{2,1,0:T(8,128)(2,1)} %add_rows.12.refs_3_), custom_call_target="tpu_custom_call" | custom-call | flops 1000 | bytes 1000 | tf_op jit(solution)/shard_map/add_rows/pallas_call | solution.py:200
  96.5 7.0 %query_products.11 = (f32[1,160,2048]{2,1,0:T(8,128)}, bf16[1,160,1024]{2,1,0:T(8,128)(2,1)}, bf16[1,160,1024]{2,1,0:T(8,128)(2,1)}) custom-call(s32[2]{0:T(128)S(1)} %pad_add_fusion.6.place_ref, bf16[320,2048]{1,0:T(8,128)(2,1)S(1)} %collective-permute-done.refs_1_.refs_0_, bf16[2048,8192]{1,0:T(8,128)(2,1)} %refs_1_.11, ...), custom_call_target="tpu_custom_call" | custom-call | flops 99999997952 | bytes 100000000 | tf_op jit(solution)/shard_map/query_products/pallas_call | solution.py:87
  104.0 0.6 fusion.4
  104.9 2.2 %sum_and_rotate.3.refs_0_ = bf16[160,2048]{1,0:T(8,128)(2,1)S(1)} custom-call(f32[160,128]{1,0:T(8,128)S(1)} %get-tuple-element.59.cos_ref, f32[160,128]{1,0:T(8,128)S(1)} %get-tuple-element.57.sin_ref, f32[2,160,2048]{2,1,0:T(8,128)} %get-tuple-element.38.refs_0_, bf16[2,160,2048]{2,1,0:T(8,128)(2,1)} %collective-permute-done.7.refs_2_.refs_1_, ...), custom_call_target="tpu_custom_call" | custom-call | flops 1000 | bytes 1000 | tf_op jit(solution)/shard_map/sum_and_rotate/pallas_call | solution.py:249
  107.3 6.5 %collective-permute-done.10.refs_2_.refs_1_ = bf16[1,160,2048]{2,1,0:T(8,128)(2,1)S(1)} collective-permute-done((bf16[1,160,2048]{2,1,0:T(8,128)(2,1)S(1)}, bf16[1,160,2048]{2,1,0:T(8,128)(2,1)S(1)}, u32[]{:S(2)}, u32[]{:S(2)}) %collective-permute-start.10) | collective-permute-done | bytes 655392 | tf_op jit(solution)/shard_map/ppermute | solution.py:443
  113.8 9.0 %collective-permute-done.15.refs_3_.refs_2_ = bf16[1,160,2048]{2,1,0:T(8,128)(2,1)S(1)} collective-permute-done((bf16[1,160,2048]{2,1,0:T(8,128)(2,1)}, bf16[1,160,2048]{2,1,0:T(8,128)(2,1)S(1)}, u32[]{:S(2)}, u32[]{:S(2)}) %collective-permute-start.15) | collective-permute-done | bytes 655392 | tf_op jit(solution)/shard_map/ppermute | solution.py:443
  122.8 2.4 %sum_and_rotate.4.refs_1_ = bf16[160,1536]{1,0:T(8,128)(2,1)} custom-call(f32[160,128]{1,0:T(8,128)S(1)} %get-tuple-element.58.cos_ref, f32[160,128]{1,0:T(8,128)S(1)} %get-tuple-element.56.sin_ref, f32[1,160,2048]{2,1,0:T(8,128)} %get-tuple-element.49.refs_0_, bf16[1,160,2048]{2,1,0:T(8,128)(2,1)S(1)} %collective-permute-done.10.refs_2_.refs_1_, ...), custom_call_target="tpu_custom_call" | custom-call | flops 1000 | bytes 1000 | tf_op jit(solution)/shard_map/sum_and_rotate/pallas_call | solution.py:249
  125.5 0.6 collective-permute-start.16
  126.4 2.7 %collective-permute-start.27 = (bf16[1,320,128]{2,1,0:T(8,128)(2,1)S(1)}, bf16[1,320,128]{2,1,0:T(8,128)(2,1)S(1)}, u32[]{:S(2)}, u32[]{:S(2)}) collective-permute-start(bf16[1,320,128]{2,1,0:T(8,128)(2,1)S(1)} %get-tuple-element.54.refs_0_), channel_id=1, source_target_pairs={{0,12},{4,8},{8,4},{12,0},{1,13},{5,9},{9,5},{13,1},{2,14},{6,10},... | collective-permute-start | bytes 245768 | tf_op jit(solution)/shard_map/ppermute | solution.py:443
  129.1 1.7 %collective-permute-start.25 = (bf16[1,320,128]{2,1,0:T(8,128)(2,1)S(1)}, bf16[1,320,128]{2,1,0:T(8,128)(2,1)S(1)}, u32[]{:S(2)}, u32[]{:S(2)}) collective-permute-start(bf16[1,320,128]{2,1,0:T(8,128)(2,1)S(1)} %get-tuple-element.54.refs_0_), channel_id=1, source_target_pairs={{0,4},{4,0},{8,12},{12,8},{1,5},{5,1},{9,13},{13,9},{2,6},{6,2},{1... | collective-permute-start | bytes 245768 | tf_op jit(solution)/shard_map/ppermute | solution.py:443
  130.9 0.6 order_and_keys.1
  131.8 2.9 %collective-permute-start.19 = (bf16[1,160,512]{2,1,0:T(8,128)(2,1)S(1)}, bf16[1,160,512]{2,1,0:T(8,128)(2,1)S(1)}, u32[]{:S(2)}, u32[]{:S(2)}) collective-permute-start(bf16[1,160,512]{2,1,0:T(8,128)(2,1)S(1)} %copy-done), channel_id=1, source_target_pairs={{0,8},{4,12},{8,0},{12,4},{1,9},{5,13},{9,1},{13,5},{2,10},{6,14},... | collective-permute-start | bytes 491528 | tf_op jit(solution)/shard_map/ppermute | solution.py:443
  134.7 7.6 %score_heads.2 = (bf16[1,16,640,640]{3,2,1,0:T(8,128)(2,1)}, f32[8,128]{1,0:T(8,128)S(1)}) custom-call(bf16[640,640]{1,0:T(8,128)(2,1)S(1)} %get-tuple-element.46.order_ref, bf16[128,640]{1,0:T(8,128)(2,1)S(1)} %get-tuple-element.47.key_t_ref, bf16[160,2048]{1,0:T(8,128)(2,1)S(1)} %sum_and_rotate.3.refs_0_, bf16[160,1536]{1,0:T(8,128)(2,1)} %sum_and_rotate.4.refs_1_, ...), custom_call_target="tpu_custom_call" | custom-call | flops 1000 | bytes 1000 | tf_op jit(solution)/shard_map/score_heads/pallas_call | solution.py:404
  142.4 0.7 collective-permute-done.18.refs_1_
  143.1 1.1 sum_and_rotate.5.refs_1_
  144.4 2.2 %order_values.1.refs_5_ = bf16[640,512]{1,0:T(8,128)(2,1)} custom-call(s32[4]{0:T(128)S(1)} %pad_add_fusion.7.place_ref, bf16[640,640]{1,0:T(8,128)(2,1)S(1)} %get-tuple-element.46.order_ref, bf16[4,320,128]{2,1,0:T(8,128)(2,1)S(1)} %stack_slots.1.refs_0_.refs_1_, bf16[4,320,128]{2,1,0:T(8,128)(2,1)S(1)} %stack_slots.1.refs_0_.refs_1_, ...), custom_call_target="tpu_custom_call" | custom-call | tf_op jit(solution)/shard_map/order_values/pallas_call | solution.py:370
  146.6 4.2 %score_heads.3 = (bf16[1,16,640,640]{3,2,1,0:T(8,128)(2,1)}, f32[8,128]{1,0:T(8,128)}) custom-call(bf16[640,640]{1,0:T(8,128)(2,1)S(1)} %get-tuple-element.46.order_ref, bf16[128,640]{1,0:T(8,128)(2,1)S(1)} %get-tuple-element.47.key_t_ref, bf16[160,2048]{1,0:T(8,128)(2,1)S(1)} %sum_and_rotate.3.refs_0_, ...), custom_call_target="tpu_custom_call", output_to_operand_aliasing={{0}: (6, {})} | custom-call | flops 1000 | bytes 1000 | tf_op jit(solution)/shard_map/score_heads/pallas_call | solution.py:404
  (70 shorter events, 4.0 us)
Async XLA Ops:
  0.6 32.5 %collective-permute-start = (bf16[320,2048]{1,0:T(8,128)(2,1)}, bf16[320,2048]{1,0:T(8,128)(2,1)S(1)}, u32[]{:S(2)}, u32[]{:S(2)}) collective-permute-start(bf16[320,2048]{1,0:T(8,128)(2,1)} %refs_0_.5), channel_id=1, source_target_pairs={{0,2},{2,0},{1,3},{3,1},{4,6},{6,4},{5,7},{7,5},{8,10},{10,8},{9,1... | collective-permute-start | bytes 3932168 | tf_op jit(solution)/shard_map/ppermute | solution.py:473
  15.2 2.3 %collective-permute-start.1 = (bf16[2,160,1024]{2,1,0:T(8,128)(2,1)}, bf16[2,160,1024]{2,1,0:T(8,128)(2,1)S(1)}, u32[]{:S(2)}, u32[]{:S(2)}) collective-permute-start(bf16[2,160,1024]{2,1,0:T(8,128)(2,1)} %get-tuple-element.30), channel_id=1, source_target_pairs={{0,1},{1,0},{2,3},{3,2},{4,5},{5,4},{6,7},{7,6},{8,9},{9,8},{10,11... | collective-permute-start | bytes 1966088 | tf_op jit(solution)/shard_map/ppermute | solution.py:446
  15.2 3.2 %collective-permute-start.2 = (bf16[2,160,1024]{2,1,0:T(8,128)(2,1)}, bf16[2,160,1024]{2,1,0:T(8,128)(2,1)S(1)}, u32[]{:S(2)}, u32[]{:S(2)}) collective-permute-start(bf16[2,160,1024]{2,1,0:T(8,128)(2,1)} %get-tuple-element.31), channel_id=1, source_target_pairs={{0,1},{1,0},{2,3},{3,2},{4,5},{5,4},{6,7},{7,6},{8,9},{9,8},{10,11... | collective-permute-start | bytes 1966088 | tf_op jit(solution)/shard_map/ppermute | solution.py:446
  19.6 36.3 %collective-permute-start.7 = (bf16[2,160,2048]{2,1,0:T(8,128)(2,1)}, bf16[2,160,2048]{2,1,0:T(8,128)(2,1)}, u32[]{:S(2)}, u32[]{:S(2)}) collective-permute-start(bf16[2,160,2048]{2,1,0:T(8,128)(2,1)} %add_rows.7.refs_2_), channel_id=1, source_target_pairs={{0,4},{4,0},{8,12},{12,8},{1,5},{5,1},{9,13},{13,9},{2,6},{6,2},{1... | collective-permute-start | bytes 3932168 | tf_op jit(solution)/shard_map/ppermute | solution.py:443
  40.2 11.0 %collective-permute-start.3 = (bf16[4,160,512]{2,1,0:T(8,128)(2,1)}, bf16[4,160,512]{2,1,0:T(8,128)(2,1)S(1)}, u32[]{:S(2)}, u32[]{:S(2)}) collective-permute-start(bf16[4,160,512]{2,1,0:T(8,128)(2,1)} %get-tuple-element.34.refs_2_), channel_id=1, source_target_pairs={{0,1},{1,0},{2,3},{3,2},{4,5},{5,4},{6,7},{7,6},{8,9},{9,8},{10,11... | collective-permute-start | bytes 1966088 | tf_op jit(solution)/shard_map/ppermute | solution.py:446
  40.2 15.8 %collective-permute-start.6 = (bf16[1,160,2048]{2,1,0:T(8,128)(2,1)}, bf16[1,160,2048]{2,1,0:T(8,128)(2,1)}, u32[]{:S(2)}, u32[]{:S(2)}) collective-permute-start(bf16[1,160,2048]{2,1,0:T(8,128)(2,1)} %get-tuple-element.32.refs_4_), channel_id=1, source_target_pairs={{0,1},{1,0},{2,3},{3,2},{4,5},{5,4},{6,7},{7,6},{8,9},{9,8},{10,11... | collective-permute-start | bytes 1966088 | tf_op jit(solution)/shard_map/ppermute | solution.py:446
  47.6 1.1 copy-start.1
  48.7 2.0 %collective-permute-start.4 = (bf16[1,160,1024]{2,1,0:T(8,128)(2,1)}, bf16[1,160,1024]{2,1,0:T(8,128)(2,1)}, u32[]{:S(2)}, u32[]{:S(2)}) collective-permute-start(bf16[1,160,1024]{2,1,0:T(8,128)(2,1)} %get-tuple-element.36), channel_id=1, source_target_pairs={{0,1},{1,0},{2,3},{3,2},{4,5},{5,4},{6,7},{7,6},{8,9},{9,8},{10,11... | collective-permute-start | bytes 983048 | tf_op jit(solution)/shard_map/ppermute | solution.py:446
  48.7 2.4 %collective-permute-start.5 = (bf16[1,160,1024]{2,1,0:T(8,128)(2,1)}, bf16[1,160,1024]{2,1,0:T(8,128)(2,1)}, u32[]{:S(2)}, u32[]{:S(2)}) collective-permute-start(bf16[1,160,1024]{2,1,0:T(8,128)(2,1)} %get-tuple-element.37), channel_id=1, source_target_pairs={{0,1},{1,0},{2,3},{3,2},{4,5},{5,4},{6,7},{7,6},{8,9},{9,8},{10,11... | collective-permute-start | bytes 983048 | tf_op jit(solution)/shard_map/ppermute | solution.py:446
  51.1 1.3 copy-start.2
  54.6 35.4 %collective-permute-start.13 = (bf16[1,160,2560]{2,1,0:T(8,128)(2,1)}, bf16[1,160,2560]{2,1,0:T(8,128)(2,1)}, u32[]{:S(2)}, u32[]{:S(2)}) collective-permute-start(bf16[1,160,2560]{2,1,0:T(8,128)(2,1)} %add_rows.8.refs_3_.refs_2_), channel_id=1, source_target_pairs={{0,4},{4,0},{8,12},{12,8},{1,5},{5,1},{9,13},{13,9},{2,6},{6,2},{1... | collective-permute-start | bytes 2457608 | tf_op jit(solution)/shard_map/ppermute | solution.py:443
  58.7 30.3 %collective-permute-start.14 = (bf16[1,160,2048]{2,1,0:T(8,128)(2,1)}, bf16[1,160,2048]{2,1,0:T(8,128)(2,1)}, u32[]{:S(2)}, u32[]{:S(2)}) collective-permute-start(bf16[1,160,2048]{2,1,0:T(8,128)(2,1)} %add_rows.9.refs_3_), channel_id=1, source_target_pairs={{0,8},{4,12},{8,0},{12,4},{1,9},{5,13},{9,1},{13,5},{2,10},{6,14},... | collective-permute-start | bytes 1966088 | tf_op jit(solution)/shard_map/ppermute | solution.py:443
  68.3 9.2 %copy-start.4 = (s32[640]{0:T(1024)S(1)}, s32[640]{0:T(1024)}, u32[]{:S(2)}) copy-start(s32[640]{0:T(1024)} %param.10) | copy-start | bytes 7684
  68.3 9.2 %copy-start.5 = (s32[640]{0:T(1024)S(1)}, s32[640]{0:T(1024)}, u32[]{:S(2)}) copy-start(s32[640]{0:T(1024)} %param.11) | copy-start | bytes 7684
  75.4 2.0 %collective-permute-start.9 = (bf16[1,160,1024]{2,1,0:T(8,128)(2,1)}, bf16[1,160,1024]{2,1,0:T(8,128)(2,1)}, u32[]{:S(2)}, u32[]{:S(2)}) collective-permute-start(bf16[1,160,1024]{2,1,0:T(8,128)(2,1)} %get-tuple-element.42), channel_id=1, source_target_pairs={{0,1},{1,0},{2,3},{3,2},{4,5},{5,4},{6,7},{7,6},{8,9},{9,8},{10,11... | collective-permute-start | bytes 983048 | tf_op jit(solution)/shard_map/ppermute | solution.py:446
  75.6 8.5 %collective-permute-start.11 = (bf16[1,160,1024]{2,1,0:T(8,128)(2,1)}, bf16[1,160,1024]{2,1,0:T(8,128)(2,1)S(1)}, u32[]{:S(2)}, u32[]{:S(2)}) collective-permute-start(bf16[1,160,1024]{2,1,0:T(8,128)(2,1)} %get-tuple-element.39.refs_2_), channel_id=1, source_target_pairs={{0,1},{1,0},{2,3},{3,2},{4,5},{5,4},{6,7},{7,6},{8,9},{9,8},{10,11... | collective-permute-start | bytes 983048 | tf_op jit(solution)/shard_map/ppermute | solution.py:446
  76.1 7.3 %collective-permute-start.12 = (bf16[1,160,1024]{2,1,0:T(8,128)(2,1)}, bf16[1,160,1024]{2,1,0:T(8,128)(2,1)S(1)}, u32[]{:S(2)}, u32[]{:S(2)}) collective-permute-start(bf16[1,160,1024]{2,1,0:T(8,128)(2,1)} %get-tuple-element.44), channel_id=1, source_target_pairs={{0,1},{1,0},{2,3},{3,2},{4,5},{5,4},{6,7},{7,6},{8,9},{9,8},{10,11... | collective-permute-start | bytes 983048 | tf_op jit(solution)/shard_map/ppermute | solution.py:446
  77.4 1.8 %collective-permute-start.8 = (bf16[1,160,1024]{2,1,0:T(8,128)(2,1)}, bf16[1,160,1024]{2,1,0:T(8,128)(2,1)S(1)}, u32[]{:S(2)}, u32[]{:S(2)}) collective-permute-start(bf16[1,160,1024]{2,1,0:T(8,128)(2,1)} %get-tuple-element.41.refs_5_), channel_id=1, source_target_pairs={{0,1},{1,0},{2,3},{3,2},{4,5},{5,4},{6,7},{7,6},{8,9},{9,8},{10,11... | collective-permute-start | bytes 983048 | tf_op jit(solution)/shard_map/ppermute | solution.py:446
  79.2 2.2 %copy-start.6 = (bf16[1,160,2048]{2,1,0:T(8,128)(2,1)S(1)}, bf16[1,160,2048]{2,1,0:T(8,128)(2,1)}, u32[]{:S(2)}) copy-start(bf16[1,160,2048]{2,1,0:T(8,128)(2,1)} %get-tuple-element.48) | copy-start | bytes 1966084
  81.5 1.9 %copy-start.3 = (bf16[1,160,2048]{2,1,0:T(8,128)(2,1)S(1)}, bf16[1,160,2048]{2,1,0:T(8,128)(2,1)}, u32[]{:S(2)}) copy-start(bf16[1,160,2048]{2,1,0:T(8,128)(2,1)} %add_rows.10.refs_2_) | copy-start | bytes 1966084
  81.5 23.5 %collective-permute-start.17 = (bf16[1,160,2048]{2,1,0:T(8,128)(2,1)S(1)}, bf16[1,160,2048]{2,1,0:T(8,128)(2,1)S(1)}, u32[]{:S(2)}, u32[]{:S(2)}) collective-permute-start(bf16[1,160,2048]{2,1,0:T(8,128)(2,1)S(1)} %copy-done.6), channel_id=1, source_target_pairs={{0,1},{1,0},{2,3},{3,2},{4,5},{5,4},{6,7},{7,6},{8,9},{9,8},{10,11... | collective-permute-start | bytes 1966088 | tf_op jit(solution)/shard_map/ppermute | solution.py:446
  83.4 30.4 %collective-permute-start.10 = (bf16[1,160,2048]{2,1,0:T(8,128)(2,1)S(1)}, bf16[1,160,2048]{2,1,0:T(8,128)(2,1)S(1)}, u32[]{:S(2)}, u32[]{:S(2)}) collective-permute-start(bf16[1,160,2048]{2,1,0:T(8,128)(2,1)S(1)} %copy-done.3), channel_id=1, source_target_pairs={{0,4},{4,0},{8,12},{12,8},{1,5},{5,1},{9,13},{13,9},{2,6},{6,2},{1... | collective-permute-start | bytes 1966088 | tf_op jit(solution)/shard_map/ppermute | solution.py:443
  92.5 30.3 %collective-permute-start.15 = (bf16[1,160,2048]{2,1,0:T(8,128)(2,1)}, bf16[1,160,2048]{2,1,0:T(8,128)(2,1)S(1)}, u32[]{:S(2)}, u32[]{:S(2)}) collective-permute-start(bf16[1,160,2048]{2,1,0:T(8,128)(2,1)} %add_rows.12.refs_3_), channel_id=1, source_target_pairs={{0,8},{4,12},{8,0},{12,4},{1,9},{5,13},{9,1},{13,5},{2,10},{6,14},... | collective-permute-start | bytes 1966088 | tf_op jit(solution)/shard_map/ppermute | solution.py:443
  103.5 1.5 copy-start
  103.5 10.3 %collective-permute-start.20 = (bf16[1,160,1024]{2,1,0:T(8,128)(2,1)}, bf16[1,160,1024]{2,1,0:T(8,128)(2,1)S(1)}, u32[]{:S(2)}, u32[]{:S(2)}) collective-permute-start(bf16[1,160,1024]{2,1,0:T(8,128)(2,1)} %get-tuple-element.50), channel_id=1, source_target_pairs={{0,1},{1,0},{2,3},{3,2},{4,5},{5,4},{6,7},{7,6},{8,9},{9,8},{10,11... | collective-permute-start | bytes 983048 | tf_op jit(solution)/shard_map/ppermute | solution.py:446
  103.5 10.3 %collective-permute-start.21 = (bf16[1,160,1024]{2,1,0:T(8,128)(2,1)}, bf16[1,160,1024]{2,1,0:T(8,128)(2,1)S(1)}, u32[]{:S(2)}, u32[]{:S(2)}) collective-permute-start(bf16[1,160,1024]{2,1,0:T(8,128)(2,1)} %get-tuple-element.51), channel_id=1, source_target_pairs={{0,1},{1,0},{2,3},{3,2},{4,5},{5,4},{6,7},{7,6},{8,9},{9,8},{10,11... | collective-permute-start | bytes 983048 | tf_op jit(solution)/shard_map/ppermute | solution.py:446
  107.2 24.3 %collective-permute-start.22 = (bf16[160,2048]{1,0:T(8,128)(2,1)S(1)}, bf16[160,2048]{1,0:T(8,128)(2,1)}, u32[]{:S(2)}, u32[]{:S(2)}) collective-permute-start(bf16[160,2048]{1,0:T(8,128)(2,1)S(1)} %sum_and_rotate.3.refs_0_), channel_id=1, source_target_pairs={{0,1},{1,0},{2,3},{3,2},{4,5},{5,4},{6,7},{7,6},{8,9},{9,8},{10,11... | collective-permute-start | bytes 1966088 | tf_op jit(solution)/shard_map/ppermute | solution.py:446
  125.2 6.7 %collective-permute-start.23 = (bf16[160,1536]{1,0:T(8,128)(2,1)}, bf16[160,1536]{1,0:T(8,128)(2,1)}, u32[]{:S(2)}, u32[]{:S(2)}) collective-permute-start(bf16[160,1536]{1,0:T(8,128)(2,1)} %sum_and_rotate.4.refs_1_), channel_id=1, source_target_pairs={{0,1},{1,0},{2,3},{3,2},{4,5},{5,4},{6,7},{7,6},{8,9},{9,8},{10,11... | collective-permute-start | bytes 1474568 | tf_op jit(solution)/shard_map/ppermute | solution.py:446
  125.5 3.5 %collective-permute-start.16 = (bf16[320,128]{1,0:T(8,128)(2,1)S(1)}, bf16[320,128]{1,0:T(8,128)(2,1)S(1)}, u32[]{:S(2)}, u32[]{:S(2)}) collective-permute-start(bf16[320,128]{1,0:T(8,128)(2,1)S(1)} %get-tuple-element.45.own_ref), channel_id=1, source_target_pairs={{0,1},{1,0},{2,3},{3,2},{4,5},{5,4},{6,7},{7,6},{8,9},{9,8},{10,11... | collective-permute-start | bytes 245768 | tf_op jit(solution)/shard_map/ppermute | solution.py:446
  126.4 15.9 %collective-permute-start.27 = (bf16[1,320,128]{2,1,0:T(8,128)(2,1)S(1)}, bf16[1,320,128]{2,1,0:T(8,128)(2,1)S(1)}, u32[]{:S(2)}, u32[]{:S(2)}) collective-permute-start(bf16[1,320,128]{2,1,0:T(8,128)(2,1)S(1)} %get-tuple-element.54.refs_0_), channel_id=1, source_target_pairs={{0,12},{4,8},{8,4},{12,0},{1,13},{5,9},{9,5},{13,1},{2,14},{6,10},... | collective-permute-start | bytes 245768 | tf_op jit(solution)/shard_map/ppermute | solution.py:443
  129.1 13.2 %collective-permute-start.26 = (bf16[1,320,128]{2,1,0:T(8,128)(2,1)S(1)}, bf16[1,320,128]{2,1,0:T(8,128)(2,1)S(1)}, u32[]{:S(2)}, u32[]{:S(2)}) collective-permute-start(bf16[1,320,128]{2,1,0:T(8,128)(2,1)S(1)} %get-tuple-element.54.refs_0_), channel_id=1, source_target_pairs={{0,8},{4,12},{8,0},{12,4},{1,9},{5,13},{9,1},{13,5},{2,10},{6,14},... | collective-permute-start | bytes 245768 | tf_op jit(solution)/shard_map/ppermute | solution.py:443
  129.1 13.2 %collective-permute-start.25 = (bf16[1,320,128]{2,1,0:T(8,128)(2,1)S(1)}, bf16[1,320,128]{2,1,0:T(8,128)(2,1)S(1)}, u32[]{:S(2)}, u32[]{:S(2)}) collective-permute-start(bf16[1,320,128]{2,1,0:T(8,128)(2,1)S(1)} %get-tuple-element.54.refs_0_), channel_id=1, source_target_pairs={{0,4},{4,0},{8,12},{12,8},{1,5},{5,1},{9,13},{13,9},{2,6},{6,2},{1... | collective-permute-start | bytes 245768 | tf_op jit(solution)/shard_map/ppermute | solution.py:443
  131.5 11.7 %collective-permute-start.18 = (bf16[1,160,512]{2,1,0:T(8,128)(2,1)}, bf16[1,160,512]{2,1,0:T(8,128)(2,1)S(1)}, u32[]{:S(2)}, u32[]{:S(2)}) collective-permute-start(bf16[1,160,512]{2,1,0:T(8,128)(2,1)} %add_rows.11.refs_7_), channel_id=1, source_target_pairs={{0,4},{4,0},{8,12},{12,8},{1,5},{5,1},{9,13},{13,9},{2,6},{6,2},{1... | collective-permute-start | bytes 491528 | tf_op jit(solution)/shard_map/ppermute | solution.py:443
  131.8 11.3 %collective-permute-start.19 = (bf16[1,160,512]{2,1,0:T(8,128)(2,1)S(1)}, bf16[1,160,512]{2,1,0:T(8,128)(2,1)S(1)}, u32[]{:S(2)}, u32[]{:S(2)}) collective-permute-start(bf16[1,160,512]{2,1,0:T(8,128)(2,1)S(1)} %copy-done), channel_id=1, source_target_pairs={{0,8},{4,12},{8,0},{12,4},{1,9},{5,13},{9,1},{13,5},{2,10},{6,14},... | collective-permute-start | bytes 491528 | tf_op jit(solution)/shard_map/ppermute | solution.py:443
  142.4 2.1 %collective-permute-start.28 = (bf16[4,320,128]{2,1,0:T(8,128)(2,1)S(1)}, bf16[4,320,128]{2,1,0:T(8,128)(2,1)S(1)}, u32[]{:S(2)}, u32[]{:S(2)}) collective-permute-start(bf16[4,320,128]{2,1,0:T(8,128)(2,1)S(1)} %stack_slots.1.refs_0_.refs_1_), channel_id=1, source_target_pairs={{0,1},{1,0},{2,3},{3,2},{4,5},{5,4},{6,7},{7,6},{8,9},{9,8},{10,11... | collective-permute-start | bytes 983048 | tf_op jit(solution)/shard_map/ppermute | solution.py:446
  144.3 2.3 %collective-permute-start.24 = (bf16[160,512]{1,0:T(8,128)(2,1)S(1)}, bf16[160,512]{1,0:T(8,128)(2,1)S(1)}, u32[]{:S(2)}, u32[]{:S(2)}) collective-permute-start(bf16[160,512]{1,0:T(8,128)(2,1)S(1)} %sum_and_rotate.5.refs_1_), channel_id=1, source_target_pairs={{0,1},{1,0},{2,3},{3,2},{4,5},{5,4},{6,7},{7,6},{8,9},{9,8},{10,11... | collective-permute-start | bytes 491528 | tf_op jit(solution)/shard_map/ppermute | solution.py:446

commit v18 on v15

--- a/solution.py
+++ b/solution.py
@@ -100,7 +100,7 @@
         compiler_params=pltpu.CompilerParams(vmem_limit_bytes=VMEM_BYTES),
         cost_estimate=cost,
         name="query_products",
-    )(place, *blocks, *in_hbm([w]), *in_hbm(after[:1]), *after[1:])
+    )(place, *blocks, *in_hbm([w, *after]))
     return outs[0], outs[1:]
 
 
@@ -504,7 +504,7 @@
             return [], behind
         keep, got = evens[b]
         summed = add_rows(
-            0, len(even), half, 0, keep, got, start, cols, pair, len(odd), (fars[b],), behind
+            0, len(even), half, 0, keep, got, start, cols, pair, len(odd), (fars[b],), behind, b == last
         )
         terms, first = spread({x: summed[k] for k, x in enumerate(even)})
         return [(term, 0, 0) for term in terms], (first,)
@@ -534,7 +534,7 @@
             evens.append((keep, got[:1] if len(even) == 1 else [jnp.concatenate(got[:-1])]))
             owns.append((keep, len(even), got[-1:]))
         else:
-            keep, got, given = project(even, [block], tile, after, HEAVY)
+            keep, got, given = project(even, [block], tile, after, HEAVY, near=True)
             evens.append((keep, got))
         after = (given,)
     near_keep, near_got, given = project([1], placed[last:], tile, after)

time: 148 us -> 148 us (level)
  waiting for transfers between devices: 28.2 us -> 30.4 us
    ppermute x10, waiting for transfers between devices: 21.1 us -> 23.2 us  [swap(): return lax.ppermute(x, 'fsdp', [(i, i ^ bit) for i in range(shards)])]
  transfers between devices with their start and end apart: 29 -> 29, of which waited for: 11 -> 11; matrix products, arithmetic and copies ran while one was open for 2% -> 2% of each run, Pallas kernels for 60% -> 59%
where the time goes in v18:
time: 148 us; the launch traced here: 147 us
  Pallas kernels  90.7 us (61%)
  waiting for transfers between devices  30.4 us (21%)
  starting transfers between devices  23.1 us (16%)
  other arithmetic  2.05 us (1%)
    pallas_call x6, Pallas kernels, project_query(): pl.pallas_call(functools.partial(query_kernel, count, pieces, by_slot), g...  51.2 us
    ppermute x10, waiting for transfers between devices, swap(): return lax.ppermute(x, 'fsdp', [(i, i ^ bit) for i in range(shards)])  23.2 us
    ppermute x10, starting transfers between devices, swap(): return lax.ppermute(x, 'fsdp', [(i, i ^ bit) for i in range(shards)])  16.2 us
    pallas_call x7, Pallas kernels, add_rows(): pl.pallas_call(functools.partial(add_kernel, len(gots), len(pair) // 2, l...  13.1 us
    pallas_call x2, Pallas kernels, score_heads(): pl.pallas_call(functools.partial(score_kernel, len(queries)), grid=(count...  10.7 us
    ppermute x18, waiting for transfers between devices, other_core(): return lax.ppermute(x, 'rep', [(0, 1), (1, 0)])  7.19 us
    pallas_call x1, Pallas kernels, project_pair(): pl.pallas_call(functools.partial(pair_kernel, count), grid_spec=pltpu.Pre...  7.11 us
    pallas_call x3, Pallas kernels, sum_and_rotate(): pl.pallas_call(functools.partial(rotate_kernel, len(terms), len(gots)), g...  4.77 us
  transfers between devices with their start and end apart: 29, of which 11 were waited for; matrix products, arithmetic and copies ran while one was open for 2% of the time, Pallas kernels for 59%

profile of v18, /device:TPU:0, one launch (start us, length us, event | category | flops | bytes accessed | tf_op | source)
XLA Modules:
  0.0 147.4 jit_solution(10470488127356699486)
XLA Ops:
  0.6 3.0 %collective-permute-start = (bf16[320,2048]{1,0:T(8,128)(2,1)}, bf16[320,2048]{1,0:T(8,128)(2,1)S(1)}, u32[]{:S(2)}, u32[]{:S(2)}) collective-permute-start(bf16[320,2048]{1,0:T(8,128)(2,1)} %refs_0_.5), channel_id=1, source_target_pairs={{0,2},{2,0},{1,3},{3,1},{4,6},{6,4},{5,7},{7,5},{8,10},{10,8},{9,1... | collective-permute-start | bytes 3932168 | tf_op jit(solution)/shard_map/ppermute | solution.py:474
  3.7 11.5 %query_products.6 = (f32[2,160,2048]{2,1,0:T(8,128)S(1)}, bf16[2,160,1024]{2,1,0:T(8,128)(2,1)}, bf16[2,160,1024]{2,1,0:T(8,128)(2,1)}) custom-call(s32[3]{0:T(128)S(1)} %pad_add_fusion.2.place_ref, bf16[320,2048]{1,0:T(8,128)(2,1)} %refs_0_.5, bf16[2048,8192]{1,0:T(8,128)(2,1)} %refs_1_.11), custom_call_target="tpu_custom_call" | custom-call | flops 1000 | bytes 1000 | tf_op jit(solution)/shard_map/query_products/pallas_call | solution.py:87
  15.2 0.5 collective-permute-start.2
  15.7 1.8 %collective-permute-done.1.refs_1_ = bf16[2,160,1024]{2,1,0:T(8,128)(2,1)S(1)} collective-permute-done((bf16[2,160,1024]{2,1,0:T(8,128)(2,1)}, bf16[2,160,1024]{2,1,0:T(8,128)(2,1)S(1)}, u32[]{:S(2)}, u32[]{:S(2)}) %collective-permute-start.1) | collective-permute-done | bytes 655392 | tf_op jit(solution)/shard_map/ppermute | solution.py:447
  17.5 0.9 collective-permute-done.2.refs_2_
  18.5 1.2 add_rows.7.refs_2_
  19.6 1.6 %collective-permute-start.7 = (bf16[2,160,2048]{2,1,0:T(8,128)(2,1)}, bf16[2,160,2048]{2,1,0:T(8,128)(2,1)}, u32[]{:S(2)}, u32[]{:S(2)}) collective-permute-start(bf16[2,160,2048]{2,1,0:T(8,128)(2,1)} %add_rows.7.refs_2_), channel_id=1, source_target_pairs={{0,4},{4,0},{8,12},{12,8},{1,5},{5,1},{9,13},{13,9},{2,6},{6,2},{1... | collective-permute-start | bytes 3932168 | tf_op jit(solution)/shard_map/ppermute | solution.py:444
  21.4 11.7 %query_products.7 = (f32[2,160,2048]{2,1,0:T(8,128)}, bf16[1,160,2048]{2,1,0:T(8,128)(2,1)}, bf16[1,160,2048]{2,1,0:T(8,128)(2,1)}) custom-call(s32[3]{0:T(128)S(1)} %pad_add_fusion.1.place_ref, bf16[320,2048]{1,0:T(8,128)(2,1)} %refs_0_.5, bf16[2048,8192]{1,0:T(8,128)(2,1)} %refs_1_.11, bf16[2,160,2048]{2,1,0:T(8,128)(2,1)} %add_rows.7.refs_2_), custom_call_target="tpu_custom_call" | custom-call | flops 1000 | bytes 1000 | tf_op jit(solution)/shard_map/query_products/pallas_call | solution.py:87
  33.1 7.1 %key_value_products.1 = (f32[4,160,512]{2,1,0:T(8,128)}, bf16[4,160,512]{2,1,0:T(8,128)(2,1)}) custom-call(s32[5]{0:T(128)S(1)} %stack.62.place_ref, bf16[320,2048]{1,0:T(8,128)(2,1)} %refs_0_.5, bf16[320,2048]{1,0:T(8,128)(2,1)S(1)} %collective-permute-done.refs_1_.refs_0_, bf16[2048,512]{1,0:T(8,128)(2,1)} %refs_2_.1, bf16[2048,512]{1,0:T(8,128)(2,1)} %refs_3_.1, ...), custom_call_target="tpu_custom_call" | custom-call | flops 1000 | bytes 1000 | tf_op jit(solution)/shard_map/key_value_products/pallas_call | solution.py:132
  40.2 0.5 collective-permute-start.6
  40.8 6.9 %query_products.8 = (f32[1,160,2048]{2,1,0:T(8,128)S(1)}, bf16[1,160,1024]{2,1,0:T(8,128)(2,1)}, bf16[1,160,1024]{2,1,0:T(8,128)(2,1)}) custom-call(s32[2]{0:T(128)S(1)} %get-tuple-element.66.place_ref, bf16[320,2048]{1,0:T(8,128)(2,1)S(1)} %collective-permute-done.refs_1_.refs_0_, bf16[2048,8192]{1,0:T(8,128)(2,1)} %refs_1_.11, ...), custom_call_target="tpu_custom_call" | custom-call | flops 1000 | bytes 1000 | tf_op jit(solution)/shard_map/query_products/pallas_call | solution.py:87
  48.3 1.4 collective-permute-done.4.refs_1_
  49.7 0.5 collective-permute-done.5.refs_2_
  50.1 2.2 %add_rows.8.refs_3_.refs_2_ = bf16[1,160,2560]{2,1,0:T(8,128)(2,1)} custom-call(f32[1,160,2048]{2,1,0:T(8,128)S(1)} %get-tuple-element.35.refs_0_, bf16[1,160,1024]{2,1,0:T(8,128)(2,1)} %collective-permute-done.4.refs_1_, bf16[1,160,1024]{2,1,0:T(8,128)(2,1)} %collective-permute-done.5.refs_2_, f32[4,160,512]{2,1,0:T(8,128)} %get-tuple-element.33.refs_3_.refs_0_, ...), custom_call_target="tpu_custom_call" | custom-call | flops 1000 | bytes 1000 | tf_op jit(solution)/shard_map/add_rows/pallas_call | solution.py:200
  52.4 1.3 collective-permute-start.13
  53.7 2.7 %add_rows.9.refs_3_ = bf16[1,160,2048]{2,1,0:T(8,128)(2,1)} custom-call(f32[2,160,2048]{2,1,0:T(8,128)} %get-tuple-element.38.refs_0_, bf16[1,160,2048]{2,1,0:T(8,128)(2,1)} %collective-permute-done.6.refs_1_, bf16[2,160,2048]{2,1,0:T(8,128)(2,1)} %collective-permute-done.7.refs_2_.refs_1_, bf16[1,160,2560]{2,1,0:T(8,128)(2,1)} %add_rows.8.refs_3_.refs_2_), custom_call_target="tpu_custom_call" | custom-call | flops 1000 | bytes 1000 | tf_op jit(solution)/shard_map/add_rows/pallas_call | solution.py:200
  56.4 2.6 %collective-permute-start.14 = (bf16[1,160,2048]{2,1,0:T(8,128)(2,1)}, bf16[1,160,2048]{2,1,0:T(8,128)(2,1)S(1)}, u32[]{:S(2)}, u32[]{:S(2)}) collective-permute-start(bf16[1,160,2048]{2,1,0:T(8,128)(2,1)} %add_rows.9.refs_3_), channel_id=1, source_target_pairs={{0,8},{4,12},{8,0},{12,4},{1,9},{5,13},{9,1},{13,5},{2,10},{6,14},... | collective-permute-start | bytes 1966088 | tf_op jit(solution)/shard_map/ppermute | solution.py:444
  59.0 6.9 %query_products.9 = (f32[1,160,2048]{2,1,0:T(8,128)S(1)}, bf16[1,160,1024]{2,1,0:T(8,128)(2,1)}, bf16[1,160,1024]{2,1,0:T(8,128)(2,1)}) custom-call(s32[2]{0:T(128)S(1)} %pad_add_fusion.4.place_ref, bf16[320,2048]{1,0:T(8,128)(2,1)S(1)} %collective-permute-done.refs_1_.refs_0_, bf16[2048,8192]{1,0:T(8,128)(2,1)} %refs_1_.11, ...), custom_call_target="tpu_custom_call" | custom-call | flops 99999997952 | bytes 100000000 | tf_op jit(solution)/shard_map/query_products/pallas_call | solution.py:87
  65.9 7.1 %query_products.10 = (f32[1,160,2048]{2,1,0:T(8,128)}, bf16[1,160,1024]{2,1,0:T(8,128)(2,1)}, bf16[1,160,1024]{2,1,0:T(8,128)(2,1)}) custom-call(s32[2]{0:T(128)S(1)} %get-tuple-element.65.place_ref, bf16[320,2048]{1,0:T(8,128)(2,1)S(1)} %collective-permute-done.refs_1_.refs_0_, bf16[2048,8192]{1,0:T(8,128)(2,1)} %refs_1_.11, ...), custom_call_target="tpu_custom_call" | custom-call | flops 1000 | bytes 1000 | tf_op jit(solution)/shard_map/query_products/pallas_call | solution.py:87
  73.3 0.5 collective-permute-start.11
  73.8 1.2 collective-permute-done.9.refs_2_.refs_1_
  75.5 1.3 collective-permute-done.8.refs_1_
  76.9 2.4 %add_rows.10.refs_2_ = bf16[1,160,2048]{2,1,0:T(8,128)(2,1)} custom-call(f32[1,160,2048]{2,1,0:T(8,128)} %get-tuple-element.40.refs_0_, bf16[1,160,1024]{2,1,0:T(8,128)(2,1)S(1)} %collective-permute-done.8.refs_1_, bf16[1,160,1024]{2,1,0:T(8,128)(2,1)} %collective-permute-done.9.refs_2_.refs_1_, f32[4,160,512]{2,1,0:T(8,128)} %get-tuple-element.33.refs_3_.refs_0_, ...), custom_call_target="tpu_custom_call" | custom-call | flops 1000 | bytes 1000 | tf_op jit(solution)/shard_map/add_rows/pallas_call | solution.py:200
  79.5 1.8 %add_rows.11.refs_7_ = bf16[1,160,512]{2,1,0:T(8,128)(2,1)} custom-call(f32[1,160,2048]{2,1,0:T(8,128)} %get-tuple-element.40.refs_0_, bf16[1,160,1024]{2,1,0:T(8,128)(2,1)} %collective-permute-done.9.refs_2_.refs_1_, bf16[1,160,2048]{2,1,0:T(8,128)(2,1)} %add_rows.10.refs_2_), custom_call_target="tpu_custom_call" | custom-call | flops 1000 | bytes 1000 | tf_op jit(solution)/shard_map/add_rows/pallas_call | solution.py:200
  81.3 0.7 collective-permute-start.10
  82.0 4.7 %collective-permute-done.14.refs_8_.refs_2_ = bf16[1,160,2048]{2,1,0:T(8,128)(2,1)S(1)} collective-permute-done((bf16[1,160,2048]{2,1,0:T(8,128)(2,1)}, bf16[1,160,2048]{2,1,0:T(8,128)(2,1)S(1)}, u32[]{:S(2)}, u32[]{:S(2)}) %collective-permute-start.14) | collective-permute-done | bytes 655392 | tf_op jit(solution)/shard_map/ppermute | solution.py:444
  86.7 1.0 collective-permute-done.13.refs_5_.refs_6_.refs_2_
  87.7 2.1 %add_rows.12.refs_3_ = bf16[1,160,2048]{2,1,0:T(8,128)(2,1)} custom-call(f32[1,160,2048]{2,1,0:T(8,128)S(1)} %copy-done.1, bf16[1,160,1024]{2,1,0:T(8,128)(2,1)S(1)} %collective-permute-done.11.refs_1_, bf16[1,160,1024]{2,1,0:T(8,128)(2,1)S(1)} %collective-permute-done.12.refs_2_.refs_1_, f32[4,160,512]{2,1,0:T(8,128)} %get-tuple-element.33.refs_3_.refs_0_, ...), custom_call_target="tpu_custom_call" | custom-call | flops 1000 | bytes 1000 | tf_op jit(solution)/shard_map/add_rows/pallas_call | solution.py:200
  89.8 2.3 %collective-permute-start.15 = (bf16[1,160,2048]{2,1,0:T(8,128)(2,1)}, bf16[1,160,2048]{2,1,0:T(8,128)(2,1)S(1)}, u32[]{:S(2)}, u32[]{:S(2)}) collective-permute-start(bf16[1,160,2048]{2,1,0:T(8,128)(2,1)} %add_rows.12.refs_3_), channel_id=1, source_target_pairs={{0,8},{4,12},{8,0},{12,4},{1,9},{5,13},{9,1},{13,5},{2,10},{6,14},... | collective-permute-start | bytes 1966088 | tf_op jit(solution)/shard_map/ppermute | solution.py:444
  92.1 0.7 add_rows.13.refs_4_.refs_2_
  92.8 7.0 %query_products.11 = (f32[1,160,2048]{2,1,0:T(8,128)}, bf16[1,160,1024]{2,1,0:T(8,128)(2,1)}, bf16[1,160,1024]{2,1,0:T(8,128)(2,1)}) custom-call(s32[2]{0:T(128)S(1)} %pad_add_fusion.6.place_ref, bf16[320,2048]{1,0:T(8,128)(2,1)S(1)} %collective-permute-done.refs_1_.refs_0_, bf16[2048,8192]{1,0:T(8,128)(2,1)} %refs_1_.11, ...), custom_call_target="tpu_custom_call" | custom-call | flops 99999997952 | bytes 100000000 | tf_op jit(solution)/shard_map/query_products/pallas_call | solution.py:87
  99.8 0.5 collective-permute-start.21
  100.3 0.6 fusion.4
  101.3 2.1 %sum_and_rotate.3.refs_0_ = bf16[160,2048]{1,0:T(8,128)(2,1)S(1)} custom-call(f32[160,128]{1,0:T(8,128)S(1)} %get-tuple-element.59.cos_ref, f32[160,128]{1,0:T(8,128)S(1)} %get-tuple-element.57.sin_ref, f32[2,160,2048]{2,1,0:T(8,128)} %get-tuple-element.38.refs_0_, bf16[2,160,2048]{2,1,0:T(8,128)(2,1)} %collective-permute-done.7.refs_2_.refs_1_, ...), custom_call_target="tpu_custom_call" | custom-call | flops 1000 | bytes 1000 | tf_op jit(solution)/shard_map/sum_and_rotate/pallas_call | solution.py:250
  103.5 8.5 %collective-permute-done.10.refs_2_.refs_1_ = bf16[1,160,2048]{2,1,0:T(8,128)(2,1)S(1)} collective-permute-done((bf16[1,160,2048]{2,1,0:T(8,128)(2,1)S(1)}, bf16[1,160,2048]{2,1,0:T(8,128)(2,1)S(1)}, u32[]{:S(2)}, u32[]{:S(2)}) %collective-permute-start.10) | collective-permute-done | bytes 655392 | tf_op jit(solution)/shard_map/ppermute | solution.py:444
  112.0 8.1 %collective-permute-done.15.refs_3_.refs_2_ = bf16[1,160,2048]{2,1,0:T(8,128)(2,1)S(1)} collective-permute-done((bf16[1,160,2048]{2,1,0:T(8,128)(2,1)}, bf16[1,160,2048]{2,1,0:T(8,128)(2,1)S(1)}, u32[]{:S(2)}, u32[]{:S(2)}) %collective-permute-start.15) | collective-permute-done | bytes 655392 | tf_op jit(solution)/shard_map/ppermute | solution.py:444
  120.1 1.6 %sum_and_rotate.4.refs_1_ = bf16[160,1536]{1,0:T(8,128)(2,1)S(1)} custom-call(f32[160,128]{1,0:T(8,128)S(1)} %get-tuple-element.58.cos_ref, f32[160,128]{1,0:T(8,128)S(1)} %get-tuple-element.56.sin_ref, f32[1,160,2048]{2,1,0:T(8,128)} %get-tuple-element.49.refs_0_, bf16[1,160,2048]{2,1,0:T(8,128)(2,1)S(1)} %collective-permute-done.10.refs_2_.refs_1_, ...), custom_call_target="tpu_custom_call" | custom-call | flops 1000 | bytes 1000 | tf_op jit(solution)/shard_map/sum_and_rotate/pallas_call | solution.py:250
  122.0 1.1 split_and_rotate.1
  123.1 0.6 collective-permute-start.16
  124.0 2.7 %collective-permute-start.27 = (bf16[1,320,128]{2,1,0:T(8,128)(2,1)S(1)}, bf16[1,320,128]{2,1,0:T(8,128)(2,1)S(1)}, u32[]{:S(2)}, u32[]{:S(2)}) collective-permute-start(bf16[1,320,128]{2,1,0:T(8,128)(2,1)S(1)} %get-tuple-element.54.refs_0_), channel_id=1, source_target_pairs={{0,12},{4,8},{8,4},{12,0},{1,13},{5,9},{9,5},{13,1},{2,14},{6,10},... | collective-permute-start | bytes 245768 | tf_op jit(solution)/shard_map/ppermute | solution.py:444
  126.7 1.7 %collective-permute-start.25 = (bf16[1,320,128]{2,1,0:T(8,128)(2,1)S(1)}, bf16[1,320,128]{2,1,0:T(8,128)(2,1)S(1)}, u32[]{:S(2)}, u32[]{:S(2)}) collective-permute-start(bf16[1,320,128]{2,1,0:T(8,128)(2,1)S(1)} %get-tuple-element.54.refs_0_), channel_id=1, source_target_pairs={{0,4},{4,0},{8,12},{12,8},{1,5},{5,1},{9,13},{13,9},{2,6},{6,2},{1... | collective-permute-start | bytes 245768 | tf_op jit(solution)/shard_map/ppermute | solution.py:444
  128.5 0.5 order_and_keys.1
  129.4 2.9 %collective-permute-start.19 = (bf16[1,160,512]{2,1,0:T(8,128)(2,1)S(1)}, bf16[1,160,512]{2,1,0:T(8,128)(2,1)S(1)}, u32[]{:S(2)}, u32[]{:S(2)}) collective-permute-start(bf16[1,160,512]{2,1,0:T(8,128)(2,1)S(1)} %copy-done.2), channel_id=1, source_target_pairs={{0,8},{4,12},{8,0},{12,4},{1,9},{5,13},{9,1},{13,5},{2,10},{6,14},... | collective-permute-start | bytes 491528 | tf_op jit(solution)/shard_map/ppermute | solution.py:444
  132.3 7.4 %score_heads.2 = (bf16[1,16,640,640]{3,2,1,0:T(8,128)(2,1)}, f32[8,128]{1,0:T(8,128)S(1)}) custom-call(bf16[640,640]{1,0:T(8,128)(2,1)S(1)} %get-tuple-element.46.order_ref, bf16[128,640]{1,0:T(8,128)(2,1)S(1)} %get-tuple-element.47.key_t_ref, bf16[160,2048]{1,0:T(8,128)(2,1)S(1)} %sum_and_rotate.3.refs_0_, bf16[160,1536]{1,0:T(8,128)(2,1)S(1)} %sum_and_rotate.4.refs_1_, ...), custom_call_target="tpu_custom_call" | custom-call | flops 1000 | bytes 1000 | tf_op jit(solution)/shard_map/score_heads/pallas_call | solution.py:405
  139.9 0.8 collective-permute-done.18.refs_1_
  140.7 1.1 sum_and_rotate.5.refs_1_
  142.0 2.2 %order_values.1.refs_5_ = bf16[640,512]{1,0:T(8,128)(2,1)} custom-call(s32[4]{0:T(128)S(1)} %pad_add_fusion.7.place_ref, bf16[640,640]{1,0:T(8,128)(2,1)S(1)} %get-tuple-element.46.order_ref, bf16[4,320,128]{2,1,0:T(8,128)(2,1)S(1)} %stack_slots.1.refs_0_.refs_1_, bf16[4,320,128]{2,1,0:T(8,128)(2,1)S(1)} %stack_slots.1.refs_0_.refs_1_, ...), custom_call_target="tpu_custom_call" | custom-call | tf_op jit(solution)/shard_map/order_values/pallas_call | solution.py:371
  144.2 3.2 %score_heads.3 = (bf16[1,16,640,640]{3,2,1,0:T(8,128)(2,1)}, f32[8,128]{1,0:T(8,128)}) custom-call(bf16[640,640]{1,0:T(8,128)(2,1)S(1)} %get-tuple-element.46.order_ref, bf16[128,640]{1,0:T(8,128)(2,1)S(1)} %get-tuple-element.47.key_t_ref, bf16[160,2048]{1,0:T(8,128)(2,1)S(1)} %sum_and_rotate.3.refs_0_, ...), custom_call_target="tpu_custom_call", output_to_operand_aliasing={{0}: (6, {})} | custom-call | flops 1000 | bytes 1000 | tf_op jit(solution)/shard_map/score_heads/pallas_call | solution.py:405
  (74 shorter events, 3.6 us)
Async XLA Ops:
  0.6 32.5 %collective-permute-start = (bf16[320,2048]{1,0:T(8,128)(2,1)}, bf16[320,2048]{1,0:T(8,128)(2,1)S(1)}, u32[]{:S(2)}, u32[]{:S(2)}) collective-permute-start(bf16[320,2048]{1,0:T(8,128)(2,1)} %refs_0_.5), channel_id=1, source_target_pairs={{0,2},{2,0},{1,3},{3,1},{4,6},{6,4},{5,7},{7,5},{8,10},{10,8},{9,1... | collective-permute-start | bytes 3932168 | tf_op jit(solution)/shard_map/ppermute | solution.py:474
  15.2 2.3 %collective-permute-start.1 = (bf16[2,160,1024]{2,1,0:T(8,128)(2,1)}, bf16[2,160,1024]{2,1,0:T(8,128)(2,1)S(1)}, u32[]{:S(2)}, u32[]{:S(2)}) collective-permute-start(bf16[2,160,1024]{2,1,0:T(8,128)(2,1)} %get-tuple-element.30), channel_id=1, source_target_pairs={{0,1},{1,0},{2,3},{3,2},{4,5},{5,4},{6,7},{7,6},{8,9},{9,8},{10,11... | collective-permute-start | bytes 1966088 | tf_op jit(solution)/shard_map/ppermute | solution.py:447
  15.2 3.2 %collective-permute-start.2 = (bf16[2,160,1024]{2,1,0:T(8,128)(2,1)}, bf16[2,160,1024]{2,1,0:T(8,128)(2,1)S(1)}, u32[]{:S(2)}, u32[]{:S(2)}) collective-permute-start(bf16[2,160,1024]{2,1,0:T(8,128)(2,1)} %get-tuple-element.31), channel_id=1, source_target_pairs={{0,1},{1,0},{2,3},{3,2},{4,5},{5,4},{6,7},{7,6},{8,9},{9,8},{10,11... | collective-permute-start | bytes 1966088 | tf_op jit(solution)/shard_map/ppermute | solution.py:447
  19.6 34.1 %collective-permute-start.7 = (bf16[2,160,2048]{2,1,0:T(8,128)(2,1)}, bf16[2,160,2048]{2,1,0:T(8,128)(2,1)}, u32[]{:S(2)}, u32[]{:S(2)}) collective-permute-start(bf16[2,160,2048]{2,1,0:T(8,128)(2,1)} %add_rows.7.refs_2_), channel_id=1, source_target_pairs={{0,4},{4,0},{8,12},{12,8},{1,5},{5,1},{9,13},{13,9},{2,6},{6,2},{1... | collective-permute-start | bytes 3932168 | tf_op jit(solution)/shard_map/ppermute | solution.py:444
  40.2 9.9 %collective-permute-start.3 = (bf16[4,160,512]{2,1,0:T(8,128)(2,1)}, bf16[4,160,512]{2,1,0:T(8,128)(2,1)S(1)}, u32[]{:S(2)}, u32[]{:S(2)}) collective-permute-start(bf16[4,160,512]{2,1,0:T(8,128)(2,1)} %get-tuple-element.34.refs_2_), channel_id=1, source_target_pairs={{0,1},{1,0},{2,3},{3,2},{4,5},{5,4},{6,7},{7,6},{8,9},{9,8},{10,11... | collective-permute-start | bytes 1966088 | tf_op jit(solution)/shard_map/ppermute | solution.py:447
  40.2 13.5 %collective-permute-start.6 = (bf16[1,160,2048]{2,1,0:T(8,128)(2,1)}, bf16[1,160,2048]{2,1,0:T(8,128)(2,1)}, u32[]{:S(2)}, u32[]{:S(2)}) collective-permute-start(bf16[1,160,2048]{2,1,0:T(8,128)(2,1)} %get-tuple-element.32.refs_4_), channel_id=1, source_target_pairs={{0,1},{1,0},{2,3},{3,2},{4,5},{5,4},{6,7},{7,6},{8,9},{9,8},{10,11... | collective-permute-start | bytes 1966088 | tf_op jit(solution)/shard_map/ppermute | solution.py:447
  47.7 2.0 %collective-permute-start.4 = (bf16[1,160,1024]{2,1,0:T(8,128)(2,1)}, bf16[1,160,1024]{2,1,0:T(8,128)(2,1)}, u32[]{:S(2)}, u32[]{:S(2)}) collective-permute-start(bf16[1,160,1024]{2,1,0:T(8,128)(2,1)} %get-tuple-element.36), channel_id=1, source_target_pairs={{0,1},{1,0},{2,3},{3,2},{4,5},{5,4},{6,7},{7,6},{8,9},{9,8},{10,11... | collective-permute-start | bytes 983048 | tf_op jit(solution)/shard_map/ppermute | solution.py:447
  47.7 2.4 %collective-permute-start.5 = (bf16[1,160,1024]{2,1,0:T(8,128)(2,1)}, bf16[1,160,1024]{2,1,0:T(8,128)(2,1)}, u32[]{:S(2)}, u32[]{:S(2)}) collective-permute-start(bf16[1,160,1024]{2,1,0:T(8,128)(2,1)} %get-tuple-element.37), channel_id=1, source_target_pairs={{0,1},{1,0},{2,3},{3,2},{4,5},{5,4},{6,7},{7,6},{8,9},{9,8},{10,11... | collective-permute-start | bytes 983048 | tf_op jit(solution)/shard_map/ppermute | solution.py:447
  52.4 35.3 %collective-permute-start.13 = (bf16[1,160,2560]{2,1,0:T(8,128)(2,1)}, bf16[1,160,2560]{2,1,0:T(8,128)(2,1)S(1)}, u32[]{:S(2)}, u32[]{:S(2)}) collective-permute-start(bf16[1,160,2560]{2,1,0:T(8,128)(2,1)} %add_rows.8.refs_3_.refs_2_), channel_id=1, source_target_pairs={{0,4},{4,0},{8,12},{12,8},{1,5},{5,1},{9,13},{13,9},{2,6},{6,2},{1... | collective-permute-start | bytes 2457608 | tf_op jit(solution)/shard_map/ppermute | solution.py:444
  56.4 30.3 %collective-permute-start.14 = (bf16[1,160,2048]{2,1,0:T(8,128)(2,1)}, bf16[1,160,2048]{2,1,0:T(8,128)(2,1)S(1)}, u32[]{:S(2)}, u32[]{:S(2)}) collective-permute-start(bf16[1,160,2048]{2,1,0:T(8,128)(2,1)} %add_rows.9.refs_3_), channel_id=1, source_target_pairs={{0,8},{4,12},{8,0},{12,4},{1,9},{5,13},{9,1},{13,5},{2,10},{6,14},... | collective-permute-start | bytes 1966088 | tf_op jit(solution)/shard_map/ppermute | solution.py:444
  65.9 7.1 %copy-start = (f32[1,160,2048]{2,1,0:T(8,128)}, f32[1,160,2048]{2,1,0:T(8,128)S(1)}, u32[]{:S(2)}) copy-start(f32[1,160,2048]{2,1,0:T(8,128)S(1)} %get-tuple-element.43.refs_0_) | copy-start | bytes 3932164
  65.9 9.2 %copy-start.6 = (s32[640]{0:T(1024)S(1)}, s32[640]{0:T(1024)}, u32[]{:S(2)}) copy-start(s32[640]{0:T(1024)} %param.10) | copy-start | bytes 7684
  65.9 9.2 %copy-start.7 = (s32[640]{0:T(1024)S(1)}, s32[640]{0:T(1024)}, u32[]{:S(2)}) copy-start(s32[640]{0:T(1024)} %param.11) | copy-start | bytes 7684
  73.1 2.0 %collective-permute-start.9 = (bf16[1,160,1024]{2,1,0:T(8,128)(2,1)}, bf16[1,160,1024]{2,1,0:T(8,128)(2,1)}, u32[]{:S(2)}, u32[]{:S(2)}) collective-permute-start(bf16[1,160,1024]{2,1,0:T(8,128)(2,1)} %get-tuple-element.42), channel_id=1, source_target_pairs={{0,1},{1,0},{2,3},{3,2},{4,5},{5,4},{6,7},{7,6},{8,9},{9,8},{10,11... | collective-permute-start | bytes 983048 | tf_op jit(solution)/shard_map/ppermute | solution.py:447
  73.3 8.7 %collective-permute-start.11 = (bf16[1,160,1024]{2,1,0:T(8,128)(2,1)}, bf16[1,160,1024]{2,1,0:T(8,128)(2,1)S(1)}, u32[]{:S(2)}, u32[]{:S(2)}) collective-permute-start(bf16[1,160,1024]{2,1,0:T(8,128)(2,1)} %get-tuple-element.39.refs_2_), channel_id=1, source_target_pairs={{0,1},{1,0},{2,3},{3,2},{4,5},{5,4},{6,7},{7,6},{8,9},{9,8},{10,11... | collective-permute-start | bytes 983048 | tf_op jit(solution)/shard_map/ppermute | solution.py:447
  73.8 7.5 %collective-permute-start.12 = (bf16[1,160,1024]{2,1,0:T(8,128)(2,1)}, bf16[1,160,1024]{2,1,0:T(8,128)(2,1)S(1)}, u32[]{:S(2)}, u32[]{:S(2)}) collective-permute-start(bf16[1,160,1024]{2,1,0:T(8,128)(2,1)} %get-tuple-element.44), channel_id=1, source_target_pairs={{0,1},{1,0},{2,3},{3,2},{4,5},{5,4},{6,7},{7,6},{8,9},{9,8},{10,11... | collective-permute-start | bytes 983048 | tf_op jit(solution)/shard_map/ppermute | solution.py:447
  75.1 1.8 %collective-permute-start.8 = (bf16[1,160,1024]{2,1,0:T(8,128)(2,1)}, bf16[1,160,1024]{2,1,0:T(8,128)(2,1)S(1)}, u32[]{:S(2)}, u32[]{:S(2)}) collective-permute-start(bf16[1,160,1024]{2,1,0:T(8,128)(2,1)} %get-tuple-element.41.refs_5_), channel_id=1, source_target_pairs={{0,1},{1,0},{2,3},{3,2},{4,5},{5,4},{6,7},{7,6},{8,9},{9,8},{10,11... | collective-permute-start | bytes 983048 | tf_op jit(solution)/shard_map/ppermute | solution.py:447
  76.9 2.4 %copy-start.8 = (bf16[1,160,2048]{2,1,0:T(8,128)(2,1)S(1)}, bf16[1,160,2048]{2,1,0:T(8,128)(2,1)}, u32[]{:S(2)}) copy-start(bf16[1,160,2048]{2,1,0:T(8,128)(2,1)} %get-tuple-element.48) | copy-start | bytes 1966084
  79.3 2.0 %copy-start.5 = (bf16[1,160,2048]{2,1,0:T(8,128)(2,1)S(1)}, bf16[1,160,2048]{2,1,0:T(8,128)(2,1)}, u32[]{:S(2)}) copy-start(bf16[1,160,2048]{2,1,0:T(8,128)(2,1)} %add_rows.10.refs_2_) | copy-start | bytes 1966084
  79.3 8.4 %copy-start.1 = (f32[1,160,2048]{2,1,0:T(8,128)S(1)}, f32[1,160,2048]{2,1,0:T(8,128)}, u32[]{:S(2)}) copy-start(f32[1,160,2048]{2,1,0:T(8,128)} %copy-done) | copy-start | bytes 3932164
  79.3 22.0 %collective-permute-start.17 = (bf16[1,160,2048]{2,1,0:T(8,128)(2,1)S(1)}, bf16[1,160,2048]{2,1,0:T(8,128)(2,1)S(1)}, u32[]{:S(2)}, u32[]{:S(2)}) collective-permute-start(bf16[1,160,2048]{2,1,0:T(8,128)(2,1)S(1)} %copy-done.8), channel_id=1, source_target_pairs={{0,1},{1,0},{2,3},{3,2},{4,5},{5,4},{6,7},{7,6},{8,9},{9,8},{10,11... | collective-permute-start | bytes 1966088 | tf_op jit(solution)/shard_map/ppermute | solution.py:447
  81.3 30.7 %collective-permute-start.10 = (bf16[1,160,2048]{2,1,0:T(8,128)(2,1)S(1)}, bf16[1,160,2048]{2,1,0:T(8,128)(2,1)S(1)}, u32[]{:S(2)}, u32[]{:S(2)}) collective-permute-start(bf16[1,160,2048]{2,1,0:T(8,128)(2,1)S(1)} %copy-done.5), channel_id=1, source_target_pairs={{0,4},{4,0},{8,12},{12,8},{1,5},{5,1},{9,13},{13,9},{2,6},{6,2},{1... | collective-permute-start | bytes 1966088 | tf_op jit(solution)/shard_map/ppermute | solution.py:444
  89.8 30.3 %collective-permute-start.15 = (bf16[1,160,2048]{2,1,0:T(8,128)(2,1)}, bf16[1,160,2048]{2,1,0:T(8,128)(2,1)S(1)}, u32[]{:S(2)}, u32[]{:S(2)}) collective-permute-start(bf16[1,160,2048]{2,1,0:T(8,128)(2,1)} %add_rows.12.refs_3_), channel_id=1, source_target_pairs={{0,8},{4,12},{8,0},{12,4},{1,9},{5,13},{9,1},{13,5},{2,10},{6,14},... | collective-permute-start | bytes 1966088 | tf_op jit(solution)/shard_map/ppermute | solution.py:444
  99.8 1.5 copy-start.2
  99.8 12.2 %collective-permute-start.20 = (bf16[1,160,1024]{2,1,0:T(8,128)(2,1)}, bf16[1,160,1024]{2,1,0:T(8,128)(2,1)S(1)}, u32[]{:S(2)}, u32[]{:S(2)}) collective-permute-start(bf16[1,160,1024]{2,1,0:T(8,128)(2,1)} %get-tuple-element.50), channel_id=1, source_target_pairs={{0,1},{1,0},{2,3},{3,2},{4,5},{5,4},{6,7},{7,6},{8,9},{9,8},{10,11... | collective-permute-start | bytes 983048 | tf_op jit(solution)/shard_map/ppermute | solution.py:447
  99.8 12.2 %collective-permute-start.21 = (bf16[1,160,1024]{2,1,0:T(8,128)(2,1)}, bf16[1,160,1024]{2,1,0:T(8,128)(2,1)S(1)}, u32[]{:S(2)}, u32[]{:S(2)}) collective-permute-start(bf16[1,160,1024]{2,1,0:T(8,128)(2,1)} %get-tuple-element.51), channel_id=1, source_target_pairs={{0,1},{1,0},{2,3},{3,2},{4,5},{5,4},{6,7},{7,6},{8,9},{9,8},{10,11... | collective-permute-start | bytes 983048 | tf_op jit(solution)/shard_map/ppermute | solution.py:447
  101.2 18.9 %copy-start.3 = (f32[160,128]{1,0:T(8,128)}, f32[160,128]{1,0:T(8,128)S(1)}, u32[]{:S(2)}) copy-start(f32[160,128]{1,0:T(8,128)S(1)} %get-tuple-element.56.sin_ref) | copy-start | bytes 245764
  103.3 25.7 %collective-permute-start.22 = (bf16[160,2048]{1,0:T(8,128)(2,1)S(1)}, bf16[160,2048]{1,0:T(8,128)(2,1)S(1)}, u32[]{:S(2)}, u32[]{:S(2)}) collective-permute-start(bf16[160,2048]{1,0:T(8,128)(2,1)S(1)} %sum_and_rotate.3.refs_0_), channel_id=1, source_target_pairs={{0,1},{1,0},{2,3},{3,2},{4,5},{5,4},{6,7},{7,6},{8,9},{9,8},{10,11... | collective-permute-start | bytes 1966088 | tf_op jit(solution)/shard_map/ppermute | solution.py:447
  121.7 7.7 %collective-permute-start.23 = (bf16[160,1536]{1,0:T(8,128)(2,1)S(1)}, bf16[160,1536]{1,0:T(8,128)(2,1)}, u32[]{:S(2)}, u32[]{:S(2)}) collective-permute-start(bf16[160,1536]{1,0:T(8,128)(2,1)S(1)} %sum_and_rotate.4.refs_1_), channel_id=1, source_target_pairs={{0,1},{1,0},{2,3},{3,2},{4,5},{5,4},{6,7},{7,6},{8,9},{9,8},{10,11... | collective-permute-start | bytes 1474568 | tf_op jit(solution)/shard_map/ppermute | solution.py:447
  123.1 3.5 %collective-permute-start.16 = (bf16[320,128]{1,0:T(8,128)(2,1)S(1)}, bf16[320,128]{1,0:T(8,128)(2,1)S(1)}, u32[]{:S(2)}, u32[]{:S(2)}) collective-permute-start(bf16[320,128]{1,0:T(8,128)(2,1)S(1)} %get-tuple-element.45.own_ref), channel_id=1, source_target_pairs={{0,1},{1,0},{2,3},{3,2},{4,5},{5,4},{6,7},{7,6},{8,9},{9,8},{10,11... | collective-permute-start | bytes 245768 | tf_op jit(solution)/shard_map/ppermute | solution.py:447
  124.0 15.8 %collective-permute-start.27 = (bf16[1,320,128]{2,1,0:T(8,128)(2,1)S(1)}, bf16[1,320,128]{2,1,0:T(8,128)(2,1)S(1)}, u32[]{:S(2)}, u32[]{:S(2)}) collective-permute-start(bf16[1,320,128]{2,1,0:T(8,128)(2,1)S(1)} %get-tuple-element.54.refs_0_), channel_id=1, source_target_pairs={{0,12},{4,8},{8,4},{12,0},{1,13},{5,9},{9,5},{13,1},{2,14},{6,10},... | collective-permute-start | bytes 245768 | tf_op jit(solution)/shard_map/ppermute | solution.py:444
  126.7 13.1 %collective-permute-start.26 = (bf16[1,320,128]{2,1,0:T(8,128)(2,1)S(1)}, bf16[1,320,128]{2,1,0:T(8,128)(2,1)S(1)}, u32[]{:S(2)}, u32[]{:S(2)}) collective-permute-start(bf16[1,320,128]{2,1,0:T(8,128)(2,1)S(1)} %get-tuple-element.54.refs_0_), channel_id=1, source_target_pairs={{0,8},{4,12},{8,0},{12,4},{1,9},{5,13},{9,1},{13,5},{2,10},{6,14},... | collective-permute-start | bytes 245768 | tf_op jit(solution)/shard_map/ppermute | solution.py:444
  126.7 13.1 %collective-permute-start.25 = (bf16[1,320,128]{2,1,0:T(8,128)(2,1)S(1)}, bf16[1,320,128]{2,1,0:T(8,128)(2,1)S(1)}, u32[]{:S(2)}, u32[]{:S(2)}) collective-permute-start(bf16[1,320,128]{2,1,0:T(8,128)(2,1)S(1)} %get-tuple-element.54.refs_0_), channel_id=1, source_target_pairs={{0,4},{4,0},{8,12},{12,8},{1,5},{5,1},{9,13},{13,9},{2,6},{6,2},{1... | collective-permute-start | bytes 245768 | tf_op jit(solution)/shard_map/ppermute | solution.py:444
  129.0 11.7 %collective-permute-start.18 = (bf16[1,160,512]{2,1,0:T(8,128)(2,1)}, bf16[1,160,512]{2,1,0:T(8,128)(2,1)S(1)}, u32[]{:S(2)}, u32[]{:S(2)}) collective-permute-start(bf16[1,160,512]{2,1,0:T(8,128)(2,1)} %add_rows.11.refs_7_), channel_id=1, source_target_pairs={{0,4},{4,0},{8,12},{12,8},{1,5},{5,1},{9,13},{13,9},{2,6},{6,2},{1... | collective-permute-start | bytes 491528 | tf_op jit(solution)/shard_map/ppermute | solution.py:444
  129.4 11.3 %collective-permute-start.19 = (bf16[1,160,512]{2,1,0:T(8,128)(2,1)S(1)}, bf16[1,160,512]{2,1,0:T(8,128)(2,1)S(1)}, u32[]{:S(2)}, u32[]{:S(2)}) collective-permute-start(bf16[1,160,512]{2,1,0:T(8,128)(2,1)S(1)} %copy-done.2), channel_id=1, source_target_pairs={{0,8},{4,12},{8,0},{12,4},{1,9},{5,13},{9,1},{13,5},{2,10},{6,14},... | collective-permute-start | bytes 491528 | tf_op jit(solution)/shard_map/ppermute | solution.py:444
  132.3 8.4 %copy-start.4 = (f32[160,128]{1,0:T(8,128)S(1)}, f32[160,128]{1,0:T(8,128)}, u32[]{:S(2)}) copy-start(f32[160,128]{1,0:T(8,128)} %copy-done.3) | copy-start | bytes 245764
  139.8 2.2 %collective-permute-start.28 = (bf16[4,320,128]{2,1,0:T(8,128)(2,1)S(1)}, bf16[4,320,128]{2,1,0:T(8,128)(2,1)S(1)}, u32[]{:S(2)}, u32[]{:S(2)}) collective-permute-start(bf16[4,320,128]{2,1,0:T(8,128)(2,1)S(1)} %stack_slots.1.refs_0_.refs_1_), channel_id=1, source_target_pairs={{0,1},{1,0},{2,3},{3,2},{4,5},{5,4},{6,7},{7,6},{8,9},{9,8},{10,11... | collective-permute-start | bytes 983048 | tf_op jit(solution)/shard_map/ppermute | solution.py:447
  141.8 2.3 %collective-permute-start.24 = (bf16[160,512]{1,0:T(8,128)(2,1)S(1)}, bf16[160,512]{1,0:T(8,128)(2,1)S(1)}, u32[]{:S(2)}, u32[]{:S(2)}) collective-permute-start(bf16[160,512]{1,0:T(8,128)(2,1)S(1)} %sum_and_rotate.5.refs_1_), channel_id=1, source_target_pairs={{0,1},{1,0},{2,3},{3,2},{4,5},{5,4},{6,7},{7,6},{8,9},{9,8},{10,11... | collective-permute-start | bytes 491528 | tf_op jit(solution)/shard_map/ppermute | solution.py:447
